TPU v7x, 32 devices: a whole 2x2x4 slice. The times are simulated.
32 devices in a mesh: groups: 2 (over y), streams: 4 (over z), heads: 2 (over x), sub: 2 (over core).
Axes of the slice: x: 2, y: 2, z: 4, core: 2. Of those that a mesh axis runs over, the one named last changes fastest.
Arguments:
- inputs: bfloat16 [4, 1024, 3584], P(None, ('groups', 'streams', 'sub')), parts along dimension 1, may hold values from -6 to 6
- input_norm_gain: float32 [3584], replicated, may hold values from 0.1 to 1.9
- projection_weight: bfloat16 [3584, 4608], P(None, 'heads'), may hold values from -0.09375 to 0.09375
- projection_bias: float32 [4608], P('heads'), may hold values from -3 to 3
- speaker: int32 [1024, 1], P(('groups', 'streams', 'sub')), parts along dimension 0, may hold values from 0 to 31; in each aligned block of 64 rows (0 to 63, 64 to 127, ...) at most 2 rows name the same one
- speaker_adapter_slot: int32 [64], P('groups'), parts along dimension 0, may hold values from 0 to 31, each once
- cache_fill_length: int32 [1024], P(('groups', 'streams', 'sub')), parts along dimension 0, may hold values from 1 to 32, as said below
- rotated_key_cache: bfloat16 [1024, 32, 512], P(('groups', 'streams', 'sub'), None, 'heads'), parts along dimension 0
- value_cache_rows: bfloat16 [1024, 32, 512], P(('groups', 'streams', 'sub'), None, 'heads'), parts along dimension 0, may hold values from -6 to 6
- adapter_down_maps: bfloat16 [64, 3584, 128], P(('groups', 'streams', 'sub'), 'heads'), parts along dimension 0, may hold values from -0.09375 to 0.09375
- adapter_query_up: bfloat16 [64, 64, 3584], P(('groups', 'streams', 'sub'), None, 'heads'), parts along dimension 0, may hold values from -0.75 to 0.75
- adapter_value_up: bfloat16 [64, 64, 512], P(('groups', 'streams', 'sub'), None, 'heads'), parts along dimension 0, may hold values from -0.75 to 0.75
- flow_decoder_owner: int32 [1024, 1], P(('groups', 'streams', 'sub')), parts along dimension 0, may hold values from 0 to 7; in each aligned block of 64 rows (0 to 63, 64 to 127, ...) at most 16 rows name the same one
Outputs:
- flow_input: bfloat16 [16, 128, 4, 3584], P(('groups', 'streams', 'sub'), None, None, 'heads'), parts along dimension 0
There are 2 independent parts, one for each index of `groups`. A program takes and returns all parts, laid end to end along the dimension named above; an argument that names none is the same for every part. Nothing has to cross between parts.
Inputs may be any that keep to these rules, and one draw needn't show every extreme that they name: In the streams of one device no speaker appears more than 2 times. `speaker_adapter_slot`: each speaker has its own slot; slot j is held by device j // 4 of the stream axes. `cache_fill_length`: the first stream of every device has a full cache. `flow_decoder_owner`: no owner gets more than 16 streams from one device.
All inputs are finite; a program needn't handle non-finite values.
Results may differ from a plain program's by a relative error of at most 0.0055.
The roundings to bfloat16 on the way count: a program that leaves them out, or rounds other values in their place, can miss the bound.
Values may be sent and summed in bfloat16 or wider, within the bound.
No kernel may reach another device: no remote copies, remote signals or barrier semaphores. Data moves between devices by JAX's collectives and lax.ppermute only.
A program may use at most 128 MiB of HBM per device.

v0:
```python
import math

import jax
import jax.numpy as jnp
from jax import lax
from jax.sharding import PartitionSpec as P

QUERY_HEADS = 28
KEY_VALUE_HEADS = 4
HEAD_WIDTH = 128
ADAPTER_RANK = 64
MOST = 2


def rms_normed(inputs, gain):
    values = inputs.astype(jnp.float32)
    mean_sq = jnp.mean(values * values, axis=-1, keepdims=True)
    return (values * lax.rsqrt(mean_sq + 1e-06) * gain).astype(jnp.bfloat16)


def rotate(vectors, cosine, sine_part):
    half = vectors.shape[-1] // 2
    first = vectors[..., :half]
    second = vectors[..., half:]
    return jnp.concatenate(
        [first * cosine - second * sine_part, second * cosine + first * sine_part], axis=-1
    )


def angles(lengths, steps_count, half):
    position = (lengths[None, :] + jnp.arange(steps_count, dtype=jnp.int32)[:, None]).astype(
        jnp.float32
    )
    freq = jnp.exp(jnp.arange(half, dtype=jnp.float32) * (-math.log(1000000.0) / half))
    return position[..., None] * freq


def attend(queries, new_keys, new_values, rotated_key_cache, value_cache_rows, lengths):
    steps_count, rows, groups, per_group, head_dim = queries.shape
    cache_count = rotated_key_cache.shape[1]
    keys_all = jnp.concatenate(
        [
            rotated_key_cache.reshape(rows, cache_count, groups, head_dim),
            jnp.transpose(new_keys, (1, 0, 2, 3)),
        ],
        axis=1,
    )
    values_all = jnp.concatenate(
        [
            value_cache_rows.reshape(rows, cache_count, groups, head_dim),
            jnp.transpose(new_values, (1, 0, 2, 3)),
        ],
        axis=1,
    )
    scores = jnp.einsum(
        "trgqd,rcgd->rgtqc", queries, keys_all, preferred_element_type=jnp.float32
    ) * head_dim ** (-0.5)
    column = jnp.arange(cache_count + steps_count, dtype=jnp.int32)
    step_index = jnp.arange(steps_count, dtype=jnp.int32)
    in_cache = column[None, None, :] < lengths[:, None, None]
    fresh = (column[None, :] - cache_count <= step_index[:, None]) & (
        column[None, :] >= cache_count
    )
    allowed = jnp.where(column[None, None, :] < cache_count, in_cache, fresh[None, :, :])
    scores = jnp.where(allowed[:, None, :, None, :], scores, -1e30)
    peak = jnp.max(scores, axis=-1, keepdims=True)
    expo = jnp.exp(scores - peak)
    weights = (expo / jnp.sum(expo, axis=-1, keepdims=True)).astype(jnp.bfloat16)
    context = jnp.einsum(
        "rgtqc,rcgd->trgqd", weights, values_all, preferred_element_type=jnp.float32
    )
    return context.astype(jnp.bfloat16).reshape(steps_count, rows, groups * per_group * head_dim)


def ranks_within(labels):
    count = labels.shape[0]
    order = jnp.arange(count, dtype=jnp.int32)
    earlier = (labels[:, None] == labels[None, :]) & (order[None, :] < order[:, None])
    return jnp.sum(earlier.astype(jnp.int32), axis=1)


def selector(places, total):
    return (jnp.arange(total, dtype=jnp.int32)[:, None] == places[None, :]).astype(jnp.bfloat16)


def on_device(
    inputs,
    input_norm_gain,
    projection_weight,
    projection_bias,
    speaker,
    speaker_adapter_slot,
    cache_fill_length,
    rotated_key_cache,
    value_cache_rows,
    adapter_down_maps,
    adapter_query_up,
    adapter_value_up,
    flow_decoder_owner,
):
    steps_count, rows, width = inputs.shape
    lanes = lax.axis_size(("streams", "sub"))
    sliced_rows = adapter_down_maps.shape[1]
    query_columns = adapter_query_up.shape[2]
    value_columns = adapter_value_up.shape[2]
    delta_cols = query_columns + value_columns
    groups = value_columns // HEAD_WIDTH
    per_group = QUERY_HEADS // KEY_VALUE_HEADS
    replica_local_slots = adapter_down_maps.shape[0]
    speakers_all = speaker_adapter_slot.shape[0]
    send_slots = speakers_all * MOST
    normed = rms_normed(inputs, input_norm_gain)
    qkv = (
        jnp.dot(
            normed.reshape(steps_count * rows, width),
            projection_weight,
            preferred_element_type=jnp.float32,
        )
        + projection_bias
    )
    qkv = qkv.reshape(steps_count, rows, groups, per_group + 2, HEAD_WIDTH)
    match = speaker[:, 0][:, None] == jnp.arange(speakers_all, dtype=jnp.int32)[None, :]
    slots = jnp.sum(jnp.where(match, speaker_adapter_slot[None, :], 0), axis=1)
    places = slots * MOST + ranks_within(slots)
    pick = selector(places, send_slots)
    own_cols = lax.dynamic_slice_in_dim(
        normed, lax.axis_index("heads") * sliced_rows, sliced_rows, 2
    )
    outgoing = jnp.einsum("jr,trd->jtd", pick, own_cols, preferred_element_type=jnp.float32).astype(
        jnp.bfloat16
    )
    outgoing = outgoing.reshape(lanes, replica_local_slots * MOST, steps_count, sliced_rows)
    arrived = lax.all_to_all(outgoing, ("streams", "sub"), split_axis=0, concat_axis=0, tiled=True)
    items = arrived.shape[2]
    regrouped_rows = arrived.reshape(lanes, replica_local_slots, MOST, items, sliced_rows)
    partial_latent = jnp.einsum(
        "zqyhc,qcx->zqyhx", regrouped_rows, adapter_down_maps, preferred_element_type=jnp.float32
    )
    adapter_latent = lax.psum(partial_latent, "heads").astype(jnp.bfloat16)
    query_adapter_delta = jnp.einsum(
        "xrpzq,rqw->xrpzw",
        adapter_latent[..., :ADAPTER_RANK],
        adapter_query_up,
        preferred_element_type=jnp.float32,
    )
    value_adapter_delta = jnp.einsum(
        "xrpzq,rqw->xrpzw",
        adapter_latent[..., ADAPTER_RANK:],
        adapter_value_up,
        preferred_element_type=jnp.float32,
    )
    joined = jnp.concatenate([query_adapter_delta, value_adapter_delta], axis=-1).astype(
        jnp.bfloat16
    )
    returned = lax.all_to_all(
        joined.reshape(lanes, replica_local_slots * MOST, items, delta_cols),
        ("streams", "sub"),
        split_axis=0,
        concat_axis=0,
        tiled=True,
    )
    returned = returned.reshape(send_slots, steps_count, delta_cols)
    gathered = jnp.einsum("jr,jtc->trc", pick, returned, preferred_element_type=jnp.float32)
    angle = angles(cache_fill_length, steps_count, HEAD_WIDTH // 2)
    cosine = jnp.cos(angle)
    sine_part = jnp.sin(angle)
    queries = qkv[..., :per_group, :] + gathered[..., :query_columns].reshape(
        steps_count, rows, groups, per_group, HEAD_WIDTH
    )
    queries = rotate(queries, cosine[:, :, None, None, :], sine_part[:, :, None, None, :]).astype(
        jnp.bfloat16
    )
    new_keys = rotate(
        qkv[..., per_group, :], cosine[:, :, None, :], sine_part[:, :, None, :]
    ).astype(jnp.bfloat16)
    new_values = (
        qkv[..., per_group + 1, :]
        + gathered[..., query_columns:].reshape(steps_count, rows, groups, HEAD_WIDTH)
    ).astype(jnp.bfloat16)
    context = attend(
        queries, new_keys, new_values, rotated_key_cache, value_cache_rows, cache_fill_length
    )
    fmost = max(2, (2 * rows + lanes - 1) // lanes)
    owner = flow_decoder_owner[:, 0]
    flow_places = owner * fmost + ranks_within(owner)
    flow_pick = selector(flow_places, lanes * fmost)
    packed = jnp.einsum(
        "jr,trc->jtc", flow_pick, context, preferred_element_type=jnp.float32
    ).astype(jnp.bfloat16)
    packed = packed.reshape(lanes, fmost, steps_count, query_columns)
    landed = lax.all_to_all(packed, ("streams", "sub"), split_axis=0, concat_axis=0, tiled=True)
    return landed.reshape(1, lanes * fmost, steps_count, query_columns)


def solution(mesh):
    placed = (
        P(None, ("groups", "streams", "sub"), None),
        P(),
        P(None, "heads"),
        P("heads"),
        P(("groups", "streams", "sub"), None),
        P("groups"),
        P(("groups", "streams", "sub")),
        P(("groups", "streams", "sub"), None, "heads"),
        P(("groups", "streams", "sub"), None, "heads"),
        P(("groups", "streams", "sub"), "heads", None),
        P(("groups", "streams", "sub"), None, "heads"),
        P(("groups", "streams", "sub"), None, "heads"),
        P(("groups", "streams", "sub"), None),
    )
    return jax.shard_map(
        on_device,
        mesh=mesh,
        in_specs=placed,
        out_specs=P(("groups", "streams", "sub"), None, None, "heads"),
        check_vma=False,
    )
```

profile of v0, /device:TPU:0, one launch (start us, length us, event | category | flops | bytes accessed | tf_op | source)
XLA Modules:
  0.0 150.7 jit_solution(18383994036145944856)
XLA Ops:
  0.0 0.9 select_reduce_fusion
  0.9 0.2 convert_reduce_fusion
  1.1 1.9 %fusion.1 = f32[4,64]{1,0:T(4,128)S(1)} fusion(bf16[4,64,3584]{2,1,0:T(8,128)(2,1)} %param.13), kind=kLoop, calls=%fused_computation.4 | loop fusion | flops 2752256 | bytes 1836032 | tf_op jit(solution)/shard_map/reduce_sum | solution.py:17
  3.0 2.0 %fusion.3 = bf16[4,64,3584]{2,1,0:T(8,128)(2,1)S(1)} fusion(bf16[4,64,3584]{2,1,0:T(8,128)(2,1)} %param.13, f32[3584]{0:T(1024)} %param.14, f32[4,64]{1,0:T(4,128)S(1)} %add_rsqrt_fusion), kind=kLoop, calls=%fused_computation.6 | loop fusion | flops 3670016 | bytes 3685376 | tf_op jit(solution)/shard_map/convert_element_type | solution.py:18
  5.1 1.2 copy-done.3
  6.3 0.5 fusion.4
  6.8 1.0 copy.69
  7.8 6.3 %all-to-all-start = ((bf16[8,8,4,1792]{3,1,2,0:T(8,128)(2,1)}), bf16[8,8,4,1792]{3,1,2,0:T(8,128)(2,1)S(1)}, u32[]{:S(2)}, u32[]{:S(2)}) async-start(bf16[8,8,4,1792]{3,1,2,0:T(8,128)(2,1)} %copy.69), calls=%async_computation | async-start | bytes 1835008 | tf_op jit(solution)/shard_map/all_to_all | solution.py:133
  14.2 12.1 %convolution_add_fusion = f32[256,2304]{1,0:T(8,128)} fusion(bf16[256,3584]{1,0:T(8,128)(2,1)} %bitcast.98, bf16[3584,2304]{1,0:T(8,128)(2,1)} %param.15, f32[2304]{0:T(1024)S(1)} %copy-done.11), kind=kOutput, calls=%fused_computation.3 | convolution fusion | flops 4228448256 | bytes 20718592 | tf_op jit(solution)/shard_map/dot_general | solution.py:114
  26.3 4.2 %reshape.175 = f32[4,64,2,9,128]{4,3,2,1,0:T(8,128)} reshape(f32[256,2304]{1,0:T(8,128)} %convolution_add_fusion) | data formatting | bytes 4718592 | tf_op jit(solution)/shard_map/reshape | solution.py:121
  30.5 0.5 iota_compare_fusion.6
  31.1 0.7 convert_reduce_fusion.1
  31.9 1.1 multiply_cosine_fusion
  33.0 2.6 %fusion.58 = (f32[4,64,2,1,128]{4,3,2,1,0:T(1,128)S(1)}, f32[4,64,2,1,128]{4,3,2,1,0:T(1,128)S(1)}) fusion(f32[4,64,2,9,128]{4,3,2,1,0:T(8,128)} %reshape.175), kind=kLoop, calls=%fused_computation.91 | loop fusion | bytes 1048576 | tf_op jit(solution)/shard_map/slice | solution.py:174
  35.6 2.4 %all-to-all-done = bf16[8,8,4,1792]{3,1,2,0:T(8,128)(2,1)S(1)} async-done(((bf16[8,8,4,1792]{3,1,2,0:T(8,128)(2,1)}), bf16[8,8,4,1792]{3,1,2,0:T(8,128)(2,1)S(1)}, u32[]{:S(2)}, u32[]{:S(2)}) %all-to-all-start) | async-done | bytes 917536 | tf_op jit(solution)/shard_map/all_to_all | solution.py:133
  38.0 0.5 copy.70
  38.5 1.1 fusion.14
  39.6 10.5 %all-reduce.1 = bf16[8,4,2,4,128]{4,0,3,2,1:T(8,128)(2,1)S(1)} all-reduce(f32[8,4,2,4,128]{4,0,3,2,1:T(8,128)} %fusion.14), channel_id=1, replica_groups=mesh['groups'=2,'streams'=4,'heads'=2,'sub'=2] {'heads'}, use_global_device_ids=true, to_apply=%region_4.5 | all-reduce | flops 32768 | bytes 196608 | tf_op jit(solution)/shard_map/psum | solution.py:139
  50.2 0.4 convolution_convert_fusion.1
  50.6 0.2 copy-done.8
  50.8 0.4 copy.71
  51.1 1.1 convolution_convert_fusion.4
  52.3 1.6 %pad_maximum_fusion = bf16[8,8,4,2048]{3,2,1,0:T(4,128)(2,1)} fusion(bf16[8,8,4,256]{3,2,1,0:T(4,128)(2,1)S(1)} %copy.72, bf16[8,8,4,1792]{3,2,1,0:T(4,128)(2,1)S(1)} %copy.71), kind=kLoop, calls=%fused_computation.34 | loop fusion | flops 2097152 | bytes 2097152 | tf_op jit(solution)/shard_map/concatenate | solution.py:152
  53.9 3.9 %all-to-all-start.1 = ((bf16[8,8,4,2048]{3,2,1,0:T(4,128)(2,1)}), bf16[8,8,4,2048]{3,2,1,0:T(4,128)(2,1)S(1)}, u32[]{:S(2)}, u32[]{:S(2)}) async-start(bf16[8,8,4,2048]{3,2,1,0:T(4,128)(2,1)} %pad_maximum_fusion), calls=%async_computation.1 | async-start | bytes 2097152 | tf_op jit(solution)/shard_map/all_to_all | solution.py:155
  57.8 0.2 copy.115
  58.0 0.2 subtract_convert_fusion.1
  58.2 0.2 maximum_bitcast_fusion.8
  58.6 0.4 copy-done.4
  59.0 1.2 copy_bitcast_fusion
  60.1 1.2 copy_bitcast_fusion.1
  61.4 22.7 %all-to-all-done.1 = bf16[8,8,4,2048]{3,2,1,0:T(4,128)(2,1)S(1)} async-done(((bf16[8,8,4,2048]{3,2,1,0:T(4,128)(2,1)}), bf16[8,8,4,2048]{3,2,1,0:T(4,128)(2,1)S(1)}, u32[]{:S(2)}, u32[]{:S(2)}) %all-to-all-start.1) | async-done | bytes 1048608 | tf_op jit(solution)/shard_map/all_to_all | solution.py:155
  84.1 0.9 convolution_bitcast_fusion
  85.0 0.1 slice.49
  85.2 1.2 copy-done.2
  86.3 1.9 %reshape.180 = f32[4,64,2,7,128]{4,3,2,1,0:T(8,128)} reshape(f32[4,64,1792]{2,1,0:T(8,128)S(1)} %slice.49) | data formatting | bytes 3670016 | tf_op jit(solution)/shard_map/reshape | solution.py:167
  88.2 2.5 %copy_add_fusion = f32[4,64,2,7,128]{4,3,0,2,1:T(8,128)S(1)} fusion(f32[4,64,2,7,128]{4,3,2,1,0:T(8,128)} %reshape.180, f32[4,64,2,9,128]{4,3,2,1,0:T(8,128)} %reshape.175), kind=kLoop, calls=%fused_computation.12 | loop fusion | flops 458752 | bytes 6029312 | tf_op jit(solution)/shard_map/add | solution.py:167
  90.7 1.9 %subtract_convert_fusion = (bf16[4,64,2,7,64]{4,3,0,2,1:T(8,128)(2,1)S(1)}, bf16[4,64,2,7,64]{4,3,0,2,1:T(8,128)(2,1)}) fusion(f32[4,64,2,7,128]{4,3,0,2,1:T(8,128)S(1)} %copy_add_fusion, f32[4,64,64]{2,0,1:T(4,128)S(1)} %get-tuple-element.12, f32[4,64,64]{2,0,1:T(4,128)S(1)} %get-tuple-element.11), kind=kLoop, calls=%fused_computation.17 | loop fusion | flops 1835008 | bytes 2883584 | tf_op jit(solution)/shard_map/convert.2
  92.6 0.1 reshape.179
  92.7 0.3 fusion.34
  93.0 4.5 %fusion.59 = (f32[64,2,4,7]{3,2,1,0:T(4,128)S(1)}, f32[64,2,4,7,36]{4,3,2,1,0:T(8,128)}) fusion(pred[64,4,36]{2,1,0:T(4,128)(4,1)S(1)} %broadcast_select_fusion, bf16[64,4,2,128]{3,1,2,0:T(4,128)(2,1)S(1)} %maximum_bitcast_fusion.8, bf16[64,32,2,128]{3,1,2,0:T(8,128)(2,1)} %copy_bitcast_fusion, bf16[4,64,2,7,64]{4,3,0,2,1:T(8,128)(2,1)} %get-tuple-element.8, ...), kind=kOutput, calls=%fused_computation.92 | convolution fusion | flops 37740580 | bytes 2636800 | tf_op jit(solution)/shard_map/sub | solution.py:67
  97.6 2.3 %fusion.8 = bf16[4,64,2,7,128]{4,3,0,2,1:T(8,128)(2,1)S(1)} fusion(bf16[64,4,2,128]{3,1,2,0:T(4,128)(2,1)S(1)} %fusion.34, bf16[64,32,2,128]{3,1,2,0:T(8,128)(2,1)S(1)} %copy-done.6, f32[64,2,4,7,36]{4,3,2,1,0:T(8,128)} %get-tuple-element.14, f32[64,2,4,7]{3,2,1,0:T(4,128)S(1)} %get-tuple-element.13), kind=kOutput, calls=%fused_computation.22 | convolution fusion | flops 36106240 | bytes 2627584 | tf_op jit(solution)/shard_map/rgtqc,rcgd->trgqd/dot_general | solution.py:69
  99.9 0.2 copy.80
  100.1 1.0 reshape.182
  101.1 0.7 convolution_convert_fusion
  101.9 0.2 copy.81
  102.0 45.9 %all_to_all.15 = bf16[8,16,4,1792]{3,1,2,0:T(8,128)(2,1)S(1)} all-to-all(bf16[8,16,4,1792]{3,1,2,0:T(8,128)(2,1)S(1)} %copy.81), channel_id=1, replica_groups=mesh['groups'=2,'streams'=4,'heads'=2,'sub'=2] {'streams','sub'}, dimensions={0} | all-to-all | bytes 3670016 | tf_op jit(solution)/shard_map/all_to_all | solution.py:191
  147.9 0.1 copy.82
  148.1 2.6 %copy.83 = bf16[1,128,4,1792]{3,2,1,0:T(4,128)(2,1)} copy(bf16[1,128,4,1792]{3,1,2,0:T(8,128)(2,1)S(1)} %bitcast.96) | data formatting | bytes 3670016 | tf_op jit(solution)/shard_map/reshape | solution.py:192
  (39 shorter events, 0.4 us)
Async XLA Ops:
  0.0 38.5 %copy-start = (bf16[4,1792,128]{2,1,0:T(8,128)(2,1)S(1)}, bf16[4,1792,128]{2,1,0:T(8,128)(2,1)}, u32[]{:S(2)}) copy-start(bf16[4,1792,128]{2,1,0:T(8,128)(2,1)} %param.22) | copy-start | bytes 5505028
  5.1 1.2 copy-start.3
  6.8 7.4 %copy-start.11 = (f32[2304]{0:T(1024)S(1)}, f32[2304]{0:T(1024)}, u32[]{:S(2)}) copy-start(f32[2304]{0:T(1024)} %param.16) | copy-start | bytes 27652
  7.8 30.1 %all-to-all-start = ((bf16[8,8,4,1792]{3,1,2,0:T(8,128)(2,1)}), bf16[8,8,4,1792]{3,1,2,0:T(8,128)(2,1)S(1)}, u32[]{:S(2)}, u32[]{:S(2)}) async-start(bf16[8,8,4,1792]{3,1,2,0:T(8,128)(2,1)} %copy.69), calls=%async_computation | async-start | bytes 1835008 | tf_op jit(solution)/shard_map/all_to_all | solution.py:133
  26.3 4.8 %copy-start.12 = (s32[64,1]{0,1:T(1,128)S(1)}, s32[64,1]{0,1:T(1,128)}, u32[]{:S(2)}) copy-start(s32[64,1]{0,1:T(1,128)} %param.25) | copy-start | bytes 772
  26.3 5.5 %copy-start.10 = (s32[64]{0:T(128)S(1)}, s32[64]{0:T(128)}, u32[]{:S(2)}) copy-start(s32[64]{0:T(128)} %param.19) | copy-start | bytes 772
  38.5 11.7 %copy-start.7 = (bf16[4,64,1792]{2,1,0:T(8,128)(2,1)S(1)}, bf16[4,64,1792]{2,1,0:T(8,128)(2,1)}, u32[]{:S(2)}) copy-start(bf16[4,64,1792]{2,1,0:T(8,128)(2,1)} %param.23) | copy-start | bytes 2752516
  50.1 0.6 copy-start.8
  50.2 1.0 copy-start.9
  53.9 4.5 %copy-start.14 = (s32[64]{0:T(128)S(1)}, s32[64]{0:T(128)}, u32[]{:S(2)}) copy-start(s32[64]{0:T(128)} %convert_reduce_fusion.1) | copy-start | bytes 772
  53.9 4.5 %copy-start.13 = (pred[36]{0:T(512)(128)(4,1)S(1)}, pred[36]{0:T(512)(128)(4,1)}, u32[]{:S(2)}) copy-start(pred[36]{0:T(512)(128)(4,1)} %iota_compare_fusion.6) | copy-start | bytes 112
  53.9 30.2 %all-to-all-start.1 = ((bf16[8,8,4,2048]{3,2,1,0:T(4,128)(2,1)}), bf16[8,8,4,2048]{3,2,1,0:T(4,128)(2,1)S(1)}, u32[]{:S(2)}, u32[]{:S(2)}) async-start(bf16[8,8,4,2048]{3,2,1,0:T(4,128)(2,1)} %pad_maximum_fusion), calls=%async_computation.1 | async-start | bytes 2097152 | tf_op jit(solution)/shard_map/all_to_all | solution.py:155
  57.8 1.2 copy-start.4
  57.8 2.4 %copy-start.5 = (bf16[64,32,256]{2,1,0:T(8,128)(2,1)S(1)}, bf16[64,32,256]{2,1,0:T(8,128)(2,1)}, u32[]{:S(2)}) copy-start(bf16[64,32,256]{2,1,0:T(8,128)(2,1)} %param.21) | copy-start | bytes 3145732
  85.0 1.3 copy-start.2
  90.7 1.9 %slice-start = ((f32[4,64,2048]{2,1,0:T(8,128)}), f32[4,64,256]{2,1,0:T(8,128)S(1)}, s32[]{:S(2)}) async-start(f32[4,64,2048]{2,1,0:T(8,128)} %copy-done.2), calls=%async_computation.3 | async-start | bytes 524288 | tf_op jit(solution)/shard_map/slice | solution.py:178
  93.0 4.5 %copy-start.6 = (bf16[64,32,2,128]{3,1,2,0:T(8,128)(2,1)S(1)}, bf16[64,32,2,128]{3,1,2,0:T(8,128)(2,1)}, u32[]{:S(2)}) copy-start(bf16[64,32,2,128]{3,1,2,0:T(8,128)(2,1)} %copy_bitcast_fusion.1) | copy-start | bytes 3145732
  147.9 2.8 %copy-start.1 = (bf16[4,1792,128]{2,1,0:T(8,128)(2,1)S(1)}, bf16[4,1792,128]{2,1,0:T(8,128)(2,1)}, u32[]{:S(2)}) copy-start(bf16[4,1792,128]{2,1,0:T(8,128)(2,1)} %param.22) | copy-start | bytes 5505028
where the time goes:
time: 151 us
  blocking collectives  56.4 us (37%)
  waiting for transfers between devices  25.1 us (17%)
  matrix products  23.6 us (16%)
  local copies, waits for them, and re-layouts  20.6 us (14%)
  other arithmetic  14.3 us (9%)
  starting transfers between devices  10.2 us (7%)
    all_to_all x1, blocking collectives, on_device(): lax.all_to_all(packed, ('streams', 'sub'), split_axis=0, concat_axis=0, t...  45.9 us
    all_to_all x1, waiting for transfers between devices, on_device(): lax.all_to_all(joined.reshape(lanes, replica_local_slots * MOST, items, d...  22.7 us
    dot_general x1, matrix products, on_device(): jnp.dot(normed.reshape(steps_count * rows, width), projection_weight, pre...  12.1 us
    psum x1, blocking collectives, on_device(): adapter_latent = lax.psum(partial_latent, 'heads').astype(jnp.bfloat16)  10.5 us
    all_to_all x1, starting transfers between devices, on_device(): lax.all_to_all(outgoing, ('streams', 'sub'), split_axis=0, concat_axis=0,...  6.33 us
    sub x1, matrix products, attend(): expo = jnp.exp(scores - peak)  4.53 us
    reshape x1, local copies, waits for them, and re-layouts, on_device(): qkv = qkv.reshape(steps_count, rows, groups, per_group + 2, HEAD_WIDTH)  4.23 us
    all_to_all x1, starting transfers between devices, on_device(): lax.all_to_all(joined.reshape(lanes, replica_local_slots * MOST, items, d...  3.87 us
  transfers between devices with their start and end apart: 2, of which 2 were waited for; matrix products, arithmetic and copies ran while one was open for 16% of the time, Pallas kernels for 0%

commit v1 on v0

--- a/solution.py
+++ b/solution.py
@@ -77,6 +77,27 @@
     order = jnp.arange(count, dtype=jnp.int32)
     earlier = (labels[:, None] == labels[None, :]) & (order[None, :] < order[:, None])
     return jnp.sum(earlier.astype(jnp.int32), axis=1)
+
+
+LANE_AXES = ("streams", "sub")
+
+
+def exchange(blocks):
+    count = len(blocks)
+    landed = [blocks[0]]
+    for shift in range(1, count):
+        pairs = [(lane, lane ^ shift) for lane in range(count)]
+        landed.append(lax.ppermute(blocks[shift], LANE_AXES, pairs))
+    return landed
+
+
+def summed_over_heads(partial):
+    count = lax.axis_size("heads")
+    total = partial
+    for shift in range(1, count):
+        pairs = [(place, (place + shift) % count) for place in range(count)]
+        total = total + lax.ppermute(partial, "heads", pairs)
+    return total
 
 
 def selector(places, total):
@@ -121,6 +142,8 @@
     qkv = qkv.reshape(steps_count, rows, groups, per_group + 2, HEAD_WIDTH)
     match = speaker[:, 0][:, None] == jnp.arange(speakers_all, dtype=jnp.int32)[None, :]
     slots = jnp.sum(jnp.where(match, speaker_adapter_slot[None, :], 0), axis=1)
+    lane = lax.axis_index(LANE_AXES)
+    slots = slots ^ (lane * replica_local_slots)
     places = slots * MOST + ranks_within(slots)
     pick = selector(places, send_slots)
     own_cols = lax.dynamic_slice_in_dim(
@@ -130,13 +153,13 @@
         jnp.bfloat16
     )
     outgoing = outgoing.reshape(lanes, replica_local_slots * MOST, steps_count, sliced_rows)
-    arrived = lax.all_to_all(outgoing, ("streams", "sub"), split_axis=0, concat_axis=0, tiled=True)
+    arrived = jnp.stack(exchange([outgoing[shift] for shift in range(lanes)]))
     items = arrived.shape[2]
     regrouped_rows = arrived.reshape(lanes, replica_local_slots, MOST, items, sliced_rows)
     partial_latent = jnp.einsum(
         "zqyhc,qcx->zqyhx", regrouped_rows, adapter_down_maps, preferred_element_type=jnp.float32
     )
-    adapter_latent = lax.psum(partial_latent, "heads").astype(jnp.bfloat16)
+    adapter_latent = summed_over_heads(partial_latent).astype(jnp.bfloat16)
     query_adapter_delta = jnp.einsum(
         "xrpzq,rqw->xrpzw",
         adapter_latent[..., :ADAPTER_RANK],
@@ -152,13 +175,8 @@
     joined = jnp.concatenate([query_adapter_delta, value_adapter_delta], axis=-1).astype(
         jnp.bfloat16
     )
-    returned = lax.all_to_all(
-        joined.reshape(lanes, replica_local_slots * MOST, items, delta_cols),
-        ("streams", "sub"),
-        split_axis=0,
-        concat_axis=0,
-        tiled=True,
-    )
+    joined = joined.reshape(lanes, replica_local_slots * MOST, items, delta_cols)
+    returned = jnp.stack(exchange([joined[shift] for shift in range(lanes)]))
     returned = returned.reshape(send_slots, steps_count, delta_cols)
     gathered = jnp.einsum("jr,jtc->trc", pick, returned, preferred_element_type=jnp.float32)
     angle = angles(cache_fill_length, steps_count, HEAD_WIDTH // 2)
@@ -181,15 +199,18 @@
         queries, new_keys, new_values, rotated_key_cache, value_cache_rows, cache_fill_length
     )
     fmost = max(2, (2 * rows + lanes - 1) // lanes)
-    owner = flow_decoder_owner[:, 0]
+    owner = flow_decoder_owner[:, 0] ^ lane
     flow_places = owner * fmost + ranks_within(owner)
     flow_pick = selector(flow_places, lanes * fmost)
     packed = jnp.einsum(
         "jr,trc->jtc", flow_pick, context, preferred_element_type=jnp.float32
     ).astype(jnp.bfloat16)
     packed = packed.reshape(lanes, fmost, steps_count, query_columns)
-    landed = lax.all_to_all(packed, ("streams", "sub"), split_axis=0, concat_axis=0, tiled=True)
-    return landed.reshape(1, lanes * fmost, steps_count, query_columns)
+    landed = exchange([packed[shift] for shift in range(lanes)])
+    flow = jnp.zeros((lanes * fmost, steps_count, query_columns), jnp.bfloat16)
+    for shift in range(lanes):
+        flow = lax.dynamic_update_slice_in_dim(flow, landed[shift], (lane ^ shift) * fmost, 0)
+    return flow[None]
 
 
 def solution(mesh):

time: 151 us -> 157 us (1.040)
  the two profiles are of different devices: /device:TPU:0 before, /device:TPU:11 now
where the time goes in v1:
time: 157 us; the launch traced here: 156 us
  waiting for transfers between devices  57.3 us (36%)
  local copies, waits for them, and re-layouts  35.1 us (22%)
  starting transfers between devices  25.1 us (16%)
  matrix products  20.9 us (13%)
  other arithmetic  17.3 us (11%)
    ppermute x21, waiting for transfers between devices, exchange(): landed.append(lax.ppermute(blocks[shift], LANE_AXES, pairs))  54.5 us
    ppermute x21, starting transfers between devices, exchange(): landed.append(lax.ppermute(blocks[shift], LANE_AXES, pairs))  24.7 us
    another operation x17, local copies, waits for them, and re-layouts, on_device(): arrived = jnp.stack(exchange([outgoing[shift] for shift in range(lanes)]))  17 us
    dot_general x1, matrix products, on_device(): jnp.dot(normed.reshape(steps_count * rows, width), projection_weight, pre...  9.63 us
    sub x1, matrix products, attend(): expo = jnp.exp(scores - peak)  4.53 us
    reshape x1, local copies, waits for them, and re-layouts, on_device(): qkv = qkv.reshape(steps_count, rows, groups, per_group + 2, HEAD_WIDTH)  4.22 us
  transfers between devices with their start and end apart: 22, of which 11 were waited for; matrix products, arithmetic and copies ran while one was open for 24% of the time, Pallas kernels for 0%

profile of v1, /device:TPU:11, one launch (start us, length us, event | category | flops | bytes accessed | tf_op | source)
XLA Modules:
  0.0 156.2 jit_solution(5529895909534582406)
XLA Ops:
  1.1 1.9 %fusion.1 = f32[4,64]{1,0:T(4,128)S(1)} fusion(bf16[4,64,3584]{2,1,0:T(8,128)(2,1)} %param.13), kind=kLoop, calls=%fused_computation.4 | loop fusion | flops 2752256 | bytes 1836032 | tf_op jit(solution)/shard_map/reduce_sum | solution.py:17
  3.1 2.0 %fusion.3 = bf16[4,64,3584]{2,1,0:T(8,128)(2,1)S(1)} fusion(bf16[4,64,3584]{2,1,0:T(8,128)(2,1)} %param.13, f32[3584]{0:T(1024)} %param.14, f32[4,64]{1,0:T(4,128)S(1)} %add_rsqrt_fusion), kind=kLoop, calls=%fused_computation.6 | loop fusion | flops 3670016 | bytes 3685376 | tf_op jit(solution)/shard_map/convert_element_type | solution.py:18
  6.6 1.5 collective-permute-start.2
  8.2 2.3 %collective-permute-start.3 = (bf16[8,4,1792]{2,0,1:T(8,128)(2,1)S(1)}, bf16[8,4,1792]{2,0,1:T(8,128)(2,1)}, u32[]{:S(2)}, u32[]{:S(2)}) collective-permute-start(bf16[8,4,1792]{2,0,1:T(8,128)(2,1)S(1)} %get-tuple-element.28), channel_id=1, source_target_pairs={{0,8},{1,9},{4,12},{5,13},{8,0},{9,1},{12,4},{13,5},{2,10},{3,11},... | collective-permute-start | bytes 344072 | tf_op jit(solution)/shard_map/ppermute | solution.py:90
  11.1 9.6 %convolution_add_fusion = f32[256,2304]{1,0:T(8,128)} fusion(bf16[256,3584]{1,0:T(8,128)(2,1)S(1)} %bitcast.138, bf16[3584,2304]{1,0:T(8,128)(2,1)} %param.15, f32[2304]{0:T(1024)S(1)} %copy-done.14), kind=kOutput, calls=%fused_computation.3 | convolution fusion | flops 4228448256 | bytes 20718592 | tf_op jit(solution)/shard_map/dot_general | solution.py:135
  20.7 4.2 %reshape.249 = f32[4,64,2,9,128]{4,3,2,1,0:T(8,128)} reshape(f32[256,2304]{1,0:T(8,128)} %convolution_add_fusion) | data formatting | bytes 4718592 | tf_op jit(solution)/shard_map/reshape | solution.py:142
  24.9 2.7 %fusion.66 = (f32[4,64,2,1,128]{4,3,2,1,0:T(1,128)S(1)}, f32[4,64,2,1,128]{4,3,2,1,0:T(1,128)S(1)}) fusion(f32[4,64,2,9,128]{4,3,2,1,0:T(8,128)} %reshape.249), kind=kLoop, calls=%fused_computation.133 | loop fusion | bytes 1048576 | tf_op jit(solution)/shard_map/slice | solution.py:192
  27.9 1.2 copy_bitcast_fusion
  29.1 1.2 copy_bitcast_fusion.1
  30.3 1.1 multiply_cosine_fusion
  32.9 1.3 collective-permute-start.5
  35.1 1.0 stack.51
  36.9 0.9 stack.52
  38.7 0.9 stack.53
  40.5 0.9 stack.54
  42.4 0.9 stack.55
  44.2 0.9 stack.56
  47.0 4.9 %stack.58 = bf16[8,4,2,4,1792]{4,0,3,2,1:T(8,128)(2,1)S(1)} concatenate(bf16[1,4,2,4,1792]{4,0,3,2,1:T(2,128)(2,1)S(1)} %copy.65, bf16[1,4,2,4,1792]{4,0,3,2,1:T(2,128)(2,1)} %copy.66, bf16[1,4,2,4,1792]{4,0,3,2,1:T(2,128)(2,1)} %copy.67, bf16[1,4,2,4,1792]{4,0,3,2,1:T(2,128)(2,1)} %copy.68, bf16[1,4,2,4,1792]{4,0,3,2,1:T(2,128)(2,1)} %copy.69, ...), dimensions={0} | concatenate | bytes 1835008 | tf_op jit(solution)/shard_map/stack | solution.py:156
  52.8 1.7 %maximum_bitcast_fusion.8 = bf16[64,4,2,128]{3,1,2,0:T(4,128)(2,1)} fusion(bf16[4,64,2,64]{3,0,2,1:T(4,128)(2,1)} %get-tuple-element.34, bf16[4,64,2,64]{3,0,2,1:T(4,128)(2,1)S(1)} %copy-done.7), kind=kLoop, calls=%fused_computation.86 | loop fusion | flops 262144 | bytes 262144 | tf_op jit(solution)/shard_map/transpose | solution.py:44
  54.6 2.8 %collective-permute-done.7 = f32[8,4,2,4,128]{4,0,3,2,1:T(8,128)S(1)} collective-permute-done((f32[8,4,2,4,128]{4,0,3,2,1:T(8,128)S(1)}, f32[8,4,2,4,128]{4,0,3,2,1:T(8,128)S(1)}, u32[]{:S(2)}, u32[]{:S(2)}) %collective-permute-start.7) | collective-permute-done | bytes 131104 | tf_op jit(solution)/shard_map/ppermute | solution.py:99
  57.4 1.6 %fusion.4 = bf16[8,4,2,4,1792]{4,0,3,2,1:T(8,128)(2,1)S(1)} fusion(bf16[4,64,1792]{2,1,0:T(8,128)(2,1)} %param.23, bf16[8,4,2,4,128]{4,0,3,2,1:T(8,128)(2,1)S(1)} %add_convert_fusion.2), kind=kOutput, calls=%fused_computation.18 | convolution fusion | flops 59179008 | bytes 1900544 | tf_op jit(solution)/shard_map/xrpzq,rqw->xrpzw/dot_general | solution.py:163
  59.2 2.8 %pad_maximum_fusion = (bf16[1,4,2,4,2048]{4,0,3,2,1:T(2,128)(2,1)S(1)}, bf16[1,4,2,4,2048]{4,0,3,2,1:T(2,128)(2,1)S(1)}, bf16[1,4,2,4,2048]{4,0,3,2,1:T(2,128)(2...) fusion(bf16[8,4,2,4,256]{4,0,3,2,1:T(8,128)(2,1)S(1)} %fusion.1, ...), kind=kLoop, calls=%fused_computation.67 | loop fusion | flops 2097152 | bytes 2097152 | tf_op jit(solution)/shard_map/concatenate | solution.py:175
  62.2 1.0 collective-permute-start.8
  63.3 2.0 %collective-permute-start.9 = (bf16[8,4,2048]{2,1,0:T(4,128)(2,1)S(1)}, bf16[8,4,2048]{2,1,0:T(4,128)(2,1)S(1)}, u32[]{:S(2)}, u32[]{:S(2)}) collective-permute-start(bf16[8,4,2048]{2,1,0:T(4,128)(2,1)S(1)} %bitcast.153), channel_id=1, source_target_pairs={{0,4},{1,5},{4,0},{5,1},{8,12},{9,13},{12,8},{13,9},{2,6},{3,7},{6... | collective-permute-start | bytes 393224 | tf_op jit(solution)/shard_map/ppermute | solution.py:90
  65.7 3.8 %collective-permute-start.11 = (bf16[8,4,2048]{2,1,0:T(4,128)(2,1)S(1)}, bf16[8,4,2048]{2,1,0:T(4,128)(2,1)S(1)}, u32[]{:S(2)}, u32[]{:S(2)}) collective-permute-start(bf16[8,4,2048]{2,1,0:T(4,128)(2,1)S(1)} %bitcast.151), channel_id=1, source_target_pairs={{0,8},{1,9},{4,12},{5,13},{8,0},{9,1},{12,4},{13,5},{2,10},{3,11},... | collective-permute-start | bytes 393224 | tf_op jit(solution)/shard_map/ppermute | solution.py:90
  70.1 1.5 collective-permute-start.13
  72.4 3.3 %collective-permute-done.10 = bf16[8,4,2048]{2,1,0:T(4,128)(2,1)S(1)} collective-permute-done((bf16[8,4,2048]{2,1,0:T(4,128)(2,1)S(1)}, bf16[8,4,2048]{2,1,0:T(4,128)(2,1)S(1)}, u32[]{:S(2)}, u32[]{:S(2)}) %collective-permute-start.10) | collective-permute-done | bytes 131104 | tf_op jit(solution)/shard_map/ppermute | solution.py:90
  75.8 7.7 %collective-permute-done.11 = bf16[8,4,2048]{2,1,0:T(4,128)(2,1)S(1)} collective-permute-done((bf16[8,4,2048]{2,1,0:T(4,128)(2,1)S(1)}, bf16[8,4,2048]{2,1,0:T(4,128)(2,1)S(1)}, u32[]{:S(2)}, u32[]{:S(2)}) %collective-permute-start.11) | collective-permute-done | bytes 131104 | tf_op jit(solution)/shard_map/ppermute | solution.py:90
  83.5 2.7 %collective-permute-done.12 = bf16[8,4,2048]{2,1,0:T(4,128)(2,1)S(1)} collective-permute-done((bf16[8,4,2048]{2,1,0:T(4,128)(2,1)S(1)}, bf16[8,4,2048]{2,1,0:T(4,128)(2,1)S(1)}, u32[]{:S(2)}, u32[]{:S(2)}) %collective-permute-start.12) | collective-permute-done | bytes 131104 | tf_op jit(solution)/shard_map/ppermute | solution.py:90
  86.3 3.1 %collective-permute-done.13 = bf16[8,4,2048]{2,1,0:T(4,128)(2,1)S(1)} collective-permute-done((bf16[8,4,2048]{2,1,0:T(4,128)(2,1)S(1)}, bf16[8,4,2048]{2,1,0:T(4,128)(2,1)S(1)}, u32[]{:S(2)}, u32[]{:S(2)}) %collective-permute-start.13) | collective-permute-done | bytes 131104 | tf_op jit(solution)/shard_map/ppermute | solution.py:90
  89.5 2.7 %collective-permute-done.14 = bf16[8,4,2048]{2,1,0:T(4,128)(2,1)S(1)} collective-permute-done((bf16[8,4,2048]{2,1,0:T(4,128)(2,1)S(1)}, bf16[8,4,2048]{2,1,0:T(4,128)(2,1)S(1)}, u32[]{:S(2)}, u32[]{:S(2)}) %collective-permute-start.14) | collective-permute-done | bytes 131104 | tf_op jit(solution)/shard_map/ppermute | solution.py:90
  93.3 1.2 copy-done.2
  94.5 1.9 %reshape.252 = f32[4,64,2,7,128]{4,3,2,1,0:T(8,128)} reshape(f32[4,64,1792]{2,1,0:T(8,128)S(1)} %slice.194) | data formatting | bytes 3670016 | tf_op jit(solution)/shard_map/reshape | solution.py:185
  96.5 2.5 %copy_add_fusion = f32[4,64,2,7,128]{4,3,0,2,1:T(8,128)S(1)} fusion(f32[4,64,2,7,128]{4,3,2,1,0:T(8,128)} %reshape.252, f32[4,64,2,9,128]{4,3,2,1,0:T(8,128)} %reshape.249), kind=kLoop, calls=%fused_computation.19 | loop fusion | flops 458752 | bytes 6029312 | tf_op jit(solution)/shard_map/add | solution.py:185
  99.0 1.9 %subtract_convert_fusion = (bf16[4,64,2,7,64]{4,3,0,2,1:T(8,128)(2,1)S(1)}, bf16[4,64,2,7,64]{4,3,0,2,1:T(8,128)(2,1)}) fusion(f32[4,64,2,7,128]{4,3,0,2,1:T(8,128)S(1)} %copy_add_fusion, f32[4,64,64]{2,0,1:T(4,128)S(1)} %get-tuple-element.36, f32[4,64,64]{2,0,1:T(4,128)S(1)} %get-tuple-element.35), kind=kLoop, calls=%fused_computation.24 | loop fusion | flops 1835008 | bytes 2883584 | tf_op jit(solution)/shard_map/convert.2
  101.4 4.5 %fusion.69 = (f32[64,2,4,7]{3,2,1,0:T(4,128)S(1)}, f32[64,2,4,7,36]{4,3,2,1,0:T(8,128)}) fusion(pred[64,4,36]{2,1,0:T(4,128)(4,1)S(1)} %copy-done.11, bf16[64,4,2,128]{3,1,2,0:T(4,128)(2,1)S(1)} %copy-done.8, bf16[64,32,2,128]{3,1,2,0:T(8,128)(2,1)} %copy_bitcast_fusion, bf16[4,64,2,7,64]{4,3,0,2,1:T(8,128)(2,1)} %get-tuple-element.8, ...), kind=kOutput, calls=%fused_computation.136 | convolution fusion | flops 37740580 | bytes 2636800 | tf_op jit(solution)/shard_map/sub | solution.py:67
  105.9 2.3 %fusion.8 = bf16[4,64,2,7,128]{4,3,0,2,1:T(8,128)(2,1)S(1)} fusion(bf16[64,4,2,128]{3,1,2,0:T(4,128)(2,1)S(1)} %fusion.42, bf16[64,32,2,128]{3,1,2,0:T(8,128)(2,1)S(1)} %copy-done.6, f32[64,2,4,7,36]{4,3,2,1,0:T(8,128)} %get-tuple-element.38, f32[64,2,4,7]{3,2,1,0:T(4,128)S(1)} %get-tuple-element.37), kind=kOutput, calls=%fused_computation.29 | convolution fusion | flops 36106240 | bytes 2627584 | tf_op jit(solution)/shard_map/rgtqc,rcgd->trgqd/dot_general | solution.py:69
  108.4 1.0 reshape.254
  111.1 1.7 %collective-permute-start.17 = (bf16[16,4,1792]{2,0,1:T(8,128)(2,1)S(1)}, bf16[16,4,1792]{2,0,1:T(8,128)(2,1)S(1)}, u32[]{:S(2)}, u32[]{:S(2)}) collective-permute-start(bf16[16,4,1792]{2,0,1:T(8,128)(2,1)S(1)} %get-tuple-element.13), channel_id=1, source_target_pairs={{0,5},{1,4},{4,1},{5,0},{8,13},{9,12},{12,9},{13,8},{2,7},{3,6},{6... | collective-permute-start | bytes 688136 | tf_op jit(solution)/shard_map/ppermute | solution.py:90
  112.8 1.4 collective-permute-start.18
  114.2 1.3 collective-permute-start.19
  116.2 1.6 %collective-permute-start.20 = (bf16[16,4,1792]{2,0,1:T(8,128)(2,1)S(1)}, bf16[16,4,1792]{2,0,1:T(8,128)(2,1)S(1)}, u32[]{:S(2)}, u32[]{:S(2)}) collective-permute-start(bf16[16,4,1792]{2,0,1:T(8,128)(2,1)S(1)} %get-tuple-element.10), channel_id=1, source_target_pairs={{0,12},{1,13},{4,8},{5,9},{8,4},{9,5},{12,0},{13,1},{2,14},{3,15},... | collective-permute-start | bytes 688136 | tf_op jit(solution)/shard_map/ppermute | solution.py:90
  117.9 7.2 %collective-permute-done.16 = bf16[16,4,1792]{2,0,1:T(8,128)(2,1)S(1)} collective-permute-done((bf16[16,4,1792]{2,0,1:T(8,128)(2,1)S(1)}, bf16[16,4,1792]{2,0,1:T(8,128)(2,1)S(1)}, u32[]{:S(2)}, u32[]{:S(2)}) %collective-permute-start.16) | collective-permute-done | bytes 229408 | tf_op jit(solution)/shard_map/ppermute | solution.py:90
  125.2 1.8 %collective-permute-start.21 = (bf16[16,4,1792]{2,0,1:T(8,128)(2,1)S(1)}, bf16[16,4,1792]{2,0,1:T(8,128)(2,1)S(1)}, u32[]{:S(2)}, u32[]{:S(2)}) collective-permute-start(bf16[16,4,1792]{2,0,1:T(8,128)(2,1)S(1)} %get-tuple-element.9), channel_id=1, source_target_pairs={{0,13},{1,12},{4,9},{5,8},{8,5},{9,4},{12,1},{13,0},{2,15},{3,14},... | collective-permute-start | bytes 688136 | tf_op jit(solution)/shard_map/ppermute | solution.py:90
  127.1 3.2 %collective-permute-done.17 = bf16[16,4,1792]{2,0,1:T(8,128)(2,1)S(1)} collective-permute-done((bf16[16,4,1792]{2,0,1:T(8,128)(2,1)S(1)}, bf16[16,4,1792]{2,0,1:T(8,128)(2,1)S(1)}, u32[]{:S(2)}, u32[]{:S(2)}) %collective-permute-start.17) | collective-permute-done | bytes 229408 | tf_op jit(solution)/shard_map/ppermute | solution.py:90
  130.5 13.0 %collective-permute-done.19 = bf16[16,4,1792]{2,0,1:T(8,128)(2,1)S(1)} collective-permute-done((bf16[16,4,1792]{2,0,1:T(8,128)(2,1)S(1)}, bf16[16,4,1792]{2,0,1:T(8,128)(2,1)S(1)}, u32[]{:S(2)}, u32[]{:S(2)}) %collective-permute-start.19) | collective-permute-done | bytes 229408 | tf_op jit(solution)/shard_map/ppermute | solution.py:90
  143.6 6.8 %collective-permute-done.20 = bf16[16,4,1792]{2,0,1:T(8,128)(2,1)S(1)} collective-permute-done((bf16[16,4,1792]{2,0,1:T(8,128)(2,1)S(1)}, bf16[16,4,1792]{2,0,1:T(8,128)(2,1)S(1)}, u32[]{:S(2)}, u32[]{:S(2)}) %collective-permute-start.20) | collective-permute-done | bytes 229408 | tf_op jit(solution)/shard_map/ppermute | solution.py:90
  150.6 4.8 %collective-permute-done.21 = bf16[16,4,1792]{2,0,1:T(8,128)(2,1)S(1)} collective-permute-done((bf16[16,4,1792]{2,0,1:T(8,128)(2,1)S(1)}, bf16[16,4,1792]{2,0,1:T(8,128)(2,1)S(1)}, u32[]{:S(2)}, u32[]{:S(2)}) %collective-permute-start.21) | collective-permute-done | bytes 229408 | tf_op jit(solution)/shard_map/ppermute | solution.py:90
  (117 shorter events, 21.0 us)
Async XLA Ops:
  0.0 51.9 %copy-start = (bf16[4,1792,128]{2,1,0:T(8,128)(2,1)S(1)}, bf16[4,1792,128]{2,1,0:T(8,128)(2,1)}, u32[]{:S(2)}) copy-start(bf16[4,1792,128]{2,1,0:T(8,128)(2,1)} %param.22) | copy-start | bytes 5505028
  5.1 5.8 %copy-start.12 = (s32[64]{0:T(128)S(1)}, s32[64]{0:T(128)}, u32[]{:S(2)}) copy-start(s32[64]{0:T(128)} %param.19) | copy-start | bytes 772
  5.1 6.0 %copy-start.14 = (f32[2304]{0:T(1024)S(1)}, f32[2304]{0:T(1024)}, u32[]{:S(2)}) copy-start(f32[2304]{0:T(1024)} %param.16) | copy-start | bytes 27652
  5.7 27.2 %collective-permute-start = (bf16[8,4,1792]{2,0,1:T(8,128)(2,1)S(1)}, bf16[8,4,1792]{2,0,1:T(8,128)(2,1)S(1)}, u32[]{:S(2)}, u32[]{:S(2)}) collective-permute-start(bf16[8,4,1792]{2,0,1:T(8,128)(2,1)S(1)} %get-tuple-element.31), channel_id=1, source_target_pairs={{0,1},{1,0},{4,5},{5,4},{8,9},{9,8},{12,13},{13,12},{2,3},{3,2},{6... | collective-permute-start | bytes 344072 | tf_op jit(solution)/shard_map/ppermute | solution.py:90
  6.5 27.8 %collective-permute-start.1 = (bf16[8,4,1792]{2,0,1:T(8,128)(2,1)S(1)}, bf16[8,4,1792]{2,0,1:T(8,128)(2,1)}, u32[]{:S(2)}, u32[]{:S(2)}) collective-permute-start(bf16[8,4,1792]{2,0,1:T(8,128)(2,1)S(1)} %get-tuple-element.30), channel_id=1, source_target_pairs={{0,4},{1,5},{4,0},{5,1},{8,12},{9,13},{12,8},{13,9},{2,6},{3,7},{6... | collective-permute-start | bytes 344072 | tf_op jit(solution)/shard_map/ppermute | solution.py:90
  6.6 32.1 %collective-permute-start.2 = (bf16[8,4,1792]{2,0,1:T(8,128)(2,1)S(1)}, bf16[8,4,1792]{2,0,1:T(8,128)(2,1)}, u32[]{:S(2)}, u32[]{:S(2)}) collective-permute-start(bf16[8,4,1792]{2,0,1:T(8,128)(2,1)S(1)} %get-tuple-element.29), channel_id=1, source_target_pairs={{0,5},{1,4},{4,1},{5,0},{8,13},{9,12},{12,9},{13,8},{2,7},{3,6},{6... | collective-permute-start | bytes 344072 | tf_op jit(solution)/shard_map/ppermute | solution.py:90
  8.2 32.4 %collective-permute-start.3 = (bf16[8,4,1792]{2,0,1:T(8,128)(2,1)S(1)}, bf16[8,4,1792]{2,0,1:T(8,128)(2,1)}, u32[]{:S(2)}, u32[]{:S(2)}) collective-permute-start(bf16[8,4,1792]{2,0,1:T(8,128)(2,1)S(1)} %get-tuple-element.28), channel_id=1, source_target_pairs={{0,8},{1,9},{4,12},{5,13},{8,0},{9,1},{12,4},{13,5},{2,10},{3,11},... | collective-permute-start | bytes 344072 | tf_op jit(solution)/shard_map/ppermute | solution.py:90
  10.5 31.9 %collective-permute-start.4 = (bf16[8,4,1792]{2,0,1:T(8,128)(2,1)S(1)}, bf16[8,4,1792]{2,0,1:T(8,128)(2,1)}, u32[]{:S(2)}, u32[]{:S(2)}) collective-permute-start(bf16[8,4,1792]{2,0,1:T(8,128)(2,1)S(1)} %get-tuple-element.27), channel_id=1, source_target_pairs={{0,9},{1,8},{4,13},{5,12},{8,1},{9,0},{12,5},{13,4},{2,11},{3,10},... | collective-permute-start | bytes 344072 | tf_op jit(solution)/shard_map/ppermute | solution.py:90
  24.9 2.9 %copy-start.4 = (bf16[64,32,256]{2,1,0:T(8,128)(2,1)S(1)}, bf16[64,32,256]{2,1,0:T(8,128)(2,1)}, u32[]{:S(2)}) copy-start(bf16[64,32,256]{2,1,0:T(8,128)(2,1)} %param.20) | copy-start | bytes 3145732
  24.9 4.2 %copy-start.5 = (bf16[64,32,256]{2,1,0:T(8,128)(2,1)S(1)}, bf16[64,32,256]{2,1,0:T(8,128)(2,1)}, u32[]{:S(2)}) copy-start(bf16[64,32,256]{2,1,0:T(8,128)(2,1)} %param.21) | copy-start | bytes 3145732
  29.1 5.6 %copy-start.13 = (s32[64,1]{0,1:T(1,128)S(1)}, s32[64,1]{0,1:T(1,128)}, u32[]{:S(2)}) copy-start(s32[64,1]{0,1:T(1,128)} %param.25) | copy-start | bytes 772
  32.9 1.7 %copy-start.10 = (bf16[8,4,1792]{2,0,1:T(8,128)(2,1)}, bf16[8,4,1792]{2,0,1:T(8,128)(2,1)S(1)}, u32[]{:S(2)}) copy-start(bf16[8,4,1792]{2,0,1:T(8,128)(2,1)S(1)} %collective-permute-done) | copy-start | bytes 344068
  32.9 11.2 %collective-permute-start.5 = (bf16[8,4,1792]{2,0,1:T(8,128)(2,1)S(1)}, bf16[8,4,1792]{2,0,1:T(8,128)(2,1)}, u32[]{:S(2)}, u32[]{:S(2)}) collective-permute-start(bf16[8,4,1792]{2,0,1:T(8,128)(2,1)S(1)} %get-tuple-element.26), channel_id=1, source_target_pairs={{0,12},{1,13},{4,8},{5,9},{8,4},{9,5},{12,0},{13,1},{2,14},{3,15},... | collective-permute-start | bytes 344072 | tf_op jit(solution)/shard_map/ppermute | solution.py:90
  34.3 11.8 %collective-permute-start.6 = (bf16[8,4,1792]{2,0,1:T(8,128)(2,1)S(1)}, bf16[8,4,1792]{2,0,1:T(8,128)(2,1)S(1)}, u32[]{:S(2)}, u32[]{:S(2)}) collective-permute-start(bf16[8,4,1792]{2,0,1:T(8,128)(2,1)S(1)} %get-tuple-element.25), channel_id=1, source_target_pairs={{0,13},{1,12},{4,9},{5,8},{8,5},{9,4},{12,1},{13,0},{2,15},{3,14},... | collective-permute-start | bytes 344072 | tf_op jit(solution)/shard_map/ppermute | solution.py:90
  51.9 0.9 copy-start.7
  52.4 6.6 %copy-start.9 = (bf16[4,64,256]{2,1,0:T(8,128)(2,1)S(1)}, bf16[4,64,256]{2,1,0:T(8,128)(2,1)}, u32[]{:S(2)}) copy-start(bf16[4,64,256]{2,1,0:T(8,128)(2,1)} %param.24) | copy-start | bytes 393220
  52.4 5.0 %collective-permute-start.7 = (f32[8,4,2,4,128]{4,0,3,2,1:T(8,128)S(1)}, f32[8,4,2,4,128]{4,0,3,2,1:T(8,128)S(1)}, u32[]{:S(2)}, u32[]{:S(2)}) collective-permute-start(f32[8,4,2,4,128]{4,0,3,2,1:T(8,128)S(1)} %fusion.14), channel_id=1, source_target_pairs={{0,2},{2,0},{1,3},{3,1},{4,6},{6,4},{5,7},{7,5},{8,10},{10,8},{9,1... | collective-permute-start | bytes 393224 | tf_op jit(solution)/shard_map/ppermute | solution.py:99
  62.2 7.8 %collective-permute-start.8 = (bf16[8,4,2048]{2,1,0:T(4,128)(2,1)S(1)}, bf16[8,4,2048]{2,1,0:T(4,128)(2,1)S(1)}, u32[]{:S(2)}, u32[]{:S(2)}) collective-permute-start(bf16[8,4,2048]{2,1,0:T(4,128)(2,1)S(1)} %bitcast.154), channel_id=1, source_target_pairs={{0,1},{1,0},{4,5},{5,4},{8,9},{9,8},{12,13},{13,12},{2,3},{3,2},{6... | collective-permute-start | bytes 393224 | tf_op jit(solution)/shard_map/ppermute | solution.py:90
  63.3 8.3 %collective-permute-start.9 = (bf16[8,4,2048]{2,1,0:T(4,128)(2,1)S(1)}, bf16[8,4,2048]{2,1,0:T(4,128)(2,1)S(1)}, u32[]{:S(2)}, u32[]{:S(2)}) collective-permute-start(bf16[8,4,2048]{2,1,0:T(4,128)(2,1)S(1)} %bitcast.153), channel_id=1, source_target_pairs={{0,4},{1,5},{4,0},{5,1},{8,12},{9,13},{12,8},{13,9},{2,6},{3,7},{6... | collective-permute-start | bytes 393224 | tf_op jit(solution)/shard_map/ppermute | solution.py:90
  65.5 10.2 %collective-permute-start.10 = (bf16[8,4,2048]{2,1,0:T(4,128)(2,1)S(1)}, bf16[8,4,2048]{2,1,0:T(4,128)(2,1)S(1)}, u32[]{:S(2)}, u32[]{:S(2)}) collective-permute-start(bf16[8,4,2048]{2,1,0:T(4,128)(2,1)S(1)} %bitcast.152), channel_id=1, source_target_pairs={{0,5},{1,4},{4,1},{5,0},{8,13},{9,12},{12,9},{13,8},{2,7},{3,6},{6... | collective-permute-start | bytes 393224 | tf_op jit(solution)/shard_map/ppermute | solution.py:90
  65.7 17.8 %collective-permute-start.11 = (bf16[8,4,2048]{2,1,0:T(4,128)(2,1)S(1)}, bf16[8,4,2048]{2,1,0:T(4,128)(2,1)S(1)}, u32[]{:S(2)}, u32[]{:S(2)}) collective-permute-start(bf16[8,4,2048]{2,1,0:T(4,128)(2,1)S(1)} %bitcast.151), channel_id=1, source_target_pairs={{0,8},{1,9},{4,12},{5,13},{8,0},{9,1},{12,4},{13,5},{2,10},{3,11},... | collective-permute-start | bytes 393224 | tf_op jit(solution)/shard_map/ppermute | solution.py:90
  69.6 16.7 %collective-permute-start.12 = (bf16[8,4,2048]{2,1,0:T(4,128)(2,1)S(1)}, bf16[8,4,2048]{2,1,0:T(4,128)(2,1)S(1)}, u32[]{:S(2)}, u32[]{:S(2)}) collective-permute-start(bf16[8,4,2048]{2,1,0:T(4,128)(2,1)S(1)} %bitcast.150), channel_id=1, source_target_pairs={{0,9},{1,8},{4,13},{5,12},{8,1},{9,0},{12,5},{13,4},{2,11},{3,10},... | collective-permute-start | bytes 393224 | tf_op jit(solution)/shard_map/ppermute | solution.py:90
  70.1 19.3 %collective-permute-start.13 = (bf16[8,4,2048]{2,1,0:T(4,128)(2,1)S(1)}, bf16[8,4,2048]{2,1,0:T(4,128)(2,1)S(1)}, u32[]{:S(2)}, u32[]{:S(2)}) collective-permute-start(bf16[8,4,2048]{2,1,0:T(4,128)(2,1)S(1)} %bitcast.149), channel_id=1, source_target_pairs={{0,12},{1,13},{4,8},{5,9},{8,4},{9,5},{12,0},{13,1},{2,14},{3,15},... | collective-permute-start | bytes 393224 | tf_op jit(solution)/shard_map/ppermute | solution.py:90
  71.7 20.5 %collective-permute-start.14 = (bf16[8,4,2048]{2,1,0:T(4,128)(2,1)S(1)}, bf16[8,4,2048]{2,1,0:T(4,128)(2,1)S(1)}, u32[]{:S(2)}, u32[]{:S(2)}) collective-permute-start(bf16[8,4,2048]{2,1,0:T(4,128)(2,1)S(1)} %bitcast.148), channel_id=1, source_target_pairs={{0,13},{1,12},{4,9},{5,8},{8,5},{9,4},{12,1},{13,0},{2,15},{3,14},... | collective-permute-start | bytes 393224 | tf_op jit(solution)/shard_map/ppermute | solution.py:90
  93.2 1.4 copy-start.2
  99.0 1.9 %slice-start = ((f32[4,64,2048]{2,1,0:T(8,128)}), f32[4,64,256]{2,1,0:T(8,128)S(1)}, s32[]{:S(2)}) async-start(f32[4,64,2048]{2,1,0:T(8,128)} %copy-done.2), calls=%async_computation | async-start | bytes 524288 | tf_op jit(solution)/shard_map/slice | solution.py:196
  99.0 2.3 %copy-start.8 = (bf16[64,4,2,128]{3,1,2,0:T(4,128)(2,1)S(1)}, bf16[64,4,2,128]{3,1,2,0:T(4,128)(2,1)}, u32[]{:S(2)}) copy-start(bf16[64,4,2,128]{3,1,2,0:T(4,128)(2,1)} %maximum_bitcast_fusion.8) | copy-start | bytes 393220
  99.0 2.3 %copy-start.11 = (pred[64,4,36]{2,1,0:T(4,128)(4,1)S(1)}, pred[64,4,36]{2,1,0:T(4,128)(4,1)}, u32[]{:S(2)}) copy-start(pred[64,4,36]{2,1,0:T(4,128)(4,1)} %broadcast_select_fusion) | copy-start | bytes 27652
  101.4 4.5 %copy-start.6 = (bf16[64,32,2,128]{3,1,2,0:T(8,128)(2,1)S(1)}, bf16[64,32,2,128]{3,1,2,0:T(8,128)(2,1)}, u32[]{:S(2)}) copy-start(bf16[64,32,2,128]{3,1,2,0:T(8,128)(2,1)} %copy_bitcast_fusion.1) | copy-start | bytes 3145732
  110.4 5.8 %collective-permute-start.15 = (bf16[16,4,1792]{2,0,1:T(8,128)(2,1)S(1)}, bf16[16,4,1792]{2,0,1:T(8,128)(2,1)S(1)}, u32[]{:S(2)}, u32[]{:S(2)}) collective-permute-start(bf16[16,4,1792]{2,0,1:T(8,128)(2,1)S(1)} %get-tuple-element.15), channel_id=1, source_target_pairs={{0,1},{1,0},{4,5},{5,4},{8,9},{9,8},{12,13},{13,12},{2,3},{3,2},{6... | collective-permute-start | bytes 688136 | tf_op jit(solution)/shard_map/ppermute | solution.py:90
  111.1 14.0 %collective-permute-start.16 = (bf16[16,4,1792]{2,0,1:T(8,128)(2,1)S(1)}, bf16[16,4,1792]{2,0,1:T(8,128)(2,1)S(1)}, u32[]{:S(2)}, u32[]{:S(2)}) collective-permute-start(bf16[16,4,1792]{2,0,1:T(8,128)(2,1)S(1)} %get-tuple-element.14), channel_id=1, source_target_pairs={{0,4},{1,5},{4,0},{5,1},{8,12},{9,13},{12,8},{13,9},{2,6},{3,7},{6... | collective-permute-start | bytes 688136 | tf_op jit(solution)/shard_map/ppermute | solution.py:90
  111.1 19.1 %collective-permute-start.17 = (bf16[16,4,1792]{2,0,1:T(8,128)(2,1)S(1)}, bf16[16,4,1792]{2,0,1:T(8,128)(2,1)S(1)}, u32[]{:S(2)}, u32[]{:S(2)}) collective-permute-start(bf16[16,4,1792]{2,0,1:T(8,128)(2,1)S(1)} %get-tuple-element.13), channel_id=1, source_target_pairs={{0,5},{1,4},{4,1},{5,0},{8,13},{9,12},{12,9},{13,8},{2,7},{3,6},{6... | collective-permute-start | bytes 688136 | tf_op jit(solution)/shard_map/ppermute | solution.py:90
  112.8 17.5 %collective-permute-start.18 = (bf16[16,4,1792]{2,0,1:T(8,128)(2,1)S(1)}, bf16[16,4,1792]{2,0,1:T(8,128)(2,1)S(1)}, u32[]{:S(2)}, u32[]{:S(2)}) collective-permute-start(bf16[16,4,1792]{2,0,1:T(8,128)(2,1)S(1)} %get-tuple-element.12), channel_id=1, source_target_pairs={{0,8},{1,9},{4,12},{5,13},{8,0},{9,1},{12,4},{13,5},{2,10},{3,11},... | collective-permute-start | bytes 688136 | tf_op jit(solution)/shard_map/ppermute | solution.py:90
  114.2 29.2 %collective-permute-start.19 = (bf16[16,4,1792]{2,0,1:T(8,128)(2,1)S(1)}, bf16[16,4,1792]{2,0,1:T(8,128)(2,1)S(1)}, u32[]{:S(2)}, u32[]{:S(2)}) collective-permute-start(bf16[16,4,1792]{2,0,1:T(8,128)(2,1)S(1)} %get-tuple-element.11), channel_id=1, source_target_pairs={{0,9},{1,8},{4,13},{5,12},{8,1},{9,0},{12,5},{13,4},{2,11},{3,10},... | collective-permute-start | bytes 688136 | tf_op jit(solution)/shard_map/ppermute | solution.py:90
  115.5 40.6 %copy-start.1 = (bf16[4,1792,128]{2,1,0:T(8,128)(2,1)S(1)}, bf16[4,1792,128]{2,1,0:T(8,128)(2,1)}, u32[]{:S(2)}) copy-start(bf16[4,1792,128]{2,1,0:T(8,128)(2,1)} %param.22) | copy-start | bytes 5505028
  116.2 34.3 %collective-permute-start.20 = (bf16[16,4,1792]{2,0,1:T(8,128)(2,1)S(1)}, bf16[16,4,1792]{2,0,1:T(8,128)(2,1)S(1)}, u32[]{:S(2)}, u32[]{:S(2)}) collective-permute-start(bf16[16,4,1792]{2,0,1:T(8,128)(2,1)S(1)} %get-tuple-element.10), channel_id=1, source_target_pairs={{0,12},{1,13},{4,8},{5,9},{8,4},{9,5},{12,0},{13,1},{2,14},{3,15},... | collective-permute-start | bytes 688136 | tf_op jit(solution)/shard_map/ppermute | solution.py:90
  125.2 30.2 %collective-permute-start.21 = (bf16[16,4,1792]{2,0,1:T(8,128)(2,1)S(1)}, bf16[16,4,1792]{2,0,1:T(8,128)(2,1)S(1)}, u32[]{:S(2)}, u32[]{:S(2)}) collective-permute-start(bf16[16,4,1792]{2,0,1:T(8,128)(2,1)S(1)} %get-tuple-element.9), channel_id=1, source_target_pairs={{0,13},{1,12},{4,9},{5,8},{8,5},{9,4},{12,1},{13,0},{2,15},{3,14},... | collective-permute-start | bytes 688136 | tf_op jit(solution)/shard_map/ppermute | solution.py:90
  150.6 4.8 %copy-start.3 = (bf16[1,128,4,1792]{3,2,1,0:T(4,128)(2,1)}, bf16[1,128,4,1792]{3,2,1,0:T(4,128)(2,1)S(1)}, u32[]{:S(2)}) copy-start(bf16[1,128,4,1792]{3,2,1,0:T(4,128)(2,1)S(1)} %copy_dynamic-update-slice_fusion.1) | copy-start | bytes 5505028

commit v2 on v0

v2 whole, which is shorter than its diff:
```python
import functools
import math

import jax
import jax.numpy as jnp
from jax import lax
from jax.experimental import pallas as pl
from jax.experimental.pallas import tpu as pltpu
from jax.sharding import PartitionSpec as P

QUERY_HEADS = 28
KEY_VALUE_HEADS = 4
HEAD_WIDTH = 128
ADAPTER_RANK = 64
MOST = 2
PER_GROUP = QUERY_HEADS // KEY_VALUE_HEADS
LANE_AXES = ("streams", "sub")
BATCH = 8
VMEM = pl.BlockSpec(memory_space=pltpu.VMEM)
MIB = 1 << 20


def iota(shape, dim):
    return lax.broadcasted_iota(jnp.int32, shape, dim)


def as_column(row):
    count = row.shape[1]
    square = (count, count)
    same = iota(square, 0) == iota(square, 1)
    return jnp.sum(jnp.where(same, jnp.broadcast_to(row, square), 0), axis=1, keepdims=True)


def ranked(labels, most):
    count = labels.shape[1]
    square = (count, count)
    earlier = (as_column(labels) == labels) & (iota(square, 0) < iota(square, 1))
    return labels * most + jnp.sum(earlier.astype(jnp.int32), axis=0, keepdims=True)


def slot_places(speaker, table, lane_base):
    speakers_all = table.shape[1]
    rows = speaker.shape[1]
    match = iota((speakers_all, rows), 0) == speaker
    slots = jnp.sum(jnp.where(match, as_column(table), 0), axis=0, keepdims=True)
    return ranked(slots ^ lane_base, MOST)


def lane_index():
    return lax.axis_index("streams") * lax.axis_size("sub") + lax.axis_index("sub")


def pack_kernel(steps, rows, local_slots, aliased, *refs):
    speaker_ref, table_ref, gain_ref, x_ref = refs[:4]
    normed_ref = refs[4 + aliased]
    message_refs = refs[5 + aliased :]
    width = x_ref.shape[1]
    sliced = message_refs[0].shape[1]
    per_message = message_refs[0].shape[0]
    spots = per_message // steps

    def one(index, carry):
        span = pl.ds(pl.multiple_of(index * 16, 16), 16)
        values = x_ref[span, :].astype(jnp.float32)
        mean_sq = jnp.sum(values * values, axis=1, keepdims=True) * (1.0 / width)
        normed = values * lax.rsqrt(mean_sq + 1e-06) * gain_ref[...]
        normed_ref[span, :] = normed.astype(jnp.bfloat16)
        return carry

    lax.fori_loop(0, steps * rows // 16, one, 0)
    places = slot_places(speaker_ref[...], table_ref[...], lane_index() * local_slots)
    total = len(message_refs) * per_message
    shape = (total, steps * rows)
    out_row = iota(shape, 0)
    wanted = out_row // per_message * spots + out_row % spots
    out_step = out_row % per_message // spots
    places = jnp.concatenate([places] * steps, axis=1)
    pick = (wanted == places) & (out_step == iota(shape, 1) // rows)
    pick = pick.astype(jnp.float32).astype(jnp.bfloat16)
    begin = pl.multiple_of(lax.axis_index("heads") * sliced, 128)
    own = normed_ref[:, pl.ds(begin, sliced)]
    packed = jnp.dot(pick, own, preferred_element_type=jnp.float32).astype(jnp.bfloat16)
    for number, message_ref in enumerate(message_refs):
        message_ref[...] = packed[number * per_message : (number + 1) * per_message]


def row_slots(shape, spots):
    return iota(shape, 0) % spots // MOST


def down_kernel(lanes, spots, *refs):
    message_refs, map_refs, partial_ref = refs[:lanes], refs[lanes:-1], refs[-1]
    rows = jnp.concatenate([ref[...] for ref in message_refs], axis=0)
    local_slots = map_refs[0].shape[0]
    own_slot = row_slots(partial_ref.shape, spots)
    total = jnp.zeros(partial_ref.shape, jnp.float32)
    for number, map_ref in enumerate(map_refs):
        for slot in range(local_slots):
            part = jnp.dot(rows, map_ref[slot], preferred_element_type=jnp.float32)
            total = jnp.where(own_slot == number * local_slots + slot, part, total)
    partial_ref[...] = total


def up_kernel(heads, subs, spots, groups, split, *refs):
    partial_refs = refs[:heads]
    query_refs = refs[heads : heads + subs]
    value_refs = refs[heads + subs : heads + 2 * subs]
    message_refs = refs[heads + 2 * subs :]
    total = partial_refs[0][...]
    for ref in partial_refs[1:]:
        total = total + ref[...]
    latent = total.astype(jnp.bfloat16).astype(jnp.float32)
    own_slot = row_slots(latent.shape, spots)
    column = iota(latent.shape, 1) // ADAPTER_RANK
    local = query_refs[0].shape[0]
    turned = pltpu.roll(latent, ADAPTER_RANK, 1)
    low = iota(latent.shape, 1) < ADAPTER_RANK
    query_pair = jnp.where(low, latent, turned)
    value_pair = jnp.where(low, turned, latent)

    def expanded(pair, number):
        pieces = []
        for block in range(local // latent.shape[1]):
            slot = number * (local // ADAPTER_RANK) + block * 2
            kept = jnp.where(own_slot == slot + column, pair, 0.0)
            pieces.append(kept.astype(jnp.bfloat16))
        return jnp.concatenate(pieces, axis=1)

    def product(pair, map_refs):
        result = None
        for number, ref in enumerate(map_refs):
            part = jnp.dot(
                expanded(pair, number), ref[...], preferred_element_type=jnp.float32
            )
            result = part if result is None else result + part
        return result.astype(jnp.bfloat16)

    queries = product(query_pair, query_refs)
    values = product(value_pair, value_refs)
    query_width = queries.shape[1] // groups
    value_width = values.shape[1] // groups
    block_width = query_width + value_width
    per_message = message_refs[0].shape[0]
    lanes = latent.shape[0] // per_message
    for lane in range(lanes):
        span = slice(lane * per_message, (lane + 1) * per_message)
        for group in range(groups):
            ref = message_refs[group * lanes + lane] if split else message_refs[lane]
            begin = 0 if split else group * block_width
            ref[:, begin : begin + query_width] = queries[
                span, group * query_width : (group + 1) * query_width
            ]
            ref[:, begin + query_width : begin + block_width] = values[
                span, group * value_width : (group + 1) * value_width
            ]


def attend_kernel(steps, rows, cache, lanes, flow_lanes, chunks, local_slots, *refs):
    speaker_ref, table_ref, owner_ref, length_ref = refs[:4]
    cos_ref, sin_ref, qkv_ref, key_ref, value_ref = refs[4:9]
    delta_refs = refs[9 : 9 + chunks * lanes]
    message_refs = refs[9 + chunks * lanes : 9 + chunks * lanes + flow_lanes]
    delta_ref, context_ref, bias_ref = refs[9 + chunks * lanes + flow_lanes :]
    chunk_steps = steps // chunks
    per_message = delta_refs[0].shape[0]
    spots = per_message // chunk_steps
    query_width = PER_GROUP * HEAD_WIDTH
    lane = lane_index()

    places = slot_places(speaker_ref[...], table_ref[...], lane * local_slots)
    column = as_column(places)
    column = jnp.concatenate([column] * chunk_steps, axis=0)
    shape = (chunk_steps * rows, lanes * per_message)
    out_row = iota(shape, 1)
    wanted = out_row // per_message * spots + out_row % spots
    pick = (wanted == column) & (out_row % per_message // spots == iota(shape, 0) // rows)
    pick = pick.astype(jnp.float32).astype(jnp.bfloat16)
    for chunk in range(chunks):
        block = [ref[...] for ref in delta_refs[chunk * lanes : (chunk + 1) * lanes]]
        begin = chunk * chunk_steps * rows
        delta_ref[begin : begin + chunk_steps * rows, :] = jnp.dot(
            pick, jnp.concatenate(block, axis=0), preferred_element_type=jnp.float32
        )

    wide = (rows, BATCH * cache)
    lengths = as_column(length_ref[...])
    slot_column = iota(wide, 1)
    allowed = (slot_column // cache == iota(wide, 0) % BATCH) & (slot_column % cache < lengths)
    bias_ref[...] = jnp.where(allowed, 0.0, -1e30)
    fresh = (steps, BATCH, steps * BATCH)
    fresh_column = iota(fresh, 2)
    fresh_allowed = (fresh_column % BATCH == iota(fresh, 1)) & (
        fresh_column // BATCH <= iota(fresh, 0)
    )
    fresh_bias = jnp.where(fresh_allowed, 0.0, -1e30)
    scale = HEAD_WIDTH ** (-0.5)
    transposed = (((1,), (1,)), ((), ()))

    def batch(index, carry):
        first = pl.multiple_of(index * BATCH, BATCH)
        query_tiles, key_tiles, value_tiles = [], [], []
        for step in range(steps):
            span = pl.ds(pl.multiple_of(step * rows + first, BATCH), BATCH)
            cosine, sine_part = cos_ref[span, :], sin_ref[span, :]

            def rotated(values):
                return values * cosine + pltpu.roll(values, HEAD_WIDTH // 2, 1) * sine_part

            for head in range(PER_GROUP):
                place = slice(head * HEAD_WIDTH, (head + 1) * HEAD_WIDTH)
                query_tiles.append(rotated(qkv_ref[span, place] + delta_ref[span, place]))
            key_place = slice(query_width, query_width + HEAD_WIDTH)
            value_place = slice(query_width + HEAD_WIDTH, query_width + 2 * HEAD_WIDTH)
            key_tiles.append(rotated(qkv_ref[span, key_place]))
            value_tiles.append(qkv_ref[span, value_place] + delta_ref[span, key_place])
        queries = jnp.concatenate(query_tiles, axis=0).astype(jnp.bfloat16)
        new_keys = jnp.concatenate(key_tiles, axis=0).astype(jnp.bfloat16)
        new_values = jnp.concatenate(value_tiles, axis=0).astype(jnp.bfloat16)
        old_keys = key_ref[pl.ds(first, BATCH)].reshape(BATCH * cache, HEAD_WIDTH)
        old_values = value_ref[pl.ds(first, BATCH)].reshape(BATCH * cache, HEAD_WIDTH)
        old_scores = lax.dot_general(
            queries, old_keys, transposed, preferred_element_type=jnp.float32
        )
        new_scores = lax.dot_general(
            queries, new_keys, transposed, preferred_element_type=jnp.float32
        )
        heads = steps * PER_GROUP
        old_scores = (old_scores * scale).reshape(heads, BATCH, BATCH * cache) + bias_ref[
            pl.ds(first, BATCH), :
        ][None]
        new_scores = (new_scores * scale).reshape(
            steps, PER_GROUP, BATCH, steps * BATCH
        ) + fresh_bias[:, None]
        new_scores = new_scores.reshape(heads, BATCH, steps * BATCH)
        peak = jnp.maximum(
            jnp.max(old_scores, axis=-1, keepdims=True), jnp.max(new_scores, axis=-1, keepdims=True)
        )
        old_scores = jnp.exp(old_scores - peak)
        new_scores = jnp.exp(new_scores - peak)
        share = 1.0 / (
            jnp.sum(old_scores, axis=-1, keepdims=True)
            + jnp.sum(new_scores, axis=-1, keepdims=True)
        )
        old_weights = (old_scores * share).reshape(heads * BATCH, BATCH * cache)
        new_weights = (new_scores * share).reshape(heads * BATCH, steps * BATCH)
        context = jnp.dot(
            old_weights.astype(jnp.bfloat16), old_values, preferred_element_type=jnp.float32
        ) + jnp.dot(
            new_weights.astype(jnp.bfloat16), new_values, preferred_element_type=jnp.float32
        )
        for step in range(steps):
            span = pl.ds(pl.multiple_of(step * rows + first, BATCH), BATCH)
            for head in range(PER_GROUP):
                begin = (step * PER_GROUP + head) * BATCH
                context_ref[span, head * HEAD_WIDTH : (head + 1) * HEAD_WIDTH] = context[
                    begin : begin + BATCH
                ]
        return carry

    lax.fori_loop(0, rows // BATCH, batch, 0)

    most = message_refs[0].shape[0]
    flow_places = ranked(owner_ref[...] ^ lane, most)
    flow_places = jnp.concatenate([flow_places] * steps, axis=1)
    context = context_ref[...].astype(jnp.bfloat16)
    shape = (most * steps, steps * rows)
    out_row = iota(shape, 0)
    same_step = out_row % steps == iota(shape, 1) // rows
    for number, message_ref in enumerate(message_refs):
        pick = (flow_places == number * most + out_row // steps) & same_step
        packed = jnp.dot(
            pick.astype(jnp.float32).astype(jnp.bfloat16),
            context,
            preferred_element_type=jnp.float32,
        )
        message_ref[...] = packed.reshape(most, steps, query_width).astype(jnp.bfloat16)


def place_kernel(flow_lanes, groups, *refs):
    block_refs, out_ref, semaphore = refs[:-2], refs[-2], refs[-1]
    lane = lane_index()
    most, _, width = block_refs[0].shape
    copies = []
    for group in range(groups):
        for number in range(flow_lanes):
            copy = pltpu.make_async_copy(
                block_refs[group * flow_lanes + number],
                out_ref.at[
                    pl.ds((lane ^ number) * most, most), :, pl.ds(group * width, width)
                ],
                semaphore.at[group * flow_lanes + number],
            )
            copy.start()
            copies.append(copy)
    for copy in copies:
        copy.wait()


def traded(blocks, axes):
    landed = list(blocks)
    count = len(blocks)
    order = sorted(range(1, count), key=lambda shift: -(shift ^ (shift >> 1)))
    for shift in order:
        pairs = [(place, place ^ shift) for place in range(count)]
        landed[shift] = lax.ppermute(blocks[shift], axes, pairs)
    return landed


def from_others(block, axis):
    count = lax.axis_size(axis)
    landed = [block]
    for shift in range(1, count):
        pairs = [(place, place ^ shift) for place in range(count)]
        landed.append(lax.ppermute(block, axis, pairs))
    return landed


def cost(flops, size):
    return pl.CostEstimate(flops=int(flops), bytes_accessed=int(size), transcendentals=0)


def on_device(
    inputs,
    input_norm_gain,
    projection_weight,
    projection_bias,
    speaker,
    speaker_adapter_slot,
    cache_fill_length,
    rotated_key_cache,
    value_cache_rows,
    adapter_down_maps,
    adapter_query_up,
    adapter_value_up,
    flow_decoder_owner,
):
    steps, rows, width = inputs.shape
    lanes = lax.axis_size("streams")
    subs = lax.axis_size("sub")
    heads = lax.axis_size("heads")
    flow_lanes = lanes * subs
    local_slots, sliced, _ = adapter_down_maps.shape
    query_columns = adapter_query_up.shape[2]
    value_columns = adapter_value_up.shape[2]
    groups = value_columns // HEAD_WIDTH
    cache = rotated_key_cache.shape[1]
    spots = subs * local_slots * MOST
    chunks = 2
    chunk_steps = steps // chunks
    chunk_rows = chunk_steps * rows
    per_message = chunk_steps * spots
    bf16, f32 = jnp.bfloat16, jnp.float32

    down_maps = from_others(adapter_down_maps, "sub")
    query_maps = from_others(
        adapter_query_up.reshape(local_slots * ADAPTER_RANK, query_columns), "sub"
    )
    value_maps = from_others(
        adapter_value_up.reshape(local_slots * ADAPTER_RANK, value_columns), "sub"
    )

    speaker_row = speaker.reshape(1, rows)
    table_row = speaker_adapter_slot.reshape(1, -1)
    owner_row = flow_decoder_owner.reshape(1, rows)
    length_row = cache_fill_length.reshape(1, rows)
    flat = inputs.reshape(steps * rows, width)
    gain = input_norm_gain.reshape(1, width)

    normed = None
    arrived = []
    for chunk in range(chunks):
        aliased = int(chunk > 0)
        operands = [speaker_row, table_row, gain, flat] + ([normed] if aliased else [])
        whole = lambda shape: pl.BlockSpec(shape, lambda i: (0,) * len(shape))
        half = pl.BlockSpec((chunk_rows, width), lambda i, chunk=chunk: (chunk, 0))
        message = jax.ShapeDtypeStruct((per_message, sliced), bf16)
        normed, *messages = pl.pallas_call(
            functools.partial(pack_kernel, chunk_steps, rows, local_slots, aliased),
            grid=(1,),
            in_specs=[whole(speaker_row.shape), whole(table_row.shape), whole(gain.shape), half]
            + [pl.BlockSpec(memory_space=pl.ANY)] * aliased,
            out_specs=[half] + [whole(message.shape)] * lanes,
            out_shape=[jax.ShapeDtypeStruct((steps * rows, width), bf16)] + [message] * lanes,
            input_output_aliases={4: 0} if aliased else {},
            compiler_params=pltpu.CompilerParams(vmem_limit_bytes=16 * MIB),
            cost_estimate=cost(2 * lanes * per_message * chunk_rows * sliced, 3 * MIB),
            name="norm_and_pack",
        )(*operands)
        arrived.append(traded(messages, "streams"))

    qkv = jnp.dot(normed, projection_weight, preferred_element_type=f32) + projection_bias

    half_width = HEAD_WIDTH // 2
    position = (
        cache_fill_length[None, :] + jnp.arange(steps, dtype=jnp.int32)[:, None]
    ).astype(f32)
    freq = jnp.exp(jnp.arange(half_width, dtype=f32) * (-math.log(1000000.0) / half_width))
    freq = jnp.concatenate([freq, freq])
    angle = position.reshape(steps * rows, 1) * freq
    sign = jnp.where(jnp.arange(HEAD_WIDTH) < half_width, -1.0, 1.0).astype(f32)
    cosine = jnp.cos(angle)
    sine_part = jnp.sin(angle) * sign

    block_width = (PER_GROUP + 1) * HEAD_WIDTH
    returned = []
    for chunk in range(chunks):
        latent = jax.ShapeDtypeStruct((lanes * per_message, 2 * ADAPTER_RANK), f32)
        partial_latent = pl.pallas_call(
            functools.partial(down_kernel, lanes, spots),
            in_specs=[VMEM] * (lanes + subs),
            out_specs=VMEM,
            out_shape=latent,
            compiler_params=pltpu.CompilerParams(vmem_limit_bytes=16 * MIB),
            cost_estimate=cost(
                2 * lanes * per_message * sliced * 128 * subs * local_slots, 4 * MIB
            ),
            name="down",
        )(*arrived[chunk], *down_maps)
        partials = from_others(partial_latent, "heads")
        split = chunk == chunks - 1
        shape = (per_message, block_width if split else groups * block_width)
        message = jax.ShapeDtypeStruct(shape, bf16)
        count = lanes * groups if split else lanes
        messages = pl.pallas_call(
            functools.partial(up_kernel, heads, subs, spots, groups, split),
            in_specs=[VMEM] * (heads + 2 * subs),
            out_specs=[VMEM] * count,
            out_shape=[message] * count,
            compiler_params=pltpu.CompilerParams(vmem_limit_bytes=24 * MIB),
            cost_estimate=cost(
                2 * lanes * per_message * subs * local_slots * 64 * groups * block_width, 3 * MIB
            ),
            name="up",
        )(*partials, *query_maps, *value_maps)
        if split:
            returned.append(
                [
                    traded(messages[group * lanes : (group + 1) * lanes], "streams")
                    for group in range(groups)
                ]
            )
        else:
            returned.append(traded(messages, "streams"))

    flow_most = max(2, (2 * rows + flow_lanes - 1) // flow_lanes)
    query_width = PER_GROUP * HEAD_WIDTH
    landed = []
    for group in range(groups):
        whole = lambda shape: pl.BlockSpec(shape, lambda i: (0,) * len(shape))
        message = jax.ShapeDtypeStruct((flow_most, steps, query_width), bf16)
        column = lambda shape: pl.BlockSpec(shape, lambda i, group=group: (0, group))
        layer = pl.BlockSpec((rows, cache, HEAD_WIDTH), lambda i, group=group: (0, 0, group))
        messages = pl.pallas_call(
            functools.partial(
                attend_kernel, steps, rows, cache, lanes, flow_lanes, chunks, local_slots
            ),
            grid=(1,),
            in_specs=[whole((1, rows)), whole(table_row.shape), whole((1, rows)), whole((1, rows))]
            + [whole(cosine.shape)] * 2
            + [column((steps * rows, (PER_GROUP + 2) * HEAD_WIDTH)), layer, layer]
            + [column((per_message, block_width))] * (lanes * (chunks - 1))
            + [whole((per_message, block_width))] * lanes,
            out_specs=[whole(message.shape)] * flow_lanes,
            out_shape=[message] * flow_lanes,
            scratch_shapes=[
                pltpu.VMEM((steps * rows, block_width), f32),
                pltpu.VMEM((steps * rows, query_width), f32),
                pltpu.VMEM((rows, BATCH * cache), f32),
            ],
            compiler_params=pltpu.CompilerParams(vmem_limit_bytes=24 * MIB),
            cost_estimate=cost(2e9, 4 * MIB),
            name="attend",
        )(
            speaker_row,
            table_row,
            owner_row,
            length_row,
            cosine,
            sine_part,
            qkv,
            rotated_key_cache,
            value_cache_rows,
            *[block for chunk in returned[:-1] for block in chunk],
            *returned[-1][group],
        )
        landed += traded(messages, LANE_AXES)

    flow = pl.pallas_call(
        functools.partial(place_kernel, flow_lanes, groups),
        in_specs=[pl.BlockSpec(memory_space=pl.ANY)] * len(landed),
        out_specs=pl.BlockSpec(memory_space=pl.ANY),
        out_shape=jax.ShapeDtypeStruct((flow_lanes * flow_most, steps, query_columns), bf16),
        scratch_shapes=[pltpu.SemaphoreType.DMA((len(landed),))],
        cost_estimate=cost(0, 4 * MIB),
        name="place",
    )(*landed)
    return flow[None]


def solution(mesh):
    placed = (
        P(None, ("groups", "streams", "sub"), None),
        P(),
        P(None, "heads"),
        P("heads"),
        P(("groups", "streams", "sub"), None),
        P("groups"),
        P(("groups", "streams", "sub")),
        P(("groups", "streams", "sub"), None, "heads"),
        P(("groups", "streams", "sub"), None, "heads"),
        P(("groups", "streams", "sub"), "heads", None),
        P(("groups", "streams", "sub"), None, "heads"),
        P(("groups", "streams", "sub"), None, "heads"),
        P(("groups", "streams", "sub"), None),
    )
    return jax.shard_map(
        on_device,
        mesh=mesh,
        in_specs=placed,
        out_specs=P(("groups", "streams", "sub"), None, None, "heads"),
        check_vma=False,
    )
```

time: 151 us -> 180 us (1.19); the launches traced: 151 us -> 177 us
  Pallas kernels: 0 us -> 78.8 us
  blocking collectives: 56.4 us -> 0 us
  starting transfers between devices: 10.2 us -> 53.9 us
  matrix products: 23.6 us -> 9.69 us
  other arithmetic: 14.3 us -> 1.74 us
  local copies, waits for them, and re-layouts: 20.6 us -> 10.4 us
  waiting for transfers between devices: 25.1 us -> 21.7 us
    pallas_call x0 -> x9, Pallas kernels: none -> 78.8 us  [the longest x1 56.8 us: on_device(): pl.pallas_call(functools.partial(place_kernel, flow_lanes, groups), in_sp...]
    ppermute x0 -> x34, starting transfers between devices: none -> 53.9 us  [the longest x29 49.9 us: traded(): landed[shift] = lax.ppermute(blocks[shift], axes, pairs)]
    all_to_all x1 -> x0, blocking collectives: 45.9 us -> none  [on_device(): lax.all_to_all(packed, ('streams', 'sub'), split_axis=0, concat_axis=0, t...]
    all_to_all x2 -> x0, waiting for transfers between devices: 25.1 us -> none  [the longest x1 22.7 us: on_device(): lax.all_to_all(joined.reshape(lanes, replica_local_slots * MOST, items, d...]
    ppermute x0 -> x34, waiting for transfers between devices: none -> 21.7 us  [the longest x29 21.7 us: traded(): landed[shift] = lax.ppermute(blocks[shift], axes, pairs)]
    reshape x9 -> x1, local copies, waits for them, and re-layouts: 13.4 us -> 0.73 us  [on_device(): gain = input_norm_gain.reshape(1, width)]
    psum x1 -> x0, blocking collectives: 10.5 us -> none  [on_device(): adapter_latent = lax.psum(partial_latent, 'heads').astype(jnp.bfloat16)]
    all_to_all x2 -> x0, starting transfers between devices: 10.2 us -> none  [the longest x1 6.33 us: on_device(): lax.all_to_all(outgoing, ('streams', 'sub'), split_axis=0, concat_axis=0,...]
  transfers between devices with their start and end apart: 2 -> 34, of which waited for: 2 -> 6; matrix products, arithmetic and copies ran while one was open for 16% -> 8% of each run, Pallas kernels for 0% -> 12%
where the time goes in v2:
time: 180 us; the launch traced here: 177 us
  Pallas kernels  78.8 us (44%)
  starting transfers between devices  53.9 us (30%)
  waiting for transfers between devices  21.7 us (12%)
  local copies, waits for them, and re-layouts  10.4 us (6%)
  matrix products  9.69 us (5%)
    pallas_call x1, Pallas kernels, on_device(): pl.pallas_call(functools.partial(place_kernel, flow_lanes, groups), in_sp...  56.8 us
    ppermute x29, starting transfers between devices, traded(): landed[shift] = lax.ppermute(blocks[shift], axes, pairs)  49.9 us
    ppermute x29, waiting for transfers between devices, traded(): landed[shift] = lax.ppermute(blocks[shift], axes, pairs)  21.7 us
    pallas_call x2, Pallas kernels, on_device(): pl.pallas_call(functools.partial(attend_kernel, steps, rows, cache, lanes...  14.8 us
    dot_general x1, matrix products, on_device(): jnp.dot(normed, projection_weight, preferred_element_type=f32)  9.69 us
    unnamed x74, local copies, waits for them, and re-layouts  8.32 us
    ppermute x5, starting transfers between devices, from_others(): landed.append(lax.ppermute(block, axis, pairs))  3.98 us
  transfers between devices with their start and end apart: 34, of which 6 were waited for; matrix products, arithmetic and copies ran while one was open for 8% of the time, Pallas kernels for 12%

profile of v2, /device:TPU:0, one launch (start us, length us, event | category | flops | bytes accessed | tf_op | source)
XLA Modules:
  0.0 176.6 jit_solution(9402113253357049024)
XLA Ops:
  0.5 0.7 reshape.53.refs_2_
  1.2 1.5 copy-done
  2.7 0.7 copy-done.6
  3.3 0.7 copy-done.8
  4.0 1.6 norm_and_pack.2
  5.7 1.6 norm_and_pack.3
  7.3 2.6 %collective-permute-start.10 = (bf16[32,1792]{1,0:T(8,128)(2,1)S(1)}, bf16[32,1792]{1,0:T(8,128)(2,1)S(1)}, u32[]{:S(2)}, u32[]{:S(2)}) collective-permute-start(bf16[32,1792]{1,0:T(8,128)(2,1)S(1)} %get-tuple-element.54), channel_id=1, source_target_pairs={{0,4},{4,0},{8,12},{12,8},{1,5},{5,1},{9,13},{13,9},{2,6},{6,2},{1... | collective-permute-start | bytes 344072 | tf_op jit(solution)/shard_map/ppermute | solution.py:305
  10.0 2.6 %collective-permute-start.11 = (bf16[32,1792]{1,0:T(8,128)(2,1)S(1)}, bf16[32,1792]{1,0:T(8,128)(2,1)S(1)}, u32[]{:S(2)}, u32[]{:S(2)}) collective-permute-start(bf16[32,1792]{1,0:T(8,128)(2,1)S(1)} %get-tuple-element.55), channel_id=1, source_target_pairs={{0,8},{4,12},{8,0},{12,4},{1,9},{5,13},{9,1},{13,5},{2,10},{6,14},... | collective-permute-start | bytes 344072 | tf_op jit(solution)/shard_map/ppermute | solution.py:305
  12.6 9.7 %convolution_add_fusion.refs_6_ = f32[256,2304]{1,0:T(8,128)} fusion(bf16[256,3584]{1,0:T(8,128)(2,1)S(1)} %get-tuple-element.44, bf16[3584,2304]{1,0:T(8,128)(2,1)} %param.15, f32[2304]{0:T(1024)S(1)} %copy-done.36), kind=kOutput, calls=%fused_computation | convolution fusion | flops 4228448256 | bytes 20718592 | tf_op jit(solution)/shard_map/dot_general | solution.py:391
  22.3 0.9 collective-permute-start
  24.0 3.5 %collective-permute-start.1 = (bf16[32,1792]{1,0:T(8,128)(2,1)S(1)}, bf16[32,1792]{1,0:T(8,128)(2,1)S(1)}, u32[]{:S(2)}, u32[]{:S(2)}) collective-permute-start(bf16[32,1792]{1,0:T(8,128)(2,1)S(1)} %get-tuple-element.47), channel_id=1, source_target_pairs={{0,8},{4,12},{8,0},{12,4},{1,9},{5,13},{9,1},{13,5},{2,10},{6,14},... | collective-permute-start | bytes 344072 | tf_op jit(solution)/shard_map/ppermute | solution.py:305
  27.5 1.1 down.3.refs_0_
  28.6 1.8 collective-permute-start.13
  30.4 5.9 %collective-permute-done.1.refs_2_ = bf16[32,1792]{1,0:T(8,128)(2,1)S(1)} collective-permute-done((bf16[32,1792]{1,0:T(8,128)(2,1)S(1)}, bf16[32,1792]{1,0:T(8,128)(2,1)S(1)}, u32[]{:S(2)}, u32[]{:S(2)}) %collective-permute-start.1) | collective-permute-done | bytes 114720 | tf_op jit(solution)/shard_map/ppermute | solution.py:305
  36.3 1.2 down.2.refs_0_
  37.5 1.6 collective-permute-start.4
  39.1 1.1 up.3
  40.2 0.6 copy-done.13
  40.8 0.6 copy-done.15
  41.5 0.6 copy-done.16
  42.1 2.7 %collective-permute-start.24 = (bf16[32,1024]{1,0:T(8,128)(2,1)}, bf16[32,1024]{1,0:T(8,128)(2,1)}, u32[]{:S(2)}, u32[]{:S(2)}) collective-permute-start(bf16[32,1024]{1,0:T(8,128)(2,1)} %get-tuple-element.70), channel_id=1, source_target_pairs={{0,4},{4,0},{8,12},{12,8},{1,5},{5,1},{9,13},{13,9},{2,6},{6,2},{1... | collective-permute-start | bytes 196616 | tf_op jit(solution)/shard_map/ppermute | solution.py:305
  45.4 1.3 convert_element_type.11
  46.8 0.8 collective-permute-start.25
  47.5 1.6 collective-permute-start.26
  49.7 1.2 collective-permute-start.7
  50.9 1.6 collective-permute-start.8
  52.5 1.6 collective-permute-start.9
  55.0 6.8 %collective-permute-start.15 = (bf16[32,1024]{1,0:T(8,128)(2,1)S(1)}, bf16[32,1024]{1,0:T(8,128)(2,1)S(1)}, u32[]{:S(2)}, u32[]{:S(2)}) collective-permute-start(bf16[32,1024]{1,0:T(8,128)(2,1)S(1)} %get-tuple-element.59), channel_id=1, source_target_pairs={{0,8},{4,12},{8,0},{12,4},{1,9},{5,13},{9,1},{13,5},{2,10},{6,14},... | collective-permute-start | bytes 196616 | tf_op jit(solution)/shard_map/ppermute | solution.py:305
  61.8 1.1 collective-permute-start.16
  62.9 3.5 %collective-permute-done.8.refs_11_ = bf16[32,2048]{1,0:T(8,128)(2,1)S(1)} collective-permute-done((bf16[32,2048]{1,0:T(8,128)(2,1)S(1)}, bf16[32,2048]{1,0:T(8,128)(2,1)S(1)}, u32[]{:S(2)}, u32[]{:S(2)}) %collective-permute-start.8) | collective-permute-done | bytes 131104 | tf_op jit(solution)/shard_map/ppermute | solution.py:305
  66.5 1.7 copy-done.18
  68.2 7.9 %attend.3 = (bf16[16,4,896]{2,1,0:T(4,128)(2,1)S(1)}, bf16[16,4,896]{2,1,0:T(4,128)(2,1)S(1)}, bf16[16,4,896]{2,1,0:T(4,128)(2,1)S(1)}, bf16[16,4,896]{2,1,0:T(4...) custom-call(s32[1,64]{1,0:T(1,128)S(1)} %bitcast.20, ...), custom_call_target="tpu_custom_call" | custom-call | flops 2000000000 | bytes 4194304 | tf_op jit(solution)/shard_map/attend/pallas_call | solution.py:453
  76.1 0.6 copy-done.4
  76.7 4.1 %collective-permute-start.28 = (bf16[16,4,896]{2,1,0:T(4,128)(2,1)S(1)}, bf16[16,4,896]{2,1,0:T(4,128)(2,1)S(1)}, u32[]{:S(2)}, u32[]{:S(2)}) collective-permute-start(bf16[16,4,896]{2,1,0:T(4,128)(2,1)S(1)} %get-tuple-element.75), channel_id=1, source_target_pairs={{0,4},{1,5},{4,0},{5,1},{8,12},{9,13},{12,8},{13,9},{2,6},{3,7},{6... | collective-permute-start | bytes 344072 | tf_op jit(solution)/shard_map/ppermute | solution.py:305
  80.9 2.5 %collective-permute-start.30 = (bf16[16,4,896]{2,1,0:T(4,128)(2,1)S(1)}, bf16[16,4,896]{2,1,0:T(4,128)(2,1)S(1)}, u32[]{:S(2)}, u32[]{:S(2)}) collective-permute-start(bf16[16,4,896]{2,1,0:T(4,128)(2,1)S(1)} %get-tuple-element.77), channel_id=1, source_target_pairs={{0,8},{1,9},{4,12},{5,13},{8,0},{9,1},{12,4},{13,5},{2,10},{3,11},... | collective-permute-start | bytes 344072 | tf_op jit(solution)/shard_map/ppermute | solution.py:305
  83.4 6.9 %attend.2 = (bf16[16,4,896]{2,1,0:T(4,128)(2,1)S(1)}, bf16[16,4,896]{2,1,0:T(4,128)(2,1)S(1)}, bf16[16,4,896]{2,1,0:T(4,128)(2,1)S(1)}, bf16[16,4,896]{2,1,0:T(4...) custom-call(s32[1,64]{1,0:T(1,128)S(1)} %bitcast.21, ...), custom_call_target="tpu_custom_call" | custom-call | flops 2000000000 | bytes 4194304 | tf_op jit(solution)/shard_map/attend/pallas_call | solution.py:453
  90.3 0.6 copy-done.5
  91.0 2.1 %collective-permute-start.32 = (bf16[16,4,896]{2,1,0:T(4,128)(2,1)S(1)}, bf16[16,4,896]{2,1,0:T(4,128)(2,1)S(1)}, u32[]{:S(2)}, u32[]{:S(2)}) collective-permute-start(bf16[16,4,896]{2,1,0:T(4,128)(2,1)S(1)} %get-tuple-element.79), channel_id=1, source_target_pairs={{0,12},{1,13},{4,8},{5,9},{8,4},{9,5},{12,0},{13,1},{2,14},{3,15},... | collective-permute-start | bytes 344072 | tf_op jit(solution)/shard_map/ppermute | solution.py:305
  93.1 1.5 collective-permute-start.33
  95.0 1.6 collective-permute-start.19
  96.6 2.4 %collective-permute-done.32.refs_14_ = bf16[16,4,896]{2,1,0:T(4,128)(2,1)S(1)} collective-permute-done((bf16[16,4,896]{2,1,0:T(4,128)(2,1)S(1)}, bf16[16,4,896]{2,1,0:T(4,128)(2,1)S(1)}, u32[]{:S(2)}, u32[]{:S(2)}) %collective-permute-start.32) | collective-permute-done | bytes 114720 | tf_op jit(solution)/shard_map/ppermute | solution.py:305
  98.9 5.4 %collective-permute-start.20 = (bf16[16,4,896]{2,1,0:T(4,128)(2,1)S(1)}, bf16[16,4,896]{2,1,0:T(4,128)(2,1)S(1)}, u32[]{:S(2)}, u32[]{:S(2)}) collective-permute-start(bf16[16,4,896]{2,1,0:T(4,128)(2,1)S(1)} %get-tuple-element.65), channel_id=1, source_target_pairs={{0,8},{1,9},{4,12},{5,13},{8,0},{9,1},{12,4},{13,5},{2,10},{3,11},... | collective-permute-start | bytes 344072 | tf_op jit(solution)/shard_map/ppermute | solution.py:305
  104.3 1.9 %collective-permute-start.21 = (bf16[16,4,896]{2,1,0:T(4,128)(2,1)S(1)}, bf16[16,4,896]{2,1,0:T(4,128)(2,1)S(1)}, u32[]{:S(2)}, u32[]{:S(2)}) collective-permute-start(bf16[16,4,896]{2,1,0:T(4,128)(2,1)S(1)} %get-tuple-element.66), channel_id=1, source_target_pairs={{0,9},{1,8},{4,13},{5,12},{8,1},{9,0},{12,5},{13,4},{2,11},{3,10},... | collective-permute-start | bytes 344072 | tf_op jit(solution)/shard_map/ppermute | solution.py:305
  106.2 1.9 %collective-permute-start.22 = (bf16[16,4,896]{2,1,0:T(4,128)(2,1)S(1)}, bf16[16,4,896]{2,1,0:T(4,128)(2,1)S(1)}, u32[]{:S(2)}, u32[]{:S(2)}) collective-permute-start(bf16[16,4,896]{2,1,0:T(4,128)(2,1)S(1)} %get-tuple-element.67), channel_id=1, source_target_pairs={{0,12},{1,13},{4,8},{5,9},{8,4},{9,5},{12,0},{13,1},{2,14},{3,15},... | collective-permute-start | bytes 344072 | tf_op jit(solution)/shard_map/ppermute | solution.py:305
  108.1 1.3 collective-permute-start.23
  109.4 8.9 %collective-permute-done.20.refs_4_ = bf16[16,4,896]{2,1,0:T(4,128)(2,1)S(1)} collective-permute-done((bf16[16,4,896]{2,1,0:T(4,128)(2,1)S(1)}, bf16[16,4,896]{2,1,0:T(4,128)(2,1)S(1)}, u32[]{:S(2)}, u32[]{:S(2)}) %collective-permute-start.20) | collective-permute-done | bytes 114720 | tf_op jit(solution)/shard_map/ppermute | solution.py:305
  118.2 0.8 collective-permute-done.21.refs_5_
  119.8 56.8 %place.1 = bf16[128,4,1792]{2,1,0:T(4,128)(2,1)} custom-call(bf16[16,4,896]{2,1,0:T(4,128)(2,1)} %copy-done.5, bf16[16,4,896]{2,1,0:T(4,128)(2,1)} %copy-done.26, bf16[16,4,896]{2,1,0:T(4,128)(2,1)} %copy-done.27, bf16[16,4,896]{2,1,0:T(4,128)(2,1)} %copy-done.28, bf16[16,4,896]{2,1,0:T(4,128)(2,1)} %copy-done.29, bf16[16,4,896]{2,1,0:T(4,128)(2,1)} %copy-done.30, ...), custom_call_target="tpu_custom_call" | custom-call | bytes 4194304 | tf_op jit(solution)/shard_map/place/pallas_call | solution.py:488
  (110 shorter events, 4.4 us)
Async XLA Ops:
  0.0 27.5 %collective-permute-start.3 = (bf16[4,1792,128]{2,1,0:T(8,128)(2,1)}, bf16[4,1792,128]{2,1,0:T(8,128)(2,1)S(1)}, u32[]{:S(2)}, u32[]{:S(2)}) collective-permute-start(bf16[4,1792,128]{2,1,0:T(8,128)(2,1)} %refs_4_.3), channel_id=1, source_target_pairs={{0,1},{1,0},{2,3},{3,2},{4,5},{5,4},{6,7},{7,6},{8,9},{9,8},{10,11... | collective-permute-start | bytes 5505032 | tf_op jit(solution)/shard_map/ppermute | solution.py:314
  7.3 15.0 %collective-permute-start.10 = (bf16[32,1792]{1,0:T(8,128)(2,1)S(1)}, bf16[32,1792]{1,0:T(8,128)(2,1)S(1)}, u32[]{:S(2)}, u32[]{:S(2)}) collective-permute-start(bf16[32,1792]{1,0:T(8,128)(2,1)S(1)} %get-tuple-element.54), channel_id=1, source_target_pairs={{0,4},{4,0},{8,12},{12,8},{1,5},{5,1},{9,13},{13,9},{2,6},{6,2},{1... | collective-permute-start | bytes 344072 | tf_op jit(solution)/shard_map/ppermute | solution.py:305
  10.0 13.8 %collective-permute-start.11 = (bf16[32,1792]{1,0:T(8,128)(2,1)S(1)}, bf16[32,1792]{1,0:T(8,128)(2,1)S(1)}, u32[]{:S(2)}, u32[]{:S(2)}) collective-permute-start(bf16[32,1792]{1,0:T(8,128)(2,1)S(1)} %get-tuple-element.55), channel_id=1, source_target_pairs={{0,8},{4,12},{8,0},{12,4},{1,9},{5,13},{9,1},{13,5},{2,10},{6,14},... | collective-permute-start | bytes 344072 | tf_op jit(solution)/shard_map/ppermute | solution.py:305
  12.6 11.4 %collective-permute-start.12 = (bf16[32,1792]{1,0:T(8,128)(2,1)S(1)}, bf16[32,1792]{1,0:T(8,128)(2,1)S(1)}, u32[]{:S(2)}, u32[]{:S(2)}) collective-permute-start(bf16[32,1792]{1,0:T(8,128)(2,1)S(1)} %get-tuple-element.56), channel_id=1, source_target_pairs={{0,12},{4,8},{8,4},{12,0},{1,13},{5,9},{9,5},{13,1},{2,14},{6,10},... | collective-permute-start | bytes 344072 | tf_op jit(solution)/shard_map/ppermute | solution.py:305
  12.6 26.5 %collective-permute-start.5 = (bf16[256,1792]{1,0:T(8,128)(2,1)S(1)}, bf16[256,1792]{1,0:T(8,128)(2,1)S(1)}, u32[]{:S(2)}, u32[]{:S(2)}) collective-permute-start(bf16[256,1792]{1,0:T(8,128)(2,1)S(1)} %bitcast.12), channel_id=1, source_target_pairs={{0,1},{1,0},{2,3},{3,2},{4,5},{5,4},{6,7},{7,6},{8,9},{9,8},{10,11... | collective-permute-start | bytes 2752520 | tf_op jit(solution)/shard_map/ppermute | solution.py:314
  12.6 14.9 %copy-start.1 = (bf16[4,1792,128]{2,1,0:T(8,128)(2,1)S(1)}, bf16[4,1792,128]{2,1,0:T(8,128)(2,1)}, u32[]{:S(2)}) copy-start(bf16[4,1792,128]{2,1,0:T(8,128)(2,1)} %refs_4_.3) | copy-start | bytes 5505028
  22.3 6.3 %collective-permute-start = (bf16[32,1792]{1,0:T(8,128)(2,1)S(1)}, bf16[32,1792]{1,0:T(8,128)(2,1)S(1)}, u32[]{:S(2)}, u32[]{:S(2)}) collective-permute-start(bf16[32,1792]{1,0:T(8,128)(2,1)S(1)} %get-tuple-element.46), channel_id=1, source_target_pairs={{0,4},{4,0},{8,12},{12,8},{1,5},{5,1},{9,13},{13,9},{2,6},{6,2},{1... | collective-permute-start | bytes 344072 | tf_op jit(solution)/shard_map/ppermute | solution.py:305
  23.8 15.3 %collective-permute-start.6 = (bf16[256,256]{1,0:T(8,128)(2,1)S(1)}, bf16[256,256]{1,0:T(8,128)(2,1)S(1)}, u32[]{:S(2)}, u32[]{:S(2)}) collective-permute-start(bf16[256,256]{1,0:T(8,128)(2,1)S(1)} %bitcast.15), channel_id=1, source_target_pairs={{0,1},{1,0},{2,3},{3,2},{4,5},{5,4},{6,7},{7,6},{8,9},{9,8},{10,11... | collective-permute-start | bytes 393224 | tf_op jit(solution)/shard_map/ppermute | solution.py:314
  24.0 12.3 %collective-permute-start.1 = (bf16[32,1792]{1,0:T(8,128)(2,1)S(1)}, bf16[32,1792]{1,0:T(8,128)(2,1)S(1)}, u32[]{:S(2)}, u32[]{:S(2)}) collective-permute-start(bf16[32,1792]{1,0:T(8,128)(2,1)S(1)} %get-tuple-element.47), channel_id=1, source_target_pairs={{0,8},{4,12},{8,0},{12,4},{1,9},{5,13},{9,1},{13,5},{2,10},{6,14},... | collective-permute-start | bytes 344072 | tf_op jit(solution)/shard_map/ppermute | solution.py:305
  27.5 8.8 %collective-permute-start.2 = (bf16[32,1792]{1,0:T(8,128)(2,1)S(1)}, bf16[32,1792]{1,0:T(8,128)(2,1)S(1)}, u32[]{:S(2)}, u32[]{:S(2)}) collective-permute-start(bf16[32,1792]{1,0:T(8,128)(2,1)S(1)} %get-tuple-element.48), channel_id=1, source_target_pairs={{0,12},{4,8},{8,4},{12,0},{1,13},{5,9},{9,5},{13,1},{2,14},{6,10},... | collective-permute-start | bytes 344072 | tf_op jit(solution)/shard_map/ppermute | solution.py:305
  28.6 10.5 %collective-permute-start.13 = (f32[128,128]{1,0:T(8,128)S(1)}, f32[128,128]{1,0:T(8,128)S(1)}, u32[]{:S(2)}, u32[]{:S(2)}) collective-permute-start(f32[128,128]{1,0:T(8,128)S(1)} %down.3.refs_0_), channel_id=1, source_target_pairs={{0,2},{2,0},{1,3},{3,1},{4,6},{6,4},{5,7},{7,5},{8,10},{10,8},{9,1... | collective-permute-start | bytes 196616 | tf_op jit(solution)/shard_map/ppermute | solution.py:314
  37.5 29.0 %copy-start.7 = (s32[64,1]{0,1:T(1,128)S(1)}, s32[64,1]{0,1:T(1,128)}, u32[]{:S(2)}) copy-start(s32[64,1]{0,1:T(1,128)} %param.17) | copy-start | bytes 772
  37.5 29.0 %copy-start.9 = (s32[32]{0:T(128)S(1)}, s32[32]{0:T(128)}, u32[]{:S(2)}) copy-start(s32[32]{0:T(128)} %param.18) | copy-start | bytes 388
  37.5 28.9 %copy-start.11 = (bf16[64,32,256]{2,1,0:T(8,128)(2,1)S(1)}, bf16[64,32,256]{2,1,0:T(8,128)(2,1)}, u32[]{:S(2)}) copy-start(bf16[64,32,256]{2,1,0:T(8,128)(2,1)} %refs_7_.3) | copy-start | bytes 3145732
  37.5 28.9 %copy-start.17 = (s32[64,1]{0,1:T(1,128)S(1)}, s32[64,1]{0,1:T(1,128)}, u32[]{:S(2)}) copy-start(s32[64,1]{0,1:T(1,128)} %param.25) | copy-start | bytes 772
  37.5 11.7 %collective-permute-start.4 = (f32[128,128]{1,0:T(8,128)S(1)}, f32[128,128]{1,0:T(8,128)S(1)}, u32[]{:S(2)}, u32[]{:S(2)}) collective-permute-start(f32[128,128]{1,0:T(8,128)S(1)} %down.2.refs_0_), channel_id=1, source_target_pairs={{0,2},{2,0},{1,3},{3,1},{4,6},{6,4},{5,7},{7,5},{8,10},{10,8},{9,1... | collective-permute-start | bytes 196616 | tf_op jit(solution)/shard_map/ppermute | solution.py:314
  42.1 10.4 %collective-permute-start.24 = (bf16[32,1024]{1,0:T(8,128)(2,1)}, bf16[32,1024]{1,0:T(8,128)(2,1)}, u32[]{:S(2)}, u32[]{:S(2)}) collective-permute-start(bf16[32,1024]{1,0:T(8,128)(2,1)} %get-tuple-element.70), channel_id=1, source_target_pairs={{0,4},{4,0},{8,12},{12,8},{1,5},{5,1},{9,13},{13,9},{2,6},{6,2},{1... | collective-permute-start | bytes 196616 | tf_op jit(solution)/shard_map/ppermute | solution.py:305
  46.7 19.7 %copy-start.12 = (bf16[64,32,256]{2,1,0:T(8,128)(2,1)S(1)}, bf16[64,32,256]{2,1,0:T(8,128)(2,1)}, u32[]{:S(2)}) copy-start(bf16[64,32,256]{2,1,0:T(8,128)(2,1)} %refs_8_.3) | copy-start | bytes 3145732
  46.7 19.7 %copy-start.14 = (bf16[32,1024]{1,0:T(8,128)(2,1)S(1)}, bf16[32,1024]{1,0:T(8,128)(2,1)}, u32[]{:S(2)}) copy-start(bf16[32,1024]{1,0:T(8,128)(2,1)} %copy-done.13) | copy-start | bytes 196612
  46.8 8.1 %collective-permute-start.25 = (bf16[32,1024]{1,0:T(8,128)(2,1)}, bf16[32,1024]{1,0:T(8,128)(2,1)S(1)}, u32[]{:S(2)}, u32[]{:S(2)}) collective-permute-start(bf16[32,1024]{1,0:T(8,128)(2,1)} %copy-done.16), channel_id=1, source_target_pairs={{0,8},{4,12},{8,0},{12,4},{1,9},{5,13},{9,1},{13,5},{2,10},{6,14},... | collective-permute-start | bytes 196616 | tf_op jit(solution)/shard_map/ppermute | solution.py:305
  47.5 7.5 %collective-permute-start.26 = (bf16[32,1024]{1,0:T(8,128)(2,1)}, bf16[32,1024]{1,0:T(8,128)(2,1)S(1)}, u32[]{:S(2)}, u32[]{:S(2)}) collective-permute-start(bf16[32,1024]{1,0:T(8,128)(2,1)} %copy-done.15), channel_id=1, source_target_pairs={{0,12},{4,8},{8,4},{12,0},{1,13},{5,9},{9,5},{13,1},{2,14},{6,10},... | collective-permute-start | bytes 196616 | tf_op jit(solution)/shard_map/ppermute | solution.py:305
  49.7 12.1 %collective-permute-start.7 = (bf16[32,2048]{1,0:T(8,128)(2,1)S(1)}, bf16[32,2048]{1,0:T(8,128)(2,1)S(1)}, u32[]{:S(2)}, u32[]{:S(2)}) collective-permute-start(bf16[32,2048]{1,0:T(8,128)(2,1)S(1)} %get-tuple-element.50), channel_id=1, source_target_pairs={{0,4},{4,0},{8,12},{12,8},{1,5},{5,1},{9,13},{13,9},{2,6},{6,2},{1... | collective-permute-start | bytes 393224 | tf_op jit(solution)/shard_map/ppermute | solution.py:305
  50.9 15.6 %collective-permute-start.8 = (bf16[32,2048]{1,0:T(8,128)(2,1)S(1)}, bf16[32,2048]{1,0:T(8,128)(2,1)S(1)}, u32[]{:S(2)}, u32[]{:S(2)}) collective-permute-start(bf16[32,2048]{1,0:T(8,128)(2,1)S(1)} %get-tuple-element.51), channel_id=1, source_target_pairs={{0,8},{4,12},{8,0},{12,4},{1,9},{5,13},{9,1},{13,5},{2,10},{6,14},... | collective-permute-start | bytes 393224 | tf_op jit(solution)/shard_map/ppermute | solution.py:305
  52.5 13.9 %collective-permute-start.9 = (bf16[32,2048]{1,0:T(8,128)(2,1)S(1)}, bf16[32,2048]{1,0:T(8,128)(2,1)S(1)}, u32[]{:S(2)}, u32[]{:S(2)}) collective-permute-start(bf16[32,2048]{1,0:T(8,128)(2,1)S(1)} %get-tuple-element.52), channel_id=1, source_target_pairs={{0,12},{4,8},{8,4},{12,0},{1,13},{5,9},{9,5},{13,1},{2,14},{6,10},... | collective-permute-start | bytes 393224 | tf_op jit(solution)/shard_map/ppermute | solution.py:305
  54.9 25.9 %collective-permute-start.14 = (bf16[32,1024]{1,0:T(8,128)(2,1)S(1)}, bf16[32,1024]{1,0:T(8,128)(2,1)S(1)}, u32[]{:S(2)}, u32[]{:S(2)}) collective-permute-start(bf16[32,1024]{1,0:T(8,128)(2,1)S(1)} %get-tuple-element.58), channel_id=1, source_target_pairs={{0,4},{4,0},{8,12},{12,8},{1,5},{5,1},{9,13},{13,9},{2,6},{6,2},{1... | collective-permute-start | bytes 196616 | tf_op jit(solution)/shard_map/ppermute | solution.py:305
  55.0 25.9 %collective-permute-start.15 = (bf16[32,1024]{1,0:T(8,128)(2,1)S(1)}, bf16[32,1024]{1,0:T(8,128)(2,1)S(1)}, u32[]{:S(2)}, u32[]{:S(2)}) collective-permute-start(bf16[32,1024]{1,0:T(8,128)(2,1)S(1)} %get-tuple-element.59), channel_id=1, source_target_pairs={{0,8},{4,12},{8,0},{12,4},{1,9},{5,13},{9,1},{13,5},{2,10},{6,14},... | collective-permute-start | bytes 196616 | tf_op jit(solution)/shard_map/ppermute | solution.py:305
  61.8 21.6 %collective-permute-start.16 = (bf16[32,1024]{1,0:T(8,128)(2,1)S(1)}, bf16[32,1024]{1,0:T(8,128)(2,1)S(1)}, u32[]{:S(2)}, u32[]{:S(2)}) collective-permute-start(bf16[32,1024]{1,0:T(8,128)(2,1)S(1)} %get-tuple-element.60), channel_id=1, source_target_pairs={{0,12},{4,8},{8,4},{12,0},{1,13},{5,9},{9,5},{13,1},{2,14},{6,10},... | collective-permute-start | bytes 196616 | tf_op jit(solution)/shard_map/ppermute | solution.py:305
  76.7 14.3 %collective-permute-start.27 = (bf16[16,4,896]{2,1,0:T(4,128)(2,1)S(1)}, bf16[16,4,896]{2,1,0:T(4,128)(2,1)S(1)}, u32[]{:S(2)}, u32[]{:S(2)}) collective-permute-start(bf16[16,4,896]{2,1,0:T(4,128)(2,1)S(1)} %get-tuple-element.74), channel_id=1, source_target_pairs={{0,1},{1,0},{4,5},{5,4},{8,9},{9,8},{12,13},{13,12},{2,3},{3,2},{6... | collective-permute-start | bytes 344072 | tf_op jit(solution)/shard_map/ppermute | solution.py:305
  76.7 16.4 %collective-permute-start.28 = (bf16[16,4,896]{2,1,0:T(4,128)(2,1)S(1)}, bf16[16,4,896]{2,1,0:T(4,128)(2,1)S(1)}, u32[]{:S(2)}, u32[]{:S(2)}) collective-permute-start(bf16[16,4,896]{2,1,0:T(4,128)(2,1)S(1)} %get-tuple-element.75), channel_id=1, source_target_pairs={{0,4},{1,5},{4,0},{5,1},{8,12},{9,13},{12,8},{13,9},{2,6},{3,7},{6... | collective-permute-start | bytes 344072 | tf_op jit(solution)/shard_map/ppermute | solution.py:305
  80.8 13.9 %collective-permute-start.29 = (bf16[16,4,896]{2,1,0:T(4,128)(2,1)S(1)}, bf16[16,4,896]{2,1,0:T(4,128)(2,1)S(1)}, u32[]{:S(2)}, u32[]{:S(2)}) collective-permute-start(bf16[16,4,896]{2,1,0:T(4,128)(2,1)S(1)} %get-tuple-element.76), channel_id=1, source_target_pairs={{0,5},{1,4},{4,1},{5,0},{8,13},{9,12},{12,9},{13,8},{2,7},{3,6},{6... | collective-permute-start | bytes 344072 | tf_op jit(solution)/shard_map/ppermute | solution.py:305
  80.9 14.0 %collective-permute-start.30 = (bf16[16,4,896]{2,1,0:T(4,128)(2,1)S(1)}, bf16[16,4,896]{2,1,0:T(4,128)(2,1)S(1)}, u32[]{:S(2)}, u32[]{:S(2)}) collective-permute-start(bf16[16,4,896]{2,1,0:T(4,128)(2,1)S(1)} %get-tuple-element.77), channel_id=1, source_target_pairs={{0,8},{1,9},{4,12},{5,13},{8,0},{9,1},{12,4},{13,5},{2,10},{3,11},... | collective-permute-start | bytes 344072 | tf_op jit(solution)/shard_map/ppermute | solution.py:305
  83.4 11.5 %collective-permute-start.31 = (bf16[16,4,896]{2,1,0:T(4,128)(2,1)S(1)}, bf16[16,4,896]{2,1,0:T(4,128)(2,1)S(1)}, u32[]{:S(2)}, u32[]{:S(2)}) collective-permute-start(bf16[16,4,896]{2,1,0:T(4,128)(2,1)S(1)} %get-tuple-element.78), channel_id=1, source_target_pairs={{0,9},{1,8},{4,13},{5,12},{8,1},{9,0},{12,5},{13,4},{2,11},{3,10},... | collective-permute-start | bytes 344072 | tf_op jit(solution)/shard_map/ppermute | solution.py:305
  91.0 28.1 %copy-start.19 = (bf16[16,4,896]{2,1,0:T(4,128)(2,1)}, bf16[16,4,896]{2,1,0:T(4,128)(2,1)S(1)}, u32[]{:S(2)}) copy-start(bf16[16,4,896]{2,1,0:T(4,128)(2,1)S(1)} %collective-permute-done.27.refs_9_) | copy-start | bytes 344068
  91.0 7.9 %collective-permute-start.32 = (bf16[16,4,896]{2,1,0:T(4,128)(2,1)S(1)}, bf16[16,4,896]{2,1,0:T(4,128)(2,1)S(1)}, u32[]{:S(2)}, u32[]{:S(2)}) collective-permute-start(bf16[16,4,896]{2,1,0:T(4,128)(2,1)S(1)} %get-tuple-element.79), channel_id=1, source_target_pairs={{0,12},{1,13},{4,8},{5,9},{8,4},{9,5},{12,0},{13,1},{2,14},{3,15},... | collective-permute-start | bytes 344072 | tf_op jit(solution)/shard_map/ppermute | solution.py:305
  93.1 25.9 %copy-start.20 = (bf16[16,4,896]{2,1,0:T(4,128)(2,1)}, bf16[16,4,896]{2,1,0:T(4,128)(2,1)S(1)}, u32[]{:S(2)}) copy-start(bf16[16,4,896]{2,1,0:T(4,128)(2,1)S(1)} %collective-permute-done.28.refs_10_) | copy-start | bytes 344068
  93.1 11.2 %collective-permute-start.33 = (bf16[16,4,896]{2,1,0:T(4,128)(2,1)S(1)}, bf16[16,4,896]{2,1,0:T(4,128)(2,1)S(1)}, u32[]{:S(2)}, u32[]{:S(2)}) collective-permute-start(bf16[16,4,896]{2,1,0:T(4,128)(2,1)S(1)} %get-tuple-element.80), channel_id=1, source_target_pairs={{0,13},{1,12},{4,9},{5,8},{8,5},{9,4},{12,1},{13,0},{2,15},{3,14},... | collective-permute-start | bytes 344072 | tf_op jit(solution)/shard_map/ppermute | solution.py:305
  94.7 24.4 %copy-start.21 = (bf16[16,4,896]{2,1,0:T(4,128)(2,1)}, bf16[16,4,896]{2,1,0:T(4,128)(2,1)S(1)}, u32[]{:S(2)}) copy-start(bf16[16,4,896]{2,1,0:T(4,128)(2,1)S(1)} %collective-permute-done.29.refs_11_) | copy-start | bytes 344068
  94.7 11.6 %collective-permute-start.17 = (bf16[16,4,896]{2,1,0:T(4,128)(2,1)S(1)}, bf16[16,4,896]{2,1,0:T(4,128)(2,1)S(1)}, u32[]{:S(2)}, u32[]{:S(2)}) collective-permute-start(bf16[16,4,896]{2,1,0:T(4,128)(2,1)S(1)} %get-tuple-element.62), channel_id=1, source_target_pairs={{0,1},{1,0},{4,5},{5,4},{8,9},{9,8},{12,13},{13,12},{2,3},{3,2},{6... | collective-permute-start | bytes 344072 | tf_op jit(solution)/shard_map/ppermute | solution.py:305
  94.9 24.2 %copy-start.22 = (bf16[16,4,896]{2,1,0:T(4,128)(2,1)}, bf16[16,4,896]{2,1,0:T(4,128)(2,1)S(1)}, u32[]{:S(2)}) copy-start(bf16[16,4,896]{2,1,0:T(4,128)(2,1)S(1)} %collective-permute-done.30.refs_12_) | copy-start | bytes 344068
  94.9 13.2 %collective-permute-start.18 = (bf16[16,4,896]{2,1,0:T(4,128)(2,1)S(1)}, bf16[16,4,896]{2,1,0:T(4,128)(2,1)S(1)}, u32[]{:S(2)}, u32[]{:S(2)}) collective-permute-start(bf16[16,4,896]{2,1,0:T(4,128)(2,1)S(1)} %get-tuple-element.63), channel_id=1, source_target_pairs={{0,4},{1,5},{4,0},{5,1},{8,12},{9,13},{12,8},{13,9},{2,6},{3,7},{6... | collective-permute-start | bytes 344072 | tf_op jit(solution)/shard_map/ppermute | solution.py:305
  95.0 24.1 %copy-start.23 = (bf16[16,4,896]{2,1,0:T(4,128)(2,1)}, bf16[16,4,896]{2,1,0:T(4,128)(2,1)S(1)}, u32[]{:S(2)}) copy-start(bf16[16,4,896]{2,1,0:T(4,128)(2,1)S(1)} %collective-permute-done.31.refs_13_) | copy-start | bytes 344068
  95.0 14.4 %collective-permute-start.19 = (bf16[16,4,896]{2,1,0:T(4,128)(2,1)S(1)}, bf16[16,4,896]{2,1,0:T(4,128)(2,1)S(1)}, u32[]{:S(2)}, u32[]{:S(2)}) collective-permute-start(bf16[16,4,896]{2,1,0:T(4,128)(2,1)S(1)} %get-tuple-element.64), channel_id=1, source_target_pairs={{0,5},{1,4},{4,1},{5,0},{8,13},{9,12},{12,9},{13,8},{2,7},{3,6},{6... | collective-permute-start | bytes 344072 | tf_op jit(solution)/shard_map/ppermute | solution.py:305
  98.9 20.2 %copy-start.24 = (bf16[16,4,896]{2,1,0:T(4,128)(2,1)}, bf16[16,4,896]{2,1,0:T(4,128)(2,1)S(1)}, u32[]{:S(2)}) copy-start(bf16[16,4,896]{2,1,0:T(4,128)(2,1)S(1)} %collective-permute-done.32.refs_14_) | copy-start | bytes 344068
  98.9 19.3 %collective-permute-start.20 = (bf16[16,4,896]{2,1,0:T(4,128)(2,1)S(1)}, bf16[16,4,896]{2,1,0:T(4,128)(2,1)S(1)}, u32[]{:S(2)}, u32[]{:S(2)}) collective-permute-start(bf16[16,4,896]{2,1,0:T(4,128)(2,1)S(1)} %get-tuple-element.65), channel_id=1, source_target_pairs={{0,8},{1,9},{4,12},{5,13},{8,0},{9,1},{12,4},{13,5},{2,10},{3,11},... | collective-permute-start | bytes 344072 | tf_op jit(solution)/shard_map/ppermute | solution.py:305
  104.3 14.8 %copy-start.25 = (bf16[16,4,896]{2,1,0:T(4,128)(2,1)}, bf16[16,4,896]{2,1,0:T(4,128)(2,1)S(1)}, u32[]{:S(2)}) copy-start(bf16[16,4,896]{2,1,0:T(4,128)(2,1)S(1)} %collective-permute-done.33.refs_15_) | copy-start | bytes 344068
  104.3 14.7 %collective-permute-start.21 = (bf16[16,4,896]{2,1,0:T(4,128)(2,1)S(1)}, bf16[16,4,896]{2,1,0:T(4,128)(2,1)S(1)}, u32[]{:S(2)}, u32[]{:S(2)}) collective-permute-start(bf16[16,4,896]{2,1,0:T(4,128)(2,1)S(1)} %get-tuple-element.66), channel_id=1, source_target_pairs={{0,9},{1,8},{4,13},{5,12},{8,1},{9,0},{12,5},{13,4},{2,11},{3,10},... | collective-permute-start | bytes 344072 | tf_op jit(solution)/shard_map/ppermute | solution.py:305
  106.2 12.8 %collective-permute-start.22 = (bf16[16,4,896]{2,1,0:T(4,128)(2,1)S(1)}, bf16[16,4,896]{2,1,0:T(4,128)(2,1)S(1)}, u32[]{:S(2)}, u32[]{:S(2)}) collective-permute-start(bf16[16,4,896]{2,1,0:T(4,128)(2,1)S(1)} %get-tuple-element.67), channel_id=1, source_target_pairs={{0,12},{1,13},{4,8},{5,9},{8,4},{9,5},{12,0},{13,1},{2,14},{3,15},... | collective-permute-start | bytes 344072 | tf_op jit(solution)/shard_map/ppermute | solution.py:305
  108.1 10.9 %collective-permute-start.23 = (bf16[16,4,896]{2,1,0:T(4,128)(2,1)S(1)}, bf16[16,4,896]{2,1,0:T(4,128)(2,1)S(1)}, u32[]{:S(2)}, u32[]{:S(2)}) collective-permute-start(bf16[16,4,896]{2,1,0:T(4,128)(2,1)S(1)} %get-tuple-element.68), channel_id=1, source_target_pairs={{0,13},{1,12},{4,9},{5,8},{8,5},{9,4},{12,1},{13,0},{2,15},{3,14},... | collective-permute-start | bytes 344072 | tf_op jit(solution)/shard_map/ppermute | solution.py:305
  (23 other events, 102.2 us)

commit v3 on v2

v3 whole, which is shorter than its diff:
```python
import functools
import math

import jax
import jax.numpy as jnp
from jax import lax
from jax.experimental import pallas as pl
from jax.experimental.pallas import tpu as pltpu
from jax.sharding import PartitionSpec as P

QUERY_HEADS = 28
KEY_VALUE_HEADS = 4
HEAD_WIDTH = 128
ADAPTER_RANK = 64
MOST = 2
PER_GROUP = QUERY_HEADS // KEY_VALUE_HEADS
LANE_AXES = ("streams", "sub")
BATCH = 8
VMEM = pl.BlockSpec(memory_space=pltpu.VMEM)
MIB = 1 << 20


def iota(shape, dim):
    return lax.broadcasted_iota(jnp.int32, shape, dim)


def as_column(row):
    count = row.shape[1]
    square = (count, count)
    same = iota(square, 0) == iota(square, 1)
    return jnp.sum(jnp.where(same, jnp.broadcast_to(row, square), 0), axis=1, keepdims=True)


def ranked(labels, most):
    count = labels.shape[1]
    square = (count, count)
    earlier = (as_column(labels) == labels) & (iota(square, 0) < iota(square, 1))
    return labels * most + jnp.sum(earlier.astype(jnp.int32), axis=0, keepdims=True)


def slot_places(speaker, table, lane_base):
    speakers_all = table.shape[1]
    rows = speaker.shape[1]
    match = iota((speakers_all, rows), 0) == speaker
    slots = jnp.sum(jnp.where(match, as_column(table), 0), axis=0, keepdims=True)
    return ranked(slots ^ lane_base, MOST)


def pack_kernel(steps, rows, flow_most, first, *refs):
    if first:
        speaker_ref, table_ref, owner_ref, gain_ref, x_ref = refs[:5]
        normed_ref, places_ref, message_refs = refs[5], refs[6], refs[7:]
    else:
        places_ref, gain_ref, x_ref, _, normed_ref = refs[:5]
        message_refs = refs[5:]
    width = x_ref.shape[1]
    per_message, sliced = message_refs[0].shape
    spots = per_message // steps
    gain = jnp.concatenate([gain_ref[i : i + 1, :] for i in range(gain_ref.shape[0])], axis=1)

    def one(index, carry):
        span = pl.ds(pl.multiple_of(index * 16, 16), 16)
        values = x_ref[span, :].astype(jnp.float32)
        mean_sq = jnp.sum(values * values, axis=1, keepdims=True) * (1.0 / width)
        normed = values * lax.rsqrt(mean_sq + 1e-06) * gain
        normed_ref[span, :] = normed.astype(jnp.bfloat16)
        return carry

    lax.fori_loop(0, steps * rows // 16, one, 0)
    if first:
        base = lax.axis_index("streams") * (spots // MOST)
        places = slot_places(speaker_ref[...], table_ref[...], base)
        lane = lax.axis_index("streams") * lax.axis_size("sub") + lax.axis_index("sub")
        places_ref[0:1, :] = places
        places_ref[1:2, :] = ranked(owner_ref[...] ^ lane, flow_most)
    else:
        places = places_ref[0:1, :]
    total = len(message_refs) * per_message
    shape = (total, steps * rows)
    out_row = iota(shape, 0)
    wanted = out_row // per_message * spots + out_row % spots
    out_step = out_row % per_message // spots
    places = jnp.concatenate([places] * steps, axis=1)
    pick = (wanted == places) & (out_step == iota(shape, 1) // rows)
    pick = pick.astype(jnp.float32).astype(jnp.bfloat16)
    begin = pl.multiple_of(lax.axis_index("heads") * sliced, 128)
    own = normed_ref[:, pl.ds(begin, sliced)]
    packed = jnp.dot(pick, own, preferred_element_type=jnp.float32).astype(jnp.bfloat16)
    for number, message_ref in enumerate(message_refs):
        message_ref[...] = packed[number * per_message : (number + 1) * per_message]


def row_slots(shape, spots):
    return iota(shape, 0) % spots // MOST


def down_kernel(lanes, spots, *refs):
    message_refs, map_ref, partial_ref = refs[:lanes], refs[-2], refs[-1]
    rows = jnp.concatenate([ref[...] for ref in message_refs], axis=0)
    own_slot = row_slots(partial_ref.shape, spots)
    total = jnp.zeros(partial_ref.shape, jnp.float32)
    for slot in range(map_ref.shape[0]):
        part = jnp.dot(rows, map_ref[slot], preferred_element_type=jnp.float32)
        total = jnp.where(own_slot == slot, part, total)
    partial_ref[...] = total


def up_kernel(heads, spots, *refs):
    partial_refs, query_ref, value_ref = refs[:heads], refs[heads], refs[heads + 1]
    message_refs = refs[heads + 2 :]
    total = partial_refs[0][...]
    for ref in partial_refs[1:]:
        total = total + ref[...]
    latent = total.astype(jnp.bfloat16).astype(jnp.float32)
    own_slot = row_slots(latent.shape, spots)
    column = iota(latent.shape, 1) // ADAPTER_RANK
    turned = pltpu.roll(latent, ADAPTER_RANK, 1)
    low = iota(latent.shape, 1) < ADAPTER_RANK
    query_pair = jnp.where(low, latent, turned)
    value_pair = jnp.where(low, turned, latent)

    def product(pair, map_ref):
        pieces = []
        for slot in range(0, map_ref.shape[0] // ADAPTER_RANK, 2):
            kept = jnp.where(own_slot == slot + column, pair, 0.0)
            pieces.append(kept.astype(jnp.bfloat16))
        wide = jnp.concatenate(pieces, axis=1)
        return jnp.dot(wide, map_ref[...], preferred_element_type=jnp.float32).astype(jnp.bfloat16)

    queries = product(query_pair, query_ref)
    values = product(value_pair, value_ref)
    query_width = queries.shape[1]
    per_message = message_refs[0].shape[0]
    for number, ref in enumerate(message_refs):
        span = slice(number * per_message, (number + 1) * per_message)
        ref[:, :query_width] = queries[span]
        ref[:, query_width:] = values[span]


def attend_kernel(before, steps, rows, cache, groups, lanes, subs, last, *refs):
    places_ref, length_ref, cos_ref, sin_ref, qkv_ref, key_ref, value_ref = refs[:7]
    delta_refs, refs = refs[7 : 7 + lanes], refs[7 + lanes :]
    if before:
        earlier_ref, refs = refs[0], refs[1:]
    if not last:
        fresh_ref, refs = refs[0], refs[1:]
    message_refs = refs[:subs]
    delta_ref, context_ref, bias_ref = refs[subs:]
    per_message = delta_refs[0].shape[0]
    spots = per_message // steps
    query_width = PER_GROUP * HEAD_WIDTH
    block_width = query_width + 2 * HEAD_WIDTH
    known = before + steps
    wide = groups * HEAD_WIDTH

    column = as_column(places_ref[0:1, :])
    column = jnp.concatenate([column] * steps, axis=0)
    shape = (steps * rows, lanes * per_message)
    out_row = iota(shape, 1)
    wanted = out_row // per_message * spots + out_row % spots
    pick = (wanted == column) & (out_row % per_message // spots == iota(shape, 0) // rows)
    pick = pick.astype(jnp.float32).astype(jnp.bfloat16)
    delta_ref[...] = jnp.dot(
        pick,
        jnp.concatenate([ref[...] for ref in delta_refs], axis=0),
        preferred_element_type=jnp.float32,
    )

    shape = (rows, BATCH * cache)
    lengths = as_column(length_ref[...])
    slot_column = iota(shape, 1)
    allowed = (slot_column // cache == iota(shape, 0) % BATCH) & (slot_column % cache < lengths)
    bias_ref[...] = jnp.where(allowed, 0.0, -1e30)
    shape = (steps, BATCH, known * BATCH)
    fresh_column = iota(shape, 2)
    allowed = (fresh_column % BATCH == iota(shape, 1)) & (
        fresh_column // BATCH <= iota(shape, 0) + before
    )
    fresh_bias = jnp.where(allowed, 0.0, -1e30)
    scale = HEAD_WIDTH ** (-0.5)
    transposed = (((1,), (1,)), ((), ()))

    def batch(index, carry):
        first = pl.multiple_of(index * BATCH, BATCH)
        spans = [pl.ds(pl.multiple_of(step * rows + first, BATCH), BATCH) for step in range(steps)]
        past = [pl.ds(pl.multiple_of(step * rows + first, BATCH), BATCH) for step in range(before)]
        for group in range(groups):
            query_tiles, key_tiles, value_tiles = [], [], []
            base = group * block_width
            lane_span = slice(group * HEAD_WIDTH, (group + 1) * HEAD_WIDTH)
            value_span = slice(wide + group * HEAD_WIDTH, wide + (group + 1) * HEAD_WIDTH)
            for span in past:
                key_tiles.append(earlier_ref[span, lane_span])
                value_tiles.append(earlier_ref[span, value_span])
            for span in spans:
                cosine, sine_part = cos_ref[span, :], sin_ref[span, :]

                def rotated(values):
                    return values * cosine + pltpu.roll(values, HEAD_WIDTH // 2, 1) * sine_part

                for head in range(PER_GROUP):
                    begin = head * HEAD_WIDTH
                    from_qkv = slice(base + begin, base + begin + HEAD_WIDTH)
                    begin += group * query_width
                    from_delta = slice(begin, begin + HEAD_WIDTH)
                    query_tiles.append(
                        rotated(qkv_ref[span, from_qkv] + delta_ref[span, from_delta])
                    )
                begin = base + query_width
                key = rotated(qkv_ref[span, begin : begin + HEAD_WIDTH])
                begin += HEAD_WIDTH
                from_delta = groups * query_width + group * HEAD_WIDTH
                value = (
                    qkv_ref[span, begin : begin + HEAD_WIDTH]
                    + delta_ref[span, from_delta : from_delta + HEAD_WIDTH]
                )
                if not last:
                    fresh_ref[span, lane_span] = key
                    fresh_ref[span, value_span] = value
                key_tiles.append(key)
                value_tiles.append(value)
            queries = jnp.concatenate(query_tiles, axis=0).astype(jnp.bfloat16)
            new_keys = jnp.concatenate(key_tiles, axis=0).astype(jnp.bfloat16)
            new_values = jnp.concatenate(value_tiles, axis=0).astype(jnp.bfloat16)
            old_keys = key_ref[pl.ds(first, BATCH), :, lane_span]
            old_keys = old_keys.reshape(BATCH * cache, HEAD_WIDTH)
            old_values = value_ref[pl.ds(first, BATCH), :, lane_span]
            old_values = old_values.reshape(BATCH * cache, HEAD_WIDTH)
            old_scores = lax.dot_general(
                queries, old_keys, transposed, preferred_element_type=jnp.float32
            )
            new_scores = lax.dot_general(
                queries, new_keys, transposed, preferred_element_type=jnp.float32
            )
            heads = steps * PER_GROUP
            old_scores = (old_scores * scale).reshape(heads, BATCH, BATCH * cache) + bias_ref[
                pl.ds(first, BATCH), :
            ][None]
            new_scores = (new_scores * scale).reshape(
                steps, PER_GROUP, BATCH, known * BATCH
            ) + fresh_bias[:, None]
            new_scores = new_scores.reshape(heads, BATCH, known * BATCH)
            peak = jnp.maximum(
                jnp.max(old_scores, axis=-1, keepdims=True),
                jnp.max(new_scores, axis=-1, keepdims=True),
            )
            old_scores = jnp.exp(old_scores - peak)
            new_scores = jnp.exp(new_scores - peak)
            share = 1.0 / (
                jnp.sum(old_scores, axis=-1, keepdims=True)
                + jnp.sum(new_scores, axis=-1, keepdims=True)
            )
            old_weights = (old_scores * share).reshape(heads * BATCH, BATCH * cache)
            new_weights = (new_scores * share).reshape(heads * BATCH, known * BATCH)
            context = jnp.dot(
                old_weights.astype(jnp.bfloat16), old_values, preferred_element_type=jnp.float32
            ) + jnp.dot(
                new_weights.astype(jnp.bfloat16), new_values, preferred_element_type=jnp.float32
            )
            for step, span in enumerate(spans):
                for head in range(PER_GROUP):
                    row = (step * PER_GROUP + head) * BATCH
                    begin = group * query_width + head * HEAD_WIDTH
                    context_ref[span, begin : begin + HEAD_WIDTH] = context[row : row + BATCH]
        return carry

    lax.fori_loop(0, rows // BATCH, batch, 0)

    flow_places = jnp.concatenate([places_ref[1:2, :]] * steps, axis=1)
    context = context_ref[...].astype(jnp.bfloat16)
    count = message_refs[0].shape[0]
    most = count // (lanes * steps)
    shape = (count, steps * rows)
    out_row = iota(shape, 0)
    spot = out_row // steps
    same_step = out_row % steps == iota(shape, 1) // rows
    for number, message_ref in enumerate(message_refs):
        wanted = (spot // most * subs + number) * most + spot % most
        pick = ((flow_places == wanted) & same_step).astype(jnp.float32).astype(jnp.bfloat16)
        message_ref[...] = jnp.dot(
            pick, context, preferred_element_type=jnp.float32
        ).astype(jnp.bfloat16)


def place_kernel(chunks, lanes, subs, most, *refs):
    out_ref = refs[-1]
    steps = out_ref.shape[1]
    chunk_steps = steps // chunks
    block = most * chunk_steps
    per_chunk = subs + lanes - 1
    here = lax.axis_index("streams")
    core = lax.axis_index("sub")
    shape = (chunks * block, chunks * block)
    out_row, in_row = iota(shape, 0), iota(shape, 1)
    step = out_row % steps
    wanted = step // chunk_steps * block + out_row // steps * chunk_steps + step % chunk_steps
    pick = (wanted == in_row).astype(jnp.float32).astype(jnp.bfloat16)
    for number in range(lanes):
        for other in range(subs):
            pieces = []
            for chunk in range(chunks):
                mine = refs[chunk * per_chunk : (chunk + 1) * per_chunk]
                if number == 0:
                    pieces.append(mine[other][...][:block])
                else:
                    landed = mine[subs + number - 1]
                    pieces.append(landed[...][other * block : (other + 1) * block])
            rows = jnp.dot(
                pick, jnp.concatenate(pieces, axis=0), preferred_element_type=jnp.float32
            )
            source = (here ^ number) * subs + (core ^ other)
            out_ref[pl.ds(source * most, most)] = rows.reshape(
                most, steps, rows.shape[1]
            ).astype(jnp.bfloat16)


def traded(blocks, axes):
    landed = list(blocks)
    count = len(blocks)
    order = sorted(range(1, count), key=lambda shift: -(shift ^ (shift >> 1)))
    for shift in order:
        pairs = [(place, place ^ shift) for place in range(count)]
        landed[shift] = lax.ppermute(blocks[shift], axes, pairs)
    return landed


def from_others(block, axis):
    count = lax.axis_size(axis)
    landed = [block]
    for shift in range(1, count):
        pairs = [(place, place ^ shift) for place in range(count)]
        landed.append(lax.ppermute(block, axis, pairs))
    return landed


def cost(flops, size):
    return pl.CostEstimate(flops=int(flops), bytes_accessed=int(size), transcendentals=0)


def on_device(
    inputs,
    input_norm_gain,
    projection_weight,
    projection_bias,
    speaker,
    speaker_adapter_slot,
    cache_fill_length,
    rotated_key_cache,
    value_cache_rows,
    adapter_down_maps,
    adapter_query_up,
    adapter_value_up,
    flow_decoder_owner,
):
    steps, rows, width = inputs.shape
    lanes = lax.axis_size("streams")
    subs = lax.axis_size("sub")
    heads = lax.axis_size("heads")
    flow_lanes = lanes * subs
    local_slots, sliced, _ = adapter_down_maps.shape
    query_columns = adapter_query_up.shape[2]
    value_columns = adapter_value_up.shape[2]
    groups = value_columns // HEAD_WIDTH
    cache = rotated_key_cache.shape[1]
    spots = subs * local_slots * MOST
    chunks = 2
    chunk_steps = steps // chunks
    chunk_rows = chunk_steps * rows
    per_message = chunk_steps * spots
    chip_slots = subs * local_slots
    flow_most = max(2, (2 * rows + flow_lanes - 1) // flow_lanes)
    bf16, f32 = jnp.bfloat16, jnp.float32

    def whole(shape):
        return pl.BlockSpec(shape, lambda i: (0,) * len(shape))

    down_maps = lax.all_gather(adapter_down_maps, "sub", axis=0, tiled=True)
    query_maps = lax.all_gather(
        adapter_query_up.reshape(local_slots * ADAPTER_RANK, query_columns),
        "sub",
        axis=0,
        tiled=True,
    )
    value_maps = lax.all_gather(
        adapter_value_up.reshape(local_slots * ADAPTER_RANK, value_columns),
        "sub",
        axis=0,
        tiled=True,
    )

    flat = inputs.reshape(steps * rows, width)
    gain = input_norm_gain.reshape(width // 128, 128)
    row_block = [
        pl.BlockSpec((chunk_rows, width), lambda i, chunk=chunk: (chunk, 0))
        for chunk in range(chunks)
    ]
    message = jax.ShapeDtypeStruct((per_message, sliced), bf16)
    normed_shape = jax.ShapeDtypeStruct((steps * rows, width), bf16)
    places_shape = jax.ShapeDtypeStruct((8, rows), jnp.int32)
    tables = [
        speaker.reshape(1, rows),
        speaker_adapter_slot.reshape(1, -1),
        flow_decoder_owner.reshape(1, rows),
    ]
    packing = dict(
        grid=(1,),
        compiler_params=pltpu.CompilerParams(vmem_limit_bytes=56 * MIB),
        cost_estimate=cost(2 * lanes * per_message * chunk_rows * sliced, 3 * MIB),
    )
    normed, places, *messages = pl.pallas_call(
        functools.partial(pack_kernel, chunk_steps, rows, flow_most, True),
        in_specs=[whole(table.shape) for table in tables] + [whole(gain.shape), row_block[0]],
        out_specs=[row_block[0], whole(places_shape.shape)] + [whole(message.shape)] * lanes,
        out_shape=[normed_shape, places_shape] + [message] * lanes,
        name="norm_and_pack",
        **packing,
    )(*tables, gain, flat)
    arrived = [traded(messages, "streams")]
    packed = []
    for chunk in range(1, chunks):
        normed, *messages = pl.pallas_call(
            functools.partial(pack_kernel, chunk_steps, rows, flow_most, False),
            in_specs=[whole(places.shape), whole(gain.shape), row_block[chunk]]
            + [pl.BlockSpec(memory_space=pl.ANY)],
            out_specs=[row_block[chunk]] + [whole(message.shape)] * lanes,
            out_shape=[normed_shape] + [message] * lanes,
            input_output_aliases={3: 0},
            name="norm_and_pack_next",
            **packing,
        )(places, gain, flat, normed)
        packed.append(messages)

    qkv = jnp.dot(normed, projection_weight, preferred_element_type=f32) + projection_bias
    qkv, packed = lax.optimization_barrier((qkv, packed))
    arrived += [traded(messages, "streams") for messages in packed]

    half_width = HEAD_WIDTH // 2
    position = jnp.concatenate([cache_fill_length + step for step in range(steps)]).astype(f32)
    freq = jnp.exp(jnp.arange(half_width, dtype=f32) * (-math.log(1000000.0) / half_width))
    freq = jnp.concatenate([freq, freq])
    angle = position[:, None] * freq
    sign = jnp.where(jnp.arange(HEAD_WIDTH) < half_width, -1.0, 1.0).astype(f32)
    cosine = jnp.cos(angle)
    sine_part = jnp.sin(angle) * sign

    returned = []
    for chunk in range(chunks):
        partial_latent = pl.pallas_call(
            functools.partial(down_kernel, lanes, spots),
            in_specs=[VMEM] * (lanes + 1),
            out_specs=VMEM,
            out_shape=jax.ShapeDtypeStruct((lanes * per_message, 2 * ADAPTER_RANK), f32),
            compiler_params=pltpu.CompilerParams(vmem_limit_bytes=16 * MIB),
            cost_estimate=cost(2 * lanes * per_message * sliced * 128 * chip_slots, 4 * MIB),
            name="down",
        )(*arrived[chunk], down_maps)
        partials = from_others(partial_latent, "heads")
        message = jax.ShapeDtypeStruct((per_message, query_columns + value_columns), bf16)
        messages = pl.pallas_call(
            functools.partial(up_kernel, heads, spots),
            in_specs=[VMEM] * (heads + 2),
            out_specs=[VMEM] * lanes,
            out_shape=[message] * lanes,
            compiler_params=pltpu.CompilerParams(vmem_limit_bytes=24 * MIB),
            cost_estimate=cost(
                2 * lanes * per_message * chip_slots * 64 * message.shape[1], 3 * MIB
            ),
            name="up",
        )(*partials, query_maps, value_maps)
        returned.append(traded(messages, "streams"))

    length_row = cache_fill_length.reshape(1, rows)
    block = flow_most * chunk_steps
    earlier = []
    landed = []
    for chunk in range(chunks):
        last = chunk == chunks - 1
        message = jax.ShapeDtypeStruct((lanes * block, query_columns), bf16)
        fresh = jax.ShapeDtypeStruct((chunk_rows, 2 * value_columns), f32)
        rows_of = lambda shape: pl.BlockSpec(shape, lambda i, chunk=chunk: (chunk, 0))
        results = pl.pallas_call(
            functools.partial(
                attend_kernel,
                chunk * chunk_steps,
                chunk_steps,
                rows,
                cache,
                groups,
                lanes,
                subs,
                last,
            ),
            grid=(1,),
            in_specs=[whole(places.shape), whole(length_row.shape)]
            + [rows_of((chunk_rows, HEAD_WIDTH))] * 2
            + [rows_of((chunk_rows, qkv.shape[1]))]
            + [whole(rotated_key_cache.shape)] * 2
            + [whole((per_message, query_columns + value_columns))] * lanes
            + [whole(block_rows.shape) for block_rows in earlier],
            out_specs=[whole(fresh.shape)] * (not last) + [whole(message.shape)] * subs,
            out_shape=[fresh] * (not last) + [message] * subs,
            scratch_shapes=[
                pltpu.VMEM((chunk_rows, query_columns + value_columns), f32),
                pltpu.VMEM((chunk_rows, query_columns), f32),
                pltpu.VMEM((rows, BATCH * cache), f32),
            ],
            compiler_params=pltpu.CompilerParams(vmem_limit_bytes=32 * MIB),
            cost_estimate=cost(2e9, 6 * MIB),
            name="attend",
        )(
            places,
            length_row,
            cosine,
            sine_part,
            qkv,
            rotated_key_cache,
            value_cache_rows,
            *returned[chunk],
            *earlier,
        )
        if not last:
            earlier, results = [results[0]], results[1:]
        parts = [results[0]]
        for shift in range(1, subs):
            pairs = [(core, core ^ shift) for core in range(subs)]
            parts.append(lax.ppermute(results[shift], "sub", pairs))
        joined = [
            jnp.concatenate([part[lane * block : (lane + 1) * block] for part in parts])
            for lane in range(1, lanes)
        ]
        landed += parts + traded([None] + joined, "streams")[1:]

    flow = pl.pallas_call(
        functools.partial(place_kernel, chunks, lanes, subs, flow_most),
        in_specs=[VMEM] * len(landed),
        out_specs=VMEM,
        out_shape=jax.ShapeDtypeStruct((flow_lanes * flow_most, steps, query_columns), bf16),
        compiler_params=pltpu.CompilerParams(vmem_limit_bytes=24 * MIB),
        cost_estimate=cost(0, 4 * MIB),
        name="place",
    )(*landed)
    return flow[None]


def solution(mesh):
    placed = (
        P(None, ("groups", "streams", "sub"), None),
        P(),
        P(None, "heads"),
        P("heads"),
        P(("groups", "streams", "sub"), None),
        P("groups"),
        P(("groups", "streams", "sub")),
        P(("groups", "streams", "sub"), None, "heads"),
        P(("groups", "streams", "sub"), None, "heads"),
        P(("groups", "streams", "sub"), "heads", None),
        P(("groups", "streams", "sub"), None, "heads"),
        P(("groups", "streams", "sub"), None, "heads"),
        P(("groups", "streams", "sub"), None),
    )
    return jax.shard_map(
        on_device,
        mesh=mesh,
        in_specs=placed,
        out_specs=P(("groups", "streams", "sub"), None, None, "heads"),
        check_vma=False,
    )
```

time: 180 us -> 152 us (0.84); the launches traced: 177 us -> 151 us
  Pallas kernels: 78.8 us -> 28.6 us
  waiting for transfers between devices: 21.7 us -> 41.4 us
  between operations: 0.41 us -> 13.7 us
  starting transfers between devices: 53.9 us -> 47 us
  local copies, waits for them, and re-layouts: 10.4 us -> 3.7 us
  matrix products: 9.69 us -> 14.1 us
  blocking collectives: 0 us -> 2.16 us
    pallas_call x7, Pallas kernels: 76.5 us -> 26.3 us  [the longest x2 16.3 us: on_device(): pl.pallas_call(functools.partial(attend_kernel, chunk * chunk_steps, chun...]
    ppermute x29 -> x18, waiting for transfers between devices: 21.7 us -> 38.8 us  [traded(): landed[shift] = lax.ppermute(blocks[shift], axes, pairs)]
    ppermute x29 -> x18, starting transfers between devices: 49.9 us -> 44.2 us  [traded(): landed[shift] = lax.ppermute(blocks[shift], axes, pairs)]
    unnamed x74 -> x38, local copies, waits for them, and re-layouts: 8.32 us -> 3.61 us
    dot_general x1, matrix products: 9.69 us -> 14.1 us  [on_device(): jnp.dot(normed, projection_weight, preferred_element_type=f32)]
    all_gather x0 -> x1, blocking collectives: none -> 2.16 us  [on_device(): lax.all_gather(adapter_value_up.reshape(local_slots * ADAPTER_RANK, value...]
    ppermute x5 -> x2, starting transfers between devices: 3.98 us -> 2.16 us  [from_others(): landed.append(lax.ppermute(block, axis, pairs))]
  transfers between devices with their start and end apart: 34 -> 24, of which waited for: 6 -> 8; matrix products, arithmetic and copies ran while one was open for 8% -> 10% of each run, Pallas kernels for 12% -> 12%
where the time goes in v3:
time: 152 us; the launch traced here: 151 us
  starting transfers between devices  47 us (31%)
  waiting for transfers between devices  41.4 us (27%)
  Pallas kernels  28.6 us (19%)
  matrix products  14.1 us (9%)
  between operations  13.7 us (9%)
  local copies, waits for them, and re-layouts  3.7 us (2%)
  blocking collectives  2.16 us (1%)
    ppermute x18, starting transfers between devices, traded(): landed[shift] = lax.ppermute(blocks[shift], axes, pairs)  44.2 us
    ppermute x18, waiting for transfers between devices, traded(): landed[shift] = lax.ppermute(blocks[shift], axes, pairs)  38.8 us
    pallas_call x2, Pallas kernels, on_device(): pl.pallas_call(functools.partial(attend_kernel, chunk * chunk_steps, chun...  16.3 us
    dot_general x1, matrix products, on_device(): jnp.dot(normed, projection_weight, preferred_element_type=f32)  14.1 us
    pallas_call x2, Pallas kernels, on_device(): pl.pallas_call(functools.partial(pack_kernel, chunk_steps, rows, flow_mos...  7.16 us
    unnamed x38, local copies, waits for them, and re-layouts  3.61 us
  transfers between devices with their start and end apart: 24, of which 8 were waited for; matrix products, arithmetic and copies ran while one was open for 10% of the time, Pallas kernels for 12%

profile of v3, /device:TPU:0, one launch (start us, length us, event | category | flops | bytes accessed | tf_op | source)
XLA Modules:
  0.0 151.5 jit_solution(7683392339775930082)
XLA Ops:
  6.5 0.7 all-gather.3.cloned.1.call-update
  7.3 0.7 all-gather.5.cloned.1.call-update
  8.0 3.7 %norm_and_pack.1 = (bf16[256,3584]{1,0:T(8,128)(2,1)}, s32[8,64]{1,0:T(8,128)}, bf16[32,1792]{1,0:T(8,128)(2,1)}, bf16[32,1792]{1,0:T(8,128)(2,1)}, bf16[32,1792]{1,0:T(8,128)(2,1)}, /*index=5*/bf16[32,1792]{1,0:T(8,128)(2,1)}) custom-call(s32[1,64]{1,0:T(1,128)} %bitcast.19, s32[1,32]{1,0:T(1,128)} %bitcast.20, s32[1,64]{1,0:T(1,128)} %bitcast.21, ...), custom_call_target="tpu_custom_call" | custom-call | flops 58720256 | bytes 3145728 | tf_op jit(solution)/shard_map/norm_and_pack/pallas_call | solution.py:410
  11.7 3.4 %norm_and_pack_next.1 = (bf16[256,3584]{1,0:T(8,128)(2,1)}, bf16[32,1792]{1,0:T(8,128)(2,1)}, bf16[32,1792]{1,0:T(8,128)(2,1)}, bf16[32,1792]{1,0:T(8,128)(2,1)}, bf16[32,1792]{1,0:T(8,128)(2,1)}) custom-call(s32[8,64]{1,0:T(8,128)} %get-tuple-element.34.refs_0_, f32[28,128]{1,0:T(8,128)} %bitcast.18, ...), custom_call_target="tpu_custom_call", output_to_operand_aliasing={{0}: (3, {})} | custom-call | flops 58720256 | bytes 3145728 | tf_op jit(solution)/shard_map/norm_and_pack_next/pallas_call | solution.py:421
  15.3 14.1 %convolution_add_fusion.refs_4_ = f32[256,2304]{1,0:T(8,128)} fusion(bf16[256,3584]{1,0:T(8,128)(2,1)} %get-tuple-element.36, bf16[3584,2304]{1,0:T(8,128)(2,1)} %param.15, f32[2304]{0:T(1024)S(1)} %copy-done.18), kind=kOutput, calls=%fused_computation | convolution fusion | flops 4228448256 | bytes 20718592 | tf_op jit(solution)/shard_map/dot_general | solution.py:433
  29.4 3.0 %collective-permute-start.11 = (bf16[32,1792]{1,0:T(8,128)(2,1)S(1)}, bf16[32,1792]{1,0:T(8,128)(2,1)S(1)}, u32[]{:S(2)}, u32[]{:S(2)}) collective-permute-start(bf16[32,1792]{1,0:T(8,128)(2,1)S(1)} %copy-done.14), channel_id=1, source_target_pairs={{0,4},{4,0},{8,12},{12,8},{1,5},{5,1},{9,13},{13,9},{2,6},{6,2},{1... | collective-permute-start | bytes 344072 | tf_op jit(solution)/shard_map/ppermute | solution.py:323
  32.4 2.6 %collective-permute-start.12 = (bf16[32,1792]{1,0:T(8,128)(2,1)S(1)}, bf16[32,1792]{1,0:T(8,128)(2,1)S(1)}, u32[]{:S(2)}, u32[]{:S(2)}) collective-permute-start(bf16[32,1792]{1,0:T(8,128)(2,1)S(1)} %copy-done.13), channel_id=1, source_target_pairs={{0,8},{4,12},{8,0},{12,4},{1,9},{5,13},{9,1},{13,5},{2,10},{6,14},... | collective-permute-start | bytes 344072 | tf_op jit(solution)/shard_map/ppermute | solution.py:323
  35.0 0.5 collective-permute-start
  35.5 0.1 collective-permute-start.1
  35.5 3.9 %collective-permute-start.2 = (bf16[32,1792]{1,0:T(8,128)(2,1)S(1)}, bf16[32,1792]{1,0:T(8,128)(2,1)S(1)}, u32[]{:S(2)}, u32[]{:S(2)}) collective-permute-start(bf16[32,1792]{1,0:T(8,128)(2,1)S(1)} %copy-done.15), channel_id=1, source_target_pairs={{0,12},{4,8},{8,4},{12,0},{1,13},{5,9},{9,5},{13,1},{2,14},{6,10},... | collective-permute-start | bytes 344072 | tf_op jit(solution)/shard_map/ppermute | solution.py:323
  39.4 0.1 compare_select_fusion
  39.5 2.3 %collective-permute-done.refs_1_ = bf16[32,1792]{1,0:T(8,128)(2,1)S(1)} collective-permute-done((bf16[32,1792]{1,0:T(8,128)(2,1)S(1)}, bf16[32,1792]{1,0:T(8,128)(2,1)S(1)}, u32[]{:S(2)}, u32[]{:S(2)}) %collective-permute-start) | collective-permute-done | bytes 114720 | tf_op jit(solution)/shard_map/ppermute | solution.py:323
  41.8 3.7 %collective-permute-start.13 = (bf16[32,1792]{1,0:T(8,128)(2,1)S(1)}, bf16[32,1792]{1,0:T(8,128)(2,1)S(1)}, u32[]{:S(2)}, u32[]{:S(2)}) collective-permute-start(bf16[32,1792]{1,0:T(8,128)(2,1)S(1)} %copy-done.12), channel_id=1, source_target_pairs={{0,12},{4,8},{8,4},{12,0},{1,13},{5,9},{9,5},{13,1},{2,14},{6,10},... | collective-permute-start | bytes 344072 | tf_op jit(solution)/shard_map/ppermute | solution.py:323
  45.5 0.1 add_convert_fusion
  45.6 5.3 %collective-permute-done.1.refs_2_ = bf16[32,1792]{1,0:T(8,128)(2,1)S(1)} collective-permute-done((bf16[32,1792]{1,0:T(8,128)(2,1)S(1)}, bf16[32,1792]{1,0:T(8,128)(2,1)S(1)}, u32[]{:S(2)}, u32[]{:S(2)}) %collective-permute-start.1) | collective-permute-done | bytes 114720 | tf_op jit(solution)/shard_map/ppermute | solution.py:323
  51.0 2.0 %copy-done = bf16[8,1792,128]{2,1,0:T(8,128)(2,1)S(1)} copy-done((bf16[8,1792,128]{2,1,0:T(8,128)(2,1)S(1)}, bf16[8,1792,128]{2,1,0:T(8,128)(2,1)}, u32[]{:S(2)}) %copy-start) | copy-done | bytes 3670040
  53.0 1.1 down.2.refs_0_
  54.1 1.6 %collective-permute-start.3 = (f32[128,128]{1,0:T(8,128)S(1)}, f32[128,128]{1,0:T(8,128)S(1)}, u32[]{:S(2)}, u32[]{:S(2)}) collective-permute-start(f32[128,128]{1,0:T(8,128)S(1)} %down.2.refs_0_), channel_id=1, source_target_pairs={{0,2},{2,0},{1,3},{3,1},{4,6},{6,4},{5,7},{7,5},{8,10},{10,8},{9,1... | collective-permute-start | bytes 196616 | tf_op jit(solution)/shard_map/ppermute | solution.py:332
  55.7 2.2 %all_gather.11.refs_3_ = bf16[512,256]{1,0:T(8,128)(2,1)S(1)} all-gather(bf16[256,256]{1,0:T(8,128)(2,1)S(1)} %bitcast.16), channel_id=1, replica_groups=mesh['groups'=2,'streams'=4,'heads'=2,'sub'=2] {'sub'}, dimensions={0}, use_global_device_ids=true | all-gather | bytes 393216 | tf_op jit(solution)/shard_map/all_gather | solution.py:384
  57.9 1.1 down.3.refs_0_
  59.1 0.6 collective-permute-start.14
  59.7 1.5 copy-done.2
  61.2 0.5 up.2
  61.7 3.1 %collective-permute-start.4 = (bf16[32,2048]{1,0:T(8,128)(2,1)S(1)}, bf16[32,2048]{1,0:T(8,128)(2,1)S(1)}, u32[]{:S(2)}, u32[]{:S(2)}) collective-permute-start(bf16[32,2048]{1,0:T(8,128)(2,1)S(1)} %get-tuple-element.47), channel_id=1, source_target_pairs={{0,4},{4,0},{8,12},{12,8},{1,5},{5,1},{9,13},{13,9},{2,6},{6,2},{1... | collective-permute-start | bytes 393224 | tf_op jit(solution)/shard_map/ppermute | solution.py:323
  64.8 1.6 %collective-permute-start.5 = (bf16[32,2048]{1,0:T(8,128)(2,1)S(1)}, bf16[32,2048]{1,0:T(8,128)(2,1)S(1)}, u32[]{:S(2)}, u32[]{:S(2)}) collective-permute-start(bf16[32,2048]{1,0:T(8,128)(2,1)S(1)} %get-tuple-element.48), channel_id=1, source_target_pairs={{0,8},{4,12},{8,0},{12,4},{1,9},{5,13},{9,1},{13,5},{2,10},{6,14},... | collective-permute-start | bytes 393224 | tf_op jit(solution)/shard_map/ppermute | solution.py:323
  66.4 1.4 collective-permute-start.6
  67.8 0.5 fusion
  68.3 0.5 up.3
  68.8 0.6 collective-permute-start.15
  69.5 2.4 %collective-permute-start.16 = (bf16[32,2048]{1,0:T(8,128)(2,1)S(1)}, bf16[32,2048]{1,0:T(8,128)(2,1)S(1)}, u32[]{:S(2)}, u32[]{:S(2)}) collective-permute-start(bf16[32,2048]{1,0:T(8,128)(2,1)S(1)} %get-tuple-element.58), channel_id=1, source_target_pairs={{0,8},{4,12},{8,0},{12,4},{1,9},{5,13},{9,1},{13,5},{2,10},{6,14},... | collective-permute-start | bytes 393224 | tf_op jit(solution)/shard_map/ppermute | solution.py:323
  71.9 1.4 collective-permute-start.17
  73.3 3.7 %collective-permute-done.5.refs_9_ = bf16[32,2048]{1,0:T(8,128)(2,1)S(1)} collective-permute-done((bf16[32,2048]{1,0:T(8,128)(2,1)S(1)}, bf16[32,2048]{1,0:T(8,128)(2,1)S(1)}, u32[]{:S(2)}, u32[]{:S(2)}) %collective-permute-start.5) | collective-permute-done | bytes 131104 | tf_op jit(solution)/shard_map/ppermute | solution.py:323
  77.0 0.8 collective-permute-done.6.refs_10_
  77.8 8.1 %attend.2 = (f32[128,512]{1,0:T(8,128)S(1)}, bf16[128,1792]{1,0:T(8,128)(2,1)S(1)}, bf16[128,1792]{1,0:T(8,128)(2,1)S(1)}) custom-call(s32[8,64]{1,0:T(8,128)S(1)} %copy-done.6, s32[1,64]{1,0:T(1,128)S(1)} %bitcast.11, f32[256,128]{1,0:T(8,128)S(1)} %get-tuple-element.76.refs_2_, f32[256,128]{1,0:T(8,128)S(1)} %get-tuple-element.75.refs_3_, ...), custom_call_target="tpu_custom_call" | custom-call | flops 2000000000 | bytes 6291456 | tf_op jit(solution)/shard_map/attend/pallas_call | solution.py:481
  86.0 2.7 %collective-permute-done.16.refs_9_ = bf16[32,2048]{1,0:T(8,128)(2,1)S(1)} collective-permute-done((bf16[32,2048]{1,0:T(8,128)(2,1)S(1)}, bf16[32,2048]{1,0:T(8,128)(2,1)S(1)}, u32[]{:S(2)}, u32[]{:S(2)}) %collective-permute-start.16) | collective-permute-done | bytes 131104 | tf_op jit(solution)/shard_map/ppermute | solution.py:323
  88.6 8.1 %attend.3 = (bf16[128,1792]{1,0:T(8,128)(2,1)S(1)}, bf16[128,1792]{1,0:T(8,128)(2,1)S(1)}) custom-call(s32[8,64]{1,0:T(8,128)S(1)} %copy-done.6, s32[1,64]{1,0:T(1,128)S(1)} %bitcast.12, f32[256,128]{1,0:T(8,128)S(1)} %get-tuple-element.76.refs_2_, f32[256,128]{1,0:T(8,128)S(1)} %get-tuple-element.75.refs_3_, f32[256,2304]{1,0:T(8,128)S(1)} %copy-done.10, ...), custom_call_target="tpu_custom_call" | custom-call | flops 2000000000 | bytes 6291456 | tf_op jit(solution)/shard_map/attend/pallas_call | solution.py:481
  96.8 0.1 collective-permute-start.18
  96.9 0.6 collective-permute-start.7
  97.5 1.2 collective-permute-done.18.refs_6_
  98.7 2.6 %collective-permute-start.21 = (bf16[64,1792]{1,0:T(8,128)(2,1)S(1)}, bf16[64,1792]{1,0:T(8,128)(2,1)S(1)}, u32[]{:S(2)}, u32[]{:S(2)}) collective-permute-start(bf16[64,1792]{1,0:T(8,128)(2,1)S(1)} %pad_maximum_fusion.5), channel_id=1, source_target_pairs={{0,12},{4,8},{8,4},{12,0},{1,13},{5,9},{9,5},{13,1},{2,14},{6,10},... | collective-permute-start | bytes 688136 | tf_op jit(solution)/shard_map/ppermute | solution.py:323
  101.4 4.9 %collective-permute-start.20 = (bf16[64,1792]{1,0:T(8,128)(2,1)S(1)}, bf16[64,1792]{1,0:T(8,128)(2,1)S(1)}, u32[]{:S(2)}, u32[]{:S(2)}) collective-permute-start(bf16[64,1792]{1,0:T(8,128)(2,1)S(1)} %pad_maximum_fusion.4), channel_id=1, source_target_pairs={{0,8},{4,12},{8,0},{12,4},{1,9},{5,13},{9,1},{13,5},{2,10},{6,14},... | collective-permute-start | bytes 688136 | tf_op jit(solution)/shard_map/ppermute | solution.py:323
  106.3 0.3 collective-permute-start.19
  106.7 2.4 %collective-permute-start.10 = (bf16[64,1792]{1,0:T(8,128)(2,1)S(1)}, bf16[64,1792]{1,0:T(8,128)(2,1)S(1)}, u32[]{:S(2)}, u32[]{:S(2)}) collective-permute-start(bf16[64,1792]{1,0:T(8,128)(2,1)S(1)} %pad_maximum_fusion.2), channel_id=1, source_target_pairs={{0,12},{4,8},{8,4},{12,0},{1,13},{5,9},{9,5},{13,1},{2,14},{6,10},... | collective-permute-start | bytes 688136 | tf_op jit(solution)/shard_map/ppermute | solution.py:323
  109.1 0.9 collective-permute-start.9
  110.1 8.7 %collective-permute-start.8 = (bf16[64,1792]{1,0:T(8,128)(2,1)S(1)}, bf16[64,1792]{1,0:T(8,128)(2,1)S(1)}, u32[]{:S(2)}, u32[]{:S(2)}) collective-permute-start(bf16[64,1792]{1,0:T(8,128)(2,1)S(1)} %pad_maximum_fusion), channel_id=1, source_target_pairs={{0,4},{4,0},{8,12},{12,8},{1,5},{5,1},{9,13},{13,9},{2,6},{6,2},{1... | collective-permute-start | bytes 688136 | tf_op jit(solution)/shard_map/ppermute | solution.py:323
  118.8 14.2 %collective-permute-done.20.refs_8_ = bf16[64,1792]{1,0:T(8,128)(2,1)S(1)} collective-permute-done((bf16[64,1792]{1,0:T(8,128)(2,1)S(1)}, bf16[64,1792]{1,0:T(8,128)(2,1)S(1)}, u32[]{:S(2)}, u32[]{:S(2)}) %collective-permute-start.20) | collective-permute-done | bytes 229408 | tf_op jit(solution)/shard_map/ppermute | solution.py:323
  132.9 9.7 %collective-permute-done.9.refs_3_ = bf16[64,1792]{1,0:T(8,128)(2,1)S(1)} collective-permute-done((bf16[64,1792]{1,0:T(8,128)(2,1)S(1)}, bf16[64,1792]{1,0:T(8,128)(2,1)S(1)}, u32[]{:S(2)}, u32[]{:S(2)}) %collective-permute-start.9) | collective-permute-done | bytes 229408 | tf_op jit(solution)/shard_map/ppermute | solution.py:323
  142.7 1.9 %place.1 = bf16[128,4,1792]{2,1,0:T(4,128)(2,1)} custom-call(bf16[128,1792]{1,0:T(8,128)(2,1)S(1)} %get-tuple-element.50.refs_0_, bf16[128,1792]{1,0:T(8,128)(2,1)S(1)} %collective-permute-done.7.refs_1_, bf16[64,1792]{1,0:T(8,128)(2,1)S(1)} %collective-permute-done.8.refs_2_, bf16[64,1792]{1,0:T(8,128)(2,1)S(1)} %collective-permute-done.9.refs_3_, ...), custom_call_target="tpu_custom_call" | custom-call | bytes 4194304 | tf_op jit(solution)/shard_map/place/pallas_call | solution.py:533
  (66 shorter events, 0.4 us)
Async XLA Ops:
  6.5 44.4 %all-gather.3.cloned.1.call-start = ((), (), s32[]{:S(2)}) async-start(), calls=%async_computation | async-start | bytes 5505024 | tf_op jit(solution)/shard_map/all_gather | solution.py:377
  7.3 52.4 %all-gather.5.cloned.1.call-start = ((), (), s32[]{:S(2)}) async-start(), calls=%async_computation.1 | async-start | bytes 2752512 | tf_op jit(solution)/shard_map/all_gather | solution.py:378
  8.0 7.2 %copy-start.18 = (f32[2304]{0:T(1024)S(1)}, f32[2304]{0:T(1024)}, u32[]{:S(2)}) copy-start(f32[2304]{0:T(1024)} %param.16) | copy-start | bytes 27652
  15.2 14.2 %copy-start.14 = (bf16[32,1792]{1,0:T(8,128)(2,1)S(1)}, bf16[32,1792]{1,0:T(8,128)(2,1)}, u32[]{:S(2)}) copy-start(bf16[32,1792]{1,0:T(8,128)(2,1)} %get-tuple-element.53) | copy-start | bytes 344068
  15.2 17.2 %copy-start.13 = (bf16[32,1792]{1,0:T(8,128)(2,1)S(1)}, bf16[32,1792]{1,0:T(8,128)(2,1)}, u32[]{:S(2)}) copy-start(bf16[32,1792]{1,0:T(8,128)(2,1)} %get-tuple-element.54) | copy-start | bytes 344068
  15.2 19.8 %copy-start.17 = (bf16[32,1792]{1,0:T(8,128)(2,1)S(1)}, bf16[32,1792]{1,0:T(8,128)(2,1)}, u32[]{:S(2)}) copy-start(bf16[32,1792]{1,0:T(8,128)(2,1)} %get-tuple-element.43) | copy-start | bytes 344068
  15.2 20.3 %copy-start.16 = (bf16[32,1792]{1,0:T(8,128)(2,1)S(1)}, bf16[32,1792]{1,0:T(8,128)(2,1)}, u32[]{:S(2)}) copy-start(bf16[32,1792]{1,0:T(8,128)(2,1)} %get-tuple-element.44) | copy-start | bytes 344068
  15.2 20.3 %copy-start.15 = (bf16[32,1792]{1,0:T(8,128)(2,1)S(1)}, bf16[32,1792]{1,0:T(8,128)(2,1)}, u32[]{:S(2)}) copy-start(bf16[32,1792]{1,0:T(8,128)(2,1)} %get-tuple-element.45) | copy-start | bytes 344068
  15.2 24.2 %copy-start.7 = (s32[64]{0:T(128)S(1)}, s32[64]{0:T(128)}, u32[]{:S(2)}) copy-start(s32[64]{0:T(128)} %param.19) | copy-start | bytes 772
  15.2 26.6 %copy-start.12 = (bf16[32,1792]{1,0:T(8,128)(2,1)S(1)}, bf16[32,1792]{1,0:T(8,128)(2,1)}, u32[]{:S(2)}) copy-start(bf16[32,1792]{1,0:T(8,128)(2,1)} %get-tuple-element.55) | copy-start | bytes 344068
  15.2 35.7 %copy-start.5 = (bf16[32,1792]{1,0:T(8,128)(2,1)S(1)}, bf16[32,1792]{1,0:T(8,128)(2,1)}, u32[]{:S(2)}) copy-start(bf16[32,1792]{1,0:T(8,128)(2,1)} %get-tuple-element.42.refs_0_) | copy-start | bytes 344068
  15.2 40.5 %copy-start.11 = (bf16[4,64,256]{2,1,0:T(8,128)(2,1)S(1)}, bf16[4,64,256]{2,1,0:T(8,128)(2,1)}, u32[]{:S(2)}) copy-start(bf16[4,64,256]{2,1,0:T(8,128)(2,1)} %param.24) | copy-start | bytes 393220
  15.3 42.6 %copy-start.4 = (bf16[32,1792]{1,0:T(8,128)(2,1)S(1)}, bf16[32,1792]{1,0:T(8,128)(2,1)}, u32[]{:S(2)}) copy-start(bf16[32,1792]{1,0:T(8,128)(2,1)} %get-tuple-element.52.refs_0_) | copy-start | bytes 344068
  29.4 28.5 %collective-permute-start.11 = (bf16[32,1792]{1,0:T(8,128)(2,1)S(1)}, bf16[32,1792]{1,0:T(8,128)(2,1)S(1)}, u32[]{:S(2)}, u32[]{:S(2)}) collective-permute-start(bf16[32,1792]{1,0:T(8,128)(2,1)S(1)} %copy-done.14), channel_id=1, source_target_pairs={{0,4},{4,0},{8,12},{12,8},{1,5},{5,1},{9,13},{13,9},{2,6},{6,2},{1... | collective-permute-start | bytes 344072 | tf_op jit(solution)/shard_map/ppermute | solution.py:323
  32.4 25.5 %collective-permute-start.12 = (bf16[32,1792]{1,0:T(8,128)(2,1)S(1)}, bf16[32,1792]{1,0:T(8,128)(2,1)S(1)}, u32[]{:S(2)}, u32[]{:S(2)}) collective-permute-start(bf16[32,1792]{1,0:T(8,128)(2,1)S(1)} %copy-done.13), channel_id=1, source_target_pairs={{0,8},{4,12},{8,0},{12,4},{1,9},{5,13},{9,1},{13,5},{2,10},{6,14},... | collective-permute-start | bytes 344072 | tf_op jit(solution)/shard_map/ppermute | solution.py:323
  35.0 6.8 %collective-permute-start = (bf16[32,1792]{1,0:T(8,128)(2,1)S(1)}, bf16[32,1792]{1,0:T(8,128)(2,1)S(1)}, u32[]{:S(2)}, u32[]{:S(2)}) collective-permute-start(bf16[32,1792]{1,0:T(8,128)(2,1)S(1)} %copy-done.17), channel_id=1, source_target_pairs={{0,4},{4,0},{8,12},{12,8},{1,5},{5,1},{9,13},{13,9},{2,6},{6,2},{1... | collective-permute-start | bytes 344072 | tf_op jit(solution)/shard_map/ppermute | solution.py:323
  35.5 15.5 %collective-permute-start.1 = (bf16[32,1792]{1,0:T(8,128)(2,1)S(1)}, bf16[32,1792]{1,0:T(8,128)(2,1)S(1)}, u32[]{:S(2)}, u32[]{:S(2)}) collective-permute-start(bf16[32,1792]{1,0:T(8,128)(2,1)S(1)} %copy-done.16), channel_id=1, source_target_pairs={{0,8},{4,12},{8,0},{12,4},{1,9},{5,13},{9,1},{13,5},{2,10},{6,14},... | collective-permute-start | bytes 344072 | tf_op jit(solution)/shard_map/ppermute | solution.py:323
  35.5 15.4 %collective-permute-start.2 = (bf16[32,1792]{1,0:T(8,128)(2,1)S(1)}, bf16[32,1792]{1,0:T(8,128)(2,1)S(1)}, u32[]{:S(2)}, u32[]{:S(2)}) collective-permute-start(bf16[32,1792]{1,0:T(8,128)(2,1)S(1)} %copy-done.15), channel_id=1, source_target_pairs={{0,12},{4,8},{8,4},{12,0},{1,13},{5,9},{9,5},{13,1},{2,14},{6,10},... | collective-permute-start | bytes 344072 | tf_op jit(solution)/shard_map/ppermute | solution.py:323
  41.8 16.1 %collective-permute-start.13 = (bf16[32,1792]{1,0:T(8,128)(2,1)S(1)}, bf16[32,1792]{1,0:T(8,128)(2,1)S(1)}, u32[]{:S(2)}, u32[]{:S(2)}) collective-permute-start(bf16[32,1792]{1,0:T(8,128)(2,1)S(1)} %copy-done.12), channel_id=1, source_target_pairs={{0,12},{4,8},{8,4},{12,0},{1,13},{5,9},{9,5},{13,1},{2,14},{6,10},... | collective-permute-start | bytes 344072 | tf_op jit(solution)/shard_map/ppermute | solution.py:323
  51.0 2.0 %copy-start = (bf16[8,1792,128]{2,1,0:T(8,128)(2,1)S(1)}, bf16[8,1792,128]{2,1,0:T(8,128)(2,1)}, u32[]{:S(2)}) copy-start(bf16[8,1792,128]{2,1,0:T(8,128)(2,1)} %all-gather.3.cloned.1.call-done.refs_4_) | copy-start | bytes 11010052
  53.0 4.9 %copy-start.1 = (bf16[8,1792,128]{2,1,0:T(8,128)(2,1)S(1)}, bf16[8,1792,128]{2,1,0:T(8,128)(2,1)}, u32[]{:S(2)}) copy-start(bf16[8,1792,128]{2,1,0:T(8,128)(2,1)} %all-gather.3.cloned.1.call-done.refs_4_) | copy-start | bytes 11010052
  54.1 5.5 %collective-permute-start.3 = (f32[128,128]{1,0:T(8,128)S(1)}, f32[128,128]{1,0:T(8,128)S(1)}, u32[]{:S(2)}, u32[]{:S(2)}) collective-permute-start(f32[128,128]{1,0:T(8,128)S(1)} %down.2.refs_0_), channel_id=1, source_target_pairs={{0,2},{2,0},{1,3},{3,1},{4,6},{6,4},{5,7},{7,5},{8,10},{10,8},{9,1... | collective-permute-start | bytes 196616 | tf_op jit(solution)/shard_map/ppermute | solution.py:332
  57.9 19.9 %copy-start.6 = (s32[8,64]{1,0:T(8,128)S(1)}, s32[8,64]{1,0:T(8,128)}, u32[]{:S(2)}) copy-start(s32[8,64]{1,0:T(8,128)} %get-tuple-element.34.refs_0_) | copy-start | bytes 6148
  57.9 19.9 %copy-start.8 = (bf16[64,32,256]{2,1,0:T(8,128)(2,1)S(1)}, bf16[64,32,256]{2,1,0:T(8,128)(2,1)}, u32[]{:S(2)}) copy-start(bf16[64,32,256]{2,1,0:T(8,128)(2,1)} %refs_5_.3) | copy-start | bytes 3145732
  57.9 19.9 %copy-start.9 = (bf16[64,32,256]{2,1,0:T(8,128)(2,1)S(1)}, bf16[64,32,256]{2,1,0:T(8,128)(2,1)}, u32[]{:S(2)}) copy-start(bf16[64,32,256]{2,1,0:T(8,128)(2,1)} %refs_6_.3) | copy-start | bytes 3145732
  59.1 9.2 %collective-permute-start.14 = (f32[128,128]{1,0:T(8,128)S(1)}, f32[128,128]{1,0:T(8,128)S(1)}, u32[]{:S(2)}, u32[]{:S(2)}) collective-permute-start(f32[128,128]{1,0:T(8,128)S(1)} %down.3.refs_0_), channel_id=1, source_target_pairs={{0,2},{2,0},{1,3},{3,1},{4,6},{6,4},{5,7},{7,5},{8,10},{10,8},{9,1... | collective-permute-start | bytes 196616 | tf_op jit(solution)/shard_map/ppermute | solution.py:332
  59.7 1.5 copy-start.2
  61.2 7.2 %copy-start.3 = (bf16[512,1792]{1,0:T(8,128)(2,1)S(1)}, bf16[512,1792]{1,0:T(8,128)(2,1)}, u32[]{:S(2)}) copy-start(bf16[512,1792]{1,0:T(8,128)(2,1)} %all-gather.5.cloned.1.call-done.refs_2_) | copy-start | bytes 5505028
  61.2 16.6 %copy-start.10 = (f32[256,2304]{1,0:T(8,128)S(1)}, f32[256,2304]{1,0:T(8,128)}, u32[]{:S(2)}) copy-start(f32[256,2304]{1,0:T(8,128)} %convolution_add_fusion.refs_4_) | copy-start | bytes 7077892
  61.7 10.2 %collective-permute-start.4 = (bf16[32,2048]{1,0:T(8,128)(2,1)S(1)}, bf16[32,2048]{1,0:T(8,128)(2,1)S(1)}, u32[]{:S(2)}, u32[]{:S(2)}) collective-permute-start(bf16[32,2048]{1,0:T(8,128)(2,1)S(1)} %get-tuple-element.47), channel_id=1, source_target_pairs={{0,4},{4,0},{8,12},{12,8},{1,5},{5,1},{9,13},{13,9},{2,6},{6,2},{1... | collective-permute-start | bytes 393224 | tf_op jit(solution)/shard_map/ppermute | solution.py:323
  64.8 12.2 %collective-permute-start.5 = (bf16[32,2048]{1,0:T(8,128)(2,1)S(1)}, bf16[32,2048]{1,0:T(8,128)(2,1)S(1)}, u32[]{:S(2)}, u32[]{:S(2)}) collective-permute-start(bf16[32,2048]{1,0:T(8,128)(2,1)S(1)} %get-tuple-element.48), channel_id=1, source_target_pairs={{0,8},{4,12},{8,0},{12,4},{1,9},{5,13},{9,1},{13,5},{2,10},{6,14},... | collective-permute-start | bytes 393224 | tf_op jit(solution)/shard_map/ppermute | solution.py:323
  66.4 11.4 %collective-permute-start.6 = (bf16[32,2048]{1,0:T(8,128)(2,1)S(1)}, bf16[32,2048]{1,0:T(8,128)(2,1)S(1)}, u32[]{:S(2)}, u32[]{:S(2)}) collective-permute-start(bf16[32,2048]{1,0:T(8,128)(2,1)S(1)} %get-tuple-element.49), channel_id=1, source_target_pairs={{0,12},{4,8},{8,4},{12,0},{1,13},{5,9},{9,5},{13,1},{2,14},{6,10},... | collective-permute-start | bytes 393224 | tf_op jit(solution)/shard_map/ppermute | solution.py:323
  68.8 17.1 %collective-permute-start.15 = (bf16[32,2048]{1,0:T(8,128)(2,1)S(1)}, bf16[32,2048]{1,0:T(8,128)(2,1)S(1)}, u32[]{:S(2)}, u32[]{:S(2)}) collective-permute-start(bf16[32,2048]{1,0:T(8,128)(2,1)S(1)} %get-tuple-element.57), channel_id=1, source_target_pairs={{0,4},{4,0},{8,12},{12,8},{1,5},{5,1},{9,13},{13,9},{2,6},{6,2},{1... | collective-permute-start | bytes 393224 | tf_op jit(solution)/shard_map/ppermute | solution.py:323
  69.5 19.2 %collective-permute-start.16 = (bf16[32,2048]{1,0:T(8,128)(2,1)S(1)}, bf16[32,2048]{1,0:T(8,128)(2,1)S(1)}, u32[]{:S(2)}, u32[]{:S(2)}) collective-permute-start(bf16[32,2048]{1,0:T(8,128)(2,1)S(1)} %get-tuple-element.58), channel_id=1, source_target_pairs={{0,8},{4,12},{8,0},{12,4},{1,9},{5,13},{9,1},{13,5},{2,10},{6,14},... | collective-permute-start | bytes 393224 | tf_op jit(solution)/shard_map/ppermute | solution.py:323
  71.9 16.7 %collective-permute-start.17 = (bf16[32,2048]{1,0:T(8,128)(2,1)S(1)}, bf16[32,2048]{1,0:T(8,128)(2,1)S(1)}, u32[]{:S(2)}, u32[]{:S(2)}) collective-permute-start(bf16[32,2048]{1,0:T(8,128)(2,1)S(1)} %get-tuple-element.59), channel_id=1, source_target_pairs={{0,12},{4,8},{8,4},{12,0},{1,13},{5,9},{9,5},{13,1},{2,14},{6,10},... | collective-permute-start | bytes 393224 | tf_op jit(solution)/shard_map/ppermute | solution.py:323
  96.8 1.9 %collective-permute-start.18 = (bf16[128,1792]{1,0:T(8,128)(2,1)S(1)}, bf16[128,1792]{1,0:T(8,128)(2,1)S(1)}, u32[]{:S(2)}, u32[]{:S(2)}) collective-permute-start(bf16[128,1792]{1,0:T(8,128)(2,1)S(1)} %get-tuple-element.62), channel_id=1, source_target_pairs={{0,1},{1,0},{2,3},{3,2},{4,5},{5,4},{6,7},{7,6},{8,9},{9,8},{10,11... | collective-permute-start | bytes 1376264 | tf_op jit(solution)/shard_map/ppermute | solution.py:526
  96.9 9.7 %collective-permute-start.7 = (bf16[128,1792]{1,0:T(8,128)(2,1)S(1)}, bf16[128,1792]{1,0:T(8,128)(2,1)S(1)}, u32[]{:S(2)}, u32[]{:S(2)}) collective-permute-start(bf16[128,1792]{1,0:T(8,128)(2,1)S(1)} %get-tuple-element.51), channel_id=1, source_target_pairs={{0,1},{1,0},{2,3},{3,2},{4,5},{5,4},{6,7},{7,6},{8,9},{9,8},{10,11... | collective-permute-start | bytes 1376264 | tf_op jit(solution)/shard_map/ppermute | solution.py:526
  98.7 11.4 %collective-permute-start.21 = (bf16[64,1792]{1,0:T(8,128)(2,1)S(1)}, bf16[64,1792]{1,0:T(8,128)(2,1)S(1)}, u32[]{:S(2)}, u32[]{:S(2)}) collective-permute-start(bf16[64,1792]{1,0:T(8,128)(2,1)S(1)} %pad_maximum_fusion.5), channel_id=1, source_target_pairs={{0,12},{4,8},{8,4},{12,0},{1,13},{5,9},{9,5},{13,1},{2,14},{6,10},... | collective-permute-start | bytes 688136 | tf_op jit(solution)/shard_map/ppermute | solution.py:323
  101.4 31.5 %collective-permute-start.20 = (bf16[64,1792]{1,0:T(8,128)(2,1)S(1)}, bf16[64,1792]{1,0:T(8,128)(2,1)S(1)}, u32[]{:S(2)}, u32[]{:S(2)}) collective-permute-start(bf16[64,1792]{1,0:T(8,128)(2,1)S(1)} %pad_maximum_fusion.4), channel_id=1, source_target_pairs={{0,8},{4,12},{8,0},{12,4},{1,9},{5,13},{9,1},{13,5},{2,10},{6,14},... | collective-permute-start | bytes 688136 | tf_op jit(solution)/shard_map/ppermute | solution.py:323
  106.3 26.6 %collective-permute-start.19 = (bf16[64,1792]{1,0:T(8,128)(2,1)S(1)}, bf16[64,1792]{1,0:T(8,128)(2,1)S(1)}, u32[]{:S(2)}, u32[]{:S(2)}) collective-permute-start(bf16[64,1792]{1,0:T(8,128)(2,1)S(1)} %pad_maximum_fusion.3), channel_id=1, source_target_pairs={{0,4},{4,0},{8,12},{12,8},{1,5},{5,1},{9,13},{13,9},{2,6},{6,2},{1... | collective-permute-start | bytes 688136 | tf_op jit(solution)/shard_map/ppermute | solution.py:323
  106.7 26.3 %collective-permute-start.10 = (bf16[64,1792]{1,0:T(8,128)(2,1)S(1)}, bf16[64,1792]{1,0:T(8,128)(2,1)S(1)}, u32[]{:S(2)}, u32[]{:S(2)}) collective-permute-start(bf16[64,1792]{1,0:T(8,128)(2,1)S(1)} %pad_maximum_fusion.2), channel_id=1, source_target_pairs={{0,12},{4,8},{8,4},{12,0},{1,13},{5,9},{9,5},{13,1},{2,14},{6,10},... | collective-permute-start | bytes 688136 | tf_op jit(solution)/shard_map/ppermute | solution.py:323
  109.1 33.6 %collective-permute-start.9 = (bf16[64,1792]{1,0:T(8,128)(2,1)S(1)}, bf16[64,1792]{1,0:T(8,128)(2,1)S(1)}, u32[]{:S(2)}, u32[]{:S(2)}) collective-permute-start(bf16[64,1792]{1,0:T(8,128)(2,1)S(1)} %pad_maximum_fusion.1), channel_id=1, source_target_pairs={{0,8},{4,12},{8,0},{12,4},{1,9},{5,13},{9,1},{13,5},{2,10},{6,14},... | collective-permute-start | bytes 688136 | tf_op jit(solution)/shard_map/ppermute | solution.py:323
  110.1 32.6 %collective-permute-start.8 = (bf16[64,1792]{1,0:T(8,128)(2,1)S(1)}, bf16[64,1792]{1,0:T(8,128)(2,1)S(1)}, u32[]{:S(2)}, u32[]{:S(2)}) collective-permute-start(bf16[64,1792]{1,0:T(8,128)(2,1)S(1)} %pad_maximum_fusion), channel_id=1, source_target_pairs={{0,4},{4,0},{8,12},{12,8},{1,5},{5,1},{9,13},{13,9},{2,6},{6,2},{1... | collective-permute-start | bytes 688136 | tf_op jit(solution)/shard_map/ppermute | solution.py:323
Sparse Core Ops, SparseCore 0:
  8.9 15.6 all-gather.2
  26.1 11.3 all-gather.4

commit v4 on v3

--- a/solution.py
+++ b/solution.py
@@ -46,37 +46,42 @@
     return ranked(slots ^ lane_base, MOST)
 
 
-def pack_kernel(steps, rows, flow_most, first, *refs):
-    if first:
-        speaker_ref, table_ref, owner_ref, gain_ref, x_ref = refs[:5]
-        normed_ref, places_ref, message_refs = refs[5], refs[6], refs[7:]
-    else:
-        places_ref, gain_ref, x_ref, _, normed_ref = refs[:5]
-        message_refs = refs[5:]
-    width = x_ref.shape[1]
+def norm_in_pieces(pieces, begin, x_hbm, gain_hbm, x_buf, gain_buf, semaphores, normed_ref):
+    count, width = x_buf.shape
+    size = count // pieces
+    gain_copy = pltpu.make_async_copy(gain_hbm, gain_buf, semaphores.at[pieces])
+    copies = []
+    for piece in range(pieces):
+        copies.append(
+            pltpu.make_async_copy(
+                x_hbm.at[pl.ds(begin + piece * size, size)],
+                x_buf.at[pl.ds(piece * size, size)],
+                semaphores.at[piece],
+            )
+        )
+        copies[-1].start()
+        if piece == 0:
+            gain_copy.start()
+    gain_copy.wait()
+    gain = jnp.concatenate([gain_buf[i : i + 1, :] for i in range(gain_buf.shape[0])], axis=1)
+    for piece in range(pieces):
+        copies[piece].wait()
+
+        def one(index, carry):
+            span = pl.ds(pl.multiple_of(piece * size + index * 16, 16), 16)
+            values = x_buf[span, :].astype(jnp.float32)
+            mean_sq = jnp.sum(values * values, axis=1, keepdims=True) * (1.0 / width)
+            normed = values * lax.rsqrt(mean_sq + 1e-06) * gain
+            normed_ref[span, :] = normed.astype(jnp.bfloat16)
+            return carry
+
+        lax.fori_loop(0, size // 16, one, 0)
+
+
+def pack_messages(steps, rows, places, normed_ref, message_refs):
     per_message, sliced = message_refs[0].shape
     spots = per_message // steps
-    gain = jnp.concatenate([gain_ref[i : i + 1, :] for i in range(gain_ref.shape[0])], axis=1)
-
-    def one(index, carry):
-        span = pl.ds(pl.multiple_of(index * 16, 16), 16)
-        values = x_ref[span, :].astype(jnp.float32)
-        mean_sq = jnp.sum(values * values, axis=1, keepdims=True) * (1.0 / width)
-        normed = values * lax.rsqrt(mean_sq + 1e-06) * gain
-        normed_ref[span, :] = normed.astype(jnp.bfloat16)
-        return carry
-
-    lax.fori_loop(0, steps * rows // 16, one, 0)
-    if first:
-        base = lax.axis_index("streams") * (spots // MOST)
-        places = slot_places(speaker_ref[...], table_ref[...], base)
-        lane = lax.axis_index("streams") * lax.axis_size("sub") + lax.axis_index("sub")
-        places_ref[0:1, :] = places
-        places_ref[1:2, :] = ranked(owner_ref[...] ^ lane, flow_most)
-    else:
-        places = places_ref[0:1, :]
-    total = len(message_refs) * per_message
-    shape = (total, steps * rows)
+    shape = (len(message_refs) * per_message, steps * rows)
     out_row = iota(shape, 0)
     wanted = out_row // per_message * spots + out_row % spots
     out_step = out_row % per_message // spots
@@ -90,24 +95,74 @@
         message_ref[...] = packed[number * per_message : (number + 1) * per_message]
 
 
+def norm_pack_kernel(steps, rows, flow_most, lanes, pieces, *refs):
+    table_hbms, gain_hbm, x_hbm = refs[:3], refs[3], refs[4]
+    normed_ref, places_ref, message_refs = refs[5], refs[6], refs[7 : 7 + lanes]
+    x_buf, gain_buf, *table_bufs, semaphores = refs[7 + lanes :]
+    copies = [
+        pltpu.make_async_copy(source, target, semaphores.at[pieces + 1 + number])
+        for number, (source, target) in enumerate(zip(table_hbms, table_bufs))
+    ]
+    for copy in copies:
+        copy.start()
+    norm_in_pieces(pieces, 0, x_hbm, gain_hbm, x_buf, gain_buf, semaphores, normed_ref)
+    for copy in copies:
+        copy.wait()
+    speaker, table, owner = [buffer[...] for buffer in table_bufs]
+    core, subs = lax.axis_index("sub"), lax.axis_size("sub")
+    spots = message_refs[0].shape[0] // steps
+    places = slot_places(speaker, table, lax.axis_index("streams") * (spots // MOST))
+    places_ref[0:1, :] = places
+    places_ref[1:2, :] = ranked(owner ^ (lax.axis_index("streams") * subs + core), flow_most)
+    pack_messages(steps, rows, places, normed_ref, message_refs)
+
+
+def norm_kernel(begin, pieces, gain_hbm, x_hbm, normed_ref, x_buf, gain_buf, semaphores):
+    norm_in_pieces(pieces, begin, x_hbm, gain_hbm, x_buf, gain_buf, semaphores, normed_ref)
+
+
+def pack_kernel(steps, rows, places_ref, normed_ref, *message_refs):
+    pack_messages(steps, rows, places_ref[0:1, :], normed_ref, message_refs)
+
+
+def project_kernel(chunks, first_row, *refs):
+    normed_refs, weight_ref, bias_ref = refs[:chunks], refs[chunks], refs[chunks + 1]
+    out_ref, rows_ref = refs[-2:]
+    size = normed_refs[0].shape[0]
+    step = pl.program_id(0)
+
+    @pl.when(step == 0)
+    def _():
+        for number, ref in enumerate(normed_refs):
+            rows_ref[number * size : (number + 1) * size, :] = ref[...]
+
+    tiles = weight_ref.shape[1] // 128
+    bias = [bias_ref[pl.ds(first_row + step * tiles + tile, 1), :] for tile in range(tiles)]
+    product = jnp.dot(rows_ref[...], weight_ref[...], preferred_element_type=jnp.float32)
+    out_ref[...] = product + jnp.concatenate(bias, axis=1)
+
+
 def row_slots(shape, spots):
     return iota(shape, 0) % spots // MOST
 
 
 def down_kernel(lanes, spots, *refs):
-    message_refs, map_ref, partial_ref = refs[:lanes], refs[-2], refs[-1]
+    message_refs, map_refs, partial_ref = refs[:lanes], refs[lanes:-1], refs[-1]
+    local_slots = map_refs[0].shape[0]
     rows = jnp.concatenate([ref[...] for ref in message_refs], axis=0)
     own_slot = row_slots(partial_ref.shape, spots)
     total = jnp.zeros(partial_ref.shape, jnp.float32)
-    for slot in range(map_ref.shape[0]):
-        part = jnp.dot(rows, map_ref[slot], preferred_element_type=jnp.float32)
-        total = jnp.where(own_slot == slot, part, total)
+    for number, map_ref in enumerate(map_refs):
+        shift = (lax.axis_index("sub") ^ number) * local_slots
+        for slot in range(local_slots):
+            part = jnp.dot(rows, map_ref[slot], preferred_element_type=jnp.float32)
+            total = jnp.where(own_slot == shift + slot, part, total)
     partial_ref[...] = total
 
 
-def up_kernel(heads, spots, *refs):
-    partial_refs, query_ref, value_ref = refs[:heads], refs[heads], refs[heads + 1]
-    message_refs = refs[heads + 2 :]
+def up_kernel(heads, subs, spots, *refs):
+    partial_refs, refs = refs[:heads], refs[heads:]
+    query_refs, value_refs, message_refs = refs[:subs], refs[subs : 2 * subs], refs[2 * subs :]
     total = partial_refs[0][...]
     for ref in partial_refs[1:]:
         total = total + ref[...]
@@ -119,16 +174,22 @@
     query_pair = jnp.where(low, latent, turned)
     value_pair = jnp.where(low, turned, latent)
 
-    def product(pair, map_ref):
-        pieces = []
-        for slot in range(0, map_ref.shape[0] // ADAPTER_RANK, 2):
-            kept = jnp.where(own_slot == slot + column, pair, 0.0)
-            pieces.append(kept.astype(jnp.bfloat16))
-        wide = jnp.concatenate(pieces, axis=1)
-        return jnp.dot(wide, map_ref[...], preferred_element_type=jnp.float32).astype(jnp.bfloat16)
-
-    queries = product(query_pair, query_ref)
-    values = product(value_pair, value_ref)
+    def product(pair, map_refs):
+        result = None
+        for number, map_ref in enumerate(map_refs):
+            local_slots = map_ref.shape[0] // ADAPTER_RANK
+            shift = (lax.axis_index("sub") ^ number) * local_slots
+            pieces = []
+            for slot in range(0, local_slots, 2):
+                kept = jnp.where(own_slot == shift + slot + column, pair, 0.0)
+                pieces.append(kept.astype(jnp.bfloat16))
+            wide = jnp.concatenate(pieces, axis=1)
+            part = jnp.dot(wide, map_ref[...], preferred_element_type=jnp.float32)
+            result = part if result is None else result + part
+        return result.astype(jnp.bfloat16)
+
+    queries = product(query_pair, query_refs)
+    values = product(value_pair, value_refs)
     query_width = queries.shape[1]
     per_message = message_refs[0].shape[0]
     for number, ref in enumerate(message_refs):
@@ -138,8 +199,9 @@
 
 
 def attend_kernel(before, steps, rows, cache, groups, lanes, subs, last, *refs):
-    places_ref, length_ref, cos_ref, sin_ref, qkv_ref, key_ref, value_ref = refs[:7]
-    delta_refs, refs = refs[7 : 7 + lanes], refs[7 + lanes :]
+    places_ref, length_ref, cos_ref, sin_ref, key_ref, value_ref = refs[:6]
+    qkv_refs, refs = refs[6 : 6 + groups], refs[6 + groups :]
+    delta_refs, refs = refs[:lanes], refs[lanes:]
     if before:
         earlier_ref, refs = refs[0], refs[1:]
     if not last:
@@ -149,7 +211,6 @@
     per_message = delta_refs[0].shape[0]
     spots = per_message // steps
     query_width = PER_GROUP * HEAD_WIDTH
-    block_width = query_width + 2 * HEAD_WIDTH
     known = before + steps
     wide = groups * HEAD_WIDTH
 
@@ -186,7 +247,7 @@
         past = [pl.ds(pl.multiple_of(step * rows + first, BATCH), BATCH) for step in range(before)]
         for group in range(groups):
             query_tiles, key_tiles, value_tiles = [], [], []
-            base = group * block_width
+            qkv_ref = qkv_refs[group]
             lane_span = slice(group * HEAD_WIDTH, (group + 1) * HEAD_WIDTH)
             value_span = slice(wide + group * HEAD_WIDTH, wide + (group + 1) * HEAD_WIDTH)
             for span in past:
@@ -200,13 +261,13 @@
 
                 for head in range(PER_GROUP):
                     begin = head * HEAD_WIDTH
-                    from_qkv = slice(base + begin, base + begin + HEAD_WIDTH)
+                    from_qkv = slice(begin, begin + HEAD_WIDTH)
                     begin += group * query_width
                     from_delta = slice(begin, begin + HEAD_WIDTH)
                     query_tiles.append(
                         rotated(qkv_ref[span, from_qkv] + delta_ref[span, from_delta])
                     )
-                begin = base + query_width
+                begin = query_width
                 key = rotated(qkv_ref[span, begin : begin + HEAD_WIDTH])
                 begin += HEAD_WIDTH
                 from_delta = groups * query_width + group * HEAD_WIDTH
@@ -303,7 +364,7 @@
                 if number == 0:
                     pieces.append(mine[other][...][:block])
                 else:
-                    landed = mine[subs + number - 1]
+                    landed = mine[subs + lanes - 1 - number]
                     pieces.append(landed[...][other * block : (other + 1) * block])
             rows = jnp.dot(
                 pick, jnp.concatenate(pieces, axis=0), preferred_element_type=jnp.float32
@@ -333,8 +394,11 @@
     return landed
 
 
-def cost(flops, size):
-    return pl.CostEstimate(flops=int(flops), bytes_accessed=int(size), transcendentals=0)
+def held(value, others):
+    return lax.optimization_barrier((value, others))[0]
+
+
+SMALL = pl.CostEstimate(flops=1, bytes_accessed=1, transcendentals=0)
 
 
 def on_device(
@@ -374,65 +438,95 @@
     def whole(shape):
         return pl.BlockSpec(shape, lambda i: (0,) * len(shape))
 
-    down_maps = lax.all_gather(adapter_down_maps, "sub", axis=0, tiled=True)
-    query_maps = lax.all_gather(
-        adapter_query_up.reshape(local_slots * ADAPTER_RANK, query_columns),
-        "sub",
-        axis=0,
-        tiled=True,
-    )
-    value_maps = lax.all_gather(
-        adapter_value_up.reshape(local_slots * ADAPTER_RANK, value_columns),
-        "sub",
-        axis=0,
-        tiled=True,
-    )
-
+    in_hbm = pl.BlockSpec(memory_space=pltpu.HBM)
+
+    down_maps = from_others(adapter_down_maps, "sub")
+    pieces = 4
     flat = inputs.reshape(steps * rows, width)
     gain = input_norm_gain.reshape(width // 128, 128)
-    row_block = [
-        pl.BlockSpec((chunk_rows, width), lambda i, chunk=chunk: (chunk, 0))
-        for chunk in range(chunks)
-    ]
     message = jax.ShapeDtypeStruct((per_message, sliced), bf16)
-    normed_shape = jax.ShapeDtypeStruct((steps * rows, width), bf16)
+    normed_shape = jax.ShapeDtypeStruct((chunk_rows, width), bf16)
     places_shape = jax.ShapeDtypeStruct((8, rows), jnp.int32)
     tables = [
         speaker.reshape(1, rows),
         speaker_adapter_slot.reshape(1, -1),
         flow_decoder_owner.reshape(1, rows),
     ]
-    packing = dict(
-        grid=(1,),
+    buffers = [pltpu.VMEM((chunk_rows, width), bf16), pltpu.VMEM(gain.shape, f32)]
+    first_normed, places, *messages = pl.pallas_call(
+        functools.partial(norm_pack_kernel, chunk_steps, rows, flow_most, lanes, pieces),
+        in_specs=[in_hbm] * 5,
+        out_specs=[VMEM] * (2 + lanes),
+        out_shape=[normed_shape, places_shape] + [message] * lanes,
+        scratch_shapes=buffers
+        + [pltpu.VMEM(table.shape, jnp.int32) for table in tables]
+        + [pltpu.SemaphoreType.DMA((pieces + 4,))],
         compiler_params=pltpu.CompilerParams(vmem_limit_bytes=56 * MIB),
-        cost_estimate=cost(2 * lanes * per_message * chunk_rows * sliced, 3 * MIB),
-    )
-    normed, places, *messages = pl.pallas_call(
-        functools.partial(pack_kernel, chunk_steps, rows, flow_most, True),
-        in_specs=[whole(table.shape) for table in tables] + [whole(gain.shape), row_block[0]],
-        out_specs=[row_block[0], whole(places_shape.shape)] + [whole(message.shape)] * lanes,
-        out_shape=[normed_shape, places_shape] + [message] * lanes,
+        cost_estimate=SMALL,
         name="norm_and_pack",
-        **packing,
     )(*tables, gain, flat)
     arrived = [traded(messages, "streams")]
-    packed = []
+    query_map = adapter_query_up.reshape(local_slots * ADAPTER_RANK, query_columns)
+    value_map = adapter_value_up.reshape(local_slots * ADAPTER_RANK, value_columns)
+    query_map, value_map, places = lax.optimization_barrier((query_map, value_map, places))
+    query_maps = from_others(query_map, "sub")
+    value_maps = from_others(value_map, "sub")
+    normed = [first_normed]
     for chunk in range(1, chunks):
-        normed, *messages = pl.pallas_call(
-            functools.partial(pack_kernel, chunk_steps, rows, flow_most, False),
-            in_specs=[whole(places.shape), whole(gain.shape), row_block[chunk]]
-            + [pl.BlockSpec(memory_space=pl.ANY)],
-            out_specs=[row_block[chunk]] + [whole(message.shape)] * lanes,
-            out_shape=[normed_shape] + [message] * lanes,
-            input_output_aliases={3: 0},
-            name="norm_and_pack_next",
-            **packing,
-        )(places, gain, flat, normed)
-        packed.append(messages)
-
-    qkv = jnp.dot(normed, projection_weight, preferred_element_type=f32) + projection_bias
-    qkv, packed = lax.optimization_barrier((qkv, packed))
-    arrived += [traded(messages, "streams") for messages in packed]
+        normed.append(
+            pl.pallas_call(
+                functools.partial(norm_kernel, chunk * chunk_rows, pieces),
+                in_specs=[in_hbm, in_hbm],
+                out_specs=VMEM,
+                out_shape=normed_shape,
+                scratch_shapes=buffers + [pltpu.SemaphoreType.DMA((pieces + 1,))],
+                compiler_params=pltpu.CompilerParams(vmem_limit_bytes=56 * MIB),
+                cost_estimate=SMALL,
+                name="norm",
+            )(held(gain, places), flat)
+        )
+
+    bias = projection_bias.reshape(-1, 128)
+    group_columns = (PER_GROUP + 2) * HEAD_WIDTH
+    cut = 3
+    block_columns = group_columns // cut
+    qkv = []
+    waited = down_maps[1:] + query_maps[1:] + value_maps[1:]
+    for group in range(groups):
+        qkv.append(
+            pl.pallas_call(
+                functools.partial(
+                    project_kernel, chunks, group * group_columns // 128
+                ),
+                grid=(cut,),
+                in_specs=[whole(normed_shape.shape)] * chunks
+                + [
+                    pl.BlockSpec(
+                        (width, block_columns), lambda i, group=group: (0, group * cut + i)
+                    ),
+                    whole(bias.shape),
+                ],
+                out_specs=pl.BlockSpec((steps * rows, block_columns), lambda i: (0, i)),
+                out_shape=jax.ShapeDtypeStruct((steps * rows, group_columns), f32),
+                scratch_shapes=[pltpu.VMEM((steps * rows, width), bf16)],
+                compiler_params=pltpu.CompilerParams(vmem_limit_bytes=56 * MIB),
+                cost_estimate=SMALL,
+                name="project",
+            )(*normed, projection_weight, held(bias, waited))
+        )
+        if group == 0:
+            for chunk in range(1, chunks):
+                messages = pl.pallas_call(
+                    functools.partial(pack_kernel, chunk_steps, rows),
+                    in_specs=[VMEM, VMEM],
+                    out_specs=[VMEM] * lanes,
+                    out_shape=[message] * lanes,
+                    compiler_params=pltpu.CompilerParams(vmem_limit_bytes=16 * MIB),
+                    cost_estimate=SMALL,
+                    name="pack",
+                )(held(places, qkv), normed[chunk])
+                arrived.append(traded(messages, "streams"))
+                waited = messages
 
     half_width = HEAD_WIDTH // 2
     position = jnp.concatenate([cache_fill_length + step for step in range(steps)]).astype(f32)
@@ -444,35 +538,35 @@
     sine_part = jnp.sin(angle) * sign
 
     returned = []
+    after = qkv
     for chunk in range(chunks):
         partial_latent = pl.pallas_call(
             functools.partial(down_kernel, lanes, spots),
-            in_specs=[VMEM] * (lanes + 1),
+            in_specs=[VMEM] * (lanes + subs),
             out_specs=VMEM,
             out_shape=jax.ShapeDtypeStruct((lanes * per_message, 2 * ADAPTER_RANK), f32),
             compiler_params=pltpu.CompilerParams(vmem_limit_bytes=16 * MIB),
-            cost_estimate=cost(2 * lanes * per_message * sliced * 128 * chip_slots, 4 * MIB),
+            cost_estimate=SMALL,
             name="down",
-        )(*arrived[chunk], down_maps)
+        )(held(arrived[chunk][0], after), *arrived[chunk][1:], *down_maps)
         partials = from_others(partial_latent, "heads")
         message = jax.ShapeDtypeStruct((per_message, query_columns + value_columns), bf16)
         messages = pl.pallas_call(
-            functools.partial(up_kernel, heads, spots),
-            in_specs=[VMEM] * (heads + 2),
+            functools.partial(up_kernel, heads, subs, spots),
+            in_specs=[VMEM] * (heads + 2 * subs),
             out_specs=[VMEM] * lanes,
             out_shape=[message] * lanes,
             compiler_params=pltpu.CompilerParams(vmem_limit_bytes=24 * MIB),
-            cost_estimate=cost(
-                2 * lanes * per_message * chip_slots * 64 * message.shape[1], 3 * MIB
-            ),
+            cost_estimate=SMALL,
             name="up",
-        )(*partials, query_maps, value_maps)
+        )(*partials, *query_maps, *value_maps)
+        after = messages
         returned.append(traded(messages, "streams"))
 
     length_row = cache_fill_length.reshape(1, rows)
     block = flow_most * chunk_steps
+    landed = []
     earlier = []
-    landed = []
     for chunk in range(chunks):
         last = chunk == chunks - 1
         message = jax.ShapeDtypeStruct((lanes * block, query_columns), bf16)
@@ -493,8 +587,8 @@
             grid=(1,),
             in_specs=[whole(places.shape), whole(length_row.shape)]
             + [rows_of((chunk_rows, HEAD_WIDTH))] * 2
-            + [rows_of((chunk_rows, qkv.shape[1]))]
             + [whole(rotated_key_cache.shape)] * 2
+            + [rows_of((chunk_rows, group_columns))] * groups
             + [whole((per_message, query_columns + value_columns))] * lanes
             + [whole(block_rows.shape) for block_rows in earlier],
             out_specs=[whole(fresh.shape)] * (not last) + [whole(message.shape)] * subs,
@@ -505,16 +599,16 @@
                 pltpu.VMEM((rows, BATCH * cache), f32),
             ],
             compiler_params=pltpu.CompilerParams(vmem_limit_bytes=32 * MIB),
-            cost_estimate=cost(2e9, 6 * MIB),
+            cost_estimate=SMALL,
             name="attend",
         )(
-            places,
+            held(places, landed[-1] if landed else after),
             length_row,
             cosine,
             sine_part,
-            qkv,
             rotated_key_cache,
             value_cache_rows,
+            *qkv,
             *returned[chunk],
             *earlier,
         )
@@ -528,7 +622,8 @@
             jnp.concatenate([part[lane * block : (lane + 1) * block] for part in parts])
             for lane in range(1, lanes)
         ]
-        landed += parts + traded([None] + joined, "streams")[1:]
+        joined = traded([None] + joined, "streams")[1:]
+        landed += parts + joined[::-1]
 
     flow = pl.pallas_call(
         functools.partial(place_kernel, chunks, lanes, subs, flow_most),
@@ -536,7 +631,7 @@
         out_specs=VMEM,
         out_shape=jax.ShapeDtypeStruct((flow_lanes * flow_most, steps, query_columns), bf16),
         compiler_params=pltpu.CompilerParams(vmem_limit_bytes=24 * MIB),
-        cost_estimate=cost(0, 4 * MIB),
+        cost_estimate=SMALL,
         name="place",
     )(*landed)
     return flow[None]

time: 152 us -> 115 us (0.76)
  Pallas kernels: 28.6 us -> 43.2 us
  matrix products: 14.1 us -> 0 us
  between operations: 13.7 us -> 0.32 us
  starting transfers between devices: 47 us -> 36.9 us
  waiting for transfers between devices: 41.4 us -> 32.3 us
  local copies, waits for them, and re-layouts: 3.7 us -> 0.14 us
  blocking collectives: 2.16 us -> 0 us
    ppermute x18, waiting for transfers between devices: 38.8 us -> 23.8 us  [traded(): landed[shift] = lax.ppermute(blocks[shift], axes, pairs)]
    pallas_call x4 -> x7, Pallas kernels: 8.13 us -> 22.8 us  [the longest x2 14.9 us: on_device(): pl.pallas_call(functools.partial(project_kernel, chunks, group * group_co...]
    dot_general x1 -> x0, matrix products: 14.1 us -> none  [on_device(): jnp.dot(normed, projection_weight, preferred_element_type=f32)]
    ppermute x18, starting transfers between devices: 44.2 us -> 32.5 us  [traded(): landed[shift] = lax.ppermute(blocks[shift], axes, pairs)]
    ppermute x2 -> x5, waiting for transfers between devices: 0.01 us -> 4.94 us  [from_others(): landed.append(lax.ppermute(block, axis, pairs))]
    unnamed x38 -> x22, local copies, waits for them, and re-layouts: 3.61 us -> 0.05 us
    ppermute x2, waiting for transfers between devices: 1.19 us -> 3.54 us  [on_device(): parts.append(lax.ppermute(results[shift], 'sub', pairs))]
    all_gather x1 -> x0, blocking collectives: 2.16 us -> none  [on_device(): lax.all_gather(adapter_value_up.reshape(local_slots * ADAPTER_RANK, value...]
  transfers between devices with their start and end apart: 24 -> 25, of which waited for: 8 -> 7; matrix products, arithmetic and copies ran while one was open for 10% -> 1% of each run, Pallas kernels for 12% -> 36%
where the time goes in v4:
time: 115 us; the launch traced here: 114 us
  Pallas kernels  43.2 us (38%)
  starting transfers between devices  36.9 us (32%)
  waiting for transfers between devices  32.3 us (28%)
    ppermute x18, starting transfers between devices, traded(): landed[shift] = lax.ppermute(blocks[shift], axes, pairs)  32.5 us
    ppermute x18, waiting for transfers between devices, traded(): landed[shift] = lax.ppermute(blocks[shift], axes, pairs)  23.8 us
    pallas_call x2, Pallas kernels, on_device(): pl.pallas_call(functools.partial(attend_kernel, chunk * chunk_steps, chun...  16.3 us
    pallas_call x2, Pallas kernels, on_device(): pl.pallas_call(functools.partial(project_kernel, chunks, group * group_co...  14.9 us
    ppermute x5, waiting for transfers between devices, from_others(): landed.append(lax.ppermute(block, axis, pairs))  4.94 us
    ppermute x5, starting transfers between devices, from_others(): landed.append(lax.ppermute(block, axis, pairs))  4.2 us
    ppermute x2, waiting for transfers between devices, on_device(): parts.append(lax.ppermute(results[shift], 'sub', pairs))  3.54 us
    pallas_call x1, Pallas kernels, on_device(): pl.pallas_call(functools.partial(norm_pack_kernel, chunk_steps, rows, flo...  3.46 us
  transfers between devices with their start and end apart: 25, of which 7 were waited for; matrix products, arithmetic and copies ran while one was open for 1% of the time, Pallas kernels for 36%

profile of v4, /device:TPU:0, one launch (start us, length us, event | category | flops | bytes accessed | tf_op | source)
XLA Modules:
  0.0 113.6 jit_solution(12112416401494462618)
XLA Ops:
  0.0 0.5 collective-permute-start
  0.5 3.5 %norm_and_pack.1 = (bf16[128,3584]{1,0:T(8,128)(2,1)}, s32[8,64]{1,0:T(8,128)}, bf16[32,1792]{1,0:T(8,128)(2,1)}, bf16[32,1792]{1,0:T(8,128)(2,1)}, bf16[32,1792]{1,0:T(8,128)(2,1)}, /*index=5*/bf16[32,1792]{1,0:T(8,128)(2,1)}) custom-call(s32[1,64]{1,0:T(1,128)} %bitcast.24, s32[1,32]{1,0:T(1,128)} %bitcast.25, s32[1,64]{1,0:T(1,128)} %bitcast.26, ...), custom_call_target="tpu_custom_call" | custom-call | flops 1 | bytes 1 | tf_op jit(solution)/shard_map/norm_and_pack/pallas_call | solution.py:456
  4.0 0.2 collective-permute-start.1
  4.2 0.4 collective-permute-start.2
  4.6 2.7 %collective-permute-start.3 = (bf16[32,1792]{1,0:T(8,128)(2,1)}, bf16[32,1792]{1,0:T(8,128)(2,1)S(1)}, u32[]{:S(2)}, u32[]{:S(2)}) collective-permute-start(bf16[32,1792]{1,0:T(8,128)(2,1)} %get-tuple-element.54), channel_id=1, source_target_pairs={{0,4},{4,0},{8,12},{12,8},{1,5},{5,1},{9,13},{13,9},{2,6},{6,2},{1... | collective-permute-start | bytes 344072 | tf_op jit(solution)/shard_map/ppermute | solution.py:384
  7.2 2.6 %collective-permute-start.4 = (bf16[32,1792]{1,0:T(8,128)(2,1)}, bf16[32,1792]{1,0:T(8,128)(2,1)S(1)}, u32[]{:S(2)}, u32[]{:S(2)}) collective-permute-start(bf16[32,1792]{1,0:T(8,128)(2,1)} %get-tuple-element.55), channel_id=1, source_target_pairs={{0,8},{4,12},{8,0},{12,4},{1,9},{5,13},{9,1},{13,5},{2,10},{6,14},... | collective-permute-start | bytes 344072 | tf_op jit(solution)/shard_map/ppermute | solution.py:384
  9.8 1.6 %collective-permute-start.5 = (bf16[32,1792]{1,0:T(8,128)(2,1)}, bf16[32,1792]{1,0:T(8,128)(2,1)S(1)}, u32[]{:S(2)}, u32[]{:S(2)}) collective-permute-start(bf16[32,1792]{1,0:T(8,128)(2,1)} %get-tuple-element.56), channel_id=1, source_target_pairs={{0,12},{4,8},{8,4},{12,0},{1,13},{5,9},{9,5},{13,1},{2,14},{6,10},... | collective-permute-start | bytes 344072 | tf_op jit(solution)/shard_map/ppermute | solution.py:384
  11.5 3.0 %norm.1.refs_1_.normed_ref = bf16[128,3584]{1,0:T(8,128)(2,1)} custom-call(f32[28,128]{1,0:T(8,128)} %bitcast.21, bf16[256,3584]{1,0:T(8,128)(2,1)} %bitcast.19), custom_call_target="tpu_custom_call" | custom-call | flops 1 | bytes 1 | tf_op jit(solution)/shard_map/norm/pallas_call | solution.py:477
  14.6 7.4 %project.2.refs_6_ = f32[256,1152]{1,0:T(8,128)} custom-call(bf16[128,3584]{1,0:T(8,128)(2,1)} %get-tuple-element.41.refs_0_, bf16[128,3584]{1,0:T(8,128)(2,1)} %norm.1.refs_1_.normed_ref, bf16[3584,2304]{1,0:T(8,128)(2,1)} %refs_2_.3, f32[18,128]{1,0:T(8,128)} %bitcast.22), custom_call_target="tpu_custom_call" | custom-call | flops 1 | bytes 1 | tf_op jit(solution)/shard_map/project/pallas_call | solution.py:497
  22.0 0.3 pack.1
  22.4 0.1 collective-permute-start.7
  22.4 2.8 %collective-permute-start.8 = (bf16[32,1792]{1,0:T(8,128)(2,1)S(1)}, bf16[32,1792]{1,0:T(8,128)(2,1)S(1)}, u32[]{:S(2)}, u32[]{:S(2)}) collective-permute-start(bf16[32,1792]{1,0:T(8,128)(2,1)S(1)} %get-tuple-element.50), channel_id=1, source_target_pairs={{0,8},{4,12},{8,0},{12,4},{1,9},{5,13},{9,1},{13,5},{2,10},{6,14},... | collective-permute-start | bytes 344072 | tf_op jit(solution)/shard_map/ppermute | solution.py:384
  25.2 1.6 %collective-permute-start.9 = (bf16[32,1792]{1,0:T(8,128)(2,1)S(1)}, bf16[32,1792]{1,0:T(8,128)(2,1)S(1)}, u32[]{:S(2)}, u32[]{:S(2)}) collective-permute-start(bf16[32,1792]{1,0:T(8,128)(2,1)S(1)} %get-tuple-element.51), channel_id=1, source_target_pairs={{0,12},{4,8},{8,4},{12,0},{1,13},{5,9},{9,5},{13,1},{2,14},{6,10},... | collective-permute-start | bytes 344072 | tf_op jit(solution)/shard_map/ppermute | solution.py:384
  26.8 0.1 compare_select_fusion
  26.9 7.5 %project.3.refs_7_ = f32[256,1152]{1,0:T(8,128)} custom-call(bf16[128,3584]{1,0:T(8,128)(2,1)} %get-tuple-element.41.refs_0_, bf16[128,3584]{1,0:T(8,128)(2,1)} %norm.1.refs_1_.normed_ref, bf16[3584,2304]{1,0:T(8,128)(2,1)} %refs_2_.3, f32[18,128]{1,0:T(8,128)} %bitcast.23), custom_call_target="tpu_custom_call" | custom-call | flops 1 | bytes 1 | tf_op jit(solution)/shard_map/project/pallas_call | solution.py:497
  34.4 1.1 down.2.refs_0_
  35.5 1.6 %collective-permute-start.6 = (f32[128,128]{1,0:T(8,128)S(1)}, f32[128,128]{1,0:T(8,128)S(1)}, u32[]{:S(2)}, u32[]{:S(2)}) collective-permute-start(f32[128,128]{1,0:T(8,128)S(1)} %down.2.refs_0_), channel_id=1, source_target_pairs={{0,2},{2,0},{1,3},{3,1},{4,6},{6,4},{5,7},{7,5},{8,10},{10,8},{9,1... | collective-permute-start | bytes 196616 | tf_op jit(solution)/shard_map/ppermute | solution.py:393
  37.1 0.1 add_convert_fusion
  37.2 2.7 %collective-permute-done.6.refs_1_ = f32[128,128]{1,0:T(8,128)S(1)} collective-permute-done((f32[128,128]{1,0:T(8,128)S(1)}, f32[128,128]{1,0:T(8,128)S(1)}, u32[]{:S(2)}, u32[]{:S(2)}) %collective-permute-start.6) | collective-permute-done | bytes 65568 | tf_op jit(solution)/shard_map/ppermute | solution.py:393
  39.9 0.5 up.2
  40.4 0.1 collective-permute-start.11
  40.5 2.8 %collective-permute-start.12 = (bf16[32,2048]{1,0:T(8,128)(2,1)S(1)}, bf16[32,2048]{1,0:T(8,128)(2,1)S(1)}, u32[]{:S(2)}, u32[]{:S(2)}) collective-permute-start(bf16[32,2048]{1,0:T(8,128)(2,1)S(1)} %get-tuple-element.59), channel_id=1, source_target_pairs={{0,8},{4,12},{8,0},{12,4},{1,9},{5,13},{9,1},{13,5},{2,10},{6,14},... | collective-permute-start | bytes 393224 | tf_op jit(solution)/shard_map/ppermute | solution.py:384
  43.3 1.6 %collective-permute-start.13 = (bf16[32,2048]{1,0:T(8,128)(2,1)S(1)}, bf16[32,2048]{1,0:T(8,128)(2,1)S(1)}, u32[]{:S(2)}, u32[]{:S(2)}) collective-permute-start(bf16[32,2048]{1,0:T(8,128)(2,1)S(1)} %get-tuple-element.60), channel_id=1, source_target_pairs={{0,12},{4,8},{8,4},{12,0},{1,13},{5,9},{9,5},{13,1},{2,14},{6,10},... | collective-permute-start | bytes 393224 | tf_op jit(solution)/shard_map/ppermute | solution.py:384
  44.8 0.0 copy-start.5
  44.9 1.1 down.3.refs_0_
  46.0 1.6 %collective-permute-start.10 = (f32[128,128]{1,0:T(8,128)S(1)}, f32[128,128]{1,0:T(8,128)S(1)}, u32[]{:S(2)}, u32[]{:S(2)}) collective-permute-start(f32[128,128]{1,0:T(8,128)S(1)} %down.3.refs_0_), channel_id=1, source_target_pairs={{0,2},{2,0},{1,3},{3,1},{4,6},{6,4},{5,7},{7,5},{8,10},{10,8},{9,1... | collective-permute-start | bytes 196616 | tf_op jit(solution)/shard_map/ppermute | solution.py:393
  47.5 0.5 fusion
  48.1 2.2 %collective-permute-done.10.refs_1_ = f32[128,128]{1,0:T(8,128)S(1)} collective-permute-done((f32[128,128]{1,0:T(8,128)S(1)}, f32[128,128]{1,0:T(8,128)S(1)}, u32[]{:S(2)}, u32[]{:S(2)}) %collective-permute-start.10) | collective-permute-done | bytes 65568 | tf_op jit(solution)/shard_map/ppermute | solution.py:393
  50.3 0.5 up.3
  50.8 0.1 collective-permute-start.18
  50.9 2.8 %collective-permute-start.19 = (bf16[32,2048]{1,0:T(8,128)(2,1)S(1)}, bf16[32,2048]{1,0:T(8,128)(2,1)S(1)}, u32[]{:S(2)}, u32[]{:S(2)}) collective-permute-start(bf16[32,2048]{1,0:T(8,128)(2,1)S(1)} %get-tuple-element.64), channel_id=1, source_target_pairs={{0,8},{4,12},{8,0},{12,4},{1,9},{5,13},{9,1},{13,5},{2,10},{6,14},... | collective-permute-start | bytes 393224 | tf_op jit(solution)/shard_map/ppermute | solution.py:384
  53.7 1.6 %collective-permute-start.20 = (bf16[32,2048]{1,0:T(8,128)(2,1)S(1)}, bf16[32,2048]{1,0:T(8,128)(2,1)S(1)}, u32[]{:S(2)}, u32[]{:S(2)}) collective-permute-start(bf16[32,2048]{1,0:T(8,128)(2,1)S(1)} %get-tuple-element.65), channel_id=1, source_target_pairs={{0,12},{4,8},{8,4},{12,0},{1,13},{5,9},{9,5},{13,1},{2,14},{6,10},... | collective-permute-start | bytes 393224 | tf_op jit(solution)/shard_map/ppermute | solution.py:384
  55.3 8.1 %attend.2 = (f32[128,512]{1,0:T(8,128)S(1)}, bf16[128,1792]{1,0:T(8,128)(2,1)S(1)}, bf16[128,1792]{1,0:T(8,128)(2,1)S(1)}) custom-call(s32[8,64]{1,0:T(8,128)S(1)} %copy-done.9, s32[1,64]{1,0:T(1,128)S(1)} %bitcast.16, f32[256,128]{1,0:T(8,128)S(1)} %get-tuple-element.86.refs_2_, f32[256,128]{1,0:T(8,128)S(1)} %get-tuple-element.85.refs_3_, ...), custom_call_target="tpu_custom_call" | custom-call | flops 1 | bytes 1 | tf_op jit(solution)/shard_map/attend/pallas_call | solution.py:575
  63.5 0.1 collective-permute-start.14
  63.6 1.8 %collective-permute-done.14.refs_1_ = bf16[128,1792]{1,0:T(8,128)(2,1)S(1)} collective-permute-done((bf16[128,1792]{1,0:T(8,128)(2,1)S(1)}, bf16[128,1792]{1,0:T(8,128)(2,1)S(1)}, u32[]{:S(2)}, u32[]{:S(2)}) %collective-permute-start.14) | collective-permute-done | bytes 458784 | tf_op jit(solution)/shard_map/ppermute | solution.py:620
  65.4 4.5 %collective-permute-start.17 = (bf16[64,1792]{1,0:T(8,128)(2,1)S(1)}, bf16[64,1792]{1,0:T(8,128)(2,1)S(1)}, u32[]{:S(2)}, u32[]{:S(2)}) collective-permute-start(bf16[64,1792]{1,0:T(8,128)(2,1)S(1)} %pad_maximum_fusion.2), channel_id=1, source_target_pairs={{0,4},{4,0},{8,12},{12,8},{1,5},{5,1},{9,13},{13,9},{2,6},{6,2},{1... | collective-permute-start | bytes 688136 | tf_op jit(solution)/shard_map/ppermute | solution.py:384
  69.9 2.1 %collective-permute-start.16 = (bf16[64,1792]{1,0:T(8,128)(2,1)S(1)}, bf16[64,1792]{1,0:T(8,128)(2,1)S(1)}, u32[]{:S(2)}, u32[]{:S(2)}) collective-permute-start(bf16[64,1792]{1,0:T(8,128)(2,1)S(1)} %pad_maximum_fusion.1), channel_id=1, source_target_pairs={{0,8},{4,12},{8,0},{12,4},{1,9},{5,13},{9,1},{13,5},{2,10},{6,14},... | collective-permute-start | bytes 688136 | tf_op jit(solution)/shard_map/ppermute | solution.py:384
  72.0 8.7 %collective-permute-done.17.refs_4_ = bf16[64,1792]{1,0:T(8,128)(2,1)S(1)} collective-permute-done((bf16[64,1792]{1,0:T(8,128)(2,1)S(1)}, bf16[64,1792]{1,0:T(8,128)(2,1)S(1)}, u32[]{:S(2)}, u32[]{:S(2)}) %collective-permute-start.17) | collective-permute-done | bytes 229408 | tf_op jit(solution)/shard_map/ppermute | solution.py:384
  80.7 1.2 %collective-permute-start.15 = (bf16[64,1792]{1,0:T(8,128)(2,1)S(1)}, bf16[64,1792]{1,0:T(8,128)(2,1)S(1)}, u32[]{:S(2)}, u32[]{:S(2)}) collective-permute-start(bf16[64,1792]{1,0:T(8,128)(2,1)S(1)} %pad_maximum_fusion), channel_id=1, source_target_pairs={{0,12},{4,8},{8,4},{12,0},{1,13},{5,9},{9,5},{13,1},{2,14},{6,10},... | collective-permute-start | bytes 688136 | tf_op jit(solution)/shard_map/ppermute | solution.py:384
  81.9 8.1 %attend.3 = (bf16[128,1792]{1,0:T(8,128)(2,1)S(1)}, bf16[128,1792]{1,0:T(8,128)(2,1)S(1)}) custom-call(s32[8,64]{1,0:T(8,128)S(1)} %copy-done.9, s32[1,64]{1,0:T(1,128)S(1)} %bitcast.17, f32[256,128]{1,0:T(8,128)S(1)} %get-tuple-element.86.refs_2_, f32[256,128]{1,0:T(8,128)S(1)} %get-tuple-element.85.refs_3_, bf16[64,32,256]{2,1,0:T(8,128)(2,1)S(1)} %copy-done.4, ...), custom_call_target="tpu_custom_call" | custom-call | flops 1 | bytes 1 | tf_op jit(solution)/shard_map/attend/pallas_call | solution.py:575
  90.0 0.1 collective-permute-start.21
  90.1 1.8 %collective-permute-done.21.refs_6_ = bf16[128,1792]{1,0:T(8,128)(2,1)S(1)} collective-permute-done((bf16[128,1792]{1,0:T(8,128)(2,1)S(1)}, bf16[128,1792]{1,0:T(8,128)(2,1)S(1)}, u32[]{:S(2)}, u32[]{:S(2)}) %collective-permute-start.21) | collective-permute-done | bytes 458784 | tf_op jit(solution)/shard_map/ppermute | solution.py:620
  91.9 0.1 collective-permute-start.24
  92.0 3.3 %collective-permute-start.23 = (bf16[64,1792]{1,0:T(8,128)(2,1)S(1)}, bf16[64,1792]{1,0:T(8,128)(2,1)S(1)}, u32[]{:S(2)}, u32[]{:S(2)}) collective-permute-start(bf16[64,1792]{1,0:T(8,128)(2,1)S(1)} %pad_maximum_fusion.4), channel_id=1, source_target_pairs={{0,8},{4,12},{8,0},{12,4},{1,9},{5,13},{9,1},{13,5},{2,10},{6,14},... | collective-permute-start | bytes 688136 | tf_op jit(solution)/shard_map/ppermute | solution.py:384
  95.4 1.2 %collective-permute-start.22 = (bf16[64,1792]{1,0:T(8,128)(2,1)S(1)}, bf16[64,1792]{1,0:T(8,128)(2,1)S(1)}, u32[]{:S(2)}, u32[]{:S(2)}) collective-permute-start(bf16[64,1792]{1,0:T(8,128)(2,1)S(1)} %pad_maximum_fusion.3), channel_id=1, source_target_pairs={{0,12},{4,8},{8,4},{12,0},{1,13},{5,9},{9,5},{13,1},{2,14},{6,10},... | collective-permute-start | bytes 688136 | tf_op jit(solution)/shard_map/ppermute | solution.py:384
  96.6 7.4 %collective-permute-done.24.refs_9_ = bf16[64,1792]{1,0:T(8,128)(2,1)S(1)} collective-permute-done((bf16[64,1792]{1,0:T(8,128)(2,1)S(1)}, bf16[64,1792]{1,0:T(8,128)(2,1)S(1)}, u32[]{:S(2)}, u32[]{:S(2)}) %collective-permute-start.24) | collective-permute-done | bytes 229408 | tf_op jit(solution)/shard_map/ppermute | solution.py:384
  104.0 7.6 %collective-permute-done.23.refs_8_ = bf16[64,1792]{1,0:T(8,128)(2,1)S(1)} collective-permute-done((bf16[64,1792]{1,0:T(8,128)(2,1)S(1)}, bf16[64,1792]{1,0:T(8,128)(2,1)S(1)}, u32[]{:S(2)}, u32[]{:S(2)}) %collective-permute-start.23) | collective-permute-done | bytes 229408 | tf_op jit(solution)/shard_map/ppermute | solution.py:384
  111.6 1.9 %place.1 = bf16[128,4,1792]{2,1,0:T(4,128)(2,1)} custom-call(bf16[128,1792]{1,0:T(8,128)(2,1)S(1)} %get-tuple-element.67.refs_0_, bf16[128,1792]{1,0:T(8,128)(2,1)S(1)} %collective-permute-done.14.refs_1_, bf16[64,1792]{1,0:T(8,128)(2,1)S(1)} %collective-permute-done.15.refs_2_, bf16[64,1792]{1,0:T(8,128)(2,1)S(1)} %collective-permute-done.16.refs_3_, ...), custom_call_target="tpu_custom_call" | custom-call | flops 1 | bytes 1 | tf_op jit(solution)/shard_map/place/pallas_call | solution.py:628
  (51 shorter events, 0.3 us)
Async XLA Ops:
  0.0 4.0 %copy-start.6 = (bf16[4,64,1792]{2,1,0:T(8,128)(2,1)S(1)}, bf16[4,64,1792]{2,1,0:T(8,128)(2,1)}, u32[]{:S(2)}) copy-start(bf16[4,64,1792]{2,1,0:T(8,128)(2,1)} %param.23) | copy-start | bytes 2752516
  0.0 4.2 %copy-start.7 = (bf16[4,64,256]{2,1,0:T(8,128)(2,1)S(1)}, bf16[4,64,256]{2,1,0:T(8,128)(2,1)}, u32[]{:S(2)}) copy-start(bf16[4,64,256]{2,1,0:T(8,128)(2,1)} %param.24) | copy-start | bytes 393220
  0.0 9.8 %copy-start.10 = (s32[64]{0:T(128)S(1)}, s32[64]{0:T(128)}, u32[]{:S(2)}) copy-start(s32[64]{0:T(128)} %param.19) | copy-start | bytes 772
  0.0 14.5 %collective-permute-start = (bf16[4,1792,128]{2,1,0:T(8,128)(2,1)}, bf16[4,1792,128]{2,1,0:T(8,128)(2,1)S(1)}, u32[]{:S(2)}, u32[]{:S(2)}) collective-permute-start(bf16[4,1792,128]{2,1,0:T(8,128)(2,1)} %refs_4_.5), channel_id=1, source_target_pairs={{0,1},{1,0},{2,3},{3,2},{4,5},{5,4},{6,7},{7,6},{8,9},{9,8},{10,11... | collective-permute-start | bytes 5505032 | tf_op jit(solution)/shard_map/ppermute | solution.py:393
  4.0 10.5 %collective-permute-start.1 = (bf16[256,1792]{1,0:T(8,128)(2,1)S(1)}, bf16[256,1792]{1,0:T(8,128)(2,1)S(1)}, u32[]{:S(2)}, u32[]{:S(2)}) collective-permute-start(bf16[256,1792]{1,0:T(8,128)(2,1)S(1)} %bitcast.10), channel_id=1, source_target_pairs={{0,1},{1,0},{2,3},{3,2},{4,5},{5,4},{6,7},{7,6},{8,9},{9,8},{10,11... | collective-permute-start | bytes 2752520 | tf_op jit(solution)/shard_map/ppermute | solution.py:393
  4.2 5.7 %collective-permute-start.2 = (bf16[256,256]{1,0:T(8,128)(2,1)S(1)}, bf16[256,256]{1,0:T(8,128)(2,1)S(1)}, u32[]{:S(2)}, u32[]{:S(2)}) collective-permute-start(bf16[256,256]{1,0:T(8,128)(2,1)S(1)} %bitcast.13), channel_id=1, source_target_pairs={{0,1},{1,0},{2,3},{3,2},{4,5},{5,4},{6,7},{7,6},{8,9},{9,8},{10,11... | collective-permute-start | bytes 393224 | tf_op jit(solution)/shard_map/ppermute | solution.py:393
  4.6 20.7 %collective-permute-start.3 = (bf16[32,1792]{1,0:T(8,128)(2,1)}, bf16[32,1792]{1,0:T(8,128)(2,1)S(1)}, u32[]{:S(2)}, u32[]{:S(2)}) collective-permute-start(bf16[32,1792]{1,0:T(8,128)(2,1)} %get-tuple-element.54), channel_id=1, source_target_pairs={{0,4},{4,0},{8,12},{12,8},{1,5},{5,1},{9,13},{13,9},{2,6},{6,2},{1... | collective-permute-start | bytes 344072 | tf_op jit(solution)/shard_map/ppermute | solution.py:384
  7.2 27.2 %collective-permute-start.4 = (bf16[32,1792]{1,0:T(8,128)(2,1)}, bf16[32,1792]{1,0:T(8,128)(2,1)S(1)}, u32[]{:S(2)}, u32[]{:S(2)}) collective-permute-start(bf16[32,1792]{1,0:T(8,128)(2,1)} %get-tuple-element.55), channel_id=1, source_target_pairs={{0,8},{4,12},{8,0},{12,4},{1,9},{5,13},{9,1},{13,5},{2,10},{6,14},... | collective-permute-start | bytes 344072 | tf_op jit(solution)/shard_map/ppermute | solution.py:384
  9.8 24.6 %collective-permute-start.5 = (bf16[32,1792]{1,0:T(8,128)(2,1)}, bf16[32,1792]{1,0:T(8,128)(2,1)S(1)}, u32[]{:S(2)}, u32[]{:S(2)}) collective-permute-start(bf16[32,1792]{1,0:T(8,128)(2,1)} %get-tuple-element.56), channel_id=1, source_target_pairs={{0,12},{4,8},{8,4},{12,0},{1,13},{5,9},{9,5},{13,1},{2,14},{6,10},... | collective-permute-start | bytes 344072 | tf_op jit(solution)/shard_map/ppermute | solution.py:384
  14.6 7.5 %copy-start = (bf16[128,3584]{1,0:T(8,128)(2,1)S(1)}, bf16[128,3584]{1,0:T(8,128)(2,1)}, u32[]{:S(2)}) copy-start(bf16[128,3584]{1,0:T(8,128)(2,1)} %norm.1.refs_1_.normed_ref) | copy-start | bytes 2752516
  14.6 7.5 %copy-start.9 = (s32[8,64]{1,0:T(8,128)S(1)}, s32[8,64]{1,0:T(8,128)}, u32[]{:S(2)}) copy-start(s32[8,64]{1,0:T(8,128)} %get-tuple-element.69.places_ref.refs_0_) | copy-start | bytes 6148
  22.4 20.9 %collective-permute-start.7 = (bf16[32,1792]{1,0:T(8,128)(2,1)S(1)}, bf16[32,1792]{1,0:T(8,128)(2,1)S(1)}, u32[]{:S(2)}, u32[]{:S(2)}) collective-permute-start(bf16[32,1792]{1,0:T(8,128)(2,1)S(1)} %get-tuple-element.49), channel_id=1, source_target_pairs={{0,4},{4,0},{8,12},{12,8},{1,5},{5,1},{9,13},{13,9},{2,6},{6,2},{1... | collective-permute-start | bytes 344072 | tf_op jit(solution)/shard_map/ppermute | solution.py:384
  22.4 22.4 %collective-permute-start.8 = (bf16[32,1792]{1,0:T(8,128)(2,1)S(1)}, bf16[32,1792]{1,0:T(8,128)(2,1)S(1)}, u32[]{:S(2)}, u32[]{:S(2)}) collective-permute-start(bf16[32,1792]{1,0:T(8,128)(2,1)S(1)} %get-tuple-element.50), channel_id=1, source_target_pairs={{0,8},{4,12},{8,0},{12,4},{1,9},{5,13},{9,1},{13,5},{2,10},{6,14},... | collective-permute-start | bytes 344072 | tf_op jit(solution)/shard_map/ppermute | solution.py:384
  25.2 19.6 %collective-permute-start.9 = (bf16[32,1792]{1,0:T(8,128)(2,1)S(1)}, bf16[32,1792]{1,0:T(8,128)(2,1)S(1)}, u32[]{:S(2)}, u32[]{:S(2)}) collective-permute-start(bf16[32,1792]{1,0:T(8,128)(2,1)S(1)} %get-tuple-element.51), channel_id=1, source_target_pairs={{0,12},{4,8},{8,4},{12,0},{1,13},{5,9},{9,5},{13,1},{2,14},{6,10},... | collective-permute-start | bytes 344072 | tf_op jit(solution)/shard_map/ppermute | solution.py:384
  26.9 7.5 %copy-start.3 = (bf16[4,1792,128]{2,1,0:T(8,128)(2,1)S(1)}, bf16[4,1792,128]{2,1,0:T(8,128)(2,1)}, u32[]{:S(2)}) copy-start(bf16[4,1792,128]{2,1,0:T(8,128)(2,1)} %refs_4_.5) | copy-start | bytes 5505028
  26.9 7.5 %copy-start.8 = (bf16[32,1792]{1,0:T(8,128)(2,1)S(1)}, bf16[32,1792]{1,0:T(8,128)(2,1)}, u32[]{:S(2)}) copy-start(bf16[32,1792]{1,0:T(8,128)(2,1)} %get-tuple-element.53.refs_0_) | copy-start | bytes 344068
  35.5 4.3 %collective-permute-start.6 = (f32[128,128]{1,0:T(8,128)S(1)}, f32[128,128]{1,0:T(8,128)S(1)}, u32[]{:S(2)}, u32[]{:S(2)}) collective-permute-start(f32[128,128]{1,0:T(8,128)S(1)} %down.2.refs_0_), channel_id=1, source_target_pairs={{0,2},{2,0},{1,3},{3,1},{4,6},{6,4},{5,7},{7,5},{8,10},{10,8},{9,1... | collective-permute-start | bytes 196616 | tf_op jit(solution)/shard_map/ppermute | solution.py:393
  40.4 13.3 %collective-permute-start.11 = (bf16[32,2048]{1,0:T(8,128)(2,1)S(1)}, bf16[32,2048]{1,0:T(8,128)(2,1)S(1)}, u32[]{:S(2)}, u32[]{:S(2)}) collective-permute-start(bf16[32,2048]{1,0:T(8,128)(2,1)S(1)} %get-tuple-element.58), channel_id=1, source_target_pairs={{0,4},{4,0},{8,12},{12,8},{1,5},{5,1},{9,13},{13,9},{2,6},{6,2},{1... | collective-permute-start | bytes 393224 | tf_op jit(solution)/shard_map/ppermute | solution.py:384
  40.5 14.8 %collective-permute-start.12 = (bf16[32,2048]{1,0:T(8,128)(2,1)S(1)}, bf16[32,2048]{1,0:T(8,128)(2,1)S(1)}, u32[]{:S(2)}, u32[]{:S(2)}) collective-permute-start(bf16[32,2048]{1,0:T(8,128)(2,1)S(1)} %get-tuple-element.59), channel_id=1, source_target_pairs={{0,8},{4,12},{8,0},{12,4},{1,9},{5,13},{9,1},{13,5},{2,10},{6,14},... | collective-permute-start | bytes 393224 | tf_op jit(solution)/shard_map/ppermute | solution.py:384
  43.3 12.0 %collective-permute-start.13 = (bf16[32,2048]{1,0:T(8,128)(2,1)S(1)}, bf16[32,2048]{1,0:T(8,128)(2,1)S(1)}, u32[]{:S(2)}, u32[]{:S(2)}) collective-permute-start(bf16[32,2048]{1,0:T(8,128)(2,1)S(1)} %get-tuple-element.60), channel_id=1, source_target_pairs={{0,12},{4,8},{8,4},{12,0},{1,13},{5,9},{9,5},{13,1},{2,14},{6,10},... | collective-permute-start | bytes 393224 | tf_op jit(solution)/shard_map/ppermute | solution.py:384
  44.8 10.4 %copy-start.4 = (bf16[64,32,256]{2,1,0:T(8,128)(2,1)S(1)}, bf16[64,32,256]{2,1,0:T(8,128)(2,1)}, u32[]{:S(2)}) copy-start(bf16[64,32,256]{2,1,0:T(8,128)(2,1)} %refs_4_.7) | copy-start | bytes 3145732
  44.8 10.4 %copy-start.5 = (bf16[64,32,256]{2,1,0:T(8,128)(2,1)S(1)}, bf16[64,32,256]{2,1,0:T(8,128)(2,1)}, u32[]{:S(2)}) copy-start(bf16[64,32,256]{2,1,0:T(8,128)(2,1)} %refs_5_.3) | copy-start | bytes 3145732
  46.0 9.3 %copy-start.1 = (f32[256,1152]{1,0:T(8,128)S(1)}, f32[256,1152]{1,0:T(8,128)}, u32[]{:S(2)}) copy-start(f32[256,1152]{1,0:T(8,128)} %project.2.refs_6_) | copy-start | bytes 3538948
  46.0 9.3 %copy-start.2 = (f32[256,1152]{1,0:T(8,128)S(1)}, f32[256,1152]{1,0:T(8,128)}, u32[]{:S(2)}) copy-start(f32[256,1152]{1,0:T(8,128)} %project.3.refs_7_) | copy-start | bytes 3538948
  46.0 4.3 %collective-permute-start.10 = (f32[128,128]{1,0:T(8,128)S(1)}, f32[128,128]{1,0:T(8,128)S(1)}, u32[]{:S(2)}, u32[]{:S(2)}) collective-permute-start(f32[128,128]{1,0:T(8,128)S(1)} %down.3.refs_0_), channel_id=1, source_target_pairs={{0,2},{2,0},{1,3},{3,1},{4,6},{6,4},{5,7},{7,5},{8,10},{10,8},{9,1... | collective-permute-start | bytes 196616 | tf_op jit(solution)/shard_map/ppermute | solution.py:393
  50.8 31.0 %collective-permute-start.18 = (bf16[32,2048]{1,0:T(8,128)(2,1)S(1)}, bf16[32,2048]{1,0:T(8,128)(2,1)S(1)}, u32[]{:S(2)}, u32[]{:S(2)}) collective-permute-start(bf16[32,2048]{1,0:T(8,128)(2,1)S(1)} %get-tuple-element.63), channel_id=1, source_target_pairs={{0,4},{4,0},{8,12},{12,8},{1,5},{5,1},{9,13},{13,9},{2,6},{6,2},{1... | collective-permute-start | bytes 393224 | tf_op jit(solution)/shard_map/ppermute | solution.py:384
  50.9 30.9 %collective-permute-start.19 = (bf16[32,2048]{1,0:T(8,128)(2,1)S(1)}, bf16[32,2048]{1,0:T(8,128)(2,1)S(1)}, u32[]{:S(2)}, u32[]{:S(2)}) collective-permute-start(bf16[32,2048]{1,0:T(8,128)(2,1)S(1)} %get-tuple-element.64), channel_id=1, source_target_pairs={{0,8},{4,12},{8,0},{12,4},{1,9},{5,13},{9,1},{13,5},{2,10},{6,14},... | collective-permute-start | bytes 393224 | tf_op jit(solution)/shard_map/ppermute | solution.py:384
  53.7 28.1 %collective-permute-start.20 = (bf16[32,2048]{1,0:T(8,128)(2,1)S(1)}, bf16[32,2048]{1,0:T(8,128)(2,1)S(1)}, u32[]{:S(2)}, u32[]{:S(2)}) collective-permute-start(bf16[32,2048]{1,0:T(8,128)(2,1)S(1)} %get-tuple-element.65), channel_id=1, source_target_pairs={{0,12},{4,8},{8,4},{12,0},{1,13},{5,9},{9,5},{13,1},{2,14},{6,10},... | collective-permute-start | bytes 393224 | tf_op jit(solution)/shard_map/ppermute | solution.py:384
  63.5 1.9 %collective-permute-start.14 = (bf16[128,1792]{1,0:T(8,128)(2,1)S(1)}, bf16[128,1792]{1,0:T(8,128)(2,1)S(1)}, u32[]{:S(2)}, u32[]{:S(2)}) collective-permute-start(bf16[128,1792]{1,0:T(8,128)(2,1)S(1)} %get-tuple-element.68), channel_id=1, source_target_pairs={{0,1},{1,0},{2,3},{3,2},{4,5},{5,4},{6,7},{7,6},{8,9},{9,8},{10,11... | collective-permute-start | bytes 1376264 | tf_op jit(solution)/shard_map/ppermute | solution.py:620
  65.4 15.3 %collective-permute-start.17 = (bf16[64,1792]{1,0:T(8,128)(2,1)S(1)}, bf16[64,1792]{1,0:T(8,128)(2,1)S(1)}, u32[]{:S(2)}, u32[]{:S(2)}) collective-permute-start(bf16[64,1792]{1,0:T(8,128)(2,1)S(1)} %pad_maximum_fusion.2), channel_id=1, source_target_pairs={{0,4},{4,0},{8,12},{12,8},{1,5},{5,1},{9,13},{13,9},{2,6},{6,2},{1... | collective-permute-start | bytes 688136 | tf_op jit(solution)/shard_map/ppermute | solution.py:384
  69.9 26.7 %collective-permute-start.16 = (bf16[64,1792]{1,0:T(8,128)(2,1)S(1)}, bf16[64,1792]{1,0:T(8,128)(2,1)S(1)}, u32[]{:S(2)}, u32[]{:S(2)}) collective-permute-start(bf16[64,1792]{1,0:T(8,128)(2,1)S(1)} %pad_maximum_fusion.1), channel_id=1, source_target_pairs={{0,8},{4,12},{8,0},{12,4},{1,9},{5,13},{9,1},{13,5},{2,10},{6,14},... | collective-permute-start | bytes 688136 | tf_op jit(solution)/shard_map/ppermute | solution.py:384
  80.7 15.9 %collective-permute-start.15 = (bf16[64,1792]{1,0:T(8,128)(2,1)S(1)}, bf16[64,1792]{1,0:T(8,128)(2,1)S(1)}, u32[]{:S(2)}, u32[]{:S(2)}) collective-permute-start(bf16[64,1792]{1,0:T(8,128)(2,1)S(1)} %pad_maximum_fusion), channel_id=1, source_target_pairs={{0,12},{4,8},{8,4},{12,0},{1,13},{5,9},{9,5},{13,1},{2,14},{6,10},... | collective-permute-start | bytes 688136 | tf_op jit(solution)/shard_map/ppermute | solution.py:384
  90.0 1.9 %collective-permute-start.21 = (bf16[128,1792]{1,0:T(8,128)(2,1)S(1)}, bf16[128,1792]{1,0:T(8,128)(2,1)S(1)}, u32[]{:S(2)}, u32[]{:S(2)}) collective-permute-start(bf16[128,1792]{1,0:T(8,128)(2,1)S(1)} %get-tuple-element.72), channel_id=1, source_target_pairs={{0,1},{1,0},{2,3},{3,2},{4,5},{5,4},{6,7},{7,6},{8,9},{9,8},{10,11... | collective-permute-start | bytes 1376264 | tf_op jit(solution)/shard_map/ppermute | solution.py:620
  91.9 12.1 %collective-permute-start.24 = (bf16[64,1792]{1,0:T(8,128)(2,1)S(1)}, bf16[64,1792]{1,0:T(8,128)(2,1)S(1)}, u32[]{:S(2)}, u32[]{:S(2)}) collective-permute-start(bf16[64,1792]{1,0:T(8,128)(2,1)S(1)} %pad_maximum_fusion.5), channel_id=1, source_target_pairs={{0,4},{4,0},{8,12},{12,8},{1,5},{5,1},{9,13},{13,9},{2,6},{6,2},{1... | collective-permute-start | bytes 688136 | tf_op jit(solution)/shard_map/ppermute | solution.py:384
  92.0 19.6 %collective-permute-start.23 = (bf16[64,1792]{1,0:T(8,128)(2,1)S(1)}, bf16[64,1792]{1,0:T(8,128)(2,1)S(1)}, u32[]{:S(2)}, u32[]{:S(2)}) collective-permute-start(bf16[64,1792]{1,0:T(8,128)(2,1)S(1)} %pad_maximum_fusion.4), channel_id=1, source_target_pairs={{0,8},{4,12},{8,0},{12,4},{1,9},{5,13},{9,1},{13,5},{2,10},{6,14},... | collective-permute-start | bytes 688136 | tf_op jit(solution)/shard_map/ppermute | solution.py:384
  95.4 16.3 %collective-permute-start.22 = (bf16[64,1792]{1,0:T(8,128)(2,1)S(1)}, bf16[64,1792]{1,0:T(8,128)(2,1)S(1)}, u32[]{:S(2)}, u32[]{:S(2)}) collective-permute-start(bf16[64,1792]{1,0:T(8,128)(2,1)S(1)} %pad_maximum_fusion.3), channel_id=1, source_target_pairs={{0,12},{4,8},{8,4},{12,0},{1,13},{5,9},{9,5},{13,1},{2,14},{6,10},... | collective-permute-start | bytes 688136 | tf_op jit(solution)/shard_map/ppermute | solution.py:384

commit v5 on v4

--- a/solution.py
+++ b/solution.py
@@ -18,6 +18,8 @@
 BATCH = 8
 VMEM = pl.BlockSpec(memory_space=pltpu.VMEM)
 MIB = 1 << 20
+PACK_LIMIT = 56
+PROJECT_LIMIT = 56
 
 
 def iota(shape, dim):
@@ -95,49 +97,39 @@
         message_ref[...] = packed[number * per_message : (number + 1) * per_message]
 
 
-def norm_pack_kernel(steps, rows, flow_most, lanes, pieces, *refs):
-    table_hbms, gain_hbm, x_hbm = refs[:3], refs[3], refs[4]
-    normed_ref, places_ref, message_refs = refs[5], refs[6], refs[7 : 7 + lanes]
-    x_buf, gain_buf, *table_bufs, semaphores = refs[7 + lanes :]
-    copies = [
-        pltpu.make_async_copy(source, target, semaphores.at[pieces + 1 + number])
-        for number, (source, target) in enumerate(zip(table_hbms, table_bufs))
-    ]
-    for copy in copies:
-        copy.start()
-    norm_in_pieces(pieces, 0, x_hbm, gain_hbm, x_buf, gain_buf, semaphores, normed_ref)
-    for copy in copies:
-        copy.wait()
-    speaker, table, owner = [buffer[...] for buffer in table_bufs]
-    core, subs = lax.axis_index("sub"), lax.axis_size("sub")
-    spots = message_refs[0].shape[0] // steps
-    places = slot_places(speaker, table, lax.axis_index("streams") * (spots // MOST))
-    places_ref[0:1, :] = places
-    places_ref[1:2, :] = ranked(owner ^ (lax.axis_index("streams") * subs + core), flow_most)
-    pack_messages(steps, rows, places, normed_ref, message_refs)
-
-
-def norm_kernel(begin, pieces, gain_hbm, x_hbm, normed_ref, x_buf, gain_buf, semaphores):
+def norm_pack_kernel(steps, rows, flow_most, lanes, pieces, chunk, *refs):
+    if chunk:
+        places_ref, gain_hbm, x_hbm, _, normed_ref = refs[:5]
+        message_refs = refs[5 : 5 + lanes]
+        x_buf, gain_buf, semaphores = refs[5 + lanes :]
+    else:
+        table_hbms, gain_hbm, x_hbm = refs[:3], refs[3], refs[4]
+        normed_ref, places_ref, message_refs = refs[5], refs[6], refs[7 : 7 + lanes]
+        x_buf, gain_buf, *table_bufs, semaphores = refs[7 + lanes :]
+        copies = [
+            pltpu.make_async_copy(source, target, semaphores.at[pieces + 1 + number])
+            for number, (source, target) in enumerate(zip(table_hbms, table_bufs))
+        ]
+        for copy in copies:
+            copy.start()
+    begin = chunk * steps * rows
     norm_in_pieces(pieces, begin, x_hbm, gain_hbm, x_buf, gain_buf, semaphores, normed_ref)
-
-
-def pack_kernel(steps, rows, places_ref, normed_ref, *message_refs):
+    if not chunk:
+        for copy in copies:
+            copy.wait()
+        speaker, table, owner = [buffer[...] for buffer in table_bufs]
+        core, subs = lax.axis_index("sub"), lax.axis_size("sub")
+        spots = message_refs[0].shape[0] // steps
+        places = slot_places(speaker, table, lax.axis_index("streams") * (spots // MOST))
+        places_ref[0:1, :] = places
+        places_ref[1:2, :] = ranked(owner ^ (lax.axis_index("streams") * subs + core), flow_most)
     pack_messages(steps, rows, places_ref[0:1, :], normed_ref, message_refs)
 
 
-def project_kernel(chunks, first_row, *refs):
-    normed_refs, weight_ref, bias_ref = refs[:chunks], refs[chunks], refs[chunks + 1]
-    out_ref, rows_ref = refs[-2:]
-    size = normed_refs[0].shape[0]
-    step = pl.program_id(0)
-
-    @pl.when(step == 0)
-    def _():
-        for number, ref in enumerate(normed_refs):
-            rows_ref[number * size : (number + 1) * size, :] = ref[...]
-
+def project_kernel(first_tile, rows_ref, weight_ref, bias_ref, out_ref):
     tiles = weight_ref.shape[1] // 128
-    bias = [bias_ref[pl.ds(first_row + step * tiles + tile, 1), :] for tile in range(tiles)]
+    tile = first_tile + pl.program_id(0) * tiles
+    bias = [bias_ref[pl.ds(tile + number, 1), :] for number in range(tiles)]
     product = jnp.dot(rows_ref[...], weight_ref[...], preferred_element_type=jnp.float32)
     out_ref[...] = product + jnp.concatenate(bias, axis=1)
 
@@ -200,7 +192,7 @@
 
 def attend_kernel(before, steps, rows, cache, groups, lanes, subs, last, *refs):
     places_ref, length_ref, cos_ref, sin_ref, key_ref, value_ref = refs[:6]
-    qkv_refs, refs = refs[6 : 6 + groups], refs[6 + groups :]
+    qkv_refs, refs = refs[6:8], refs[8:]
     delta_refs, refs = refs[:lanes], refs[lanes:]
     if before:
         earlier_ref, refs = refs[0], refs[1:]
@@ -212,6 +204,14 @@
     spots = per_message // steps
     query_width = PER_GROUP * HEAD_WIDTH
     known = before + steps
+
+    def qkv_tile(span, group, head):
+        begin = (group * (PER_GROUP + 2) + head) * HEAD_WIDTH
+        edge = qkv_refs[0].shape[1]
+        if begin < edge:
+            return qkv_refs[0][span, begin : begin + HEAD_WIDTH]
+        return qkv_refs[1][span, begin - edge : begin - edge + HEAD_WIDTH]
+
     wide = groups * HEAD_WIDTH
 
     column = as_column(places_ref[0:1, :])
@@ -247,7 +247,6 @@
         past = [pl.ds(pl.multiple_of(step * rows + first, BATCH), BATCH) for step in range(before)]
         for group in range(groups):
             query_tiles, key_tiles, value_tiles = [], [], []
-            qkv_ref = qkv_refs[group]
             lane_span = slice(group * HEAD_WIDTH, (group + 1) * HEAD_WIDTH)
             value_span = slice(wide + group * HEAD_WIDTH, wide + (group + 1) * HEAD_WIDTH)
             for span in past:
@@ -260,21 +259,13 @@
                     return values * cosine + pltpu.roll(values, HEAD_WIDTH // 2, 1) * sine_part
 
                 for head in range(PER_GROUP):
-                    begin = head * HEAD_WIDTH
-                    from_qkv = slice(begin, begin + HEAD_WIDTH)
-                    begin += group * query_width
-                    from_delta = slice(begin, begin + HEAD_WIDTH)
-                    query_tiles.append(
-                        rotated(qkv_ref[span, from_qkv] + delta_ref[span, from_delta])
-                    )
-                begin = query_width
-                key = rotated(qkv_ref[span, begin : begin + HEAD_WIDTH])
-                begin += HEAD_WIDTH
-                from_delta = groups * query_width + group * HEAD_WIDTH
-                value = (
-                    qkv_ref[span, begin : begin + HEAD_WIDTH]
-                    + delta_ref[span, from_delta : from_delta + HEAD_WIDTH]
-                )
+                    begin = group * query_width + head * HEAD_WIDTH
+                    change = delta_ref[span, begin : begin + HEAD_WIDTH]
+                    query_tiles.append(rotated(qkv_tile(span, group, head) + change))
+                key = rotated(qkv_tile(span, group, PER_GROUP))
+                begin = groups * query_width + group * HEAD_WIDTH
+                change = delta_ref[span, begin : begin + HEAD_WIDTH]
+                value = qkv_tile(span, group, PER_GROUP + 1) + change
                 if not last:
                     fresh_ref[span, lane_span] = key
                     fresh_ref[span, value_span] = value
@@ -441,11 +432,18 @@
     in_hbm = pl.BlockSpec(memory_space=pltpu.HBM)
 
     down_maps = from_others(adapter_down_maps, "sub")
+    query_maps = from_others(
+        adapter_query_up.reshape(local_slots * ADAPTER_RANK, query_columns), "sub"
+    )
+    value_maps = from_others(
+        adapter_value_up.reshape(local_slots * ADAPTER_RANK, value_columns), "sub"
+    )
+
     pieces = 4
     flat = inputs.reshape(steps * rows, width)
     gain = input_norm_gain.reshape(width // 128, 128)
     message = jax.ShapeDtypeStruct((per_message, sliced), bf16)
-    normed_shape = jax.ShapeDtypeStruct((chunk_rows, width), bf16)
+    normed_shape = jax.ShapeDtypeStruct((steps * rows, width), bf16)
     places_shape = jax.ShapeDtypeStruct((8, rows), jnp.int32)
     tables = [
         speaker.reshape(1, rows),
@@ -453,93 +451,61 @@
         flow_decoder_owner.reshape(1, rows),
     ]
     buffers = [pltpu.VMEM((chunk_rows, width), bf16), pltpu.VMEM(gain.shape, f32)]
-    first_normed, places, *messages = pl.pallas_call(
-        functools.partial(norm_pack_kernel, chunk_steps, rows, flow_most, lanes, pieces),
-        in_specs=[in_hbm] * 5,
-        out_specs=[VMEM] * (2 + lanes),
-        out_shape=[normed_shape, places_shape] + [message] * lanes,
-        scratch_shapes=buffers
-        + [pltpu.VMEM(table.shape, jnp.int32) for table in tables]
-        + [pltpu.SemaphoreType.DMA((pieces + 4,))],
-        compiler_params=pltpu.CompilerParams(vmem_limit_bytes=56 * MIB),
-        cost_estimate=SMALL,
-        name="norm_and_pack",
-    )(*tables, gain, flat)
-    arrived = [traded(messages, "streams")]
-    query_map = adapter_query_up.reshape(local_slots * ADAPTER_RANK, query_columns)
-    value_map = adapter_value_up.reshape(local_slots * ADAPTER_RANK, value_columns)
-    query_map, value_map, places = lax.optimization_barrier((query_map, value_map, places))
-    query_maps = from_others(query_map, "sub")
-    value_maps = from_others(value_map, "sub")
-    normed = [first_normed]
-    for chunk in range(1, chunks):
-        normed.append(
-            pl.pallas_call(
-                functools.partial(norm_kernel, chunk * chunk_rows, pieces),
-                in_specs=[in_hbm, in_hbm],
-                out_specs=VMEM,
-                out_shape=normed_shape,
-                scratch_shapes=buffers + [pltpu.SemaphoreType.DMA((pieces + 1,))],
-                compiler_params=pltpu.CompilerParams(vmem_limit_bytes=56 * MIB),
-                cost_estimate=SMALL,
-                name="norm",
-            )(held(gain, places), flat)
-        )
+    table_buffers = [pltpu.VMEM(table.shape, jnp.int32) for table in tables]
+    arrived = []
+    for chunk in range(chunks):
+        rows_block = pl.BlockSpec((chunk_rows, width), lambda i, chunk=chunk: (chunk, 0))
+        first = chunk == 0
+        operands = [gain, flat]
+        if first:
+            operands = tables + operands
+        else:
+            adapters = down_maps[1:], query_maps[1:], value_maps[1:]
+            operands = [held(places, adapters)] + operands + [normed]
+        normed, *messages = pl.pallas_call(
+            functools.partial(
+                norm_pack_kernel, chunk_steps, rows, flow_most, lanes, pieces, chunk
+            ),
+            grid=(1,),
+            in_specs=[in_hbm] * 5 if first else [whole(places_shape.shape)] + [in_hbm] * 3,
+            out_specs=[rows_block]
+            + [whole(places_shape.shape)] * first
+            + [whole(message.shape)] * lanes,
+            out_shape=[normed_shape] + [places_shape] * first + [message] * lanes,
+            scratch_shapes=buffers
+            + table_buffers * first
+            + [pltpu.SemaphoreType.DMA((pieces + 4,))],
+            input_output_aliases={} if first else {3: 0},
+            compiler_params=pltpu.CompilerParams(vmem_limit_bytes=PACK_LIMIT * MIB),
+            cost_estimate=SMALL,
+            name="norm_and_pack",
+        )(*operands)
+        if first:
+            places, *messages = messages
+        arrived.append(traded(messages, "streams"))
 
     bias = projection_bias.reshape(-1, 128)
-    group_columns = (PER_GROUP + 2) * HEAD_WIDTH
-    cut = 3
-    block_columns = group_columns // cut
-    qkv = []
-    waited = down_maps[1:] + query_maps[1:] + value_maps[1:]
-    for group in range(groups):
-        qkv.append(
-            pl.pallas_call(
-                functools.partial(
-                    project_kernel, chunks, group * group_columns // 128
-                ),
-                grid=(cut,),
-                in_specs=[whole(normed_shape.shape)] * chunks
-                + [
-                    pl.BlockSpec(
-                        (width, block_columns), lambda i, group=group: (0, group * cut + i)
-                    ),
-                    whole(bias.shape),
-                ],
-                out_specs=pl.BlockSpec((steps * rows, block_columns), lambda i: (0, i)),
-                out_shape=jax.ShapeDtypeStruct((steps * rows, group_columns), f32),
-                scratch_shapes=[pltpu.VMEM((steps * rows, width), bf16)],
-                compiler_params=pltpu.CompilerParams(vmem_limit_bytes=56 * MIB),
-                cost_estimate=SMALL,
-                name="project",
-            )(*normed, projection_weight, held(bias, waited))
-        )
-        if group == 0:
-            for chunk in range(1, chunks):
-                messages = pl.pallas_call(
-                    functools.partial(pack_kernel, chunk_steps, rows),
-                    in_specs=[VMEM, VMEM],
-                    out_specs=[VMEM] * lanes,
-                    out_shape=[message] * lanes,
-                    compiler_params=pltpu.CompilerParams(vmem_limit_bytes=16 * MIB),
-                    cost_estimate=SMALL,
-                    name="pack",
-                )(held(places, qkv), normed[chunk])
-                arrived.append(traded(messages, "streams"))
-                waited = messages
-
-    half_width = HEAD_WIDTH // 2
-    position = jnp.concatenate([cache_fill_length + step for step in range(steps)]).astype(f32)
-    freq = jnp.exp(jnp.arange(half_width, dtype=f32) * (-math.log(1000000.0) / half_width))
-    freq = jnp.concatenate([freq, freq])
-    angle = position[:, None] * freq
-    sign = jnp.where(jnp.arange(HEAD_WIDTH) < half_width, -1.0, 1.0).astype(f32)
-    cosine = jnp.cos(angle)
-    sine_part = jnp.sin(angle) * sign
-
-    returned = []
-    after = qkv
-    for chunk in range(chunks):
+    columns = projection_weight.shape[1]
+    block_columns = 256 if columns % 256 == 0 else 384
+    blocks = columns // block_columns
+
+    def project(begin, end, after):
+        return pl.pallas_call(
+            functools.partial(project_kernel, begin * block_columns // 128),
+            grid=(end - begin,),
+            in_specs=[
+                whole(normed_shape.shape),
+                pl.BlockSpec((width, block_columns), lambda i: (0, begin + i)),
+                whole(bias.shape),
+            ],
+            out_specs=pl.BlockSpec((steps * rows, block_columns), lambda i: (0, i)),
+            out_shape=jax.ShapeDtypeStruct((steps * rows, (end - begin) * block_columns), f32),
+            compiler_params=pltpu.CompilerParams(vmem_limit_bytes=PROJECT_LIMIT * MIB),
+            cost_estimate=SMALL,
+            name="project",
+        )(normed, projection_weight, held(bias, after))
+
+    def down(chunk, after):
         partial_latent = pl.pallas_call(
             functools.partial(down_kernel, lanes, spots),
             in_specs=[VMEM] * (lanes + subs),
@@ -549,7 +515,9 @@
             cost_estimate=SMALL,
             name="down",
         )(held(arrived[chunk][0], after), *arrived[chunk][1:], *down_maps)
-        partials = from_others(partial_latent, "heads")
+        return from_others(partial_latent, "heads")
+
+    def up(partials, after):
         message = jax.ShapeDtypeStruct((per_message, query_columns + value_columns), bf16)
         messages = pl.pallas_call(
             functools.partial(up_kernel, heads, subs, spots),
@@ -559,9 +527,30 @@
             compiler_params=pltpu.CompilerParams(vmem_limit_bytes=24 * MIB),
             cost_estimate=SMALL,
             name="up",
-        )(*partials, *query_maps, *value_maps)
-        after = messages
-        returned.append(traded(messages, "streams"))
+        )(held(partials[0], after), *partials[1:], *query_maps, *value_maps)
+        return messages, traded(messages, "streams")
+
+    cut = blocks // 2
+    qkv = [project(0, cut, messages)]
+    partials = down(0, qkv)
+    qkv.append(project(cut, blocks, partials[0]))
+
+    half_width = HEAD_WIDTH // 2
+    position = jnp.concatenate([cache_fill_length + step for step in range(steps)]).astype(f32)
+    freq = jnp.exp(jnp.arange(half_width, dtype=f32) * (-math.log(1000000.0) / half_width))
+    freq = jnp.concatenate([freq, freq])
+    angle = position[:, None] * freq
+    sign = jnp.where(jnp.arange(HEAD_WIDTH) < half_width, -1.0, 1.0).astype(f32)
+    cosine = jnp.cos(angle)
+    sine_part = jnp.sin(angle) * sign
+
+    returned = []
+    after = qkv
+    for chunk in range(chunks):
+        if chunk:
+            partials = down(chunk, after)
+        after, arrivals = up(partials, after)
+        returned.append(arrivals)
 
     length_row = cache_fill_length.reshape(1, rows)
     block = flow_most * chunk_steps
@@ -588,7 +577,7 @@
             in_specs=[whole(places.shape), whole(length_row.shape)]
             + [rows_of((chunk_rows, HEAD_WIDTH))] * 2
             + [whole(rotated_key_cache.shape)] * 2
-            + [rows_of((chunk_rows, group_columns))] * groups
+            + [rows_of((chunk_rows, part.shape[1])) for part in qkv]
             + [whole((per_message, query_columns + value_columns))] * lanes
             + [whole(block_rows.shape) for block_rows in earlier],
             out_specs=[whole(fresh.shape)] * (not last) + [whole(message.shape)] * subs,

time: 115 us -> 115 us (level)
    pallas_call x1 -> x2, Pallas kernels: 3.46 us -> 7.32 us  [on_device(): pl.pallas_call(functools.partial(norm_pack_kernel, chunk_steps, rows, flo...]
    pallas_call x8 -> x6, Pallas kernels: 21.5 us -> 17.9 us  [the longest x2 14.7 us: project(): pl.pallas_call(functools.partial(project_kernel, begin * block_columns //...]
    ppermute x5, waiting for transfers between devices: 4.94 us -> 3.2 us  [from_others(): landed.append(lax.ppermute(block, axis, pairs))]
  transfers between devices with their start and end apart: 25 -> 25, of which waited for: 7 -> 6; matrix products, arithmetic and copies ran while one was open for 1% -> 1% of each run, Pallas kernels for 36% -> 37%
where the time goes in v5:
time: 115 us; the launch traced here: 113 us
  Pallas kernels  43.5 us (38%)
  starting transfers between devices  36.8 us (32%)
  waiting for transfers between devices  31.3 us (27%)
    ppermute x18, starting transfers between devices, traded(): landed[shift] = lax.ppermute(blocks[shift], axes, pairs)  33.6 us
    ppermute x18, waiting for transfers between devices, traded(): landed[shift] = lax.ppermute(blocks[shift], axes, pairs)  24.5 us
    pallas_call x2, Pallas kernels, on_device(): pl.pallas_call(functools.partial(attend_kernel, chunk * chunk_steps, chun...  16.3 us
    pallas_call x2, Pallas kernels, project(): pl.pallas_call(functools.partial(project_kernel, begin * block_columns //...  14.7 us
    pallas_call x2, Pallas kernels, on_device(): pl.pallas_call(functools.partial(norm_pack_kernel, chunk_steps, rows, flo...  7.32 us
    ppermute x2, waiting for transfers between devices, on_device(): parts.append(lax.ppermute(results[shift], 'sub', pairs))  3.54 us
    ppermute x5, waiting for transfers between devices, from_others(): landed.append(lax.ppermute(block, axis, pairs))  3.2 us
    ppermute x5, starting transfers between devices, from_others(): landed.append(lax.ppermute(block, axis, pairs))  3.12 us
  transfers between devices with their start and end apart: 25, of which 6 were waited for; matrix products, arithmetic and copies ran while one was open for 1% of the time, Pallas kernels for 37%

profile of v5, /device:TPU:0, one launch (start us, length us, event | category | flops | bytes accessed | tf_op | source)
XLA Modules:
  0.0 112.8 jit_solution(5899738560426507090)
XLA Ops:
  0.0 0.5 collective-permute-start
  0.5 0.1 collective-permute-start.1
  0.5 0.4 collective-permute-start.2
  1.0 3.5 %norm_and_pack.2 = (bf16[256,3584]{1,0:T(8,128)(2,1)}, s32[8,64]{1,0:T(8,128)}, bf16[32,1792]{1,0:T(8,128)(2,1)}, bf16[32,1792]{1,0:T(8,128)(2,1)}, bf16[32,1792]{1,0:T(8,128)(2,1)}, /*index=5*/bf16[32,1792]{1,0:T(8,128)(2,1)}) custom-call(s32[1,64]{1,0:T(1,128)} %bitcast.24, s32[1,32]{1,0:T(1,128)} %bitcast.25, s32[1,64]{1,0:T(1,128)} %bitcast.26, ...), custom_call_target="tpu_custom_call" | custom-call | flops 1 | bytes 1 | tf_op jit(solution)/shard_map/norm_and_pack/pallas_call | solution.py:465
  4.4 2.7 %collective-permute-start.3 = (bf16[32,1792]{1,0:T(8,128)(2,1)}, bf16[32,1792]{1,0:T(8,128)(2,1)S(1)}, u32[]{:S(2)}, u32[]{:S(2)}) collective-permute-start(bf16[32,1792]{1,0:T(8,128)(2,1)} %get-tuple-element.49), channel_id=1, source_target_pairs={{0,4},{4,0},{8,12},{12,8},{1,5},{5,1},{9,13},{13,9},{2,6},{6,2},{1... | collective-permute-start | bytes 344072 | tf_op jit(solution)/shard_map/ppermute | solution.py:375
  7.1 2.6 %collective-permute-start.4 = (bf16[32,1792]{1,0:T(8,128)(2,1)}, bf16[32,1792]{1,0:T(8,128)(2,1)S(1)}, u32[]{:S(2)}, u32[]{:S(2)}) collective-permute-start(bf16[32,1792]{1,0:T(8,128)(2,1)} %get-tuple-element.50), channel_id=1, source_target_pairs={{0,8},{4,12},{8,0},{12,4},{1,9},{5,13},{9,1},{13,5},{2,10},{6,14},... | collective-permute-start | bytes 344072 | tf_op jit(solution)/shard_map/ppermute | solution.py:375
  9.7 0.8 collective-permute-start.5
  10.6 0.0 collective-permute-done.1.refs_3_
  10.6 3.9 %norm_and_pack.3 = (bf16[256,3584]{1,0:T(8,128)(2,1)}, bf16[32,1792]{1,0:T(8,128)(2,1)}, bf16[32,1792]{1,0:T(8,128)(2,1)}, bf16[32,1792]{1,0:T(8,128)(2,1)}, bf16[32,1792]{1,0:T(8,128)(2,1)}) custom-call(s32[8,64]{1,0:T(8,128)} %get-tuple-element.67.refs_0_, f32[28,128]{1,0:T(8,128)} %bitcast.21, ...), custom_call_target="tpu_custom_call", output_to_operand_aliasing={{0}: (3, {})} | custom-call | flops 1 | bytes 1 | tf_op jit(solution)/shard_map/norm_and_pack/pallas_call | solution.py:465
  14.4 0.2 collective-permute-start.7
  14.7 3.5 %collective-permute-start.8 = (bf16[32,1792]{1,0:T(8,128)(2,1)}, bf16[32,1792]{1,0:T(8,128)(2,1)S(1)}, u32[]{:S(2)}, u32[]{:S(2)}) collective-permute-start(bf16[32,1792]{1,0:T(8,128)(2,1)} %get-tuple-element.45), channel_id=1, source_target_pairs={{0,8},{4,12},{8,0},{12,4},{1,9},{5,13},{9,1},{13,5},{2,10},{6,14},... | collective-permute-start | bytes 344072 | tf_op jit(solution)/shard_map/ppermute | solution.py:375
  18.1 0.8 collective-permute-start.9
  18.9 0.1 compare_select_fusion
  19.0 6.7 %project.2.refs_6_ = f32[256,1024]{1,0:T(8,128)} custom-call(bf16[256,3584]{1,0:T(8,128)(2,1)} %get-tuple-element.43.rows_ref, bf16[3584,2304]{1,0:T(8,128)(2,1)} %weight_ref.3, f32[18,128]{1,0:T(8,128)} %bitcast.22), custom_call_target="tpu_custom_call" | custom-call | flops 1 | bytes 1 | tf_op jit(solution)/shard_map/project/pallas_call | solution.py:493
  25.7 1.1 down.2.refs_0_
  26.8 1.6 %collective-permute-start.6 = (f32[128,128]{1,0:T(8,128)S(1)}, f32[128,128]{1,0:T(8,128)S(1)}, u32[]{:S(2)}, u32[]{:S(2)}) collective-permute-start(f32[128,128]{1,0:T(8,128)S(1)} %down.2.refs_0_), channel_id=1, source_target_pairs={{0,2},{2,0},{1,3},{3,1},{4,6},{6,4},{5,7},{7,5},{8,10},{10,8},{9,1... | collective-permute-start | bytes 196616 | tf_op jit(solution)/shard_map/ppermute | solution.py:384
  28.3 0.1 add_convert_fusion
  28.4 8.1 %project.3.refs_7_ = f32[256,1280]{1,0:T(8,128)} custom-call(bf16[256,3584]{1,0:T(8,128)(2,1)} %get-tuple-element.43.rows_ref, bf16[3584,2304]{1,0:T(8,128)(2,1)} %weight_ref.3, f32[18,128]{1,0:T(8,128)} %bitcast.23), custom_call_target="tpu_custom_call" | custom-call | flops 1 | bytes 1 | tf_op jit(solution)/shard_map/project/pallas_call | solution.py:493
  36.5 0.5 up.2
  37.0 1.5 %collective-permute-start.11 = (bf16[32,2048]{1,0:T(8,128)(2,1)S(1)}, bf16[32,2048]{1,0:T(8,128)(2,1)S(1)}, u32[]{:S(2)}, u32[]{:S(2)}) collective-permute-start(bf16[32,2048]{1,0:T(8,128)(2,1)S(1)} %get-tuple-element.55), channel_id=1, source_target_pairs={{0,4},{4,0},{8,12},{12,8},{1,5},{5,1},{9,13},{13,9},{2,6},{6,2},{1... | collective-permute-start | bytes 393224 | tf_op jit(solution)/shard_map/ppermute | solution.py:375
  38.5 2.2 %collective-permute-start.12 = (bf16[32,2048]{1,0:T(8,128)(2,1)S(1)}, bf16[32,2048]{1,0:T(8,128)(2,1)S(1)}, u32[]{:S(2)}, u32[]{:S(2)}) collective-permute-start(bf16[32,2048]{1,0:T(8,128)(2,1)S(1)} %get-tuple-element.56), channel_id=1, source_target_pairs={{0,8},{4,12},{8,0},{12,4},{1,9},{5,13},{9,1},{13,5},{2,10},{6,14},... | collective-permute-start | bytes 393224 | tf_op jit(solution)/shard_map/ppermute | solution.py:375
  40.7 0.7 collective-permute-start.13
  41.5 0.0 copy-start.3
  41.5 0.0 copy-start.4
  41.5 1.1 down.3.refs_0_
  42.7 0.6 collective-permute-start.10
  43.3 0.5 fusion
  43.8 3.2 %collective-permute-done.10.refs_1_ = f32[128,128]{1,0:T(8,128)S(1)} collective-permute-done((f32[128,128]{1,0:T(8,128)S(1)}, f32[128,128]{1,0:T(8,128)S(1)}, u32[]{:S(2)}, u32[]{:S(2)}) %collective-permute-start.10) | collective-permute-done | bytes 65568 | tf_op jit(solution)/shard_map/ppermute | solution.py:384
  47.0 0.5 up.3
  47.5 0.6 collective-permute-start.18
  48.1 3.1 %collective-permute-start.19 = (bf16[32,2048]{1,0:T(8,128)(2,1)S(1)}, bf16[32,2048]{1,0:T(8,128)(2,1)S(1)}, u32[]{:S(2)}, u32[]{:S(2)}) collective-permute-start(bf16[32,2048]{1,0:T(8,128)(2,1)S(1)} %get-tuple-element.62), channel_id=1, source_target_pairs={{0,8},{4,12},{8,0},{12,4},{1,9},{5,13},{9,1},{13,5},{2,10},{6,14},... | collective-permute-start | bytes 393224 | tf_op jit(solution)/shard_map/ppermute | solution.py:375
  51.2 0.7 collective-permute-start.20
  52.0 8.1 %attend.2 = (f32[128,512]{1,0:T(8,128)S(1)}, bf16[128,1792]{1,0:T(8,128)(2,1)S(1)}, bf16[128,1792]{1,0:T(8,128)(2,1)S(1)}) custom-call(s32[8,64]{1,0:T(8,128)S(1)} %copy-done.9, s32[1,64]{1,0:T(1,128)S(1)} %bitcast.16, f32[256,128]{1,0:T(8,128)S(1)} %get-tuple-element.84.refs_2_, f32[256,128]{1,0:T(8,128)S(1)} %get-tuple-element.83.refs_3_, ...), custom_call_target="tpu_custom_call" | custom-call | flops 1 | bytes 1 | tf_op jit(solution)/shard_map/attend/pallas_call | solution.py:564
  60.1 0.1 collective-permute-start.14
  60.2 1.8 %collective-permute-done.14.refs_1_ = bf16[128,1792]{1,0:T(8,128)(2,1)S(1)} collective-permute-done((bf16[128,1792]{1,0:T(8,128)(2,1)S(1)}, bf16[128,1792]{1,0:T(8,128)(2,1)S(1)}, u32[]{:S(2)}, u32[]{:S(2)}) %collective-permute-start.14) | collective-permute-done | bytes 458784 | tf_op jit(solution)/shard_map/ppermute | solution.py:609
  62.1 7.1 %collective-permute-start.17 = (bf16[64,1792]{1,0:T(8,128)(2,1)S(1)}, bf16[64,1792]{1,0:T(8,128)(2,1)S(1)}, u32[]{:S(2)}, u32[]{:S(2)}) collective-permute-start(bf16[64,1792]{1,0:T(8,128)(2,1)S(1)} %pad_maximum_fusion.2), channel_id=1, source_target_pairs={{0,4},{4,0},{8,12},{12,8},{1,5},{5,1},{9,13},{13,9},{2,6},{6,2},{1... | collective-permute-start | bytes 688136 | tf_op jit(solution)/shard_map/ppermute | solution.py:375
  69.2 1.2 %collective-permute-start.16 = (bf16[64,1792]{1,0:T(8,128)(2,1)S(1)}, bf16[64,1792]{1,0:T(8,128)(2,1)S(1)}, u32[]{:S(2)}, u32[]{:S(2)}) collective-permute-start(bf16[64,1792]{1,0:T(8,128)(2,1)S(1)} %pad_maximum_fusion.1), channel_id=1, source_target_pairs={{0,8},{4,12},{8,0},{12,4},{1,9},{5,13},{9,1},{13,5},{2,10},{6,14},... | collective-permute-start | bytes 688136 | tf_op jit(solution)/shard_map/ppermute | solution.py:375
  70.4 9.5 %collective-permute-done.17.refs_4_ = bf16[64,1792]{1,0:T(8,128)(2,1)S(1)} collective-permute-done((bf16[64,1792]{1,0:T(8,128)(2,1)S(1)}, bf16[64,1792]{1,0:T(8,128)(2,1)S(1)}, u32[]{:S(2)}, u32[]{:S(2)}) %collective-permute-start.17) | collective-permute-done | bytes 229408 | tf_op jit(solution)/shard_map/ppermute | solution.py:375
  79.9 1.2 %collective-permute-start.15 = (bf16[64,1792]{1,0:T(8,128)(2,1)S(1)}, bf16[64,1792]{1,0:T(8,128)(2,1)S(1)}, u32[]{:S(2)}, u32[]{:S(2)}) collective-permute-start(bf16[64,1792]{1,0:T(8,128)(2,1)S(1)} %pad_maximum_fusion), channel_id=1, source_target_pairs={{0,12},{4,8},{8,4},{12,0},{1,13},{5,9},{9,5},{13,1},{2,14},{6,10},... | collective-permute-start | bytes 688136 | tf_op jit(solution)/shard_map/ppermute | solution.py:375
  81.2 8.1 %attend.3 = (bf16[128,1792]{1,0:T(8,128)(2,1)S(1)}, bf16[128,1792]{1,0:T(8,128)(2,1)S(1)}) custom-call(s32[8,64]{1,0:T(8,128)S(1)} %copy-done.9, s32[1,64]{1,0:T(1,128)S(1)} %bitcast.17, f32[256,128]{1,0:T(8,128)S(1)} %get-tuple-element.84.refs_2_, f32[256,128]{1,0:T(8,128)S(1)} %get-tuple-element.83.refs_3_, bf16[64,32,256]{2,1,0:T(8,128)(2,1)S(1)} %copy-done.3, ...), custom_call_target="tpu_custom_call" | custom-call | flops 1 | bytes 1 | tf_op jit(solution)/shard_map/attend/pallas_call | solution.py:564
  89.3 0.1 collective-permute-start.21
  89.4 1.8 %collective-permute-done.21.refs_6_ = bf16[128,1792]{1,0:T(8,128)(2,1)S(1)} collective-permute-done((bf16[128,1792]{1,0:T(8,128)(2,1)S(1)}, bf16[128,1792]{1,0:T(8,128)(2,1)S(1)}, u32[]{:S(2)}, u32[]{:S(2)}) %collective-permute-start.21) | collective-permute-done | bytes 458784 | tf_op jit(solution)/shard_map/ppermute | solution.py:609
  91.2 0.1 collective-permute-start.24
  91.3 3.2 %collective-permute-start.23 = (bf16[64,1792]{1,0:T(8,128)(2,1)S(1)}, bf16[64,1792]{1,0:T(8,128)(2,1)S(1)}, u32[]{:S(2)}, u32[]{:S(2)}) collective-permute-start(bf16[64,1792]{1,0:T(8,128)(2,1)S(1)} %pad_maximum_fusion.4), channel_id=1, source_target_pairs={{0,8},{4,12},{8,0},{12,4},{1,9},{5,13},{9,1},{13,5},{2,10},{6,14},... | collective-permute-start | bytes 688136 | tf_op jit(solution)/shard_map/ppermute | solution.py:375
  94.6 1.3 %collective-permute-start.22 = (bf16[64,1792]{1,0:T(8,128)(2,1)S(1)}, bf16[64,1792]{1,0:T(8,128)(2,1)S(1)}, u32[]{:S(2)}, u32[]{:S(2)}) collective-permute-start(bf16[64,1792]{1,0:T(8,128)(2,1)S(1)} %pad_maximum_fusion.3), channel_id=1, source_target_pairs={{0,12},{4,8},{8,4},{12,0},{1,13},{5,9},{9,5},{13,1},{2,14},{6,10},... | collective-permute-start | bytes 688136 | tf_op jit(solution)/shard_map/ppermute | solution.py:375
  95.9 7.4 %collective-permute-done.24.refs_9_ = bf16[64,1792]{1,0:T(8,128)(2,1)S(1)} collective-permute-done((bf16[64,1792]{1,0:T(8,128)(2,1)S(1)}, bf16[64,1792]{1,0:T(8,128)(2,1)S(1)}, u32[]{:S(2)}, u32[]{:S(2)}) %collective-permute-start.24) | collective-permute-done | bytes 229408 | tf_op jit(solution)/shard_map/ppermute | solution.py:375
  103.3 7.6 %collective-permute-done.23.refs_8_ = bf16[64,1792]{1,0:T(8,128)(2,1)S(1)} collective-permute-done((bf16[64,1792]{1,0:T(8,128)(2,1)S(1)}, bf16[64,1792]{1,0:T(8,128)(2,1)S(1)}, u32[]{:S(2)}, u32[]{:S(2)}) %collective-permute-start.23) | collective-permute-done | bytes 229408 | tf_op jit(solution)/shard_map/ppermute | solution.py:375
  110.9 1.9 %place.1 = bf16[128,4,1792]{2,1,0:T(4,128)(2,1)} custom-call(bf16[128,1792]{1,0:T(8,128)(2,1)S(1)} %get-tuple-element.65.refs_0_, bf16[128,1792]{1,0:T(8,128)(2,1)S(1)} %collective-permute-done.14.refs_1_, bf16[64,1792]{1,0:T(8,128)(2,1)S(1)} %collective-permute-done.15.refs_2_, bf16[64,1792]{1,0:T(8,128)(2,1)S(1)} %collective-permute-done.16.refs_3_, ...), custom_call_target="tpu_custom_call" | custom-call | flops 1 | bytes 1 | tf_op jit(solution)/shard_map/place/pallas_call | solution.py:617
  (50 shorter events, 0.3 us)
Async XLA Ops:
  0.0 9.7 %copy-start.10 = (s32[64]{0:T(128)S(1)}, s32[64]{0:T(128)}, u32[]{:S(2)}) copy-start(s32[64]{0:T(128)} %param.19) | copy-start | bytes 772
  0.0 10.6 %collective-permute-start = (bf16[4,1792,128]{2,1,0:T(8,128)(2,1)}, bf16[4,1792,128]{2,1,0:T(8,128)(2,1)S(1)}, u32[]{:S(2)}, u32[]{:S(2)}) collective-permute-start(bf16[4,1792,128]{2,1,0:T(8,128)(2,1)} %refs_4_.5), channel_id=1, source_target_pairs={{0,1},{1,0},{2,3},{3,2},{4,5},{5,4},{6,7},{7,6},{8,9},{9,8},{10,11... | collective-permute-start | bytes 5505032 | tf_op jit(solution)/shard_map/ppermute | solution.py:384
  0.5 10.1 %collective-permute-start.1 = (bf16[256,1792]{1,0:T(8,128)(2,1)}, bf16[256,1792]{1,0:T(8,128)(2,1)S(1)}, u32[]{:S(2)}, u32[]{:S(2)}) collective-permute-start(bf16[256,1792]{1,0:T(8,128)(2,1)} %bitcast.10), channel_id=1, source_target_pairs={{0,1},{1,0},{2,3},{3,2},{4,5},{5,4},{6,7},{7,6},{8,9},{9,8},{10,11... | collective-permute-start | bytes 2752520 | tf_op jit(solution)/shard_map/ppermute | solution.py:384
  0.5 9.2 %collective-permute-start.2 = (bf16[256,256]{1,0:T(8,128)(2,1)}, bf16[256,256]{1,0:T(8,128)(2,1)S(1)}, u32[]{:S(2)}, u32[]{:S(2)}) collective-permute-start(bf16[256,256]{1,0:T(8,128)(2,1)} %bitcast.13), channel_id=1, source_target_pairs={{0,1},{1,0},{2,3},{3,2},{4,5},{5,4},{6,7},{7,6},{8,9},{9,8},{10,11... | collective-permute-start | bytes 393224 | tf_op jit(solution)/shard_map/ppermute | solution.py:384
  4.4 13.7 %collective-permute-start.3 = (bf16[32,1792]{1,0:T(8,128)(2,1)}, bf16[32,1792]{1,0:T(8,128)(2,1)S(1)}, u32[]{:S(2)}, u32[]{:S(2)}) collective-permute-start(bf16[32,1792]{1,0:T(8,128)(2,1)} %get-tuple-element.49), channel_id=1, source_target_pairs={{0,4},{4,0},{8,12},{12,8},{1,5},{5,1},{9,13},{13,9},{2,6},{6,2},{1... | collective-permute-start | bytes 344072 | tf_op jit(solution)/shard_map/ppermute | solution.py:375
  7.1 18.5 %collective-permute-start.4 = (bf16[32,1792]{1,0:T(8,128)(2,1)}, bf16[32,1792]{1,0:T(8,128)(2,1)S(1)}, u32[]{:S(2)}, u32[]{:S(2)}) collective-permute-start(bf16[32,1792]{1,0:T(8,128)(2,1)} %get-tuple-element.50), channel_id=1, source_target_pairs={{0,8},{4,12},{8,0},{12,4},{1,9},{5,13},{9,1},{13,5},{2,10},{6,14},... | collective-permute-start | bytes 344072 | tf_op jit(solution)/shard_map/ppermute | solution.py:375
  9.7 15.9 %collective-permute-start.5 = (bf16[32,1792]{1,0:T(8,128)(2,1)}, bf16[32,1792]{1,0:T(8,128)(2,1)S(1)}, u32[]{:S(2)}, u32[]{:S(2)}) collective-permute-start(bf16[32,1792]{1,0:T(8,128)(2,1)} %get-tuple-element.51), channel_id=1, source_target_pairs={{0,12},{4,8},{8,4},{12,0},{1,13},{5,9},{9,5},{13,1},{2,14},{6,10},... | collective-permute-start | bytes 344072 | tf_op jit(solution)/shard_map/ppermute | solution.py:375
  14.4 26.3 %collective-permute-start.7 = (bf16[32,1792]{1,0:T(8,128)(2,1)}, bf16[32,1792]{1,0:T(8,128)(2,1)S(1)}, u32[]{:S(2)}, u32[]{:S(2)}) collective-permute-start(bf16[32,1792]{1,0:T(8,128)(2,1)} %get-tuple-element.44), channel_id=1, source_target_pairs={{0,4},{4,0},{8,12},{12,8},{1,5},{5,1},{9,13},{13,9},{2,6},{6,2},{1... | collective-permute-start | bytes 344072 | tf_op jit(solution)/shard_map/ppermute | solution.py:375
  14.7 26.8 %collective-permute-start.8 = (bf16[32,1792]{1,0:T(8,128)(2,1)}, bf16[32,1792]{1,0:T(8,128)(2,1)S(1)}, u32[]{:S(2)}, u32[]{:S(2)}) collective-permute-start(bf16[32,1792]{1,0:T(8,128)(2,1)} %get-tuple-element.45), channel_id=1, source_target_pairs={{0,8},{4,12},{8,0},{12,4},{1,9},{5,13},{9,1},{13,5},{2,10},{6,14},... | collective-permute-start | bytes 344072 | tf_op jit(solution)/shard_map/ppermute | solution.py:375
  18.1 23.3 %collective-permute-start.9 = (bf16[32,1792]{1,0:T(8,128)(2,1)}, bf16[32,1792]{1,0:T(8,128)(2,1)S(1)}, u32[]{:S(2)}, u32[]{:S(2)}) collective-permute-start(bf16[32,1792]{1,0:T(8,128)(2,1)} %get-tuple-element.46), channel_id=1, source_target_pairs={{0,12},{4,8},{8,4},{12,0},{1,13},{5,9},{9,5},{13,1},{2,14},{6,10},... | collective-permute-start | bytes 344072 | tf_op jit(solution)/shard_map/ppermute | solution.py:375
  19.0 6.7 %copy-start.2 = (bf16[4,1792,128]{2,1,0:T(8,128)(2,1)S(1)}, bf16[4,1792,128]{2,1,0:T(8,128)(2,1)}, u32[]{:S(2)}) copy-start(bf16[4,1792,128]{2,1,0:T(8,128)(2,1)} %refs_4_.5) | copy-start | bytes 5505028
  19.0 6.7 %copy-start.8 = (bf16[32,1792]{1,0:T(8,128)(2,1)S(1)}, bf16[32,1792]{1,0:T(8,128)(2,1)}, u32[]{:S(2)}) copy-start(bf16[32,1792]{1,0:T(8,128)(2,1)} %get-tuple-element.48.refs_0_) | copy-start | bytes 344068
  26.8 9.7 %collective-permute-start.6 = (f32[128,128]{1,0:T(8,128)S(1)}, f32[128,128]{1,0:T(8,128)S(1)}, u32[]{:S(2)}, u32[]{:S(2)}) collective-permute-start(f32[128,128]{1,0:T(8,128)S(1)} %down.2.refs_0_), channel_id=1, source_target_pairs={{0,2},{2,0},{1,3},{3,1},{4,6},{6,4},{5,7},{7,5},{8,10},{10,8},{9,1... | collective-permute-start | bytes 196616 | tf_op jit(solution)/shard_map/ppermute | solution.py:384
  28.4 8.1 %copy-start.5 = (bf16[4,64,1792]{2,1,0:T(8,128)(2,1)S(1)}, bf16[4,64,1792]{2,1,0:T(8,128)(2,1)}, u32[]{:S(2)}) copy-start(bf16[4,64,1792]{2,1,0:T(8,128)(2,1)} %param.23) | copy-start | bytes 2752516
  28.4 8.1 %copy-start.6 = (bf16[4,64,256]{2,1,0:T(8,128)(2,1)S(1)}, bf16[4,64,256]{2,1,0:T(8,128)(2,1)}, u32[]{:S(2)}) copy-start(bf16[4,64,256]{2,1,0:T(8,128)(2,1)} %param.24) | copy-start | bytes 393220
  36.5 5.0 %copy-start.7 = (bf16[32,1792]{1,0:T(8,128)(2,1)S(1)}, bf16[32,1792]{1,0:T(8,128)(2,1)}, u32[]{:S(2)}) copy-start(bf16[32,1792]{1,0:T(8,128)(2,1)} %get-tuple-element.58.refs_0_) | copy-start | bytes 344068
  37.0 14.2 %collective-permute-start.11 = (bf16[32,2048]{1,0:T(8,128)(2,1)S(1)}, bf16[32,2048]{1,0:T(8,128)(2,1)S(1)}, u32[]{:S(2)}, u32[]{:S(2)}) collective-permute-start(bf16[32,2048]{1,0:T(8,128)(2,1)S(1)} %get-tuple-element.55), channel_id=1, source_target_pairs={{0,4},{4,0},{8,12},{12,8},{1,5},{5,1},{9,13},{13,9},{2,6},{6,2},{1... | collective-permute-start | bytes 393224 | tf_op jit(solution)/shard_map/ppermute | solution.py:375
  38.5 13.4 %collective-permute-start.12 = (bf16[32,2048]{1,0:T(8,128)(2,1)S(1)}, bf16[32,2048]{1,0:T(8,128)(2,1)S(1)}, u32[]{:S(2)}, u32[]{:S(2)}) collective-permute-start(bf16[32,2048]{1,0:T(8,128)(2,1)S(1)} %get-tuple-element.56), channel_id=1, source_target_pairs={{0,8},{4,12},{8,0},{12,4},{1,9},{5,13},{9,1},{13,5},{2,10},{6,14},... | collective-permute-start | bytes 393224 | tf_op jit(solution)/shard_map/ppermute | solution.py:375
  40.7 11.2 %collective-permute-start.13 = (bf16[32,2048]{1,0:T(8,128)(2,1)S(1)}, bf16[32,2048]{1,0:T(8,128)(2,1)S(1)}, u32[]{:S(2)}, u32[]{:S(2)}) collective-permute-start(bf16[32,2048]{1,0:T(8,128)(2,1)S(1)} %get-tuple-element.57), channel_id=1, source_target_pairs={{0,12},{4,8},{8,4},{12,0},{1,13},{5,9},{9,5},{13,1},{2,14},{6,10},... | collective-permute-start | bytes 393224 | tf_op jit(solution)/shard_map/ppermute | solution.py:375
  41.5 10.5 %copy-start.3 = (bf16[64,32,256]{2,1,0:T(8,128)(2,1)S(1)}, bf16[64,32,256]{2,1,0:T(8,128)(2,1)}, u32[]{:S(2)}) copy-start(bf16[64,32,256]{2,1,0:T(8,128)(2,1)} %refs_4_.7) | copy-start | bytes 3145732
  41.5 10.5 %copy-start.4 = (bf16[64,32,256]{2,1,0:T(8,128)(2,1)S(1)}, bf16[64,32,256]{2,1,0:T(8,128)(2,1)}, u32[]{:S(2)}) copy-start(bf16[64,32,256]{2,1,0:T(8,128)(2,1)} %refs_5_.3) | copy-start | bytes 3145732
  42.6 9.3 %copy-start = (f32[256,1280]{1,0:T(8,128)S(1)}, f32[256,1280]{1,0:T(8,128)}, u32[]{:S(2)}) copy-start(f32[256,1280]{1,0:T(8,128)} %project.3.refs_7_) | copy-start | bytes 3932164
  42.6 9.3 %copy-start.1 = (f32[256,1024]{1,0:T(8,128)S(1)}, f32[256,1024]{1,0:T(8,128)}, u32[]{:S(2)}) copy-start(f32[256,1024]{1,0:T(8,128)} %project.2.refs_6_) | copy-start | bytes 3145732
  42.6 9.3 %copy-start.9 = (s32[8,64]{1,0:T(8,128)S(1)}, s32[8,64]{1,0:T(8,128)}, u32[]{:S(2)}) copy-start(s32[8,64]{1,0:T(8,128)} %get-tuple-element.67.refs_0_) | copy-start | bytes 6148
  42.7 4.3 %collective-permute-start.10 = (f32[128,128]{1,0:T(8,128)S(1)}, f32[128,128]{1,0:T(8,128)S(1)}, u32[]{:S(2)}, u32[]{:S(2)}) collective-permute-start(f32[128,128]{1,0:T(8,128)S(1)} %down.3.refs_0_), channel_id=1, source_target_pairs={{0,2},{2,0},{1,3},{3,1},{4,6},{6,4},{5,7},{7,5},{8,10},{10,8},{9,1... | collective-permute-start | bytes 196616 | tf_op jit(solution)/shard_map/ppermute | solution.py:384
  47.5 33.7 %collective-permute-start.18 = (bf16[32,2048]{1,0:T(8,128)(2,1)S(1)}, bf16[32,2048]{1,0:T(8,128)(2,1)S(1)}, u32[]{:S(2)}, u32[]{:S(2)}) collective-permute-start(bf16[32,2048]{1,0:T(8,128)(2,1)S(1)} %get-tuple-element.61), channel_id=1, source_target_pairs={{0,4},{4,0},{8,12},{12,8},{1,5},{5,1},{9,13},{13,9},{2,6},{6,2},{1... | collective-permute-start | bytes 393224 | tf_op jit(solution)/shard_map/ppermute | solution.py:375
  48.1 33.0 %collective-permute-start.19 = (bf16[32,2048]{1,0:T(8,128)(2,1)S(1)}, bf16[32,2048]{1,0:T(8,128)(2,1)S(1)}, u32[]{:S(2)}, u32[]{:S(2)}) collective-permute-start(bf16[32,2048]{1,0:T(8,128)(2,1)S(1)} %get-tuple-element.62), channel_id=1, source_target_pairs={{0,8},{4,12},{8,0},{12,4},{1,9},{5,13},{9,1},{13,5},{2,10},{6,14},... | collective-permute-start | bytes 393224 | tf_op jit(solution)/shard_map/ppermute | solution.py:375
  51.2 30.0 %collective-permute-start.20 = (bf16[32,2048]{1,0:T(8,128)(2,1)S(1)}, bf16[32,2048]{1,0:T(8,128)(2,1)S(1)}, u32[]{:S(2)}, u32[]{:S(2)}) collective-permute-start(bf16[32,2048]{1,0:T(8,128)(2,1)S(1)} %get-tuple-element.63), channel_id=1, source_target_pairs={{0,12},{4,8},{8,4},{12,0},{1,13},{5,9},{9,5},{13,1},{2,14},{6,10},... | collective-permute-start | bytes 393224 | tf_op jit(solution)/shard_map/ppermute | solution.py:375
  60.1 1.9 %collective-permute-start.14 = (bf16[128,1792]{1,0:T(8,128)(2,1)S(1)}, bf16[128,1792]{1,0:T(8,128)(2,1)S(1)}, u32[]{:S(2)}, u32[]{:S(2)}) collective-permute-start(bf16[128,1792]{1,0:T(8,128)(2,1)S(1)} %get-tuple-element.66), channel_id=1, source_target_pairs={{0,1},{1,0},{2,3},{3,2},{4,5},{5,4},{6,7},{7,6},{8,9},{9,8},{10,11... | collective-permute-start | bytes 1376264 | tf_op jit(solution)/shard_map/ppermute | solution.py:609
  62.1 17.9 %collective-permute-start.17 = (bf16[64,1792]{1,0:T(8,128)(2,1)S(1)}, bf16[64,1792]{1,0:T(8,128)(2,1)S(1)}, u32[]{:S(2)}, u32[]{:S(2)}) collective-permute-start(bf16[64,1792]{1,0:T(8,128)(2,1)S(1)} %pad_maximum_fusion.2), channel_id=1, source_target_pairs={{0,4},{4,0},{8,12},{12,8},{1,5},{5,1},{9,13},{13,9},{2,6},{6,2},{1... | collective-permute-start | bytes 688136 | tf_op jit(solution)/shard_map/ppermute | solution.py:375
  69.2 26.7 %collective-permute-start.16 = (bf16[64,1792]{1,0:T(8,128)(2,1)S(1)}, bf16[64,1792]{1,0:T(8,128)(2,1)S(1)}, u32[]{:S(2)}, u32[]{:S(2)}) collective-permute-start(bf16[64,1792]{1,0:T(8,128)(2,1)S(1)} %pad_maximum_fusion.1), channel_id=1, source_target_pairs={{0,8},{4,12},{8,0},{12,4},{1,9},{5,13},{9,1},{13,5},{2,10},{6,14},... | collective-permute-start | bytes 688136 | tf_op jit(solution)/shard_map/ppermute | solution.py:375
  79.9 15.9 %collective-permute-start.15 = (bf16[64,1792]{1,0:T(8,128)(2,1)S(1)}, bf16[64,1792]{1,0:T(8,128)(2,1)S(1)}, u32[]{:S(2)}, u32[]{:S(2)}) collective-permute-start(bf16[64,1792]{1,0:T(8,128)(2,1)S(1)} %pad_maximum_fusion), channel_id=1, source_target_pairs={{0,12},{4,8},{8,4},{12,0},{1,13},{5,9},{9,5},{13,1},{2,14},{6,10},... | collective-permute-start | bytes 688136 | tf_op jit(solution)/shard_map/ppermute | solution.py:375
  89.3 1.9 %collective-permute-start.21 = (bf16[128,1792]{1,0:T(8,128)(2,1)S(1)}, bf16[128,1792]{1,0:T(8,128)(2,1)S(1)}, u32[]{:S(2)}, u32[]{:S(2)}) collective-permute-start(bf16[128,1792]{1,0:T(8,128)(2,1)S(1)} %get-tuple-element.70), channel_id=1, source_target_pairs={{0,1},{1,0},{2,3},{3,2},{4,5},{5,4},{6,7},{7,6},{8,9},{9,8},{10,11... | collective-permute-start | bytes 1376264 | tf_op jit(solution)/shard_map/ppermute | solution.py:609
  91.2 12.1 %collective-permute-start.24 = (bf16[64,1792]{1,0:T(8,128)(2,1)S(1)}, bf16[64,1792]{1,0:T(8,128)(2,1)S(1)}, u32[]{:S(2)}, u32[]{:S(2)}) collective-permute-start(bf16[64,1792]{1,0:T(8,128)(2,1)S(1)} %pad_maximum_fusion.5), channel_id=1, source_target_pairs={{0,4},{4,0},{8,12},{12,8},{1,5},{5,1},{9,13},{13,9},{2,6},{6,2},{1... | collective-permute-start | bytes 688136 | tf_op jit(solution)/shard_map/ppermute | solution.py:375
  91.3 19.5 %collective-permute-start.23 = (bf16[64,1792]{1,0:T(8,128)(2,1)S(1)}, bf16[64,1792]{1,0:T(8,128)(2,1)S(1)}, u32[]{:S(2)}, u32[]{:S(2)}) collective-permute-start(bf16[64,1792]{1,0:T(8,128)(2,1)S(1)} %pad_maximum_fusion.4), channel_id=1, source_target_pairs={{0,8},{4,12},{8,0},{12,4},{1,9},{5,13},{9,1},{13,5},{2,10},{6,14},... | collective-permute-start | bytes 688136 | tf_op jit(solution)/shard_map/ppermute | solution.py:375
  94.6 16.3 %collective-permute-start.22 = (bf16[64,1792]{1,0:T(8,128)(2,1)S(1)}, bf16[64,1792]{1,0:T(8,128)(2,1)S(1)}, u32[]{:S(2)}, u32[]{:S(2)}) collective-permute-start(bf16[64,1792]{1,0:T(8,128)(2,1)S(1)} %pad_maximum_fusion.3), channel_id=1, source_target_pairs={{0,12},{4,8},{8,4},{12,0},{1,13},{5,9},{9,5},{13,1},{2,14},{6,10},... | collective-permute-start | bytes 688136 | tf_op jit(solution)/shard_map/ppermute | solution.py:375

commit v6 on v5

--- a/solution.py
+++ b/solution.py
@@ -16,10 +16,12 @@
 PER_GROUP = QUERY_HEADS // KEY_VALUE_HEADS
 LANE_AXES = ("streams", "sub")
 BATCH = 8
+TOGETHER = 2
 VMEM = pl.BlockSpec(memory_space=pltpu.VMEM)
 MIB = 1 << 20
 PACK_LIMIT = 56
 PROJECT_LIMIT = 56
+DEPTH_CUTS = 4
 
 
 def iota(shape, dim):
@@ -126,12 +128,17 @@
     pack_messages(steps, rows, places_ref[0:1, :], normed_ref, message_refs)
 
 
-def project_kernel(first_tile, rows_ref, weight_ref, bias_ref, out_ref):
-    tiles = weight_ref.shape[1] // 128
+def project_kernel(first_tile, rows_ref, bias_ref, *refs):
+    weight_refs, out_ref = refs[:-1], refs[-1]
+    depth, columns = weight_refs[0].shape
+    tiles = columns // 128
     tile = first_tile + pl.program_id(0) * tiles
     bias = [bias_ref[pl.ds(tile + number, 1), :] for number in range(tiles)]
-    product = jnp.dot(rows_ref[...], weight_ref[...], preferred_element_type=jnp.float32)
-    out_ref[...] = product + jnp.concatenate(bias, axis=1)
+    total = jnp.concatenate(bias, axis=1)
+    for number, ref in enumerate(weight_refs):
+        rows = rows_ref[:, number * depth : (number + 1) * depth]
+        total = total + jnp.dot(rows, ref[...], preferred_element_type=jnp.float32)
+    out_ref[...] = total
 
 
 def row_slots(shape, spots):
@@ -198,8 +205,8 @@
         earlier_ref, refs = refs[0], refs[1:]
     if not last:
         fresh_ref, refs = refs[0], refs[1:]
-    message_refs = refs[:subs]
-    delta_ref, context_ref, bias_ref = refs[subs:]
+    message_refs = refs[:lanes]
+    delta_ref, context_ref, bias_ref = refs[lanes:]
     per_message = delta_refs[0].shape[0]
     spots = per_message // steps
     query_width = PER_GROUP * HEAD_WIDTH
@@ -241,105 +248,109 @@
     scale = HEAD_WIDTH ** (-0.5)
     transposed = (((1,), (1,)), ((), ()))
 
+    def scored(first, group):
+        spans = [pl.ds(pl.multiple_of(step * rows + first, BATCH), BATCH) for step in range(known)]
+        query_tiles, key_tiles, value_tiles = [], [], []
+        lane_span = slice(group * HEAD_WIDTH, (group + 1) * HEAD_WIDTH)
+        value_span = slice(wide + group * HEAD_WIDTH, wide + (group + 1) * HEAD_WIDTH)
+        for span in spans[:before]:
+            key_tiles.append(earlier_ref[span, lane_span])
+            value_tiles.append(earlier_ref[span, value_span])
+        for span in spans[:steps]:
+            cosine, sine_part = cos_ref[span, :], sin_ref[span, :]
+
+            def rotated(values):
+                return values * cosine + pltpu.roll(values, HEAD_WIDTH // 2, 1) * sine_part
+
+            for head in range(PER_GROUP):
+                begin = group * query_width + head * HEAD_WIDTH
+                change = delta_ref[span, begin : begin + HEAD_WIDTH]
+                query_tiles.append(rotated(qkv_tile(span, group, head) + change))
+            key = rotated(qkv_tile(span, group, PER_GROUP))
+            begin = groups * query_width + group * HEAD_WIDTH
+            change = delta_ref[span, begin : begin + HEAD_WIDTH]
+            value = qkv_tile(span, group, PER_GROUP + 1) + change
+            if not last:
+                fresh_ref[span, lane_span] = key
+                fresh_ref[span, value_span] = value
+            key_tiles.append(key)
+            value_tiles.append(value)
+        queries = jnp.concatenate(query_tiles, axis=0).astype(jnp.bfloat16)
+        new_keys = jnp.concatenate(key_tiles, axis=0).astype(jnp.bfloat16)
+        new_values = jnp.concatenate(value_tiles, axis=0).astype(jnp.bfloat16)
+        old_keys = key_ref[pl.ds(first, BATCH), :, lane_span].reshape(BATCH * cache, HEAD_WIDTH)
+        old_scores = lax.dot_general(
+            queries, old_keys, transposed, preferred_element_type=jnp.float32
+        )
+        new_scores = lax.dot_general(
+            queries, new_keys, transposed, preferred_element_type=jnp.float32
+        )
+        return old_scores, new_scores, new_values
+
+    def weighed(first, old_scores, new_scores):
+        heads = steps * PER_GROUP
+        old_scores = (old_scores * scale).reshape(heads, BATCH, BATCH * cache)
+        old_scores = old_scores + bias_ref[pl.ds(first, BATCH), :][None]
+        new_scores = (new_scores * scale).reshape(steps, PER_GROUP, BATCH, known * BATCH)
+        new_scores = (new_scores + fresh_bias[:, None]).reshape(heads, BATCH, known * BATCH)
+        peak = jnp.maximum(
+            jnp.max(old_scores, axis=-1, keepdims=True),
+            jnp.max(new_scores, axis=-1, keepdims=True),
+        )
+        old_scores = jnp.exp(old_scores - peak)
+        new_scores = jnp.exp(new_scores - peak)
+        share = 1.0 / (
+            jnp.sum(old_scores, axis=-1, keepdims=True)
+            + jnp.sum(new_scores, axis=-1, keepdims=True)
+        )
+        old_weights = (old_scores * share).reshape(heads * BATCH, BATCH * cache)
+        new_weights = (new_scores * share).reshape(heads * BATCH, known * BATCH)
+        return old_weights.astype(jnp.bfloat16), new_weights.astype(jnp.bfloat16)
+
     def batch(index, carry):
-        first = pl.multiple_of(index * BATCH, BATCH)
-        spans = [pl.ds(pl.multiple_of(step * rows + first, BATCH), BATCH) for step in range(steps)]
-        past = [pl.ds(pl.multiple_of(step * rows + first, BATCH), BATCH) for step in range(before)]
-        for group in range(groups):
-            query_tiles, key_tiles, value_tiles = [], [], []
+        chains = []
+        for number in range(TOGETHER):
+            first = pl.multiple_of((index * TOGETHER + number) * BATCH, BATCH)
+            chains += [(first, group) for group in range(groups)]
+        scores = [scored(*chain) for chain in chains]
+        weights = [weighed(chain[0], *score[:2]) for chain, score in zip(chains, scores)]
+        for (first, group), (old_weights, new_weights), score in zip(chains, weights, scores):
             lane_span = slice(group * HEAD_WIDTH, (group + 1) * HEAD_WIDTH)
-            value_span = slice(wide + group * HEAD_WIDTH, wide + (group + 1) * HEAD_WIDTH)
-            for span in past:
-                key_tiles.append(earlier_ref[span, lane_span])
-                value_tiles.append(earlier_ref[span, value_span])
-            for span in spans:
-                cosine, sine_part = cos_ref[span, :], sin_ref[span, :]
-
-                def rotated(values):
-                    return values * cosine + pltpu.roll(values, HEAD_WIDTH // 2, 1) * sine_part
-
-                for head in range(PER_GROUP):
-                    begin = group * query_width + head * HEAD_WIDTH
-                    change = delta_ref[span, begin : begin + HEAD_WIDTH]
-                    query_tiles.append(rotated(qkv_tile(span, group, head) + change))
-                key = rotated(qkv_tile(span, group, PER_GROUP))
-                begin = groups * query_width + group * HEAD_WIDTH
-                change = delta_ref[span, begin : begin + HEAD_WIDTH]
-                value = qkv_tile(span, group, PER_GROUP + 1) + change
-                if not last:
-                    fresh_ref[span, lane_span] = key
-                    fresh_ref[span, value_span] = value
-                key_tiles.append(key)
-                value_tiles.append(value)
-            queries = jnp.concatenate(query_tiles, axis=0).astype(jnp.bfloat16)
-            new_keys = jnp.concatenate(key_tiles, axis=0).astype(jnp.bfloat16)
-            new_values = jnp.concatenate(value_tiles, axis=0).astype(jnp.bfloat16)
-            old_keys = key_ref[pl.ds(first, BATCH), :, lane_span]
-            old_keys = old_keys.reshape(BATCH * cache, HEAD_WIDTH)
             old_values = value_ref[pl.ds(first, BATCH), :, lane_span]
             old_values = old_values.reshape(BATCH * cache, HEAD_WIDTH)
-            old_scores = lax.dot_general(
-                queries, old_keys, transposed, preferred_element_type=jnp.float32
-            )
-            new_scores = lax.dot_general(
-                queries, new_keys, transposed, preferred_element_type=jnp.float32
-            )
-            heads = steps * PER_GROUP
-            old_scores = (old_scores * scale).reshape(heads, BATCH, BATCH * cache) + bias_ref[
-                pl.ds(first, BATCH), :
-            ][None]
-            new_scores = (new_scores * scale).reshape(
-                steps, PER_GROUP, BATCH, known * BATCH
-            ) + fresh_bias[:, None]
-            new_scores = new_scores.reshape(heads, BATCH, known * BATCH)
-            peak = jnp.maximum(
-                jnp.max(old_scores, axis=-1, keepdims=True),
-                jnp.max(new_scores, axis=-1, keepdims=True),
-            )
-            old_scores = jnp.exp(old_scores - peak)
-            new_scores = jnp.exp(new_scores - peak)
-            share = 1.0 / (
-                jnp.sum(old_scores, axis=-1, keepdims=True)
-                + jnp.sum(new_scores, axis=-1, keepdims=True)
-            )
-            old_weights = (old_scores * share).reshape(heads * BATCH, BATCH * cache)
-            new_weights = (new_scores * share).reshape(heads * BATCH, known * BATCH)
             context = jnp.dot(
-                old_weights.astype(jnp.bfloat16), old_values, preferred_element_type=jnp.float32
-            ) + jnp.dot(
-                new_weights.astype(jnp.bfloat16), new_values, preferred_element_type=jnp.float32
-            )
-            for step, span in enumerate(spans):
+                old_weights, old_values, preferred_element_type=jnp.float32
+            ) + jnp.dot(new_weights, score[2], preferred_element_type=jnp.float32)
+            for step in range(steps):
+                span = pl.ds(pl.multiple_of(step * rows + first, BATCH), BATCH)
                 for head in range(PER_GROUP):
                     row = (step * PER_GROUP + head) * BATCH
                     begin = group * query_width + head * HEAD_WIDTH
                     context_ref[span, begin : begin + HEAD_WIDTH] = context[row : row + BATCH]
         return carry
 
-    lax.fori_loop(0, rows // BATCH, batch, 0)
+    lax.fori_loop(0, rows // (BATCH * TOGETHER), batch, 0)
 
     flow_places = jnp.concatenate([places_ref[1:2, :]] * steps, axis=1)
     context = context_ref[...].astype(jnp.bfloat16)
     count = message_refs[0].shape[0]
-    most = count // (lanes * steps)
     shape = (count, steps * rows)
     out_row = iota(shape, 0)
-    spot = out_row // steps
     same_step = out_row % steps == iota(shape, 1) // rows
     for number, message_ref in enumerate(message_refs):
-        wanted = (spot // most * subs + number) * most + spot % most
+        wanted = number * (count // steps) + out_row // steps
         pick = ((flow_places == wanted) & same_step).astype(jnp.float32).astype(jnp.bfloat16)
         message_ref[...] = jnp.dot(
             pick, context, preferred_element_type=jnp.float32
         ).astype(jnp.bfloat16)
 
 
-def place_kernel(chunks, lanes, subs, most, *refs):
+def place_kernel(found, lanes, subs, most, *refs):
+    chunks = len(found)
     out_ref = refs[-1]
     steps = out_ref.shape[1]
     chunk_steps = steps // chunks
     block = most * chunk_steps
-    per_chunk = subs + lanes - 1
     here = lax.axis_index("streams")
     core = lax.axis_index("sub")
     shape = (chunks * block, chunks * block)
@@ -351,12 +362,8 @@
         for other in range(subs):
             pieces = []
             for chunk in range(chunks):
-                mine = refs[chunk * per_chunk : (chunk + 1) * per_chunk]
-                if number == 0:
-                    pieces.append(mine[other][...][:block])
-                else:
-                    landed = mine[subs + lanes - 1 - number]
-                    pieces.append(landed[...][other * block : (other + 1) * block])
+                array, begin = found[chunk][number][other]
+                pieces.append(refs[array][...][begin : begin + block])
             rows = jnp.dot(
                 pick, jnp.concatenate(pieces, axis=0), preferred_element_type=jnp.float32
             )
@@ -482,7 +489,8 @@
         )(*operands)
         if first:
             places, *messages = messages
-        arrived.append(traded(messages, "streams"))
+        if first:
+            arrived.append(traded(messages, "streams"))
 
     bias = projection_bias.reshape(-1, 128)
     columns = projection_weight.shape[1]
@@ -493,17 +501,20 @@
         return pl.pallas_call(
             functools.partial(project_kernel, begin * block_columns // 128),
             grid=(end - begin,),
-            in_specs=[
-                whole(normed_shape.shape),
-                pl.BlockSpec((width, block_columns), lambda i: (0, begin + i)),
-                whole(bias.shape),
+            in_specs=[whole(normed_shape.shape), whole(bias.shape)]
+            + [
+                pl.BlockSpec(
+                    (width // DEPTH_CUTS, block_columns),
+                    lambda i, number=number: (number, begin + i),
+                )
+                for number in range(DEPTH_CUTS)
             ],
             out_specs=pl.BlockSpec((steps * rows, block_columns), lambda i: (0, i)),
             out_shape=jax.ShapeDtypeStruct((steps * rows, (end - begin) * block_columns), f32),
             compiler_params=pltpu.CompilerParams(vmem_limit_bytes=PROJECT_LIMIT * MIB),
             cost_estimate=SMALL,
             name="project",
-        )(normed, projection_weight, held(bias, after))
+        )(normed, held(bias, after), *[projection_weight] * DEPTH_CUTS)
 
     def down(chunk, after):
         partial_latent = pl.pallas_call(
@@ -528,10 +539,14 @@
             cost_estimate=SMALL,
             name="up",
         )(held(partials[0], after), *partials[1:], *query_maps, *value_maps)
-        return messages, traded(messages, "streams")
+        return messages
 
     cut = blocks // 2
     qkv = [project(0, cut, messages)]
+    messages = [messages[0]] + [
+        held(message, (before, qkv)) for message, before in zip(messages[1:], arrived[0][1:])
+    ]
+    arrived.append(traded(messages, "streams"))
     partials = down(0, qkv)
     qkv.append(project(cut, blocks, partials[0]))
 
@@ -549,16 +564,19 @@
     for chunk in range(chunks):
         if chunk:
             partials = down(chunk, after)
-        after, arrivals = up(partials, after)
-        returned.append(arrivals)
+        after = up(partials, after)
+        messages = list(after)
+        if chunk:
+            for lane in range(1, lanes):
+                messages[lane] = held(messages[lane], returned[-1][lane])
+        returned.append(traded(messages, "streams"))
 
     length_row = cache_fill_length.reshape(1, rows)
     block = flow_most * chunk_steps
-    landed = []
-    earlier = []
+    earlier, along, alongs = [], [], []
     for chunk in range(chunks):
         last = chunk == chunks - 1
-        message = jax.ShapeDtypeStruct((lanes * block, query_columns), bf16)
+        message = jax.ShapeDtypeStruct((subs * block, query_columns), bf16)
         fresh = jax.ShapeDtypeStruct((chunk_rows, 2 * value_columns), f32)
         rows_of = lambda shape: pl.BlockSpec(shape, lambda i, chunk=chunk: (chunk, 0))
         results = pl.pallas_call(
@@ -580,8 +598,8 @@
             + [rows_of((chunk_rows, part.shape[1])) for part in qkv]
             + [whole((per_message, query_columns + value_columns))] * lanes
             + [whole(block_rows.shape) for block_rows in earlier],
-            out_specs=[whole(fresh.shape)] * (not last) + [whole(message.shape)] * subs,
-            out_shape=[fresh] * (not last) + [message] * subs,
+            out_specs=[whole(fresh.shape)] * (not last) + [whole(message.shape)] * lanes,
+            out_shape=[fresh] * (not last) + [message] * lanes,
             scratch_shapes=[
                 pltpu.VMEM((chunk_rows, query_columns + value_columns), f32),
                 pltpu.VMEM((chunk_rows, query_columns), f32),
@@ -591,7 +609,7 @@
             cost_estimate=SMALL,
             name="attend",
         )(
-            held(places, landed[-1] if landed else after),
+            places if chunk else held(places, after),
             length_row,
             cosine,
             sine_part,
@@ -603,19 +621,34 @@
         )
         if not last:
             earlier, results = [results[0]], results[1:]
-        parts = [results[0]]
+        results = list(results)
+        ahead = along or returned[-1]
+        for lane in range(1, lanes):
+            results[lane] = held(results[lane], ahead[1:])
+        along = traded(results, "streams")
+        alongs.append(along)
+
+    landed, found = [], []
+    for chunk, along in enumerate(alongs):
+        base = len(landed)
+        landed += along
+        where = [[(base + lane, 0)] for lane in range(lanes)]
         for shift in range(1, subs):
             pairs = [(core, core ^ shift) for core in range(subs)]
-            parts.append(lax.ppermute(results[shift], "sub", pairs))
-        joined = [
-            jnp.concatenate([part[lane * block : (lane + 1) * block] for part in parts])
-            for lane in range(1, lanes)
-        ]
-        joined = traded([None] + joined, "streams")[1:]
-        landed += parts + joined[::-1]
+            span = slice(shift * block, (shift + 1) * block)
+            if chunk < chunks - 1:
+                joined = jnp.concatenate([block_rows[span] for block_rows in along])
+                for lane in range(lanes):
+                    where[lane].append((len(landed), lane * block))
+                landed.append(lax.ppermute(joined, "sub", pairs))
+            else:
+                for lane, block_rows in enumerate(along):
+                    where[lane].append((len(landed), shift * block))
+                    landed.append(lax.ppermute(block_rows, "sub", pairs))
+        found.append(where)
 
     flow = pl.pallas_call(
-        functools.partial(place_kernel, chunks, lanes, subs, flow_most),
+        functools.partial(place_kernel, found, lanes, subs, flow_most),
         in_specs=[VMEM] * len(landed),
         out_specs=VMEM,
         out_shape=jax.ShapeDtypeStruct((flow_lanes * flow_most, steps, query_columns), bf16),

time: 115 us -> 105 us (0.913); the launches traced: 113 us -> 105 us
  Pallas kernels: 43.5 us -> 35.3 us
  waiting for transfers between devices: 31.3 us -> 37.1 us
  starting transfers between devices: 36.8 us -> 31.6 us
    pallas_call x2, Pallas kernels: 16.3 us -> 7.38 us  [on_device(): pl.pallas_call(functools.partial(attend_kernel, chunk * chunk_steps, chun...]
    ppermute x18, waiting for transfers between devices: 24.5 us -> 32 us  [traded(): landed[shift] = lax.ppermute(blocks[shift], axes, pairs)]
    ppermute x18, starting transfers between devices: 33.6 us -> 27.7 us  [traded(): landed[shift] = lax.ppermute(blocks[shift], axes, pairs)]
    ppermute x2 -> x5, waiting for transfers between devices: 3.54 us -> 1.3 us  [the longest x4 1.29 us: on_device(): landed.append(lax.ppermute(block_rows, 'sub', pairs))]
  transfers between devices with their start and end apart: 25 -> 28, of which waited for: 6 -> 10; matrix products, arithmetic and copies ran while one was open for 1% -> 1% of each run, Pallas kernels for 37% -> 32%
where the time goes in v6:
time: 105 us
  waiting for transfers between devices  37.1 us (35%)
  Pallas kernels  35.3 us (34%)
  starting transfers between devices  31.6 us (30%)
    ppermute x18, waiting for transfers between devices, traded(): landed[shift] = lax.ppermute(blocks[shift], axes, pairs)  32 us
    ppermute x18, starting transfers between devices, traded(): landed[shift] = lax.ppermute(blocks[shift], axes, pairs)  27.7 us
    pallas_call x2, Pallas kernels, project(): pl.pallas_call(functools.partial(project_kernel, begin * block_columns //...  15.5 us
    pallas_call x2, Pallas kernels, on_device(): pl.pallas_call(functools.partial(attend_kernel, chunk * chunk_steps, chun...  7.38 us
    pallas_call x2, Pallas kernels, on_device(): pl.pallas_call(functools.partial(norm_pack_kernel, chunk_steps, rows, flo...  7.32 us
    ppermute x5, waiting for transfers between devices, from_others(): landed.append(lax.ppermute(block, axis, pairs))  3.83 us
    ppermute x5, starting transfers between devices, from_others(): landed.append(lax.ppermute(block, axis, pairs))  3.12 us
    pallas_call x2, Pallas kernels, down(): pl.pallas_call(functools.partial(down_kernel, lanes, spots), in_specs=[VM...  2.22 us
  transfers between devices with their start and end apart: 28, of which 10 were waited for; matrix products, arithmetic and copies ran while one was open for 1% of the time, Pallas kernels for 32%

profile of v6, /device:TPU:0, one launch (start us, length us, event | category | flops | bytes accessed | tf_op | source)
XLA Modules:
  0.0 105.2 jit_solution(8126836093175203249)
XLA Ops:
  0.0 0.5 collective-permute-start
  0.5 0.1 collective-permute-start.1
  0.5 0.5 collective-permute-start.2
  1.0 3.5 %norm_and_pack.2 = (bf16[256,3584]{1,0:T(8,128)(2,1)}, s32[8,64]{1,0:T(8,128)}, bf16[32,1792]{1,0:T(8,128)(2,1)}, bf16[32,1792]{1,0:T(8,128)(2,1)}, bf16[32,1792]{1,0:T(8,128)(2,1)}, /*index=5*/bf16[32,1792]{1,0:T(8,128)(2,1)}) custom-call(s32[1,64]{1,0:T(1,128)} %bitcast.24, s32[1,32]{1,0:T(1,128)} %bitcast.25, s32[1,64]{1,0:T(1,128)} %bitcast.26, ...), custom_call_target="tpu_custom_call" | custom-call | flops 1 | bytes 1 | tf_op jit(solution)/shard_map/norm_and_pack/pallas_call | solution.py:472
  4.4 4.7 %collective-permute-start.5 = (bf16[32,1792]{1,0:T(8,128)(2,1)}, bf16[32,1792]{1,0:T(8,128)(2,1)S(1)}, u32[]{:S(2)}, u32[]{:S(2)}) collective-permute-start(bf16[32,1792]{1,0:T(8,128)(2,1)} %get-tuple-element.66), channel_id=1, source_target_pairs={{0,12},{4,8},{8,4},{12,0},{1,13},{5,9},{9,5},{13,1},{2,14},{6,10},... | collective-permute-start | bytes 344072 | tf_op jit(solution)/shard_map/ppermute | solution.py:382
  9.1 0.6 collective-permute-start.3
  9.7 3.9 %norm_and_pack.3 = (bf16[256,3584]{1,0:T(8,128)(2,1)}, bf16[32,1792]{1,0:T(8,128)(2,1)}, bf16[32,1792]{1,0:T(8,128)(2,1)}, bf16[32,1792]{1,0:T(8,128)(2,1)}, bf16[32,1792]{1,0:T(8,128)(2,1)}) custom-call(s32[8,64]{1,0:T(8,128)} %get-tuple-element.82.refs_0_, f32[28,128]{1,0:T(8,128)} %bitcast.21, ...), custom_call_target="tpu_custom_call", output_to_operand_aliasing={{0}: (3, {})} | custom-call | flops 1 | bytes 1 | tf_op jit(solution)/shard_map/norm_and_pack/pallas_call | solution.py:472
  13.6 0.0 copy-start.10
  13.7 0.0 copy-start.2
  13.7 7.1 %project.2.refs_6_ = f32[256,1024]{1,0:T(8,128)} custom-call(bf16[256,3584]{1,0:T(8,128)(2,1)} %get-tuple-element.58.rows_ref, f32[18,128]{1,0:T(8,128)} %bitcast.22, bf16[3584,2304]{1,0:T(8,128)(2,1)} %refs_3_.3, bf16[3584,2304]{1,0:T(8,128)(2,1)} %refs_3_.3, bf16[3584,2304]{1,0:T(8,128)(2,1)} %refs_3_.3, bf16[3584,2304]{1,0:T(8,128)(2,1)} %refs_3_.3), custom_call_target="tpu_custom_call" | custom-call | flops 1 | bytes 1 | tf_op jit(solution)/shard_map/project/pallas_call | solution.py:501
  20.8 3.8 %collective-permute-start.9 = (bf16[32,1792]{1,0:T(8,128)(2,1)S(1)}, bf16[32,1792]{1,0:T(8,128)(2,1)S(1)}, u32[]{:S(2)}, u32[]{:S(2)}) collective-permute-start(bf16[32,1792]{1,0:T(8,128)(2,1)S(1)} %copy-done.13), channel_id=1, source_target_pairs={{0,12},{4,8},{8,4},{12,0},{1,13},{5,9},{9,5},{13,1},{2,14},{6,10},... | collective-permute-start | bytes 344072 | tf_op jit(solution)/shard_map/ppermute | solution.py:382
  24.7 0.1 collective-permute-start.8
  24.8 0.6 collective-permute-start.7
  25.4 1.1 %down.2.refs_0_ = f32[128,128]{1,0:T(8,128)S(1)} custom-call(bf16[32,1792]{1,0:T(8,128)(2,1)S(1)} %copy-done.8, bf16[32,1792]{1,0:T(8,128)(2,1)S(1)} %collective-permute-done.3.refs_1_, bf16[32,1792]{1,0:T(8,128)(2,1)S(1)} %collective-permute-done.4.refs_2_, bf16[32,1792]{1,0:T(8,128)(2,1)S(1)} %collective-permute-done.5.refs_3_, ...), custom_call_target="tpu_custom_call" | custom-call | flops 1 | bytes 1 | tf_op jit(solution)/shard_map/down/pallas_call | solution.py:520
  26.5 1.7 %collective-permute-start.6 = (f32[128,128]{1,0:T(8,128)S(1)}, f32[128,128]{1,0:T(8,128)S(1)}, u32[]{:S(2)}, u32[]{:S(2)}) collective-permute-start(f32[128,128]{1,0:T(8,128)S(1)} %down.2.refs_0_), channel_id=1, source_target_pairs={{0,2},{2,0},{1,3},{3,1},{4,6},{6,4},{5,7},{7,5},{8,10},{10,8},{9,1... | collective-permute-start | bytes 196616 | tf_op jit(solution)/shard_map/ppermute | solution.py:391
  28.2 8.3 %project.3.refs_7_ = f32[256,1280]{1,0:T(8,128)} custom-call(bf16[256,3584]{1,0:T(8,128)(2,1)} %get-tuple-element.58.rows_ref, f32[18,128]{1,0:T(8,128)} %bitcast.23, bf16[3584,2304]{1,0:T(8,128)(2,1)} %refs_3_.3, bf16[3584,2304]{1,0:T(8,128)(2,1)} %refs_3_.3, bf16[3584,2304]{1,0:T(8,128)(2,1)} %refs_3_.3, bf16[3584,2304]{1,0:T(8,128)(2,1)} %refs_3_.3), custom_call_target="tpu_custom_call" | custom-call | flops 1 | bytes 1 | tf_op jit(solution)/shard_map/project/pallas_call | solution.py:501
  36.6 0.5 up.2
  37.1 3.6 %collective-permute-start.13 = (bf16[32,2048]{1,0:T(8,128)(2,1)S(1)}, bf16[32,2048]{1,0:T(8,128)(2,1)S(1)}, u32[]{:S(2)}, u32[]{:S(2)}) collective-permute-start(bf16[32,2048]{1,0:T(8,128)(2,1)S(1)} %get-tuple-element.72), channel_id=1, source_target_pairs={{0,12},{4,8},{8,4},{12,0},{1,13},{5,9},{9,5},{13,1},{2,14},{6,10},... | collective-permute-start | bytes 393224 | tf_op jit(solution)/shard_map/ppermute | solution.py:382
  40.7 0.8 collective-permute-start.11
  41.5 0.1 compare_select_fusion
  41.6 0.0 copy-start.3
  41.7 1.1 %down.3.refs_0_ = f32[128,128]{1,0:T(8,128)S(1)} custom-call(bf16[32,1792]{1,0:T(8,128)(2,1)S(1)} %copy-done.7, bf16[32,1792]{1,0:T(8,128)(2,1)S(1)} %collective-permute-done.7.refs_1_, bf16[32,1792]{1,0:T(8,128)(2,1)S(1)} %collective-permute-done.8.refs_2_, bf16[32,1792]{1,0:T(8,128)(2,1)S(1)} %collective-permute-done.9.refs_3_, ...), custom_call_target="tpu_custom_call" | custom-call | flops 1 | bytes 1 | tf_op jit(solution)/shard_map/down/pallas_call | solution.py:520
  42.8 0.4 collective-permute-start.10
  43.2 0.1 add_convert_fusion
  43.3 3.8 %collective-permute-done.10.refs_1_ = f32[128,128]{1,0:T(8,128)S(1)} collective-permute-done((f32[128,128]{1,0:T(8,128)S(1)}, f32[128,128]{1,0:T(8,128)S(1)}, u32[]{:S(2)}, u32[]{:S(2)}) %collective-permute-start.10) | collective-permute-done | bytes 65568 | tf_op jit(solution)/shard_map/ppermute | solution.py:391
  47.1 0.5 up.3
  47.6 3.6 %collective-permute-start.16 = (bf16[32,2048]{1,0:T(8,128)(2,1)S(1)}, bf16[32,2048]{1,0:T(8,128)(2,1)S(1)}, u32[]{:S(2)}, u32[]{:S(2)}) collective-permute-start(bf16[32,2048]{1,0:T(8,128)(2,1)S(1)} %get-tuple-element.87), channel_id=1, source_target_pairs={{0,12},{4,8},{8,4},{12,0},{1,13},{5,9},{9,5},{13,1},{2,14},{6,10},... | collective-permute-start | bytes 393224 | tf_op jit(solution)/shard_map/ppermute | solution.py:382
  51.3 4.5 %collective-permute-done.12.refs_10_ = bf16[32,2048]{1,0:T(8,128)(2,1)S(1)} collective-permute-done((bf16[32,2048]{1,0:T(8,128)(2,1)S(1)}, bf16[32,2048]{1,0:T(8,128)(2,1)S(1)}, u32[]{:S(2)}, u32[]{:S(2)}) %collective-permute-start.12) | collective-permute-done | bytes 131104 | tf_op jit(solution)/shard_map/ppermute | solution.py:382
  55.8 1.0 collective-permute-start.14
  56.8 0.5 fusion
  57.4 3.7 %attend.2 = (f32[128,512]{1,0:T(8,128)S(1)}, bf16[64,1792]{1,0:T(8,128)(2,1)S(1)}, bf16[64,1792]{1,0:T(8,128)(2,1)S(1)}, bf16[64,1792]{1,0:T(8,128)(2,1)S(1)}, bf16[64,1792]{1,0:T(8,128)(2,1)S(1)}) custom-call(s32[8,64]{1,0:T(8,128)S(1)} %copy-done.9, s32[1,64]{1,0:T(1,128)S(1)} %bitcast.16, f32[256,128]{1,0:T(8,128)S(1)} %get-tuple-element.102.refs_2_, ...), custom_call_target="tpu_custom_call" | custom-call | flops 1 | bytes 1 | tf_op jit(solution)/shard_map/attend/pallas_call | solution.py:582
  61.1 1.3 %collective-permute-done.15.refs_10_ = bf16[32,2048]{1,0:T(8,128)(2,1)S(1)} collective-permute-done((bf16[32,2048]{1,0:T(8,128)(2,1)S(1)}, bf16[32,2048]{1,0:T(8,128)(2,1)S(1)}, u32[]{:S(2)}, u32[]{:S(2)}) %collective-permute-start.15) | collective-permute-done | bytes 131104 | tf_op jit(solution)/shard_map/ppermute | solution.py:382
  62.4 0.2 collective-permute-done.14.refs_9_
  62.6 2.0 %collective-permute-start.19 = (bf16[64,1792]{1,0:T(8,128)(2,1)S(1)}, bf16[64,1792]{1,0:T(8,128)(2,1)S(1)}, u32[]{:S(2)}, u32[]{:S(2)}) collective-permute-start(bf16[64,1792]{1,0:T(8,128)(2,1)S(1)} %get-tuple-element.92), channel_id=1, source_target_pairs={{0,12},{4,8},{8,4},{12,0},{1,13},{5,9},{9,5},{13,1},{2,14},{6,10},... | collective-permute-start | bytes 688136 | tf_op jit(solution)/shard_map/ppermute | solution.py:382
  64.6 2.4 %collective-permute-start.17 = (bf16[64,1792]{1,0:T(8,128)(2,1)S(1)}, bf16[64,1792]{1,0:T(8,128)(2,1)S(1)}, u32[]{:S(2)}, u32[]{:S(2)}) collective-permute-start(bf16[64,1792]{1,0:T(8,128)(2,1)S(1)} %get-tuple-element.88), channel_id=1, source_target_pairs={{0,4},{4,0},{8,12},{12,8},{1,5},{5,1},{9,13},{13,9},{2,6},{6,2},{1... | collective-permute-start | bytes 688136 | tf_op jit(solution)/shard_map/ppermute | solution.py:382
  67.0 3.7 %attend.3 = (bf16[64,1792]{1,0:T(8,128)(2,1)S(1)}, bf16[64,1792]{1,0:T(8,128)(2,1)S(1)}, bf16[64,1792]{1,0:T(8,128)(2,1)S(1)}, bf16[64,1792]{1,0:T(8,128)(2,1)S(1)}) custom-call(s32[8,64]{1,0:T(8,128)S(1)} %copy-done.9, s32[1,64]{1,0:T(1,128)S(1)} %bitcast.17, f32[256,128]{1,0:T(8,128)S(1)} %get-tuple-element.102.refs_2_, ...), custom_call_target="tpu_custom_call" | custom-call | flops 1 | bytes 1 | tf_op jit(solution)/shard_map/attend/pallas_call | solution.py:582
  70.7 2.2 %collective-permute-done.19.refs_3_ = bf16[64,1792]{1,0:T(8,128)(2,1)S(1)} collective-permute-done((bf16[64,1792]{1,0:T(8,128)(2,1)S(1)}, bf16[64,1792]{1,0:T(8,128)(2,1)S(1)}, u32[]{:S(2)}, u32[]{:S(2)}) %collective-permute-start.19) | collective-permute-done | bytes 229408 | tf_op jit(solution)/shard_map/ppermute | solution.py:382
  73.0 8.6 %collective-permute-done.18.refs_2_ = bf16[64,1792]{1,0:T(8,128)(2,1)S(1)} collective-permute-done((bf16[64,1792]{1,0:T(8,128)(2,1)S(1)}, bf16[64,1792]{1,0:T(8,128)(2,1)S(1)}, u32[]{:S(2)}, u32[]{:S(2)}) %collective-permute-start.18) | collective-permute-done | bytes 229408 | tf_op jit(solution)/shard_map/ppermute | solution.py:382
  81.6 2.9 %collective-permute-start.23 = (bf16[64,1792]{1,0:T(8,128)(2,1)S(1)}, bf16[64,1792]{1,0:T(8,128)(2,1)S(1)}, u32[]{:S(2)}, u32[]{:S(2)}) collective-permute-start(bf16[64,1792]{1,0:T(8,128)(2,1)S(1)} %get-tuple-element.100), channel_id=1, source_target_pairs={{0,12},{4,8},{8,4},{12,0},{1,13},{5,9},{9,5},{13,1},{2,14},{6,10},... | collective-permute-start | bytes 688136 | tf_op jit(solution)/shard_map/ppermute | solution.py:382
  84.6 0.1 collective-permute-start.20
  84.6 1.5 %collective-permute-start.21 = (bf16[64,1792]{1,0:T(8,128)(2,1)S(1)}, bf16[64,1792]{1,0:T(8,128)(2,1)S(1)}, u32[]{:S(2)}, u32[]{:S(2)}) collective-permute-start(bf16[64,1792]{1,0:T(8,128)(2,1)S(1)} %get-tuple-element.96), channel_id=1, source_target_pairs={{0,4},{4,0},{8,12},{12,8},{1,5},{5,1},{9,13},{13,9},{2,6},{6,2},{1... | collective-permute-start | bytes 688136 | tf_op jit(solution)/shard_map/ppermute | solution.py:382
  86.2 0.2 collective-permute-start.24
  86.3 5.2 %collective-permute-done.23.refs_8_ = bf16[64,1792]{1,0:T(8,128)(2,1)S(1)} collective-permute-done((bf16[64,1792]{1,0:T(8,128)(2,1)S(1)}, bf16[64,1792]{1,0:T(8,128)(2,1)S(1)}, u32[]{:S(2)}, u32[]{:S(2)}) %collective-permute-start.23) | collective-permute-done | bytes 229408 | tf_op jit(solution)/shard_map/ppermute | solution.py:382
  91.5 9.9 %collective-permute-done.22.refs_7_ = bf16[64,1792]{1,0:T(8,128)(2,1)S(1)} collective-permute-done((bf16[64,1792]{1,0:T(8,128)(2,1)S(1)}, bf16[64,1792]{1,0:T(8,128)(2,1)S(1)}, u32[]{:S(2)}, u32[]{:S(2)}) %collective-permute-start.22) | collective-permute-done | bytes 229408 | tf_op jit(solution)/shard_map/ppermute | solution.py:382
  101.4 0.5 collective-permute-start.25
  102.0 1.0 collective-permute-done.26.refs_11_
  102.9 0.3 collective-permute-done.25.refs_10_
  103.3 1.9 %place.1 = bf16[128,4,1792]{2,1,0:T(4,128)(2,1)} custom-call(bf16[64,1792]{1,0:T(8,128)(2,1)S(1)} %get-tuple-element.83.refs_0_, bf16[64,1792]{1,0:T(8,128)(2,1)S(1)} %collective-permute-done.17.refs_1_, bf16[64,1792]{1,0:T(8,128)(2,1)S(1)} %collective-permute-done.18.refs_2_, bf16[64,1792]{1,0:T(8,128)(2,1)S(1)} %collective-permute-done.19.refs_3_, ...), custom_call_target="tpu_custom_call" | custom-call | flops 1 | bytes 1 | tf_op jit(solution)/shard_map/place/pallas_call | solution.py:650
  (57 shorter events, 0.2 us)
Async XLA Ops:
  0.0 9.7 %collective-permute-start = (bf16[4,1792,128]{2,1,0:T(8,128)(2,1)}, bf16[4,1792,128]{2,1,0:T(8,128)(2,1)S(1)}, u32[]{:S(2)}, u32[]{:S(2)}) collective-permute-start(bf16[4,1792,128]{2,1,0:T(8,128)(2,1)} %refs_4_.5), channel_id=1, source_target_pairs={{0,1},{1,0},{2,3},{3,2},{4,5},{5,4},{6,7},{7,6},{8,9},{9,8},{10,11... | collective-permute-start | bytes 5505032 | tf_op jit(solution)/shard_map/ppermute | solution.py:391
  0.5 9.3 %collective-permute-start.1 = (bf16[256,1792]{1,0:T(8,128)(2,1)}, bf16[256,1792]{1,0:T(8,128)(2,1)S(1)}, u32[]{:S(2)}, u32[]{:S(2)}) collective-permute-start(bf16[256,1792]{1,0:T(8,128)(2,1)} %bitcast.10), channel_id=1, source_target_pairs={{0,1},{1,0},{2,3},{3,2},{4,5},{5,4},{6,7},{7,6},{8,9},{9,8},{10,11... | collective-permute-start | bytes 2752520 | tf_op jit(solution)/shard_map/ppermute | solution.py:391
  0.5 8.6 %collective-permute-start.2 = (bf16[256,256]{1,0:T(8,128)(2,1)}, bf16[256,256]{1,0:T(8,128)(2,1)S(1)}, u32[]{:S(2)}, u32[]{:S(2)}) collective-permute-start(bf16[256,256]{1,0:T(8,128)(2,1)} %bitcast.13), channel_id=1, source_target_pairs={{0,1},{1,0},{2,3},{3,2},{4,5},{5,4},{6,7},{7,6},{8,9},{9,8},{10,11... | collective-permute-start | bytes 393224 | tf_op jit(solution)/shard_map/ppermute | solution.py:391
  4.4 16.4 %collective-permute-start.5 = (bf16[32,1792]{1,0:T(8,128)(2,1)}, bf16[32,1792]{1,0:T(8,128)(2,1)S(1)}, u32[]{:S(2)}, u32[]{:S(2)}) collective-permute-start(bf16[32,1792]{1,0:T(8,128)(2,1)} %get-tuple-element.66), channel_id=1, source_target_pairs={{0,12},{4,8},{8,4},{12,0},{1,13},{5,9},{9,5},{13,1},{2,14},{6,10},... | collective-permute-start | bytes 344072 | tf_op jit(solution)/shard_map/ppermute | solution.py:382
  9.1 15.6 %collective-permute-start.4 = (bf16[32,1792]{1,0:T(8,128)(2,1)}, bf16[32,1792]{1,0:T(8,128)(2,1)S(1)}, u32[]{:S(2)}, u32[]{:S(2)}) collective-permute-start(bf16[32,1792]{1,0:T(8,128)(2,1)} %get-tuple-element.65), channel_id=1, source_target_pairs={{0,8},{4,12},{8,0},{12,4},{1,9},{5,13},{9,1},{13,5},{2,10},{6,14},... | collective-permute-start | bytes 344072 | tf_op jit(solution)/shard_map/ppermute | solution.py:382
  9.1 15.6 %collective-permute-start.3 = (bf16[32,1792]{1,0:T(8,128)(2,1)}, bf16[32,1792]{1,0:T(8,128)(2,1)S(1)}, u32[]{:S(2)}, u32[]{:S(2)}) collective-permute-start(bf16[32,1792]{1,0:T(8,128)(2,1)} %get-tuple-element.64), channel_id=1, source_target_pairs={{0,4},{4,0},{8,12},{12,8},{1,5},{5,1},{9,13},{13,9},{2,6},{6,2},{1... | collective-permute-start | bytes 344072 | tf_op jit(solution)/shard_map/ppermute | solution.py:382
  13.6 7.2 %copy-start.13 = (bf16[32,1792]{1,0:T(8,128)(2,1)S(1)}, bf16[32,1792]{1,0:T(8,128)(2,1)}, u32[]{:S(2)}) copy-start(bf16[32,1792]{1,0:T(8,128)(2,1)} %get-tuple-element.76) | copy-start | bytes 344068
  13.6 11.0 %copy-start.10 = (s32[64]{0:T(128)S(1)}, s32[64]{0:T(128)}, u32[]{:S(2)}) copy-start(s32[64]{0:T(128)} %param.19) | copy-start | bytes 772
  13.6 11.0 %copy-start.12 = (bf16[32,1792]{1,0:T(8,128)(2,1)S(1)}, bf16[32,1792]{1,0:T(8,128)(2,1)}, u32[]{:S(2)}) copy-start(bf16[32,1792]{1,0:T(8,128)(2,1)} %get-tuple-element.75) | copy-start | bytes 344068
  13.7 11.1 %copy-start.11 = (bf16[32,1792]{1,0:T(8,128)(2,1)S(1)}, bf16[32,1792]{1,0:T(8,128)(2,1)}, u32[]{:S(2)}) copy-start(bf16[32,1792]{1,0:T(8,128)(2,1)} %get-tuple-element.74) | copy-start | bytes 344068
  13.7 11.7 %copy-start.2 = (bf16[4,1792,128]{2,1,0:T(8,128)(2,1)S(1)}, bf16[4,1792,128]{2,1,0:T(8,128)(2,1)}, u32[]{:S(2)}) copy-start(bf16[4,1792,128]{2,1,0:T(8,128)(2,1)} %refs_4_.5) | copy-start | bytes 5505028
  13.7 11.7 %copy-start.8 = (bf16[32,1792]{1,0:T(8,128)(2,1)S(1)}, bf16[32,1792]{1,0:T(8,128)(2,1)}, u32[]{:S(2)}) copy-start(bf16[32,1792]{1,0:T(8,128)(2,1)} %get-tuple-element.63.refs_0_) | copy-start | bytes 344068
  20.8 19.9 %collective-permute-start.9 = (bf16[32,1792]{1,0:T(8,128)(2,1)S(1)}, bf16[32,1792]{1,0:T(8,128)(2,1)S(1)}, u32[]{:S(2)}, u32[]{:S(2)}) collective-permute-start(bf16[32,1792]{1,0:T(8,128)(2,1)S(1)} %copy-done.13), channel_id=1, source_target_pairs={{0,12},{4,8},{8,4},{12,0},{1,13},{5,9},{9,5},{13,1},{2,14},{6,10},... | collective-permute-start | bytes 344072 | tf_op jit(solution)/shard_map/ppermute | solution.py:382
  24.7 17.0 %collective-permute-start.8 = (bf16[32,1792]{1,0:T(8,128)(2,1)S(1)}, bf16[32,1792]{1,0:T(8,128)(2,1)S(1)}, u32[]{:S(2)}, u32[]{:S(2)}) collective-permute-start(bf16[32,1792]{1,0:T(8,128)(2,1)S(1)} %copy-done.12), channel_id=1, source_target_pairs={{0,8},{4,12},{8,0},{12,4},{1,9},{5,13},{9,1},{13,5},{2,10},{6,14},... | collective-permute-start | bytes 344072 | tf_op jit(solution)/shard_map/ppermute | solution.py:382
  24.8 16.9 %collective-permute-start.7 = (bf16[32,1792]{1,0:T(8,128)(2,1)S(1)}, bf16[32,1792]{1,0:T(8,128)(2,1)S(1)}, u32[]{:S(2)}, u32[]{:S(2)}) collective-permute-start(bf16[32,1792]{1,0:T(8,128)(2,1)S(1)} %copy-done.11), channel_id=1, source_target_pairs={{0,4},{4,0},{8,12},{12,8},{1,5},{5,1},{9,13},{13,9},{2,6},{6,2},{1... | collective-permute-start | bytes 344072 | tf_op jit(solution)/shard_map/ppermute | solution.py:382
  26.5 10.1 %collective-permute-start.6 = (f32[128,128]{1,0:T(8,128)S(1)}, f32[128,128]{1,0:T(8,128)S(1)}, u32[]{:S(2)}, u32[]{:S(2)}) collective-permute-start(f32[128,128]{1,0:T(8,128)S(1)} %down.2.refs_0_), channel_id=1, source_target_pairs={{0,2},{2,0},{1,3},{3,1},{4,6},{6,4},{5,7},{7,5},{8,10},{10,8},{9,1... | collective-permute-start | bytes 196616 | tf_op jit(solution)/shard_map/ppermute | solution.py:391
  28.2 8.3 %copy-start.5 = (bf16[4,64,1792]{2,1,0:T(8,128)(2,1)S(1)}, bf16[4,64,1792]{2,1,0:T(8,128)(2,1)}, u32[]{:S(2)}) copy-start(bf16[4,64,1792]{2,1,0:T(8,128)(2,1)} %param.23) | copy-start | bytes 2752516
  28.2 8.4 %copy-start.6 = (bf16[4,64,256]{2,1,0:T(8,128)(2,1)S(1)}, bf16[4,64,256]{2,1,0:T(8,128)(2,1)}, u32[]{:S(2)}) copy-start(bf16[4,64,256]{2,1,0:T(8,128)(2,1)} %param.24) | copy-start | bytes 393220
  36.6 5.1 %copy-start.7 = (bf16[32,1792]{1,0:T(8,128)(2,1)S(1)}, bf16[32,1792]{1,0:T(8,128)(2,1)}, u32[]{:S(2)}) copy-start(bf16[32,1792]{1,0:T(8,128)(2,1)} %get-tuple-element.73.refs_0_) | copy-start | bytes 344068
  37.1 10.6 %collective-permute-start.13 = (bf16[32,2048]{1,0:T(8,128)(2,1)S(1)}, bf16[32,2048]{1,0:T(8,128)(2,1)S(1)}, u32[]{:S(2)}, u32[]{:S(2)}) collective-permute-start(bf16[32,2048]{1,0:T(8,128)(2,1)S(1)} %get-tuple-element.72), channel_id=1, source_target_pairs={{0,12},{4,8},{8,4},{12,0},{1,13},{5,9},{9,5},{13,1},{2,14},{6,10},... | collective-permute-start | bytes 393224 | tf_op jit(solution)/shard_map/ppermute | solution.py:382
  40.7 15.1 %collective-permute-start.12 = (bf16[32,2048]{1,0:T(8,128)(2,1)S(1)}, bf16[32,2048]{1,0:T(8,128)(2,1)S(1)}, u32[]{:S(2)}, u32[]{:S(2)}) collective-permute-start(bf16[32,2048]{1,0:T(8,128)(2,1)S(1)} %get-tuple-element.71), channel_id=1, source_target_pairs={{0,8},{4,12},{8,0},{12,4},{1,9},{5,13},{9,1},{13,5},{2,10},{6,14},... | collective-permute-start | bytes 393224 | tf_op jit(solution)/shard_map/ppermute | solution.py:382
  40.7 15.1 %collective-permute-start.11 = (bf16[32,2048]{1,0:T(8,128)(2,1)S(1)}, bf16[32,2048]{1,0:T(8,128)(2,1)S(1)}, u32[]{:S(2)}, u32[]{:S(2)}) collective-permute-start(bf16[32,2048]{1,0:T(8,128)(2,1)S(1)} %get-tuple-element.70), channel_id=1, source_target_pairs={{0,4},{4,0},{8,12},{12,8},{1,5},{5,1},{9,13},{13,9},{2,6},{6,2},{1... | collective-permute-start | bytes 393224 | tf_op jit(solution)/shard_map/ppermute | solution.py:382
  41.6 15.7 %copy-start.3 = (bf16[64,32,256]{2,1,0:T(8,128)(2,1)S(1)}, bf16[64,32,256]{2,1,0:T(8,128)(2,1)}, u32[]{:S(2)}) copy-start(bf16[64,32,256]{2,1,0:T(8,128)(2,1)} %refs_4_.7) | copy-start | bytes 3145732
  41.6 15.7 %copy-start.4 = (bf16[64,32,256]{2,1,0:T(8,128)(2,1)S(1)}, bf16[64,32,256]{2,1,0:T(8,128)(2,1)}, u32[]{:S(2)}) copy-start(bf16[64,32,256]{2,1,0:T(8,128)(2,1)} %refs_5_.3) | copy-start | bytes 3145732
  42.8 14.6 %copy-start = (f32[256,1280]{1,0:T(8,128)S(1)}, f32[256,1280]{1,0:T(8,128)}, u32[]{:S(2)}) copy-start(f32[256,1280]{1,0:T(8,128)} %project.3.refs_7_) | copy-start | bytes 3932164
  42.8 14.6 %copy-start.1 = (f32[256,1024]{1,0:T(8,128)S(1)}, f32[256,1024]{1,0:T(8,128)}, u32[]{:S(2)}) copy-start(f32[256,1024]{1,0:T(8,128)} %project.2.refs_6_) | copy-start | bytes 3145732
  42.8 14.6 %copy-start.9 = (s32[8,64]{1,0:T(8,128)S(1)}, s32[8,64]{1,0:T(8,128)}, u32[]{:S(2)}) copy-start(s32[8,64]{1,0:T(8,128)} %get-tuple-element.82.refs_0_) | copy-start | bytes 6148
  42.8 4.3 %collective-permute-start.10 = (f32[128,128]{1,0:T(8,128)S(1)}, f32[128,128]{1,0:T(8,128)S(1)}, u32[]{:S(2)}, u32[]{:S(2)}) collective-permute-start(f32[128,128]{1,0:T(8,128)S(1)} %down.3.refs_0_), channel_id=1, source_target_pairs={{0,2},{2,0},{1,3},{3,1},{4,6},{6,4},{5,7},{7,5},{8,10},{10,8},{9,1... | collective-permute-start | bytes 196616 | tf_op jit(solution)/shard_map/ppermute | solution.py:391
  47.6 13.5 %collective-permute-start.16 = (bf16[32,2048]{1,0:T(8,128)(2,1)S(1)}, bf16[32,2048]{1,0:T(8,128)(2,1)S(1)}, u32[]{:S(2)}, u32[]{:S(2)}) collective-permute-start(bf16[32,2048]{1,0:T(8,128)(2,1)S(1)} %get-tuple-element.87), channel_id=1, source_target_pairs={{0,12},{4,8},{8,4},{12,0},{1,13},{5,9},{9,5},{13,1},{2,14},{6,10},... | collective-permute-start | bytes 393224 | tf_op jit(solution)/shard_map/ppermute | solution.py:382
  55.8 6.6 %collective-permute-start.15 = (bf16[32,2048]{1,0:T(8,128)(2,1)S(1)}, bf16[32,2048]{1,0:T(8,128)(2,1)S(1)}, u32[]{:S(2)}, u32[]{:S(2)}) collective-permute-start(bf16[32,2048]{1,0:T(8,128)(2,1)S(1)} %get-tuple-element.86), channel_id=1, source_target_pairs={{0,8},{4,12},{8,0},{12,4},{1,9},{5,13},{9,1},{13,5},{2,10},{6,14},... | collective-permute-start | bytes 393224 | tf_op jit(solution)/shard_map/ppermute | solution.py:382
  55.8 6.8 %collective-permute-start.14 = (bf16[32,2048]{1,0:T(8,128)(2,1)S(1)}, bf16[32,2048]{1,0:T(8,128)(2,1)S(1)}, u32[]{:S(2)}, u32[]{:S(2)}) collective-permute-start(bf16[32,2048]{1,0:T(8,128)(2,1)S(1)} %get-tuple-element.85), channel_id=1, source_target_pairs={{0,4},{4,0},{8,12},{12,8},{1,5},{5,1},{9,13},{13,9},{2,6},{6,2},{1... | collective-permute-start | bytes 393224 | tf_op jit(solution)/shard_map/ppermute | solution.py:382
  62.6 10.3 %collective-permute-start.19 = (bf16[64,1792]{1,0:T(8,128)(2,1)S(1)}, bf16[64,1792]{1,0:T(8,128)(2,1)S(1)}, u32[]{:S(2)}, u32[]{:S(2)}) collective-permute-start(bf16[64,1792]{1,0:T(8,128)(2,1)S(1)} %get-tuple-element.92), channel_id=1, source_target_pairs={{0,12},{4,8},{8,4},{12,0},{1,13},{5,9},{9,5},{13,1},{2,14},{6,10},... | collective-permute-start | bytes 688136 | tf_op jit(solution)/shard_map/ppermute | solution.py:382
  64.6 17.0 %collective-permute-start.18 = (bf16[64,1792]{1,0:T(8,128)(2,1)S(1)}, bf16[64,1792]{1,0:T(8,128)(2,1)S(1)}, u32[]{:S(2)}, u32[]{:S(2)}) collective-permute-start(bf16[64,1792]{1,0:T(8,128)(2,1)S(1)} %get-tuple-element.90), channel_id=1, source_target_pairs={{0,8},{4,12},{8,0},{12,4},{1,9},{5,13},{9,1},{13,5},{2,10},{6,14},... | collective-permute-start | bytes 688136 | tf_op jit(solution)/shard_map/ppermute | solution.py:382
  64.6 17.0 %collective-permute-start.17 = (bf16[64,1792]{1,0:T(8,128)(2,1)S(1)}, bf16[64,1792]{1,0:T(8,128)(2,1)S(1)}, u32[]{:S(2)}, u32[]{:S(2)}) collective-permute-start(bf16[64,1792]{1,0:T(8,128)(2,1)S(1)} %get-tuple-element.88), channel_id=1, source_target_pairs={{0,4},{4,0},{8,12},{12,8},{1,5},{5,1},{9,13},{13,9},{2,6},{6,2},{1... | collective-permute-start | bytes 688136 | tf_op jit(solution)/shard_map/ppermute | solution.py:382
  81.6 9.9 %collective-permute-start.23 = (bf16[64,1792]{1,0:T(8,128)(2,1)S(1)}, bf16[64,1792]{1,0:T(8,128)(2,1)S(1)}, u32[]{:S(2)}, u32[]{:S(2)}) collective-permute-start(bf16[64,1792]{1,0:T(8,128)(2,1)S(1)} %get-tuple-element.100), channel_id=1, source_target_pairs={{0,12},{4,8},{8,4},{12,0},{1,13},{5,9},{9,5},{13,1},{2,14},{6,10},... | collective-permute-start | bytes 688136 | tf_op jit(solution)/shard_map/ppermute | solution.py:382
  84.5 17.0 %collective-permute-start.22 = (bf16[64,1792]{1,0:T(8,128)(2,1)S(1)}, bf16[64,1792]{1,0:T(8,128)(2,1)S(1)}, u32[]{:S(2)}, u32[]{:S(2)}) collective-permute-start(bf16[64,1792]{1,0:T(8,128)(2,1)S(1)} %get-tuple-element.98), channel_id=1, source_target_pairs={{0,8},{4,12},{8,0},{12,4},{1,9},{5,13},{9,1},{13,5},{2,10},{6,14},... | collective-permute-start | bytes 688136 | tf_op jit(solution)/shard_map/ppermute | solution.py:382
  84.6 17.4 %collective-permute-start.20 = (bf16[128,1792]{1,0:T(8,128)(2,1)S(1)}, bf16[128,1792]{1,0:T(8,128)(2,1)S(1)}, u32[]{:S(2)}, u32[]{:S(2)}) collective-permute-start(bf16[128,1792]{1,0:T(8,128)(2,1)S(1)} %pad_maximum_fusion), channel_id=1, source_target_pairs={{0,1},{1,0},{2,3},{3,2},{4,5},{5,4},{6,7},{7,6},{8,9},{9,8},{10,11... | collective-permute-start | bytes 1376264 | tf_op jit(solution)/shard_map/ppermute | solution.py:643
  84.6 16.8 %collective-permute-start.21 = (bf16[64,1792]{1,0:T(8,128)(2,1)S(1)}, bf16[64,1792]{1,0:T(8,128)(2,1)S(1)}, u32[]{:S(2)}, u32[]{:S(2)}) collective-permute-start(bf16[64,1792]{1,0:T(8,128)(2,1)S(1)} %get-tuple-element.96), channel_id=1, source_target_pairs={{0,4},{4,0},{8,12},{12,8},{1,5},{5,1},{9,13},{13,9},{2,6},{6,2},{1... | collective-permute-start | bytes 688136 | tf_op jit(solution)/shard_map/ppermute | solution.py:382
  86.2 15.8 %collective-permute-start.24 = (bf16[64,1792]{1,0:T(8,128)(2,1)S(1)}, bf16[64,1792]{1,0:T(8,128)(2,1)S(1)}, u32[]{:S(2)}, u32[]{:S(2)}) collective-permute-start(bf16[64,1792]{1,0:T(8,128)(2,1)S(1)} %get-tuple-element.94.refs_5_), channel_id=1, source_target_pairs={{0,1},{1,0},{2,3},{3,2},{4,5},{5,4},{6,7},{7,6},{8,9},{9,8},{10,11... | collective-permute-start | bytes 688136 | tf_op jit(solution)/shard_map/ppermute | solution.py:647
  91.5 10.5 %collective-permute-start.27 = (bf16[64,1792]{1,0:T(8,128)(2,1)S(1)}, bf16[64,1792]{1,0:T(8,128)(2,1)S(1)}, u32[]{:S(2)}, u32[]{:S(2)}) collective-permute-start(bf16[64,1792]{1,0:T(8,128)(2,1)S(1)} %collective-permute-done.23.refs_8_), channel_id=1, source_target_pairs={{0,1},{1,0},{2,3},{3,2},{4,5},{5,4},{6,7},{7,6},{8,9},{9,8},{10,11... | collective-permute-start | bytes 688136 | tf_op jit(solution)/shard_map/ppermute | solution.py:647
  101.4 1.5 %collective-permute-start.26 = (bf16[64,1792]{1,0:T(8,128)(2,1)S(1)}, bf16[64,1792]{1,0:T(8,128)(2,1)S(1)}, u32[]{:S(2)}, u32[]{:S(2)}) collective-permute-start(bf16[64,1792]{1,0:T(8,128)(2,1)S(1)} %collective-permute-done.22.refs_7_), channel_id=1, source_target_pairs={{0,1},{1,0},{2,3},{3,2},{4,5},{5,4},{6,7},{7,6},{8,9},{9,8},{10,11... | collective-permute-start | bytes 688136 | tf_op jit(solution)/shard_map/ppermute | solution.py:647
  101.4 1.8 %collective-permute-start.25 = (bf16[64,1792]{1,0:T(8,128)(2,1)S(1)}, bf16[64,1792]{1,0:T(8,128)(2,1)S(1)}, u32[]{:S(2)}, u32[]{:S(2)}) collective-permute-start(bf16[64,1792]{1,0:T(8,128)(2,1)S(1)} %collective-permute-done.21.refs_6_), channel_id=1, source_target_pairs={{0,1},{1,0},{2,3},{3,2},{4,5},{5,4},{6,7},{7,6},{8,9},{9,8},{10,11... | collective-permute-start | bytes 688136 | tf_op jit(solution)/shard_map/ppermute | solution.py:647

commit v7 on v6

--- a/solution.py
+++ b/solution.py
@@ -20,8 +20,7 @@
 VMEM = pl.BlockSpec(memory_space=pltpu.VMEM)
 MIB = 1 << 20
 PACK_LIMIT = 56
-PROJECT_LIMIT = 56
-DEPTH_CUTS = 4
+PROJECT_LIMIT = 49
 
 
 def iota(shape, dim):
@@ -50,7 +49,9 @@
     return ranked(slots ^ lane_base, MOST)
 
 
-def norm_in_pieces(pieces, begin, x_hbm, gain_hbm, x_buf, gain_buf, semaphores, normed_ref):
+def norm_in_pieces(
+    pieces, begin, x_hbm, gain_hbm, x_buf, gain_buf, semaphores, normed_ref, started=None
+):
     count, width = x_buf.shape
     size = count // pieces
     gain_copy = pltpu.make_async_copy(gain_hbm, gain_buf, semaphores.at[pieces])
@@ -66,6 +67,8 @@
         copies[-1].start()
         if piece == 0:
             gain_copy.start()
+    if started is not None:
+        started()
     gain_copy.wait()
     gain = jnp.concatenate([gain_buf[i : i + 1, :] for i in range(gain_buf.shape[0])], axis=1)
     for piece in range(pieces):
@@ -99,46 +102,91 @@
         message_ref[...] = packed[number * per_message : (number + 1) * per_message]
 
 
-def norm_pack_kernel(steps, rows, flow_most, lanes, pieces, chunk, *refs):
-    if chunk:
-        places_ref, gain_hbm, x_hbm, _, normed_ref = refs[:5]
-        message_refs = refs[5 : 5 + lanes]
-        x_buf, gain_buf, semaphores = refs[5 + lanes :]
-    else:
-        table_hbms, gain_hbm, x_hbm = refs[:3], refs[3], refs[4]
-        normed_ref, places_ref, message_refs = refs[5], refs[6], refs[7 : 7 + lanes]
-        x_buf, gain_buf, *table_bufs, semaphores = refs[7 + lanes :]
-        copies = [
-            pltpu.make_async_copy(source, target, semaphores.at[pieces + 1 + number])
-            for number, (source, target) in enumerate(zip(table_hbms, table_bufs))
-        ]
+def table_copies(table_hbms, table_bufs, semaphores, first):
+    copies = [
+        pltpu.make_async_copy(source, target, semaphores.at[first + number])
+        for number, (source, target) in enumerate(zip(table_hbms, table_bufs))
+    ]
+    for copy in copies:
+        copy.start()
+    return copies
+
+
+def places_from(table_bufs, spots, flow_most):
+    speaker, table, owner = [buffer[...] for buffer in table_bufs]
+    here, core, subs = lax.axis_index("streams"), lax.axis_index("sub"), lax.axis_size("sub")
+    places = slot_places(speaker, table, here * (spots // MOST))
+    return places, ranked(owner ^ (here * subs + core), flow_most)
+
+
+def norm_pack_kernel(steps, rows, flow_most, lanes, pieces, *refs):
+    table_hbms, gain_hbm, x_hbm, message_refs = refs[:3], refs[3], refs[4], refs[5 : 5 + lanes]
+    x_buf, gain_buf, *table_bufs, semaphores, normed_ref = refs[5 + lanes :]
+    copies = table_copies(table_hbms, table_bufs, semaphores, pieces + 1)
+    norm_in_pieces(pieces, 0, x_hbm, gain_hbm, x_buf, gain_buf, semaphores, normed_ref)
+    for copy in copies:
+        copy.wait()
+    spots = message_refs[0].shape[0] // steps
+    places, _ = places_from(table_bufs, spots, flow_most)
+    pack_messages(steps, rows, places, normed_ref, message_refs)
+
+
+def weight_copies(begin, weight_hbm, weight_buf, semaphores):
+    columns = weight_buf.shape[2]
+    return [
+        pltpu.make_async_copy(
+            weight_hbm.at[:, pl.ds((begin + block) * columns, columns)],
+            weight_buf.at[block],
+            semaphores.at[block],
+        )
+        for block in range(weight_buf.shape[0])
+    ]
+
+
+def project_blocks(begin, copies, rows_ref, weight_buf, bias_ref, out_ref):
+    columns = weight_buf.shape[2]
+    tiles = columns // 128
+    for block, copy in enumerate(copies):
+        first = (begin + block) * tiles
+        bias = [bias_ref[tile : tile + 1, :] for tile in range(first, first + tiles)]
+        copy.wait()
+        product = jnp.dot(rows_ref[...], weight_buf[block], preferred_element_type=jnp.float32)
+        out_ref[:, block * columns : (block + 1) * columns] = product + jnp.concatenate(
+            bias, axis=1
+        )
+
+
+def norm_pack_project_kernel(steps, rows, flow_most, lanes, pieces, chunk, *refs):
+    table_hbms, bias_ref, gain_hbm, x_hbm, weight_hbm = refs[:3], *refs[3:7]
+    normed_ref, out_ref, places_ref, message_refs = *refs[7:10], refs[10 : 10 + lanes]
+    x_buf, gain_buf, *table_bufs, semaphores, weight_buf, weight_semaphores = refs[10 + lanes :]
+    copies = weight_copies(0, weight_hbm, weight_buf, weight_semaphores)
+    tables = table_copies(table_hbms, table_bufs, semaphores, pieces + 1)
+
+    def start_weights():
         for copy in copies:
             copy.start()
-    begin = chunk * steps * rows
-    norm_in_pieces(pieces, begin, x_hbm, gain_hbm, x_buf, gain_buf, semaphores, normed_ref)
-    if not chunk:
-        for copy in copies:
-            copy.wait()
-        speaker, table, owner = [buffer[...] for buffer in table_bufs]
-        core, subs = lax.axis_index("sub"), lax.axis_size("sub")
-        spots = message_refs[0].shape[0] // steps
-        places = slot_places(speaker, table, lax.axis_index("streams") * (spots // MOST))
-        places_ref[0:1, :] = places
-        places_ref[1:2, :] = ranked(owner ^ (lax.axis_index("streams") * subs + core), flow_most)
-    pack_messages(steps, rows, places_ref[0:1, :], normed_ref, message_refs)
-
-
-def project_kernel(first_tile, rows_ref, bias_ref, *refs):
-    weight_refs, out_ref = refs[:-1], refs[-1]
-    depth, columns = weight_refs[0].shape
-    tiles = columns // 128
-    tile = first_tile + pl.program_id(0) * tiles
-    bias = [bias_ref[pl.ds(tile + number, 1), :] for number in range(tiles)]
-    total = jnp.concatenate(bias, axis=1)
-    for number, ref in enumerate(weight_refs):
-        rows = rows_ref[:, number * depth : (number + 1) * depth]
-        total = total + jnp.dot(rows, ref[...], preferred_element_type=jnp.float32)
-    out_ref[...] = total
+
+    norm_in_pieces(
+        pieces, 0, x_hbm, gain_hbm, x_buf, gain_buf, semaphores, normed_ref, start_weights
+    )
+    for copy in tables:
+        copy.wait()
+    spots = message_refs[0].shape[0] // steps
+    places, flow_places = places_from(table_bufs, spots, flow_most)
+    places_ref[0:1, :] = places
+    places_ref[1:2, :] = flow_places
+    count = steps * rows
+    own_ref = normed_ref.at[pl.ds(chunk * count, count)]
+    pack_messages(steps, rows, places, own_ref, message_refs)
+    project_blocks(0, copies, normed_ref, weight_buf, bias_ref, out_ref)
+
+
+def project_kernel(begin, rows_ref, bias_ref, weight_hbm, out_ref, weight_buf, semaphores):
+    copies = weight_copies(begin, weight_hbm, weight_buf, semaphores)
+    for copy in copies:
+        copy.start()
+    project_blocks(begin, copies, rows_ref, weight_buf, bias_ref, out_ref)
 
 
 def row_slots(shape, spots):
@@ -450,71 +498,79 @@
     flat = inputs.reshape(steps * rows, width)
     gain = input_norm_gain.reshape(width // 128, 128)
     message = jax.ShapeDtypeStruct((per_message, sliced), bf16)
-    normed_shape = jax.ShapeDtypeStruct((steps * rows, width), bf16)
     places_shape = jax.ShapeDtypeStruct((8, rows), jnp.int32)
     tables = [
         speaker.reshape(1, rows),
         speaker_adapter_slot.reshape(1, -1),
         flow_decoder_owner.reshape(1, rows),
     ]
-    buffers = [pltpu.VMEM((chunk_rows, width), bf16), pltpu.VMEM(gain.shape, f32)]
-    table_buffers = [pltpu.VMEM(table.shape, jnp.int32) for table in tables]
-    arrived = []
-    for chunk in range(chunks):
-        rows_block = pl.BlockSpec((chunk_rows, width), lambda i, chunk=chunk: (chunk, 0))
-        first = chunk == 0
-        operands = [gain, flat]
-        if first:
-            operands = tables + operands
-        else:
-            adapters = down_maps[1:], query_maps[1:], value_maps[1:]
-            operands = [held(places, adapters)] + operands + [normed]
-        normed, *messages = pl.pallas_call(
-            functools.partial(
-                norm_pack_kernel, chunk_steps, rows, flow_most, lanes, pieces, chunk
-            ),
-            grid=(1,),
-            in_specs=[in_hbm] * 5 if first else [whole(places_shape.shape)] + [in_hbm] * 3,
-            out_specs=[rows_block]
-            + [whole(places_shape.shape)] * first
-            + [whole(message.shape)] * lanes,
-            out_shape=[normed_shape] + [places_shape] * first + [message] * lanes,
-            scratch_shapes=buffers
-            + table_buffers * first
-            + [pltpu.SemaphoreType.DMA((pieces + 4,))],
-            input_output_aliases={} if first else {3: 0},
-            compiler_params=pltpu.CompilerParams(vmem_limit_bytes=PACK_LIMIT * MIB),
-            cost_estimate=SMALL,
-            name="norm_and_pack",
-        )(*operands)
-        if first:
-            places, *messages = messages
-        if first:
-            arrived.append(traded(messages, "streams"))
+
+    def row_buffers(count):
+        return (
+            [pltpu.VMEM((count, width), bf16), pltpu.VMEM(gain.shape, f32)]
+            + [pltpu.VMEM(table.shape, jnp.int32) for table in tables]
+            + [pltpu.SemaphoreType.DMA((pieces + 4,))]
+        )
+
+    messages = pl.pallas_call(
+        functools.partial(norm_pack_kernel, chunk_steps, rows, flow_most, lanes, pieces),
+        in_specs=[in_hbm] * 5,
+        out_specs=[VMEM] * lanes,
+        out_shape=[message] * lanes,
+        scratch_shapes=row_buffers(chunk_rows) + [pltpu.VMEM((chunk_rows, width), bf16)],
+        compiler_params=pltpu.CompilerParams(vmem_limit_bytes=PACK_LIMIT * MIB),
+        cost_estimate=SMALL,
+        name="norm_and_pack",
+    )(*tables, gain, flat)
+    arrived = [traded(messages, "streams")]
 
     bias = projection_bias.reshape(-1, 128)
     columns = projection_weight.shape[1]
     block_columns = 256 if columns % 256 == 0 else 384
     blocks = columns // block_columns
-
-    def project(begin, end, after):
+    cut = blocks // 2
+
+    def weight_buffers(count):
+        return [
+            pltpu.VMEM((count, width, block_columns), bf16),
+            pltpu.SemaphoreType.DMA((count,)),
+        ]
+
+    def projected(count):
+        return jax.ShapeDtypeStruct((steps * rows, count * block_columns), f32)
+
+    adapters = down_maps[1:], query_maps[1:], value_maps[1:]
+    weight_buf, weight_semaphores = weight_buffers(cut)
+    normed, first_qkv, places, *messages = pl.pallas_call(
+        functools.partial(
+            norm_pack_project_kernel, chunk_steps, rows, flow_most, lanes, 2 * pieces, 1
+        ),
+        in_specs=[in_hbm] * 3 + [VMEM] + [in_hbm] * 3,
+        out_specs=[VMEM] * (3 + lanes),
+        out_shape=[jax.ShapeDtypeStruct((steps * rows, width), bf16), projected(cut)]
+        + [places_shape]
+        + [message] * lanes,
+        scratch_shapes=row_buffers(steps * rows)[:-1]
+        + [pltpu.SemaphoreType.DMA((2 * pieces + 4,))]
+        + [weight_buf, weight_semaphores],
+        compiler_params=pltpu.CompilerParams(vmem_limit_bytes=PROJECT_LIMIT * MIB),
+        cost_estimate=SMALL,
+        name="norm_pack_project",
+    )(*tables, held(bias, (adapters, messages)), gain, flat, projection_weight)
+    arrived.append(traded(messages, "streams"))
+    qkv = [first_qkv]
+
+    def project(after):
         return pl.pallas_call(
-            functools.partial(project_kernel, begin * block_columns // 128),
-            grid=(end - begin,),
-            in_specs=[whole(normed_shape.shape), whole(bias.shape)]
-            + [
-                pl.BlockSpec(
-                    (width // DEPTH_CUTS, block_columns),
-                    lambda i, number=number: (number, begin + i),
-                )
-                for number in range(DEPTH_CUTS)
-            ],
-            out_specs=pl.BlockSpec((steps * rows, block_columns), lambda i: (0, i)),
-            out_shape=jax.ShapeDtypeStruct((steps * rows, (end - begin) * block_columns), f32),
+            functools.partial(project_kernel, cut),
+            in_specs=[VMEM, VMEM, in_hbm],
+            out_specs=VMEM,
+            out_shape=projected(blocks - cut),
+            scratch_shapes=weight_buffers(blocks - cut),
             compiler_params=pltpu.CompilerParams(vmem_limit_bytes=PROJECT_LIMIT * MIB),
             cost_estimate=SMALL,
             name="project",
-        )(normed, held(bias, after), *[projection_weight] * DEPTH_CUTS)
+        )(normed, held(bias, after), projection_weight)
 
     def down(chunk, after):
         partial_latent = pl.pallas_call(
@@ -541,15 +597,6 @@
         )(held(partials[0], after), *partials[1:], *query_maps, *value_maps)
         return messages
 
-    cut = blocks // 2
-    qkv = [project(0, cut, messages)]
-    messages = [messages[0]] + [
-        held(message, (before, qkv)) for message, before in zip(messages[1:], arrived[0][1:])
-    ]
-    arrived.append(traded(messages, "streams"))
-    partials = down(0, qkv)
-    qkv.append(project(cut, blocks, partials[0]))
-
     half_width = HEAD_WIDTH // 2
     position = jnp.concatenate([cache_fill_length + step for step in range(steps)]).astype(f32)
     freq = jnp.exp(jnp.arange(half_width, dtype=f32) * (-math.log(1000000.0) / half_width))
@@ -562,9 +609,10 @@
     returned = []
     after = qkv
     for chunk in range(chunks):
+        partials = down(chunk, after)
         if chunk:
-            partials = down(chunk, after)
-        after = up(partials, after)
+            qkv.append(project(partials[0]))
+        after = up(partials, qkv)
         messages = list(after)
         if chunk:
             for lane in range(1, lanes):

time: 105 us -> 105 us (level)
  Pallas kernels: 35.3 us -> 31.4 us
  waiting for transfers between devices: 37.1 us -> 39.2 us
  starting transfers between devices: 31.6 us -> 32.8 us
    ppermute x18, waiting for transfers between devices: 32 us -> 37.9 us  [traded(): landed[shift] = lax.ppermute(blocks[shift], axes, pairs)]
    pallas_call x2 -> x1, Pallas kernels: 7.32 us -> 3.45 us  [on_device(): pl.pallas_call(functools.partial(norm_pack_kernel, chunk_steps, rows, flo...]
    ppermute x5, waiting for transfers between devices: 3.83 us -> 0.01 us  [from_others(): landed.append(lax.ppermute(block, axis, pairs))]
    ppermute x18, starting transfers between devices: 27.7 us -> 28.9 us  [traded(): landed[shift] = lax.ppermute(blocks[shift], axes, pairs)]
  transfers between devices with their start and end apart: 28 -> 28, of which waited for: 10 -> 8; matrix products, arithmetic and copies ran while one was open for 1% -> 1% of each run, Pallas kernels for 32% -> 28%
where the time goes in v7:
time: 105 us
  waiting for transfers between devices  39.2 us (37%)
  starting transfers between devices  32.8 us (31%)
  Pallas kernels  31.4 us (30%)
    ppermute x18, waiting for transfers between devices, traded(): landed[shift] = lax.ppermute(blocks[shift], axes, pairs)  37.9 us
    ppermute x18, starting transfers between devices, traded(): landed[shift] = lax.ppermute(blocks[shift], axes, pairs)  28.9 us
    pallas_call x1, Pallas kernels, on_device(): pl.pallas_call(functools.partial(norm_pack_project_kernel, chunk_steps, r...  8.69 us
    pallas_call x2, Pallas kernels, on_device(): pl.pallas_call(functools.partial(attend_kernel, chunk * chunk_steps, chun...  7.53 us
    pallas_call x1, Pallas kernels, project(): pl.pallas_call(functools.partial(project_kernel, cut), in_specs=[VMEM, VM...  6.56 us
    pallas_call x1, Pallas kernels, on_device(): pl.pallas_call(functools.partial(norm_pack_kernel, chunk_steps, rows, flo...  3.45 us
    ppermute x5, starting transfers between devices, from_others(): landed.append(lax.ppermute(block, axis, pairs))  3.2 us
    pallas_call x2, Pallas kernels, down(): pl.pallas_call(functools.partial(down_kernel, lanes, spots), in_specs=[VM...  2.3 us
  transfers between devices with their start and end apart: 28, of which 8 were waited for; matrix products, arithmetic and copies ran while one was open for 1% of the time, Pallas kernels for 28%

profile of v7, /device:TPU:0, one launch (start us, length us, event | category | flops | bytes accessed | tf_op | source)
XLA Modules:
  0.0 104.6 jit_solution(6483507176768660870)
XLA Ops:
  0.0 0.5 collective-permute-start
  0.5 0.1 collective-permute-start.1
  0.6 0.4 collective-permute-start.2
  1.1 3.5 %norm_and_pack.1 = (bf16[32,1792]{1,0:T(8,128)(2,1)}, bf16[32,1792]{1,0:T(8,128)(2,1)}, bf16[32,1792]{1,0:T(8,128)(2,1)}, bf16[32,1792]{1,0:T(8,128)(2,1)}) custom-call(s32[1,64]{1,0:T(1,128)} %bitcast.22, s32[1,32]{1,0:T(1,128)} %bitcast.24, s32[1,64]{1,0:T(1,128)} %bitcast.26, f32[28,128]{1,0:T(8,128)} %bitcast.16, bf16[256,3584]{1,0:T(8,128)(2,1)} %bitcast.28), custom_call_target="tpu_custom_call" | custom-call | flops 1 | bytes 1 | tf_op jit(solution)/shard_map/norm_and_pack/pallas_call | solution.py:515
  4.5 2.7 %collective-permute-start.3 = (bf16[32,1792]{1,0:T(8,128)(2,1)}, bf16[32,1792]{1,0:T(8,128)(2,1)S(1)}, u32[]{:S(2)}, u32[]{:S(2)}) collective-permute-start(bf16[32,1792]{1,0:T(8,128)(2,1)} %get-tuple-element.50), channel_id=1, source_target_pairs={{0,4},{4,0},{8,12},{12,8},{1,5},{5,1},{9,13},{13,9},{2,6},{6,2},{1... | collective-permute-start | bytes 344072 | tf_op jit(solution)/shard_map/ppermute | solution.py:430
  7.2 2.6 %collective-permute-start.4 = (bf16[32,1792]{1,0:T(8,128)(2,1)}, bf16[32,1792]{1,0:T(8,128)(2,1)S(1)}, u32[]{:S(2)}, u32[]{:S(2)}) collective-permute-start(bf16[32,1792]{1,0:T(8,128)(2,1)} %get-tuple-element.51), channel_id=1, source_target_pairs={{0,8},{4,12},{8,0},{12,4},{1,9},{5,13},{9,1},{13,5},{2,10},{6,14},... | collective-permute-start | bytes 344072 | tf_op jit(solution)/shard_map/ppermute | solution.py:430
  9.8 0.8 collective-permute-start.5
  10.7 0.0 copy-start.8
  10.7 0.0 copy-start
  10.7 0.0 copy-start.5
  10.7 8.7 %norm_pack_project.1 = (bf16[256,3584]{1,0:T(8,128)(2,1)S(1)}, f32[256,1024]{1,0:T(8,128)S(1)}, s32[8,64]{1,0:T(8,128)S(1)}, bf16[32,1792]{1,0:T(8,128)(2,1)S(1)...) custom-call(s32[1,64]{1,0:T(1,128)S(1)} %bitcast.23, ...), custom_call_target="tpu_custom_call" | custom-call | flops 1 | bytes 1 | tf_op jit(solution)/shard_map/norm_pack_project/pallas_call | solution.py:544
  19.4 0.2 collective-permute-start.7
  19.6 1.2 %down.2.refs_0_ = f32[128,128]{1,0:T(8,128)S(1)} custom-call(bf16[32,1792]{1,0:T(8,128)(2,1)S(1)} %copy-done.5, bf16[32,1792]{1,0:T(8,128)(2,1)S(1)} %collective-permute-done.3.refs_1_, bf16[32,1792]{1,0:T(8,128)(2,1)S(1)} %collective-permute-done.4.refs_2_, bf16[32,1792]{1,0:T(8,128)(2,1)S(1)} %collective-permute-done.5.refs_3_, ...), custom_call_target="tpu_custom_call" | custom-call | flops 1 | bytes 1 | tf_op jit(solution)/shard_map/down/pallas_call | solution.py:576
  20.8 1.6 %collective-permute-start.6 = (f32[128,128]{1,0:T(8,128)S(1)}, f32[128,128]{1,0:T(8,128)S(1)}, u32[]{:S(2)}, u32[]{:S(2)}) collective-permute-start(f32[128,128]{1,0:T(8,128)S(1)} %down.2.refs_0_), channel_id=1, source_target_pairs={{0,2},{2,0},{1,3},{3,1},{4,6},{6,4},{5,7},{7,5},{8,10},{10,8},{9,1... | collective-permute-start | bytes 196616 | tf_op jit(solution)/shard_map/ppermute | solution.py:439
  22.4 3.5 %collective-permute-start.8 = (bf16[32,1792]{1,0:T(8,128)(2,1)S(1)}, bf16[32,1792]{1,0:T(8,128)(2,1)S(1)}, u32[]{:S(2)}, u32[]{:S(2)}) collective-permute-start(bf16[32,1792]{1,0:T(8,128)(2,1)S(1)} %get-tuple-element.65), channel_id=1, source_target_pairs={{0,8},{4,12},{8,0},{12,4},{1,9},{5,13},{9,1},{13,5},{2,10},{6,14},... | collective-permute-start | bytes 344072 | tf_op jit(solution)/shard_map/ppermute | solution.py:430
  25.9 0.8 collective-permute-start.9
  26.7 0.5 up.2
  27.2 3.1 %collective-permute-start.13 = (bf16[32,2048]{1,0:T(8,128)(2,1)S(1)}, bf16[32,2048]{1,0:T(8,128)(2,1)S(1)}, u32[]{:S(2)}, u32[]{:S(2)}) collective-permute-start(bf16[32,2048]{1,0:T(8,128)(2,1)S(1)} %get-tuple-element.62), channel_id=1, source_target_pairs={{0,12},{4,8},{8,4},{12,0},{1,13},{5,9},{9,5},{13,1},{2,14},{6,10},... | collective-permute-start | bytes 393224 | tf_op jit(solution)/shard_map/ppermute | solution.py:430
  30.3 1.4 %collective-permute-start.11 = (bf16[32,2048]{1,0:T(8,128)(2,1)S(1)}, bf16[32,2048]{1,0:T(8,128)(2,1)S(1)}, u32[]{:S(2)}, u32[]{:S(2)}) collective-permute-start(bf16[32,2048]{1,0:T(8,128)(2,1)S(1)} %get-tuple-element.60), channel_id=1, source_target_pairs={{0,4},{4,0},{8,12},{12,8},{1,5},{5,1},{9,13},{13,9},{2,6},{6,2},{1... | collective-permute-start | bytes 393224 | tf_op jit(solution)/shard_map/ppermute | solution.py:430
  31.7 0.1 compare_select_fusion
  31.7 8.0 %collective-permute-done.8.refs_2_ = bf16[32,1792]{1,0:T(8,128)(2,1)S(1)} collective-permute-done((bf16[32,1792]{1,0:T(8,128)(2,1)S(1)}, bf16[32,1792]{1,0:T(8,128)(2,1)S(1)}, u32[]{:S(2)}, u32[]{:S(2)}) %collective-permute-start.8) | collective-permute-done | bytes 114720 | tf_op jit(solution)/shard_map/ppermute | solution.py:430
  39.7 1.1 %down.3.refs_0_ = f32[128,128]{1,0:T(8,128)S(1)} custom-call(bf16[32,1792]{1,0:T(8,128)(2,1)S(1)} %get-tuple-element.63.refs_0_, bf16[32,1792]{1,0:T(8,128)(2,1)S(1)} %collective-permute-done.7.refs_1_, bf16[32,1792]{1,0:T(8,128)(2,1)S(1)} %collective-permute-done.8.refs_2_, bf16[32,1792]{1,0:T(8,128)(2,1)S(1)} %collective-permute-done.9.refs_3_, ...), custom_call_target="tpu_custom_call" | custom-call | flops 1 | bytes 1 | tf_op jit(solution)/shard_map/down/pallas_call | solution.py:576
  40.9 0.6 collective-permute-start.10
  41.5 0.1 add_convert_fusion
  41.5 6.6 %project.1.refs_7_ = f32[256,1280]{1,0:T(8,128)S(1)} custom-call(bf16[256,3584]{1,0:T(8,128)(2,1)S(1)} %get-tuple-element.67.rows_ref, f32[18,128]{1,0:T(8,128)S(1)} %bitcast.19, bf16[3584,2304]{1,0:T(8,128)(2,1)} %weight_hbm.1), custom_call_target="tpu_custom_call" | custom-call | flops 1 | bytes 1 | tf_op jit(solution)/shard_map/project/pallas_call | solution.py:564
  48.1 0.0 copy-start.1
  48.2 0.5 up.3
  48.7 2.8 %collective-permute-start.16 = (bf16[32,2048]{1,0:T(8,128)(2,1)S(1)}, bf16[32,2048]{1,0:T(8,128)(2,1)S(1)}, u32[]{:S(2)}, u32[]{:S(2)}) collective-permute-start(bf16[32,2048]{1,0:T(8,128)(2,1)S(1)} %get-tuple-element.79), channel_id=1, source_target_pairs={{0,12},{4,8},{8,4},{12,0},{1,13},{5,9},{9,5},{13,1},{2,14},{6,10},... | collective-permute-start | bytes 393224 | tf_op jit(solution)/shard_map/ppermute | solution.py:430
  51.5 1.7 %collective-permute-start.15 = (bf16[32,2048]{1,0:T(8,128)(2,1)S(1)}, bf16[32,2048]{1,0:T(8,128)(2,1)S(1)}, u32[]{:S(2)}, u32[]{:S(2)}) collective-permute-start(bf16[32,2048]{1,0:T(8,128)(2,1)S(1)} %get-tuple-element.78), channel_id=1, source_target_pairs={{0,8},{4,12},{8,0},{12,4},{1,9},{5,13},{9,1},{13,5},{2,10},{6,14},... | collective-permute-start | bytes 393224 | tf_op jit(solution)/shard_map/ppermute | solution.py:430
  53.2 0.5 collective-permute-start.14
  53.7 0.5 fusion
  54.3 3.8 %attend.2 = (f32[128,512]{1,0:T(8,128)S(1)}, bf16[64,1792]{1,0:T(8,128)(2,1)S(1)}, bf16[64,1792]{1,0:T(8,128)(2,1)S(1)}, bf16[64,1792]{1,0:T(8,128)(2,1)S(1)}, bf16[64,1792]{1,0:T(8,128)(2,1)S(1)}) custom-call(s32[8,64]{1,0:T(8,128)S(1)} %get-tuple-element.74.refs_0_, s32[1,64]{1,0:T(1,128)S(1)} %bitcast.20, f32[256,128]{1,0:T(8,128)S(1)} %get-tuple-element.94.refs_2_, ...), custom_call_target="tpu_custom_call" | custom-call | flops 1 | bytes 1 | tf_op jit(solution)/shard_map/attend/pallas_call | solution.py:630
  58.1 4.7 %collective-permute-done.15.refs_10_ = bf16[32,2048]{1,0:T(8,128)(2,1)S(1)} collective-permute-done((bf16[32,2048]{1,0:T(8,128)(2,1)S(1)}, bf16[32,2048]{1,0:T(8,128)(2,1)S(1)}, u32[]{:S(2)}, u32[]{:S(2)}) %collective-permute-start.15) | collective-permute-done | bytes 131104 | tf_op jit(solution)/shard_map/ppermute | solution.py:430
  62.8 1.0 collective-permute-start.19
  63.9 3.3 %collective-permute-start.17 = (bf16[64,1792]{1,0:T(8,128)(2,1)S(1)}, bf16[64,1792]{1,0:T(8,128)(2,1)S(1)}, u32[]{:S(2)}, u32[]{:S(2)}) collective-permute-start(bf16[64,1792]{1,0:T(8,128)(2,1)S(1)} %get-tuple-element.80), channel_id=1, source_target_pairs={{0,4},{4,0},{8,12},{12,8},{1,5},{5,1},{9,13},{13,9},{2,6},{6,2},{1... | collective-permute-start | bytes 688136 | tf_op jit(solution)/shard_map/ppermute | solution.py:430
  67.2 3.7 %attend.3 = (bf16[64,1792]{1,0:T(8,128)(2,1)S(1)}, bf16[64,1792]{1,0:T(8,128)(2,1)S(1)}, bf16[64,1792]{1,0:T(8,128)(2,1)S(1)}, bf16[64,1792]{1,0:T(8,128)(2,1)S(1)}) custom-call(s32[8,64]{1,0:T(8,128)S(1)} %get-tuple-element.74.refs_0_, s32[1,64]{1,0:T(1,128)S(1)} %bitcast.21, f32[256,128]{1,0:T(8,128)S(1)} %get-tuple-element.94.refs_2_, ...), custom_call_target="tpu_custom_call" | custom-call | flops 1 | bytes 1 | tf_op jit(solution)/shard_map/attend/pallas_call | solution.py:630
  70.9 2.2 %collective-permute-done.19.refs_3_ = bf16[64,1792]{1,0:T(8,128)(2,1)S(1)} collective-permute-done((bf16[64,1792]{1,0:T(8,128)(2,1)S(1)}, bf16[64,1792]{1,0:T(8,128)(2,1)S(1)}, u32[]{:S(2)}, u32[]{:S(2)}) %collective-permute-start.19) | collective-permute-done | bytes 229408 | tf_op jit(solution)/shard_map/ppermute | solution.py:430
  73.2 8.9 %collective-permute-done.18.refs_2_ = bf16[64,1792]{1,0:T(8,128)(2,1)S(1)} collective-permute-done((bf16[64,1792]{1,0:T(8,128)(2,1)S(1)}, bf16[64,1792]{1,0:T(8,128)(2,1)S(1)}, u32[]{:S(2)}, u32[]{:S(2)}) %collective-permute-start.18) | collective-permute-done | bytes 229408 | tf_op jit(solution)/shard_map/ppermute | solution.py:430
  82.1 2.0 %collective-permute-start.23 = (bf16[64,1792]{1,0:T(8,128)(2,1)S(1)}, bf16[64,1792]{1,0:T(8,128)(2,1)S(1)}, u32[]{:S(2)}, u32[]{:S(2)}) collective-permute-start(bf16[64,1792]{1,0:T(8,128)(2,1)S(1)} %get-tuple-element.92), channel_id=1, source_target_pairs={{0,12},{4,8},{8,4},{12,0},{1,13},{5,9},{9,5},{13,1},{2,14},{6,10},... | collective-permute-start | bytes 688136 | tf_op jit(solution)/shard_map/ppermute | solution.py:430
  84.2 0.1 collective-permute-start.20
  84.2 2.5 %collective-permute-start.21 = (bf16[64,1792]{1,0:T(8,128)(2,1)S(1)}, bf16[64,1792]{1,0:T(8,128)(2,1)S(1)}, u32[]{:S(2)}, u32[]{:S(2)}) collective-permute-start(bf16[64,1792]{1,0:T(8,128)(2,1)S(1)} %get-tuple-element.88), channel_id=1, source_target_pairs={{0,4},{4,0},{8,12},{12,8},{1,5},{5,1},{9,13},{13,9},{2,6},{6,2},{1... | collective-permute-start | bytes 688136 | tf_op jit(solution)/shard_map/ppermute | solution.py:430
  86.7 0.2 collective-permute-start.24
  86.9 4.2 %collective-permute-done.23.refs_8_ = bf16[64,1792]{1,0:T(8,128)(2,1)S(1)} collective-permute-done((bf16[64,1792]{1,0:T(8,128)(2,1)S(1)}, bf16[64,1792]{1,0:T(8,128)(2,1)S(1)}, u32[]{:S(2)}, u32[]{:S(2)}) %collective-permute-start.23) | collective-permute-done | bytes 229408 | tf_op jit(solution)/shard_map/ppermute | solution.py:430
  91.1 9.8 %collective-permute-done.22.refs_7_ = bf16[64,1792]{1,0:T(8,128)(2,1)S(1)} collective-permute-done((bf16[64,1792]{1,0:T(8,128)(2,1)S(1)}, bf16[64,1792]{1,0:T(8,128)(2,1)S(1)}, u32[]{:S(2)}, u32[]{:S(2)}) %collective-permute-start.22) | collective-permute-done | bytes 229408 | tf_op jit(solution)/shard_map/ppermute | solution.py:430
  100.9 0.5 collective-permute-start.25
  101.4 1.0 collective-permute-done.26.refs_11_
  102.4 0.3 collective-permute-done.25.refs_10_
  102.7 1.9 %place.1 = bf16[128,4,1792]{2,1,0:T(4,128)(2,1)} custom-call(bf16[64,1792]{1,0:T(8,128)(2,1)S(1)} %get-tuple-element.75.refs_0_, bf16[64,1792]{1,0:T(8,128)(2,1)S(1)} %collective-permute-done.17.refs_1_, bf16[64,1792]{1,0:T(8,128)(2,1)S(1)} %collective-permute-done.18.refs_2_, bf16[64,1792]{1,0:T(8,128)(2,1)S(1)} %collective-permute-done.19.refs_3_, ...), custom_call_target="tpu_custom_call" | custom-call | flops 1 | bytes 1 | tf_op jit(solution)/shard_map/place/pallas_call | solution.py:698
  (52 shorter events, 0.2 us)
Async XLA Ops:
  0.0 10.6 %copy-start.9 = (s32[64,1]{0,1:T(1,128)S(1)}, s32[64,1]{0,1:T(1,128)}, u32[]{:S(2)}) copy-start(s32[64,1]{0,1:T(1,128)} %param.17) | copy-start | bytes 772
  0.0 10.7 %copy-start.10 = (s32[32]{0:T(128)S(1)}, s32[32]{0:T(128)}, u32[]{:S(2)}) copy-start(s32[32]{0:T(128)} %param.18) | copy-start | bytes 388
  0.0 10.7 %copy-start.11 = (s32[64,1]{0,1:T(1,128)S(1)}, s32[64,1]{0,1:T(1,128)}, u32[]{:S(2)}) copy-start(s32[64,1]{0,1:T(1,128)} %param.25) | copy-start | bytes 772
  0.0 10.7 %copy-start.6 = (f32[3584]{0:T(1024)S(1)}, f32[3584]{0:T(1024)}, u32[]{:S(2)}) copy-start(f32[3584]{0:T(1024)} %param.14) | copy-start | bytes 43012
  0.0 10.7 %copy-start.7 = (f32[2304]{0:T(1024)S(1)}, f32[2304]{0:T(1024)}, u32[]{:S(2)}) copy-start(f32[2304]{0:T(1024)} %param.16) | copy-start | bytes 27652
  0.0 10.6 %collective-permute-start = (bf16[4,1792,128]{2,1,0:T(8,128)(2,1)}, bf16[4,1792,128]{2,1,0:T(8,128)(2,1)S(1)}, u32[]{:S(2)}, u32[]{:S(2)}) collective-permute-start(bf16[4,1792,128]{2,1,0:T(8,128)(2,1)} %refs_4_.5), channel_id=1, source_target_pairs={{0,1},{1,0},{2,3},{3,2},{4,5},{5,4},{6,7},{7,6},{8,9},{9,8},{10,11... | collective-permute-start | bytes 5505032 | tf_op jit(solution)/shard_map/ppermute | solution.py:439
  0.5 10.1 %collective-permute-start.1 = (bf16[256,1792]{1,0:T(8,128)(2,1)}, bf16[256,1792]{1,0:T(8,128)(2,1)S(1)}, u32[]{:S(2)}, u32[]{:S(2)}) collective-permute-start(bf16[256,1792]{1,0:T(8,128)(2,1)} %bitcast.10), channel_id=1, source_target_pairs={{0,1},{1,0},{2,3},{3,2},{4,5},{5,4},{6,7},{7,6},{8,9},{9,8},{10,11... | collective-permute-start | bytes 2752520 | tf_op jit(solution)/shard_map/ppermute | solution.py:439
  0.6 9.2 %collective-permute-start.2 = (bf16[256,256]{1,0:T(8,128)(2,1)}, bf16[256,256]{1,0:T(8,128)(2,1)S(1)}, u32[]{:S(2)}, u32[]{:S(2)}) collective-permute-start(bf16[256,256]{1,0:T(8,128)(2,1)} %bitcast.13), channel_id=1, source_target_pairs={{0,1},{1,0},{2,3},{3,2},{4,5},{5,4},{6,7},{7,6},{8,9},{9,8},{10,11... | collective-permute-start | bytes 393224 | tf_op jit(solution)/shard_map/ppermute | solution.py:439
  4.5 15.1 %collective-permute-start.3 = (bf16[32,1792]{1,0:T(8,128)(2,1)}, bf16[32,1792]{1,0:T(8,128)(2,1)S(1)}, u32[]{:S(2)}, u32[]{:S(2)}) collective-permute-start(bf16[32,1792]{1,0:T(8,128)(2,1)} %get-tuple-element.50), channel_id=1, source_target_pairs={{0,4},{4,0},{8,12},{12,8},{1,5},{5,1},{9,13},{13,9},{2,6},{6,2},{1... | collective-permute-start | bytes 344072 | tf_op jit(solution)/shard_map/ppermute | solution.py:430
  7.2 12.4 %collective-permute-start.4 = (bf16[32,1792]{1,0:T(8,128)(2,1)}, bf16[32,1792]{1,0:T(8,128)(2,1)S(1)}, u32[]{:S(2)}, u32[]{:S(2)}) collective-permute-start(bf16[32,1792]{1,0:T(8,128)(2,1)} %get-tuple-element.51), channel_id=1, source_target_pairs={{0,8},{4,12},{8,0},{12,4},{1,9},{5,13},{9,1},{13,5},{2,10},{6,14},... | collective-permute-start | bytes 344072 | tf_op jit(solution)/shard_map/ppermute | solution.py:430
  9.8 9.8 %collective-permute-start.5 = (bf16[32,1792]{1,0:T(8,128)(2,1)}, bf16[32,1792]{1,0:T(8,128)(2,1)S(1)}, u32[]{:S(2)}, u32[]{:S(2)}) collective-permute-start(bf16[32,1792]{1,0:T(8,128)(2,1)} %get-tuple-element.52), channel_id=1, source_target_pairs={{0,12},{4,8},{8,4},{12,0},{1,13},{5,9},{9,5},{13,1},{2,14},{6,10},... | collective-permute-start | bytes 344072 | tf_op jit(solution)/shard_map/ppermute | solution.py:430
  10.7 8.9 %copy-start.8 = (s32[64]{0:T(128)S(1)}, s32[64]{0:T(128)}, u32[]{:S(2)}) copy-start(s32[64]{0:T(128)} %param.19) | copy-start | bytes 772
  10.7 8.9 %copy-start = (bf16[4,1792,128]{2,1,0:T(8,128)(2,1)S(1)}, bf16[4,1792,128]{2,1,0:T(8,128)(2,1)}, u32[]{:S(2)}) copy-start(bf16[4,1792,128]{2,1,0:T(8,128)(2,1)} %refs_4_.5) | copy-start | bytes 5505028
  10.7 8.9 %copy-start.5 = (bf16[32,1792]{1,0:T(8,128)(2,1)S(1)}, bf16[32,1792]{1,0:T(8,128)(2,1)}, u32[]{:S(2)}) copy-start(bf16[32,1792]{1,0:T(8,128)(2,1)} %get-tuple-element.57.refs_0_) | copy-start | bytes 344068
  19.4 10.9 %collective-permute-start.7 = (bf16[32,1792]{1,0:T(8,128)(2,1)S(1)}, bf16[32,1792]{1,0:T(8,128)(2,1)S(1)}, u32[]{:S(2)}, u32[]{:S(2)}) collective-permute-start(bf16[32,1792]{1,0:T(8,128)(2,1)S(1)} %get-tuple-element.64), channel_id=1, source_target_pairs={{0,4},{4,0},{8,12},{12,8},{1,5},{5,1},{9,13},{13,9},{2,6},{6,2},{1... | collective-permute-start | bytes 344072 | tf_op jit(solution)/shard_map/ppermute | solution.py:430
  19.6 7.1 %copy-start.3 = (bf16[4,64,1792]{2,1,0:T(8,128)(2,1)S(1)}, bf16[4,64,1792]{2,1,0:T(8,128)(2,1)}, u32[]{:S(2)}) copy-start(bf16[4,64,1792]{2,1,0:T(8,128)(2,1)} %param.23) | copy-start | bytes 2752516
  19.6 7.1 %copy-start.4 = (bf16[4,64,256]{2,1,0:T(8,128)(2,1)S(1)}, bf16[4,64,256]{2,1,0:T(8,128)(2,1)}, u32[]{:S(2)}) copy-start(bf16[4,64,256]{2,1,0:T(8,128)(2,1)} %param.24) | copy-start | bytes 393220
  20.8 5.9 %collective-permute-start.6 = (f32[128,128]{1,0:T(8,128)S(1)}, f32[128,128]{1,0:T(8,128)S(1)}, u32[]{:S(2)}, u32[]{:S(2)}) collective-permute-start(f32[128,128]{1,0:T(8,128)S(1)} %down.2.refs_0_), channel_id=1, source_target_pairs={{0,2},{2,0},{1,3},{3,1},{4,6},{6,4},{5,7},{7,5},{8,10},{10,8},{9,1... | collective-permute-start | bytes 196616 | tf_op jit(solution)/shard_map/ppermute | solution.py:439
  22.4 17.4 %collective-permute-start.8 = (bf16[32,1792]{1,0:T(8,128)(2,1)S(1)}, bf16[32,1792]{1,0:T(8,128)(2,1)S(1)}, u32[]{:S(2)}, u32[]{:S(2)}) collective-permute-start(bf16[32,1792]{1,0:T(8,128)(2,1)S(1)} %get-tuple-element.65), channel_id=1, source_target_pairs={{0,8},{4,12},{8,0},{12,4},{1,9},{5,13},{9,1},{13,5},{2,10},{6,14},... | collective-permute-start | bytes 344072 | tf_op jit(solution)/shard_map/ppermute | solution.py:430
  25.9 13.9 %collective-permute-start.9 = (bf16[32,1792]{1,0:T(8,128)(2,1)S(1)}, bf16[32,1792]{1,0:T(8,128)(2,1)S(1)}, u32[]{:S(2)}, u32[]{:S(2)}) collective-permute-start(bf16[32,1792]{1,0:T(8,128)(2,1)S(1)} %get-tuple-element.66), channel_id=1, source_target_pairs={{0,12},{4,8},{8,4},{12,0},{1,13},{5,9},{9,5},{13,1},{2,14},{6,10},... | collective-permute-start | bytes 344072 | tf_op jit(solution)/shard_map/ppermute | solution.py:430
  27.2 21.4 %collective-permute-start.13 = (bf16[32,2048]{1,0:T(8,128)(2,1)S(1)}, bf16[32,2048]{1,0:T(8,128)(2,1)S(1)}, u32[]{:S(2)}, u32[]{:S(2)}) collective-permute-start(bf16[32,2048]{1,0:T(8,128)(2,1)S(1)} %get-tuple-element.62), channel_id=1, source_target_pairs={{0,12},{4,8},{8,4},{12,0},{1,13},{5,9},{9,5},{13,1},{2,14},{6,10},... | collective-permute-start | bytes 393224 | tf_op jit(solution)/shard_map/ppermute | solution.py:430
  30.3 21.2 %collective-permute-start.12 = (bf16[32,2048]{1,0:T(8,128)(2,1)S(1)}, bf16[32,2048]{1,0:T(8,128)(2,1)S(1)}, u32[]{:S(2)}, u32[]{:S(2)}) collective-permute-start(bf16[32,2048]{1,0:T(8,128)(2,1)S(1)} %get-tuple-element.61), channel_id=1, source_target_pairs={{0,8},{4,12},{8,0},{12,4},{1,9},{5,13},{9,1},{13,5},{2,10},{6,14},... | collective-permute-start | bytes 393224 | tf_op jit(solution)/shard_map/ppermute | solution.py:430
  30.3 22.9 %collective-permute-start.11 = (bf16[32,2048]{1,0:T(8,128)(2,1)S(1)}, bf16[32,2048]{1,0:T(8,128)(2,1)S(1)}, u32[]{:S(2)}, u32[]{:S(2)}) collective-permute-start(bf16[32,2048]{1,0:T(8,128)(2,1)S(1)} %get-tuple-element.60), channel_id=1, source_target_pairs={{0,4},{4,0},{8,12},{12,8},{1,5},{5,1},{9,13},{13,9},{2,6},{6,2},{1... | collective-permute-start | bytes 393224 | tf_op jit(solution)/shard_map/ppermute | solution.py:430
  40.9 7.3 %collective-permute-start.10 = (f32[128,128]{1,0:T(8,128)S(1)}, f32[128,128]{1,0:T(8,128)S(1)}, u32[]{:S(2)}, u32[]{:S(2)}) collective-permute-start(f32[128,128]{1,0:T(8,128)S(1)} %down.3.refs_0_), channel_id=1, source_target_pairs={{0,2},{2,0},{1,3},{3,1},{4,6},{6,4},{5,7},{7,5},{8,10},{10,8},{9,1... | collective-permute-start | bytes 196616 | tf_op jit(solution)/shard_map/ppermute | solution.py:439
  48.1 6.1 %copy-start.1 = (bf16[64,32,256]{2,1,0:T(8,128)(2,1)S(1)}, bf16[64,32,256]{2,1,0:T(8,128)(2,1)}, u32[]{:S(2)}) copy-start(bf16[64,32,256]{2,1,0:T(8,128)(2,1)} %refs_4_.7) | copy-start | bytes 3145732
  48.1 6.1 %copy-start.2 = (bf16[64,32,256]{2,1,0:T(8,128)(2,1)S(1)}, bf16[64,32,256]{2,1,0:T(8,128)(2,1)}, u32[]{:S(2)}) copy-start(bf16[64,32,256]{2,1,0:T(8,128)(2,1)} %refs_5_.3) | copy-start | bytes 3145732
  48.7 9.4 %collective-permute-start.16 = (bf16[32,2048]{1,0:T(8,128)(2,1)S(1)}, bf16[32,2048]{1,0:T(8,128)(2,1)S(1)}, u32[]{:S(2)}, u32[]{:S(2)}) collective-permute-start(bf16[32,2048]{1,0:T(8,128)(2,1)S(1)} %get-tuple-element.79), channel_id=1, source_target_pairs={{0,12},{4,8},{8,4},{12,0},{1,13},{5,9},{9,5},{13,1},{2,14},{6,10},... | collective-permute-start | bytes 393224 | tf_op jit(solution)/shard_map/ppermute | solution.py:430
  51.5 11.3 %collective-permute-start.15 = (bf16[32,2048]{1,0:T(8,128)(2,1)S(1)}, bf16[32,2048]{1,0:T(8,128)(2,1)S(1)}, u32[]{:S(2)}, u32[]{:S(2)}) collective-permute-start(bf16[32,2048]{1,0:T(8,128)(2,1)S(1)} %get-tuple-element.78), channel_id=1, source_target_pairs={{0,8},{4,12},{8,0},{12,4},{1,9},{5,13},{9,1},{13,5},{2,10},{6,14},... | collective-permute-start | bytes 393224 | tf_op jit(solution)/shard_map/ppermute | solution.py:430
  53.2 9.6 %collective-permute-start.14 = (bf16[32,2048]{1,0:T(8,128)(2,1)S(1)}, bf16[32,2048]{1,0:T(8,128)(2,1)S(1)}, u32[]{:S(2)}, u32[]{:S(2)}) collective-permute-start(bf16[32,2048]{1,0:T(8,128)(2,1)S(1)} %get-tuple-element.77), channel_id=1, source_target_pairs={{0,4},{4,0},{8,12},{12,8},{1,5},{5,1},{9,13},{13,9},{2,6},{6,2},{1... | collective-permute-start | bytes 393224 | tf_op jit(solution)/shard_map/ppermute | solution.py:430
  62.8 10.3 %collective-permute-start.19 = (bf16[64,1792]{1,0:T(8,128)(2,1)S(1)}, bf16[64,1792]{1,0:T(8,128)(2,1)S(1)}, u32[]{:S(2)}, u32[]{:S(2)}) collective-permute-start(bf16[64,1792]{1,0:T(8,128)(2,1)S(1)} %get-tuple-element.84), channel_id=1, source_target_pairs={{0,12},{4,8},{8,4},{12,0},{1,13},{5,9},{9,5},{13,1},{2,14},{6,10},... | collective-permute-start | bytes 688136 | tf_op jit(solution)/shard_map/ppermute | solution.py:430
  63.9 18.2 %collective-permute-start.18 = (bf16[64,1792]{1,0:T(8,128)(2,1)S(1)}, bf16[64,1792]{1,0:T(8,128)(2,1)S(1)}, u32[]{:S(2)}, u32[]{:S(2)}) collective-permute-start(bf16[64,1792]{1,0:T(8,128)(2,1)S(1)} %get-tuple-element.82), channel_id=1, source_target_pairs={{0,8},{4,12},{8,0},{12,4},{1,9},{5,13},{9,1},{13,5},{2,10},{6,14},... | collective-permute-start | bytes 688136 | tf_op jit(solution)/shard_map/ppermute | solution.py:430
  63.9 18.2 %collective-permute-start.17 = (bf16[64,1792]{1,0:T(8,128)(2,1)S(1)}, bf16[64,1792]{1,0:T(8,128)(2,1)S(1)}, u32[]{:S(2)}, u32[]{:S(2)}) collective-permute-start(bf16[64,1792]{1,0:T(8,128)(2,1)S(1)} %get-tuple-element.80), channel_id=1, source_target_pairs={{0,4},{4,0},{8,12},{12,8},{1,5},{5,1},{9,13},{13,9},{2,6},{6,2},{1... | collective-permute-start | bytes 688136 | tf_op jit(solution)/shard_map/ppermute | solution.py:430
  82.1 9.0 %collective-permute-start.23 = (bf16[64,1792]{1,0:T(8,128)(2,1)S(1)}, bf16[64,1792]{1,0:T(8,128)(2,1)S(1)}, u32[]{:S(2)}, u32[]{:S(2)}) collective-permute-start(bf16[64,1792]{1,0:T(8,128)(2,1)S(1)} %get-tuple-element.92), channel_id=1, source_target_pairs={{0,12},{4,8},{8,4},{12,0},{1,13},{5,9},{9,5},{13,1},{2,14},{6,10},... | collective-permute-start | bytes 688136 | tf_op jit(solution)/shard_map/ppermute | solution.py:430
  84.1 16.8 %collective-permute-start.22 = (bf16[64,1792]{1,0:T(8,128)(2,1)S(1)}, bf16[64,1792]{1,0:T(8,128)(2,1)S(1)}, u32[]{:S(2)}, u32[]{:S(2)}) collective-permute-start(bf16[64,1792]{1,0:T(8,128)(2,1)S(1)} %get-tuple-element.90), channel_id=1, source_target_pairs={{0,8},{4,12},{8,0},{12,4},{1,9},{5,13},{9,1},{13,5},{2,10},{6,14},... | collective-permute-start | bytes 688136 | tf_op jit(solution)/shard_map/ppermute | solution.py:430
  84.2 17.3 %collective-permute-start.20 = (bf16[128,1792]{1,0:T(8,128)(2,1)S(1)}, bf16[128,1792]{1,0:T(8,128)(2,1)S(1)}, u32[]{:S(2)}, u32[]{:S(2)}) collective-permute-start(bf16[128,1792]{1,0:T(8,128)(2,1)S(1)} %pad_maximum_fusion), channel_id=1, source_target_pairs={{0,1},{1,0},{2,3},{3,2},{4,5},{5,4},{6,7},{7,6},{8,9},{9,8},{10,11... | collective-permute-start | bytes 1376264 | tf_op jit(solution)/shard_map/ppermute | solution.py:691
  84.2 16.7 %collective-permute-start.21 = (bf16[64,1792]{1,0:T(8,128)(2,1)S(1)}, bf16[64,1792]{1,0:T(8,128)(2,1)S(1)}, u32[]{:S(2)}, u32[]{:S(2)}) collective-permute-start(bf16[64,1792]{1,0:T(8,128)(2,1)S(1)} %get-tuple-element.88), channel_id=1, source_target_pairs={{0,4},{4,0},{8,12},{12,8},{1,5},{5,1},{9,13},{13,9},{2,6},{6,2},{1... | collective-permute-start | bytes 688136 | tf_op jit(solution)/shard_map/ppermute | solution.py:430
  86.7 14.7 %collective-permute-start.24 = (bf16[64,1792]{1,0:T(8,128)(2,1)S(1)}, bf16[64,1792]{1,0:T(8,128)(2,1)S(1)}, u32[]{:S(2)}, u32[]{:S(2)}) collective-permute-start(bf16[64,1792]{1,0:T(8,128)(2,1)S(1)} %get-tuple-element.86.refs_5_), channel_id=1, source_target_pairs={{0,1},{1,0},{2,3},{3,2},{4,5},{5,4},{6,7},{7,6},{8,9},{9,8},{10,11... | collective-permute-start | bytes 688136 | tf_op jit(solution)/shard_map/ppermute | solution.py:695
  91.1 10.4 %collective-permute-start.27 = (bf16[64,1792]{1,0:T(8,128)(2,1)S(1)}, bf16[64,1792]{1,0:T(8,128)(2,1)S(1)}, u32[]{:S(2)}, u32[]{:S(2)}) collective-permute-start(bf16[64,1792]{1,0:T(8,128)(2,1)S(1)} %collective-permute-done.23.refs_8_), channel_id=1, source_target_pairs={{0,1},{1,0},{2,3},{3,2},{4,5},{5,4},{6,7},{7,6},{8,9},{9,8},{10,11... | collective-permute-start | bytes 688136 | tf_op jit(solution)/shard_map/ppermute | solution.py:695
  100.9 1.5 %collective-permute-start.26 = (bf16[64,1792]{1,0:T(8,128)(2,1)S(1)}, bf16[64,1792]{1,0:T(8,128)(2,1)S(1)}, u32[]{:S(2)}, u32[]{:S(2)}) collective-permute-start(bf16[64,1792]{1,0:T(8,128)(2,1)S(1)} %collective-permute-done.22.refs_7_), channel_id=1, source_target_pairs={{0,1},{1,0},{2,3},{3,2},{4,5},{5,4},{6,7},{7,6},{8,9},{9,8},{10,11... | collective-permute-start | bytes 688136 | tf_op jit(solution)/shard_map/ppermute | solution.py:695
  100.9 1.8 %collective-permute-start.25 = (bf16[64,1792]{1,0:T(8,128)(2,1)S(1)}, bf16[64,1792]{1,0:T(8,128)(2,1)S(1)}, u32[]{:S(2)}, u32[]{:S(2)}) collective-permute-start(bf16[64,1792]{1,0:T(8,128)(2,1)S(1)} %collective-permute-done.21.refs_6_), channel_id=1, source_target_pairs={{0,1},{1,0},{2,3},{3,2},{4,5},{5,4},{6,7},{7,6},{8,9},{9,8},{10,11... | collective-permute-start | bytes 688136 | tf_op jit(solution)/shard_map/ppermute | solution.py:695

commit v8 on v7

--- a/solution.py
+++ b/solution.py
@@ -609,9 +609,9 @@
     returned = []
     after = qkv
     for chunk in range(chunks):
-        partials = down(chunk, after)
         if chunk:
-            qkv.append(project(partials[0]))
+            qkv.append(project(after))
+        partials = down(chunk, qkv)
         after = up(partials, qkv)
         messages = list(after)
         if chunk:

time: 105 us -> 102 us (0.971)
  waiting for transfers between devices: 39.2 us -> 35 us
  starting transfers between devices: 32.8 us -> 33.9 us
    ppermute x18, waiting for transfers between devices: 37.9 us -> 30 us  [traded(): landed[shift] = lax.ppermute(blocks[shift], axes, pairs)]
    ppermute x5, waiting for transfers between devices: 0.01 us -> 3.67 us  [from_others(): landed.append(lax.ppermute(block, axis, pairs))]
    ppermute x18, starting transfers between devices: 28.9 us -> 30 us  [traded(): landed[shift] = lax.ppermute(blocks[shift], axes, pairs)]
  transfers between devices with their start and end apart: 28 -> 28, of which waited for: 8 -> 9; matrix products, arithmetic and copies ran while one was open for 1% -> 1% of each run, Pallas kernels for 28% -> 29%
where the time goes in v8:
time: 102 us; the launch traced here: 101 us
  waiting for transfers between devices  35 us (34%)
  starting transfers between devices  33.9 us (33%)
  Pallas kernels  31.4 us (31%)
    ppermute x18, waiting for transfers between devices, traded(): landed[shift] = lax.ppermute(blocks[shift], axes, pairs)  30 us
    ppermute x18, starting transfers between devices, traded(): landed[shift] = lax.ppermute(blocks[shift], axes, pairs)  30 us
    pallas_call x1, Pallas kernels, on_device(): pl.pallas_call(functools.partial(norm_pack_project_kernel, chunk_steps, r...  8.69 us
    pallas_call x2, Pallas kernels, on_device(): pl.pallas_call(functools.partial(attend_kernel, chunk * chunk_steps, chun...  7.54 us
    pallas_call x1, Pallas kernels, project(): pl.pallas_call(functools.partial(project_kernel, cut), in_specs=[VMEM, VM...  6.56 us
    ppermute x5, waiting for transfers between devices, from_others(): landed.append(lax.ppermute(block, axis, pairs))  3.67 us
    pallas_call x1, Pallas kernels, on_device(): pl.pallas_call(functools.partial(norm_pack_kernel, chunk_steps, rows, flo...  3.45 us
    ppermute x5, starting transfers between devices, from_others(): landed.append(lax.ppermute(block, axis, pairs))  3.2 us
  transfers between devices with their start and end apart: 28, of which 9 were waited for; matrix products, arithmetic and copies ran while one was open for 1% of the time, Pallas kernels for 29%

profile of v8, /device:TPU:0, one launch (start us, length us, event | category | flops | bytes accessed | tf_op | source)
XLA Modules:
  0.0 101.5 jit_solution(5330170171176864591)
XLA Ops:
  0.0 0.5 collective-permute-start
  0.5 0.1 collective-permute-start.1
  0.6 0.4 collective-permute-start.2
  1.1 3.5 %norm_and_pack.1 = (bf16[32,1792]{1,0:T(8,128)(2,1)}, bf16[32,1792]{1,0:T(8,128)(2,1)}, bf16[32,1792]{1,0:T(8,128)(2,1)}, bf16[32,1792]{1,0:T(8,128)(2,1)}) custom-call(s32[1,64]{1,0:T(1,128)} %bitcast.22, s32[1,32]{1,0:T(1,128)} %bitcast.24, s32[1,64]{1,0:T(1,128)} %bitcast.26, f32[28,128]{1,0:T(8,128)} %bitcast.16, bf16[256,3584]{1,0:T(8,128)(2,1)} %bitcast.28), custom_call_target="tpu_custom_call" | custom-call | flops 1 | bytes 1 | tf_op jit(solution)/shard_map/norm_and_pack/pallas_call | solution.py:515
  4.5 2.7 %collective-permute-start.3 = (bf16[32,1792]{1,0:T(8,128)(2,1)}, bf16[32,1792]{1,0:T(8,128)(2,1)S(1)}, u32[]{:S(2)}, u32[]{:S(2)}) collective-permute-start(bf16[32,1792]{1,0:T(8,128)(2,1)} %get-tuple-element.50), channel_id=1, source_target_pairs={{0,4},{4,0},{8,12},{12,8},{1,5},{5,1},{9,13},{13,9},{2,6},{6,2},{1... | collective-permute-start | bytes 344072 | tf_op jit(solution)/shard_map/ppermute | solution.py:430
  7.2 2.6 %collective-permute-start.4 = (bf16[32,1792]{1,0:T(8,128)(2,1)}, bf16[32,1792]{1,0:T(8,128)(2,1)S(1)}, u32[]{:S(2)}, u32[]{:S(2)}) collective-permute-start(bf16[32,1792]{1,0:T(8,128)(2,1)} %get-tuple-element.51), channel_id=1, source_target_pairs={{0,8},{4,12},{8,0},{12,4},{1,9},{5,13},{9,1},{13,5},{2,10},{6,14},... | collective-permute-start | bytes 344072 | tf_op jit(solution)/shard_map/ppermute | solution.py:430
  9.8 0.8 collective-permute-start.5
  10.7 0.0 copy-start.8
  10.7 0.0 copy-start
  10.7 0.0 copy-start.5
  10.7 8.7 %norm_pack_project.1 = (bf16[256,3584]{1,0:T(8,128)(2,1)S(1)}, f32[256,1024]{1,0:T(8,128)S(1)}, s32[8,64]{1,0:T(8,128)S(1)}, bf16[32,1792]{1,0:T(8,128)(2,1)S(1)...) custom-call(s32[1,64]{1,0:T(1,128)S(1)} %bitcast.23, ...), custom_call_target="tpu_custom_call" | custom-call | flops 1 | bytes 1 | tf_op jit(solution)/shard_map/norm_pack_project/pallas_call | solution.py:544
  19.4 0.2 collective-permute-start.7
  19.6 1.2 %down.2.refs_0_ = f32[128,128]{1,0:T(8,128)S(1)} custom-call(bf16[32,1792]{1,0:T(8,128)(2,1)S(1)} %copy-done.5, bf16[32,1792]{1,0:T(8,128)(2,1)S(1)} %collective-permute-done.3.refs_1_, bf16[32,1792]{1,0:T(8,128)(2,1)S(1)} %collective-permute-done.4.refs_2_, bf16[32,1792]{1,0:T(8,128)(2,1)S(1)} %collective-permute-done.5.refs_3_, ...), custom_call_target="tpu_custom_call" | custom-call | flops 1 | bytes 1 | tf_op jit(solution)/shard_map/down/pallas_call | solution.py:576
  20.8 1.6 %collective-permute-start.6 = (f32[128,128]{1,0:T(8,128)S(1)}, f32[128,128]{1,0:T(8,128)S(1)}, u32[]{:S(2)}, u32[]{:S(2)}) collective-permute-start(f32[128,128]{1,0:T(8,128)S(1)} %down.2.refs_0_), channel_id=1, source_target_pairs={{0,2},{2,0},{1,3},{3,1},{4,6},{6,4},{5,7},{7,5},{8,10},{10,8},{9,1... | collective-permute-start | bytes 196616 | tf_op jit(solution)/shard_map/ppermute | solution.py:439
  22.4 3.5 %collective-permute-start.8 = (bf16[32,1792]{1,0:T(8,128)(2,1)S(1)}, bf16[32,1792]{1,0:T(8,128)(2,1)S(1)}, u32[]{:S(2)}, u32[]{:S(2)}) collective-permute-start(bf16[32,1792]{1,0:T(8,128)(2,1)S(1)} %get-tuple-element.67), channel_id=1, source_target_pairs={{0,8},{4,12},{8,0},{12,4},{1,9},{5,13},{9,1},{13,5},{2,10},{6,14},... | collective-permute-start | bytes 344072 | tf_op jit(solution)/shard_map/ppermute | solution.py:430
  25.9 0.8 collective-permute-start.9
  26.7 0.5 up.2
  27.2 3.1 %collective-permute-start.13 = (bf16[32,2048]{1,0:T(8,128)(2,1)S(1)}, bf16[32,2048]{1,0:T(8,128)(2,1)S(1)}, u32[]{:S(2)}, u32[]{:S(2)}) collective-permute-start(bf16[32,2048]{1,0:T(8,128)(2,1)S(1)} %get-tuple-element.63), channel_id=1, source_target_pairs={{0,12},{4,8},{8,4},{12,0},{1,13},{5,9},{9,5},{13,1},{2,14},{6,10},... | collective-permute-start | bytes 393224 | tf_op jit(solution)/shard_map/ppermute | solution.py:430
  30.3 1.4 %collective-permute-start.11 = (bf16[32,2048]{1,0:T(8,128)(2,1)S(1)}, bf16[32,2048]{1,0:T(8,128)(2,1)S(1)}, u32[]{:S(2)}, u32[]{:S(2)}) collective-permute-start(bf16[32,2048]{1,0:T(8,128)(2,1)S(1)} %get-tuple-element.61), channel_id=1, source_target_pairs={{0,4},{4,0},{8,12},{12,8},{1,5},{5,1},{9,13},{13,9},{2,6},{6,2},{1... | collective-permute-start | bytes 393224 | tf_op jit(solution)/shard_map/ppermute | solution.py:430
  31.7 0.1 compare_select_fusion
  31.7 6.6 %project.1.refs_7_ = f32[256,1280]{1,0:T(8,128)S(1)} custom-call(bf16[256,3584]{1,0:T(8,128)(2,1)S(1)} %get-tuple-element.57.rows_ref, f32[18,128]{1,0:T(8,128)S(1)} %bitcast.19, bf16[3584,2304]{1,0:T(8,128)(2,1)} %weight_hbm.1), custom_call_target="tpu_custom_call" | custom-call | flops 1 | bytes 1 | tf_op jit(solution)/shard_map/project/pallas_call | solution.py:564
  38.3 1.4 %collective-permute-done.8.refs_2_ = bf16[32,1792]{1,0:T(8,128)(2,1)S(1)} collective-permute-done((bf16[32,1792]{1,0:T(8,128)(2,1)S(1)}, bf16[32,1792]{1,0:T(8,128)(2,1)S(1)}, u32[]{:S(2)}, u32[]{:S(2)}) %collective-permute-start.8) | collective-permute-done | bytes 114720 | tf_op jit(solution)/shard_map/ppermute | solution.py:430
  39.7 1.1 %down.3.refs_0_ = f32[128,128]{1,0:T(8,128)S(1)} custom-call(bf16[32,1792]{1,0:T(8,128)(2,1)S(1)} %get-tuple-element.65.refs_0_, bf16[32,1792]{1,0:T(8,128)(2,1)S(1)} %collective-permute-done.7.refs_1_, bf16[32,1792]{1,0:T(8,128)(2,1)S(1)} %collective-permute-done.8.refs_2_, bf16[32,1792]{1,0:T(8,128)(2,1)S(1)} %collective-permute-done.9.refs_3_, ...), custom_call_target="tpu_custom_call" | custom-call | flops 1 | bytes 1 | tf_op jit(solution)/shard_map/down/pallas_call | solution.py:576
  40.9 0.6 collective-permute-start.10
  41.5 0.1 add_convert_fusion
  41.6 3.7 %collective-permute-done.10.refs_1_ = f32[128,128]{1,0:T(8,128)S(1)} collective-permute-done((f32[128,128]{1,0:T(8,128)S(1)}, f32[128,128]{1,0:T(8,128)S(1)}, u32[]{:S(2)}, u32[]{:S(2)}) %collective-permute-start.10) | collective-permute-done | bytes 65568 | tf_op jit(solution)/shard_map/ppermute | solution.py:439
  45.2 0.5 up.3
  45.7 2.8 %collective-permute-start.16 = (bf16[32,2048]{1,0:T(8,128)(2,1)S(1)}, bf16[32,2048]{1,0:T(8,128)(2,1)S(1)}, u32[]{:S(2)}, u32[]{:S(2)}) collective-permute-start(bf16[32,2048]{1,0:T(8,128)(2,1)S(1)} %get-tuple-element.79), channel_id=1, source_target_pairs={{0,12},{4,8},{8,4},{12,0},{1,13},{5,9},{9,5},{13,1},{2,14},{6,10},... | collective-permute-start | bytes 393224 | tf_op jit(solution)/shard_map/ppermute | solution.py:430
  48.5 1.7 %collective-permute-start.15 = (bf16[32,2048]{1,0:T(8,128)(2,1)S(1)}, bf16[32,2048]{1,0:T(8,128)(2,1)S(1)}, u32[]{:S(2)}, u32[]{:S(2)}) collective-permute-start(bf16[32,2048]{1,0:T(8,128)(2,1)S(1)} %get-tuple-element.78), channel_id=1, source_target_pairs={{0,8},{4,12},{8,0},{12,4},{1,9},{5,13},{9,1},{13,5},{2,10},{6,14},... | collective-permute-start | bytes 393224 | tf_op jit(solution)/shard_map/ppermute | solution.py:430
  50.3 1.6 %collective-permute-start.14 = (bf16[32,2048]{1,0:T(8,128)(2,1)S(1)}, bf16[32,2048]{1,0:T(8,128)(2,1)S(1)}, u32[]{:S(2)}, u32[]{:S(2)}) collective-permute-start(bf16[32,2048]{1,0:T(8,128)(2,1)S(1)} %get-tuple-element.77), channel_id=1, source_target_pairs={{0,4},{4,0},{8,12},{12,8},{1,5},{5,1},{9,13},{13,9},{2,6},{6,2},{1... | collective-permute-start | bytes 393224 | tf_op jit(solution)/shard_map/ppermute | solution.py:430
  51.8 0.5 fusion
  52.4 3.8 %attend.2 = (f32[128,512]{1,0:T(8,128)S(1)}, bf16[64,1792]{1,0:T(8,128)(2,1)S(1)}, bf16[64,1792]{1,0:T(8,128)(2,1)S(1)}, bf16[64,1792]{1,0:T(8,128)(2,1)S(1)}, bf16[64,1792]{1,0:T(8,128)(2,1)S(1)}) custom-call(s32[8,64]{1,0:T(8,128)S(1)} %get-tuple-element.74.refs_0_, s32[1,64]{1,0:T(1,128)S(1)} %bitcast.20, f32[256,128]{1,0:T(8,128)S(1)} %get-tuple-element.94.refs_2_, ...), custom_call_target="tpu_custom_call" | custom-call | flops 1 | bytes 1 | tf_op jit(solution)/shard_map/attend/pallas_call | solution.py:630
  56.2 2.5 %collective-permute-done.15.refs_10_ = bf16[32,2048]{1,0:T(8,128)(2,1)S(1)} collective-permute-done((bf16[32,2048]{1,0:T(8,128)(2,1)S(1)}, bf16[32,2048]{1,0:T(8,128)(2,1)S(1)}, u32[]{:S(2)}, u32[]{:S(2)}) %collective-permute-start.15) | collective-permute-done | bytes 131104 | tf_op jit(solution)/shard_map/ppermute | solution.py:430
  58.8 2.5 %collective-permute-start.19 = (bf16[64,1792]{1,0:T(8,128)(2,1)S(1)}, bf16[64,1792]{1,0:T(8,128)(2,1)S(1)}, u32[]{:S(2)}, u32[]{:S(2)}) collective-permute-start(bf16[64,1792]{1,0:T(8,128)(2,1)S(1)} %get-tuple-element.84), channel_id=1, source_target_pairs={{0,12},{4,8},{8,4},{12,0},{1,13},{5,9},{9,5},{13,1},{2,14},{6,10},... | collective-permute-start | bytes 688136 | tf_op jit(solution)/shard_map/ppermute | solution.py:430
  61.3 1.9 %collective-permute-start.17 = (bf16[64,1792]{1,0:T(8,128)(2,1)S(1)}, bf16[64,1792]{1,0:T(8,128)(2,1)S(1)}, u32[]{:S(2)}, u32[]{:S(2)}) collective-permute-start(bf16[64,1792]{1,0:T(8,128)(2,1)S(1)} %get-tuple-element.80), channel_id=1, source_target_pairs={{0,4},{4,0},{8,12},{12,8},{1,5},{5,1},{9,13},{13,9},{2,6},{6,2},{1... | collective-permute-start | bytes 688136 | tf_op jit(solution)/shard_map/ppermute | solution.py:430
  63.2 3.7 %attend.3 = (bf16[64,1792]{1,0:T(8,128)(2,1)S(1)}, bf16[64,1792]{1,0:T(8,128)(2,1)S(1)}, bf16[64,1792]{1,0:T(8,128)(2,1)S(1)}, bf16[64,1792]{1,0:T(8,128)(2,1)S(1)}) custom-call(s32[8,64]{1,0:T(8,128)S(1)} %get-tuple-element.74.refs_0_, s32[1,64]{1,0:T(1,128)S(1)} %bitcast.21, f32[256,128]{1,0:T(8,128)S(1)} %get-tuple-element.94.refs_2_, ...), custom_call_target="tpu_custom_call" | custom-call | flops 1 | bytes 1 | tf_op jit(solution)/shard_map/attend/pallas_call | solution.py:630
  66.9 2.2 %collective-permute-done.19.refs_3_ = bf16[64,1792]{1,0:T(8,128)(2,1)S(1)} collective-permute-done((bf16[64,1792]{1,0:T(8,128)(2,1)S(1)}, bf16[64,1792]{1,0:T(8,128)(2,1)S(1)}, u32[]{:S(2)}, u32[]{:S(2)}) %collective-permute-start.19) | collective-permute-done | bytes 229408 | tf_op jit(solution)/shard_map/ppermute | solution.py:430
  69.1 9.5 %collective-permute-done.18.refs_2_ = bf16[64,1792]{1,0:T(8,128)(2,1)S(1)} collective-permute-done((bf16[64,1792]{1,0:T(8,128)(2,1)S(1)}, bf16[64,1792]{1,0:T(8,128)(2,1)S(1)}, u32[]{:S(2)}, u32[]{:S(2)}) %collective-permute-start.18) | collective-permute-done | bytes 229408 | tf_op jit(solution)/shard_map/ppermute | solution.py:430
  78.6 2.9 %collective-permute-start.23 = (bf16[64,1792]{1,0:T(8,128)(2,1)S(1)}, bf16[64,1792]{1,0:T(8,128)(2,1)S(1)}, u32[]{:S(2)}, u32[]{:S(2)}) collective-permute-start(bf16[64,1792]{1,0:T(8,128)(2,1)S(1)} %get-tuple-element.92), channel_id=1, source_target_pairs={{0,12},{4,8},{8,4},{12,0},{1,13},{5,9},{9,5},{13,1},{2,14},{6,10},... | collective-permute-start | bytes 688136 | tf_op jit(solution)/shard_map/ppermute | solution.py:430
  81.6 0.1 collective-permute-start.20
  81.7 1.6 %collective-permute-start.21 = (bf16[64,1792]{1,0:T(8,128)(2,1)S(1)}, bf16[64,1792]{1,0:T(8,128)(2,1)S(1)}, u32[]{:S(2)}, u32[]{:S(2)}) collective-permute-start(bf16[64,1792]{1,0:T(8,128)(2,1)S(1)} %get-tuple-element.88), channel_id=1, source_target_pairs={{0,4},{4,0},{8,12},{12,8},{1,5},{5,1},{9,13},{13,9},{2,6},{6,2},{1... | collective-permute-start | bytes 688136 | tf_op jit(solution)/shard_map/ppermute | solution.py:430
  83.3 0.2 collective-permute-start.24
  83.4 4.1 %collective-permute-done.23.refs_8_ = bf16[64,1792]{1,0:T(8,128)(2,1)S(1)} collective-permute-done((bf16[64,1792]{1,0:T(8,128)(2,1)S(1)}, bf16[64,1792]{1,0:T(8,128)(2,1)S(1)}, u32[]{:S(2)}, u32[]{:S(2)}) %collective-permute-start.23) | collective-permute-done | bytes 229408 | tf_op jit(solution)/shard_map/ppermute | solution.py:430
  87.6 10.2 %collective-permute-done.22.refs_7_ = bf16[64,1792]{1,0:T(8,128)(2,1)S(1)} collective-permute-done((bf16[64,1792]{1,0:T(8,128)(2,1)S(1)}, bf16[64,1792]{1,0:T(8,128)(2,1)S(1)}, u32[]{:S(2)}, u32[]{:S(2)}) %collective-permute-start.22) | collective-permute-done | bytes 229408 | tf_op jit(solution)/shard_map/ppermute | solution.py:430
  97.7 0.5 collective-permute-start.25
  98.2 1.0 collective-permute-done.26.refs_11_
  99.2 0.3 collective-permute-done.25.refs_10_
  99.5 1.9 %place.1 = bf16[128,4,1792]{2,1,0:T(4,128)(2,1)} custom-call(bf16[64,1792]{1,0:T(8,128)(2,1)S(1)} %get-tuple-element.75.refs_0_, bf16[64,1792]{1,0:T(8,128)(2,1)S(1)} %collective-permute-done.17.refs_1_, bf16[64,1792]{1,0:T(8,128)(2,1)S(1)} %collective-permute-done.18.refs_2_, bf16[64,1792]{1,0:T(8,128)(2,1)S(1)} %collective-permute-done.19.refs_3_, ...), custom_call_target="tpu_custom_call" | custom-call | flops 1 | bytes 1 | tf_op jit(solution)/shard_map/place/pallas_call | solution.py:698
  (52 shorter events, 0.2 us)
Async XLA Ops:
  0.0 10.6 %copy-start.9 = (s32[64,1]{0,1:T(1,128)S(1)}, s32[64,1]{0,1:T(1,128)}, u32[]{:S(2)}) copy-start(s32[64,1]{0,1:T(1,128)} %param.17) | copy-start | bytes 772
  0.0 10.7 %copy-start.10 = (s32[32]{0:T(128)S(1)}, s32[32]{0:T(128)}, u32[]{:S(2)}) copy-start(s32[32]{0:T(128)} %param.18) | copy-start | bytes 388
  0.0 10.7 %copy-start.11 = (s32[64,1]{0,1:T(1,128)S(1)}, s32[64,1]{0,1:T(1,128)}, u32[]{:S(2)}) copy-start(s32[64,1]{0,1:T(1,128)} %param.25) | copy-start | bytes 772
  0.0 10.7 %copy-start.6 = (f32[3584]{0:T(1024)S(1)}, f32[3584]{0:T(1024)}, u32[]{:S(2)}) copy-start(f32[3584]{0:T(1024)} %param.14) | copy-start | bytes 43012
  0.0 10.7 %copy-start.7 = (f32[2304]{0:T(1024)S(1)}, f32[2304]{0:T(1024)}, u32[]{:S(2)}) copy-start(f32[2304]{0:T(1024)} %param.16) | copy-start | bytes 27652
  0.0 10.6 %collective-permute-start = (bf16[4,1792,128]{2,1,0:T(8,128)(2,1)}, bf16[4,1792,128]{2,1,0:T(8,128)(2,1)S(1)}, u32[]{:S(2)}, u32[]{:S(2)}) collective-permute-start(bf16[4,1792,128]{2,1,0:T(8,128)(2,1)} %refs_4_.5), channel_id=1, source_target_pairs={{0,1},{1,0},{2,3},{3,2},{4,5},{5,4},{6,7},{7,6},{8,9},{9,8},{10,11... | collective-permute-start | bytes 5505032 | tf_op jit(solution)/shard_map/ppermute | solution.py:439
  0.5 10.1 %collective-permute-start.1 = (bf16[256,1792]{1,0:T(8,128)(2,1)}, bf16[256,1792]{1,0:T(8,128)(2,1)S(1)}, u32[]{:S(2)}, u32[]{:S(2)}) collective-permute-start(bf16[256,1792]{1,0:T(8,128)(2,1)} %bitcast.10), channel_id=1, source_target_pairs={{0,1},{1,0},{2,3},{3,2},{4,5},{5,4},{6,7},{7,6},{8,9},{9,8},{10,11... | collective-permute-start | bytes 2752520 | tf_op jit(solution)/shard_map/ppermute | solution.py:439
  0.6 9.2 %collective-permute-start.2 = (bf16[256,256]{1,0:T(8,128)(2,1)}, bf16[256,256]{1,0:T(8,128)(2,1)S(1)}, u32[]{:S(2)}, u32[]{:S(2)}) collective-permute-start(bf16[256,256]{1,0:T(8,128)(2,1)} %bitcast.13), channel_id=1, source_target_pairs={{0,1},{1,0},{2,3},{3,2},{4,5},{5,4},{6,7},{7,6},{8,9},{9,8},{10,11... | collective-permute-start | bytes 393224 | tf_op jit(solution)/shard_map/ppermute | solution.py:439
  4.5 15.1 %collective-permute-start.3 = (bf16[32,1792]{1,0:T(8,128)(2,1)}, bf16[32,1792]{1,0:T(8,128)(2,1)S(1)}, u32[]{:S(2)}, u32[]{:S(2)}) collective-permute-start(bf16[32,1792]{1,0:T(8,128)(2,1)} %get-tuple-element.50), channel_id=1, source_target_pairs={{0,4},{4,0},{8,12},{12,8},{1,5},{5,1},{9,13},{13,9},{2,6},{6,2},{1... | collective-permute-start | bytes 344072 | tf_op jit(solution)/shard_map/ppermute | solution.py:430
  7.2 12.4 %collective-permute-start.4 = (bf16[32,1792]{1,0:T(8,128)(2,1)}, bf16[32,1792]{1,0:T(8,128)(2,1)S(1)}, u32[]{:S(2)}, u32[]{:S(2)}) collective-permute-start(bf16[32,1792]{1,0:T(8,128)(2,1)} %get-tuple-element.51), channel_id=1, source_target_pairs={{0,8},{4,12},{8,0},{12,4},{1,9},{5,13},{9,1},{13,5},{2,10},{6,14},... | collective-permute-start | bytes 344072 | tf_op jit(solution)/shard_map/ppermute | solution.py:430
  9.8 9.8 %collective-permute-start.5 = (bf16[32,1792]{1,0:T(8,128)(2,1)}, bf16[32,1792]{1,0:T(8,128)(2,1)S(1)}, u32[]{:S(2)}, u32[]{:S(2)}) collective-permute-start(bf16[32,1792]{1,0:T(8,128)(2,1)} %get-tuple-element.52), channel_id=1, source_target_pairs={{0,12},{4,8},{8,4},{12,0},{1,13},{5,9},{9,5},{13,1},{2,14},{6,10},... | collective-permute-start | bytes 344072 | tf_op jit(solution)/shard_map/ppermute | solution.py:430
  10.7 8.9 %copy-start.8 = (s32[64]{0:T(128)S(1)}, s32[64]{0:T(128)}, u32[]{:S(2)}) copy-start(s32[64]{0:T(128)} %param.19) | copy-start | bytes 772
  10.7 8.9 %copy-start = (bf16[4,1792,128]{2,1,0:T(8,128)(2,1)S(1)}, bf16[4,1792,128]{2,1,0:T(8,128)(2,1)}, u32[]{:S(2)}) copy-start(bf16[4,1792,128]{2,1,0:T(8,128)(2,1)} %refs_4_.5) | copy-start | bytes 5505028
  10.7 8.9 %copy-start.5 = (bf16[32,1792]{1,0:T(8,128)(2,1)S(1)}, bf16[32,1792]{1,0:T(8,128)(2,1)}, u32[]{:S(2)}) copy-start(bf16[32,1792]{1,0:T(8,128)(2,1)} %get-tuple-element.58.refs_0_) | copy-start | bytes 344068
  19.4 10.9 %collective-permute-start.7 = (bf16[32,1792]{1,0:T(8,128)(2,1)S(1)}, bf16[32,1792]{1,0:T(8,128)(2,1)S(1)}, u32[]{:S(2)}, u32[]{:S(2)}) collective-permute-start(bf16[32,1792]{1,0:T(8,128)(2,1)S(1)} %get-tuple-element.66), channel_id=1, source_target_pairs={{0,4},{4,0},{8,12},{12,8},{1,5},{5,1},{9,13},{13,9},{2,6},{6,2},{1... | collective-permute-start | bytes 344072 | tf_op jit(solution)/shard_map/ppermute | solution.py:430
  19.6 7.1 %copy-start.3 = (bf16[4,64,1792]{2,1,0:T(8,128)(2,1)S(1)}, bf16[4,64,1792]{2,1,0:T(8,128)(2,1)}, u32[]{:S(2)}) copy-start(bf16[4,64,1792]{2,1,0:T(8,128)(2,1)} %param.23) | copy-start | bytes 2752516
  19.6 7.1 %copy-start.4 = (bf16[4,64,256]{2,1,0:T(8,128)(2,1)S(1)}, bf16[4,64,256]{2,1,0:T(8,128)(2,1)}, u32[]{:S(2)}) copy-start(bf16[4,64,256]{2,1,0:T(8,128)(2,1)} %param.24) | copy-start | bytes 393220
  20.8 5.9 %collective-permute-start.6 = (f32[128,128]{1,0:T(8,128)S(1)}, f32[128,128]{1,0:T(8,128)S(1)}, u32[]{:S(2)}, u32[]{:S(2)}) collective-permute-start(f32[128,128]{1,0:T(8,128)S(1)} %down.2.refs_0_), channel_id=1, source_target_pairs={{0,2},{2,0},{1,3},{3,1},{4,6},{6,4},{5,7},{7,5},{8,10},{10,8},{9,1... | collective-permute-start | bytes 196616 | tf_op jit(solution)/shard_map/ppermute | solution.py:439
  22.4 17.4 %collective-permute-start.8 = (bf16[32,1792]{1,0:T(8,128)(2,1)S(1)}, bf16[32,1792]{1,0:T(8,128)(2,1)S(1)}, u32[]{:S(2)}, u32[]{:S(2)}) collective-permute-start(bf16[32,1792]{1,0:T(8,128)(2,1)S(1)} %get-tuple-element.67), channel_id=1, source_target_pairs={{0,8},{4,12},{8,0},{12,4},{1,9},{5,13},{9,1},{13,5},{2,10},{6,14},... | collective-permute-start | bytes 344072 | tf_op jit(solution)/shard_map/ppermute | solution.py:430
  25.9 13.9 %collective-permute-start.9 = (bf16[32,1792]{1,0:T(8,128)(2,1)S(1)}, bf16[32,1792]{1,0:T(8,128)(2,1)S(1)}, u32[]{:S(2)}, u32[]{:S(2)}) collective-permute-start(bf16[32,1792]{1,0:T(8,128)(2,1)S(1)} %get-tuple-element.68), channel_id=1, source_target_pairs={{0,12},{4,8},{8,4},{12,0},{1,13},{5,9},{9,5},{13,1},{2,14},{6,10},... | collective-permute-start | bytes 344072 | tf_op jit(solution)/shard_map/ppermute | solution.py:430
  27.2 18.5 %collective-permute-start.13 = (bf16[32,2048]{1,0:T(8,128)(2,1)S(1)}, bf16[32,2048]{1,0:T(8,128)(2,1)S(1)}, u32[]{:S(2)}, u32[]{:S(2)}) collective-permute-start(bf16[32,2048]{1,0:T(8,128)(2,1)S(1)} %get-tuple-element.63), channel_id=1, source_target_pairs={{0,12},{4,8},{8,4},{12,0},{1,13},{5,9},{9,5},{13,1},{2,14},{6,10},... | collective-permute-start | bytes 393224 | tf_op jit(solution)/shard_map/ppermute | solution.py:430
  30.3 18.2 %collective-permute-start.12 = (bf16[32,2048]{1,0:T(8,128)(2,1)S(1)}, bf16[32,2048]{1,0:T(8,128)(2,1)S(1)}, u32[]{:S(2)}, u32[]{:S(2)}) collective-permute-start(bf16[32,2048]{1,0:T(8,128)(2,1)S(1)} %get-tuple-element.62), channel_id=1, source_target_pairs={{0,8},{4,12},{8,0},{12,4},{1,9},{5,13},{9,1},{13,5},{2,10},{6,14},... | collective-permute-start | bytes 393224 | tf_op jit(solution)/shard_map/ppermute | solution.py:430
  30.3 20.0 %collective-permute-start.11 = (bf16[32,2048]{1,0:T(8,128)(2,1)S(1)}, bf16[32,2048]{1,0:T(8,128)(2,1)S(1)}, u32[]{:S(2)}, u32[]{:S(2)}) collective-permute-start(bf16[32,2048]{1,0:T(8,128)(2,1)S(1)} %get-tuple-element.61), channel_id=1, source_target_pairs={{0,4},{4,0},{8,12},{12,8},{1,5},{5,1},{9,13},{13,9},{2,6},{6,2},{1... | collective-permute-start | bytes 393224 | tf_op jit(solution)/shard_map/ppermute | solution.py:430
  40.9 11.5 %copy-start.1 = (bf16[64,32,256]{2,1,0:T(8,128)(2,1)S(1)}, bf16[64,32,256]{2,1,0:T(8,128)(2,1)}, u32[]{:S(2)}) copy-start(bf16[64,32,256]{2,1,0:T(8,128)(2,1)} %refs_4_.7) | copy-start | bytes 3145732
  40.9 11.5 %copy-start.2 = (bf16[64,32,256]{2,1,0:T(8,128)(2,1)S(1)}, bf16[64,32,256]{2,1,0:T(8,128)(2,1)}, u32[]{:S(2)}) copy-start(bf16[64,32,256]{2,1,0:T(8,128)(2,1)} %refs_5_.3) | copy-start | bytes 3145732
  40.9 4.3 %collective-permute-start.10 = (f32[128,128]{1,0:T(8,128)S(1)}, f32[128,128]{1,0:T(8,128)S(1)}, u32[]{:S(2)}, u32[]{:S(2)}) collective-permute-start(f32[128,128]{1,0:T(8,128)S(1)} %down.3.refs_0_), channel_id=1, source_target_pairs={{0,2},{2,0},{1,3},{3,1},{4,6},{6,4},{5,7},{7,5},{8,10},{10,8},{9,1... | collective-permute-start | bytes 196616 | tf_op jit(solution)/shard_map/ppermute | solution.py:439
  45.7 10.5 %collective-permute-start.16 = (bf16[32,2048]{1,0:T(8,128)(2,1)S(1)}, bf16[32,2048]{1,0:T(8,128)(2,1)S(1)}, u32[]{:S(2)}, u32[]{:S(2)}) collective-permute-start(bf16[32,2048]{1,0:T(8,128)(2,1)S(1)} %get-tuple-element.79), channel_id=1, source_target_pairs={{0,12},{4,8},{8,4},{12,0},{1,13},{5,9},{9,5},{13,1},{2,14},{6,10},... | collective-permute-start | bytes 393224 | tf_op jit(solution)/shard_map/ppermute | solution.py:430
  48.5 10.2 %collective-permute-start.15 = (bf16[32,2048]{1,0:T(8,128)(2,1)S(1)}, bf16[32,2048]{1,0:T(8,128)(2,1)S(1)}, u32[]{:S(2)}, u32[]{:S(2)}) collective-permute-start(bf16[32,2048]{1,0:T(8,128)(2,1)S(1)} %get-tuple-element.78), channel_id=1, source_target_pairs={{0,8},{4,12},{8,0},{12,4},{1,9},{5,13},{9,1},{13,5},{2,10},{6,14},... | collective-permute-start | bytes 393224 | tf_op jit(solution)/shard_map/ppermute | solution.py:430
  50.3 8.5 %collective-permute-start.14 = (bf16[32,2048]{1,0:T(8,128)(2,1)S(1)}, bf16[32,2048]{1,0:T(8,128)(2,1)S(1)}, u32[]{:S(2)}, u32[]{:S(2)}) collective-permute-start(bf16[32,2048]{1,0:T(8,128)(2,1)S(1)} %get-tuple-element.77), channel_id=1, source_target_pairs={{0,4},{4,0},{8,12},{12,8},{1,5},{5,1},{9,13},{13,9},{2,6},{6,2},{1... | collective-permute-start | bytes 393224 | tf_op jit(solution)/shard_map/ppermute | solution.py:430
  58.8 10.3 %collective-permute-start.19 = (bf16[64,1792]{1,0:T(8,128)(2,1)S(1)}, bf16[64,1792]{1,0:T(8,128)(2,1)S(1)}, u32[]{:S(2)}, u32[]{:S(2)}) collective-permute-start(bf16[64,1792]{1,0:T(8,128)(2,1)S(1)} %get-tuple-element.84), channel_id=1, source_target_pairs={{0,12},{4,8},{8,4},{12,0},{1,13},{5,9},{9,5},{13,1},{2,14},{6,10},... | collective-permute-start | bytes 688136 | tf_op jit(solution)/shard_map/ppermute | solution.py:430
  61.3 17.4 %collective-permute-start.18 = (bf16[64,1792]{1,0:T(8,128)(2,1)S(1)}, bf16[64,1792]{1,0:T(8,128)(2,1)S(1)}, u32[]{:S(2)}, u32[]{:S(2)}) collective-permute-start(bf16[64,1792]{1,0:T(8,128)(2,1)S(1)} %get-tuple-element.82), channel_id=1, source_target_pairs={{0,8},{4,12},{8,0},{12,4},{1,9},{5,13},{9,1},{13,5},{2,10},{6,14},... | collective-permute-start | bytes 688136 | tf_op jit(solution)/shard_map/ppermute | solution.py:430
  61.3 17.4 %collective-permute-start.17 = (bf16[64,1792]{1,0:T(8,128)(2,1)S(1)}, bf16[64,1792]{1,0:T(8,128)(2,1)S(1)}, u32[]{:S(2)}, u32[]{:S(2)}) collective-permute-start(bf16[64,1792]{1,0:T(8,128)(2,1)S(1)} %get-tuple-element.80), channel_id=1, source_target_pairs={{0,4},{4,0},{8,12},{12,8},{1,5},{5,1},{9,13},{13,9},{2,6},{6,2},{1... | collective-permute-start | bytes 688136 | tf_op jit(solution)/shard_map/ppermute | solution.py:430
  78.6 8.9 %collective-permute-start.23 = (bf16[64,1792]{1,0:T(8,128)(2,1)S(1)}, bf16[64,1792]{1,0:T(8,128)(2,1)S(1)}, u32[]{:S(2)}, u32[]{:S(2)}) collective-permute-start(bf16[64,1792]{1,0:T(8,128)(2,1)S(1)} %get-tuple-element.92), channel_id=1, source_target_pairs={{0,12},{4,8},{8,4},{12,0},{1,13},{5,9},{9,5},{13,1},{2,14},{6,10},... | collective-permute-start | bytes 688136 | tf_op jit(solution)/shard_map/ppermute | solution.py:430
  81.5 16.2 %collective-permute-start.22 = (bf16[64,1792]{1,0:T(8,128)(2,1)S(1)}, bf16[64,1792]{1,0:T(8,128)(2,1)S(1)}, u32[]{:S(2)}, u32[]{:S(2)}) collective-permute-start(bf16[64,1792]{1,0:T(8,128)(2,1)S(1)} %get-tuple-element.90), channel_id=1, source_target_pairs={{0,8},{4,12},{8,0},{12,4},{1,9},{5,13},{9,1},{13,5},{2,10},{6,14},... | collective-permute-start | bytes 688136 | tf_op jit(solution)/shard_map/ppermute | solution.py:430
  81.6 16.6 %collective-permute-start.20 = (bf16[128,1792]{1,0:T(8,128)(2,1)S(1)}, bf16[128,1792]{1,0:T(8,128)(2,1)S(1)}, u32[]{:S(2)}, u32[]{:S(2)}) collective-permute-start(bf16[128,1792]{1,0:T(8,128)(2,1)S(1)} %pad_maximum_fusion), channel_id=1, source_target_pairs={{0,1},{1,0},{2,3},{3,2},{4,5},{5,4},{6,7},{7,6},{8,9},{9,8},{10,11... | collective-permute-start | bytes 1376264 | tf_op jit(solution)/shard_map/ppermute | solution.py:691
  81.7 16.0 %collective-permute-start.21 = (bf16[64,1792]{1,0:T(8,128)(2,1)S(1)}, bf16[64,1792]{1,0:T(8,128)(2,1)S(1)}, u32[]{:S(2)}, u32[]{:S(2)}) collective-permute-start(bf16[64,1792]{1,0:T(8,128)(2,1)S(1)} %get-tuple-element.88), channel_id=1, source_target_pairs={{0,4},{4,0},{8,12},{12,8},{1,5},{5,1},{9,13},{13,9},{2,6},{6,2},{1... | collective-permute-start | bytes 688136 | tf_op jit(solution)/shard_map/ppermute | solution.py:430
  83.3 15.0 %collective-permute-start.24 = (bf16[64,1792]{1,0:T(8,128)(2,1)S(1)}, bf16[64,1792]{1,0:T(8,128)(2,1)S(1)}, u32[]{:S(2)}, u32[]{:S(2)}) collective-permute-start(bf16[64,1792]{1,0:T(8,128)(2,1)S(1)} %get-tuple-element.86.refs_5_), channel_id=1, source_target_pairs={{0,1},{1,0},{2,3},{3,2},{4,5},{5,4},{6,7},{7,6},{8,9},{9,8},{10,11... | collective-permute-start | bytes 688136 | tf_op jit(solution)/shard_map/ppermute | solution.py:695
  87.6 10.7 %collective-permute-start.27 = (bf16[64,1792]{1,0:T(8,128)(2,1)S(1)}, bf16[64,1792]{1,0:T(8,128)(2,1)S(1)}, u32[]{:S(2)}, u32[]{:S(2)}) collective-permute-start(bf16[64,1792]{1,0:T(8,128)(2,1)S(1)} %collective-permute-done.23.refs_8_), channel_id=1, source_target_pairs={{0,1},{1,0},{2,3},{3,2},{4,5},{5,4},{6,7},{7,6},{8,9},{9,8},{10,11... | collective-permute-start | bytes 688136 | tf_op jit(solution)/shard_map/ppermute | solution.py:695
  97.7 1.5 %collective-permute-start.26 = (bf16[64,1792]{1,0:T(8,128)(2,1)S(1)}, bf16[64,1792]{1,0:T(8,128)(2,1)S(1)}, u32[]{:S(2)}, u32[]{:S(2)}) collective-permute-start(bf16[64,1792]{1,0:T(8,128)(2,1)S(1)} %collective-permute-done.22.refs_7_), channel_id=1, source_target_pairs={{0,1},{1,0},{2,3},{3,2},{4,5},{5,4},{6,7},{7,6},{8,9},{9,8},{10,11... | collective-permute-start | bytes 688136 | tf_op jit(solution)/shard_map/ppermute | solution.py:695
  97.7 1.8 %collective-permute-start.25 = (bf16[64,1792]{1,0:T(8,128)(2,1)S(1)}, bf16[64,1792]{1,0:T(8,128)(2,1)S(1)}, u32[]{:S(2)}, u32[]{:S(2)}) collective-permute-start(bf16[64,1792]{1,0:T(8,128)(2,1)S(1)} %collective-permute-done.21.refs_6_), channel_id=1, source_target_pairs={{0,1},{1,0},{2,3},{3,2},{4,5},{5,4},{6,7},{7,6},{8,9},{9,8},{10,11... | collective-permute-start | bytes 688136 | tf_op jit(solution)/shard_map/ppermute | solution.py:695

commit v9 on v7

--- a/solution.py
+++ b/solution.py
@@ -17,6 +17,7 @@
 LANE_AXES = ("streams", "sub")
 BATCH = 8
 TOGETHER = 2
+IN_FLIGHT = 5
 VMEM = pl.BlockSpec(memory_space=pltpu.VMEM)
 MIB = 1 << 20
 PACK_LIMIT = 56
@@ -194,7 +195,7 @@
 
 
 def down_kernel(lanes, spots, *refs):
-    message_refs, map_refs, partial_ref = refs[:lanes], refs[lanes:-1], refs[-1]
+    message_refs, map_refs, partial_ref = refs[:lanes][::-1], refs[lanes:-1], refs[-1]
     local_slots = map_refs[0].shape[0]
     rows = jnp.concatenate([ref[...] for ref in message_refs], axis=0)
     own_slot = row_slots(partial_ref.shape, spots)
@@ -248,13 +249,12 @@
 def attend_kernel(before, steps, rows, cache, groups, lanes, subs, last, *refs):
     places_ref, length_ref, cos_ref, sin_ref, key_ref, value_ref = refs[:6]
     qkv_refs, refs = refs[6:8], refs[8:]
-    delta_refs, refs = refs[:lanes], refs[lanes:]
+    delta_refs, refs = refs[:lanes][::-1], refs[lanes:]
     if before:
         earlier_ref, refs = refs[0], refs[1:]
     if not last:
         fresh_ref, refs = refs[0], refs[1:]
-    message_refs = refs[:lanes]
-    delta_ref, context_ref, bias_ref = refs[lanes:]
+    *message_refs, delta_ref, context_ref, bias_ref = refs
     per_message = delta_refs[0].shape[0]
     spots = per_message // steps
     query_width = PER_GROUP * HEAD_WIDTH
@@ -393,9 +393,9 @@
         ).astype(jnp.bfloat16)
 
 
-def place_kernel(found, lanes, subs, most, *refs):
-    chunks = len(found)
-    out_ref = refs[-1]
+def place_kernel(chunks, lanes, subs, most, *refs):
+    *refs, out_ref = refs
+    refs = refs[::-1]
     steps = out_ref.shape[1]
     chunk_steps = steps // chunks
     block = most * chunk_steps
@@ -410,8 +410,7 @@
         for other in range(subs):
             pieces = []
             for chunk in range(chunks):
-                array, begin = found[chunk][number][other]
-                pieces.append(refs[array][...][begin : begin + block])
+                pieces.append(refs[(chunk * lanes + number) * subs + other][...])
             rows = jnp.dot(
                 pick, jnp.concatenate(pieces, axis=0), preferred_element_type=jnp.float32
             )
@@ -424,8 +423,7 @@
 def traded(blocks, axes):
     landed = list(blocks)
     count = len(blocks)
-    order = sorted(range(1, count), key=lambda shift: -(shift ^ (shift >> 1)))
-    for shift in order:
+    for shift in range(1, count):
         pairs = [(place, place ^ shift) for place in range(count)]
         landed[shift] = lax.ppermute(blocks[shift], axes, pairs)
     return landed
@@ -486,14 +484,6 @@
 
     in_hbm = pl.BlockSpec(memory_space=pltpu.HBM)
 
-    down_maps = from_others(adapter_down_maps, "sub")
-    query_maps = from_others(
-        adapter_query_up.reshape(local_slots * ADAPTER_RANK, query_columns), "sub"
-    )
-    value_maps = from_others(
-        adapter_value_up.reshape(local_slots * ADAPTER_RANK, value_columns), "sub"
-    )
-
     pieces = 4
     flat = inputs.reshape(steps * rows, width)
     gain = input_norm_gain.reshape(width // 128, 128)
@@ -523,6 +513,13 @@
         name="norm_and_pack",
     )(*tables, gain, flat)
     arrived = [traded(messages, "streams")]
+    maps = [
+        adapter_down_maps,
+        adapter_query_up.reshape(local_slots * ADAPTER_RANK, query_columns),
+        adapter_value_up.reshape(local_slots * ADAPTER_RANK, value_columns),
+    ]
+    maps = held(maps, messages)
+    down_maps, query_maps, value_maps = [from_others(each, "sub") for each in maps]
 
     bias = projection_bias.reshape(-1, 128)
     columns = projection_weight.shape[1]
@@ -581,7 +578,7 @@
             compiler_params=pltpu.CompilerParams(vmem_limit_bytes=16 * MIB),
             cost_estimate=SMALL,
             name="down",
-        )(held(arrived[chunk][0], after), *arrived[chunk][1:], *down_maps)
+        )(*arrived[chunk][:0:-1], held(arrived[chunk][0], after), *down_maps)
         return from_others(partial_latent, "heads")
 
     def up(partials, after):
@@ -614,17 +611,17 @@
             qkv.append(project(partials[0]))
         after = up(partials, qkv)
         messages = list(after)
-        if chunk:
-            for lane in range(1, lanes):
-                messages[lane] = held(messages[lane], returned[-1][lane])
+        ahead = returned[-1] if chunk else arrived[-1]
+        for lane in range(lanes - 1, 0, -1):
+            messages[lane] = held(messages[lane], ahead[lane:])
         returned.append(traded(messages, "streams"))
 
     length_row = cache_fill_length.reshape(1, rows)
     block = flow_most * chunk_steps
-    earlier, along, alongs = [], [], []
+    earlier, blocks_out = [], []
     for chunk in range(chunks):
         last = chunk == chunks - 1
-        message = jax.ShapeDtypeStruct((subs * block, query_columns), bf16)
+        message = jax.ShapeDtypeStruct((block, query_columns), bf16)
         fresh = jax.ShapeDtypeStruct((chunk_rows, 2 * value_columns), f32)
         rows_of = lambda shape: pl.BlockSpec(shape, lambda i, chunk=chunk: (chunk, 0))
         results = pl.pallas_call(
@@ -646,8 +643,8 @@
             + [rows_of((chunk_rows, part.shape[1])) for part in qkv]
             + [whole((per_message, query_columns + value_columns))] * lanes
             + [whole(block_rows.shape) for block_rows in earlier],
-            out_specs=[whole(fresh.shape)] * (not last) + [whole(message.shape)] * lanes,
-            out_shape=[fresh] * (not last) + [message] * lanes,
+            out_specs=[whole(fresh.shape)] * (not last) + [whole(message.shape)] * flow_lanes,
+            out_shape=[fresh] * (not last) + [message] * flow_lanes,
             scratch_shapes=[
                 pltpu.VMEM((chunk_rows, query_columns + value_columns), f32),
                 pltpu.VMEM((chunk_rows, query_columns), f32),
@@ -664,46 +661,37 @@
             rotated_key_cache,
             value_cache_rows,
             *qkv,
-            *returned[chunk],
+            *returned[chunk][::-1],
             *earlier,
         )
         if not last:
             earlier, results = [results[0]], results[1:]
         results = list(results)
-        ahead = along or returned[-1]
-        for lane in range(1, lanes):
-            results[lane] = held(results[lane], ahead[1:])
-        along = traded(results, "streams")
-        alongs.append(along)
-
-    landed, found = [], []
-    for chunk, along in enumerate(alongs):
-        base = len(landed)
-        landed += along
-        where = [[(base + lane, 0)] for lane in range(lanes)]
-        for shift in range(1, subs):
-            pairs = [(core, core ^ shift) for core in range(subs)]
-            span = slice(shift * block, (shift + 1) * block)
-            if chunk < chunks - 1:
-                joined = jnp.concatenate([block_rows[span] for block_rows in along])
-                for lane in range(lanes):
-                    where[lane].append((len(landed), lane * block))
-                landed.append(lax.ppermute(joined, "sub", pairs))
-            else:
-                for lane, block_rows in enumerate(along):
-                    where[lane].append((len(landed), shift * block))
-                    landed.append(lax.ppermute(block_rows, "sub", pairs))
-        found.append(where)
+        blocks_out.append(results)
+
+    landed = [[results[0]] + [None] * (flow_lanes - 1) for results in blocks_out]
+    turns = [(chunk, lane) for chunk in range(chunks) for lane in range(flow_lanes - 1, 0, -1)]
+    for number, (chunk, lane) in enumerate(turns):
+        if number < IN_FLIGHT:
+            before = returned[-1][1:]
+        else:
+            other, other_lane = turns[number - IN_FLIGHT]
+            before = landed[other][other_lane]
+        pairs = [(place, place ^ lane) for place in range(flow_lanes)]
+        landed[chunk][lane] = lax.ppermute(
+            held(blocks_out[chunk][lane], before), LANE_AXES, pairs
+        )
+    landed = [block_rows for chunk_rows in landed for block_rows in chunk_rows]
 
     flow = pl.pallas_call(
-        functools.partial(place_kernel, found, lanes, subs, flow_most),
+        functools.partial(place_kernel, chunks, lanes, subs, flow_most),
         in_specs=[VMEM] * len(landed),
         out_specs=VMEM,
         out_shape=jax.ShapeDtypeStruct((flow_lanes * flow_most, steps, query_columns), bf16),
         compiler_params=pltpu.CompilerParams(vmem_limit_bytes=24 * MIB),
         cost_estimate=SMALL,
         name="place",
-    )(*landed)
+    )(*landed[::-1])
     return flow[None]
 
 

time: 105 us -> 105 us (level)
  waiting for transfers between devices: 39.2 us -> 18.8 us
  starting transfers between devices: 32.8 us -> 52 us
    ppermute x18 -> x12, waiting for transfers between devices: 37.9 us -> 5.74 us  [traded(): landed[shift] = lax.ppermute(blocks[shift], axes, pairs)]
    ppermute x5 -> x14, starting transfers between devices: 0.75 us -> 27.4 us  [on_device(): lax.ppermute(held(blocks_out[chunk][lane], before), LANE_AXES, pairs)]
    ppermute x5 -> x14, waiting for transfers between devices: 1.3 us -> 10.3 us  [on_device(): lax.ppermute(held(blocks_out[chunk][lane], before), LANE_AXES, pairs)]
    ppermute x18 -> x12, starting transfers between devices: 28.9 us -> 20.5 us  [traded(): landed[shift] = lax.ppermute(blocks[shift], axes, pairs)]
    ppermute x5, waiting for transfers between devices: 0.01 us -> 2.78 us  [from_others(): landed.append(lax.ppermute(block, axis, pairs))]
  transfers between devices with their start and end apart: 28 -> 31, of which waited for: 8 -> 7; matrix products, arithmetic and copies ran while one was open for 1% -> 1% of each run, Pallas kernels for 28% -> 25%
where the time goes in v9:
time: 105 us; the launch traced here: 104 us
  starting transfers between devices  52 us (50%)
  Pallas kernels  31.9 us (30%)
  waiting for transfers between devices  18.8 us (18%)
    ppermute x14, starting transfers between devices, on_device(): lax.ppermute(held(blocks_out[chunk][lane], before), LANE_AXES, pairs)  27.4 us
    ppermute x12, starting transfers between devices, traded(): landed[shift] = lax.ppermute(blocks[shift], axes, pairs)  20.5 us
    ppermute x14, waiting for transfers between devices, on_device(): lax.ppermute(held(blocks_out[chunk][lane], before), LANE_AXES, pairs)  10.3 us
    pallas_call x1, Pallas kernels, on_device(): pl.pallas_call(functools.partial(norm_pack_project_kernel, chunk_steps, r...  8.6 us
    pallas_call x2, Pallas kernels, on_device(): pl.pallas_call(functools.partial(attend_kernel, chunk * chunk_steps, chun...  7.96 us
    pallas_call x1, Pallas kernels, project(): pl.pallas_call(functools.partial(project_kernel, cut), in_specs=[VMEM, VM...  6.56 us
    ppermute x12, waiting for transfers between devices, traded(): landed[shift] = lax.ppermute(blocks[shift], axes, pairs)  5.74 us
    ppermute x5, starting transfers between devices, from_others(): landed.append(lax.ppermute(block, axis, pairs))  4.16 us
  transfers between devices with their start and end apart: 31, of which 7 were waited for; matrix products, arithmetic and copies ran while one was open for 1% of the time, Pallas kernels for 25%

profile of v9, /device:TPU:0, one launch (start us, length us, event | category | flops | bytes accessed | tf_op | source)
XLA Modules:
  0.0 103.9 jit_solution(17620554866301608889)
XLA Ops:
  0.0 3.6 %norm_and_pack.1 = (bf16[32,1792]{1,0:T(8,128)(2,1)}, bf16[32,1792]{1,0:T(8,128)(2,1)}, bf16[32,1792]{1,0:T(8,128)(2,1)}, bf16[32,1792]{1,0:T(8,128)(2,1)}) custom-call(s32[1,64]{1,0:T(1,128)} %bitcast.22, s32[1,32]{1,0:T(1,128)} %bitcast.24, s32[1,64]{1,0:T(1,128)} %bitcast.26, f32[28,128]{1,0:T(8,128)} %bitcast.16, bf16[256,3584]{1,0:T(8,128)(2,1)} %bitcast.28), custom_call_target="tpu_custom_call" | custom-call | flops 1 | bytes 1 | tf_op jit(solution)/shard_map/norm_and_pack/pallas_call | solution.py:505
  3.6 0.5 collective-permute-start
  4.2 0.1 collective-permute-start.1
  4.2 0.4 collective-permute-start.2
  4.7 4.7 %collective-permute-start.6 = (bf16[32,1792]{1,0:T(8,128)(2,1)}, bf16[32,1792]{1,0:T(8,128)(2,1)S(1)}, u32[]{:S(2)}, u32[]{:S(2)}) collective-permute-start(bf16[32,1792]{1,0:T(8,128)(2,1)} %get-tuple-element.74), channel_id=1, source_target_pairs={{0,12},{4,8},{8,4},{12,0},{1,13},{5,9},{9,5},{13,1},{2,14},{6,10},... | collective-permute-start | bytes 344072 | tf_op jit(solution)/shard_map/ppermute | solution.py:428
  9.4 2.5 %collective-permute-start.8 = (bf16[32,1792]{1,0:T(8,128)(2,1)}, bf16[32,1792]{1,0:T(8,128)(2,1)S(1)}, u32[]{:S(2)}, u32[]{:S(2)}) collective-permute-start(bf16[32,1792]{1,0:T(8,128)(2,1)} %get-tuple-element.72), channel_id=1, source_target_pairs={{0,4},{4,0},{8,12},{12,8},{1,5},{5,1},{9,13},{13,9},{2,6},{6,2},{1... | collective-permute-start | bytes 344072 | tf_op jit(solution)/shard_map/ppermute | solution.py:428
  11.9 0.0 copy-start.8
  12.0 0.0 copy-start.5
  12.0 8.6 %norm_pack_project.1 = (bf16[256,3584]{1,0:T(8,128)(2,1)S(1)}, f32[256,1024]{1,0:T(8,128)S(1)}, s32[8,64]{1,0:T(8,128)S(1)}, bf16[32,1792]{1,0:T(8,128)(2,1)S(1)...) custom-call(s32[1,64]{1,0:T(1,128)S(1)} %bitcast.23, ...), custom_call_target="tpu_custom_call" | custom-call | flops 1 | bytes 1 | tf_op jit(solution)/shard_map/norm_pack_project/pallas_call | solution.py:541
  20.6 2.5 %collective-permute-start.3 = (bf16[32,1792]{1,0:T(8,128)(2,1)S(1)}, bf16[32,1792]{1,0:T(8,128)(2,1)S(1)}, u32[]{:S(2)}, u32[]{:S(2)}) collective-permute-start(bf16[32,1792]{1,0:T(8,128)(2,1)S(1)} %get-tuple-element.82), channel_id=1, source_target_pairs={{0,12},{4,8},{8,4},{12,0},{1,13},{5,9},{9,5},{13,1},{2,14},{6,10},... | collective-permute-start | bytes 344072 | tf_op jit(solution)/shard_map/ppermute | solution.py:428
  23.1 0.2 collective-permute-start.4
  23.3 1.7 %collective-permute-start.5 = (bf16[32,1792]{1,0:T(8,128)(2,1)S(1)}, bf16[32,1792]{1,0:T(8,128)(2,1)S(1)}, u32[]{:S(2)}, u32[]{:S(2)}) collective-permute-start(bf16[32,1792]{1,0:T(8,128)(2,1)S(1)} %get-tuple-element.84), channel_id=1, source_target_pairs={{0,4},{4,0},{8,12},{12,8},{1,5},{5,1},{9,13},{13,9},{2,6},{6,2},{1... | collective-permute-start | bytes 344072 | tf_op jit(solution)/shard_map/ppermute | solution.py:428
  25.1 1.2 %down.2.refs_0_ = f32[128,128]{1,0:T(8,128)S(1)} custom-call(bf16[32,1792]{1,0:T(8,128)(2,1)S(1)} %collective-permute-done.6.refs_0_, bf16[32,1792]{1,0:T(8,128)(2,1)S(1)} %collective-permute-done.7.refs_1_, bf16[32,1792]{1,0:T(8,128)(2,1)S(1)} %collective-permute-done.8.refs_2_, bf16[32,1792]{1,0:T(8,128)(2,1)S(1)} %copy-done.5, ...), custom_call_target="tpu_custom_call" | custom-call | flops 1 | bytes 1 | tf_op jit(solution)/shard_map/down/pallas_call | solution.py:573
  26.3 1.6 %collective-permute-start.9 = (f32[128,128]{1,0:T(8,128)S(1)}, f32[128,128]{1,0:T(8,128)S(1)}, u32[]{:S(2)}, u32[]{:S(2)}) collective-permute-start(f32[128,128]{1,0:T(8,128)S(1)} %down.2.refs_0_), channel_id=1, source_target_pairs={{0,2},{2,0},{1,3},{3,1},{4,6},{6,4},{5,7},{7,5},{8,10},{10,8},{9,1... | collective-permute-start | bytes 196616 | tf_op jit(solution)/shard_map/ppermute | solution.py:437
  27.8 2.8 %collective-permute-done.9.refs_1_ = f32[128,128]{1,0:T(8,128)S(1)} collective-permute-done((f32[128,128]{1,0:T(8,128)S(1)}, f32[128,128]{1,0:T(8,128)S(1)}, u32[]{:S(2)}, u32[]{:S(2)}) %collective-permute-start.9) | collective-permute-done | bytes 65568 | tf_op jit(solution)/shard_map/ppermute | solution.py:437
  30.6 0.5 up.2
  31.1 2.9 %collective-permute-done.4.refs_1_ = bf16[32,1792]{1,0:T(8,128)(2,1)S(1)} collective-permute-done((bf16[32,1792]{1,0:T(8,128)(2,1)S(1)}, bf16[32,1792]{1,0:T(8,128)(2,1)S(1)}, u32[]{:S(2)}, u32[]{:S(2)}) %collective-permute-start.4) | collective-permute-done | bytes 114720 | tf_op jit(solution)/shard_map/ppermute | solution.py:428
  34.0 3.2 %collective-permute-start.13 = (bf16[32,2048]{1,0:T(8,128)(2,1)S(1)}, bf16[32,2048]{1,0:T(8,128)(2,1)S(1)}, u32[]{:S(2)}, u32[]{:S(2)}) collective-permute-start(bf16[32,2048]{1,0:T(8,128)(2,1)S(1)} %get-tuple-element.99), channel_id=1, source_target_pairs={{0,8},{4,12},{8,0},{12,4},{1,9},{5,13},{9,1},{13,5},{2,10},{6,14},... | collective-permute-start | bytes 393224 | tf_op jit(solution)/shard_map/ppermute | solution.py:428
  37.2 1.2 %collective-permute-start.11 = (bf16[32,2048]{1,0:T(8,128)(2,1)S(1)}, bf16[32,2048]{1,0:T(8,128)(2,1)S(1)}, u32[]{:S(2)}, u32[]{:S(2)}) collective-permute-start(bf16[32,2048]{1,0:T(8,128)(2,1)S(1)} %get-tuple-element.96), channel_id=1, source_target_pairs={{0,12},{4,8},{8,4},{12,0},{1,13},{5,9},{9,5},{13,1},{2,14},{6,10},... | collective-permute-start | bytes 393224 | tf_op jit(solution)/shard_map/ppermute | solution.py:428
  38.4 0.1 compare_select_fusion
  38.4 1.1 %down.3.refs_0_ = f32[128,128]{1,0:T(8,128)S(1)} custom-call(bf16[32,1792]{1,0:T(8,128)(2,1)S(1)} %collective-permute-done.3.refs_0_, bf16[32,1792]{1,0:T(8,128)(2,1)S(1)} %collective-permute-done.4.refs_1_, bf16[32,1792]{1,0:T(8,128)(2,1)S(1)} %collective-permute-done.5.refs_2_, bf16[32,1792]{1,0:T(8,128)(2,1)S(1)} %get-tuple-element.92.refs_3_, ...), custom_call_target="tpu_custom_call" | custom-call | flops 1 | bytes 1 | tf_op jit(solution)/shard_map/down/pallas_call | solution.py:573
  39.6 1.6 %collective-permute-start.10 = (f32[128,128]{1,0:T(8,128)S(1)}, f32[128,128]{1,0:T(8,128)S(1)}, u32[]{:S(2)}, u32[]{:S(2)}) collective-permute-start(f32[128,128]{1,0:T(8,128)S(1)} %down.3.refs_0_), channel_id=1, source_target_pairs={{0,2},{2,0},{1,3},{3,1},{4,6},{6,4},{5,7},{7,5},{8,10},{10,8},{9,1... | collective-permute-start | bytes 196616 | tf_op jit(solution)/shard_map/ppermute | solution.py:437
  41.1 0.1 add_convert_fusion
  41.2 6.6 %project.1.refs_7_ = f32[256,1280]{1,0:T(8,128)S(1)} custom-call(bf16[256,3584]{1,0:T(8,128)(2,1)S(1)} %get-tuple-element.81.rows_ref, f32[18,128]{1,0:T(8,128)S(1)} %bitcast.19, bf16[3584,2304]{1,0:T(8,128)(2,1)} %weight_hbm.1), custom_call_target="tpu_custom_call" | custom-call | flops 1 | bytes 1 | tf_op jit(solution)/shard_map/project/pallas_call | solution.py:561
  47.8 0.5 up.3
  48.4 0.5 collective-permute-start.16
  48.9 2.8 %collective-permute-start.14 = (bf16[32,2048]{1,0:T(8,128)(2,1)S(1)}, bf16[32,2048]{1,0:T(8,128)(2,1)S(1)}, u32[]{:S(2)}, u32[]{:S(2)}) collective-permute-start(bf16[32,2048]{1,0:T(8,128)(2,1)S(1)} %get-tuple-element.100), channel_id=1, source_target_pairs={{0,8},{4,12},{8,0},{12,4},{1,9},{5,13},{9,1},{13,5},{2,10},{6,14},... | collective-permute-start | bytes 393224 | tf_op jit(solution)/shard_map/ppermute | solution.py:428
  51.6 1.2 %collective-permute-start.12 = (bf16[32,2048]{1,0:T(8,128)(2,1)S(1)}, bf16[32,2048]{1,0:T(8,128)(2,1)S(1)}, u32[]{:S(2)}, u32[]{:S(2)}) collective-permute-start(bf16[32,2048]{1,0:T(8,128)(2,1)S(1)} %get-tuple-element.97), channel_id=1, source_target_pairs={{0,12},{4,8},{8,4},{12,0},{1,13},{5,9},{9,5},{13,1},{2,14},{6,10},... | collective-permute-start | bytes 393224 | tf_op jit(solution)/shard_map/ppermute | solution.py:428
  52.8 0.5 fusion
  53.4 4.1 %attend.2 = (f32[128,512]{1,0:T(8,128)S(1)}, bf16[32,1792]{1,0:T(8,128)(2,1)S(1)}, bf16[32,1792]{1,0:T(8,128)(2,1)S(1)}, bf16[32,1792]{1,0:T(8,128)(2,1)S(1)}, b...) custom-call(s32[8,64]{1,0:T(8,128)S(1)} %get-tuple-element.105.refs_, ...), custom_call_target="tpu_custom_call" | custom-call | flops 1 | bytes 1 | tf_op jit(solution)/shard_map/attend/pallas_call | solution.py:627
  57.5 2.8 %collective-permute-done.14.refs_9_ = bf16[32,2048]{1,0:T(8,128)(2,1)S(1)} collective-permute-done((bf16[32,2048]{1,0:T(8,128)(2,1)S(1)}, bf16[32,2048]{1,0:T(8,128)(2,1)S(1)}, u32[]{:S(2)}, u32[]{:S(2)}) %collective-permute-start.14) | collective-permute-done | bytes 131104 | tf_op jit(solution)/shard_map/ppermute | solution.py:428
  60.3 3.0 %collective-permute-start.19 = (bf16[32,1792]{1,0:T(8,128)(2,1)S(1)}, bf16[32,1792]{1,0:T(8,128)(2,1)S(1)}, u32[]{:S(2)}, u32[]{:S(2)}) collective-permute-start(bf16[32,1792]{1,0:T(8,128)(2,1)S(1)} %get-tuple-element.113), channel_id=1, source_target_pairs={{0,8},{1,9},{4,12},{5,13},{8,0},{9,1},{12,4},{13,5},{2,10},{3,11},... | collective-permute-start | bytes 344072 | tf_op jit(solution)/shard_map/ppermute | solution.py:681
  63.3 1.3 %collective-permute-start.26 = (bf16[32,1792]{1,0:T(8,128)(2,1)S(1)}, bf16[32,1792]{1,0:T(8,128)(2,1)S(1)}, u32[]{:S(2)}, u32[]{:S(2)}) collective-permute-start(bf16[32,1792]{1,0:T(8,128)(2,1)S(1)} %get-tuple-element.128), channel_id=1, source_target_pairs={{0,12},{1,13},{4,8},{5,9},{8,4},{9,5},{12,0},{13,1},{2,14},{3,15},... | collective-permute-start | bytes 344072 | tf_op jit(solution)/shard_map/ppermute | solution.py:681
  64.6 2.0 %collective-permute-start.23 = (bf16[32,1792]{1,0:T(8,128)(2,1)S(1)}, bf16[32,1792]{1,0:T(8,128)(2,1)S(1)}, u32[]{:S(2)}, u32[]{:S(2)}) collective-permute-start(bf16[32,1792]{1,0:T(8,128)(2,1)S(1)} %get-tuple-element.122), channel_id=1, source_target_pairs={{0,13},{1,12},{4,9},{5,8},{8,5},{9,4},{12,1},{13,0},{2,15},{3,14},... | collective-permute-start | bytes 344072 | tf_op jit(solution)/shard_map/ppermute | solution.py:681
  66.6 3.9 %attend.3 = (bf16[32,1792]{1,0:T(8,128)(2,1)S(1)}, bf16[32,1792]{1,0:T(8,128)(2,1)S(1)}, bf16[32,1792]{1,0:T(8,128)(2,1)S(1)}, bf16[32,1792]{1,0:T(8,128)(2,1)S(...) custom-call(s32[8,64]{1,0:T(8,128)S(1)} %get-tuple-element.105.refs_, ...), custom_call_target="tpu_custom_call" | custom-call | flops 1 | bytes 1 | tf_op jit(solution)/shard_map/attend/pallas_call | solution.py:627
  70.5 5.1 %collective-permute-start.20 = (bf16[32,1792]{1,0:T(8,128)(2,1)S(1)}, bf16[32,1792]{1,0:T(8,128)(2,1)S(1)}, u32[]{:S(2)}, u32[]{:S(2)}) collective-permute-start(bf16[32,1792]{1,0:T(8,128)(2,1)S(1)} %get-tuple-element.114), channel_id=1, source_target_pairs={{0,12},{1,13},{4,8},{5,9},{8,4},{9,5},{12,0},{13,1},{2,14},{3,15},... | collective-permute-start | bytes 344072 | tf_op jit(solution)/shard_map/ppermute | solution.py:681
  75.6 4.4 %collective-permute-done.17.refs_10_ = bf16[32,1792]{1,0:T(8,128)(2,1)S(1)} collective-permute-done((bf16[32,1792]{1,0:T(8,128)(2,1)S(1)}, bf16[32,1792]{1,0:T(8,128)(2,1)S(1)}, u32[]{:S(2)}, u32[]{:S(2)}) %collective-permute-start.17) | collective-permute-done | bytes 114720 | tf_op jit(solution)/shard_map/ppermute | solution.py:681
  79.9 0.4 collective-permute-start.18
  80.3 0.5 collective-permute-start.27
  80.8 7.0 %collective-permute-start.24 = (bf16[32,1792]{1,0:T(8,128)(2,1)S(1)}, bf16[32,1792]{1,0:T(8,128)(2,1)S(1)}, u32[]{:S(2)}, u32[]{:S(2)}) collective-permute-start(bf16[32,1792]{1,0:T(8,128)(2,1)S(1)} %get-tuple-element.123), channel_id=1, source_target_pairs={{0,4},{1,5},{4,0},{5,1},{8,12},{9,13},{12,8},{13,9},{2,6},{3,7},{6... | collective-permute-start | bytes 344072 | tf_op jit(solution)/shard_map/ppermute | solution.py:681
  87.8 0.2 collective-permute-start.22
  88.0 0.4 collective-permute-start.30
  88.4 4.4 %collective-permute-start.29 = (bf16[32,1792]{1,0:T(8,128)(2,1)S(1)}, bf16[32,1792]{1,0:T(8,128)(2,1)S(1)}, u32[]{:S(2)}, u32[]{:S(2)}) collective-permute-start(bf16[32,1792]{1,0:T(8,128)(2,1)S(1)} %get-tuple-element.132), channel_id=1, source_target_pairs={{0,4},{1,5},{4,0},{5,1},{8,12},{9,13},{12,8},{13,9},{2,6},{3,7},{6... | collective-permute-start | bytes 344072 | tf_op jit(solution)/shard_map/ppermute | solution.py:681
  92.9 3.1 %collective-permute-start.25 = (bf16[32,1792]{1,0:T(8,128)(2,1)S(1)}, bf16[32,1792]{1,0:T(8,128)(2,1)S(1)}, u32[]{:S(2)}, u32[]{:S(2)}) collective-permute-start(bf16[32,1792]{1,0:T(8,128)(2,1)S(1)} %get-tuple-element.124), channel_id=1, source_target_pairs={{0,8},{1,9},{4,12},{5,13},{8,0},{9,1},{12,4},{13,5},{2,10},{3,11},... | collective-permute-start | bytes 344072 | tf_op jit(solution)/shard_map/ppermute | solution.py:681
  96.0 1.0 collective-permute-done.22.refs_2_
  97.0 3.3 %collective-permute-done.29.refs_5_ = bf16[32,1792]{1,0:T(8,128)(2,1)S(1)} collective-permute-done((bf16[32,1792]{1,0:T(8,128)(2,1)S(1)}, bf16[32,1792]{1,0:T(8,128)(2,1)S(1)}, u32[]{:S(2)}, u32[]{:S(2)}) %collective-permute-start.29) | collective-permute-done | bytes 114720 | tf_op jit(solution)/shard_map/ppermute | solution.py:681
  100.2 1.7 %collective-permute-done.28.refs_4_ = bf16[32,1792]{1,0:T(8,128)(2,1)S(1)} collective-permute-done((bf16[32,1792]{1,0:T(8,128)(2,1)S(1)}, bf16[32,1792]{1,0:T(8,128)(2,1)S(1)}, u32[]{:S(2)}, u32[]{:S(2)}) %collective-permute-start.28) | collective-permute-done | bytes 114720 | tf_op jit(solution)/shard_map/ppermute | solution.py:681
  101.9 1.9 %place.1 = bf16[128,4,1792]{2,1,0:T(4,128)(2,1)} custom-call(bf16[32,1792]{1,0:T(8,128)(2,1)S(1)} %collective-permute-done.18.refs_0_, bf16[32,1792]{1,0:T(8,128)(2,1)S(1)} %collective-permute-done.20.refs_1_, bf16[32,1792]{1,0:T(8,128)(2,1)S(1)} %collective-permute-done.22.refs_2_, bf16[32,1792]{1,0:T(8,128)(2,1)S(1)} %collective-permute-done.25.refs_3_, ...), custom_call_target="tpu_custom_call" | custom-call | flops 1 | bytes 1 | tf_op jit(solution)/shard_map/place/pallas_call | solution.py:686
  (53 shorter events, 0.1 us)
Async XLA Ops:
  0.0 11.9 %copy-start.9 = (s32[64,1]{0,1:T(1,128)S(1)}, s32[64,1]{0,1:T(1,128)}, u32[]{:S(2)}) copy-start(s32[64,1]{0,1:T(1,128)} %param.17) | copy-start | bytes 772
  0.0 11.9 %copy-start.10 = (s32[32]{0:T(128)S(1)}, s32[32]{0:T(128)}, u32[]{:S(2)}) copy-start(s32[32]{0:T(128)} %param.18) | copy-start | bytes 388
  0.0 11.9 %copy-start.11 = (s32[64,1]{0,1:T(1,128)S(1)}, s32[64,1]{0,1:T(1,128)}, u32[]{:S(2)}) copy-start(s32[64,1]{0,1:T(1,128)} %param.25) | copy-start | bytes 772
  0.0 11.9 %copy-start.6 = (f32[3584]{0:T(1024)S(1)}, f32[3584]{0:T(1024)}, u32[]{:S(2)}) copy-start(f32[3584]{0:T(1024)} %param.14) | copy-start | bytes 43012
  0.0 3.6 %copy-start = (bf16[4,1792,128]{2,1,0:T(8,128)(2,1)S(1)}, bf16[4,1792,128]{2,1,0:T(8,128)(2,1)}, u32[]{:S(2)}) copy-start(bf16[4,1792,128]{2,1,0:T(8,128)(2,1)} %refs_4_.3) | copy-start | bytes 5505028
  0.0 11.9 %copy-start.7 = (f32[2304]{0:T(1024)S(1)}, f32[2304]{0:T(1024)}, u32[]{:S(2)}) copy-start(f32[2304]{0:T(1024)} %param.16) | copy-start | bytes 27652
  3.6 8.3 %collective-permute-start = (bf16[4,1792,128]{2,1,0:T(8,128)(2,1)S(1)}, bf16[4,1792,128]{2,1,0:T(8,128)(2,1)S(1)}, u32[]{:S(2)}, u32[]{:S(2)}) collective-permute-start(bf16[4,1792,128]{2,1,0:T(8,128)(2,1)S(1)} %copy-done), channel_id=1, source_target_pairs={{0,1},{1,0},{2,3},{3,2},{4,5},{5,4},{6,7},{7,6},{8,9},{9,8},{10,11... | collective-permute-start | bytes 5505032 | tf_op jit(solution)/shard_map/ppermute | solution.py:437
  4.2 7.7 %collective-permute-start.1 = (bf16[256,1792]{1,0:T(8,128)(2,1)}, bf16[256,1792]{1,0:T(8,128)(2,1)S(1)}, u32[]{:S(2)}, u32[]{:S(2)}) collective-permute-start(bf16[256,1792]{1,0:T(8,128)(2,1)} %bitcast.10), channel_id=1, source_target_pairs={{0,1},{1,0},{2,3},{3,2},{4,5},{5,4},{6,7},{7,6},{8,9},{9,8},{10,11... | collective-permute-start | bytes 2752520 | tf_op jit(solution)/shard_map/ppermute | solution.py:437
  4.2 5.1 %collective-permute-start.2 = (bf16[256,256]{1,0:T(8,128)(2,1)}, bf16[256,256]{1,0:T(8,128)(2,1)S(1)}, u32[]{:S(2)}, u32[]{:S(2)}) collective-permute-start(bf16[256,256]{1,0:T(8,128)(2,1)} %bitcast.13), channel_id=1, source_target_pairs={{0,1},{1,0},{2,3},{3,2},{4,5},{5,4},{6,7},{7,6},{8,9},{9,8},{10,11... | collective-permute-start | bytes 393224 | tf_op jit(solution)/shard_map/ppermute | solution.py:437
  4.7 18.6 %collective-permute-start.6 = (bf16[32,1792]{1,0:T(8,128)(2,1)}, bf16[32,1792]{1,0:T(8,128)(2,1)S(1)}, u32[]{:S(2)}, u32[]{:S(2)}) collective-permute-start(bf16[32,1792]{1,0:T(8,128)(2,1)} %get-tuple-element.74), channel_id=1, source_target_pairs={{0,12},{4,8},{8,4},{12,0},{1,13},{5,9},{9,5},{13,1},{2,14},{6,10},... | collective-permute-start | bytes 344072 | tf_op jit(solution)/shard_map/ppermute | solution.py:428
  9.3 15.7 %collective-permute-start.7 = (bf16[32,1792]{1,0:T(8,128)(2,1)}, bf16[32,1792]{1,0:T(8,128)(2,1)S(1)}, u32[]{:S(2)}, u32[]{:S(2)}) collective-permute-start(bf16[32,1792]{1,0:T(8,128)(2,1)} %get-tuple-element.73), channel_id=1, source_target_pairs={{0,8},{4,12},{8,0},{12,4},{1,9},{5,13},{9,1},{13,5},{2,10},{6,14},... | collective-permute-start | bytes 344072 | tf_op jit(solution)/shard_map/ppermute | solution.py:428
  9.4 15.7 %collective-permute-start.8 = (bf16[32,1792]{1,0:T(8,128)(2,1)}, bf16[32,1792]{1,0:T(8,128)(2,1)S(1)}, u32[]{:S(2)}, u32[]{:S(2)}) collective-permute-start(bf16[32,1792]{1,0:T(8,128)(2,1)} %get-tuple-element.72), channel_id=1, source_target_pairs={{0,4},{4,0},{8,12},{12,8},{1,5},{5,1},{9,13},{13,9},{2,6},{6,2},{1... | collective-permute-start | bytes 344072 | tf_op jit(solution)/shard_map/ppermute | solution.py:428
  11.9 13.1 %copy-start.8 = (s32[64]{0:T(128)S(1)}, s32[64]{0:T(128)}, u32[]{:S(2)}) copy-start(s32[64]{0:T(128)} %param.19) | copy-start | bytes 772
  12.0 13.1 %copy-start.5 = (bf16[32,1792]{1,0:T(8,128)(2,1)S(1)}, bf16[32,1792]{1,0:T(8,128)(2,1)}, u32[]{:S(2)}) copy-start(bf16[32,1792]{1,0:T(8,128)(2,1)} %get-tuple-element.86.refs_3_) | copy-start | bytes 344068
  20.6 10.5 %collective-permute-start.3 = (bf16[32,1792]{1,0:T(8,128)(2,1)S(1)}, bf16[32,1792]{1,0:T(8,128)(2,1)S(1)}, u32[]{:S(2)}, u32[]{:S(2)}) collective-permute-start(bf16[32,1792]{1,0:T(8,128)(2,1)S(1)} %get-tuple-element.82), channel_id=1, source_target_pairs={{0,12},{4,8},{8,4},{12,0},{1,13},{5,9},{9,5},{13,1},{2,14},{6,10},... | collective-permute-start | bytes 344072 | tf_op jit(solution)/shard_map/ppermute | solution.py:428
  23.1 10.9 %collective-permute-start.4 = (bf16[32,1792]{1,0:T(8,128)(2,1)S(1)}, bf16[32,1792]{1,0:T(8,128)(2,1)S(1)}, u32[]{:S(2)}, u32[]{:S(2)}) collective-permute-start(bf16[32,1792]{1,0:T(8,128)(2,1)S(1)} %get-tuple-element.83), channel_id=1, source_target_pairs={{0,8},{4,12},{8,0},{12,4},{1,9},{5,13},{9,1},{13,5},{2,10},{6,14},... | collective-permute-start | bytes 344072 | tf_op jit(solution)/shard_map/ppermute | solution.py:428
  23.3 10.7 %collective-permute-start.5 = (bf16[32,1792]{1,0:T(8,128)(2,1)S(1)}, bf16[32,1792]{1,0:T(8,128)(2,1)S(1)}, u32[]{:S(2)}, u32[]{:S(2)}) collective-permute-start(bf16[32,1792]{1,0:T(8,128)(2,1)S(1)} %get-tuple-element.84), channel_id=1, source_target_pairs={{0,4},{4,0},{8,12},{12,8},{1,5},{5,1},{9,13},{13,9},{2,6},{6,2},{1... | collective-permute-start | bytes 344072 | tf_op jit(solution)/shard_map/ppermute | solution.py:428
  25.0 5.5 %copy-start.3 = (bf16[4,64,1792]{2,1,0:T(8,128)(2,1)S(1)}, bf16[4,64,1792]{2,1,0:T(8,128)(2,1)}, u32[]{:S(2)}) copy-start(bf16[4,64,1792]{2,1,0:T(8,128)(2,1)} %param.23) | copy-start | bytes 2752516
  25.0 5.5 %copy-start.4 = (bf16[4,64,256]{2,1,0:T(8,128)(2,1)S(1)}, bf16[4,64,256]{2,1,0:T(8,128)(2,1)}, u32[]{:S(2)}) copy-start(bf16[4,64,256]{2,1,0:T(8,128)(2,1)} %param.24) | copy-start | bytes 393220
  26.3 4.3 %collective-permute-start.9 = (f32[128,128]{1,0:T(8,128)S(1)}, f32[128,128]{1,0:T(8,128)S(1)}, u32[]{:S(2)}, u32[]{:S(2)}) collective-permute-start(f32[128,128]{1,0:T(8,128)S(1)} %down.2.refs_0_), channel_id=1, source_target_pairs={{0,2},{2,0},{1,3},{3,1},{4,6},{6,4},{5,7},{7,5},{8,10},{10,8},{9,1... | collective-permute-start | bytes 196616 | tf_op jit(solution)/shard_map/ppermute | solution.py:437
  34.0 14.3 %collective-permute-start.15 = (bf16[32,2048]{1,0:T(8,128)(2,1)S(1)}, bf16[32,2048]{1,0:T(8,128)(2,1)S(1)}, u32[]{:S(2)}, u32[]{:S(2)}) collective-permute-start(bf16[32,2048]{1,0:T(8,128)(2,1)S(1)} %get-tuple-element.102), channel_id=1, source_target_pairs={{0,4},{4,0},{8,12},{12,8},{1,5},{5,1},{9,13},{13,9},{2,6},{6,2},{1... | collective-permute-start | bytes 393224 | tf_op jit(solution)/shard_map/ppermute | solution.py:428
  34.0 14.4 %collective-permute-start.13 = (bf16[32,2048]{1,0:T(8,128)(2,1)S(1)}, bf16[32,2048]{1,0:T(8,128)(2,1)S(1)}, u32[]{:S(2)}, u32[]{:S(2)}) collective-permute-start(bf16[32,2048]{1,0:T(8,128)(2,1)S(1)} %get-tuple-element.99), channel_id=1, source_target_pairs={{0,8},{4,12},{8,0},{12,4},{1,9},{5,13},{9,1},{13,5},{2,10},{6,14},... | collective-permute-start | bytes 393224 | tf_op jit(solution)/shard_map/ppermute | solution.py:428
  37.2 11.2 %collective-permute-start.11 = (bf16[32,2048]{1,0:T(8,128)(2,1)S(1)}, bf16[32,2048]{1,0:T(8,128)(2,1)S(1)}, u32[]{:S(2)}, u32[]{:S(2)}) collective-permute-start(bf16[32,2048]{1,0:T(8,128)(2,1)S(1)} %get-tuple-element.96), channel_id=1, source_target_pairs={{0,12},{4,8},{8,4},{12,0},{1,13},{5,9},{9,5},{13,1},{2,14},{6,10},... | collective-permute-start | bytes 393224 | tf_op jit(solution)/shard_map/ppermute | solution.py:428
  39.6 8.2 %collective-permute-start.10 = (f32[128,128]{1,0:T(8,128)S(1)}, f32[128,128]{1,0:T(8,128)S(1)}, u32[]{:S(2)}, u32[]{:S(2)}) collective-permute-start(f32[128,128]{1,0:T(8,128)S(1)} %down.3.refs_0_), channel_id=1, source_target_pairs={{0,2},{2,0},{1,3},{3,1},{4,6},{6,4},{5,7},{7,5},{8,10},{10,8},{9,1... | collective-permute-start | bytes 196616 | tf_op jit(solution)/shard_map/ppermute | solution.py:437
  47.8 5.6 %copy-start.1 = (bf16[64,32,256]{2,1,0:T(8,128)(2,1)S(1)}, bf16[64,32,256]{2,1,0:T(8,128)(2,1)}, u32[]{:S(2)}) copy-start(bf16[64,32,256]{2,1,0:T(8,128)(2,1)} %refs_4_.5) | copy-start | bytes 3145732
  47.8 5.6 %copy-start.2 = (bf16[64,32,256]{2,1,0:T(8,128)(2,1)S(1)}, bf16[64,32,256]{2,1,0:T(8,128)(2,1)}, u32[]{:S(2)}) copy-start(bf16[64,32,256]{2,1,0:T(8,128)(2,1)} %refs_5_.3) | copy-start | bytes 3145732
  48.4 9.1 %collective-permute-start.16 = (bf16[32,2048]{1,0:T(8,128)(2,1)S(1)}, bf16[32,2048]{1,0:T(8,128)(2,1)S(1)}, u32[]{:S(2)}, u32[]{:S(2)}) collective-permute-start(bf16[32,2048]{1,0:T(8,128)(2,1)S(1)} %get-tuple-element.103), channel_id=1, source_target_pairs={{0,4},{4,0},{8,12},{12,8},{1,5},{5,1},{9,13},{13,9},{2,6},{6,2},{1... | collective-permute-start | bytes 393224 | tf_op jit(solution)/shard_map/ppermute | solution.py:428
  48.9 11.4 %collective-permute-start.14 = (bf16[32,2048]{1,0:T(8,128)(2,1)S(1)}, bf16[32,2048]{1,0:T(8,128)(2,1)S(1)}, u32[]{:S(2)}, u32[]{:S(2)}) collective-permute-start(bf16[32,2048]{1,0:T(8,128)(2,1)S(1)} %get-tuple-element.100), channel_id=1, source_target_pairs={{0,8},{4,12},{8,0},{12,4},{1,9},{5,13},{9,1},{13,5},{2,10},{6,14},... | collective-permute-start | bytes 393224 | tf_op jit(solution)/shard_map/ppermute | solution.py:428
  51.6 8.7 %collective-permute-start.12 = (bf16[32,2048]{1,0:T(8,128)(2,1)S(1)}, bf16[32,2048]{1,0:T(8,128)(2,1)S(1)}, u32[]{:S(2)}, u32[]{:S(2)}) collective-permute-start(bf16[32,2048]{1,0:T(8,128)(2,1)S(1)} %get-tuple-element.97), channel_id=1, source_target_pairs={{0,12},{4,8},{8,4},{12,0},{1,13},{5,9},{9,5},{13,1},{2,14},{6,10},... | collective-permute-start | bytes 393224 | tf_op jit(solution)/shard_map/ppermute | solution.py:428
  60.3 10.2 %collective-permute-start.19 = (bf16[32,1792]{1,0:T(8,128)(2,1)S(1)}, bf16[32,1792]{1,0:T(8,128)(2,1)S(1)}, u32[]{:S(2)}, u32[]{:S(2)}) collective-permute-start(bf16[32,1792]{1,0:T(8,128)(2,1)S(1)} %get-tuple-element.113), channel_id=1, source_target_pairs={{0,8},{1,9},{4,12},{5,13},{8,0},{9,1},{12,4},{13,5},{2,10},{3,11},... | collective-permute-start | bytes 344072 | tf_op jit(solution)/shard_map/ppermute | solution.py:681
  63.3 16.6 %collective-permute-start.17 = (bf16[32,1792]{1,0:T(8,128)(2,1)S(1)}, bf16[32,1792]{1,0:T(8,128)(2,1)S(1)}, u32[]{:S(2)}, u32[]{:S(2)}) collective-permute-start(bf16[32,1792]{1,0:T(8,128)(2,1)S(1)} %get-tuple-element.109), channel_id=1, source_target_pairs={{0,9},{1,8},{4,13},{5,12},{8,1},{9,0},{12,5},{13,4},{2,11},{3,10},... | collective-permute-start | bytes 344072 | tf_op jit(solution)/shard_map/ppermute | solution.py:681
  63.3 17.0 %collective-permute-start.26 = (bf16[32,1792]{1,0:T(8,128)(2,1)S(1)}, bf16[32,1792]{1,0:T(8,128)(2,1)S(1)}, u32[]{:S(2)}, u32[]{:S(2)}) collective-permute-start(bf16[32,1792]{1,0:T(8,128)(2,1)S(1)} %get-tuple-element.128), channel_id=1, source_target_pairs={{0,12},{1,13},{4,8},{5,9},{8,4},{9,5},{12,0},{13,1},{2,14},{3,15},... | collective-permute-start | bytes 344072 | tf_op jit(solution)/shard_map/ppermute | solution.py:681
  64.6 16.1 %collective-permute-start.23 = (bf16[32,1792]{1,0:T(8,128)(2,1)S(1)}, bf16[32,1792]{1,0:T(8,128)(2,1)S(1)}, u32[]{:S(2)}, u32[]{:S(2)}) collective-permute-start(bf16[32,1792]{1,0:T(8,128)(2,1)S(1)} %get-tuple-element.122), channel_id=1, source_target_pairs={{0,13},{1,12},{4,9},{5,8},{8,5},{9,4},{12,1},{13,0},{2,15},{3,14},... | collective-permute-start | bytes 344072 | tf_op jit(solution)/shard_map/ppermute | solution.py:681
  66.6 21.2 %collective-permute-start.21 = (bf16[32,1792]{1,0:T(8,128)(2,1)S(1)}, bf16[32,1792]{1,0:T(8,128)(2,1)S(1)}, u32[]{:S(2)}, u32[]{:S(2)}) collective-permute-start(bf16[32,1792]{1,0:T(8,128)(2,1)S(1)} %get-tuple-element.117), channel_id=1, source_target_pairs={{0,5},{1,4},{4,1},{5,0},{8,13},{9,12},{12,9},{13,8},{2,7},{3,6},{6... | collective-permute-start | bytes 344072 | tf_op jit(solution)/shard_map/ppermute | solution.py:681
  70.5 17.5 %collective-permute-start.20 = (bf16[32,1792]{1,0:T(8,128)(2,1)S(1)}, bf16[32,1792]{1,0:T(8,128)(2,1)S(1)}, u32[]{:S(2)}, u32[]{:S(2)}) collective-permute-start(bf16[32,1792]{1,0:T(8,128)(2,1)S(1)} %get-tuple-element.114), channel_id=1, source_target_pairs={{0,12},{1,13},{4,8},{5,9},{8,4},{9,5},{12,0},{13,1},{2,14},{3,15},... | collective-permute-start | bytes 344072 | tf_op jit(solution)/shard_map/ppermute | solution.py:681
  79.9 8.5 %collective-permute-start.18 = (bf16[32,1792]{1,0:T(8,128)(2,1)S(1)}, bf16[32,1792]{1,0:T(8,128)(2,1)S(1)}, u32[]{:S(2)}, u32[]{:S(2)}) collective-permute-start(bf16[32,1792]{1,0:T(8,128)(2,1)S(1)} %get-tuple-element.110), channel_id=1, source_target_pairs={{0,13},{1,12},{4,9},{5,8},{8,5},{9,4},{12,1},{13,0},{2,15},{3,14},... | collective-permute-start | bytes 344072 | tf_op jit(solution)/shard_map/ppermute | solution.py:681
  80.3 12.5 %collective-permute-start.27 = (bf16[32,1792]{1,0:T(8,128)(2,1)S(1)}, bf16[32,1792]{1,0:T(8,128)(2,1)S(1)}, u32[]{:S(2)}, u32[]{:S(2)}) collective-permute-start(bf16[32,1792]{1,0:T(8,128)(2,1)S(1)} %get-tuple-element.129), channel_id=1, source_target_pairs={{0,1},{1,0},{4,5},{5,4},{8,9},{9,8},{12,13},{13,12},{2,3},{3,2},{6... | collective-permute-start | bytes 344072 | tf_op jit(solution)/shard_map/ppermute | solution.py:681
  80.8 12.1 %collective-permute-start.24 = (bf16[32,1792]{1,0:T(8,128)(2,1)S(1)}, bf16[32,1792]{1,0:T(8,128)(2,1)S(1)}, u32[]{:S(2)}, u32[]{:S(2)}) collective-permute-start(bf16[32,1792]{1,0:T(8,128)(2,1)S(1)} %get-tuple-element.123), channel_id=1, source_target_pairs={{0,4},{1,5},{4,0},{5,1},{8,12},{9,13},{12,8},{13,9},{2,6},{3,7},{6... | collective-permute-start | bytes 344072 | tf_op jit(solution)/shard_map/ppermute | solution.py:681
  87.8 9.1 %collective-permute-start.22 = (bf16[32,1792]{1,0:T(8,128)(2,1)S(1)}, bf16[32,1792]{1,0:T(8,128)(2,1)S(1)}, u32[]{:S(2)}, u32[]{:S(2)}) collective-permute-start(bf16[32,1792]{1,0:T(8,128)(2,1)S(1)} %get-tuple-element.118), channel_id=1, source_target_pairs={{0,9},{1,8},{4,13},{5,12},{8,1},{9,0},{12,5},{13,4},{2,11},{3,10},... | collective-permute-start | bytes 344072 | tf_op jit(solution)/shard_map/ppermute | solution.py:681
  88.0 8.9 %collective-permute-start.30 = (bf16[32,1792]{1,0:T(8,128)(2,1)S(1)}, bf16[32,1792]{1,0:T(8,128)(2,1)S(1)}, u32[]{:S(2)}, u32[]{:S(2)}) collective-permute-start(bf16[32,1792]{1,0:T(8,128)(2,1)S(1)} %get-tuple-element.134), channel_id=1, source_target_pairs={{0,1},{1,0},{4,5},{5,4},{8,9},{9,8},{12,13},{13,12},{2,3},{3,2},{6... | collective-permute-start | bytes 344072 | tf_op jit(solution)/shard_map/ppermute | solution.py:681
  88.4 11.8 %collective-permute-start.29 = (bf16[32,1792]{1,0:T(8,128)(2,1)S(1)}, bf16[32,1792]{1,0:T(8,128)(2,1)S(1)}, u32[]{:S(2)}, u32[]{:S(2)}) collective-permute-start(bf16[32,1792]{1,0:T(8,128)(2,1)S(1)} %get-tuple-element.132), channel_id=1, source_target_pairs={{0,4},{1,5},{4,0},{5,1},{8,12},{9,13},{12,8},{13,9},{2,6},{3,7},{6... | collective-permute-start | bytes 344072 | tf_op jit(solution)/shard_map/ppermute | solution.py:681
  92.8 9.1 %collective-permute-start.28 = (bf16[32,1792]{1,0:T(8,128)(2,1)S(1)}, bf16[32,1792]{1,0:T(8,128)(2,1)S(1)}, u32[]{:S(2)}, u32[]{:S(2)}) collective-permute-start(bf16[32,1792]{1,0:T(8,128)(2,1)S(1)} %get-tuple-element.130), channel_id=1, source_target_pairs={{0,5},{1,4},{4,1},{5,0},{8,13},{9,12},{12,9},{13,8},{2,7},{3,6},{6... | collective-permute-start | bytes 344072 | tf_op jit(solution)/shard_map/ppermute | solution.py:681
  92.9 9.1 %collective-permute-start.25 = (bf16[32,1792]{1,0:T(8,128)(2,1)S(1)}, bf16[32,1792]{1,0:T(8,128)(2,1)S(1)}, u32[]{:S(2)}, u32[]{:S(2)}) collective-permute-start(bf16[32,1792]{1,0:T(8,128)(2,1)S(1)} %get-tuple-element.124), channel_id=1, source_target_pairs={{0,8},{1,9},{4,12},{5,13},{8,0},{9,1},{12,4},{13,5},{2,10},{3,11},... | collective-permute-start | bytes 344072 | tf_op jit(solution)/shard_map/ppermute | solution.py:681

commit v10 on v7

--- a/solution.py
+++ b/solution.py
@@ -50,7 +50,7 @@
 
 
 def norm_in_pieces(
-    pieces, begin, x_hbm, gain_hbm, x_buf, gain_buf, semaphores, normed_ref, started=None
+    pieces, begin, x_hbm, gain_hbm, x_buf, gain_buf, semaphores, normed_ref
 ):
     count, width = x_buf.shape
     size = count // pieces
@@ -67,8 +67,6 @@
         copies[-1].start()
         if piece == 0:
             gain_copy.start()
-    if started is not None:
-        started()
     gain_copy.wait()
     gain = jnp.concatenate([gain_buf[i : i + 1, :] for i in range(gain_buf.shape[0])], axis=1)
     for piece in range(pieces):
@@ -156,21 +154,13 @@
         )
 
 
-def norm_pack_project_kernel(steps, rows, flow_most, lanes, pieces, chunk, *refs):
-    table_hbms, bias_ref, gain_hbm, x_hbm, weight_hbm = refs[:3], *refs[3:7]
-    normed_ref, out_ref, places_ref, message_refs = *refs[7:10], refs[10 : 10 + lanes]
-    x_buf, gain_buf, *table_bufs, semaphores, weight_buf, weight_semaphores = refs[10 + lanes :]
-    copies = weight_copies(0, weight_hbm, weight_buf, weight_semaphores)
-    tables = table_copies(table_hbms, table_bufs, semaphores, pieces + 1)
-
-    def start_weights():
-        for copy in copies:
-            copy.start()
-
-    norm_in_pieces(
-        pieces, 0, x_hbm, gain_hbm, x_buf, gain_buf, semaphores, normed_ref, start_weights
-    )
-    for copy in tables:
+def norm_all_pack_kernel(steps, rows, flow_most, lanes, pieces, chunk, *refs):
+    table_hbms, gain_hbm, x_hbm = refs[:3], refs[3], refs[4]
+    normed_ref, places_ref, message_refs = refs[5], refs[6], refs[7 : 7 + lanes]
+    x_buf, gain_buf, *table_bufs, semaphores = refs[7 + lanes :]
+    copies = table_copies(table_hbms, table_bufs, semaphores, pieces + 1)
+    norm_in_pieces(pieces, 0, x_hbm, gain_hbm, x_buf, gain_buf, semaphores, normed_ref)
+    for copy in copies:
         copy.wait()
     spots = message_refs[0].shape[0] // steps
     places, flow_places = places_from(table_bufs, spots, flow_most)
@@ -179,7 +169,6 @@
     count = steps * rows
     own_ref = normed_ref.at[pl.ds(chunk * count, count)]
     pack_messages(steps, rows, places, own_ref, message_refs)
-    project_blocks(0, copies, normed_ref, weight_buf, bias_ref, out_ref)
 
 
 def project_kernel(begin, rows_ref, bias_ref, weight_hbm, out_ref, weight_buf, semaphores):
@@ -194,7 +183,7 @@
 
 
 def down_kernel(lanes, spots, *refs):
-    message_refs, map_refs, partial_ref = refs[:lanes], refs[lanes:-1], refs[-1]
+    message_refs, map_refs, partial_ref = refs[:lanes][::-1], refs[lanes:-1], refs[-1]
     local_slots = map_refs[0].shape[0]
     rows = jnp.concatenate([ref[...] for ref in message_refs], axis=0)
     own_slot = row_slots(partial_ref.shape, spots)
@@ -247,7 +236,7 @@
 
 def attend_kernel(before, steps, rows, cache, groups, lanes, subs, last, *refs):
     places_ref, length_ref, cos_ref, sin_ref, key_ref, value_ref = refs[:6]
-    qkv_refs, refs = refs[6:8], refs[8:]
+    qkv_refs, refs = refs[6:9], refs[9:]
     delta_refs, refs = refs[:lanes], refs[lanes:]
     if before:
         earlier_ref, refs = refs[0], refs[1:]
@@ -261,11 +250,8 @@
     known = before + steps
 
     def qkv_tile(span, group, head):
-        begin = (group * (PER_GROUP + 2) + head) * HEAD_WIDTH
-        edge = qkv_refs[0].shape[1]
-        if begin < edge:
-            return qkv_refs[0][span, begin : begin + HEAD_WIDTH]
-        return qkv_refs[1][span, begin - edge : begin - edge + HEAD_WIDTH]
+        part, begin = divmod((group * (PER_GROUP + 2) + head) * HEAD_WIDTH, qkv_refs[0].shape[1])
+        return qkv_refs[part][span, begin : begin + HEAD_WIDTH]
 
     wide = groups * HEAD_WIDTH
 
@@ -524,53 +510,46 @@
     )(*tables, gain, flat)
     arrived = [traded(messages, "streams")]
 
+    adapters = down_maps[1:], query_maps[1:], value_maps[1:]
+    normed, places, *messages = pl.pallas_call(
+        functools.partial(
+            norm_all_pack_kernel, chunk_steps, rows, flow_most, lanes, 2 * pieces, 1
+        ),
+        in_specs=[in_hbm] * 5,
+        out_specs=[VMEM] * (2 + lanes),
+        out_shape=[jax.ShapeDtypeStruct((steps * rows, width), bf16), places_shape]
+        + [message] * lanes,
+        scratch_shapes=row_buffers(steps * rows)[:-1]
+        + [pltpu.SemaphoreType.DMA((2 * pieces + 4,))],
+        compiler_params=pltpu.CompilerParams(vmem_limit_bytes=PROJECT_LIMIT * MIB),
+        cost_estimate=SMALL,
+        name="norm_and_pack_next",
+    )(*tables, held(gain, (adapters, messages)), flat)
+    arrived.append(traded(messages, "streams"))
+
     bias = projection_bias.reshape(-1, 128)
     columns = projection_weight.shape[1]
     block_columns = 256 if columns % 256 == 0 else 384
-    blocks = columns // block_columns
-    cut = blocks // 2
-
-    def weight_buffers(count):
-        return [
-            pltpu.VMEM((count, width, block_columns), bf16),
-            pltpu.SemaphoreType.DMA((count,)),
-        ]
-
-    def projected(count):
-        return jax.ShapeDtypeStruct((steps * rows, count * block_columns), f32)
-
-    adapters = down_maps[1:], query_maps[1:], value_maps[1:]
-    weight_buf, weight_semaphores = weight_buffers(cut)
-    normed, first_qkv, places, *messages = pl.pallas_call(
-        functools.partial(
-            norm_pack_project_kernel, chunk_steps, rows, flow_most, lanes, 2 * pieces, 1
-        ),
-        in_specs=[in_hbm] * 3 + [VMEM] + [in_hbm] * 3,
-        out_specs=[VMEM] * (3 + lanes),
-        out_shape=[jax.ShapeDtypeStruct((steps * rows, width), bf16), projected(cut)]
-        + [places_shape]
-        + [message] * lanes,
-        scratch_shapes=row_buffers(steps * rows)[:-1]
-        + [pltpu.SemaphoreType.DMA((2 * pieces + 4,))]
-        + [weight_buf, weight_semaphores],
-        compiler_params=pltpu.CompilerParams(vmem_limit_bytes=PROJECT_LIMIT * MIB),
-        cost_estimate=SMALL,
-        name="norm_pack_project",
-    )(*tables, held(bias, (adapters, messages)), gain, flat, projection_weight)
-    arrived.append(traded(messages, "streams"))
-    qkv = [first_qkv]
+    third = columns // block_columns // 3
+    qkv = []
 
     def project(after):
-        return pl.pallas_call(
-            functools.partial(project_kernel, cut),
-            in_specs=[VMEM, VMEM, in_hbm],
-            out_specs=VMEM,
-            out_shape=projected(blocks - cut),
-            scratch_shapes=weight_buffers(blocks - cut),
-            compiler_params=pltpu.CompilerParams(vmem_limit_bytes=PROJECT_LIMIT * MIB),
-            cost_estimate=SMALL,
-            name="project",
-        )(normed, held(bias, after), projection_weight)
+        begin = len(qkv) * third
+        qkv.append(
+            pl.pallas_call(
+                functools.partial(project_kernel, begin),
+                in_specs=[VMEM, VMEM, in_hbm],
+                out_specs=VMEM,
+                out_shape=jax.ShapeDtypeStruct((steps * rows, third * block_columns), f32),
+                scratch_shapes=[
+                    pltpu.VMEM((third, width, block_columns), bf16),
+                    pltpu.SemaphoreType.DMA((third,)),
+                ],
+                compiler_params=pltpu.CompilerParams(vmem_limit_bytes=PROJECT_LIMIT * MIB),
+                cost_estimate=SMALL,
+                name="project",
+            )(normed, held(bias, after), projection_weight)
+        )
 
     def down(chunk, after):
         partial_latent = pl.pallas_call(
@@ -581,7 +560,7 @@
             compiler_params=pltpu.CompilerParams(vmem_limit_bytes=16 * MIB),
             cost_estimate=SMALL,
             name="down",
-        )(held(arrived[chunk][0], after), *arrived[chunk][1:], *down_maps)
+        )(*arrived[chunk][:0:-1], held(arrived[chunk][0], after), *down_maps)
         return from_others(partial_latent, "heads")
 
     def up(partials, after):
@@ -607,11 +586,11 @@
     sine_part = jnp.sin(angle) * sign
 
     returned = []
+    project(messages)
     after = qkv
     for chunk in range(chunks):
         partials = down(chunk, after)
-        if chunk:
-            qkv.append(project(partials[0]))
+        project(partials[0])
         after = up(partials, qkv)
         messages = list(after)
         if chunk:

time: 105 us -> 103 us (0.981)
  the two profiles are of different devices: /device:TPU:0 before, /device:TPU:9 now
where the time goes in v10:
time: 103 us
  waiting for transfers between devices  39.7 us (39%)
  Pallas kernels  34.8 us (34%)
  starting transfers between devices  27.5 us (27%)
    ppermute x18, waiting for transfers between devices, traded(): landed[shift] = lax.ppermute(blocks[shift], axes, pairs)  38.6 us
    ppermute x18, starting transfers between devices, traded(): landed[shift] = lax.ppermute(blocks[shift], axes, pairs)  20.3 us
    pallas_call x3, Pallas kernels, project(): pl.pallas_call(functools.partial(project_kernel, begin), in_specs=[VMEM,...  13.3 us
    pallas_call x2, Pallas kernels, on_device(): pl.pallas_call(functools.partial(attend_kernel, chunk * chunk_steps, chun...  7.49 us
    pallas_call x1, Pallas kernels, on_device(): pl.pallas_call(functools.partial(norm_all_pack_kernel, chunk_steps, rows,...  5.27 us
    ppermute x4, starting transfers between devices, on_device(): landed.append(lax.ppermute(block_rows, 'sub', pairs))  3.83 us
    pallas_call x1, Pallas kernels, on_device(): pl.pallas_call(functools.partial(norm_pack_kernel, chunk_steps, rows, flo...  3.47 us
    ppermute x5, starting transfers between devices, from_others(): landed.append(lax.ppermute(block, axis, pairs))  2.85 us
  transfers between devices with their start and end apart: 28, of which 8 were waited for; matrix products, arithmetic and copies ran while one was open for 1% of the time, Pallas kernels for 32%

profile of v10, /device:TPU:9, one launch (start us, length us, event | category | flops | bytes accessed | tf_op | source)
XLA Modules:
  0.0 103.2 jit_solution(17408255151418709299)
XLA Ops:
  0.0 0.7 collective-permute-start
  0.8 0.1 collective-permute-start.1
  0.9 0.4 collective-permute-start.2
  1.3 3.5 %norm_and_pack.1 = (bf16[32,1792]{1,0:T(8,128)(2,1)}, bf16[32,1792]{1,0:T(8,128)(2,1)}, bf16[32,1792]{1,0:T(8,128)(2,1)}, bf16[32,1792]{1,0:T(8,128)(2,1)}) custom-call(s32[1,64]{1,0:T(1,128)} %bitcast.25, s32[1,32]{1,0:T(1,128)} %bitcast.27, s32[1,64]{1,0:T(1,128)} %bitcast.29, f32[28,128]{1,0:T(8,128)} %bitcast.21, bf16[256,3584]{1,0:T(8,128)(2,1)} %bitcast.10), custom_call_target="tpu_custom_call" | custom-call | flops 1 | bytes 1 | tf_op jit(solution)/shard_map/norm_and_pack/pallas_call | solution.py:501
  4.8 1.4 %collective-permute-start.6 = (bf16[32,1792]{1,0:T(8,128)(2,1)}, bf16[32,1792]{1,0:T(8,128)(2,1)S(1)}, u32[]{:S(2)}, u32[]{:S(2)}) collective-permute-start(bf16[32,1792]{1,0:T(8,128)(2,1)} %get-tuple-element.53), channel_id=1, source_target_pairs={{0,12},{4,8},{8,4},{12,0},{1,13},{5,9},{9,5},{13,1},{2,14},{6,10},... | collective-permute-start | bytes 344072 | tf_op jit(solution)/shard_map/ppermute | solution.py:416
  6.1 1.1 %collective-permute-start.7 = (bf16[32,1792]{1,0:T(8,128)(2,1)}, bf16[32,1792]{1,0:T(8,128)(2,1)S(1)}, u32[]{:S(2)}, u32[]{:S(2)}) collective-permute-start(bf16[32,1792]{1,0:T(8,128)(2,1)} %get-tuple-element.52), channel_id=1, source_target_pairs={{0,8},{4,12},{8,0},{12,4},{1,9},{5,13},{9,1},{13,5},{2,10},{6,14},... | collective-permute-start | bytes 344072 | tf_op jit(solution)/shard_map/ppermute | solution.py:416
  7.2 1.1 %collective-permute-start.8 = (bf16[32,1792]{1,0:T(8,128)(2,1)}, bf16[32,1792]{1,0:T(8,128)(2,1)S(1)}, u32[]{:S(2)}, u32[]{:S(2)}) collective-permute-start(bf16[32,1792]{1,0:T(8,128)(2,1)} %get-tuple-element.51), channel_id=1, source_target_pairs={{0,4},{4,0},{8,12},{12,8},{1,5},{5,1},{9,13},{13,9},{2,6},{6,2},{1... | collective-permute-start | bytes 344072 | tf_op jit(solution)/shard_map/ppermute | solution.py:416
  8.4 5.3 %norm_and_pack_next.1 = (bf16[256,3584]{1,0:T(8,128)(2,1)S(1)}, s32[8,64]{1,0:T(8,128)S(1)}, bf16[32,1792]{1,0:T(8,128)(2,1)S(1)}, bf16[32,1792]{1,0:T(8,128)(2,...) custom-call(s32[1,64]{1,0:T(1,128)S(1)} %bitcast.26, s32[1,32]{1,0:T(1,128)S(1)} %bitcast.28, ...), custom_call_target="tpu_custom_call" | custom-call | flops 1 | bytes 1 | tf_op jit(solution)/shard_map/norm_and_pack_next/pallas_call | solution.py:514
  13.7 1.3 %collective-permute-start.3 = (bf16[32,1792]{1,0:T(8,128)(2,1)S(1)}, bf16[32,1792]{1,0:T(8,128)(2,1)S(1)}, u32[]{:S(2)}, u32[]{:S(2)}) collective-permute-start(bf16[32,1792]{1,0:T(8,128)(2,1)S(1)} %get-tuple-element.56), channel_id=1, source_target_pairs={{0,12},{4,8},{8,4},{12,0},{1,13},{5,9},{9,5},{13,1},{2,14},{6,10},... | collective-permute-start | bytes 344072 | tf_op jit(solution)/shard_map/ppermute | solution.py:416
  14.9 1.3 %collective-permute-start.4 = (bf16[32,1792]{1,0:T(8,128)(2,1)S(1)}, bf16[32,1792]{1,0:T(8,128)(2,1)S(1)}, u32[]{:S(2)}, u32[]{:S(2)}) collective-permute-start(bf16[32,1792]{1,0:T(8,128)(2,1)S(1)} %get-tuple-element.57), channel_id=1, source_target_pairs={{0,8},{4,12},{8,0},{12,4},{1,9},{5,13},{9,1},{13,5},{2,10},{6,14},... | collective-permute-start | bytes 344072 | tf_op jit(solution)/shard_map/ppermute | solution.py:416
  16.2 4.5 %project.3.refs_6_ = f32[256,768]{1,0:T(8,128)S(1)} custom-call(bf16[256,3584]{1,0:T(8,128)(2,1)S(1)} %get-tuple-element.60.rows_ref, f32[18,128]{1,0:T(8,128)S(1)} %bitcast.18, bf16[3584,2304]{1,0:T(8,128)(2,1)} %weight_hbm.5), custom_call_target="tpu_custom_call" | custom-call | flops 1 | bytes 1 | tf_op jit(solution)/shard_map/project/pallas_call | solution.py:539
  20.7 1.2 %collective-permute-start.5 = (bf16[32,1792]{1,0:T(8,128)(2,1)S(1)}, bf16[32,1792]{1,0:T(8,128)(2,1)S(1)}, u32[]{:S(2)}, u32[]{:S(2)}) collective-permute-start(bf16[32,1792]{1,0:T(8,128)(2,1)S(1)} %get-tuple-element.58), channel_id=1, source_target_pairs={{0,4},{4,0},{8,12},{12,8},{1,5},{5,1},{9,13},{13,9},{2,6},{6,2},{1... | collective-permute-start | bytes 344072 | tf_op jit(solution)/shard_map/ppermute | solution.py:416
  21.9 1.2 %down.2.refs_0_ = f32[128,128]{1,0:T(8,128)S(1)} custom-call(bf16[32,1792]{1,0:T(8,128)(2,1)S(1)} %collective-permute-done.6.refs_0_, bf16[32,1792]{1,0:T(8,128)(2,1)S(1)} %collective-permute-done.7.refs_1_, bf16[32,1792]{1,0:T(8,128)(2,1)S(1)} %collective-permute-done.8.refs_2_, bf16[32,1792]{1,0:T(8,128)(2,1)S(1)} %copy-done.6, ...), custom_call_target="tpu_custom_call" | custom-call | flops 1 | bytes 1 | tf_op jit(solution)/shard_map/down/pallas_call | solution.py:555
  23.1 1.3 %collective-permute-start.9 = (f32[128,128]{1,0:T(8,128)S(1)}, f32[128,128]{1,0:T(8,128)S(1)}, u32[]{:S(2)}, u32[]{:S(2)}) collective-permute-start(f32[128,128]{1,0:T(8,128)S(1)} %down.2.refs_0_), channel_id=1, source_target_pairs={{0,2},{2,0},{1,3},{3,1},{4,6},{6,4},{5,7},{7,5},{8,10},{10,8},{9,1... | collective-permute-start | bytes 196616 | tf_op jit(solution)/shard_map/ppermute | solution.py:425
  24.4 4.4 %project.4.refs_7_ = f32[256,768]{1,0:T(8,128)S(1)} custom-call(bf16[256,3584]{1,0:T(8,128)(2,1)S(1)} %get-tuple-element.60.rows_ref, f32[18,128]{1,0:T(8,128)S(1)} %bitcast.19, bf16[3584,2304]{1,0:T(8,128)(2,1)} %weight_hbm.5), custom_call_target="tpu_custom_call" | custom-call | flops 1 | bytes 1 | tf_op jit(solution)/shard_map/project/pallas_call | solution.py:539
  28.9 0.5 up.2
  29.4 0.4 collective-permute-start.11
  29.8 2.1 %collective-permute-start.12 = (bf16[32,2048]{1,0:T(8,128)(2,1)S(1)}, bf16[32,2048]{1,0:T(8,128)(2,1)S(1)}, u32[]{:S(2)}, u32[]{:S(2)}) collective-permute-start(bf16[32,2048]{1,0:T(8,128)(2,1)S(1)} %get-tuple-element.67), channel_id=1, source_target_pairs={{0,8},{4,12},{8,0},{12,4},{1,9},{5,13},{9,1},{13,5},{2,10},{6,14},... | collective-permute-start | bytes 393224 | tf_op jit(solution)/shard_map/ppermute | solution.py:416
  31.9 0.2 collective-permute-start.13
  32.2 1.2 %down.3.refs_0_ = f32[128,128]{1,0:T(8,128)S(1)} custom-call(bf16[32,1792]{1,0:T(8,128)(2,1)S(1)} %collective-permute-done.3.refs_0_, bf16[32,1792]{1,0:T(8,128)(2,1)S(1)} %collective-permute-done.4.refs_1_, bf16[32,1792]{1,0:T(8,128)(2,1)S(1)} %collective-permute-done.5.refs_2_, bf16[32,1792]{1,0:T(8,128)(2,1)S(1)} %get-tuple-element.69.refs_3_, ...), custom_call_target="tpu_custom_call" | custom-call | flops 1 | bytes 1 | tf_op jit(solution)/shard_map/down/pallas_call | solution.py:555
  33.3 0.3 collective-permute-start.10
  33.7 4.4 %project.5.refs_8_ = f32[256,768]{1,0:T(8,128)S(1)} custom-call(bf16[256,3584]{1,0:T(8,128)(2,1)S(1)} %get-tuple-element.60.rows_ref, f32[18,128]{1,0:T(8,128)S(1)} %bitcast.20, bf16[3584,2304]{1,0:T(8,128)(2,1)} %weight_hbm.5), custom_call_target="tpu_custom_call" | custom-call | flops 1 | bytes 1 | tf_op jit(solution)/shard_map/project/pallas_call | solution.py:539
  38.1 0.5 up.3
  38.6 1.3 %collective-permute-start.14 = (bf16[32,2048]{1,0:T(8,128)(2,1)S(1)}, bf16[32,2048]{1,0:T(8,128)(2,1)S(1)}, u32[]{:S(2)}, u32[]{:S(2)}) collective-permute-start(bf16[32,2048]{1,0:T(8,128)(2,1)S(1)} %get-tuple-element.79), channel_id=1, source_target_pairs={{0,4},{4,0},{8,12},{12,8},{1,5},{5,1},{9,13},{13,9},{2,6},{6,2},{1... | collective-permute-start | bytes 393224 | tf_op jit(solution)/shard_map/ppermute | solution.py:416
  40.0 2.1 %collective-permute-start.15 = (bf16[32,2048]{1,0:T(8,128)(2,1)S(1)}, bf16[32,2048]{1,0:T(8,128)(2,1)S(1)}, u32[]{:S(2)}, u32[]{:S(2)}) collective-permute-start(bf16[32,2048]{1,0:T(8,128)(2,1)S(1)} %get-tuple-element.80), channel_id=1, source_target_pairs={{0,8},{4,12},{8,0},{12,4},{1,9},{5,13},{9,1},{13,5},{2,10},{6,14},... | collective-permute-start | bytes 393224 | tf_op jit(solution)/shard_map/ppermute | solution.py:416
  42.0 0.8 collective-permute-done.13.refs_12_
  42.8 0.9 collective-permute-start.16
  43.7 0.5 fusion
  44.3 3.8 %attend.2 = (f32[128,512]{1,0:T(8,128)S(1)}, bf16[64,1792]{1,0:T(8,128)(2,1)S(1)}, bf16[64,1792]{1,0:T(8,128)(2,1)S(1)}, bf16[64,1792]{1,0:T(8,128)(2,1)S(1)}, bf16[64,1792]{1,0:T(8,128)(2,1)S(1)}) custom-call(s32[8,64]{1,0:T(8,128)S(1)} %get-tuple-element.76.refs_0_, s32[1,64]{1,0:T(1,128)S(1)} %bitcast.23, f32[256,128]{1,0:T(8,128)S(1)} %get-tuple-element.96.refs_2_, ...), custom_call_target="tpu_custom_call" | custom-call | flops 1 | bytes 1 | tf_op jit(solution)/shard_map/attend/pallas_call | solution.py:609
  48.1 6.3 %collective-permute-done.16.refs_12_ = bf16[32,2048]{1,0:T(8,128)(2,1)S(1)} collective-permute-done((bf16[32,2048]{1,0:T(8,128)(2,1)S(1)}, bf16[32,2048]{1,0:T(8,128)(2,1)S(1)}, u32[]{:S(2)}, u32[]{:S(2)}) %collective-permute-start.16) | collective-permute-done | bytes 131104 | tf_op jit(solution)/shard_map/ppermute | solution.py:416
  54.5 0.8 collective-permute-start.19
  55.3 1.8 %collective-permute-start.17 = (bf16[64,1792]{1,0:T(8,128)(2,1)S(1)}, bf16[64,1792]{1,0:T(8,128)(2,1)S(1)}, u32[]{:S(2)}, u32[]{:S(2)}) collective-permute-start(bf16[64,1792]{1,0:T(8,128)(2,1)S(1)} %get-tuple-element.82), channel_id=1, source_target_pairs={{0,4},{4,0},{8,12},{12,8},{1,5},{5,1},{9,13},{13,9},{2,6},{6,2},{1... | collective-permute-start | bytes 688136 | tf_op jit(solution)/shard_map/ppermute | solution.py:416
  57.1 3.7 %attend.3 = (bf16[64,1792]{1,0:T(8,128)(2,1)S(1)}, bf16[64,1792]{1,0:T(8,128)(2,1)S(1)}, bf16[64,1792]{1,0:T(8,128)(2,1)S(1)}, bf16[64,1792]{1,0:T(8,128)(2,1)S(1)}) custom-call(s32[8,64]{1,0:T(8,128)S(1)} %get-tuple-element.76.refs_0_, s32[1,64]{1,0:T(1,128)S(1)} %bitcast.24, f32[256,128]{1,0:T(8,128)S(1)} %get-tuple-element.96.refs_2_, ...), custom_call_target="tpu_custom_call" | custom-call | flops 1 | bytes 1 | tf_op jit(solution)/shard_map/attend/pallas_call | solution.py:609
  60.8 9.0 %collective-permute-done.19.refs_3_ = bf16[64,1792]{1,0:T(8,128)(2,1)S(1)} collective-permute-done((bf16[64,1792]{1,0:T(8,128)(2,1)S(1)}, bf16[64,1792]{1,0:T(8,128)(2,1)S(1)}, u32[]{:S(2)}, u32[]{:S(2)}) %collective-permute-start.19) | collective-permute-done | bytes 229408 | tf_op jit(solution)/shard_map/ppermute | solution.py:416
  69.8 4.9 %collective-permute-done.18.refs_2_ = bf16[64,1792]{1,0:T(8,128)(2,1)S(1)} collective-permute-done((bf16[64,1792]{1,0:T(8,128)(2,1)S(1)}, bf16[64,1792]{1,0:T(8,128)(2,1)S(1)}, u32[]{:S(2)}, u32[]{:S(2)}) %collective-permute-start.18) | collective-permute-done | bytes 229408 | tf_op jit(solution)/shard_map/ppermute | solution.py:416
  74.8 0.6 collective-permute-start.20
  75.4 1.8 %collective-permute-start.21 = (bf16[64,1792]{1,0:T(8,128)(2,1)S(1)}, bf16[64,1792]{1,0:T(8,128)(2,1)S(1)}, u32[]{:S(2)}, u32[]{:S(2)}) collective-permute-start(bf16[64,1792]{1,0:T(8,128)(2,1)S(1)} %get-tuple-element.90), channel_id=1, source_target_pairs={{0,4},{4,0},{8,12},{12,8},{1,5},{5,1},{9,13},{13,9},{2,6},{6,2},{1... | collective-permute-start | bytes 688136 | tf_op jit(solution)/shard_map/ppermute | solution.py:416
  77.2 1.3 %collective-permute-start.22 = (bf16[64,1792]{1,0:T(8,128)(2,1)S(1)}, bf16[64,1792]{1,0:T(8,128)(2,1)S(1)}, u32[]{:S(2)}, u32[]{:S(2)}) collective-permute-start(bf16[64,1792]{1,0:T(8,128)(2,1)S(1)} %get-tuple-element.92), channel_id=1, source_target_pairs={{0,8},{4,12},{8,0},{12,4},{1,9},{5,13},{9,1},{13,5},{2,10},{6,14},... | collective-permute-start | bytes 688136 | tf_op jit(solution)/shard_map/ppermute | solution.py:416
  78.5 0.3 collective-permute-start.23
  78.8 0.6 collective-permute-start.24
  79.4 7.3 %collective-permute-done.21.refs_6_ = bf16[64,1792]{1,0:T(8,128)(2,1)S(1)} collective-permute-done((bf16[64,1792]{1,0:T(8,128)(2,1)S(1)}, bf16[64,1792]{1,0:T(8,128)(2,1)S(1)}, u32[]{:S(2)}, u32[]{:S(2)}) %collective-permute-start.21) | collective-permute-done | bytes 229408 | tf_op jit(solution)/shard_map/ppermute | solution.py:416
  86.7 0.8 collective-permute-start.25
  87.6 5.6 %collective-permute-done.22.refs_7_ = bf16[64,1792]{1,0:T(8,128)(2,1)S(1)} collective-permute-done((bf16[64,1792]{1,0:T(8,128)(2,1)S(1)}, bf16[64,1792]{1,0:T(8,128)(2,1)S(1)}, u32[]{:S(2)}, u32[]{:S(2)}) %collective-permute-start.22) | collective-permute-done | bytes 229408 | tf_op jit(solution)/shard_map/ppermute | solution.py:416
  93.2 1.5 %collective-permute-start.26 = (bf16[64,1792]{1,0:T(8,128)(2,1)S(1)}, bf16[64,1792]{1,0:T(8,128)(2,1)S(1)}, u32[]{:S(2)}, u32[]{:S(2)}) collective-permute-start(bf16[64,1792]{1,0:T(8,128)(2,1)S(1)} %collective-permute-done.22.refs_7_), channel_id=1, source_target_pairs={{0,1},{1,0},{2,3},{3,2},{4,5},{5,4},{6,7},{7,6},{8,9},{9,8},{10,11... | collective-permute-start | bytes 688136 | tf_op jit(solution)/shard_map/ppermute | solution.py:674
  94.7 4.5 %collective-permute-done.23.refs_8_ = bf16[64,1792]{1,0:T(8,128)(2,1)S(1)} collective-permute-done((bf16[64,1792]{1,0:T(8,128)(2,1)S(1)}, bf16[64,1792]{1,0:T(8,128)(2,1)S(1)}, u32[]{:S(2)}, u32[]{:S(2)}) %collective-permute-start.23) | collective-permute-done | bytes 229408 | tf_op jit(solution)/shard_map/ppermute | solution.py:416
  99.3 0.8 collective-permute-start.27
  100.1 1.1 %collective-permute-done.27.refs_12_ = bf16[64,1792]{1,0:T(8,128)(2,1)S(1)} collective-permute-done((bf16[64,1792]{1,0:T(8,128)(2,1)S(1)}, bf16[64,1792]{1,0:T(8,128)(2,1)S(1)}, u32[]{:S(2)}, u32[]{:S(2)}) %collective-permute-start.27) | collective-permute-done | bytes 229408 | tf_op jit(solution)/shard_map/ppermute | solution.py:674
  101.2 1.9 %place.1 = bf16[128,4,1792]{2,1,0:T(4,128)(2,1)} custom-call(bf16[64,1792]{1,0:T(8,128)(2,1)S(1)} %get-tuple-element.77.refs_0_, bf16[64,1792]{1,0:T(8,128)(2,1)S(1)} %collective-permute-done.17.refs_1_, bf16[64,1792]{1,0:T(8,128)(2,1)S(1)} %collective-permute-done.18.refs_2_, bf16[64,1792]{1,0:T(8,128)(2,1)S(1)} %collective-permute-done.19.refs_3_, ...), custom_call_target="tpu_custom_call" | custom-call | flops 1 | bytes 1 | tf_op jit(solution)/shard_map/place/pallas_call | solution.py:677
  (56 shorter events, 0.3 us)
Async XLA Ops:
  0.0 8.4 %copy-start.10 = (s32[64,1]{0,1:T(1,128)S(1)}, s32[64,1]{0,1:T(1,128)}, u32[]{:S(2)}) copy-start(s32[64,1]{0,1:T(1,128)} %param.17) | copy-start | bytes 772
  0.0 8.4 %copy-start.11 = (s32[32]{0:T(128)S(1)}, s32[32]{0:T(128)}, u32[]{:S(2)}) copy-start(s32[32]{0:T(128)} %param.18) | copy-start | bytes 388
  0.0 8.4 %copy-start.12 = (s32[64,1]{0,1:T(1,128)S(1)}, s32[64,1]{0,1:T(1,128)}, u32[]{:S(2)}) copy-start(s32[64,1]{0,1:T(1,128)} %param.25) | copy-start | bytes 772
  0.0 8.4 %copy-start.8 = (f32[3584]{0:T(1024)S(1)}, f32[3584]{0:T(1024)}, u32[]{:S(2)}) copy-start(f32[3584]{0:T(1024)} %param.14) | copy-start | bytes 43012
  0.0 8.4 %copy-start = (bf16[4,64,3584]{2,1,0:T(8,128)(2,1)S(1)}, bf16[4,64,3584]{2,1,0:T(8,128)(2,1)}, u32[]{:S(2)}) copy-start(bf16[4,64,3584]{2,1,0:T(8,128)(2,1)} %param.13) | copy-start | bytes 5505028
  0.0 8.3 %collective-permute-start = (bf16[4,1792,128]{2,1,0:T(8,128)(2,1)}, bf16[4,1792,128]{2,1,0:T(8,128)(2,1)S(1)}, u32[]{:S(2)}, u32[]{:S(2)}) collective-permute-start(bf16[4,1792,128]{2,1,0:T(8,128)(2,1)} %refs_4_.5), channel_id=1, source_target_pairs={{0,1},{1,0},{2,3},{3,2},{4,5},{5,4},{6,7},{7,6},{8,9},{9,8},{10,11... | collective-permute-start | bytes 5505032 | tf_op jit(solution)/shard_map/ppermute | solution.py:425
  0.8 7.6 %collective-permute-start.1 = (bf16[256,1792]{1,0:T(8,128)(2,1)}, bf16[256,1792]{1,0:T(8,128)(2,1)S(1)}, u32[]{:S(2)}, u32[]{:S(2)}) collective-permute-start(bf16[256,1792]{1,0:T(8,128)(2,1)} %bitcast.12), channel_id=1, source_target_pairs={{0,1},{1,0},{2,3},{3,2},{4,5},{5,4},{6,7},{7,6},{8,9},{9,8},{10,11... | collective-permute-start | bytes 2752520 | tf_op jit(solution)/shard_map/ppermute | solution.py:425
  0.9 6.4 %collective-permute-start.2 = (bf16[256,256]{1,0:T(8,128)(2,1)}, bf16[256,256]{1,0:T(8,128)(2,1)S(1)}, u32[]{:S(2)}, u32[]{:S(2)}) collective-permute-start(bf16[256,256]{1,0:T(8,128)(2,1)} %bitcast.15), channel_id=1, source_target_pairs={{0,1},{1,0},{2,3},{3,2},{4,5},{5,4},{6,7},{7,6},{8,9},{9,8},{10,11... | collective-permute-start | bytes 393224 | tf_op jit(solution)/shard_map/ppermute | solution.py:425
  1.3 13.7 %copy-start.9 = (s32[64]{0:T(128)S(1)}, s32[64]{0:T(128)}, u32[]{:S(2)}) copy-start(s32[64]{0:T(128)} %param.19) | copy-start | bytes 772
  1.3 14.9 %copy-start.7 = (f32[2304]{0:T(1024)S(1)}, f32[2304]{0:T(1024)}, u32[]{:S(2)}) copy-start(f32[2304]{0:T(1024)} %param.16) | copy-start | bytes 27652
  4.8 16.0 %collective-permute-start.6 = (bf16[32,1792]{1,0:T(8,128)(2,1)}, bf16[32,1792]{1,0:T(8,128)(2,1)S(1)}, u32[]{:S(2)}, u32[]{:S(2)}) collective-permute-start(bf16[32,1792]{1,0:T(8,128)(2,1)} %get-tuple-element.53), channel_id=1, source_target_pairs={{0,12},{4,8},{8,4},{12,0},{1,13},{5,9},{9,5},{13,1},{2,14},{6,10},... | collective-permute-start | bytes 344072 | tf_op jit(solution)/shard_map/ppermute | solution.py:416
  6.1 15.8 %collective-permute-start.7 = (bf16[32,1792]{1,0:T(8,128)(2,1)}, bf16[32,1792]{1,0:T(8,128)(2,1)S(1)}, u32[]{:S(2)}, u32[]{:S(2)}) collective-permute-start(bf16[32,1792]{1,0:T(8,128)(2,1)} %get-tuple-element.52), channel_id=1, source_target_pairs={{0,8},{4,12},{8,0},{12,4},{1,9},{5,13},{9,1},{13,5},{2,10},{6,14},... | collective-permute-start | bytes 344072 | tf_op jit(solution)/shard_map/ppermute | solution.py:416
  7.2 14.7 %collective-permute-start.8 = (bf16[32,1792]{1,0:T(8,128)(2,1)}, bf16[32,1792]{1,0:T(8,128)(2,1)S(1)}, u32[]{:S(2)}, u32[]{:S(2)}) collective-permute-start(bf16[32,1792]{1,0:T(8,128)(2,1)} %get-tuple-element.51), channel_id=1, source_target_pairs={{0,4},{4,0},{8,12},{12,8},{1,5},{5,1},{9,13},{13,9},{2,6},{6,2},{1... | collective-permute-start | bytes 344072 | tf_op jit(solution)/shard_map/ppermute | solution.py:416
  13.7 18.2 %collective-permute-start.3 = (bf16[32,1792]{1,0:T(8,128)(2,1)S(1)}, bf16[32,1792]{1,0:T(8,128)(2,1)S(1)}, u32[]{:S(2)}, u32[]{:S(2)}) collective-permute-start(bf16[32,1792]{1,0:T(8,128)(2,1)S(1)} %get-tuple-element.56), channel_id=1, source_target_pairs={{0,12},{4,8},{8,4},{12,0},{1,13},{5,9},{9,5},{13,1},{2,14},{6,10},... | collective-permute-start | bytes 344072 | tf_op jit(solution)/shard_map/ppermute | solution.py:416
  14.9 17.2 %collective-permute-start.4 = (bf16[32,1792]{1,0:T(8,128)(2,1)S(1)}, bf16[32,1792]{1,0:T(8,128)(2,1)S(1)}, u32[]{:S(2)}, u32[]{:S(2)}) collective-permute-start(bf16[32,1792]{1,0:T(8,128)(2,1)S(1)} %get-tuple-element.57), channel_id=1, source_target_pairs={{0,8},{4,12},{8,0},{12,4},{1,9},{5,13},{9,1},{13,5},{2,10},{6,14},... | collective-permute-start | bytes 344072 | tf_op jit(solution)/shard_map/ppermute | solution.py:416
  16.2 5.7 %copy-start.1 = (bf16[4,1792,128]{2,1,0:T(8,128)(2,1)S(1)}, bf16[4,1792,128]{2,1,0:T(8,128)(2,1)}, u32[]{:S(2)}) copy-start(bf16[4,1792,128]{2,1,0:T(8,128)(2,1)} %refs_4_.5) | copy-start | bytes 5505028
  16.2 5.7 %copy-start.6 = (bf16[32,1792]{1,0:T(8,128)(2,1)S(1)}, bf16[32,1792]{1,0:T(8,128)(2,1)}, u32[]{:S(2)}) copy-start(bf16[32,1792]{1,0:T(8,128)(2,1)} %get-tuple-element.62.refs_3_) | copy-start | bytes 344068
  20.7 11.5 %collective-permute-start.5 = (bf16[32,1792]{1,0:T(8,128)(2,1)S(1)}, bf16[32,1792]{1,0:T(8,128)(2,1)S(1)}, u32[]{:S(2)}, u32[]{:S(2)}) collective-permute-start(bf16[32,1792]{1,0:T(8,128)(2,1)S(1)} %get-tuple-element.58), channel_id=1, source_target_pairs={{0,4},{4,0},{8,12},{12,8},{1,5},{5,1},{9,13},{13,9},{2,6},{6,2},{1... | collective-permute-start | bytes 344072 | tf_op jit(solution)/shard_map/ppermute | solution.py:416
  23.1 5.8 %collective-permute-start.9 = (f32[128,128]{1,0:T(8,128)S(1)}, f32[128,128]{1,0:T(8,128)S(1)}, u32[]{:S(2)}, u32[]{:S(2)}) collective-permute-start(f32[128,128]{1,0:T(8,128)S(1)} %down.2.refs_0_), channel_id=1, source_target_pairs={{0,2},{2,0},{1,3},{3,1},{4,6},{6,4},{5,7},{7,5},{8,10},{10,8},{9,1... | collective-permute-start | bytes 196616 | tf_op jit(solution)/shard_map/ppermute | solution.py:425
  24.4 4.5 %copy-start.4 = (bf16[4,64,1792]{2,1,0:T(8,128)(2,1)S(1)}, bf16[4,64,1792]{2,1,0:T(8,128)(2,1)}, u32[]{:S(2)}) copy-start(bf16[4,64,1792]{2,1,0:T(8,128)(2,1)} %param.23) | copy-start | bytes 2752516
  24.4 4.5 %copy-start.5 = (bf16[4,64,256]{2,1,0:T(8,128)(2,1)S(1)}, bf16[4,64,256]{2,1,0:T(8,128)(2,1)}, u32[]{:S(2)}) copy-start(bf16[4,64,256]{2,1,0:T(8,128)(2,1)} %param.24) | copy-start | bytes 393220
  29.4 9.3 %collective-permute-start.11 = (bf16[32,2048]{1,0:T(8,128)(2,1)S(1)}, bf16[32,2048]{1,0:T(8,128)(2,1)S(1)}, u32[]{:S(2)}, u32[]{:S(2)}) collective-permute-start(bf16[32,2048]{1,0:T(8,128)(2,1)S(1)} %get-tuple-element.66), channel_id=1, source_target_pairs={{0,4},{4,0},{8,12},{12,8},{1,5},{5,1},{9,13},{13,9},{2,6},{6,2},{1... | collective-permute-start | bytes 393224 | tf_op jit(solution)/shard_map/ppermute | solution.py:416
  29.8 10.2 %collective-permute-start.12 = (bf16[32,2048]{1,0:T(8,128)(2,1)S(1)}, bf16[32,2048]{1,0:T(8,128)(2,1)S(1)}, u32[]{:S(2)}, u32[]{:S(2)}) collective-permute-start(bf16[32,2048]{1,0:T(8,128)(2,1)S(1)} %get-tuple-element.67), channel_id=1, source_target_pairs={{0,8},{4,12},{8,0},{12,4},{1,9},{5,13},{9,1},{13,5},{2,10},{6,14},... | collective-permute-start | bytes 393224 | tf_op jit(solution)/shard_map/ppermute | solution.py:416
  31.9 11.0 %collective-permute-start.13 = (bf16[32,2048]{1,0:T(8,128)(2,1)S(1)}, bf16[32,2048]{1,0:T(8,128)(2,1)S(1)}, u32[]{:S(2)}, u32[]{:S(2)}) collective-permute-start(bf16[32,2048]{1,0:T(8,128)(2,1)S(1)} %get-tuple-element.68), channel_id=1, source_target_pairs={{0,12},{4,8},{8,4},{12,0},{1,13},{5,9},{9,5},{13,1},{2,14},{6,10},... | collective-permute-start | bytes 393224 | tf_op jit(solution)/shard_map/ppermute | solution.py:416
  33.3 4.8 %collective-permute-start.10 = (f32[128,128]{1,0:T(8,128)S(1)}, f32[128,128]{1,0:T(8,128)S(1)}, u32[]{:S(2)}, u32[]{:S(2)}) collective-permute-start(f32[128,128]{1,0:T(8,128)S(1)} %down.3.refs_0_), channel_id=1, source_target_pairs={{0,2},{2,0},{1,3},{3,1},{4,6},{6,4},{5,7},{7,5},{8,10},{10,8},{9,1... | collective-permute-start | bytes 196616 | tf_op jit(solution)/shard_map/ppermute | solution.py:425
  38.1 6.2 %copy-start.2 = (bf16[64,32,256]{2,1,0:T(8,128)(2,1)S(1)}, bf16[64,32,256]{2,1,0:T(8,128)(2,1)}, u32[]{:S(2)}) copy-start(bf16[64,32,256]{2,1,0:T(8,128)(2,1)} %refs_4_.7) | copy-start | bytes 3145732
  38.1 6.2 %copy-start.3 = (bf16[64,32,256]{2,1,0:T(8,128)(2,1)S(1)}, bf16[64,32,256]{2,1,0:T(8,128)(2,1)}, u32[]{:S(2)}) copy-start(bf16[64,32,256]{2,1,0:T(8,128)(2,1)} %refs_5_.3) | copy-start | bytes 3145732
  38.6 9.5 %collective-permute-start.14 = (bf16[32,2048]{1,0:T(8,128)(2,1)S(1)}, bf16[32,2048]{1,0:T(8,128)(2,1)S(1)}, u32[]{:S(2)}, u32[]{:S(2)}) collective-permute-start(bf16[32,2048]{1,0:T(8,128)(2,1)S(1)} %get-tuple-element.79), channel_id=1, source_target_pairs={{0,4},{4,0},{8,12},{12,8},{1,5},{5,1},{9,13},{13,9},{2,6},{6,2},{1... | collective-permute-start | bytes 393224 | tf_op jit(solution)/shard_map/ppermute | solution.py:416
  40.0 8.2 %collective-permute-start.15 = (bf16[32,2048]{1,0:T(8,128)(2,1)S(1)}, bf16[32,2048]{1,0:T(8,128)(2,1)S(1)}, u32[]{:S(2)}, u32[]{:S(2)}) collective-permute-start(bf16[32,2048]{1,0:T(8,128)(2,1)S(1)} %get-tuple-element.80), channel_id=1, source_target_pairs={{0,8},{4,12},{8,0},{12,4},{1,9},{5,13},{9,1},{13,5},{2,10},{6,14},... | collective-permute-start | bytes 393224 | tf_op jit(solution)/shard_map/ppermute | solution.py:416
  42.8 11.6 %collective-permute-start.16 = (bf16[32,2048]{1,0:T(8,128)(2,1)S(1)}, bf16[32,2048]{1,0:T(8,128)(2,1)S(1)}, u32[]{:S(2)}, u32[]{:S(2)}) collective-permute-start(bf16[32,2048]{1,0:T(8,128)(2,1)S(1)} %get-tuple-element.81), channel_id=1, source_target_pairs={{0,12},{4,8},{8,4},{12,0},{1,13},{5,9},{9,5},{13,1},{2,14},{6,10},... | collective-permute-start | bytes 393224 | tf_op jit(solution)/shard_map/ppermute | solution.py:416
  54.5 15.3 %collective-permute-start.19 = (bf16[64,1792]{1,0:T(8,128)(2,1)S(1)}, bf16[64,1792]{1,0:T(8,128)(2,1)S(1)}, u32[]{:S(2)}, u32[]{:S(2)}) collective-permute-start(bf16[64,1792]{1,0:T(8,128)(2,1)S(1)} %get-tuple-element.86), channel_id=1, source_target_pairs={{0,12},{4,8},{8,4},{12,0},{1,13},{5,9},{9,5},{13,1},{2,14},{6,10},... | collective-permute-start | bytes 688136 | tf_op jit(solution)/shard_map/ppermute | solution.py:416
  55.3 19.4 %collective-permute-start.18 = (bf16[64,1792]{1,0:T(8,128)(2,1)S(1)}, bf16[64,1792]{1,0:T(8,128)(2,1)S(1)}, u32[]{:S(2)}, u32[]{:S(2)}) collective-permute-start(bf16[64,1792]{1,0:T(8,128)(2,1)S(1)} %get-tuple-element.84), channel_id=1, source_target_pairs={{0,8},{4,12},{8,0},{12,4},{1,9},{5,13},{9,1},{13,5},{2,10},{6,14},... | collective-permute-start | bytes 688136 | tf_op jit(solution)/shard_map/ppermute | solution.py:416
  55.3 19.4 %collective-permute-start.17 = (bf16[64,1792]{1,0:T(8,128)(2,1)S(1)}, bf16[64,1792]{1,0:T(8,128)(2,1)S(1)}, u32[]{:S(2)}, u32[]{:S(2)}) collective-permute-start(bf16[64,1792]{1,0:T(8,128)(2,1)S(1)} %get-tuple-element.82), channel_id=1, source_target_pairs={{0,4},{4,0},{8,12},{12,8},{1,5},{5,1},{9,13},{13,9},{2,6},{6,2},{1... | collective-permute-start | bytes 688136 | tf_op jit(solution)/shard_map/ppermute | solution.py:416
  74.8 25.3 %collective-permute-start.20 = (bf16[128,1792]{1,0:T(8,128)(2,1)S(1)}, bf16[128,1792]{1,0:T(8,128)(2,1)S(1)}, u32[]{:S(2)}, u32[]{:S(2)}) collective-permute-start(bf16[128,1792]{1,0:T(8,128)(2,1)S(1)} %pad_maximum_fusion), channel_id=1, source_target_pairs={{0,1},{1,0},{2,3},{3,2},{4,5},{5,4},{6,7},{7,6},{8,9},{9,8},{10,11... | collective-permute-start | bytes 1376264 | tf_op jit(solution)/shard_map/ppermute | solution.py:670
  75.4 11.4 %collective-permute-start.21 = (bf16[64,1792]{1,0:T(8,128)(2,1)S(1)}, bf16[64,1792]{1,0:T(8,128)(2,1)S(1)}, u32[]{:S(2)}, u32[]{:S(2)}) collective-permute-start(bf16[64,1792]{1,0:T(8,128)(2,1)S(1)} %get-tuple-element.90), channel_id=1, source_target_pairs={{0,4},{4,0},{8,12},{12,8},{1,5},{5,1},{9,13},{13,9},{2,6},{6,2},{1... | collective-permute-start | bytes 688136 | tf_op jit(solution)/shard_map/ppermute | solution.py:416
  77.2 16.0 %collective-permute-start.22 = (bf16[64,1792]{1,0:T(8,128)(2,1)S(1)}, bf16[64,1792]{1,0:T(8,128)(2,1)S(1)}, u32[]{:S(2)}, u32[]{:S(2)}) collective-permute-start(bf16[64,1792]{1,0:T(8,128)(2,1)S(1)} %get-tuple-element.92), channel_id=1, source_target_pairs={{0,8},{4,12},{8,0},{12,4},{1,9},{5,13},{9,1},{13,5},{2,10},{6,14},... | collective-permute-start | bytes 688136 | tf_op jit(solution)/shard_map/ppermute | solution.py:416
  78.5 20.8 %collective-permute-start.23 = (bf16[64,1792]{1,0:T(8,128)(2,1)S(1)}, bf16[64,1792]{1,0:T(8,128)(2,1)S(1)}, u32[]{:S(2)}, u32[]{:S(2)}) collective-permute-start(bf16[64,1792]{1,0:T(8,128)(2,1)S(1)} %get-tuple-element.94), channel_id=1, source_target_pairs={{0,12},{4,8},{8,4},{12,0},{1,13},{5,9},{9,5},{13,1},{2,14},{6,10},... | collective-permute-start | bytes 688136 | tf_op jit(solution)/shard_map/ppermute | solution.py:416
  78.8 21.3 %collective-permute-start.24 = (bf16[64,1792]{1,0:T(8,128)(2,1)S(1)}, bf16[64,1792]{1,0:T(8,128)(2,1)S(1)}, u32[]{:S(2)}, u32[]{:S(2)}) collective-permute-start(bf16[64,1792]{1,0:T(8,128)(2,1)S(1)} %get-tuple-element.88.refs_5_), channel_id=1, source_target_pairs={{0,1},{1,0},{2,3},{3,2},{4,5},{5,4},{6,7},{7,6},{8,9},{9,8},{10,11... | collective-permute-start | bytes 688136 | tf_op jit(solution)/shard_map/ppermute | solution.py:674
  86.7 13.4 %collective-permute-start.25 = (bf16[64,1792]{1,0:T(8,128)(2,1)S(1)}, bf16[64,1792]{1,0:T(8,128)(2,1)S(1)}, u32[]{:S(2)}, u32[]{:S(2)}) collective-permute-start(bf16[64,1792]{1,0:T(8,128)(2,1)S(1)} %collective-permute-done.21.refs_6_), channel_id=1, source_target_pairs={{0,1},{1,0},{2,3},{3,2},{4,5},{5,4},{6,7},{7,6},{8,9},{9,8},{10,11... | collective-permute-start | bytes 688136 | tf_op jit(solution)/shard_map/ppermute | solution.py:674
  93.2 6.9 %collective-permute-start.26 = (bf16[64,1792]{1,0:T(8,128)(2,1)S(1)}, bf16[64,1792]{1,0:T(8,128)(2,1)S(1)}, u32[]{:S(2)}, u32[]{:S(2)}) collective-permute-start(bf16[64,1792]{1,0:T(8,128)(2,1)S(1)} %collective-permute-done.22.refs_7_), channel_id=1, source_target_pairs={{0,1},{1,0},{2,3},{3,2},{4,5},{5,4},{6,7},{7,6},{8,9},{9,8},{10,11... | collective-permute-start | bytes 688136 | tf_op jit(solution)/shard_map/ppermute | solution.py:674
  99.3 2.0 %collective-permute-start.27 = (bf16[64,1792]{1,0:T(8,128)(2,1)S(1)}, bf16[64,1792]{1,0:T(8,128)(2,1)S(1)}, u32[]{:S(2)}, u32[]{:S(2)}) collective-permute-start(bf16[64,1792]{1,0:T(8,128)(2,1)S(1)} %collective-permute-done.23.refs_8_), channel_id=1, source_target_pairs={{0,1},{1,0},{2,3},{3,2},{4,5},{5,4},{6,7},{7,6},{8,9},{9,8},{10,11... | collective-permute-start | bytes 688136 | tf_op jit(solution)/shard_map/ppermute | solution.py:674

commit v11 on v7

--- a/solution.py
+++ b/solution.py
@@ -17,6 +17,7 @@
 LANE_AXES = ("streams", "sub")
 BATCH = 8
 TOGETHER = 2
+PIECE = 32
 VMEM = pl.BlockSpec(memory_space=pltpu.VMEM)
 MIB = 1 << 20
 PACK_LIMIT = 56
@@ -156,7 +157,7 @@
         )
 
 
-def norm_pack_project_kernel(steps, rows, flow_most, lanes, pieces, chunk, *refs):
+def norm_pack_project_kernel(steps, rows, flow_most, lanes, pieces, begin, *refs):
     table_hbms, bias_ref, gain_hbm, x_hbm, weight_hbm = refs[:3], *refs[3:7]
     normed_ref, out_ref, places_ref, message_refs = *refs[7:10], refs[10 : 10 + lanes]
     x_buf, gain_buf, *table_bufs, semaphores, weight_buf, weight_semaphores = refs[10 + lanes :]
@@ -176,8 +177,7 @@
     places, flow_places = places_from(table_bufs, spots, flow_most)
     places_ref[0:1, :] = places
     places_ref[1:2, :] = flow_places
-    count = steps * rows
-    own_ref = normed_ref.at[pl.ds(chunk * count, count)]
+    own_ref = normed_ref.at[pl.ds(begin, steps * rows)]
     pack_messages(steps, rows, places, own_ref, message_refs)
     project_blocks(0, copies, normed_ref, weight_buf, bias_ref, out_ref)
 
@@ -194,7 +194,7 @@
 
 
 def down_kernel(lanes, spots, *refs):
-    message_refs, map_refs, partial_ref = refs[:lanes], refs[lanes:-1], refs[-1]
+    message_refs, map_refs, partial_ref = refs[:lanes][::-1], refs[lanes:-1], refs[-1]
     local_slots = map_refs[0].shape[0]
     rows = jnp.concatenate([ref[...] for ref in message_refs], axis=0)
     own_slot = row_slots(partial_ref.shape, spots)
@@ -247,7 +247,7 @@
 
 def attend_kernel(before, steps, rows, cache, groups, lanes, subs, last, *refs):
     places_ref, length_ref, cos_ref, sin_ref, key_ref, value_ref = refs[:6]
-    qkv_refs, refs = refs[6:8], refs[8:]
+    qkv_refs, refs = refs[6:9], refs[9:]
     delta_refs, refs = refs[:lanes], refs[lanes:]
     if before:
         earlier_ref, refs = refs[0], refs[1:]
@@ -261,14 +261,10 @@
     known = before + steps
 
     def qkv_tile(span, group, head):
-        begin = (group * (PER_GROUP + 2) + head) * HEAD_WIDTH
-        edge = qkv_refs[0].shape[1]
-        if begin < edge:
-            return qkv_refs[0][span, begin : begin + HEAD_WIDTH]
-        return qkv_refs[1][span, begin - edge : begin - edge + HEAD_WIDTH]
+        part, begin = divmod((group * (PER_GROUP + 2) + head) * HEAD_WIDTH, qkv_refs[0].shape[1])
+        return qkv_refs[part][span, begin : begin + HEAD_WIDTH]
 
     wide = groups * HEAD_WIDTH
-
     column = as_column(places_ref[0:1, :])
     column = jnp.concatenate([column] * steps, axis=0)
     shape = (steps * rows, lanes * per_message)
@@ -393,25 +389,28 @@
         ).astype(jnp.bfloat16)
 
 
-def place_kernel(found, lanes, subs, most, *refs):
-    chunks = len(found)
+def place_kernel(parts, found, lanes, subs, most, *refs):
     out_ref = refs[-1]
     steps = out_ref.shape[1]
-    chunk_steps = steps // chunks
-    block = most * chunk_steps
     here = lax.axis_index("streams")
     core = lax.axis_index("sub")
-    shape = (chunks * block, chunks * block)
+    shape = (most * steps, most * steps)
     out_row, in_row = iota(shape, 0), iota(shape, 1)
-    step = out_row % steps
-    wanted = step // chunk_steps * block + out_row // steps * chunk_steps + step % chunk_steps
-    pick = (wanted == in_row).astype(jnp.float32).astype(jnp.bfloat16)
+    step, rank = out_row % steps, out_row // steps
+    pick = jnp.zeros(shape, jnp.float32)
+    begin = 0
+    for part in parts:
+        here_step = (step >= begin) & (step < begin + part)
+        wanted = most * begin + rank * part + step - begin
+        pick = jnp.where(here_step & (wanted == in_row), 1.0, pick)
+        begin += part
+    pick = pick.astype(jnp.bfloat16)
     for number in range(lanes):
         for other in range(subs):
             pieces = []
-            for chunk in range(chunks):
-                array, begin = found[chunk][number][other]
-                pieces.append(refs[array][...][begin : begin + block])
+            for part, where in zip(parts, found):
+                array, begin = where[number][other]
+                pieces.append(refs[array][...][begin : begin + most * part])
             rows = jnp.dot(
                 pick, jnp.concatenate(pieces, axis=0), preferred_element_type=jnp.float32
             )
@@ -473,10 +472,8 @@
     groups = value_columns // HEAD_WIDTH
     cache = rotated_key_cache.shape[1]
     spots = subs * local_slots * MOST
-    chunks = 2
-    chunk_steps = steps // chunks
-    chunk_rows = chunk_steps * rows
-    per_message = chunk_steps * spots
+    parts = [steps - 1, 1]
+    chunks = len(parts)
     chip_slots = subs * local_slots
     flow_most = max(2, (2 * rows + flow_lanes - 1) // flow_lanes)
     bf16, f32 = jnp.bfloat16, jnp.float32
@@ -494,10 +491,11 @@
         adapter_value_up.reshape(local_slots * ADAPTER_RANK, value_columns), "sub"
     )
 
-    pieces = 4
     flat = inputs.reshape(steps * rows, width)
     gain = input_norm_gain.reshape(width // 128, 128)
-    message = jax.ShapeDtypeStruct((per_message, sliced), bf16)
+    messages_shape = [
+        [jax.ShapeDtypeStruct((part * spots, sliced), bf16)] * lanes for part in parts
+    ]
     places_shape = jax.ShapeDtypeStruct((8, rows), jnp.int32)
     tables = [
         speaker.reshape(1, rows),
@@ -505,19 +503,23 @@
         flow_decoder_owner.reshape(1, rows),
     ]
 
-    def row_buffers(count):
+    def row_buffers(count, pieces):
         return (
             [pltpu.VMEM((count, width), bf16), pltpu.VMEM(gain.shape, f32)]
             + [pltpu.VMEM(table.shape, jnp.int32) for table in tables]
             + [pltpu.SemaphoreType.DMA((pieces + 4,))]
         )
 
+    first_rows = parts[0] * rows
+    pieces = first_rows // PIECE
+
     messages = pl.pallas_call(
-        functools.partial(norm_pack_kernel, chunk_steps, rows, flow_most, lanes, pieces),
+        functools.partial(norm_pack_kernel, parts[0], rows, flow_most, lanes, pieces),
         in_specs=[in_hbm] * 5,
         out_specs=[VMEM] * lanes,
-        out_shape=[message] * lanes,
-        scratch_shapes=row_buffers(chunk_rows) + [pltpu.VMEM((chunk_rows, width), bf16)],
+        out_shape=messages_shape[0],
+        scratch_shapes=row_buffers(first_rows, pieces)
+        + [pltpu.VMEM((first_rows, width), bf16)],
         compiler_params=pltpu.CompilerParams(vmem_limit_bytes=PACK_LIMIT * MIB),
         cost_estimate=SMALL,
         name="norm_and_pack",
@@ -528,7 +530,7 @@
     columns = projection_weight.shape[1]
     block_columns = 256 if columns % 256 == 0 else 384
     blocks = columns // block_columns
-    cut = blocks // 2
+    cut = blocks // 3
 
     def weight_buffers(count):
         return [
@@ -541,18 +543,17 @@
 
     adapters = down_maps[1:], query_maps[1:], value_maps[1:]
     weight_buf, weight_semaphores = weight_buffers(cut)
+    pieces = steps * rows // PIECE
     normed, first_qkv, places, *messages = pl.pallas_call(
         functools.partial(
-            norm_pack_project_kernel, chunk_steps, rows, flow_most, lanes, 2 * pieces, 1
+            norm_pack_project_kernel, parts[1], rows, flow_most, lanes, pieces, first_rows
         ),
         in_specs=[in_hbm] * 3 + [VMEM] + [in_hbm] * 3,
         out_specs=[VMEM] * (3 + lanes),
         out_shape=[jax.ShapeDtypeStruct((steps * rows, width), bf16), projected(cut)]
         + [places_shape]
-        + [message] * lanes,
-        scratch_shapes=row_buffers(steps * rows)[:-1]
-        + [pltpu.SemaphoreType.DMA((2 * pieces + 4,))]
-        + [weight_buf, weight_semaphores],
+        + messages_shape[1],
+        scratch_shapes=row_buffers(steps * rows, pieces) + [weight_buf, weight_semaphores],
         compiler_params=pltpu.CompilerParams(vmem_limit_bytes=PROJECT_LIMIT * MIB),
         cost_estimate=SMALL,
         name="norm_pack_project",
@@ -562,11 +563,11 @@
 
     def project(after):
         return pl.pallas_call(
-            functools.partial(project_kernel, cut),
+            functools.partial(project_kernel, cut * len(qkv)),
             in_specs=[VMEM, VMEM, in_hbm],
             out_specs=VMEM,
-            out_shape=projected(blocks - cut),
-            scratch_shapes=weight_buffers(blocks - cut),
+            out_shape=projected(cut),
+            scratch_shapes=weight_buffers(cut),
             compiler_params=pltpu.CompilerParams(vmem_limit_bytes=PROJECT_LIMIT * MIB),
             cost_estimate=SMALL,
             name="project",
@@ -577,15 +578,19 @@
             functools.partial(down_kernel, lanes, spots),
             in_specs=[VMEM] * (lanes + subs),
             out_specs=VMEM,
-            out_shape=jax.ShapeDtypeStruct((lanes * per_message, 2 * ADAPTER_RANK), f32),
+            out_shape=jax.ShapeDtypeStruct(
+                (lanes * parts[chunk] * spots, 2 * ADAPTER_RANK), f32
+            ),
             compiler_params=pltpu.CompilerParams(vmem_limit_bytes=16 * MIB),
             cost_estimate=SMALL,
             name="down",
-        )(held(arrived[chunk][0], after), *arrived[chunk][1:], *down_maps)
+        )(*arrived[chunk][:0:-1], held(arrived[chunk][0], after), *down_maps)
         return from_others(partial_latent, "heads")
 
-    def up(partials, after):
-        message = jax.ShapeDtypeStruct((per_message, query_columns + value_columns), bf16)
+    def up(chunk, partials, after):
+        message = jax.ShapeDtypeStruct(
+            (parts[chunk] * spots, query_columns + value_columns), bf16
+        )
         messages = pl.pallas_call(
             functools.partial(up_kernel, heads, subs, spots),
             in_specs=[VMEM] * (heads + 2 * subs),
@@ -610,28 +615,28 @@
     after = qkv
     for chunk in range(chunks):
         partials = down(chunk, after)
-        if chunk:
-            qkv.append(project(partials[0]))
-        after = up(partials, qkv)
+        qkv.append(project(partials[0]))
+        after = up(chunk, partials, qkv)
         messages = list(after)
-        if chunk:
-            for lane in range(1, lanes):
-                messages[lane] = held(messages[lane], returned[-1][lane])
+        ahead = returned[-1] if chunk else arrived[-1]
+        for lane in range(1, lanes):
+            messages[lane] = held(messages[lane], ahead[lane:])
         returned.append(traded(messages, "streams"))
 
     length_row = cache_fill_length.reshape(1, rows)
-    block = flow_most * chunk_steps
     earlier, along, alongs = [], [], []
     for chunk in range(chunks):
         last = chunk == chunks - 1
-        message = jax.ShapeDtypeStruct((subs * block, query_columns), bf16)
+        begin, part = sum(parts[:chunk]), parts[chunk]
+        chunk_rows = part * rows
+        message = jax.ShapeDtypeStruct((subs * flow_most * part, query_columns), bf16)
         fresh = jax.ShapeDtypeStruct((chunk_rows, 2 * value_columns), f32)
-        rows_of = lambda shape: pl.BlockSpec(shape, lambda i, chunk=chunk: (chunk, 0))
+        rows_of = lambda shape: pl.BlockSpec(shape, lambda i, place=begin // part: (place, 0))
         results = pl.pallas_call(
             functools.partial(
                 attend_kernel,
-                chunk * chunk_steps,
-                chunk_steps,
+                begin,
+                part,
                 rows,
                 cache,
                 groups,
@@ -644,7 +649,7 @@
             + [rows_of((chunk_rows, HEAD_WIDTH))] * 2
             + [whole(rotated_key_cache.shape)] * 2
             + [rows_of((chunk_rows, part.shape[1])) for part in qkv]
-            + [whole((per_message, query_columns + value_columns))] * lanes
+            + [whole((part * spots, query_columns + value_columns))] * lanes
             + [whole(block_rows.shape) for block_rows in earlier],
             out_specs=[whole(fresh.shape)] * (not last) + [whole(message.shape)] * lanes,
             out_shape=[fresh] * (not last) + [message] * lanes,
@@ -679,12 +684,14 @@
     landed, found = [], []
     for chunk, along in enumerate(alongs):
         base = len(landed)
+        block = flow_most * parts[chunk]
         landed += along
         where = [[(base + lane, 0)] for lane in range(lanes)]
         for shift in range(1, subs):
             pairs = [(core, core ^ shift) for core in range(subs)]
             span = slice(shift * block, (shift + 1) * block)
             if chunk < chunks - 1:
+                along = held(along[::-1], results)[::-1]
                 joined = jnp.concatenate([block_rows[span] for block_rows in along])
                 for lane in range(lanes):
                     where[lane].append((len(landed), lane * block))
@@ -696,7 +703,7 @@
         found.append(where)
 
     flow = pl.pallas_call(
-        functools.partial(place_kernel, found, lanes, subs, flow_most),
+        functools.partial(place_kernel, parts, found, lanes, subs, flow_most),
         in_specs=[VMEM] * len(landed),
         out_specs=VMEM,
         out_shape=jax.ShapeDtypeStruct((flow_lanes * flow_most, steps, query_columns), bf16),

time: 105 us -> 112 us (1.067)
  Pallas kernels: 31.4 us -> 34.3 us
  waiting for transfers between devices: 39.2 us -> 41.9 us
  starting transfers between devices: 32.8 us -> 34.6 us
    ppermute x18, waiting for transfers between devices: 37.9 us -> 41 us  [traded(): landed[shift] = lax.ppermute(blocks[shift], axes, pairs)]
    pallas_call x6 -> x7, Pallas kernels: 28.2 us -> 30.8 us  [the longest x2 8.8 us: project(): pl.pallas_call(functools.partial(project_kernel, cut * len(qkv)), in_spec...]
    ppermute x18, starting transfers between devices: 28.9 us -> 30.8 us  [traded(): landed[shift] = lax.ppermute(blocks[shift], axes, pairs)]
  transfers between devices with their start and end apart: 28 -> 28, of which waited for: 8 -> 8; matrix products, arithmetic and copies ran while one was open for 1% -> 1% of each run, Pallas kernels for 28% -> 29%
where the time goes in v11:
time: 112 us
  waiting for transfers between devices  41.9 us (37%)
  starting transfers between devices  34.6 us (31%)
  Pallas kernels  34.3 us (31%)
    ppermute x18, waiting for transfers between devices, traded(): landed[shift] = lax.ppermute(blocks[shift], axes, pairs)  41 us
    ppermute x18, starting transfers between devices, traded(): landed[shift] = lax.ppermute(blocks[shift], axes, pairs)  30.8 us
    pallas_call x2, Pallas kernels, project(): pl.pallas_call(functools.partial(project_kernel, cut * len(qkv)), in_spec...  8.8 us
    pallas_call x1, Pallas kernels, on_device(): pl.pallas_call(functools.partial(norm_pack_project_kernel, parts[1], rows...  8.02 us
    pallas_call x2, Pallas kernels, on_device(): pl.pallas_call(functools.partial(attend_kernel, begin, part, rows, cache,...  7.89 us
    pallas_call x1, Pallas kernels, on_device(): pl.pallas_call(functools.partial(norm_pack_kernel, parts[0], rows, flow_m...  4.16 us
    ppermute x5, starting transfers between devices, from_others(): landed.append(lax.ppermute(block, axis, pairs))  3.2 us
    pallas_call x2, Pallas kernels, down(): pl.pallas_call(functools.partial(down_kernel, lanes, spots), in_specs=[VM...  2.33 us
  transfers between devices with their start and end apart: 28, of which 8 were waited for; matrix products, arithmetic and copies ran while one was open for 1% of the time, Pallas kernels for 29%

profile of v11, /device:TPU:0, one launch (start us, length us, event | category | flops | bytes accessed | tf_op | source)
XLA Modules:
  0.0 112.1 jit_solution(6433458020825562382)
XLA Ops:
  0.0 0.5 collective-permute-start
  0.6 0.1 collective-permute-start.1
  0.6 0.4 collective-permute-start.2
  1.1 4.2 %norm_and_pack.1 = (bf16[48,1792]{1,0:T(8,128)(2,1)}, bf16[48,1792]{1,0:T(8,128)(2,1)}, bf16[48,1792]{1,0:T(8,128)(2,1)}, bf16[48,1792]{1,0:T(8,128)(2,1)}) custom-call(s32[1,64]{1,0:T(1,128)} %bitcast.25, s32[1,32]{1,0:T(1,128)} %bitcast.27, s32[1,64]{1,0:T(1,128)} %bitcast.29, f32[28,128]{1,0:T(8,128)} %bitcast.21, bf16[256,3584]{1,0:T(8,128)(2,1)} %bitcast.10), custom_call_target="tpu_custom_call" | custom-call | flops 1 | bytes 1 | tf_op jit(solution)/shard_map/norm_and_pack/pallas_call | solution.py:516
  5.2 4.7 %collective-permute-start.6 = (bf16[48,1792]{1,0:T(8,128)(2,1)}, bf16[48,1792]{1,0:T(8,128)(2,1)S(1)}, u32[]{:S(2)}, u32[]{:S(2)}) collective-permute-start(bf16[48,1792]{1,0:T(8,128)(2,1)} %get-tuple-element.60), channel_id=1, source_target_pairs={{0,12},{4,8},{8,4},{12,0},{1,13},{5,9},{9,5},{13,1},{2,14},{6,10},... | collective-permute-start | bytes 516104 | tf_op jit(solution)/shard_map/ppermute | solution.py:429
  10.0 0.6 collective-permute-start.8
  10.7 0.0 copy-start.6
  10.7 8.0 %norm_pack_project.1 = (bf16[256,3584]{1,0:T(8,128)(2,1)S(1)}, f32[256,768]{1,0:T(8,128)S(1)}, s32[8,64]{1,0:T(8,128)S(1)}, bf16[16,1792]{1,0:T(8,128)(2,1)S(1)}...) custom-call(s32[1,64]{1,0:T(1,128)S(1)} %bitcast.26, ...), custom_call_target="tpu_custom_call" | custom-call | flops 1 | bytes 1 | tf_op jit(solution)/shard_map/norm_pack_project/pallas_call | solution.py:547
  18.8 3.8 %collective-permute-start.3 = (bf16[16,1792]{1,0:T(8,128)(2,1)S(1)}, bf16[16,1792]{1,0:T(8,128)(2,1)S(1)}, u32[]{:S(2)}, u32[]{:S(2)}) collective-permute-start(bf16[16,1792]{1,0:T(8,128)(2,1)S(1)} %get-tuple-element.63), channel_id=1, source_target_pairs={{0,12},{4,8},{8,4},{12,0},{1,13},{5,9},{9,5},{13,1},{2,14},{6,10},... | collective-permute-start | bytes 172040 | tf_op jit(solution)/shard_map/ppermute | solution.py:429
  22.6 0.6 collective-permute-start.5
  23.2 5.1 %collective-permute-done.7.refs_1_ = bf16[48,1792]{1,0:T(8,128)(2,1)S(1)} collective-permute-done((bf16[48,1792]{1,0:T(8,128)(2,1)}, bf16[48,1792]{1,0:T(8,128)(2,1)S(1)}, u32[]{:S(2)}, u32[]{:S(2)}) %collective-permute-start.7) | collective-permute-done | bytes 172064 | tf_op jit(solution)/shard_map/ppermute | solution.py:429
  28.4 1.6 %down.2.refs_0_ = f32[192,128]{1,0:T(8,128)S(1)} custom-call(bf16[48,1792]{1,0:T(8,128)(2,1)S(1)} %collective-permute-done.6.refs_0_, bf16[48,1792]{1,0:T(8,128)(2,1)S(1)} %collective-permute-done.7.refs_1_, bf16[48,1792]{1,0:T(8,128)(2,1)S(1)} %collective-permute-done.8.refs_2_, bf16[48,1792]{1,0:T(8,128)(2,1)S(1)} %copy-done.6, ...), custom_call_target="tpu_custom_call" | custom-call | flops 1 | bytes 1 | tf_op jit(solution)/shard_map/down/pallas_call | solution.py:577
  30.0 1.6 %collective-permute-start.9 = (f32[192,128]{1,0:T(8,128)S(1)}, f32[192,128]{1,0:T(8,128)S(1)}, u32[]{:S(2)}, u32[]{:S(2)}) collective-permute-start(f32[192,128]{1,0:T(8,128)S(1)} %down.2.refs_0_), channel_id=1, source_target_pairs={{0,2},{2,0},{1,3},{3,1},{4,6},{6,4},{5,7},{7,5},{8,10},{10,8},{9,1... | collective-permute-start | bytes 294920 | tf_op jit(solution)/shard_map/ppermute | solution.py:438
  31.6 4.4 %project.2.refs_7_ = f32[256,768]{1,0:T(8,128)S(1)} custom-call(bf16[256,3584]{1,0:T(8,128)(2,1)S(1)} %get-tuple-element.69.rows_ref, f32[18,128]{1,0:T(8,128)S(1)} %bitcast.19, bf16[3584,2304]{1,0:T(8,128)(2,1)} %weight_hbm.3), custom_call_target="tpu_custom_call" | custom-call | flops 1 | bytes 1 | tf_op jit(solution)/shard_map/project/pallas_call | solution.py:565
  36.1 0.6 up.2
  36.8 0.1 collective-permute-start.11
  36.8 3.0 %collective-permute-start.12 = (bf16[48,2048]{1,0:T(8,128)(2,1)S(1)}, bf16[48,2048]{1,0:T(8,128)(2,1)S(1)}, u32[]{:S(2)}, u32[]{:S(2)}) collective-permute-start(bf16[48,2048]{1,0:T(8,128)(2,1)S(1)} %get-tuple-element.85), channel_id=1, source_target_pairs={{0,8},{4,12},{8,0},{12,4},{1,9},{5,13},{9,1},{13,5},{2,10},{6,14},... | collective-permute-start | bytes 589832 | tf_op jit(solution)/shard_map/ppermute | solution.py:429
  39.8 1.4 %collective-permute-start.13 = (bf16[48,2048]{1,0:T(8,128)(2,1)S(1)}, bf16[48,2048]{1,0:T(8,128)(2,1)S(1)}, u32[]{:S(2)}, u32[]{:S(2)}) collective-permute-start(bf16[48,2048]{1,0:T(8,128)(2,1)S(1)} %get-tuple-element.86), channel_id=1, source_target_pairs={{0,12},{4,8},{8,4},{12,0},{1,13},{5,9},{9,5},{13,1},{2,14},{6,10},... | collective-permute-start | bytes 589832 | tf_op jit(solution)/shard_map/ppermute | solution.py:429
  41.2 0.1 compare_select_fusion
  41.3 0.7 down.3.refs_0_
  42.0 0.6 collective-permute-start.10
  42.6 0.1 add_convert_fusion
  42.7 4.4 %project.3.refs_8_ = f32[256,768]{1,0:T(8,128)S(1)} custom-call(bf16[256,3584]{1,0:T(8,128)(2,1)S(1)} %get-tuple-element.69.rows_ref, f32[18,128]{1,0:T(8,128)S(1)} %bitcast.20, bf16[3584,2304]{1,0:T(8,128)(2,1)} %weight_hbm.3), custom_call_target="tpu_custom_call" | custom-call | flops 1 | bytes 1 | tf_op jit(solution)/shard_map/project/pallas_call | solution.py:565
  47.0 0.0 copy-start.2
  47.1 0.5 up.3
  47.6 6.5 %collective-permute-done.12.refs_11_ = bf16[48,2048]{1,0:T(8,128)(2,1)S(1)} collective-permute-done((bf16[48,2048]{1,0:T(8,128)(2,1)S(1)}, bf16[48,2048]{1,0:T(8,128)(2,1)S(1)}, u32[]{:S(2)}, u32[]{:S(2)}) %collective-permute-start.12) | collective-permute-done | bytes 196640 | tf_op jit(solution)/shard_map/ppermute | solution.py:429
  54.1 2.7 %collective-permute-start.14 = (bf16[16,2048]{1,0:T(8,128)(2,1)S(1)}, bf16[16,2048]{1,0:T(8,128)(2,1)S(1)}, u32[]{:S(2)}, u32[]{:S(2)}) collective-permute-start(bf16[16,2048]{1,0:T(8,128)(2,1)S(1)} %get-tuple-element.89), channel_id=1, source_target_pairs={{0,4},{4,0},{8,12},{12,8},{1,5},{5,1},{9,13},{13,9},{2,6},{6,2},{1... | collective-permute-start | bytes 196616 | tf_op jit(solution)/shard_map/ppermute | solution.py:429
  56.8 1.0 collective-permute-start.15
  57.7 1.5 %collective-permute-start.16 = (bf16[16,2048]{1,0:T(8,128)(2,1)S(1)}, bf16[16,2048]{1,0:T(8,128)(2,1)S(1)}, u32[]{:S(2)}, u32[]{:S(2)}) collective-permute-start(bf16[16,2048]{1,0:T(8,128)(2,1)S(1)} %get-tuple-element.91), channel_id=1, source_target_pairs={{0,12},{4,8},{8,4},{12,0},{1,13},{5,9},{9,5},{13,1},{2,14},{6,10},... | collective-permute-start | bytes 196616 | tf_op jit(solution)/shard_map/ppermute | solution.py:429
  59.2 0.5 fusion
  59.8 4.9 %attend.2 = (f32[192,512]{1,0:T(8,128)S(1)}, bf16[96,1792]{1,0:T(8,128)(2,1)S(1)}, bf16[96,1792]{1,0:T(8,128)(2,1)S(1)}, bf16[96,1792]{1,0:T(8,128)(2,1)S(1)}, bf16[96,1792]{1,0:T(8,128)(2,1)S(1)}) custom-call(s32[8,64]{1,0:T(8,128)S(1)} %get-tuple-element.83.refs_0_, s32[1,64]{1,0:T(1,128)S(1)} %bitcast.23, f32[256,128]{1,0:T(8,128)S(1)} %get-tuple-element.110.refs_2_, ...), custom_call_target="tpu_custom_call" | custom-call | flops 1 | bytes 1 | tf_op jit(solution)/shard_map/attend/pallas_call | solution.py:635
  64.7 1.1 collective-permute-start.17
  65.8 1.9 %collective-permute-start.18 = (bf16[96,1792]{1,0:T(8,128)(2,1)S(1)}, bf16[96,1792]{1,0:T(8,128)(2,1)S(1)}, u32[]{:S(2)}, u32[]{:S(2)}) collective-permute-start(bf16[96,1792]{1,0:T(8,128)(2,1)S(1)} %get-tuple-element.94), channel_id=1, source_target_pairs={{0,8},{4,12},{8,0},{12,4},{1,9},{5,13},{9,1},{13,5},{2,10},{6,14},... | collective-permute-start | bytes 1032200 | tf_op jit(solution)/shard_map/ppermute | solution.py:429
  67.7 1.5 %collective-permute-start.19 = (bf16[96,1792]{1,0:T(8,128)(2,1)S(1)}, bf16[96,1792]{1,0:T(8,128)(2,1)S(1)}, u32[]{:S(2)}, u32[]{:S(2)}) collective-permute-start(bf16[96,1792]{1,0:T(8,128)(2,1)S(1)} %get-tuple-element.96), channel_id=1, source_target_pairs={{0,12},{4,8},{8,4},{12,0},{1,13},{5,9},{9,5},{13,1},{2,14},{6,10},... | collective-permute-start | bytes 1032200 | tf_op jit(solution)/shard_map/ppermute | solution.py:429
  69.1 3.0 %attend.3 = (bf16[32,1792]{1,0:T(8,128)(2,1)S(1)}, bf16[32,1792]{1,0:T(8,128)(2,1)S(1)}, bf16[32,1792]{1,0:T(8,128)(2,1)S(1)}, bf16[32,1792]{1,0:T(8,128)(2,1)S(1)}) custom-call(s32[8,64]{1,0:T(8,128)S(1)} %get-tuple-element.83.refs_0_, s32[1,64]{1,0:T(1,128)S(1)} %bitcast.24, f32[256,128]{1,0:T(8,128)S(1)} %get-tuple-element.110.refs_2_, ...), custom_call_target="tpu_custom_call" | custom-call | flops 1 | bytes 1 | tf_op jit(solution)/shard_map/attend/pallas_call | solution.py:635
  72.2 6.2 %collective-permute-done.17.refs_1_ = bf16[96,1792]{1,0:T(8,128)(2,1)S(1)} collective-permute-done((bf16[96,1792]{1,0:T(8,128)(2,1)S(1)}, bf16[96,1792]{1,0:T(8,128)(2,1)S(1)}, u32[]{:S(2)}, u32[]{:S(2)}) %collective-permute-start.17) | collective-permute-done | bytes 344096 | tf_op jit(solution)/shard_map/ppermute | solution.py:429
  78.3 14.0 %collective-permute-done.18.refs_2_ = bf16[96,1792]{1,0:T(8,128)(2,1)S(1)} collective-permute-done((bf16[96,1792]{1,0:T(8,128)(2,1)S(1)}, bf16[96,1792]{1,0:T(8,128)(2,1)S(1)}, u32[]{:S(2)}, u32[]{:S(2)}) %collective-permute-start.18) | collective-permute-done | bytes 344096 | tf_op jit(solution)/shard_map/ppermute | solution.py:429
  92.4 0.1 pad_maximum_fusion
  92.5 0.1 collective-permute-start.20
  92.5 4.3 %collective-permute-start.21 = (bf16[32,1792]{1,0:T(8,128)(2,1)S(1)}, bf16[32,1792]{1,0:T(8,128)(2,1)S(1)}, u32[]{:S(2)}, u32[]{:S(2)}) collective-permute-start(bf16[32,1792]{1,0:T(8,128)(2,1)S(1)} %get-tuple-element.100), channel_id=1, source_target_pairs={{0,4},{4,0},{8,12},{12,8},{1,5},{5,1},{9,13},{13,9},{2,6},{6,2},{1... | collective-permute-start | bytes 344072 | tf_op jit(solution)/shard_map/ppermute | solution.py:429
  96.9 1.3 %collective-permute-start.22 = (bf16[32,1792]{1,0:T(8,128)(2,1)S(1)}, bf16[32,1792]{1,0:T(8,128)(2,1)S(1)}, u32[]{:S(2)}, u32[]{:S(2)}) collective-permute-start(bf16[32,1792]{1,0:T(8,128)(2,1)S(1)} %get-tuple-element.102), channel_id=1, source_target_pairs={{0,8},{4,12},{8,0},{12,4},{1,9},{5,13},{9,1},{13,5},{2,10},{6,14},... | collective-permute-start | bytes 344072 | tf_op jit(solution)/shard_map/ppermute | solution.py:429
  98.1 1.4 %collective-permute-start.23 = (bf16[32,1792]{1,0:T(8,128)(2,1)S(1)}, bf16[32,1792]{1,0:T(8,128)(2,1)S(1)}, u32[]{:S(2)}, u32[]{:S(2)}) collective-permute-start(bf16[32,1792]{1,0:T(8,128)(2,1)S(1)} %get-tuple-element.104), channel_id=1, source_target_pairs={{0,12},{4,8},{8,4},{12,0},{1,13},{5,9},{9,5},{13,1},{2,14},{6,10},... | collective-permute-start | bytes 344072 | tf_op jit(solution)/shard_map/ppermute | solution.py:429
  99.5 1.1 collective-permute-done.21.refs_6_
  100.6 8.1 %collective-permute-done.22.refs_7_ = bf16[32,1792]{1,0:T(8,128)(2,1)S(1)} collective-permute-done((bf16[32,1792]{1,0:T(8,128)(2,1)S(1)}, bf16[32,1792]{1,0:T(8,128)(2,1)S(1)}, u32[]{:S(2)}, u32[]{:S(2)}) %collective-permute-start.22) | collective-permute-done | bytes 114720 | tf_op jit(solution)/shard_map/ppermute | solution.py:429
  108.7 0.5 collective-permute-start.27
  109.2 0.8 collective-permute-done.26.refs_11_
  110.0 0.2 collective-permute-done.27.refs_12_
  110.2 1.9 %place.1 = bf16[128,4,1792]{2,1,0:T(4,128)(2,1)} custom-call(bf16[96,1792]{1,0:T(8,128)(2,1)S(1)} %get-tuple-element.105.refs_0_, bf16[96,1792]{1,0:T(8,128)(2,1)S(1)} %collective-permute-done.17.refs_1_, bf16[96,1792]{1,0:T(8,128)(2,1)S(1)} %collective-permute-done.18.refs_2_, bf16[96,1792]{1,0:T(8,128)(2,1)S(1)} %collective-permute-done.19.refs_3_, ...), custom_call_target="tpu_custom_call" | custom-call | flops 1 | bytes 1 | tf_op jit(solution)/shard_map/place/pallas_call | solution.py:705
  (55 shorter events, 0.2 us)
Async XLA Ops:
  0.0 10.7 %copy-start.10 = (s32[64,1]{0,1:T(1,128)S(1)}, s32[64,1]{0,1:T(1,128)}, u32[]{:S(2)}) copy-start(s32[64,1]{0,1:T(1,128)} %param.17) | copy-start | bytes 772
  0.0 10.7 %copy-start.11 = (s32[32]{0:T(128)S(1)}, s32[32]{0:T(128)}, u32[]{:S(2)}) copy-start(s32[32]{0:T(128)} %param.18) | copy-start | bytes 388
  0.0 10.7 %copy-start.12 = (s32[64,1]{0,1:T(1,128)S(1)}, s32[64,1]{0,1:T(1,128)}, u32[]{:S(2)}) copy-start(s32[64,1]{0,1:T(1,128)} %param.25) | copy-start | bytes 772
  0.0 10.7 %copy-start.8 = (f32[3584]{0:T(1024)S(1)}, f32[3584]{0:T(1024)}, u32[]{:S(2)}) copy-start(f32[3584]{0:T(1024)} %param.14) | copy-start | bytes 43012
  0.0 10.7 %copy-start = (bf16[4,64,3584]{2,1,0:T(8,128)(2,1)S(1)}, bf16[4,64,3584]{2,1,0:T(8,128)(2,1)}, u32[]{:S(2)}) copy-start(bf16[4,64,3584]{2,1,0:T(8,128)(2,1)} %param.13) | copy-start | bytes 5505028
  0.0 10.6 %copy-start.9 = (s32[64]{0:T(128)S(1)}, s32[64]{0:T(128)}, u32[]{:S(2)}) copy-start(s32[64]{0:T(128)} %param.19) | copy-start | bytes 772
  0.0 10.7 %copy-start.7 = (f32[2304]{0:T(1024)S(1)}, f32[2304]{0:T(1024)}, u32[]{:S(2)}) copy-start(f32[2304]{0:T(1024)} %param.16) | copy-start | bytes 27652
  0.0 10.6 %collective-permute-start = (bf16[4,1792,128]{2,1,0:T(8,128)(2,1)}, bf16[4,1792,128]{2,1,0:T(8,128)(2,1)S(1)}, u32[]{:S(2)}, u32[]{:S(2)}) collective-permute-start(bf16[4,1792,128]{2,1,0:T(8,128)(2,1)} %refs_4_.5), channel_id=1, source_target_pairs={{0,1},{1,0},{2,3},{3,2},{4,5},{5,4},{6,7},{7,6},{8,9},{9,8},{10,11... | collective-permute-start | bytes 5505032 | tf_op jit(solution)/shard_map/ppermute | solution.py:438
  0.6 10.1 %collective-permute-start.1 = (bf16[256,1792]{1,0:T(8,128)(2,1)}, bf16[256,1792]{1,0:T(8,128)(2,1)S(1)}, u32[]{:S(2)}, u32[]{:S(2)}) collective-permute-start(bf16[256,1792]{1,0:T(8,128)(2,1)} %bitcast.12), channel_id=1, source_target_pairs={{0,1},{1,0},{2,3},{3,2},{4,5},{5,4},{6,7},{7,6},{8,9},{9,8},{10,11... | collective-permute-start | bytes 2752520 | tf_op jit(solution)/shard_map/ppermute | solution.py:438
  0.6 9.3 %collective-permute-start.2 = (bf16[256,256]{1,0:T(8,128)(2,1)}, bf16[256,256]{1,0:T(8,128)(2,1)S(1)}, u32[]{:S(2)}, u32[]{:S(2)}) collective-permute-start(bf16[256,256]{1,0:T(8,128)(2,1)} %bitcast.15), channel_id=1, source_target_pairs={{0,1},{1,0},{2,3},{3,2},{4,5},{5,4},{6,7},{7,6},{8,9},{9,8},{10,11... | collective-permute-start | bytes 393224 | tf_op jit(solution)/shard_map/ppermute | solution.py:438
  5.2 17.3 %collective-permute-start.6 = (bf16[48,1792]{1,0:T(8,128)(2,1)}, bf16[48,1792]{1,0:T(8,128)(2,1)S(1)}, u32[]{:S(2)}, u32[]{:S(2)}) collective-permute-start(bf16[48,1792]{1,0:T(8,128)(2,1)} %get-tuple-element.60), channel_id=1, source_target_pairs={{0,12},{4,8},{8,4},{12,0},{1,13},{5,9},{9,5},{13,1},{2,14},{6,10},... | collective-permute-start | bytes 516104 | tf_op jit(solution)/shard_map/ppermute | solution.py:429
  10.0 18.4 %collective-permute-start.7 = (bf16[48,1792]{1,0:T(8,128)(2,1)}, bf16[48,1792]{1,0:T(8,128)(2,1)S(1)}, u32[]{:S(2)}, u32[]{:S(2)}) collective-permute-start(bf16[48,1792]{1,0:T(8,128)(2,1)} %get-tuple-element.59), channel_id=1, source_target_pairs={{0,8},{4,12},{8,0},{12,4},{1,9},{5,13},{9,1},{13,5},{2,10},{6,14},... | collective-permute-start | bytes 516104 | tf_op jit(solution)/shard_map/ppermute | solution.py:429
  10.0 18.4 %collective-permute-start.8 = (bf16[48,1792]{1,0:T(8,128)(2,1)}, bf16[48,1792]{1,0:T(8,128)(2,1)S(1)}, u32[]{:S(2)}, u32[]{:S(2)}) collective-permute-start(bf16[48,1792]{1,0:T(8,128)(2,1)} %get-tuple-element.58), channel_id=1, source_target_pairs={{0,4},{4,0},{8,12},{12,8},{1,5},{5,1},{9,13},{13,9},{2,6},{6,2},{1... | collective-permute-start | bytes 516104 | tf_op jit(solution)/shard_map/ppermute | solution.py:429
  10.7 17.6 %copy-start.1 = (bf16[4,1792,128]{2,1,0:T(8,128)(2,1)S(1)}, bf16[4,1792,128]{2,1,0:T(8,128)(2,1)}, u32[]{:S(2)}) copy-start(bf16[4,1792,128]{2,1,0:T(8,128)(2,1)} %refs_4_.5) | copy-start | bytes 5505028
  10.7 17.6 %copy-start.6 = (bf16[48,1792]{1,0:T(8,128)(2,1)S(1)}, bf16[48,1792]{1,0:T(8,128)(2,1)}, u32[]{:S(2)}) copy-start(bf16[48,1792]{1,0:T(8,128)(2,1)} %get-tuple-element.68.refs_3_) | copy-start | bytes 516100
  18.8 18.0 %collective-permute-start.3 = (bf16[16,1792]{1,0:T(8,128)(2,1)S(1)}, bf16[16,1792]{1,0:T(8,128)(2,1)S(1)}, u32[]{:S(2)}, u32[]{:S(2)}) collective-permute-start(bf16[16,1792]{1,0:T(8,128)(2,1)S(1)} %get-tuple-element.63), channel_id=1, source_target_pairs={{0,12},{4,8},{8,4},{12,0},{1,13},{5,9},{9,5},{13,1},{2,14},{6,10},... | collective-permute-start | bytes 172040 | tf_op jit(solution)/shard_map/ppermute | solution.py:429
  22.6 14.2 %collective-permute-start.4 = (bf16[16,1792]{1,0:T(8,128)(2,1)S(1)}, bf16[16,1792]{1,0:T(8,128)(2,1)S(1)}, u32[]{:S(2)}, u32[]{:S(2)}) collective-permute-start(bf16[16,1792]{1,0:T(8,128)(2,1)S(1)} %get-tuple-element.64), channel_id=1, source_target_pairs={{0,8},{4,12},{8,0},{12,4},{1,9},{5,13},{9,1},{13,5},{2,10},{6,14},... | collective-permute-start | bytes 172040 | tf_op jit(solution)/shard_map/ppermute | solution.py:429
  22.6 14.2 %collective-permute-start.5 = (bf16[16,1792]{1,0:T(8,128)(2,1)S(1)}, bf16[16,1792]{1,0:T(8,128)(2,1)S(1)}, u32[]{:S(2)}, u32[]{:S(2)}) collective-permute-start(bf16[16,1792]{1,0:T(8,128)(2,1)S(1)} %get-tuple-element.65), channel_id=1, source_target_pairs={{0,4},{4,0},{8,12},{12,8},{1,5},{5,1},{9,13},{13,9},{2,6},{6,2},{1... | collective-permute-start | bytes 172040 | tf_op jit(solution)/shard_map/ppermute | solution.py:429
  30.0 6.0 %collective-permute-start.9 = (f32[192,128]{1,0:T(8,128)S(1)}, f32[192,128]{1,0:T(8,128)S(1)}, u32[]{:S(2)}, u32[]{:S(2)}) collective-permute-start(f32[192,128]{1,0:T(8,128)S(1)} %down.2.refs_0_), channel_id=1, source_target_pairs={{0,2},{2,0},{1,3},{3,1},{4,6},{6,4},{5,7},{7,5},{8,10},{10,8},{9,1... | collective-permute-start | bytes 294920 | tf_op jit(solution)/shard_map/ppermute | solution.py:438
  31.6 4.5 %copy-start.4 = (bf16[4,64,1792]{2,1,0:T(8,128)(2,1)S(1)}, bf16[4,64,1792]{2,1,0:T(8,128)(2,1)}, u32[]{:S(2)}) copy-start(bf16[4,64,1792]{2,1,0:T(8,128)(2,1)} %param.23) | copy-start | bytes 2752516
  31.6 4.5 %copy-start.5 = (bf16[4,64,256]{2,1,0:T(8,128)(2,1)S(1)}, bf16[4,64,256]{2,1,0:T(8,128)(2,1)}, u32[]{:S(2)}) copy-start(bf16[4,64,256]{2,1,0:T(8,128)(2,1)} %param.24) | copy-start | bytes 393220
  36.8 10.8 %collective-permute-start.11 = (bf16[48,2048]{1,0:T(8,128)(2,1)S(1)}, bf16[48,2048]{1,0:T(8,128)(2,1)S(1)}, u32[]{:S(2)}, u32[]{:S(2)}) collective-permute-start(bf16[48,2048]{1,0:T(8,128)(2,1)S(1)} %get-tuple-element.84), channel_id=1, source_target_pairs={{0,4},{4,0},{8,12},{12,8},{1,5},{5,1},{9,13},{13,9},{2,6},{6,2},{1... | collective-permute-start | bytes 589832 | tf_op jit(solution)/shard_map/ppermute | solution.py:429
  36.8 17.2 %collective-permute-start.12 = (bf16[48,2048]{1,0:T(8,128)(2,1)S(1)}, bf16[48,2048]{1,0:T(8,128)(2,1)S(1)}, u32[]{:S(2)}, u32[]{:S(2)}) collective-permute-start(bf16[48,2048]{1,0:T(8,128)(2,1)S(1)} %get-tuple-element.85), channel_id=1, source_target_pairs={{0,8},{4,12},{8,0},{12,4},{1,9},{5,13},{9,1},{13,5},{2,10},{6,14},... | collective-permute-start | bytes 589832 | tf_op jit(solution)/shard_map/ppermute | solution.py:429
  39.8 14.3 %collective-permute-start.13 = (bf16[48,2048]{1,0:T(8,128)(2,1)S(1)}, bf16[48,2048]{1,0:T(8,128)(2,1)S(1)}, u32[]{:S(2)}, u32[]{:S(2)}) collective-permute-start(bf16[48,2048]{1,0:T(8,128)(2,1)S(1)} %get-tuple-element.86), channel_id=1, source_target_pairs={{0,12},{4,8},{8,4},{12,0},{1,13},{5,9},{9,5},{13,1},{2,14},{6,10},... | collective-permute-start | bytes 589832 | tf_op jit(solution)/shard_map/ppermute | solution.py:429
  42.0 5.1 %collective-permute-start.10 = (f32[64,128]{1,0:T(8,128)S(1)}, f32[64,128]{1,0:T(8,128)S(1)}, u32[]{:S(2)}, u32[]{:S(2)}) collective-permute-start(f32[64,128]{1,0:T(8,128)S(1)} %down.3.refs_0_), channel_id=1, source_target_pairs={{0,2},{2,0},{1,3},{3,1},{4,6},{6,4},{5,7},{7,5},{8,10},{10,8},{9,1... | collective-permute-start | bytes 98312 | tf_op jit(solution)/shard_map/ppermute | solution.py:438
  47.0 12.7 %copy-start.2 = (bf16[64,32,256]{2,1,0:T(8,128)(2,1)S(1)}, bf16[64,32,256]{2,1,0:T(8,128)(2,1)}, u32[]{:S(2)}) copy-start(bf16[64,32,256]{2,1,0:T(8,128)(2,1)} %refs_4_.7) | copy-start | bytes 3145732
  47.0 12.7 %copy-start.3 = (bf16[64,32,256]{2,1,0:T(8,128)(2,1)S(1)}, bf16[64,32,256]{2,1,0:T(8,128)(2,1)}, u32[]{:S(2)}) copy-start(bf16[64,32,256]{2,1,0:T(8,128)(2,1)} %refs_5_.3) | copy-start | bytes 3145732
  54.1 10.6 %collective-permute-start.14 = (bf16[16,2048]{1,0:T(8,128)(2,1)S(1)}, bf16[16,2048]{1,0:T(8,128)(2,1)S(1)}, u32[]{:S(2)}, u32[]{:S(2)}) collective-permute-start(bf16[16,2048]{1,0:T(8,128)(2,1)S(1)} %get-tuple-element.89), channel_id=1, source_target_pairs={{0,4},{4,0},{8,12},{12,8},{1,5},{5,1},{9,13},{13,9},{2,6},{6,2},{1... | collective-permute-start | bytes 196616 | tf_op jit(solution)/shard_map/ppermute | solution.py:429
  56.8 7.9 %collective-permute-start.15 = (bf16[16,2048]{1,0:T(8,128)(2,1)S(1)}, bf16[16,2048]{1,0:T(8,128)(2,1)S(1)}, u32[]{:S(2)}, u32[]{:S(2)}) collective-permute-start(bf16[16,2048]{1,0:T(8,128)(2,1)S(1)} %get-tuple-element.90), channel_id=1, source_target_pairs={{0,8},{4,12},{8,0},{12,4},{1,9},{5,13},{9,1},{13,5},{2,10},{6,14},... | collective-permute-start | bytes 196616 | tf_op jit(solution)/shard_map/ppermute | solution.py:429
  57.7 6.9 %collective-permute-start.16 = (bf16[16,2048]{1,0:T(8,128)(2,1)S(1)}, bf16[16,2048]{1,0:T(8,128)(2,1)S(1)}, u32[]{:S(2)}, u32[]{:S(2)}) collective-permute-start(bf16[16,2048]{1,0:T(8,128)(2,1)S(1)} %get-tuple-element.91), channel_id=1, source_target_pairs={{0,12},{4,8},{8,4},{12,0},{1,13},{5,9},{9,5},{13,1},{2,14},{6,10},... | collective-permute-start | bytes 196616 | tf_op jit(solution)/shard_map/ppermute | solution.py:429
  64.7 13.7 %collective-permute-start.17 = (bf16[96,1792]{1,0:T(8,128)(2,1)S(1)}, bf16[96,1792]{1,0:T(8,128)(2,1)S(1)}, u32[]{:S(2)}, u32[]{:S(2)}) collective-permute-start(bf16[96,1792]{1,0:T(8,128)(2,1)S(1)} %get-tuple-element.92), channel_id=1, source_target_pairs={{0,4},{4,0},{8,12},{12,8},{1,5},{5,1},{9,13},{13,9},{2,6},{6,2},{1... | collective-permute-start | bytes 1032200 | tf_op jit(solution)/shard_map/ppermute | solution.py:429
  65.8 26.5 %collective-permute-start.18 = (bf16[96,1792]{1,0:T(8,128)(2,1)S(1)}, bf16[96,1792]{1,0:T(8,128)(2,1)S(1)}, u32[]{:S(2)}, u32[]{:S(2)}) collective-permute-start(bf16[96,1792]{1,0:T(8,128)(2,1)S(1)} %get-tuple-element.94), channel_id=1, source_target_pairs={{0,8},{4,12},{8,0},{12,4},{1,9},{5,13},{9,1},{13,5},{2,10},{6,14},... | collective-permute-start | bytes 1032200 | tf_op jit(solution)/shard_map/ppermute | solution.py:429
  67.7 24.7 %collective-permute-start.19 = (bf16[96,1792]{1,0:T(8,128)(2,1)S(1)}, bf16[96,1792]{1,0:T(8,128)(2,1)S(1)}, u32[]{:S(2)}, u32[]{:S(2)}) collective-permute-start(bf16[96,1792]{1,0:T(8,128)(2,1)S(1)} %get-tuple-element.96), channel_id=1, source_target_pairs={{0,12},{4,8},{8,4},{12,0},{1,13},{5,9},{9,5},{13,1},{2,14},{6,10},... | collective-permute-start | bytes 1032200 | tf_op jit(solution)/shard_map/ppermute | solution.py:429
  92.5 17.7 %collective-permute-start.20 = (bf16[192,1792]{1,0:T(8,128)(2,1)S(1)}, bf16[192,1792]{1,0:T(8,128)(2,1)S(1)}, u32[]{:S(2)}, u32[]{:S(2)}) collective-permute-start(bf16[192,1792]{1,0:T(8,128)(2,1)S(1)} %pad_maximum_fusion), channel_id=1, source_target_pairs={{0,1},{1,0},{2,3},{3,2},{4,5},{5,4},{6,7},{7,6},{8,9},{9,8},{10,11... | collective-permute-start | bytes 2064392 | tf_op jit(solution)/shard_map/ppermute | solution.py:698
  92.5 8.1 %collective-permute-start.21 = (bf16[32,1792]{1,0:T(8,128)(2,1)S(1)}, bf16[32,1792]{1,0:T(8,128)(2,1)S(1)}, u32[]{:S(2)}, u32[]{:S(2)}) collective-permute-start(bf16[32,1792]{1,0:T(8,128)(2,1)S(1)} %get-tuple-element.100), channel_id=1, source_target_pairs={{0,4},{4,0},{8,12},{12,8},{1,5},{5,1},{9,13},{13,9},{2,6},{6,2},{1... | collective-permute-start | bytes 344072 | tf_op jit(solution)/shard_map/ppermute | solution.py:429
  96.9 11.8 %collective-permute-start.22 = (bf16[32,1792]{1,0:T(8,128)(2,1)S(1)}, bf16[32,1792]{1,0:T(8,128)(2,1)S(1)}, u32[]{:S(2)}, u32[]{:S(2)}) collective-permute-start(bf16[32,1792]{1,0:T(8,128)(2,1)S(1)} %get-tuple-element.102), channel_id=1, source_target_pairs={{0,8},{4,12},{8,0},{12,4},{1,9},{5,13},{9,1},{13,5},{2,10},{6,14},... | collective-permute-start | bytes 344072 | tf_op jit(solution)/shard_map/ppermute | solution.py:429
  98.1 10.6 %collective-permute-start.23 = (bf16[32,1792]{1,0:T(8,128)(2,1)S(1)}, bf16[32,1792]{1,0:T(8,128)(2,1)S(1)}, u32[]{:S(2)}, u32[]{:S(2)}) collective-permute-start(bf16[32,1792]{1,0:T(8,128)(2,1)S(1)} %get-tuple-element.104), channel_id=1, source_target_pairs={{0,12},{4,8},{8,4},{12,0},{1,13},{5,9},{9,5},{13,1},{2,14},{6,10},... | collective-permute-start | bytes 344072 | tf_op jit(solution)/shard_map/ppermute | solution.py:429
  99.5 9.7 %collective-permute-start.24 = (bf16[32,1792]{1,0:T(8,128)(2,1)S(1)}, bf16[32,1792]{1,0:T(8,128)(2,1)S(1)}, u32[]{:S(2)}, u32[]{:S(2)}) collective-permute-start(bf16[32,1792]{1,0:T(8,128)(2,1)S(1)} %get-tuple-element.98.refs_5_), channel_id=1, source_target_pairs={{0,1},{1,0},{2,3},{3,2},{4,5},{5,4},{6,7},{7,6},{8,9},{9,8},{10,11... | collective-permute-start | bytes 344072 | tf_op jit(solution)/shard_map/ppermute | solution.py:702
  100.6 8.6 %collective-permute-start.25 = (bf16[32,1792]{1,0:T(8,128)(2,1)S(1)}, bf16[32,1792]{1,0:T(8,128)(2,1)S(1)}, u32[]{:S(2)}, u32[]{:S(2)}) collective-permute-start(bf16[32,1792]{1,0:T(8,128)(2,1)S(1)} %collective-permute-done.21.refs_6_), channel_id=1, source_target_pairs={{0,1},{1,0},{2,3},{3,2},{4,5},{5,4},{6,7},{7,6},{8,9},{9,8},{10,11... | collective-permute-start | bytes 344072 | tf_op jit(solution)/shard_map/ppermute | solution.py:702
  108.7 1.3 %collective-permute-start.26 = (bf16[32,1792]{1,0:T(8,128)(2,1)S(1)}, bf16[32,1792]{1,0:T(8,128)(2,1)S(1)}, u32[]{:S(2)}, u32[]{:S(2)}) collective-permute-start(bf16[32,1792]{1,0:T(8,128)(2,1)S(1)} %collective-permute-done.22.refs_7_), channel_id=1, source_target_pairs={{0,1},{1,0},{2,3},{3,2},{4,5},{5,4},{6,7},{7,6},{8,9},{9,8},{10,11... | collective-permute-start | bytes 344072 | tf_op jit(solution)/shard_map/ppermute | solution.py:702
  108.7 1.5 %collective-permute-start.27 = (bf16[32,1792]{1,0:T(8,128)(2,1)S(1)}, bf16[32,1792]{1,0:T(8,128)(2,1)S(1)}, u32[]{:S(2)}, u32[]{:S(2)}) collective-permute-start(bf16[32,1792]{1,0:T(8,128)(2,1)S(1)} %collective-permute-done.23.refs_8_), channel_id=1, source_target_pairs={{0,1},{1,0},{2,3},{3,2},{4,5},{5,4},{6,7},{7,6},{8,9},{9,8},{10,11... | collective-permute-start | bytes 344072 | tf_op jit(solution)/shard_map/ppermute | solution.py:702

commit v12 on v8

--- a/solution.py
+++ b/solution.py
@@ -194,7 +194,7 @@
 
 
 def down_kernel(lanes, spots, *refs):
-    message_refs, map_refs, partial_ref = refs[:lanes], refs[lanes:-1], refs[-1]
+    message_refs, map_refs, partial_ref = refs[:lanes][::-1], refs[lanes:-1], refs[-1]
     local_slots = map_refs[0].shape[0]
     rows = jnp.concatenate([ref[...] for ref in message_refs], axis=0)
     own_slot = row_slots(partial_ref.shape, spots)
@@ -248,7 +248,7 @@
 def attend_kernel(before, steps, rows, cache, groups, lanes, subs, last, *refs):
     places_ref, length_ref, cos_ref, sin_ref, key_ref, value_ref = refs[:6]
     qkv_refs, refs = refs[6:8], refs[8:]
-    delta_refs, refs = refs[:lanes], refs[lanes:]
+    delta_refs, refs = refs[:lanes][::-1], refs[lanes:]
     if before:
         earlier_ref, refs = refs[0], refs[1:]
     if not last:
@@ -395,7 +395,8 @@
 
 def place_kernel(found, lanes, subs, most, *refs):
     chunks = len(found)
-    out_ref = refs[-1]
+    *refs, out_ref = refs
+    refs = refs[::-1]
     steps = out_ref.shape[1]
     chunk_steps = steps // chunks
     block = most * chunk_steps
@@ -581,7 +582,7 @@
             compiler_params=pltpu.CompilerParams(vmem_limit_bytes=16 * MIB),
             cost_estimate=SMALL,
             name="down",
-        )(held(arrived[chunk][0], after), *arrived[chunk][1:], *down_maps)
+        )(*arrived[chunk][:0:-1], held(arrived[chunk][0], after), *down_maps)
         return from_others(partial_latent, "heads")
 
     def up(partials, after):
@@ -664,15 +665,15 @@
             rotated_key_cache,
             value_cache_rows,
             *qkv,
-            *returned[chunk],
+            *returned[chunk][::-1],
             *earlier,
         )
         if not last:
             earlier, results = [results[0]], results[1:]
         results = list(results)
-        ahead = along or returned[-1]
         for lane in range(1, lanes):
-            results[lane] = held(results[lane], ahead[1:])
+            if not alongs:
+                results[lane] = held(results[lane], returned[-1][1:])
         along = traded(results, "streams")
         alongs.append(along)
 
@@ -685,9 +686,9 @@
             pairs = [(core, core ^ shift) for core in range(subs)]
             span = slice(shift * block, (shift + 1) * block)
             if chunk < chunks - 1:
-                joined = jnp.concatenate([block_rows[span] for block_rows in along])
+                joined = jnp.concatenate([block_rows[span] for block_rows in along[::-1]])
                 for lane in range(lanes):
-                    where[lane].append((len(landed), lane * block))
+                    where[lane].append((len(landed), (lanes - 1 - lane) * block))
                 landed.append(lax.ppermute(joined, "sub", pairs))
             else:
                 for lane, block_rows in enumerate(along):
@@ -703,7 +704,7 @@
         compiler_params=pltpu.CompilerParams(vmem_limit_bytes=24 * MIB),
         cost_estimate=SMALL,
         name="place",
-    )(*landed)
+    )(*landed[::-1])
     return flow[None]
 
 

time: 102 us -> 101 us (level)
  waiting for transfers between devices: 35 us -> 21.7 us
  starting transfers between devices: 33.9 us -> 46.2 us
    ppermute x18, waiting for transfers between devices: 30 us -> 15.7 us  [traded(): landed[shift] = lax.ppermute(blocks[shift], axes, pairs)]
    ppermute x18, starting transfers between devices: 30 us -> 40.9 us  [traded(): landed[shift] = lax.ppermute(blocks[shift], axes, pairs)]
  transfers between devices with their start and end apart: 28 -> 28, of which waited for: 9 -> 7; matrix products, arithmetic and copies ran while one was open for 1% -> 1% of each run, Pallas kernels for 29% -> 29%
where the time goes in v12:
time: 101 us; the launch traced here: 100 us
  starting transfers between devices  46.2 us (46%)
  Pallas kernels  31.4 us (31%)
  waiting for transfers between devices  21.7 us (21%)
    ppermute x18, starting transfers between devices, traded(): landed[shift] = lax.ppermute(blocks[shift], axes, pairs)  40.9 us
    ppermute x18, waiting for transfers between devices, traded(): landed[shift] = lax.ppermute(blocks[shift], axes, pairs)  15.7 us
    pallas_call x1, Pallas kernels, on_device(): pl.pallas_call(functools.partial(norm_pack_project_kernel, chunk_steps, r...  8.69 us
    pallas_call x2, Pallas kernels, on_device(): pl.pallas_call(functools.partial(attend_kernel, chunk * chunk_steps, chun...  7.53 us
    pallas_call x1, Pallas kernels, project(): pl.pallas_call(functools.partial(project_kernel, cut), in_specs=[VMEM, VM...  6.56 us
    ppermute x5, waiting for transfers between devices, from_others(): landed.append(lax.ppermute(block, axis, pairs))  4.68 us
    ppermute x5, starting transfers between devices, from_others(): landed.append(lax.ppermute(block, axis, pairs))  4.16 us
    pallas_call x1, Pallas kernels, on_device(): pl.pallas_call(functools.partial(norm_pack_kernel, chunk_steps, rows, flo...  3.45 us
  transfers between devices with their start and end apart: 28, of which 7 were waited for; matrix products, arithmetic and copies ran while one was open for 1% of the time, Pallas kernels for 29%

profile of v12, /device:TPU:0, one launch (start us, length us, event | category | flops | bytes accessed | tf_op | source)
XLA Modules:
  0.0 100.5 jit_solution(4905773990281188215)
XLA Ops:
  0.0 0.5 collective-permute-start
  0.5 0.1 collective-permute-start.1
  0.6 0.4 collective-permute-start.2
  1.1 3.5 %norm_and_pack.1 = (bf16[32,1792]{1,0:T(8,128)(2,1)}, bf16[32,1792]{1,0:T(8,128)(2,1)}, bf16[32,1792]{1,0:T(8,128)(2,1)}, bf16[32,1792]{1,0:T(8,128)(2,1)}) custom-call(s32[1,64]{1,0:T(1,128)} %bitcast.22, s32[1,32]{1,0:T(1,128)} %bitcast.24, s32[1,64]{1,0:T(1,128)} %bitcast.26, f32[28,128]{1,0:T(8,128)} %bitcast.16, bf16[256,3584]{1,0:T(8,128)(2,1)} %bitcast.28), custom_call_target="tpu_custom_call" | custom-call | flops 1 | bytes 1 | tf_op jit(solution)/shard_map/norm_and_pack/pallas_call | solution.py:516
  4.5 4.7 %collective-permute-start.3 = (bf16[32,1792]{1,0:T(8,128)(2,1)}, bf16[32,1792]{1,0:T(8,128)(2,1)S(1)}, u32[]{:S(2)}, u32[]{:S(2)}) collective-permute-start(bf16[32,1792]{1,0:T(8,128)(2,1)} %get-tuple-element.49), channel_id=1, source_target_pairs={{0,12},{4,8},{8,4},{12,0},{1,13},{5,9},{9,5},{13,1},{2,14},{6,10},... | collective-permute-start | bytes 344072 | tf_op jit(solution)/shard_map/ppermute | solution.py:431
  9.3 0.6 collective-permute-start.5
  10.0 0.0 copy-start.8
  10.0 0.0 copy-start
  10.0 0.0 copy-start.5
  10.0 8.7 %norm_pack_project.1 = (bf16[256,3584]{1,0:T(8,128)(2,1)S(1)}, f32[256,1024]{1,0:T(8,128)S(1)}, s32[8,64]{1,0:T(8,128)S(1)}, bf16[32,1792]{1,0:T(8,128)(2,1)S(1)...) custom-call(s32[1,64]{1,0:T(1,128)S(1)} %bitcast.23, ...), custom_call_target="tpu_custom_call" | custom-call | flops 1 | bytes 1 | tf_op jit(solution)/shard_map/norm_pack_project/pallas_call | solution.py:545
  18.7 3.8 %collective-permute-start.7 = (bf16[32,1792]{1,0:T(8,128)(2,1)S(1)}, bf16[32,1792]{1,0:T(8,128)(2,1)S(1)}, u32[]{:S(2)}, u32[]{:S(2)}) collective-permute-start(bf16[32,1792]{1,0:T(8,128)(2,1)S(1)} %get-tuple-element.61), channel_id=1, source_target_pairs={{0,12},{4,8},{8,4},{12,0},{1,13},{5,9},{9,5},{13,1},{2,14},{6,10},... | collective-permute-start | bytes 344072 | tf_op jit(solution)/shard_map/ppermute | solution.py:431
  22.6 1.2 %down.2.refs_0_ = f32[128,128]{1,0:T(8,128)S(1)} custom-call(bf16[32,1792]{1,0:T(8,128)(2,1)S(1)} %collective-permute-done.3.refs_0_, bf16[32,1792]{1,0:T(8,128)(2,1)S(1)} %collective-permute-done.4.refs_1_, bf16[32,1792]{1,0:T(8,128)(2,1)S(1)} %collective-permute-done.5.refs_2_, bf16[32,1792]{1,0:T(8,128)(2,1)S(1)} %copy-done.5, ...), custom_call_target="tpu_custom_call" | custom-call | flops 1 | bytes 1 | tf_op jit(solution)/shard_map/down/pallas_call | solution.py:577
  23.7 1.6 %collective-permute-start.6 = (f32[128,128]{1,0:T(8,128)S(1)}, f32[128,128]{1,0:T(8,128)S(1)}, u32[]{:S(2)}, u32[]{:S(2)}) collective-permute-start(f32[128,128]{1,0:T(8,128)S(1)} %down.2.refs_0_), channel_id=1, source_target_pairs={{0,2},{2,0},{1,3},{3,1},{4,6},{6,4},{5,7},{7,5},{8,10},{10,8},{9,1... | collective-permute-start | bytes 196616 | tf_op jit(solution)/shard_map/ppermute | solution.py:440
  25.3 0.8 collective-permute-start.9
  26.1 2.0 %collective-permute-done.6.refs_1_ = f32[128,128]{1,0:T(8,128)S(1)} collective-permute-done((f32[128,128]{1,0:T(8,128)S(1)}, f32[128,128]{1,0:T(8,128)S(1)}, u32[]{:S(2)}, u32[]{:S(2)}) %collective-permute-start.6) | collective-permute-done | bytes 65568 | tf_op jit(solution)/shard_map/ppermute | solution.py:440
  28.1 0.5 up.2
  28.6 1.7 %collective-permute-start.11 = (bf16[32,2048]{1,0:T(8,128)(2,1)S(1)}, bf16[32,2048]{1,0:T(8,128)(2,1)S(1)}, u32[]{:S(2)}, u32[]{:S(2)}) collective-permute-start(bf16[32,2048]{1,0:T(8,128)(2,1)S(1)} %get-tuple-element.59), channel_id=1, source_target_pairs={{0,12},{4,8},{8,4},{12,0},{1,13},{5,9},{9,5},{13,1},{2,14},{6,10},... | collective-permute-start | bytes 393224 | tf_op jit(solution)/shard_map/ppermute | solution.py:431
  30.3 2.7 %collective-permute-start.15 = (bf16[32,2048]{1,0:T(8,128)(2,1)S(1)}, bf16[32,2048]{1,0:T(8,128)(2,1)S(1)}, u32[]{:S(2)}, u32[]{:S(2)}) collective-permute-start(bf16[32,2048]{1,0:T(8,128)(2,1)S(1)} %get-tuple-element.57), channel_id=1, source_target_pairs={{0,4},{4,0},{8,12},{12,8},{1,5},{5,1},{9,13},{13,9},{2,6},{6,2},{1... | collective-permute-start | bytes 393224 | tf_op jit(solution)/shard_map/ppermute | solution.py:431
  33.0 0.1 compare_select_fusion
  33.1 6.6 %project.1.refs_7_ = f32[256,1280]{1,0:T(8,128)S(1)} custom-call(bf16[256,3584]{1,0:T(8,128)(2,1)S(1)} %get-tuple-element.53.rows_ref, f32[18,128]{1,0:T(8,128)S(1)} %bitcast.19, bf16[3584,2304]{1,0:T(8,128)(2,1)} %weight_hbm.1), custom_call_target="tpu_custom_call" | custom-call | flops 1 | bytes 1 | tf_op jit(solution)/shard_map/project/pallas_call | solution.py:565
  39.7 1.1 %down.3.refs_0_ = f32[128,128]{1,0:T(8,128)S(1)} custom-call(bf16[32,1792]{1,0:T(8,128)(2,1)S(1)} %collective-permute-done.7.refs_0_, bf16[32,1792]{1,0:T(8,128)(2,1)S(1)} %collective-permute-done.8.refs_1_, bf16[32,1792]{1,0:T(8,128)(2,1)S(1)} %collective-permute-done.9.refs_2_, bf16[32,1792]{1,0:T(8,128)(2,1)S(1)} %get-tuple-element.65.refs_3_, ...), custom_call_target="tpu_custom_call" | custom-call | flops 1 | bytes 1 | tf_op jit(solution)/shard_map/down/pallas_call | solution.py:577
  40.8 0.0 copy-start.1
  40.8 1.6 %collective-permute-start.10 = (f32[128,128]{1,0:T(8,128)S(1)}, f32[128,128]{1,0:T(8,128)S(1)}, u32[]{:S(2)}, u32[]{:S(2)}) collective-permute-start(f32[128,128]{1,0:T(8,128)S(1)} %down.3.refs_0_), channel_id=1, source_target_pairs={{0,2},{2,0},{1,3},{3,1},{4,6},{6,4},{5,7},{7,5},{8,10},{10,8},{9,1... | collective-permute-start | bytes 196616 | tf_op jit(solution)/shard_map/ppermute | solution.py:440
  42.4 0.1 add_convert_fusion
  42.5 2.7 %collective-permute-done.10.refs_1_ = f32[128,128]{1,0:T(8,128)S(1)} collective-permute-done((f32[128,128]{1,0:T(8,128)S(1)}, f32[128,128]{1,0:T(8,128)S(1)}, u32[]{:S(2)}, u32[]{:S(2)}) %collective-permute-start.10) | collective-permute-done | bytes 65568 | tf_op jit(solution)/shard_map/ppermute | solution.py:440
  45.2 0.5 up.3
  45.7 0.1 collective-permute-start.16
  45.8 2.2 %collective-permute-start.14 = (bf16[32,2048]{1,0:T(8,128)(2,1)S(1)}, bf16[32,2048]{1,0:T(8,128)(2,1)S(1)}, u32[]{:S(2)}, u32[]{:S(2)}) collective-permute-start(bf16[32,2048]{1,0:T(8,128)(2,1)S(1)} %get-tuple-element.70), channel_id=1, source_target_pairs={{0,8},{4,12},{8,0},{12,4},{1,9},{5,13},{9,1},{13,5},{2,10},{6,14},... | collective-permute-start | bytes 393224 | tf_op jit(solution)/shard_map/ppermute | solution.py:431
  48.0 2.2 %collective-permute-start.12 = (bf16[32,2048]{1,0:T(8,128)(2,1)S(1)}, bf16[32,2048]{1,0:T(8,128)(2,1)S(1)}, u32[]{:S(2)}, u32[]{:S(2)}) collective-permute-start(bf16[32,2048]{1,0:T(8,128)(2,1)S(1)} %get-tuple-element.68), channel_id=1, source_target_pairs={{0,12},{4,8},{8,4},{12,0},{1,13},{5,9},{9,5},{13,1},{2,14},{6,10},... | collective-permute-start | bytes 393224 | tf_op jit(solution)/shard_map/ppermute | solution.py:431
  50.2 0.5 fusion
  50.7 3.8 %attend.2 = (f32[128,512]{1,0:T(8,128)S(1)}, bf16[64,1792]{1,0:T(8,128)(2,1)S(1)}, bf16[64,1792]{1,0:T(8,128)(2,1)S(1)}, bf16[64,1792]{1,0:T(8,128)(2,1)S(1)}, bf16[64,1792]{1,0:T(8,128)(2,1)S(1)}) custom-call(s32[8,64]{1,0:T(8,128)S(1)} %get-tuple-element.74.refs_0_, s32[1,64]{1,0:T(1,128)S(1)} %bitcast.20, f32[256,128]{1,0:T(8,128)S(1)} %get-tuple-element.88.refs_2_, ...), custom_call_target="tpu_custom_call" | custom-call | flops 1 | bytes 1 | tf_op jit(solution)/shard_map/attend/pallas_call | solution.py:631
  54.6 1.4 %collective-permute-done.14.refs_9_ = bf16[32,2048]{1,0:T(8,128)(2,1)S(1)} collective-permute-done((bf16[32,2048]{1,0:T(8,128)(2,1)S(1)}, bf16[32,2048]{1,0:T(8,128)(2,1)S(1)}, u32[]{:S(2)}, u32[]{:S(2)}) %collective-permute-start.14) | collective-permute-done | bytes 131104 | tf_op jit(solution)/shard_map/ppermute | solution.py:431
  56.0 2.0 %collective-permute-start.24 = (bf16[64,1792]{1,0:T(8,128)(2,1)S(1)}, bf16[64,1792]{1,0:T(8,128)(2,1)S(1)}, u32[]{:S(2)}, u32[]{:S(2)}) collective-permute-start(bf16[64,1792]{1,0:T(8,128)(2,1)S(1)} %get-tuple-element.81), channel_id=1, source_target_pairs={{0,12},{4,8},{8,4},{12,0},{1,13},{5,9},{9,5},{13,1},{2,14},{6,10},... | collective-permute-start | bytes 688136 | tf_op jit(solution)/shard_map/ppermute | solution.py:431
  58.0 4.1 %collective-permute-start.25 = (bf16[64,1792]{1,0:T(8,128)(2,1)S(1)}, bf16[64,1792]{1,0:T(8,128)(2,1)S(1)}, u32[]{:S(2)}, u32[]{:S(2)}) collective-permute-start(bf16[64,1792]{1,0:T(8,128)(2,1)S(1)} %get-tuple-element.83), channel_id=1, source_target_pairs={{0,8},{4,12},{8,0},{12,4},{1,9},{5,13},{9,1},{13,5},{2,10},{6,14},... | collective-permute-start | bytes 688136 | tf_op jit(solution)/shard_map/ppermute | solution.py:431
  62.2 0.3 collective-permute-start.26
  62.5 3.7 %attend.3 = (bf16[64,1792]{1,0:T(8,128)(2,1)S(1)}, bf16[64,1792]{1,0:T(8,128)(2,1)S(1)}, bf16[64,1792]{1,0:T(8,128)(2,1)S(1)}, bf16[64,1792]{1,0:T(8,128)(2,1)S(1)}) custom-call(s32[8,64]{1,0:T(8,128)S(1)} %get-tuple-element.74.refs_0_, s32[1,64]{1,0:T(1,128)S(1)} %bitcast.21, f32[256,128]{1,0:T(8,128)S(1)} %get-tuple-element.88.refs_2_, ...), custom_call_target="tpu_custom_call" | custom-call | flops 1 | bytes 1 | tf_op jit(solution)/shard_map/attend/pallas_call | solution.py:631
  66.2 2.4 %collective-permute-start.17 = (bf16[64,1792]{1,0:T(8,128)(2,1)S(1)}, bf16[64,1792]{1,0:T(8,128)(2,1)S(1)}, u32[]{:S(2)}, u32[]{:S(2)}) collective-permute-start(bf16[64,1792]{1,0:T(8,128)(2,1)S(1)} %get-tuple-element.76), channel_id=1, source_target_pairs={{0,12},{4,8},{8,4},{12,0},{1,13},{5,9},{9,5},{13,1},{2,14},{6,10},... | collective-permute-start | bytes 688136 | tf_op jit(solution)/shard_map/ppermute | solution.py:431
  68.6 0.8 collective-permute-start.19
  69.4 12.3 %collective-permute-start.21 = (bf16[64,1792]{1,0:T(8,128)(2,1)S(1)}, bf16[64,1792]{1,0:T(8,128)(2,1)S(1)}, u32[]{:S(2)}, u32[]{:S(2)}) collective-permute-start(bf16[64,1792]{1,0:T(8,128)(2,1)S(1)} %get-tuple-element.78), channel_id=1, source_target_pairs={{0,4},{4,0},{8,12},{12,8},{1,5},{5,1},{9,13},{13,9},{2,6},{6,2},{1... | collective-permute-start | bytes 688136 | tf_op jit(solution)/shard_map/ppermute | solution.py:431
  81.8 6.8 %collective-permute-done.25.refs_10_ = bf16[64,1792]{1,0:T(8,128)(2,1)S(1)} collective-permute-done((bf16[64,1792]{1,0:T(8,128)(2,1)S(1)}, bf16[64,1792]{1,0:T(8,128)(2,1)S(1)}, u32[]{:S(2)}, u32[]{:S(2)}) %collective-permute-start.25) | collective-permute-done | bytes 229408 | tf_op jit(solution)/shard_map/ppermute | solution.py:431
  88.6 0.1 collective-permute-start.27
  88.7 0.5 collective-permute-start.23
  89.2 0.1 collective-permute-start.18
  89.3 7.4 %collective-permute-done.19.refs_5_ = bf16[64,1792]{1,0:T(8,128)(2,1)S(1)} collective-permute-done((bf16[64,1792]{1,0:T(8,128)(2,1)S(1)}, bf16[64,1792]{1,0:T(8,128)(2,1)S(1)}, u32[]{:S(2)}, u32[]{:S(2)}) %collective-permute-start.19) | collective-permute-done | bytes 229408 | tf_op jit(solution)/shard_map/ppermute | solution.py:431
  96.7 0.5 collective-permute-start.22
  97.2 1.0 collective-permute-done.20.refs_1_
  98.2 0.3 collective-permute-done.22.refs_2_
  98.5 1.9 %place.1 = bf16[128,4,1792]{2,1,0:T(4,128)(2,1)} custom-call(bf16[64,1792]{1,0:T(8,128)(2,1)S(1)} %collective-permute-done.18.refs_0_, bf16[64,1792]{1,0:T(8,128)(2,1)S(1)} %collective-permute-done.20.refs_1_, bf16[64,1792]{1,0:T(8,128)(2,1)S(1)} %collective-permute-done.22.refs_2_, bf16[64,1792]{1,0:T(8,128)(2,1)S(1)} %collective-permute-done.23.refs_3_, ...), custom_call_target="tpu_custom_call" | custom-call | flops 1 | bytes 1 | tf_op jit(solution)/shard_map/place/pallas_call | solution.py:699
  (52 shorter events, 0.2 us)
Async XLA Ops:
  0.0 9.9 %copy-start.9 = (s32[64,1]{0,1:T(1,128)S(1)}, s32[64,1]{0,1:T(1,128)}, u32[]{:S(2)}) copy-start(s32[64,1]{0,1:T(1,128)} %param.17) | copy-start | bytes 772
  0.0 9.9 %copy-start.10 = (s32[32]{0:T(128)S(1)}, s32[32]{0:T(128)}, u32[]{:S(2)}) copy-start(s32[32]{0:T(128)} %param.18) | copy-start | bytes 388
  0.0 9.9 %copy-start.11 = (s32[64,1]{0,1:T(1,128)S(1)}, s32[64,1]{0,1:T(1,128)}, u32[]{:S(2)}) copy-start(s32[64,1]{0,1:T(1,128)} %param.25) | copy-start | bytes 772
  0.0 9.9 %copy-start.6 = (f32[3584]{0:T(1024)S(1)}, f32[3584]{0:T(1024)}, u32[]{:S(2)}) copy-start(f32[3584]{0:T(1024)} %param.14) | copy-start | bytes 43012
  0.0 9.9 %copy-start.7 = (f32[2304]{0:T(1024)S(1)}, f32[2304]{0:T(1024)}, u32[]{:S(2)}) copy-start(f32[2304]{0:T(1024)} %param.16) | copy-start | bytes 27652
  0.0 9.9 %collective-permute-start = (bf16[4,1792,128]{2,1,0:T(8,128)(2,1)}, bf16[4,1792,128]{2,1,0:T(8,128)(2,1)S(1)}, u32[]{:S(2)}, u32[]{:S(2)}) collective-permute-start(bf16[4,1792,128]{2,1,0:T(8,128)(2,1)} %refs_4_.5), channel_id=1, source_target_pairs={{0,1},{1,0},{2,3},{3,2},{4,5},{5,4},{6,7},{7,6},{8,9},{9,8},{10,11... | collective-permute-start | bytes 5505032 | tf_op jit(solution)/shard_map/ppermute | solution.py:440
  0.5 9.4 %collective-permute-start.1 = (bf16[256,1792]{1,0:T(8,128)(2,1)}, bf16[256,1792]{1,0:T(8,128)(2,1)S(1)}, u32[]{:S(2)}, u32[]{:S(2)}) collective-permute-start(bf16[256,1792]{1,0:T(8,128)(2,1)} %bitcast.10), channel_id=1, source_target_pairs={{0,1},{1,0},{2,3},{3,2},{4,5},{5,4},{6,7},{7,6},{8,9},{9,8},{10,11... | collective-permute-start | bytes 2752520 | tf_op jit(solution)/shard_map/ppermute | solution.py:440
  0.6 8.6 %collective-permute-start.2 = (bf16[256,256]{1,0:T(8,128)(2,1)}, bf16[256,256]{1,0:T(8,128)(2,1)S(1)}, u32[]{:S(2)}, u32[]{:S(2)}) collective-permute-start(bf16[256,256]{1,0:T(8,128)(2,1)} %bitcast.13), channel_id=1, source_target_pairs={{0,1},{1,0},{2,3},{3,2},{4,5},{5,4},{6,7},{7,6},{8,9},{9,8},{10,11... | collective-permute-start | bytes 393224 | tf_op jit(solution)/shard_map/ppermute | solution.py:440
  4.5 18.0 %collective-permute-start.3 = (bf16[32,1792]{1,0:T(8,128)(2,1)}, bf16[32,1792]{1,0:T(8,128)(2,1)S(1)}, u32[]{:S(2)}, u32[]{:S(2)}) collective-permute-start(bf16[32,1792]{1,0:T(8,128)(2,1)} %get-tuple-element.49), channel_id=1, source_target_pairs={{0,12},{4,8},{8,4},{12,0},{1,13},{5,9},{9,5},{13,1},{2,14},{6,10},... | collective-permute-start | bytes 344072 | tf_op jit(solution)/shard_map/ppermute | solution.py:431
  9.3 13.3 %collective-permute-start.4 = (bf16[32,1792]{1,0:T(8,128)(2,1)}, bf16[32,1792]{1,0:T(8,128)(2,1)S(1)}, u32[]{:S(2)}, u32[]{:S(2)}) collective-permute-start(bf16[32,1792]{1,0:T(8,128)(2,1)} %get-tuple-element.48), channel_id=1, source_target_pairs={{0,8},{4,12},{8,0},{12,4},{1,9},{5,13},{9,1},{13,5},{2,10},{6,14},... | collective-permute-start | bytes 344072 | tf_op jit(solution)/shard_map/ppermute | solution.py:431
  9.3 13.3 %collective-permute-start.5 = (bf16[32,1792]{1,0:T(8,128)(2,1)}, bf16[32,1792]{1,0:T(8,128)(2,1)S(1)}, u32[]{:S(2)}, u32[]{:S(2)}) collective-permute-start(bf16[32,1792]{1,0:T(8,128)(2,1)} %get-tuple-element.47), channel_id=1, source_target_pairs={{0,4},{4,0},{8,12},{12,8},{1,5},{5,1},{9,13},{13,9},{2,6},{6,2},{1... | collective-permute-start | bytes 344072 | tf_op jit(solution)/shard_map/ppermute | solution.py:431
  10.0 12.6 %copy-start.8 = (s32[64]{0:T(128)S(1)}, s32[64]{0:T(128)}, u32[]{:S(2)}) copy-start(s32[64]{0:T(128)} %param.19) | copy-start | bytes 772
  10.0 12.6 %copy-start = (bf16[4,1792,128]{2,1,0:T(8,128)(2,1)S(1)}, bf16[4,1792,128]{2,1,0:T(8,128)(2,1)}, u32[]{:S(2)}) copy-start(bf16[4,1792,128]{2,1,0:T(8,128)(2,1)} %refs_4_.5) | copy-start | bytes 5505028
  10.0 12.6 %copy-start.5 = (bf16[32,1792]{1,0:T(8,128)(2,1)S(1)}, bf16[32,1792]{1,0:T(8,128)(2,1)}, u32[]{:S(2)}) copy-start(bf16[32,1792]{1,0:T(8,128)(2,1)} %get-tuple-element.54.refs_3_) | copy-start | bytes 344068
  18.7 11.6 %collective-permute-start.7 = (bf16[32,1792]{1,0:T(8,128)(2,1)S(1)}, bf16[32,1792]{1,0:T(8,128)(2,1)S(1)}, u32[]{:S(2)}, u32[]{:S(2)}) collective-permute-start(bf16[32,1792]{1,0:T(8,128)(2,1)S(1)} %get-tuple-element.61), channel_id=1, source_target_pairs={{0,12},{4,8},{8,4},{12,0},{1,13},{5,9},{9,5},{13,1},{2,14},{6,10},... | collective-permute-start | bytes 344072 | tf_op jit(solution)/shard_map/ppermute | solution.py:431
  22.5 5.6 %copy-start.3 = (bf16[4,64,1792]{2,1,0:T(8,128)(2,1)S(1)}, bf16[4,64,1792]{2,1,0:T(8,128)(2,1)}, u32[]{:S(2)}) copy-start(bf16[4,64,1792]{2,1,0:T(8,128)(2,1)} %param.23) | copy-start | bytes 2752516
  22.5 5.6 %copy-start.4 = (bf16[4,64,256]{2,1,0:T(8,128)(2,1)S(1)}, bf16[4,64,256]{2,1,0:T(8,128)(2,1)}, u32[]{:S(2)}) copy-start(bf16[4,64,256]{2,1,0:T(8,128)(2,1)} %param.24) | copy-start | bytes 393220
  23.7 4.3 %collective-permute-start.6 = (f32[128,128]{1,0:T(8,128)S(1)}, f32[128,128]{1,0:T(8,128)S(1)}, u32[]{:S(2)}, u32[]{:S(2)}) collective-permute-start(f32[128,128]{1,0:T(8,128)S(1)} %down.2.refs_0_), channel_id=1, source_target_pairs={{0,2},{2,0},{1,3},{3,1},{4,6},{6,4},{5,7},{7,5},{8,10},{10,8},{9,1... | collective-permute-start | bytes 196616 | tf_op jit(solution)/shard_map/ppermute | solution.py:440
  25.3 14.4 %collective-permute-start.8 = (bf16[32,1792]{1,0:T(8,128)(2,1)S(1)}, bf16[32,1792]{1,0:T(8,128)(2,1)S(1)}, u32[]{:S(2)}, u32[]{:S(2)}) collective-permute-start(bf16[32,1792]{1,0:T(8,128)(2,1)S(1)} %get-tuple-element.62), channel_id=1, source_target_pairs={{0,8},{4,12},{8,0},{12,4},{1,9},{5,13},{9,1},{13,5},{2,10},{6,14},... | collective-permute-start | bytes 344072 | tf_op jit(solution)/shard_map/ppermute | solution.py:431
  25.3 14.4 %collective-permute-start.9 = (bf16[32,1792]{1,0:T(8,128)(2,1)S(1)}, bf16[32,1792]{1,0:T(8,128)(2,1)S(1)}, u32[]{:S(2)}, u32[]{:S(2)}) collective-permute-start(bf16[32,1792]{1,0:T(8,128)(2,1)S(1)} %get-tuple-element.63), channel_id=1, source_target_pairs={{0,4},{4,0},{8,12},{12,8},{1,5},{5,1},{9,13},{13,9},{2,6},{6,2},{1... | collective-permute-start | bytes 344072 | tf_op jit(solution)/shard_map/ppermute | solution.py:431
  28.6 19.4 %collective-permute-start.11 = (bf16[32,2048]{1,0:T(8,128)(2,1)S(1)}, bf16[32,2048]{1,0:T(8,128)(2,1)S(1)}, u32[]{:S(2)}, u32[]{:S(2)}) collective-permute-start(bf16[32,2048]{1,0:T(8,128)(2,1)S(1)} %get-tuple-element.59), channel_id=1, source_target_pairs={{0,12},{4,8},{8,4},{12,0},{1,13},{5,9},{9,5},{13,1},{2,14},{6,10},... | collective-permute-start | bytes 393224 | tf_op jit(solution)/shard_map/ppermute | solution.py:431
  30.3 15.5 %collective-permute-start.13 = (bf16[32,2048]{1,0:T(8,128)(2,1)S(1)}, bf16[32,2048]{1,0:T(8,128)(2,1)S(1)}, u32[]{:S(2)}, u32[]{:S(2)}) collective-permute-start(bf16[32,2048]{1,0:T(8,128)(2,1)S(1)} %get-tuple-element.58), channel_id=1, source_target_pairs={{0,8},{4,12},{8,0},{12,4},{1,9},{5,13},{9,1},{13,5},{2,10},{6,14},... | collective-permute-start | bytes 393224 | tf_op jit(solution)/shard_map/ppermute | solution.py:431
  30.3 15.4 %collective-permute-start.15 = (bf16[32,2048]{1,0:T(8,128)(2,1)S(1)}, bf16[32,2048]{1,0:T(8,128)(2,1)S(1)}, u32[]{:S(2)}, u32[]{:S(2)}) collective-permute-start(bf16[32,2048]{1,0:T(8,128)(2,1)S(1)} %get-tuple-element.57), channel_id=1, source_target_pairs={{0,4},{4,0},{8,12},{12,8},{1,5},{5,1},{9,13},{13,9},{2,6},{6,2},{1... | collective-permute-start | bytes 393224 | tf_op jit(solution)/shard_map/ppermute | solution.py:431
  40.8 9.9 %copy-start.1 = (bf16[64,32,256]{2,1,0:T(8,128)(2,1)S(1)}, bf16[64,32,256]{2,1,0:T(8,128)(2,1)}, u32[]{:S(2)}) copy-start(bf16[64,32,256]{2,1,0:T(8,128)(2,1)} %refs_4_.7) | copy-start | bytes 3145732
  40.8 9.9 %copy-start.2 = (bf16[64,32,256]{2,1,0:T(8,128)(2,1)S(1)}, bf16[64,32,256]{2,1,0:T(8,128)(2,1)}, u32[]{:S(2)}) copy-start(bf16[64,32,256]{2,1,0:T(8,128)(2,1)} %refs_5_.3) | copy-start | bytes 3145732
  40.8 4.3 %collective-permute-start.10 = (f32[128,128]{1,0:T(8,128)S(1)}, f32[128,128]{1,0:T(8,128)S(1)}, u32[]{:S(2)}, u32[]{:S(2)}) collective-permute-start(f32[128,128]{1,0:T(8,128)S(1)} %down.3.refs_0_), channel_id=1, source_target_pairs={{0,2},{2,0},{1,3},{3,1},{4,6},{6,4},{5,7},{7,5},{8,10},{10,8},{9,1... | collective-permute-start | bytes 196616 | tf_op jit(solution)/shard_map/ppermute | solution.py:440
  45.7 8.9 %collective-permute-start.16 = (bf16[32,2048]{1,0:T(8,128)(2,1)S(1)}, bf16[32,2048]{1,0:T(8,128)(2,1)S(1)}, u32[]{:S(2)}, u32[]{:S(2)}) collective-permute-start(bf16[32,2048]{1,0:T(8,128)(2,1)S(1)} %get-tuple-element.72), channel_id=1, source_target_pairs={{0,4},{4,0},{8,12},{12,8},{1,5},{5,1},{9,13},{13,9},{2,6},{6,2},{1... | collective-permute-start | bytes 393224 | tf_op jit(solution)/shard_map/ppermute | solution.py:431
  45.8 10.2 %collective-permute-start.14 = (bf16[32,2048]{1,0:T(8,128)(2,1)S(1)}, bf16[32,2048]{1,0:T(8,128)(2,1)S(1)}, u32[]{:S(2)}, u32[]{:S(2)}) collective-permute-start(bf16[32,2048]{1,0:T(8,128)(2,1)S(1)} %get-tuple-element.70), channel_id=1, source_target_pairs={{0,8},{4,12},{8,0},{12,4},{1,9},{5,13},{9,1},{13,5},{2,10},{6,14},... | collective-permute-start | bytes 393224 | tf_op jit(solution)/shard_map/ppermute | solution.py:431
  48.0 8.0 %collective-permute-start.12 = (bf16[32,2048]{1,0:T(8,128)(2,1)S(1)}, bf16[32,2048]{1,0:T(8,128)(2,1)S(1)}, u32[]{:S(2)}, u32[]{:S(2)}) collective-permute-start(bf16[32,2048]{1,0:T(8,128)(2,1)S(1)} %get-tuple-element.68), channel_id=1, source_target_pairs={{0,12},{4,8},{8,4},{12,0},{1,13},{5,9},{9,5},{13,1},{2,14},{6,10},... | collective-permute-start | bytes 393224 | tf_op jit(solution)/shard_map/ppermute | solution.py:431
  56.0 13.4 %collective-permute-start.24 = (bf16[64,1792]{1,0:T(8,128)(2,1)S(1)}, bf16[64,1792]{1,0:T(8,128)(2,1)S(1)}, u32[]{:S(2)}, u32[]{:S(2)}) collective-permute-start(bf16[64,1792]{1,0:T(8,128)(2,1)S(1)} %get-tuple-element.81), channel_id=1, source_target_pairs={{0,12},{4,8},{8,4},{12,0},{1,13},{5,9},{9,5},{13,1},{2,14},{6,10},... | collective-permute-start | bytes 688136 | tf_op jit(solution)/shard_map/ppermute | solution.py:431
  58.0 30.5 %collective-permute-start.25 = (bf16[64,1792]{1,0:T(8,128)(2,1)S(1)}, bf16[64,1792]{1,0:T(8,128)(2,1)S(1)}, u32[]{:S(2)}, u32[]{:S(2)}) collective-permute-start(bf16[64,1792]{1,0:T(8,128)(2,1)S(1)} %get-tuple-element.83), channel_id=1, source_target_pairs={{0,8},{4,12},{8,0},{12,4},{1,9},{5,13},{9,1},{13,5},{2,10},{6,14},... | collective-permute-start | bytes 688136 | tf_op jit(solution)/shard_map/ppermute | solution.py:431
  62.2 26.4 %collective-permute-start.26 = (bf16[64,1792]{1,0:T(8,128)(2,1)S(1)}, bf16[64,1792]{1,0:T(8,128)(2,1)S(1)}, u32[]{:S(2)}, u32[]{:S(2)}) collective-permute-start(bf16[64,1792]{1,0:T(8,128)(2,1)S(1)} %get-tuple-element.85), channel_id=1, source_target_pairs={{0,4},{4,0},{8,12},{12,8},{1,5},{5,1},{9,13},{13,9},{2,6},{6,2},{1... | collective-permute-start | bytes 688136 | tf_op jit(solution)/shard_map/ppermute | solution.py:431
  66.2 23.0 %collective-permute-start.17 = (bf16[64,1792]{1,0:T(8,128)(2,1)S(1)}, bf16[64,1792]{1,0:T(8,128)(2,1)S(1)}, u32[]{:S(2)}, u32[]{:S(2)}) collective-permute-start(bf16[64,1792]{1,0:T(8,128)(2,1)S(1)} %get-tuple-element.76), channel_id=1, source_target_pairs={{0,12},{4,8},{8,4},{12,0},{1,13},{5,9},{9,5},{13,1},{2,14},{6,10},... | collective-permute-start | bytes 688136 | tf_op jit(solution)/shard_map/ppermute | solution.py:431
  68.6 28.1 %collective-permute-start.19 = (bf16[64,1792]{1,0:T(8,128)(2,1)S(1)}, bf16[64,1792]{1,0:T(8,128)(2,1)S(1)}, u32[]{:S(2)}, u32[]{:S(2)}) collective-permute-start(bf16[64,1792]{1,0:T(8,128)(2,1)S(1)} %get-tuple-element.77), channel_id=1, source_target_pairs={{0,8},{4,12},{8,0},{12,4},{1,9},{5,13},{9,1},{13,5},{2,10},{6,14},... | collective-permute-start | bytes 688136 | tf_op jit(solution)/shard_map/ppermute | solution.py:431
  69.4 27.3 %collective-permute-start.21 = (bf16[64,1792]{1,0:T(8,128)(2,1)S(1)}, bf16[64,1792]{1,0:T(8,128)(2,1)S(1)}, u32[]{:S(2)}, u32[]{:S(2)}) collective-permute-start(bf16[64,1792]{1,0:T(8,128)(2,1)S(1)} %get-tuple-element.78), channel_id=1, source_target_pairs={{0,4},{4,0},{8,12},{12,8},{1,5},{5,1},{9,13},{13,9},{2,6},{6,2},{1... | collective-permute-start | bytes 688136 | tf_op jit(solution)/shard_map/ppermute | solution.py:431
  88.6 9.9 %collective-permute-start.27 = (bf16[128,1792]{1,0:T(8,128)(2,1)S(1)}, bf16[128,1792]{1,0:T(8,128)(2,1)S(1)}, u32[]{:S(2)}, u32[]{:S(2)}) collective-permute-start(bf16[128,1792]{1,0:T(8,128)(2,1)S(1)} %pad_maximum_fusion), channel_id=1, source_target_pairs={{0,1},{1,0},{2,3},{3,2},{4,5},{5,4},{6,7},{7,6},{8,9},{9,8},{10,11... | collective-permute-start | bytes 1376264 | tf_op jit(solution)/shard_map/ppermute | solution.py:692
  88.7 8.5 %collective-permute-start.23 = (bf16[64,1792]{1,0:T(8,128)(2,1)S(1)}, bf16[64,1792]{1,0:T(8,128)(2,1)S(1)}, u32[]{:S(2)}, u32[]{:S(2)}) collective-permute-start(bf16[64,1792]{1,0:T(8,128)(2,1)S(1)} %get-tuple-element.79.refs_7_), channel_id=1, source_target_pairs={{0,1},{1,0},{2,3},{3,2},{4,5},{5,4},{6,7},{7,6},{8,9},{9,8},{10,11... | collective-permute-start | bytes 688136 | tf_op jit(solution)/shard_map/ppermute | solution.py:696
  89.2 8.0 %collective-permute-start.18 = (bf16[64,1792]{1,0:T(8,128)(2,1)S(1)}, bf16[64,1792]{1,0:T(8,128)(2,1)S(1)}, u32[]{:S(2)}, u32[]{:S(2)}) collective-permute-start(bf16[64,1792]{1,0:T(8,128)(2,1)S(1)} %collective-permute-done.17.refs_4_), channel_id=1, source_target_pairs={{0,1},{1,0},{2,3},{3,2},{4,5},{5,4},{6,7},{7,6},{8,9},{9,8},{10,11... | collective-permute-start | bytes 688136 | tf_op jit(solution)/shard_map/ppermute | solution.py:696
  96.7 1.5 %collective-permute-start.20 = (bf16[64,1792]{1,0:T(8,128)(2,1)S(1)}, bf16[64,1792]{1,0:T(8,128)(2,1)S(1)}, u32[]{:S(2)}, u32[]{:S(2)}) collective-permute-start(bf16[64,1792]{1,0:T(8,128)(2,1)S(1)} %collective-permute-done.19.refs_5_), channel_id=1, source_target_pairs={{0,1},{1,0},{2,3},{3,2},{4,5},{5,4},{6,7},{7,6},{8,9},{9,8},{10,11... | collective-permute-start | bytes 688136 | tf_op jit(solution)/shard_map/ppermute | solution.py:696
  96.7 1.8 %collective-permute-start.22 = (bf16[64,1792]{1,0:T(8,128)(2,1)S(1)}, bf16[64,1792]{1,0:T(8,128)(2,1)S(1)}, u32[]{:S(2)}, u32[]{:S(2)}) collective-permute-start(bf16[64,1792]{1,0:T(8,128)(2,1)S(1)} %collective-permute-done.21.refs_6_), channel_id=1, source_target_pairs={{0,1},{1,0},{2,3},{3,2},{4,5},{5,4},{6,7},{7,6},{8,9},{9,8},{10,11... | collective-permute-start | bytes 688136 | tf_op jit(solution)/shard_map/ppermute | solution.py:696

commit v13 on v12

--- a/solution.py
+++ b/solution.py
@@ -610,9 +610,7 @@
     returned = []
     after = qkv
     for chunk in range(chunks):
-        if chunk:
-            qkv.append(project(after))
-        partials = down(chunk, qkv)
+        partials = down(chunk, after)
         after = up(partials, qkv)
         messages = list(after)
         if chunk:
@@ -620,6 +618,7 @@
                 messages[lane] = held(messages[lane], returned[-1][lane])
         returned.append(traded(messages, "streams"))
 
+    qkv.append(project(after))
     length_row = cache_fill_length.reshape(1, rows)
     block = flow_most * chunk_steps
     earlier, along, alongs = [], [], []

time: 101 us -> 103 us (1.020)
  waiting for transfers between devices: 21.7 us -> 25.7 us
  starting transfers between devices: 46.2 us -> 44.3 us
    ppermute x18, waiting for transfers between devices: 15.7 us -> 20.2 us  [traded(): landed[shift] = lax.ppermute(blocks[shift], axes, pairs)]
    ppermute x18, starting transfers between devices: 40.9 us -> 36.8 us  [traded(): landed[shift] = lax.ppermute(blocks[shift], axes, pairs)]
    ppermute x5, starting transfers between devices: 4.16 us -> 6.27 us  [from_others(): landed.append(lax.ppermute(block, axis, pairs))]
  transfers between devices with their start and end apart: 28 -> 28, of which waited for: 7 -> 8; matrix products, arithmetic and copies ran while one was open for 1% -> 1% of each run, Pallas kernels for 29% -> 29%
where the time goes in v13:
time: 103 us
  starting transfers between devices  44.3 us (43%)
  Pallas kernels  31.5 us (31%)
  waiting for transfers between devices  25.7 us (25%)
    ppermute x18, starting transfers between devices, traded(): landed[shift] = lax.ppermute(blocks[shift], axes, pairs)  36.8 us
    ppermute x18, waiting for transfers between devices, traded(): landed[shift] = lax.ppermute(blocks[shift], axes, pairs)  20.2 us
    pallas_call x1, Pallas kernels, on_device(): pl.pallas_call(functools.partial(norm_pack_project_kernel, chunk_steps, r...  8.69 us
    pallas_call x2, Pallas kernels, on_device(): pl.pallas_call(functools.partial(attend_kernel, chunk * chunk_steps, chun...  7.45 us
    pallas_call x1, Pallas kernels, project(): pl.pallas_call(functools.partial(project_kernel, cut), in_specs=[VMEM, VM...  6.71 us
    ppermute x5, starting transfers between devices, from_others(): landed.append(lax.ppermute(block, axis, pairs))  6.27 us
    ppermute x5, waiting for transfers between devices, from_others(): landed.append(lax.ppermute(block, axis, pairs))  4.16 us
    pallas_call x1, Pallas kernels, on_device(): pl.pallas_call(functools.partial(norm_pack_kernel, chunk_steps, rows, flo...  3.45 us
  transfers between devices with their start and end apart: 28, of which 8 were waited for; matrix products, arithmetic and copies ran while one was open for 1% of the time, Pallas kernels for 29%

profile of v13, /device:TPU:0, one launch (start us, length us, event | category | flops | bytes accessed | tf_op | source)
XLA Modules:
  0.0 102.6 jit_solution(7261679859376141198)
XLA Ops:
  0.0 0.5 collective-permute-start
  0.5 0.1 collective-permute-start.1
  0.6 0.4 collective-permute-start.2
  1.1 3.5 %norm_and_pack.1 = (bf16[32,1792]{1,0:T(8,128)(2,1)}, bf16[32,1792]{1,0:T(8,128)(2,1)}, bf16[32,1792]{1,0:T(8,128)(2,1)}, bf16[32,1792]{1,0:T(8,128)(2,1)}) custom-call(s32[1,64]{1,0:T(1,128)} %bitcast.22, s32[1,32]{1,0:T(1,128)} %bitcast.24, s32[1,64]{1,0:T(1,128)} %bitcast.26, f32[28,128]{1,0:T(8,128)} %bitcast.16, bf16[256,3584]{1,0:T(8,128)(2,1)} %bitcast.28), custom_call_target="tpu_custom_call" | custom-call | flops 1 | bytes 1 | tf_op jit(solution)/shard_map/norm_and_pack/pallas_call | solution.py:516
  4.5 4.7 %collective-permute-start.6 = (bf16[32,1792]{1,0:T(8,128)(2,1)}, bf16[32,1792]{1,0:T(8,128)(2,1)S(1)}, u32[]{:S(2)}, u32[]{:S(2)}) collective-permute-start(bf16[32,1792]{1,0:T(8,128)(2,1)} %get-tuple-element.49), channel_id=1, source_target_pairs={{0,12},{4,8},{8,4},{12,0},{1,13},{5,9},{9,5},{13,1},{2,14},{6,10},... | collective-permute-start | bytes 344072 | tf_op jit(solution)/shard_map/ppermute | solution.py:431
  9.3 0.6 collective-permute-start.8
  10.0 0.0 copy-start.8
  10.0 0.0 copy-start
  10.0 0.0 copy-start.5
  10.0 8.7 %norm_pack_project.1 = (bf16[256,3584]{1,0:T(8,128)(2,1)S(1)}, f32[256,1024]{1,0:T(8,128)S(1)}, s32[8,64]{1,0:T(8,128)S(1)}, bf16[32,1792]{1,0:T(8,128)(2,1)S(1)...) custom-call(s32[1,64]{1,0:T(1,128)S(1)} %bitcast.23, ...), custom_call_target="tpu_custom_call" | custom-call | flops 1 | bytes 1 | tf_op jit(solution)/shard_map/norm_pack_project/pallas_call | solution.py:545
  18.7 3.8 %collective-permute-start.3 = (bf16[32,1792]{1,0:T(8,128)(2,1)S(1)}, bf16[32,1792]{1,0:T(8,128)(2,1)S(1)}, u32[]{:S(2)}, u32[]{:S(2)}) collective-permute-start(bf16[32,1792]{1,0:T(8,128)(2,1)S(1)} %get-tuple-element.54), channel_id=1, source_target_pairs={{0,12},{4,8},{8,4},{12,0},{1,13},{5,9},{9,5},{13,1},{2,14},{6,10},... | collective-permute-start | bytes 344072 | tf_op jit(solution)/shard_map/ppermute | solution.py:431
  22.6 1.2 %down.2.refs_0_ = f32[128,128]{1,0:T(8,128)S(1)} custom-call(bf16[32,1792]{1,0:T(8,128)(2,1)S(1)} %collective-permute-done.6.refs_0_, bf16[32,1792]{1,0:T(8,128)(2,1)S(1)} %collective-permute-done.7.refs_1_, bf16[32,1792]{1,0:T(8,128)(2,1)S(1)} %collective-permute-done.8.refs_2_, bf16[32,1792]{1,0:T(8,128)(2,1)S(1)} %copy-done.5, ...), custom_call_target="tpu_custom_call" | custom-call | flops 1 | bytes 1 | tf_op jit(solution)/shard_map/down/pallas_call | solution.py:577
  23.7 1.6 %collective-permute-start.9 = (f32[128,128]{1,0:T(8,128)S(1)}, f32[128,128]{1,0:T(8,128)S(1)}, u32[]{:S(2)}, u32[]{:S(2)}) collective-permute-start(f32[128,128]{1,0:T(8,128)S(1)} %down.2.refs_0_), channel_id=1, source_target_pairs={{0,2},{2,0},{1,3},{3,1},{4,6},{6,4},{5,7},{7,5},{8,10},{10,8},{9,1... | collective-permute-start | bytes 196616 | tf_op jit(solution)/shard_map/ppermute | solution.py:440
  25.3 0.8 collective-permute-start.5
  26.1 2.0 %collective-permute-done.9.refs_1_ = f32[128,128]{1,0:T(8,128)S(1)} collective-permute-done((f32[128,128]{1,0:T(8,128)S(1)}, f32[128,128]{1,0:T(8,128)S(1)}, u32[]{:S(2)}, u32[]{:S(2)}) %collective-permute-start.9) | collective-permute-done | bytes 65568 | tf_op jit(solution)/shard_map/ppermute | solution.py:440
  28.1 0.5 up.2
  28.6 1.7 %collective-permute-start.11 = (bf16[32,2048]{1,0:T(8,128)(2,1)S(1)}, bf16[32,2048]{1,0:T(8,128)(2,1)S(1)}, u32[]{:S(2)}, u32[]{:S(2)}) collective-permute-start(bf16[32,2048]{1,0:T(8,128)(2,1)S(1)} %get-tuple-element.63), channel_id=1, source_target_pairs={{0,12},{4,8},{8,4},{12,0},{1,13},{5,9},{9,5},{13,1},{2,14},{6,10},... | collective-permute-start | bytes 393224 | tf_op jit(solution)/shard_map/ppermute | solution.py:431
  30.3 2.7 %collective-permute-start.15 = (bf16[32,2048]{1,0:T(8,128)(2,1)S(1)}, bf16[32,2048]{1,0:T(8,128)(2,1)S(1)}, u32[]{:S(2)}, u32[]{:S(2)}) collective-permute-start(bf16[32,2048]{1,0:T(8,128)(2,1)S(1)} %get-tuple-element.61), channel_id=1, source_target_pairs={{0,4},{4,0},{8,12},{12,8},{1,5},{5,1},{9,13},{13,9},{2,6},{6,2},{1... | collective-permute-start | bytes 393224 | tf_op jit(solution)/shard_map/ppermute | solution.py:431
  33.0 0.1 compare_select_fusion
  33.1 3.3 %collective-permute-done.4.refs_1_ = bf16[32,1792]{1,0:T(8,128)(2,1)S(1)} collective-permute-done((bf16[32,1792]{1,0:T(8,128)(2,1)S(1)}, bf16[32,1792]{1,0:T(8,128)(2,1)S(1)}, u32[]{:S(2)}, u32[]{:S(2)}) %collective-permute-start.4) | collective-permute-done | bytes 114720 | tf_op jit(solution)/shard_map/ppermute | solution.py:431
  36.5 1.1 %down.3.refs_0_ = f32[128,128]{1,0:T(8,128)S(1)} custom-call(bf16[32,1792]{1,0:T(8,128)(2,1)S(1)} %collective-permute-done.3.refs_0_, bf16[32,1792]{1,0:T(8,128)(2,1)S(1)} %collective-permute-done.4.refs_1_, bf16[32,1792]{1,0:T(8,128)(2,1)S(1)} %collective-permute-done.5.refs_2_, bf16[32,1792]{1,0:T(8,128)(2,1)S(1)} %get-tuple-element.64.refs_3_, ...), custom_call_target="tpu_custom_call" | custom-call | flops 1 | bytes 1 | tf_op jit(solution)/shard_map/down/pallas_call | solution.py:577
  37.6 3.7 %collective-permute-start.10 = (f32[128,128]{1,0:T(8,128)S(1)}, f32[128,128]{1,0:T(8,128)S(1)}, u32[]{:S(2)}, u32[]{:S(2)}) collective-permute-start(f32[128,128]{1,0:T(8,128)S(1)} %down.3.refs_0_), channel_id=1, source_target_pairs={{0,2},{2,0},{1,3},{3,1},{4,6},{6,4},{5,7},{7,5},{8,10},{10,8},{9,1... | collective-permute-start | bytes 196616 | tf_op jit(solution)/shard_map/ppermute | solution.py:440
  41.3 0.1 add_convert_fusion
  41.3 2.2 %collective-permute-done.10.refs_1_ = f32[128,128]{1,0:T(8,128)S(1)} collective-permute-done((f32[128,128]{1,0:T(8,128)S(1)}, f32[128,128]{1,0:T(8,128)S(1)}, u32[]{:S(2)}, u32[]{:S(2)}) %collective-permute-start.10) | collective-permute-done | bytes 65568 | tf_op jit(solution)/shard_map/ppermute | solution.py:440
  43.5 0.5 up.3
  44.0 0.1 collective-permute-start.16
  44.1 1.6 %collective-permute-start.14 = (bf16[32,2048]{1,0:T(8,128)(2,1)S(1)}, bf16[32,2048]{1,0:T(8,128)(2,1)S(1)}, u32[]{:S(2)}, u32[]{:S(2)}) collective-permute-start(bf16[32,2048]{1,0:T(8,128)(2,1)S(1)} %get-tuple-element.72), channel_id=1, source_target_pairs={{0,8},{4,12},{8,0},{12,4},{1,9},{5,13},{9,1},{13,5},{2,10},{6,14},... | collective-permute-start | bytes 393224 | tf_op jit(solution)/shard_map/ppermute | solution.py:431
  45.7 2.8 %collective-permute-start.12 = (bf16[32,2048]{1,0:T(8,128)(2,1)S(1)}, bf16[32,2048]{1,0:T(8,128)(2,1)S(1)}, u32[]{:S(2)}, u32[]{:S(2)}) collective-permute-start(bf16[32,2048]{1,0:T(8,128)(2,1)S(1)} %get-tuple-element.71), channel_id=1, source_target_pairs={{0,12},{4,8},{8,4},{12,0},{1,13},{5,9},{9,5},{13,1},{2,14},{6,10},... | collective-permute-start | bytes 393224 | tf_op jit(solution)/shard_map/ppermute | solution.py:431
  48.5 0.5 fusion
  49.0 0.0 copy-start.1
  49.1 6.7 %project.1.refs_7_ = f32[256,1280]{1,0:T(8,128)S(1)} custom-call(bf16[256,3584]{1,0:T(8,128)(2,1)S(1)} %get-tuple-element.53.rows_ref, f32[18,128]{1,0:T(8,128)S(1)} %bitcast.19, bf16[3584,2304]{1,0:T(8,128)(2,1)} %weight_hbm.1), custom_call_target="tpu_custom_call" | custom-call | flops 1 | bytes 1 | tf_op jit(solution)/shard_map/project/pallas_call | solution.py:565
  55.8 3.8 %attend.2 = (f32[128,512]{1,0:T(8,128)S(1)}, bf16[64,1792]{1,0:T(8,128)(2,1)S(1)}, bf16[64,1792]{1,0:T(8,128)(2,1)S(1)}, bf16[64,1792]{1,0:T(8,128)(2,1)S(1)}, bf16[64,1792]{1,0:T(8,128)(2,1)S(1)}) custom-call(s32[8,64]{1,0:T(8,128)S(1)} %get-tuple-element.74.refs_0_, s32[1,64]{1,0:T(1,128)S(1)} %bitcast.20, f32[256,128]{1,0:T(8,128)S(1)} %get-tuple-element.88.refs_2_, ...), custom_call_target="tpu_custom_call" | custom-call | flops 1 | bytes 1 | tf_op jit(solution)/shard_map/attend/pallas_call | solution.py:630
  59.6 1.1 %collective-permute-start.24 = (bf16[64,1792]{1,0:T(8,128)(2,1)S(1)}, bf16[64,1792]{1,0:T(8,128)(2,1)S(1)}, u32[]{:S(2)}, u32[]{:S(2)}) collective-permute-start(bf16[64,1792]{1,0:T(8,128)(2,1)S(1)} %get-tuple-element.81), channel_id=1, source_target_pairs={{0,12},{4,8},{8,4},{12,0},{1,13},{5,9},{9,5},{13,1},{2,14},{6,10},... | collective-permute-start | bytes 688136 | tf_op jit(solution)/shard_map/ppermute | solution.py:431
  60.8 3.3 %collective-permute-start.26 = (bf16[64,1792]{1,0:T(8,128)(2,1)S(1)}, bf16[64,1792]{1,0:T(8,128)(2,1)S(1)}, u32[]{:S(2)}, u32[]{:S(2)}) collective-permute-start(bf16[64,1792]{1,0:T(8,128)(2,1)S(1)} %get-tuple-element.85), channel_id=1, source_target_pairs={{0,4},{4,0},{8,12},{12,8},{1,5},{5,1},{9,13},{13,9},{2,6},{6,2},{1... | collective-permute-start | bytes 688136 | tf_op jit(solution)/shard_map/ppermute | solution.py:431
  64.1 3.6 %attend.3 = (bf16[64,1792]{1,0:T(8,128)(2,1)S(1)}, bf16[64,1792]{1,0:T(8,128)(2,1)S(1)}, bf16[64,1792]{1,0:T(8,128)(2,1)S(1)}, bf16[64,1792]{1,0:T(8,128)(2,1)S(1)}) custom-call(s32[8,64]{1,0:T(8,128)S(1)} %get-tuple-element.74.refs_0_, s32[1,64]{1,0:T(1,128)S(1)} %bitcast.21, f32[256,128]{1,0:T(8,128)S(1)} %get-tuple-element.88.refs_2_, ...), custom_call_target="tpu_custom_call" | custom-call | flops 1 | bytes 1 | tf_op jit(solution)/shard_map/attend/pallas_call | solution.py:630
  67.8 1.1 %collective-permute-start.17 = (bf16[64,1792]{1,0:T(8,128)(2,1)S(1)}, bf16[64,1792]{1,0:T(8,128)(2,1)S(1)}, u32[]{:S(2)}, u32[]{:S(2)}) collective-permute-start(bf16[64,1792]{1,0:T(8,128)(2,1)S(1)} %get-tuple-element.76), channel_id=1, source_target_pairs={{0,12},{4,8},{8,4},{12,0},{1,13},{5,9},{9,5},{13,1},{2,14},{6,10},... | collective-permute-start | bytes 688136 | tf_op jit(solution)/shard_map/ppermute | solution.py:431
  68.9 0.4 collective-permute-start.19
  69.3 0.7 collective-permute-done.24.refs_9_
  70.0 12.0 %collective-permute-start.21 = (bf16[64,1792]{1,0:T(8,128)(2,1)S(1)}, bf16[64,1792]{1,0:T(8,128)(2,1)S(1)}, u32[]{:S(2)}, u32[]{:S(2)}) collective-permute-start(bf16[64,1792]{1,0:T(8,128)(2,1)S(1)} %get-tuple-element.78), channel_id=1, source_target_pairs={{0,4},{4,0},{8,12},{12,8},{1,5},{5,1},{9,13},{13,9},{2,6},{6,2},{1... | collective-permute-start | bytes 688136 | tf_op jit(solution)/shard_map/ppermute | solution.py:431
  82.0 8.5 %collective-permute-done.25.refs_10_ = bf16[64,1792]{1,0:T(8,128)(2,1)S(1)} collective-permute-done((bf16[64,1792]{1,0:T(8,128)(2,1)S(1)}, bf16[64,1792]{1,0:T(8,128)(2,1)S(1)}, u32[]{:S(2)}, u32[]{:S(2)}) %collective-permute-start.25) | collective-permute-done | bytes 229408 | tf_op jit(solution)/shard_map/ppermute | solution.py:431
  90.6 0.1 collective-permute-start.27
  90.7 0.5 collective-permute-start.23
  91.2 0.1 collective-permute-start.18
  91.2 7.6 %collective-permute-done.19.refs_5_ = bf16[64,1792]{1,0:T(8,128)(2,1)S(1)} collective-permute-done((bf16[64,1792]{1,0:T(8,128)(2,1)S(1)}, bf16[64,1792]{1,0:T(8,128)(2,1)S(1)}, u32[]{:S(2)}, u32[]{:S(2)}) %collective-permute-start.19) | collective-permute-done | bytes 229408 | tf_op jit(solution)/shard_map/ppermute | solution.py:431
  98.9 0.5 collective-permute-start.22
  99.4 1.0 collective-permute-done.20.refs_1_
  100.4 0.3 collective-permute-done.22.refs_2_
  100.7 1.9 %place.1 = bf16[128,4,1792]{2,1,0:T(4,128)(2,1)} custom-call(bf16[64,1792]{1,0:T(8,128)(2,1)S(1)} %collective-permute-done.18.refs_0_, bf16[64,1792]{1,0:T(8,128)(2,1)S(1)} %collective-permute-done.20.refs_1_, bf16[64,1792]{1,0:T(8,128)(2,1)S(1)} %collective-permute-done.22.refs_2_, bf16[64,1792]{1,0:T(8,128)(2,1)S(1)} %collective-permute-done.23.refs_3_, ...), custom_call_target="tpu_custom_call" | custom-call | flops 1 | bytes 1 | tf_op jit(solution)/shard_map/place/pallas_call | solution.py:698
  (52 shorter events, 0.2 us)
Async XLA Ops:
  0.0 9.9 %copy-start.9 = (s32[64,1]{0,1:T(1,128)S(1)}, s32[64,1]{0,1:T(1,128)}, u32[]{:S(2)}) copy-start(s32[64,1]{0,1:T(1,128)} %param.17) | copy-start | bytes 772
  0.0 9.9 %copy-start.10 = (s32[32]{0:T(128)S(1)}, s32[32]{0:T(128)}, u32[]{:S(2)}) copy-start(s32[32]{0:T(128)} %param.18) | copy-start | bytes 388
  0.0 9.9 %copy-start.11 = (s32[64,1]{0,1:T(1,128)S(1)}, s32[64,1]{0,1:T(1,128)}, u32[]{:S(2)}) copy-start(s32[64,1]{0,1:T(1,128)} %param.25) | copy-start | bytes 772
  0.0 9.9 %copy-start.6 = (f32[3584]{0:T(1024)S(1)}, f32[3584]{0:T(1024)}, u32[]{:S(2)}) copy-start(f32[3584]{0:T(1024)} %param.14) | copy-start | bytes 43012
  0.0 9.9 %copy-start.7 = (f32[2304]{0:T(1024)S(1)}, f32[2304]{0:T(1024)}, u32[]{:S(2)}) copy-start(f32[2304]{0:T(1024)} %param.16) | copy-start | bytes 27652
  0.0 9.9 %collective-permute-start = (bf16[4,1792,128]{2,1,0:T(8,128)(2,1)}, bf16[4,1792,128]{2,1,0:T(8,128)(2,1)S(1)}, u32[]{:S(2)}, u32[]{:S(2)}) collective-permute-start(bf16[4,1792,128]{2,1,0:T(8,128)(2,1)} %refs_4_.5), channel_id=1, source_target_pairs={{0,1},{1,0},{2,3},{3,2},{4,5},{5,4},{6,7},{7,6},{8,9},{9,8},{10,11... | collective-permute-start | bytes 5505032 | tf_op jit(solution)/shard_map/ppermute | solution.py:440
  0.5 9.4 %collective-permute-start.1 = (bf16[256,1792]{1,0:T(8,128)(2,1)}, bf16[256,1792]{1,0:T(8,128)(2,1)S(1)}, u32[]{:S(2)}, u32[]{:S(2)}) collective-permute-start(bf16[256,1792]{1,0:T(8,128)(2,1)} %bitcast.10), channel_id=1, source_target_pairs={{0,1},{1,0},{2,3},{3,2},{4,5},{5,4},{6,7},{7,6},{8,9},{9,8},{10,11... | collective-permute-start | bytes 2752520 | tf_op jit(solution)/shard_map/ppermute | solution.py:440
  0.6 8.6 %collective-permute-start.2 = (bf16[256,256]{1,0:T(8,128)(2,1)}, bf16[256,256]{1,0:T(8,128)(2,1)S(1)}, u32[]{:S(2)}, u32[]{:S(2)}) collective-permute-start(bf16[256,256]{1,0:T(8,128)(2,1)} %bitcast.13), channel_id=1, source_target_pairs={{0,1},{1,0},{2,3},{3,2},{4,5},{5,4},{6,7},{7,6},{8,9},{9,8},{10,11... | collective-permute-start | bytes 393224 | tf_op jit(solution)/shard_map/ppermute | solution.py:440
  4.5 18.0 %collective-permute-start.6 = (bf16[32,1792]{1,0:T(8,128)(2,1)}, bf16[32,1792]{1,0:T(8,128)(2,1)S(1)}, u32[]{:S(2)}, u32[]{:S(2)}) collective-permute-start(bf16[32,1792]{1,0:T(8,128)(2,1)} %get-tuple-element.49), channel_id=1, source_target_pairs={{0,12},{4,8},{8,4},{12,0},{1,13},{5,9},{9,5},{13,1},{2,14},{6,10},... | collective-permute-start | bytes 344072 | tf_op jit(solution)/shard_map/ppermute | solution.py:431
  9.3 13.3 %collective-permute-start.7 = (bf16[32,1792]{1,0:T(8,128)(2,1)}, bf16[32,1792]{1,0:T(8,128)(2,1)S(1)}, u32[]{:S(2)}, u32[]{:S(2)}) collective-permute-start(bf16[32,1792]{1,0:T(8,128)(2,1)} %get-tuple-element.48), channel_id=1, source_target_pairs={{0,8},{4,12},{8,0},{12,4},{1,9},{5,13},{9,1},{13,5},{2,10},{6,14},... | collective-permute-start | bytes 344072 | tf_op jit(solution)/shard_map/ppermute | solution.py:431
  9.3 13.3 %collective-permute-start.8 = (bf16[32,1792]{1,0:T(8,128)(2,1)}, bf16[32,1792]{1,0:T(8,128)(2,1)S(1)}, u32[]{:S(2)}, u32[]{:S(2)}) collective-permute-start(bf16[32,1792]{1,0:T(8,128)(2,1)} %get-tuple-element.47), channel_id=1, source_target_pairs={{0,4},{4,0},{8,12},{12,8},{1,5},{5,1},{9,13},{13,9},{2,6},{6,2},{1... | collective-permute-start | bytes 344072 | tf_op jit(solution)/shard_map/ppermute | solution.py:431
  10.0 12.6 %copy-start.8 = (s32[64]{0:T(128)S(1)}, s32[64]{0:T(128)}, u32[]{:S(2)}) copy-start(s32[64]{0:T(128)} %param.19) | copy-start | bytes 772
  10.0 12.6 %copy-start = (bf16[4,1792,128]{2,1,0:T(8,128)(2,1)S(1)}, bf16[4,1792,128]{2,1,0:T(8,128)(2,1)}, u32[]{:S(2)}) copy-start(bf16[4,1792,128]{2,1,0:T(8,128)(2,1)} %refs_4_.5) | copy-start | bytes 5505028
  10.0 12.6 %copy-start.5 = (bf16[32,1792]{1,0:T(8,128)(2,1)S(1)}, bf16[32,1792]{1,0:T(8,128)(2,1)}, u32[]{:S(2)}) copy-start(bf16[32,1792]{1,0:T(8,128)(2,1)} %get-tuple-element.58.refs_3_) | copy-start | bytes 344068
  18.7 11.6 %collective-permute-start.3 = (bf16[32,1792]{1,0:T(8,128)(2,1)S(1)}, bf16[32,1792]{1,0:T(8,128)(2,1)S(1)}, u32[]{:S(2)}, u32[]{:S(2)}) collective-permute-start(bf16[32,1792]{1,0:T(8,128)(2,1)S(1)} %get-tuple-element.54), channel_id=1, source_target_pairs={{0,12},{4,8},{8,4},{12,0},{1,13},{5,9},{9,5},{13,1},{2,14},{6,10},... | collective-permute-start | bytes 344072 | tf_op jit(solution)/shard_map/ppermute | solution.py:431
  22.5 5.6 %copy-start.3 = (bf16[4,64,1792]{2,1,0:T(8,128)(2,1)S(1)}, bf16[4,64,1792]{2,1,0:T(8,128)(2,1)}, u32[]{:S(2)}) copy-start(bf16[4,64,1792]{2,1,0:T(8,128)(2,1)} %param.23) | copy-start | bytes 2752516
  22.5 5.6 %copy-start.4 = (bf16[4,64,256]{2,1,0:T(8,128)(2,1)S(1)}, bf16[4,64,256]{2,1,0:T(8,128)(2,1)}, u32[]{:S(2)}) copy-start(bf16[4,64,256]{2,1,0:T(8,128)(2,1)} %param.24) | copy-start | bytes 393220
  23.7 4.3 %collective-permute-start.9 = (f32[128,128]{1,0:T(8,128)S(1)}, f32[128,128]{1,0:T(8,128)S(1)}, u32[]{:S(2)}, u32[]{:S(2)}) collective-permute-start(f32[128,128]{1,0:T(8,128)S(1)} %down.2.refs_0_), channel_id=1, source_target_pairs={{0,2},{2,0},{1,3},{3,1},{4,6},{6,4},{5,7},{7,5},{8,10},{10,8},{9,1... | collective-permute-start | bytes 196616 | tf_op jit(solution)/shard_map/ppermute | solution.py:440
  25.3 11.2 %collective-permute-start.4 = (bf16[32,1792]{1,0:T(8,128)(2,1)S(1)}, bf16[32,1792]{1,0:T(8,128)(2,1)S(1)}, u32[]{:S(2)}, u32[]{:S(2)}) collective-permute-start(bf16[32,1792]{1,0:T(8,128)(2,1)S(1)} %get-tuple-element.55), channel_id=1, source_target_pairs={{0,8},{4,12},{8,0},{12,4},{1,9},{5,13},{9,1},{13,5},{2,10},{6,14},... | collective-permute-start | bytes 344072 | tf_op jit(solution)/shard_map/ppermute | solution.py:431
  25.3 11.2 %collective-permute-start.5 = (bf16[32,1792]{1,0:T(8,128)(2,1)S(1)}, bf16[32,1792]{1,0:T(8,128)(2,1)S(1)}, u32[]{:S(2)}, u32[]{:S(2)}) collective-permute-start(bf16[32,1792]{1,0:T(8,128)(2,1)S(1)} %get-tuple-element.56), channel_id=1, source_target_pairs={{0,4},{4,0},{8,12},{12,8},{1,5},{5,1},{9,13},{13,9},{2,6},{6,2},{1... | collective-permute-start | bytes 344072 | tf_op jit(solution)/shard_map/ppermute | solution.py:431
  28.6 17.2 %collective-permute-start.11 = (bf16[32,2048]{1,0:T(8,128)(2,1)S(1)}, bf16[32,2048]{1,0:T(8,128)(2,1)S(1)}, u32[]{:S(2)}, u32[]{:S(2)}) collective-permute-start(bf16[32,2048]{1,0:T(8,128)(2,1)S(1)} %get-tuple-element.63), channel_id=1, source_target_pairs={{0,12},{4,8},{8,4},{12,0},{1,13},{5,9},{9,5},{13,1},{2,14},{6,10},... | collective-permute-start | bytes 393224 | tf_op jit(solution)/shard_map/ppermute | solution.py:431
  30.3 13.8 %collective-permute-start.13 = (bf16[32,2048]{1,0:T(8,128)(2,1)S(1)}, bf16[32,2048]{1,0:T(8,128)(2,1)S(1)}, u32[]{:S(2)}, u32[]{:S(2)}) collective-permute-start(bf16[32,2048]{1,0:T(8,128)(2,1)S(1)} %get-tuple-element.62), channel_id=1, source_target_pairs={{0,8},{4,12},{8,0},{12,4},{1,9},{5,13},{9,1},{13,5},{2,10},{6,14},... | collective-permute-start | bytes 393224 | tf_op jit(solution)/shard_map/ppermute | solution.py:431
  30.3 13.7 %collective-permute-start.15 = (bf16[32,2048]{1,0:T(8,128)(2,1)S(1)}, bf16[32,2048]{1,0:T(8,128)(2,1)S(1)}, u32[]{:S(2)}, u32[]{:S(2)}) collective-permute-start(bf16[32,2048]{1,0:T(8,128)(2,1)S(1)} %get-tuple-element.61), channel_id=1, source_target_pairs={{0,4},{4,0},{8,12},{12,8},{1,5},{5,1},{9,13},{13,9},{2,6},{6,2},{1... | collective-permute-start | bytes 393224 | tf_op jit(solution)/shard_map/ppermute | solution.py:431
  37.6 5.9 %collective-permute-start.10 = (f32[128,128]{1,0:T(8,128)S(1)}, f32[128,128]{1,0:T(8,128)S(1)}, u32[]{:S(2)}, u32[]{:S(2)}) collective-permute-start(f32[128,128]{1,0:T(8,128)S(1)} %down.3.refs_0_), channel_id=1, source_target_pairs={{0,2},{2,0},{1,3},{3,1},{4,6},{6,4},{5,7},{7,5},{8,10},{10,8},{9,1... | collective-permute-start | bytes 196616 | tf_op jit(solution)/shard_map/ppermute | solution.py:440
  44.0 15.6 %collective-permute-start.16 = (bf16[32,2048]{1,0:T(8,128)(2,1)S(1)}, bf16[32,2048]{1,0:T(8,128)(2,1)S(1)}, u32[]{:S(2)}, u32[]{:S(2)}) collective-permute-start(bf16[32,2048]{1,0:T(8,128)(2,1)S(1)} %get-tuple-element.73), channel_id=1, source_target_pairs={{0,4},{4,0},{8,12},{12,8},{1,5},{5,1},{9,13},{13,9},{2,6},{6,2},{1... | collective-permute-start | bytes 393224 | tf_op jit(solution)/shard_map/ppermute | solution.py:431
  44.1 15.5 %collective-permute-start.14 = (bf16[32,2048]{1,0:T(8,128)(2,1)S(1)}, bf16[32,2048]{1,0:T(8,128)(2,1)S(1)}, u32[]{:S(2)}, u32[]{:S(2)}) collective-permute-start(bf16[32,2048]{1,0:T(8,128)(2,1)S(1)} %get-tuple-element.72), channel_id=1, source_target_pairs={{0,8},{4,12},{8,0},{12,4},{1,9},{5,13},{9,1},{13,5},{2,10},{6,14},... | collective-permute-start | bytes 393224 | tf_op jit(solution)/shard_map/ppermute | solution.py:431
  45.7 13.9 %collective-permute-start.12 = (bf16[32,2048]{1,0:T(8,128)(2,1)S(1)}, bf16[32,2048]{1,0:T(8,128)(2,1)S(1)}, u32[]{:S(2)}, u32[]{:S(2)}) collective-permute-start(bf16[32,2048]{1,0:T(8,128)(2,1)S(1)} %get-tuple-element.71), channel_id=1, source_target_pairs={{0,12},{4,8},{8,4},{12,0},{1,13},{5,9},{9,5},{13,1},{2,14},{6,10},... | collective-permute-start | bytes 393224 | tf_op jit(solution)/shard_map/ppermute | solution.py:431
  49.0 6.7 %copy-start.1 = (bf16[64,32,256]{2,1,0:T(8,128)(2,1)S(1)}, bf16[64,32,256]{2,1,0:T(8,128)(2,1)}, u32[]{:S(2)}) copy-start(bf16[64,32,256]{2,1,0:T(8,128)(2,1)} %refs_4_.7) | copy-start | bytes 3145732
  49.0 6.7 %copy-start.2 = (bf16[64,32,256]{2,1,0:T(8,128)(2,1)S(1)}, bf16[64,32,256]{2,1,0:T(8,128)(2,1)}, u32[]{:S(2)}) copy-start(bf16[64,32,256]{2,1,0:T(8,128)(2,1)} %refs_5_.3) | copy-start | bytes 3145732
  59.6 10.4 %collective-permute-start.24 = (bf16[64,1792]{1,0:T(8,128)(2,1)S(1)}, bf16[64,1792]{1,0:T(8,128)(2,1)S(1)}, u32[]{:S(2)}, u32[]{:S(2)}) collective-permute-start(bf16[64,1792]{1,0:T(8,128)(2,1)S(1)} %get-tuple-element.81), channel_id=1, source_target_pairs={{0,12},{4,8},{8,4},{12,0},{1,13},{5,9},{9,5},{13,1},{2,14},{6,10},... | collective-permute-start | bytes 688136 | tf_op jit(solution)/shard_map/ppermute | solution.py:431
  60.8 29.7 %collective-permute-start.25 = (bf16[64,1792]{1,0:T(8,128)(2,1)S(1)}, bf16[64,1792]{1,0:T(8,128)(2,1)S(1)}, u32[]{:S(2)}, u32[]{:S(2)}) collective-permute-start(bf16[64,1792]{1,0:T(8,128)(2,1)S(1)} %get-tuple-element.83), channel_id=1, source_target_pairs={{0,8},{4,12},{8,0},{12,4},{1,9},{5,13},{9,1},{13,5},{2,10},{6,14},... | collective-permute-start | bytes 688136 | tf_op jit(solution)/shard_map/ppermute | solution.py:431
  60.8 29.7 %collective-permute-start.26 = (bf16[64,1792]{1,0:T(8,128)(2,1)S(1)}, bf16[64,1792]{1,0:T(8,128)(2,1)S(1)}, u32[]{:S(2)}, u32[]{:S(2)}) collective-permute-start(bf16[64,1792]{1,0:T(8,128)(2,1)S(1)} %get-tuple-element.85), channel_id=1, source_target_pairs={{0,4},{4,0},{8,12},{12,8},{1,5},{5,1},{9,13},{13,9},{2,6},{6,2},{1... | collective-permute-start | bytes 688136 | tf_op jit(solution)/shard_map/ppermute | solution.py:431
  67.8 23.4 %collective-permute-start.17 = (bf16[64,1792]{1,0:T(8,128)(2,1)S(1)}, bf16[64,1792]{1,0:T(8,128)(2,1)S(1)}, u32[]{:S(2)}, u32[]{:S(2)}) collective-permute-start(bf16[64,1792]{1,0:T(8,128)(2,1)S(1)} %get-tuple-element.76), channel_id=1, source_target_pairs={{0,12},{4,8},{8,4},{12,0},{1,13},{5,9},{9,5},{13,1},{2,14},{6,10},... | collective-permute-start | bytes 688136 | tf_op jit(solution)/shard_map/ppermute | solution.py:431
  68.9 30.0 %collective-permute-start.19 = (bf16[64,1792]{1,0:T(8,128)(2,1)S(1)}, bf16[64,1792]{1,0:T(8,128)(2,1)S(1)}, u32[]{:S(2)}, u32[]{:S(2)}) collective-permute-start(bf16[64,1792]{1,0:T(8,128)(2,1)S(1)} %get-tuple-element.77), channel_id=1, source_target_pairs={{0,8},{4,12},{8,0},{12,4},{1,9},{5,13},{9,1},{13,5},{2,10},{6,14},... | collective-permute-start | bytes 688136 | tf_op jit(solution)/shard_map/ppermute | solution.py:431
  70.0 28.8 %collective-permute-start.21 = (bf16[64,1792]{1,0:T(8,128)(2,1)S(1)}, bf16[64,1792]{1,0:T(8,128)(2,1)S(1)}, u32[]{:S(2)}, u32[]{:S(2)}) collective-permute-start(bf16[64,1792]{1,0:T(8,128)(2,1)S(1)} %get-tuple-element.78), channel_id=1, source_target_pairs={{0,4},{4,0},{8,12},{12,8},{1,5},{5,1},{9,13},{13,9},{2,6},{6,2},{1... | collective-permute-start | bytes 688136 | tf_op jit(solution)/shard_map/ppermute | solution.py:431
  90.6 10.1 %collective-permute-start.27 = (bf16[128,1792]{1,0:T(8,128)(2,1)S(1)}, bf16[128,1792]{1,0:T(8,128)(2,1)S(1)}, u32[]{:S(2)}, u32[]{:S(2)}) collective-permute-start(bf16[128,1792]{1,0:T(8,128)(2,1)S(1)} %pad_maximum_fusion), channel_id=1, source_target_pairs={{0,1},{1,0},{2,3},{3,2},{4,5},{5,4},{6,7},{7,6},{8,9},{9,8},{10,11... | collective-permute-start | bytes 1376264 | tf_op jit(solution)/shard_map/ppermute | solution.py:691
  90.7 8.7 %collective-permute-start.23 = (bf16[64,1792]{1,0:T(8,128)(2,1)S(1)}, bf16[64,1792]{1,0:T(8,128)(2,1)S(1)}, u32[]{:S(2)}, u32[]{:S(2)}) collective-permute-start(bf16[64,1792]{1,0:T(8,128)(2,1)S(1)} %get-tuple-element.79.refs_7_), channel_id=1, source_target_pairs={{0,1},{1,0},{2,3},{3,2},{4,5},{5,4},{6,7},{7,6},{8,9},{9,8},{10,11... | collective-permute-start | bytes 688136 | tf_op jit(solution)/shard_map/ppermute | solution.py:695
  91.2 8.2 %collective-permute-start.18 = (bf16[64,1792]{1,0:T(8,128)(2,1)S(1)}, bf16[64,1792]{1,0:T(8,128)(2,1)S(1)}, u32[]{:S(2)}, u32[]{:S(2)}) collective-permute-start(bf16[64,1792]{1,0:T(8,128)(2,1)S(1)} %collective-permute-done.17.refs_4_), channel_id=1, source_target_pairs={{0,1},{1,0},{2,3},{3,2},{4,5},{5,4},{6,7},{7,6},{8,9},{9,8},{10,11... | collective-permute-start | bytes 688136 | tf_op jit(solution)/shard_map/ppermute | solution.py:695
  98.9 1.5 %collective-permute-start.20 = (bf16[64,1792]{1,0:T(8,128)(2,1)S(1)}, bf16[64,1792]{1,0:T(8,128)(2,1)S(1)}, u32[]{:S(2)}, u32[]{:S(2)}) collective-permute-start(bf16[64,1792]{1,0:T(8,128)(2,1)S(1)} %collective-permute-done.19.refs_5_), channel_id=1, source_target_pairs={{0,1},{1,0},{2,3},{3,2},{4,5},{5,4},{6,7},{7,6},{8,9},{9,8},{10,11... | collective-permute-start | bytes 688136 | tf_op jit(solution)/shard_map/ppermute | solution.py:695
  98.9 1.8 %collective-permute-start.22 = (bf16[64,1792]{1,0:T(8,128)(2,1)S(1)}, bf16[64,1792]{1,0:T(8,128)(2,1)S(1)}, u32[]{:S(2)}, u32[]{:S(2)}) collective-permute-start(bf16[64,1792]{1,0:T(8,128)(2,1)S(1)} %collective-permute-done.21.refs_6_), channel_id=1, source_target_pairs={{0,1},{1,0},{2,3},{3,2},{4,5},{5,4},{6,7},{7,6},{8,9},{9,8},{10,11... | collective-permute-start | bytes 688136 | tf_op jit(solution)/shard_map/ppermute | solution.py:695

commit v14 on v12

--- a/solution.py
+++ b/solution.py
@@ -247,7 +247,7 @@
 
 def attend_kernel(before, steps, rows, cache, groups, lanes, subs, last, *refs):
     places_ref, length_ref, cos_ref, sin_ref, key_ref, value_ref = refs[:6]
-    qkv_refs, refs = refs[6:8], refs[8:]
+    qkv_refs, refs = refs[6:9], refs[9:]
     delta_refs, refs = refs[:lanes][::-1], refs[lanes:]
     if before:
         earlier_ref, refs = refs[0], refs[1:]
@@ -262,13 +262,12 @@
 
     def qkv_tile(span, group, head):
         begin = (group * (PER_GROUP + 2) + head) * HEAD_WIDTH
-        edge = qkv_refs[0].shape[1]
-        if begin < edge:
-            return qkv_refs[0][span, begin : begin + HEAD_WIDTH]
-        return qkv_refs[1][span, begin - edge : begin - edge + HEAD_WIDTH]
+        for ref in qkv_refs:
+            if begin < ref.shape[1]:
+                return ref[span, begin : begin + HEAD_WIDTH]
+            begin -= ref.shape[1]
 
     wide = groups * HEAD_WIDTH
-
     column = as_column(places_ref[0:1, :])
     column = jnp.concatenate([column] * steps, axis=0)
     shape = (steps * rows, lanes * per_message)
@@ -395,8 +394,7 @@
 
 def place_kernel(found, lanes, subs, most, *refs):
     chunks = len(found)
-    *refs, out_ref = refs
-    refs = refs[::-1]
+    out_ref = refs[-1]
     steps = out_ref.shape[1]
     chunk_steps = steps // chunks
     block = most * chunk_steps
@@ -529,7 +527,8 @@
     columns = projection_weight.shape[1]
     block_columns = 256 if columns % 256 == 0 else 384
     blocks = columns // block_columns
-    cut = blocks // 2
+    cuts = [4, 6, 9] if blocks == 9 else [blocks // 3, 2 * blocks // 3, blocks]
+    cut = cuts[0]
 
     def weight_buffers(count):
         return [
@@ -562,12 +561,13 @@
     qkv = [first_qkv]
 
     def project(after):
+        begin, end = cuts[len(qkv) - 1 : len(qkv) + 1]
         return pl.pallas_call(
-            functools.partial(project_kernel, cut),
+            functools.partial(project_kernel, begin),
             in_specs=[VMEM, VMEM, in_hbm],
             out_specs=VMEM,
-            out_shape=projected(blocks - cut),
-            scratch_shapes=weight_buffers(blocks - cut),
+            out_shape=projected(end - begin),
+            scratch_shapes=weight_buffers(end - begin),
             compiler_params=pltpu.CompilerParams(vmem_limit_bytes=PROJECT_LIMIT * MIB),
             cost_estimate=SMALL,
             name="project",
@@ -613,6 +613,8 @@
         if chunk:
             qkv.append(project(after))
         partials = down(chunk, qkv)
+        if chunk:
+            qkv.append(project(partials[0]))
         after = up(partials, qkv)
         messages = list(after)
         if chunk:
@@ -686,9 +688,9 @@
             pairs = [(core, core ^ shift) for core in range(subs)]
             span = slice(shift * block, (shift + 1) * block)
             if chunk < chunks - 1:
-                joined = jnp.concatenate([block_rows[span] for block_rows in along[::-1]])
+                joined = jnp.concatenate([block_rows[span] for block_rows in along])
                 for lane in range(lanes):
-                    where[lane].append((len(landed), (lanes - 1 - lane) * block))
+                    where[lane].append((len(landed), lane * block))
                 landed.append(lax.ppermute(joined, "sub", pairs))
             else:
                 for lane, block_rows in enumerate(along):
@@ -704,7 +706,7 @@
         compiler_params=pltpu.CompilerParams(vmem_limit_bytes=24 * MIB),
         cost_estimate=SMALL,
         name="place",
-    )(*landed[::-1])
+    )(*landed)
     return flow[None]
 
 

time: 101 us -> 98.9 us (0.979)
  starting transfers between devices: 46.2 us -> 39 us
  waiting for transfers between devices: 21.7 us -> 25.7 us
  Pallas kernels: 31.4 us -> 33 us
    ppermute x18, starting transfers between devices: 40.9 us -> 33.4 us  [traded(): landed[shift] = lax.ppermute(blocks[shift], axes, pairs)]
    ppermute x18, waiting for transfers between devices: 15.7 us -> 21.7 us  [traded(): landed[shift] = lax.ppermute(blocks[shift], axes, pairs)]
    ppermute x5, waiting for transfers between devices: 4.68 us -> 2.65 us  [from_others(): landed.append(lax.ppermute(block, axis, pairs))]
    pallas_call x1 -> x2, Pallas kernels: 6.56 us -> 8.06 us  [project(): pl.pallas_call(functools.partial(project_kernel, begin), in_specs=[VMEM,...]
  transfers between devices with their start and end apart: 28 -> 28, of which waited for: 7 -> 6; matrix products, arithmetic and copies ran while one was open for 1% -> 1% of each run, Pallas kernels for 29% -> 31%
where the time goes in v14:
time: 98.9 us; the launch traced here: 98.8 us
  starting transfers between devices  39 us (39%)
  Pallas kernels  33 us (33%)
  waiting for transfers between devices  25.7 us (26%)
    ppermute x18, starting transfers between devices, traded(): landed[shift] = lax.ppermute(blocks[shift], axes, pairs)  33.4 us
    ppermute x18, waiting for transfers between devices, traded(): landed[shift] = lax.ppermute(blocks[shift], axes, pairs)  21.7 us
    pallas_call x1, Pallas kernels, on_device(): pl.pallas_call(functools.partial(norm_pack_project_kernel, chunk_steps, r...  8.69 us
    pallas_call x2, Pallas kernels, project(): pl.pallas_call(functools.partial(project_kernel, begin), in_specs=[VMEM,...  8.06 us
    pallas_call x2, Pallas kernels, on_device(): pl.pallas_call(functools.partial(attend_kernel, chunk * chunk_steps, chun...  7.56 us
    ppermute x5, starting transfers between devices, from_others(): landed.append(lax.ppermute(block, axis, pairs))  4.4 us
    pallas_call x1, Pallas kernels, on_device(): pl.pallas_call(functools.partial(norm_pack_kernel, chunk_steps, rows, flo...  3.45 us
    ppermute x5, waiting for transfers between devices, from_others(): landed.append(lax.ppermute(block, axis, pairs))  2.65 us
  transfers between devices with their start and end apart: 28, of which 6 were waited for; matrix products, arithmetic and copies ran while one was open for 1% of the time, Pallas kernels for 31%

profile of v14, /device:TPU:0, one launch (start us, length us, event | category | flops | bytes accessed | tf_op | source)
XLA Modules:
  0.0 98.8 jit_solution(13472483077564617296)
XLA Ops:
  0.0 0.5 collective-permute-start
  0.5 0.1 collective-permute-start.1
  0.6 0.4 collective-permute-start.2
  1.1 3.5 %norm_and_pack.1 = (bf16[32,1792]{1,0:T(8,128)(2,1)}, bf16[32,1792]{1,0:T(8,128)(2,1)}, bf16[32,1792]{1,0:T(8,128)(2,1)}, bf16[32,1792]{1,0:T(8,128)(2,1)}) custom-call(s32[1,64]{1,0:T(1,128)} %bitcast.23, s32[1,32]{1,0:T(1,128)} %bitcast.25, s32[1,64]{1,0:T(1,128)} %bitcast.27, f32[28,128]{1,0:T(8,128)} %bitcast.19, bf16[256,3584]{1,0:T(8,128)(2,1)} %bitcast.29), custom_call_target="tpu_custom_call" | custom-call | flops 1 | bytes 1 | tf_op jit(solution)/shard_map/norm_and_pack/pallas_call | solution.py:514
  4.5 4.7 %collective-permute-start.6 = (bf16[32,1792]{1,0:T(8,128)(2,1)}, bf16[32,1792]{1,0:T(8,128)(2,1)S(1)}, u32[]{:S(2)}, u32[]{:S(2)}) collective-permute-start(bf16[32,1792]{1,0:T(8,128)(2,1)} %get-tuple-element.50), channel_id=1, source_target_pairs={{0,12},{4,8},{8,4},{12,0},{1,13},{5,9},{9,5},{13,1},{2,14},{6,10},... | collective-permute-start | bytes 344072 | tf_op jit(solution)/shard_map/ppermute | solution.py:429
  9.3 0.6 collective-permute-start.8
  10.0 0.0 copy-start.5
  10.0 8.7 %norm_pack_project.1 = (bf16[256,3584]{1,0:T(8,128)(2,1)S(1)}, f32[256,1024]{1,0:T(8,128)S(1)}, s32[8,64]{1,0:T(8,128)S(1)}, bf16[32,1792]{1,0:T(8,128)(2,1)S(1)...) custom-call(s32[1,64]{1,0:T(1,128)S(1)} %bitcast.24, ...), custom_call_target="tpu_custom_call" | custom-call | flops 1 | bytes 1 | tf_op jit(solution)/shard_map/norm_pack_project/pallas_call | solution.py:544
  18.7 3.8 %collective-permute-start.3 = (bf16[32,1792]{1,0:T(8,128)(2,1)S(1)}, bf16[32,1792]{1,0:T(8,128)(2,1)S(1)}, u32[]{:S(2)}, u32[]{:S(2)}) collective-permute-start(bf16[32,1792]{1,0:T(8,128)(2,1)S(1)} %get-tuple-element.53), channel_id=1, source_target_pairs={{0,12},{4,8},{8,4},{12,0},{1,13},{5,9},{9,5},{13,1},{2,14},{6,10},... | collective-permute-start | bytes 344072 | tf_op jit(solution)/shard_map/ppermute | solution.py:429
  22.5 0.0 copy-start.3
  22.6 0.6 collective-permute-start.5
  23.2 1.2 %down.2.refs_0_ = f32[128,128]{1,0:T(8,128)S(1)} custom-call(bf16[32,1792]{1,0:T(8,128)(2,1)S(1)} %collective-permute-done.6.refs_0_, bf16[32,1792]{1,0:T(8,128)(2,1)S(1)} %collective-permute-done.7.refs_1_, bf16[32,1792]{1,0:T(8,128)(2,1)S(1)} %collective-permute-done.8.refs_2_, bf16[32,1792]{1,0:T(8,128)(2,1)S(1)} %copy-done.5, ...), custom_call_target="tpu_custom_call" | custom-call | flops 1 | bytes 1 | tf_op jit(solution)/shard_map/down/pallas_call | solution.py:577
  24.4 1.7 %collective-permute-start.9 = (f32[128,128]{1,0:T(8,128)S(1)}, f32[128,128]{1,0:T(8,128)S(1)}, u32[]{:S(2)}, u32[]{:S(2)}) collective-permute-start(f32[128,128]{1,0:T(8,128)S(1)} %down.2.refs_0_), channel_id=1, source_target_pairs={{0,2},{2,0},{1,3},{3,1},{4,6},{6,4},{5,7},{7,5},{8,10},{10,8},{9,1... | collective-permute-start | bytes 196616 | tf_op jit(solution)/shard_map/ppermute | solution.py:438
  26.1 2.6 %collective-permute-done.9.refs_1_ = f32[128,128]{1,0:T(8,128)S(1)} collective-permute-done((f32[128,128]{1,0:T(8,128)S(1)}, f32[128,128]{1,0:T(8,128)S(1)}, u32[]{:S(2)}, u32[]{:S(2)}) %collective-permute-start.9) | collective-permute-done | bytes 65568 | tf_op jit(solution)/shard_map/ppermute | solution.py:438
  28.7 0.5 up.2
  29.2 3.8 %collective-permute-start.11 = (bf16[32,2048]{1,0:T(8,128)(2,1)S(1)}, bf16[32,2048]{1,0:T(8,128)(2,1)S(1)}, u32[]{:S(2)}, u32[]{:S(2)}) collective-permute-start(bf16[32,2048]{1,0:T(8,128)(2,1)S(1)} %get-tuple-element.64), channel_id=1, source_target_pairs={{0,12},{4,8},{8,4},{12,0},{1,13},{5,9},{9,5},{13,1},{2,14},{6,10},... | collective-permute-start | bytes 393224 | tf_op jit(solution)/shard_map/ppermute | solution.py:429
  33.0 0.7 collective-permute-start.13
  33.7 0.1 compare_select_fusion
  33.7 3.7 %project.2.refs_7_ = f32[256,512]{1,0:T(8,128)S(1)} custom-call(bf16[256,3584]{1,0:T(8,128)(2,1)S(1)} %get-tuple-element.58.rows_ref, f32[18,128]{1,0:T(8,128)S(1)} %bitcast.17, bf16[3584,2304]{1,0:T(8,128)(2,1)} %weight_hbm.3), custom_call_target="tpu_custom_call" | custom-call | flops 1 | bytes 1 | tf_op jit(solution)/shard_map/project/pallas_call | solution.py:565
  37.5 1.2 %down.3.refs_0_ = f32[128,128]{1,0:T(8,128)S(1)} custom-call(bf16[32,1792]{1,0:T(8,128)(2,1)S(1)} %collective-permute-done.3.refs_0_, bf16[32,1792]{1,0:T(8,128)(2,1)S(1)} %collective-permute-done.4.refs_1_, bf16[32,1792]{1,0:T(8,128)(2,1)S(1)} %collective-permute-done.5.refs_2_, bf16[32,1792]{1,0:T(8,128)(2,1)S(1)} %get-tuple-element.66.refs_3_, ...), custom_call_target="tpu_custom_call" | custom-call | flops 1 | bytes 1 | tf_op jit(solution)/shard_map/down/pallas_call | solution.py:577
  38.6 1.7 %collective-permute-start.10 = (f32[128,128]{1,0:T(8,128)S(1)}, f32[128,128]{1,0:T(8,128)S(1)}, u32[]{:S(2)}, u32[]{:S(2)}) collective-permute-start(f32[128,128]{1,0:T(8,128)S(1)} %down.3.refs_0_), channel_id=1, source_target_pairs={{0,2},{2,0},{1,3},{3,1},{4,6},{6,4},{5,7},{7,5},{8,10},{10,8},{9,1... | collective-permute-start | bytes 196616 | tf_op jit(solution)/shard_map/ppermute | solution.py:438
  40.3 0.1 add_convert_fusion
  40.4 4.4 %project.3.refs_8_ = f32[256,768]{1,0:T(8,128)S(1)} custom-call(bf16[256,3584]{1,0:T(8,128)(2,1)S(1)} %get-tuple-element.58.rows_ref, f32[18,128]{1,0:T(8,128)S(1)} %bitcast.18, bf16[3584,2304]{1,0:T(8,128)(2,1)} %weight_hbm.3), custom_call_target="tpu_custom_call" | custom-call | flops 1 | bytes 1 | tf_op jit(solution)/shard_map/project/pallas_call | solution.py:565
  44.8 0.0 copy-start.1
  44.8 0.0 copy-start.2
  44.8 0.5 up.3
  45.3 1.3 %collective-permute-start.14 = (bf16[32,2048]{1,0:T(8,128)(2,1)S(1)}, bf16[32,2048]{1,0:T(8,128)(2,1)S(1)}, u32[]{:S(2)}, u32[]{:S(2)}) collective-permute-start(bf16[32,2048]{1,0:T(8,128)(2,1)S(1)} %get-tuple-element.76), channel_id=1, source_target_pairs={{0,4},{4,0},{8,12},{12,8},{1,5},{5,1},{9,13},{13,9},{2,6},{6,2},{1... | collective-permute-start | bytes 393224 | tf_op jit(solution)/shard_map/ppermute | solution.py:429
  46.6 2.9 %collective-permute-start.15 = (bf16[32,2048]{1,0:T(8,128)(2,1)S(1)}, bf16[32,2048]{1,0:T(8,128)(2,1)S(1)}, u32[]{:S(2)}, u32[]{:S(2)}) collective-permute-start(bf16[32,2048]{1,0:T(8,128)(2,1)S(1)} %get-tuple-element.77), channel_id=1, source_target_pairs={{0,8},{4,12},{8,0},{12,4},{1,9},{5,13},{9,1},{13,5},{2,10},{6,14},... | collective-permute-start | bytes 393224 | tf_op jit(solution)/shard_map/ppermute | solution.py:429
  49.5 0.2 collective-permute-start.16
  49.8 0.5 fusion
  50.3 3.9 %attend.2 = (f32[128,512]{1,0:T(8,128)S(1)}, bf16[64,1792]{1,0:T(8,128)(2,1)S(1)}, bf16[64,1792]{1,0:T(8,128)(2,1)S(1)}, bf16[64,1792]{1,0:T(8,128)(2,1)S(1)}, bf16[64,1792]{1,0:T(8,128)(2,1)S(1)}) custom-call(s32[8,64]{1,0:T(8,128)S(1)} %get-tuple-element.73.refs_0_, s32[1,64]{1,0:T(1,128)S(1)} %bitcast.21, f32[256,128]{1,0:T(8,128)S(1)} %get-tuple-element.90.refs_2_, ...), custom_call_target="tpu_custom_call" | custom-call | flops 1 | bytes 1 | tf_op jit(solution)/shard_map/attend/pallas_call | solution.py:633
  54.2 2.5 %collective-permute-done.15.refs_10_ = bf16[32,2048]{1,0:T(8,128)(2,1)S(1)} collective-permute-done((bf16[32,2048]{1,0:T(8,128)(2,1)S(1)}, bf16[32,2048]{1,0:T(8,128)(2,1)S(1)}, u32[]{:S(2)}, u32[]{:S(2)}) %collective-permute-start.15) | collective-permute-done | bytes 131104 | tf_op jit(solution)/shard_map/ppermute | solution.py:429
  56.7 5.2 %collective-permute-start.19 = (bf16[64,1792]{1,0:T(8,128)(2,1)S(1)}, bf16[64,1792]{1,0:T(8,128)(2,1)S(1)}, u32[]{:S(2)}, u32[]{:S(2)}) collective-permute-start(bf16[64,1792]{1,0:T(8,128)(2,1)S(1)} %get-tuple-element.83), channel_id=1, source_target_pairs={{0,12},{4,8},{8,4},{12,0},{1,13},{5,9},{9,5},{13,1},{2,14},{6,10},... | collective-permute-start | bytes 688136 | tf_op jit(solution)/shard_map/ppermute | solution.py:429
  62.0 4.9 %collective-permute-start.18 = (bf16[64,1792]{1,0:T(8,128)(2,1)S(1)}, bf16[64,1792]{1,0:T(8,128)(2,1)S(1)}, u32[]{:S(2)}, u32[]{:S(2)}) collective-permute-start(bf16[64,1792]{1,0:T(8,128)(2,1)S(1)} %get-tuple-element.81), channel_id=1, source_target_pairs={{0,8},{4,12},{8,0},{12,4},{1,9},{5,13},{9,1},{13,5},{2,10},{6,14},... | collective-permute-start | bytes 688136 | tf_op jit(solution)/shard_map/ppermute | solution.py:429
  66.9 0.0 collective-permute-start.17
  66.9 3.7 %attend.3 = (bf16[64,1792]{1,0:T(8,128)(2,1)S(1)}, bf16[64,1792]{1,0:T(8,128)(2,1)S(1)}, bf16[64,1792]{1,0:T(8,128)(2,1)S(1)}, bf16[64,1792]{1,0:T(8,128)(2,1)S(1)}) custom-call(s32[8,64]{1,0:T(8,128)S(1)} %get-tuple-element.73.refs_0_, s32[1,64]{1,0:T(1,128)S(1)} %bitcast.22, f32[256,128]{1,0:T(8,128)S(1)} %get-tuple-element.90.refs_2_, ...), custom_call_target="tpu_custom_call" | custom-call | flops 1 | bytes 1 | tf_op jit(solution)/shard_map/attend/pallas_call | solution.py:633
  70.6 2.1 %collective-permute-start.21 = (bf16[64,1792]{1,0:T(8,128)(2,1)S(1)}, bf16[64,1792]{1,0:T(8,128)(2,1)S(1)}, u32[]{:S(2)}, u32[]{:S(2)}) collective-permute-start(bf16[64,1792]{1,0:T(8,128)(2,1)S(1)} %get-tuple-element.86), channel_id=1, source_target_pairs={{0,4},{4,0},{8,12},{12,8},{1,5},{5,1},{9,13},{13,9},{2,6},{6,2},{1... | collective-permute-start | bytes 688136 | tf_op jit(solution)/shard_map/ppermute | solution.py:429
  72.7 1.0 %collective-permute-start.22 = (bf16[64,1792]{1,0:T(8,128)(2,1)S(1)}, bf16[64,1792]{1,0:T(8,128)(2,1)S(1)}, u32[]{:S(2)}, u32[]{:S(2)}) collective-permute-start(bf16[64,1792]{1,0:T(8,128)(2,1)S(1)} %get-tuple-element.87), channel_id=1, source_target_pairs={{0,8},{4,12},{8,0},{12,4},{1,9},{5,13},{9,1},{13,5},{2,10},{6,14},... | collective-permute-start | bytes 688136 | tf_op jit(solution)/shard_map/ppermute | solution.py:429
  73.7 1.4 %collective-permute-start.23 = (bf16[64,1792]{1,0:T(8,128)(2,1)S(1)}, bf16[64,1792]{1,0:T(8,128)(2,1)S(1)}, u32[]{:S(2)}, u32[]{:S(2)}) collective-permute-start(bf16[64,1792]{1,0:T(8,128)(2,1)S(1)} %get-tuple-element.88), channel_id=1, source_target_pairs={{0,12},{4,8},{8,4},{12,0},{1,13},{5,9},{9,5},{13,1},{2,14},{6,10},... | collective-permute-start | bytes 688136 | tf_op jit(solution)/shard_map/ppermute | solution.py:429
  75.2 15.5 %collective-permute-done.18.refs_2_ = bf16[64,1792]{1,0:T(8,128)(2,1)S(1)} collective-permute-done((bf16[64,1792]{1,0:T(8,128)(2,1)S(1)}, bf16[64,1792]{1,0:T(8,128)(2,1)S(1)}, u32[]{:S(2)}, u32[]{:S(2)}) %collective-permute-start.18) | collective-permute-done | bytes 229408 | tf_op jit(solution)/shard_map/ppermute | solution.py:429
  90.8 0.1 collective-permute-start.20
  90.8 0.5 collective-permute-start.24
  91.3 0.1 collective-permute-start.25
  91.4 3.6 %collective-permute-done.22.refs_7_ = bf16[64,1792]{1,0:T(8,128)(2,1)S(1)} collective-permute-done((bf16[64,1792]{1,0:T(8,128)(2,1)S(1)}, bf16[64,1792]{1,0:T(8,128)(2,1)S(1)}, u32[]{:S(2)}, u32[]{:S(2)}) %collective-permute-start.22) | collective-permute-done | bytes 229408 | tf_op jit(solution)/shard_map/ppermute | solution.py:429
  95.1 0.5 collective-permute-start.27
  95.6 1.0 collective-permute-done.26.refs_11_
  96.5 0.3 collective-permute-done.27.refs_12_
  96.9 1.9 %place.1 = bf16[128,4,1792]{2,1,0:T(4,128)(2,1)} custom-call(bf16[64,1792]{1,0:T(8,128)(2,1)S(1)} %get-tuple-element.74.refs_0_, bf16[64,1792]{1,0:T(8,128)(2,1)S(1)} %collective-permute-done.17.refs_1_, bf16[64,1792]{1,0:T(8,128)(2,1)S(1)} %collective-permute-done.18.refs_2_, bf16[64,1792]{1,0:T(8,128)(2,1)S(1)} %collective-permute-done.19.refs_3_, ...), custom_call_target="tpu_custom_call" | custom-call | flops 1 | bytes 1 | tf_op jit(solution)/shard_map/place/pallas_call | solution.py:701
  (53 shorter events, 0.2 us)
Async XLA Ops:
  0.0 9.9 %copy-start.9 = (s32[64,1]{0,1:T(1,128)S(1)}, s32[64,1]{0,1:T(1,128)}, u32[]{:S(2)}) copy-start(s32[64,1]{0,1:T(1,128)} %param.17) | copy-start | bytes 772
  0.0 9.9 %copy-start.10 = (s32[32]{0:T(128)S(1)}, s32[32]{0:T(128)}, u32[]{:S(2)}) copy-start(s32[32]{0:T(128)} %param.18) | copy-start | bytes 388
  0.0 9.9 %copy-start.11 = (s32[64,1]{0,1:T(1,128)S(1)}, s32[64,1]{0,1:T(1,128)}, u32[]{:S(2)}) copy-start(s32[64,1]{0,1:T(1,128)} %param.25) | copy-start | bytes 772
  0.0 9.9 %copy-start.7 = (f32[3584]{0:T(1024)S(1)}, f32[3584]{0:T(1024)}, u32[]{:S(2)}) copy-start(f32[3584]{0:T(1024)} %param.14) | copy-start | bytes 43012
  0.0 9.9 %copy-start.6 = (f32[2304]{0:T(1024)S(1)}, f32[2304]{0:T(1024)}, u32[]{:S(2)}) copy-start(f32[2304]{0:T(1024)} %param.16) | copy-start | bytes 27652
  0.0 9.9 %collective-permute-start = (bf16[4,1792,128]{2,1,0:T(8,128)(2,1)}, bf16[4,1792,128]{2,1,0:T(8,128)(2,1)S(1)}, u32[]{:S(2)}, u32[]{:S(2)}) collective-permute-start(bf16[4,1792,128]{2,1,0:T(8,128)(2,1)} %refs_4_.5), channel_id=1, source_target_pairs={{0,1},{1,0},{2,3},{3,2},{4,5},{5,4},{6,7},{7,6},{8,9},{9,8},{10,11... | collective-permute-start | bytes 5505032 | tf_op jit(solution)/shard_map/ppermute | solution.py:438
  0.5 9.4 %collective-permute-start.1 = (bf16[256,1792]{1,0:T(8,128)(2,1)}, bf16[256,1792]{1,0:T(8,128)(2,1)S(1)}, u32[]{:S(2)}, u32[]{:S(2)}) collective-permute-start(bf16[256,1792]{1,0:T(8,128)(2,1)} %bitcast.10), channel_id=1, source_target_pairs={{0,1},{1,0},{2,3},{3,2},{4,5},{5,4},{6,7},{7,6},{8,9},{9,8},{10,11... | collective-permute-start | bytes 2752520 | tf_op jit(solution)/shard_map/ppermute | solution.py:438
  0.6 8.6 %collective-permute-start.2 = (bf16[256,256]{1,0:T(8,128)(2,1)}, bf16[256,256]{1,0:T(8,128)(2,1)S(1)}, u32[]{:S(2)}, u32[]{:S(2)}) collective-permute-start(bf16[256,256]{1,0:T(8,128)(2,1)} %bitcast.13), channel_id=1, source_target_pairs={{0,1},{1,0},{2,3},{3,2},{4,5},{5,4},{6,7},{7,6},{8,9},{9,8},{10,11... | collective-permute-start | bytes 393224 | tf_op jit(solution)/shard_map/ppermute | solution.py:438
  4.5 18.0 %collective-permute-start.6 = (bf16[32,1792]{1,0:T(8,128)(2,1)}, bf16[32,1792]{1,0:T(8,128)(2,1)S(1)}, u32[]{:S(2)}, u32[]{:S(2)}) collective-permute-start(bf16[32,1792]{1,0:T(8,128)(2,1)} %get-tuple-element.50), channel_id=1, source_target_pairs={{0,12},{4,8},{8,4},{12,0},{1,13},{5,9},{9,5},{13,1},{2,14},{6,10},... | collective-permute-start | bytes 344072 | tf_op jit(solution)/shard_map/ppermute | solution.py:429
  9.3 13.9 %collective-permute-start.7 = (bf16[32,1792]{1,0:T(8,128)(2,1)}, bf16[32,1792]{1,0:T(8,128)(2,1)S(1)}, u32[]{:S(2)}, u32[]{:S(2)}) collective-permute-start(bf16[32,1792]{1,0:T(8,128)(2,1)} %get-tuple-element.49), channel_id=1, source_target_pairs={{0,8},{4,12},{8,0},{12,4},{1,9},{5,13},{9,1},{13,5},{2,10},{6,14},... | collective-permute-start | bytes 344072 | tf_op jit(solution)/shard_map/ppermute | solution.py:429
  9.3 13.9 %collective-permute-start.8 = (bf16[32,1792]{1,0:T(8,128)(2,1)}, bf16[32,1792]{1,0:T(8,128)(2,1)S(1)}, u32[]{:S(2)}, u32[]{:S(2)}) collective-permute-start(bf16[32,1792]{1,0:T(8,128)(2,1)} %get-tuple-element.48), channel_id=1, source_target_pairs={{0,4},{4,0},{8,12},{12,8},{1,5},{5,1},{9,13},{13,9},{2,6},{6,2},{1... | collective-permute-start | bytes 344072 | tf_op jit(solution)/shard_map/ppermute | solution.py:429
  10.0 12.6 %copy-start.8 = (s32[64]{0:T(128)S(1)}, s32[64]{0:T(128)}, u32[]{:S(2)}) copy-start(s32[64]{0:T(128)} %param.19) | copy-start | bytes 772
  10.0 13.2 %copy-start = (bf16[4,1792,128]{2,1,0:T(8,128)(2,1)S(1)}, bf16[4,1792,128]{2,1,0:T(8,128)(2,1)}, u32[]{:S(2)}) copy-start(bf16[4,1792,128]{2,1,0:T(8,128)(2,1)} %refs_4_.5) | copy-start | bytes 5505028
  10.0 13.2 %copy-start.5 = (bf16[32,1792]{1,0:T(8,128)(2,1)S(1)}, bf16[32,1792]{1,0:T(8,128)(2,1)}, u32[]{:S(2)}) copy-start(bf16[32,1792]{1,0:T(8,128)(2,1)} %get-tuple-element.59.refs_3_) | copy-start | bytes 344068
  18.7 14.3 %collective-permute-start.3 = (bf16[32,1792]{1,0:T(8,128)(2,1)S(1)}, bf16[32,1792]{1,0:T(8,128)(2,1)S(1)}, u32[]{:S(2)}, u32[]{:S(2)}) collective-permute-start(bf16[32,1792]{1,0:T(8,128)(2,1)S(1)} %get-tuple-element.53), channel_id=1, source_target_pairs={{0,12},{4,8},{8,4},{12,0},{1,13},{5,9},{9,5},{13,1},{2,14},{6,10},... | collective-permute-start | bytes 344072 | tf_op jit(solution)/shard_map/ppermute | solution.py:429
  22.5 14.9 %collective-permute-start.4 = (bf16[32,1792]{1,0:T(8,128)(2,1)S(1)}, bf16[32,1792]{1,0:T(8,128)(2,1)S(1)}, u32[]{:S(2)}, u32[]{:S(2)}) collective-permute-start(bf16[32,1792]{1,0:T(8,128)(2,1)S(1)} %get-tuple-element.54), channel_id=1, source_target_pairs={{0,8},{4,12},{8,0},{12,4},{1,9},{5,13},{9,1},{13,5},{2,10},{6,14},... | collective-permute-start | bytes 344072 | tf_op jit(solution)/shard_map/ppermute | solution.py:429
  22.5 6.2 %copy-start.3 = (bf16[4,64,1792]{2,1,0:T(8,128)(2,1)S(1)}, bf16[4,64,1792]{2,1,0:T(8,128)(2,1)}, u32[]{:S(2)}) copy-start(bf16[4,64,1792]{2,1,0:T(8,128)(2,1)} %param.23) | copy-start | bytes 2752516
  22.5 6.2 %copy-start.4 = (bf16[4,64,256]{2,1,0:T(8,128)(2,1)S(1)}, bf16[4,64,256]{2,1,0:T(8,128)(2,1)}, u32[]{:S(2)}) copy-start(bf16[4,64,256]{2,1,0:T(8,128)(2,1)} %param.24) | copy-start | bytes 393220
  22.6 14.9 %collective-permute-start.5 = (bf16[32,1792]{1,0:T(8,128)(2,1)S(1)}, bf16[32,1792]{1,0:T(8,128)(2,1)S(1)}, u32[]{:S(2)}, u32[]{:S(2)}) collective-permute-start(bf16[32,1792]{1,0:T(8,128)(2,1)S(1)} %get-tuple-element.55), channel_id=1, source_target_pairs={{0,4},{4,0},{8,12},{12,8},{1,5},{5,1},{9,13},{13,9},{2,6},{6,2},{1... | collective-permute-start | bytes 344072 | tf_op jit(solution)/shard_map/ppermute | solution.py:429
  24.4 4.3 %collective-permute-start.9 = (f32[128,128]{1,0:T(8,128)S(1)}, f32[128,128]{1,0:T(8,128)S(1)}, u32[]{:S(2)}, u32[]{:S(2)}) collective-permute-start(f32[128,128]{1,0:T(8,128)S(1)} %down.2.refs_0_), channel_id=1, source_target_pairs={{0,2},{2,0},{1,3},{3,1},{4,6},{6,4},{5,7},{7,5},{8,10},{10,8},{9,1... | collective-permute-start | bytes 196616 | tf_op jit(solution)/shard_map/ppermute | solution.py:438
  29.2 20.3 %collective-permute-start.11 = (bf16[32,2048]{1,0:T(8,128)(2,1)S(1)}, bf16[32,2048]{1,0:T(8,128)(2,1)S(1)}, u32[]{:S(2)}, u32[]{:S(2)}) collective-permute-start(bf16[32,2048]{1,0:T(8,128)(2,1)S(1)} %get-tuple-element.64), channel_id=1, source_target_pairs={{0,12},{4,8},{8,4},{12,0},{1,13},{5,9},{9,5},{13,1},{2,14},{6,10},... | collective-permute-start | bytes 393224 | tf_op jit(solution)/shard_map/ppermute | solution.py:429
  33.0 13.6 %collective-permute-start.12 = (bf16[32,2048]{1,0:T(8,128)(2,1)S(1)}, bf16[32,2048]{1,0:T(8,128)(2,1)S(1)}, u32[]{:S(2)}, u32[]{:S(2)}) collective-permute-start(bf16[32,2048]{1,0:T(8,128)(2,1)S(1)} %get-tuple-element.63), channel_id=1, source_target_pairs={{0,8},{4,12},{8,0},{12,4},{1,9},{5,13},{9,1},{13,5},{2,10},{6,14},... | collective-permute-start | bytes 393224 | tf_op jit(solution)/shard_map/ppermute | solution.py:429
  33.0 12.3 %collective-permute-start.13 = (bf16[32,2048]{1,0:T(8,128)(2,1)S(1)}, bf16[32,2048]{1,0:T(8,128)(2,1)S(1)}, u32[]{:S(2)}, u32[]{:S(2)}) collective-permute-start(bf16[32,2048]{1,0:T(8,128)(2,1)S(1)} %get-tuple-element.62), channel_id=1, source_target_pairs={{0,4},{4,0},{8,12},{12,8},{1,5},{5,1},{9,13},{13,9},{2,6},{6,2},{1... | collective-permute-start | bytes 393224 | tf_op jit(solution)/shard_map/ppermute | solution.py:429
  38.6 6.2 %collective-permute-start.10 = (f32[128,128]{1,0:T(8,128)S(1)}, f32[128,128]{1,0:T(8,128)S(1)}, u32[]{:S(2)}, u32[]{:S(2)}) collective-permute-start(f32[128,128]{1,0:T(8,128)S(1)} %down.3.refs_0_), channel_id=1, source_target_pairs={{0,2},{2,0},{1,3},{3,1},{4,6},{6,4},{5,7},{7,5},{8,10},{10,8},{9,1... | collective-permute-start | bytes 196616 | tf_op jit(solution)/shard_map/ppermute | solution.py:438
  44.8 5.5 %copy-start.1 = (bf16[64,32,256]{2,1,0:T(8,128)(2,1)S(1)}, bf16[64,32,256]{2,1,0:T(8,128)(2,1)}, u32[]{:S(2)}) copy-start(bf16[64,32,256]{2,1,0:T(8,128)(2,1)} %refs_4_.7) | copy-start | bytes 3145732
  44.8 5.5 %copy-start.2 = (bf16[64,32,256]{2,1,0:T(8,128)(2,1)S(1)}, bf16[64,32,256]{2,1,0:T(8,128)(2,1)}, u32[]{:S(2)}) copy-start(bf16[64,32,256]{2,1,0:T(8,128)(2,1)} %refs_5_.3) | copy-start | bytes 3145732
  45.3 8.9 %collective-permute-start.14 = (bf16[32,2048]{1,0:T(8,128)(2,1)S(1)}, bf16[32,2048]{1,0:T(8,128)(2,1)S(1)}, u32[]{:S(2)}, u32[]{:S(2)}) collective-permute-start(bf16[32,2048]{1,0:T(8,128)(2,1)S(1)} %get-tuple-element.76), channel_id=1, source_target_pairs={{0,4},{4,0},{8,12},{12,8},{1,5},{5,1},{9,13},{13,9},{2,6},{6,2},{1... | collective-permute-start | bytes 393224 | tf_op jit(solution)/shard_map/ppermute | solution.py:429
  46.6 10.1 %collective-permute-start.15 = (bf16[32,2048]{1,0:T(8,128)(2,1)S(1)}, bf16[32,2048]{1,0:T(8,128)(2,1)S(1)}, u32[]{:S(2)}, u32[]{:S(2)}) collective-permute-start(bf16[32,2048]{1,0:T(8,128)(2,1)S(1)} %get-tuple-element.77), channel_id=1, source_target_pairs={{0,8},{4,12},{8,0},{12,4},{1,9},{5,13},{9,1},{13,5},{2,10},{6,14},... | collective-permute-start | bytes 393224 | tf_op jit(solution)/shard_map/ppermute | solution.py:429
  49.5 7.2 %collective-permute-start.16 = (bf16[32,2048]{1,0:T(8,128)(2,1)S(1)}, bf16[32,2048]{1,0:T(8,128)(2,1)S(1)}, u32[]{:S(2)}, u32[]{:S(2)}) collective-permute-start(bf16[32,2048]{1,0:T(8,128)(2,1)S(1)} %get-tuple-element.78), channel_id=1, source_target_pairs={{0,12},{4,8},{8,4},{12,0},{1,13},{5,9},{9,5},{13,1},{2,14},{6,10},... | collective-permute-start | bytes 393224 | tf_op jit(solution)/shard_map/ppermute | solution.py:429
  56.7 17.0 %collective-permute-start.19 = (bf16[64,1792]{1,0:T(8,128)(2,1)S(1)}, bf16[64,1792]{1,0:T(8,128)(2,1)S(1)}, u32[]{:S(2)}, u32[]{:S(2)}) collective-permute-start(bf16[64,1792]{1,0:T(8,128)(2,1)S(1)} %get-tuple-element.83), channel_id=1, source_target_pairs={{0,12},{4,8},{8,4},{12,0},{1,13},{5,9},{9,5},{13,1},{2,14},{6,10},... | collective-permute-start | bytes 688136 | tf_op jit(solution)/shard_map/ppermute | solution.py:429
  62.0 28.7 %collective-permute-start.18 = (bf16[64,1792]{1,0:T(8,128)(2,1)S(1)}, bf16[64,1792]{1,0:T(8,128)(2,1)S(1)}, u32[]{:S(2)}, u32[]{:S(2)}) collective-permute-start(bf16[64,1792]{1,0:T(8,128)(2,1)S(1)} %get-tuple-element.81), channel_id=1, source_target_pairs={{0,8},{4,12},{8,0},{12,4},{1,9},{5,13},{9,1},{13,5},{2,10},{6,14},... | collective-permute-start | bytes 688136 | tf_op jit(solution)/shard_map/ppermute | solution.py:429
  66.9 23.8 %collective-permute-start.17 = (bf16[64,1792]{1,0:T(8,128)(2,1)S(1)}, bf16[64,1792]{1,0:T(8,128)(2,1)S(1)}, u32[]{:S(2)}, u32[]{:S(2)}) collective-permute-start(bf16[64,1792]{1,0:T(8,128)(2,1)S(1)} %get-tuple-element.79), channel_id=1, source_target_pairs={{0,4},{4,0},{8,12},{12,8},{1,5},{5,1},{9,13},{13,9},{2,6},{6,2},{1... | collective-permute-start | bytes 688136 | tf_op jit(solution)/shard_map/ppermute | solution.py:429
  70.6 20.7 %collective-permute-start.21 = (bf16[64,1792]{1,0:T(8,128)(2,1)S(1)}, bf16[64,1792]{1,0:T(8,128)(2,1)S(1)}, u32[]{:S(2)}, u32[]{:S(2)}) collective-permute-start(bf16[64,1792]{1,0:T(8,128)(2,1)S(1)} %get-tuple-element.86), channel_id=1, source_target_pairs={{0,4},{4,0},{8,12},{12,8},{1,5},{5,1},{9,13},{13,9},{2,6},{6,2},{1... | collective-permute-start | bytes 688136 | tf_op jit(solution)/shard_map/ppermute | solution.py:429
  72.7 22.3 %collective-permute-start.22 = (bf16[64,1792]{1,0:T(8,128)(2,1)S(1)}, bf16[64,1792]{1,0:T(8,128)(2,1)S(1)}, u32[]{:S(2)}, u32[]{:S(2)}) collective-permute-start(bf16[64,1792]{1,0:T(8,128)(2,1)S(1)} %get-tuple-element.87), channel_id=1, source_target_pairs={{0,8},{4,12},{8,0},{12,4},{1,9},{5,13},{9,1},{13,5},{2,10},{6,14},... | collective-permute-start | bytes 688136 | tf_op jit(solution)/shard_map/ppermute | solution.py:429
  73.7 21.4 %collective-permute-start.23 = (bf16[64,1792]{1,0:T(8,128)(2,1)S(1)}, bf16[64,1792]{1,0:T(8,128)(2,1)S(1)}, u32[]{:S(2)}, u32[]{:S(2)}) collective-permute-start(bf16[64,1792]{1,0:T(8,128)(2,1)S(1)} %get-tuple-element.88), channel_id=1, source_target_pairs={{0,12},{4,8},{8,4},{12,0},{1,13},{5,9},{9,5},{13,1},{2,14},{6,10},... | collective-permute-start | bytes 688136 | tf_op jit(solution)/shard_map/ppermute | solution.py:429
  90.8 6.1 %collective-permute-start.20 = (bf16[128,1792]{1,0:T(8,128)(2,1)S(1)}, bf16[128,1792]{1,0:T(8,128)(2,1)S(1)}, u32[]{:S(2)}, u32[]{:S(2)}) collective-permute-start(bf16[128,1792]{1,0:T(8,128)(2,1)S(1)} %pad_maximum_fusion), channel_id=1, source_target_pairs={{0,1},{1,0},{2,3},{3,2},{4,5},{5,4},{6,7},{7,6},{8,9},{9,8},{10,11... | collective-permute-start | bytes 1376264 | tf_op jit(solution)/shard_map/ppermute | solution.py:694
  90.8 4.7 %collective-permute-start.24 = (bf16[64,1792]{1,0:T(8,128)(2,1)S(1)}, bf16[64,1792]{1,0:T(8,128)(2,1)S(1)}, u32[]{:S(2)}, u32[]{:S(2)}) collective-permute-start(bf16[64,1792]{1,0:T(8,128)(2,1)S(1)} %get-tuple-element.85.refs_5_), channel_id=1, source_target_pairs={{0,1},{1,0},{2,3},{3,2},{4,5},{5,4},{6,7},{7,6},{8,9},{9,8},{10,11... | collective-permute-start | bytes 688136 | tf_op jit(solution)/shard_map/ppermute | solution.py:698
  91.3 4.2 %collective-permute-start.25 = (bf16[64,1792]{1,0:T(8,128)(2,1)S(1)}, bf16[64,1792]{1,0:T(8,128)(2,1)S(1)}, u32[]{:S(2)}, u32[]{:S(2)}) collective-permute-start(bf16[64,1792]{1,0:T(8,128)(2,1)S(1)} %collective-permute-done.21.refs_6_), channel_id=1, source_target_pairs={{0,1},{1,0},{2,3},{3,2},{4,5},{5,4},{6,7},{7,6},{8,9},{9,8},{10,11... | collective-permute-start | bytes 688136 | tf_op jit(solution)/shard_map/ppermute | solution.py:698
  95.1 1.5 %collective-permute-start.26 = (bf16[64,1792]{1,0:T(8,128)(2,1)S(1)}, bf16[64,1792]{1,0:T(8,128)(2,1)S(1)}, u32[]{:S(2)}, u32[]{:S(2)}) collective-permute-start(bf16[64,1792]{1,0:T(8,128)(2,1)S(1)} %collective-permute-done.22.refs_7_), channel_id=1, source_target_pairs={{0,1},{1,0},{2,3},{3,2},{4,5},{5,4},{6,7},{7,6},{8,9},{9,8},{10,11... | collective-permute-start | bytes 688136 | tf_op jit(solution)/shard_map/ppermute | solution.py:698
  95.1 1.8 %collective-permute-start.27 = (bf16[64,1792]{1,0:T(8,128)(2,1)S(1)}, bf16[64,1792]{1,0:T(8,128)(2,1)S(1)}, u32[]{:S(2)}, u32[]{:S(2)}) collective-permute-start(bf16[64,1792]{1,0:T(8,128)(2,1)S(1)} %collective-permute-done.23.refs_8_), channel_id=1, source_target_pairs={{0,1},{1,0},{2,3},{3,2},{4,5},{5,4},{6,7},{7,6},{8,9},{9,8},{10,11... | collective-permute-start | bytes 688136 | tf_op jit(solution)/shard_map/ppermute | solution.py:698

commit v15 on v14

--- a/solution.py
+++ b/solution.py
@@ -610,11 +610,8 @@
     returned = []
     after = qkv
     for chunk in range(chunks):
-        if chunk:
-            qkv.append(project(after))
-        partials = down(chunk, qkv)
-        if chunk:
-            qkv.append(project(partials[0]))
+        partials = down(chunk, after)
+        qkv.append(project(partials[0]))
         after = up(partials, qkv)
         messages = list(after)
         if chunk:

time: 98.9 us -> 98.7 us (level)
  the two profiles are of different devices: /device:TPU:0 before, /device:TPU:11 now
where the time goes in v15:
time: 98.7 us; the launch traced here: 98.5 us
  starting transfers between devices  37.5 us (38%)
  Pallas kernels  33.1 us (34%)
  waiting for transfers between devices  26.7 us (27%)
    ppermute x18, waiting for transfers between devices, traded(): landed[shift] = lax.ppermute(blocks[shift], axes, pairs)  25.6 us
    ppermute x18, starting transfers between devices, traded(): landed[shift] = lax.ppermute(blocks[shift], axes, pairs)  20.1 us
    pallas_call x1, Pallas kernels, on_device(): pl.pallas_call(functools.partial(norm_pack_project_kernel, chunk_steps, r...  8.7 us
    pallas_call x2, Pallas kernels, project(): pl.pallas_call(functools.partial(project_kernel, begin), in_specs=[VMEM,...  8.15 us
    pallas_call x2, Pallas kernels, on_device(): pl.pallas_call(functools.partial(attend_kernel, chunk * chunk_steps, chun...  7.59 us
    ppermute x4, starting transfers between devices, on_device(): landed.append(lax.ppermute(block_rows, 'sub', pairs))  7.4 us
    ppermute x1, starting transfers between devices, on_device(): landed.append(lax.ppermute(joined, 'sub', pairs))  7.22 us
    pallas_call x1, Pallas kernels, on_device(): pl.pallas_call(functools.partial(norm_pack_kernel, chunk_steps, rows, flo...  3.45 us
  transfers between devices with their start and end apart: 28, of which 6 were waited for; matrix products, arithmetic and copies ran while one was open for 1% of the time, Pallas kernels for 32%

profile of v15, /device:TPU:11, one launch (start us, length us, event | category | flops | bytes accessed | tf_op | source)
XLA Modules:
  0.0 98.5 jit_solution(5796467640260805967)
XLA Ops:
  0.0 0.7 collective-permute-start
  0.8 0.1 collective-permute-start.1
  0.9 0.4 collective-permute-start.2
  1.3 3.5 %norm_and_pack.1 = (bf16[32,1792]{1,0:T(8,128)(2,1)}, bf16[32,1792]{1,0:T(8,128)(2,1)}, bf16[32,1792]{1,0:T(8,128)(2,1)}, bf16[32,1792]{1,0:T(8,128)(2,1)}) custom-call(s32[1,64]{1,0:T(1,128)} %bitcast.23, s32[1,32]{1,0:T(1,128)} %bitcast.25, s32[1,64]{1,0:T(1,128)} %bitcast.27, f32[28,128]{1,0:T(8,128)} %bitcast.19, bf16[256,3584]{1,0:T(8,128)(2,1)} %bitcast.29), custom_call_target="tpu_custom_call" | custom-call | flops 1 | bytes 1 | tf_op jit(solution)/shard_map/norm_and_pack/pallas_call | solution.py:514
  4.7 1.4 %collective-permute-start.6 = (bf16[32,1792]{1,0:T(8,128)(2,1)}, bf16[32,1792]{1,0:T(8,128)(2,1)S(1)}, u32[]{:S(2)}, u32[]{:S(2)}) collective-permute-start(bf16[32,1792]{1,0:T(8,128)(2,1)} %get-tuple-element.50), channel_id=1, source_target_pairs={{0,12},{4,8},{8,4},{12,0},{1,13},{5,9},{9,5},{13,1},{2,14},{6,10},... | collective-permute-start | bytes 344072 | tf_op jit(solution)/shard_map/ppermute | solution.py:429
  6.1 1.1 %collective-permute-start.7 = (bf16[32,1792]{1,0:T(8,128)(2,1)}, bf16[32,1792]{1,0:T(8,128)(2,1)S(1)}, u32[]{:S(2)}, u32[]{:S(2)}) collective-permute-start(bf16[32,1792]{1,0:T(8,128)(2,1)} %get-tuple-element.49), channel_id=1, source_target_pairs={{0,8},{4,12},{8,0},{12,4},{1,9},{5,13},{9,1},{13,5},{2,10},{6,14},... | collective-permute-start | bytes 344072 | tf_op jit(solution)/shard_map/ppermute | solution.py:429
  7.2 1.1 %collective-permute-start.8 = (bf16[32,1792]{1,0:T(8,128)(2,1)}, bf16[32,1792]{1,0:T(8,128)(2,1)S(1)}, u32[]{:S(2)}, u32[]{:S(2)}) collective-permute-start(bf16[32,1792]{1,0:T(8,128)(2,1)} %get-tuple-element.48), channel_id=1, source_target_pairs={{0,4},{4,0},{8,12},{12,8},{1,5},{5,1},{9,13},{13,9},{2,6},{6,2},{1... | collective-permute-start | bytes 344072 | tf_op jit(solution)/shard_map/ppermute | solution.py:429
  8.4 0.0 copy-start.8
  8.4 0.0 copy-start
  8.4 8.7 %norm_pack_project.1 = (bf16[256,3584]{1,0:T(8,128)(2,1)S(1)}, f32[256,1024]{1,0:T(8,128)S(1)}, s32[8,64]{1,0:T(8,128)S(1)}, bf16[32,1792]{1,0:T(8,128)(2,1)S(1)...) custom-call(s32[1,64]{1,0:T(1,128)S(1)} %bitcast.24, ...), custom_call_target="tpu_custom_call" | custom-call | flops 1 | bytes 1 | tf_op jit(solution)/shard_map/norm_pack_project/pallas_call | solution.py:544
  17.1 1.3 %collective-permute-start.3 = (bf16[32,1792]{1,0:T(8,128)(2,1)S(1)}, bf16[32,1792]{1,0:T(8,128)(2,1)S(1)}, u32[]{:S(2)}, u32[]{:S(2)}) collective-permute-start(bf16[32,1792]{1,0:T(8,128)(2,1)S(1)} %get-tuple-element.53), channel_id=1, source_target_pairs={{0,12},{4,8},{8,4},{12,0},{1,13},{5,9},{9,5},{13,1},{2,14},{6,10},... | collective-permute-start | bytes 344072 | tf_op jit(solution)/shard_map/ppermute | solution.py:429
  18.4 1.3 %collective-permute-start.4 = (bf16[32,1792]{1,0:T(8,128)(2,1)S(1)}, bf16[32,1792]{1,0:T(8,128)(2,1)S(1)}, u32[]{:S(2)}, u32[]{:S(2)}) collective-permute-start(bf16[32,1792]{1,0:T(8,128)(2,1)S(1)} %get-tuple-element.54), channel_id=1, source_target_pairs={{0,8},{4,12},{8,0},{12,4},{1,9},{5,13},{9,1},{13,5},{2,10},{6,14},... | collective-permute-start | bytes 344072 | tf_op jit(solution)/shard_map/ppermute | solution.py:429
  19.6 1.2 %collective-permute-start.5 = (bf16[32,1792]{1,0:T(8,128)(2,1)S(1)}, bf16[32,1792]{1,0:T(8,128)(2,1)S(1)}, u32[]{:S(2)}, u32[]{:S(2)}) collective-permute-start(bf16[32,1792]{1,0:T(8,128)(2,1)S(1)} %get-tuple-element.55), channel_id=1, source_target_pairs={{0,4},{4,0},{8,12},{12,8},{1,5},{5,1},{9,13},{13,9},{2,6},{6,2},{1... | collective-permute-start | bytes 344072 | tf_op jit(solution)/shard_map/ppermute | solution.py:429
  20.8 1.1 %down.2.refs_0_ = f32[128,128]{1,0:T(8,128)S(1)} custom-call(bf16[32,1792]{1,0:T(8,128)(2,1)S(1)} %collective-permute-done.6.refs_0_, bf16[32,1792]{1,0:T(8,128)(2,1)S(1)} %collective-permute-done.7.refs_1_, bf16[32,1792]{1,0:T(8,128)(2,1)S(1)} %collective-permute-done.8.refs_2_, bf16[32,1792]{1,0:T(8,128)(2,1)S(1)} %copy-done.5, ...), custom_call_target="tpu_custom_call" | custom-call | flops 1 | bytes 1 | tf_op jit(solution)/shard_map/down/pallas_call | solution.py:577
  22.0 0.3 collective-permute-start.9
  22.3 3.8 %project.2.refs_7_ = f32[256,512]{1,0:T(8,128)S(1)} custom-call(bf16[256,3584]{1,0:T(8,128)(2,1)S(1)} %get-tuple-element.59.rows_ref, f32[18,128]{1,0:T(8,128)S(1)} %bitcast.17, bf16[3584,2304]{1,0:T(8,128)(2,1)} %weight_hbm.3), custom_call_target="tpu_custom_call" | custom-call | flops 1 | bytes 1 | tf_op jit(solution)/shard_map/project/pallas_call | solution.py:565
  26.1 0.5 up.2
  26.6 1.2 %collective-permute-start.11 = (bf16[32,2048]{1,0:T(8,128)(2,1)S(1)}, bf16[32,2048]{1,0:T(8,128)(2,1)S(1)}, u32[]{:S(2)}, u32[]{:S(2)}) collective-permute-start(bf16[32,2048]{1,0:T(8,128)(2,1)S(1)} %get-tuple-element.65), channel_id=1, source_target_pairs={{0,12},{4,8},{8,4},{12,0},{1,13},{5,9},{9,5},{13,1},{2,14},{6,10},... | collective-permute-start | bytes 393224 | tf_op jit(solution)/shard_map/ppermute | solution.py:429
  27.8 1.3 %collective-permute-start.12 = (bf16[32,2048]{1,0:T(8,128)(2,1)S(1)}, bf16[32,2048]{1,0:T(8,128)(2,1)S(1)}, u32[]{:S(2)}, u32[]{:S(2)}) collective-permute-start(bf16[32,2048]{1,0:T(8,128)(2,1)S(1)} %get-tuple-element.64), channel_id=1, source_target_pairs={{0,8},{4,12},{8,0},{12,4},{1,9},{5,13},{9,1},{13,5},{2,10},{6,14},... | collective-permute-start | bytes 393224 | tf_op jit(solution)/shard_map/ppermute | solution.py:429
  29.1 1.1 %collective-permute-start.13 = (bf16[32,2048]{1,0:T(8,128)(2,1)S(1)}, bf16[32,2048]{1,0:T(8,128)(2,1)S(1)}, u32[]{:S(2)}, u32[]{:S(2)}) collective-permute-start(bf16[32,2048]{1,0:T(8,128)(2,1)S(1)} %get-tuple-element.63), channel_id=1, source_target_pairs={{0,4},{4,0},{8,12},{12,8},{1,5},{5,1},{9,13},{13,9},{2,6},{6,2},{1... | collective-permute-start | bytes 393224 | tf_op jit(solution)/shard_map/ppermute | solution.py:429
  30.2 0.1 compare_select_fusion
  30.3 1.2 %down.3.refs_0_ = f32[128,128]{1,0:T(8,128)S(1)} custom-call(bf16[32,1792]{1,0:T(8,128)(2,1)S(1)} %collective-permute-done.3.refs_0_, bf16[32,1792]{1,0:T(8,128)(2,1)S(1)} %collective-permute-done.4.refs_1_, bf16[32,1792]{1,0:T(8,128)(2,1)S(1)} %collective-permute-done.5.refs_2_, bf16[32,1792]{1,0:T(8,128)(2,1)S(1)} %get-tuple-element.66.refs_3_, ...), custom_call_target="tpu_custom_call" | custom-call | flops 1 | bytes 1 | tf_op jit(solution)/shard_map/down/pallas_call | solution.py:577
  31.4 1.3 %collective-permute-start.10 = (f32[128,128]{1,0:T(8,128)S(1)}, f32[128,128]{1,0:T(8,128)S(1)}, u32[]{:S(2)}, u32[]{:S(2)}) collective-permute-start(f32[128,128]{1,0:T(8,128)S(1)} %down.3.refs_0_), channel_id=1, source_target_pairs={{0,2},{2,0},{1,3},{3,1},{4,6},{6,4},{5,7},{7,5},{8,10},{10,8},{9,1... | collective-permute-start | bytes 196616 | tf_op jit(solution)/shard_map/ppermute | solution.py:438
  32.7 0.1 add_convert_fusion
  32.8 4.4 %project.3.refs_8_ = f32[256,768]{1,0:T(8,128)S(1)} custom-call(bf16[256,3584]{1,0:T(8,128)(2,1)S(1)} %get-tuple-element.59.rows_ref, f32[18,128]{1,0:T(8,128)S(1)} %bitcast.18, bf16[3584,2304]{1,0:T(8,128)(2,1)} %weight_hbm.3), custom_call_target="tpu_custom_call" | custom-call | flops 1 | bytes 1 | tf_op jit(solution)/shard_map/project/pallas_call | solution.py:565
  37.2 0.5 up.3
  37.7 0.4 collective-permute-start.14
  38.1 2.8 %collective-permute-start.15 = (bf16[32,2048]{1,0:T(8,128)(2,1)S(1)}, bf16[32,2048]{1,0:T(8,128)(2,1)S(1)}, u32[]{:S(2)}, u32[]{:S(2)}) collective-permute-start(bf16[32,2048]{1,0:T(8,128)(2,1)S(1)} %get-tuple-element.77), channel_id=1, source_target_pairs={{0,8},{4,12},{8,0},{12,4},{1,9},{5,13},{9,1},{13,5},{2,10},{6,14},... | collective-permute-start | bytes 393224 | tf_op jit(solution)/shard_map/ppermute | solution.py:429
  40.9 1.6 %collective-permute-start.16 = (bf16[32,2048]{1,0:T(8,128)(2,1)S(1)}, bf16[32,2048]{1,0:T(8,128)(2,1)S(1)}, u32[]{:S(2)}, u32[]{:S(2)}) collective-permute-start(bf16[32,2048]{1,0:T(8,128)(2,1)S(1)} %get-tuple-element.78), channel_id=1, source_target_pairs={{0,12},{4,8},{8,4},{12,0},{1,13},{5,9},{9,5},{13,1},{2,14},{6,10},... | collective-permute-start | bytes 393224 | tf_op jit(solution)/shard_map/ppermute | solution.py:429
  42.5 0.5 fusion
  43.1 3.9 %attend.2 = (f32[128,512]{1,0:T(8,128)S(1)}, bf16[64,1792]{1,0:T(8,128)(2,1)S(1)}, bf16[64,1792]{1,0:T(8,128)(2,1)S(1)}, bf16[64,1792]{1,0:T(8,128)(2,1)S(1)}, bf16[64,1792]{1,0:T(8,128)(2,1)S(1)}) custom-call(s32[8,64]{1,0:T(8,128)S(1)} %get-tuple-element.73.refs_0_, s32[1,64]{1,0:T(1,128)S(1)} %bitcast.21, f32[256,128]{1,0:T(8,128)S(1)} %get-tuple-element.90.refs_2_, ...), custom_call_target="tpu_custom_call" | custom-call | flops 1 | bytes 1 | tf_op jit(solution)/shard_map/attend/pallas_call | solution.py:630
  47.0 8.4 %collective-permute-done.16.refs_9_ = bf16[32,2048]{1,0:T(8,128)(2,1)S(1)} collective-permute-done((bf16[32,2048]{1,0:T(8,128)(2,1)S(1)}, bf16[32,2048]{1,0:T(8,128)(2,1)S(1)}, u32[]{:S(2)}, u32[]{:S(2)}) %collective-permute-start.16) | collective-permute-done | bytes 131104 | tf_op jit(solution)/shard_map/ppermute | solution.py:429
  55.5 0.6 collective-permute-start.19
  56.0 2.1 %collective-permute-start.17 = (bf16[64,1792]{1,0:T(8,128)(2,1)S(1)}, bf16[64,1792]{1,0:T(8,128)(2,1)S(1)}, u32[]{:S(2)}, u32[]{:S(2)}) collective-permute-start(bf16[64,1792]{1,0:T(8,128)(2,1)S(1)} %get-tuple-element.79), channel_id=1, source_target_pairs={{0,4},{4,0},{8,12},{12,8},{1,5},{5,1},{9,13},{13,9},{2,6},{6,2},{1... | collective-permute-start | bytes 688136 | tf_op jit(solution)/shard_map/ppermute | solution.py:429
  58.1 3.7 %attend.3 = (bf16[64,1792]{1,0:T(8,128)(2,1)S(1)}, bf16[64,1792]{1,0:T(8,128)(2,1)S(1)}, bf16[64,1792]{1,0:T(8,128)(2,1)S(1)}, bf16[64,1792]{1,0:T(8,128)(2,1)S(1)}) custom-call(s32[8,64]{1,0:T(8,128)S(1)} %get-tuple-element.73.refs_0_, s32[1,64]{1,0:T(1,128)S(1)} %bitcast.22, f32[256,128]{1,0:T(8,128)S(1)} %get-tuple-element.90.refs_2_, ...), custom_call_target="tpu_custom_call" | custom-call | flops 1 | bytes 1 | tf_op jit(solution)/shard_map/attend/pallas_call | solution.py:630
  61.8 0.1 collective-permute-start.21
  61.9 1.7 %collective-permute-start.22 = (bf16[64,1792]{1,0:T(8,128)(2,1)S(1)}, bf16[64,1792]{1,0:T(8,128)(2,1)S(1)}, u32[]{:S(2)}, u32[]{:S(2)}) collective-permute-start(bf16[64,1792]{1,0:T(8,128)(2,1)S(1)} %get-tuple-element.87), channel_id=1, source_target_pairs={{0,8},{4,12},{8,0},{12,4},{1,9},{5,13},{9,1},{13,5},{2,10},{6,14},... | collective-permute-start | bytes 688136 | tf_op jit(solution)/shard_map/ppermute | solution.py:429
  63.6 4.1 %collective-permute-done.19.refs_3_ = bf16[64,1792]{1,0:T(8,128)(2,1)S(1)} collective-permute-done((bf16[64,1792]{1,0:T(8,128)(2,1)S(1)}, bf16[64,1792]{1,0:T(8,128)(2,1)S(1)}, u32[]{:S(2)}, u32[]{:S(2)}) %collective-permute-start.19) | collective-permute-done | bytes 229408 | tf_op jit(solution)/shard_map/ppermute | solution.py:429
  67.8 4.0 %collective-permute-done.18.refs_2_ = bf16[64,1792]{1,0:T(8,128)(2,1)S(1)} collective-permute-done((bf16[64,1792]{1,0:T(8,128)(2,1)S(1)}, bf16[64,1792]{1,0:T(8,128)(2,1)S(1)}, u32[]{:S(2)}, u32[]{:S(2)}) %collective-permute-start.18) | collective-permute-done | bytes 229408 | tf_op jit(solution)/shard_map/ppermute | solution.py:429
  71.8 7.2 %collective-permute-start.20 = (bf16[128,1792]{1,0:T(8,128)(2,1)S(1)}, bf16[128,1792]{1,0:T(8,128)(2,1)S(1)}, u32[]{:S(2)}, u32[]{:S(2)}) collective-permute-start(bf16[128,1792]{1,0:T(8,128)(2,1)S(1)} %pad_maximum_fusion), channel_id=1, source_target_pairs={{0,1},{1,0},{2,3},{3,2},{4,5},{5,4},{6,7},{7,6},{8,9},{9,8},{10,11... | collective-permute-start | bytes 1376264 | tf_op jit(solution)/shard_map/ppermute | solution.py:691
  79.0 0.1 collective-permute-start.24
  79.1 1.0 collective-permute-start.25
  80.1 6.4 %collective-permute-done.22.refs_7_ = bf16[64,1792]{1,0:T(8,128)(2,1)S(1)} collective-permute-done((bf16[64,1792]{1,0:T(8,128)(2,1)S(1)}, bf16[64,1792]{1,0:T(8,128)(2,1)S(1)}, u32[]{:S(2)}, u32[]{:S(2)}) %collective-permute-start.22) | collective-permute-done | bytes 229408 | tf_op jit(solution)/shard_map/ppermute | solution.py:429
  86.5 4.3 %collective-permute-start.26 = (bf16[64,1792]{1,0:T(8,128)(2,1)S(1)}, bf16[64,1792]{1,0:T(8,128)(2,1)S(1)}, u32[]{:S(2)}, u32[]{:S(2)}) collective-permute-start(bf16[64,1792]{1,0:T(8,128)(2,1)S(1)} %collective-permute-done.22.refs_7_), channel_id=1, source_target_pairs={{0,1},{1,0},{2,3},{3,2},{4,5},{5,4},{6,7},{7,6},{8,9},{9,8},{10,11... | collective-permute-start | bytes 688136 | tf_op jit(solution)/shard_map/ppermute | solution.py:695
  90.9 2.6 %collective-permute-done.23.refs_8_ = bf16[64,1792]{1,0:T(8,128)(2,1)S(1)} collective-permute-done((bf16[64,1792]{1,0:T(8,128)(2,1)S(1)}, bf16[64,1792]{1,0:T(8,128)(2,1)S(1)}, u32[]{:S(2)}, u32[]{:S(2)}) %collective-permute-start.23) | collective-permute-done | bytes 229408 | tf_op jit(solution)/shard_map/ppermute | solution.py:429
  93.5 2.0 %collective-permute-start.27 = (bf16[64,1792]{1,0:T(8,128)(2,1)S(1)}, bf16[64,1792]{1,0:T(8,128)(2,1)S(1)}, u32[]{:S(2)}, u32[]{:S(2)}) collective-permute-start(bf16[64,1792]{1,0:T(8,128)(2,1)S(1)} %collective-permute-done.23.refs_8_), channel_id=1, source_target_pairs={{0,1},{1,0},{2,3},{3,2},{4,5},{5,4},{6,7},{7,6},{8,9},{9,8},{10,11... | collective-permute-start | bytes 688136 | tf_op jit(solution)/shard_map/ppermute | solution.py:695
  95.5 1.1 %collective-permute-done.27.refs_12_ = bf16[64,1792]{1,0:T(8,128)(2,1)S(1)} collective-permute-done((bf16[64,1792]{1,0:T(8,128)(2,1)S(1)}, bf16[64,1792]{1,0:T(8,128)(2,1)S(1)}, u32[]{:S(2)}, u32[]{:S(2)}) %collective-permute-start.27) | collective-permute-done | bytes 229408 | tf_op jit(solution)/shard_map/ppermute | solution.py:695
  96.6 1.9 %place.1 = bf16[128,4,1792]{2,1,0:T(4,128)(2,1)} custom-call(bf16[64,1792]{1,0:T(8,128)(2,1)S(1)} %get-tuple-element.74.refs_0_, bf16[64,1792]{1,0:T(8,128)(2,1)S(1)} %collective-permute-done.17.refs_1_, bf16[64,1792]{1,0:T(8,128)(2,1)S(1)} %collective-permute-done.18.refs_2_, bf16[64,1792]{1,0:T(8,128)(2,1)S(1)} %collective-permute-done.19.refs_3_, ...), custom_call_target="tpu_custom_call" | custom-call | flops 1 | bytes 1 | tf_op jit(solution)/shard_map/place/pallas_call | solution.py:698
  (53 shorter events, 0.2 us)
Async XLA Ops:
  0.0 8.3 %copy-start.9 = (s32[64,1]{0,1:T(1,128)S(1)}, s32[64,1]{0,1:T(1,128)}, u32[]{:S(2)}) copy-start(s32[64,1]{0,1:T(1,128)} %param.17) | copy-start | bytes 772
  0.0 8.3 %copy-start.10 = (s32[32]{0:T(128)S(1)}, s32[32]{0:T(128)}, u32[]{:S(2)}) copy-start(s32[32]{0:T(128)} %param.18) | copy-start | bytes 388
  0.0 8.3 %copy-start.11 = (s32[64,1]{0,1:T(1,128)S(1)}, s32[64,1]{0,1:T(1,128)}, u32[]{:S(2)}) copy-start(s32[64,1]{0,1:T(1,128)} %param.25) | copy-start | bytes 772
  0.0 8.3 %copy-start.7 = (f32[3584]{0:T(1024)S(1)}, f32[3584]{0:T(1024)}, u32[]{:S(2)}) copy-start(f32[3584]{0:T(1024)} %param.14) | copy-start | bytes 43012
  0.0 8.3 %copy-start.6 = (f32[2304]{0:T(1024)S(1)}, f32[2304]{0:T(1024)}, u32[]{:S(2)}) copy-start(f32[2304]{0:T(1024)} %param.16) | copy-start | bytes 27652
  0.0 8.3 %collective-permute-start = (bf16[4,1792,128]{2,1,0:T(8,128)(2,1)}, bf16[4,1792,128]{2,1,0:T(8,128)(2,1)S(1)}, u32[]{:S(2)}, u32[]{:S(2)}) collective-permute-start(bf16[4,1792,128]{2,1,0:T(8,128)(2,1)} %refs_4_.5), channel_id=1, source_target_pairs={{0,1},{1,0},{2,3},{3,2},{4,5},{5,4},{6,7},{7,6},{8,9},{9,8},{10,11... | collective-permute-start | bytes 5505032 | tf_op jit(solution)/shard_map/ppermute | solution.py:438
  0.8 7.6 %collective-permute-start.1 = (bf16[256,1792]{1,0:T(8,128)(2,1)}, bf16[256,1792]{1,0:T(8,128)(2,1)S(1)}, u32[]{:S(2)}, u32[]{:S(2)}) collective-permute-start(bf16[256,1792]{1,0:T(8,128)(2,1)} %bitcast.10), channel_id=1, source_target_pairs={{0,1},{1,0},{2,3},{3,2},{4,5},{5,4},{6,7},{7,6},{8,9},{9,8},{10,11... | collective-permute-start | bytes 2752520 | tf_op jit(solution)/shard_map/ppermute | solution.py:438
  0.9 6.3 %collective-permute-start.2 = (bf16[256,256]{1,0:T(8,128)(2,1)}, bf16[256,256]{1,0:T(8,128)(2,1)S(1)}, u32[]{:S(2)}, u32[]{:S(2)}) collective-permute-start(bf16[256,256]{1,0:T(8,128)(2,1)} %bitcast.13), channel_id=1, source_target_pairs={{0,1},{1,0},{2,3},{3,2},{4,5},{5,4},{6,7},{7,6},{8,9},{9,8},{10,11... | collective-permute-start | bytes 393224 | tf_op jit(solution)/shard_map/ppermute | solution.py:438
  4.7 14.9 %collective-permute-start.6 = (bf16[32,1792]{1,0:T(8,128)(2,1)}, bf16[32,1792]{1,0:T(8,128)(2,1)S(1)}, u32[]{:S(2)}, u32[]{:S(2)}) collective-permute-start(bf16[32,1792]{1,0:T(8,128)(2,1)} %get-tuple-element.50), channel_id=1, source_target_pairs={{0,12},{4,8},{8,4},{12,0},{1,13},{5,9},{9,5},{13,1},{2,14},{6,10},... | collective-permute-start | bytes 344072 | tf_op jit(solution)/shard_map/ppermute | solution.py:429
  6.1 14.7 %collective-permute-start.7 = (bf16[32,1792]{1,0:T(8,128)(2,1)}, bf16[32,1792]{1,0:T(8,128)(2,1)S(1)}, u32[]{:S(2)}, u32[]{:S(2)}) collective-permute-start(bf16[32,1792]{1,0:T(8,128)(2,1)} %get-tuple-element.49), channel_id=1, source_target_pairs={{0,8},{4,12},{8,0},{12,4},{1,9},{5,13},{9,1},{13,5},{2,10},{6,14},... | collective-permute-start | bytes 344072 | tf_op jit(solution)/shard_map/ppermute | solution.py:429
  7.2 13.6 %collective-permute-start.8 = (bf16[32,1792]{1,0:T(8,128)(2,1)}, bf16[32,1792]{1,0:T(8,128)(2,1)S(1)}, u32[]{:S(2)}, u32[]{:S(2)}) collective-permute-start(bf16[32,1792]{1,0:T(8,128)(2,1)} %get-tuple-element.48), channel_id=1, source_target_pairs={{0,4},{4,0},{8,12},{12,8},{1,5},{5,1},{9,13},{13,9},{2,6},{6,2},{1... | collective-permute-start | bytes 344072 | tf_op jit(solution)/shard_map/ppermute | solution.py:429
  8.4 10.0 %copy-start.8 = (s32[64]{0:T(128)S(1)}, s32[64]{0:T(128)}, u32[]{:S(2)}) copy-start(s32[64]{0:T(128)} %param.19) | copy-start | bytes 772
  8.4 12.4 %copy-start = (bf16[4,1792,128]{2,1,0:T(8,128)(2,1)S(1)}, bf16[4,1792,128]{2,1,0:T(8,128)(2,1)}, u32[]{:S(2)}) copy-start(bf16[4,1792,128]{2,1,0:T(8,128)(2,1)} %refs_4_.5) | copy-start | bytes 5505028
  8.4 12.4 %copy-start.5 = (bf16[32,1792]{1,0:T(8,128)(2,1)S(1)}, bf16[32,1792]{1,0:T(8,128)(2,1)}, u32[]{:S(2)}) copy-start(bf16[32,1792]{1,0:T(8,128)(2,1)} %get-tuple-element.58.refs_3_) | copy-start | bytes 344068
  17.1 12.0 %collective-permute-start.3 = (bf16[32,1792]{1,0:T(8,128)(2,1)S(1)}, bf16[32,1792]{1,0:T(8,128)(2,1)S(1)}, u32[]{:S(2)}, u32[]{:S(2)}) collective-permute-start(bf16[32,1792]{1,0:T(8,128)(2,1)S(1)} %get-tuple-element.53), channel_id=1, source_target_pairs={{0,12},{4,8},{8,4},{12,0},{1,13},{5,9},{9,5},{13,1},{2,14},{6,10},... | collective-permute-start | bytes 344072 | tf_op jit(solution)/shard_map/ppermute | solution.py:429
  18.4 11.9 %collective-permute-start.4 = (bf16[32,1792]{1,0:T(8,128)(2,1)S(1)}, bf16[32,1792]{1,0:T(8,128)(2,1)S(1)}, u32[]{:S(2)}, u32[]{:S(2)}) collective-permute-start(bf16[32,1792]{1,0:T(8,128)(2,1)S(1)} %get-tuple-element.54), channel_id=1, source_target_pairs={{0,8},{4,12},{8,0},{12,4},{1,9},{5,13},{9,1},{13,5},{2,10},{6,14},... | collective-permute-start | bytes 344072 | tf_op jit(solution)/shard_map/ppermute | solution.py:429
  19.6 10.6 %collective-permute-start.5 = (bf16[32,1792]{1,0:T(8,128)(2,1)S(1)}, bf16[32,1792]{1,0:T(8,128)(2,1)S(1)}, u32[]{:S(2)}, u32[]{:S(2)}) collective-permute-start(bf16[32,1792]{1,0:T(8,128)(2,1)S(1)} %get-tuple-element.55), channel_id=1, source_target_pairs={{0,4},{4,0},{8,12},{12,8},{1,5},{5,1},{9,13},{13,9},{2,6},{6,2},{1... | collective-permute-start | bytes 344072 | tf_op jit(solution)/shard_map/ppermute | solution.py:429
  22.0 4.1 %collective-permute-start.9 = (f32[128,128]{1,0:T(8,128)S(1)}, f32[128,128]{1,0:T(8,128)S(1)}, u32[]{:S(2)}, u32[]{:S(2)}) collective-permute-start(f32[128,128]{1,0:T(8,128)S(1)} %down.2.refs_0_), channel_id=1, source_target_pairs={{0,2},{2,0},{1,3},{3,1},{4,6},{6,4},{5,7},{7,5},{8,10},{10,8},{9,1... | collective-permute-start | bytes 196616 | tf_op jit(solution)/shard_map/ppermute | solution.py:438
  22.3 3.8 %copy-start.3 = (bf16[4,64,1792]{2,1,0:T(8,128)(2,1)S(1)}, bf16[4,64,1792]{2,1,0:T(8,128)(2,1)}, u32[]{:S(2)}) copy-start(bf16[4,64,1792]{2,1,0:T(8,128)(2,1)} %param.23) | copy-start | bytes 2752516
  22.3 3.8 %copy-start.4 = (bf16[4,64,256]{2,1,0:T(8,128)(2,1)S(1)}, bf16[4,64,256]{2,1,0:T(8,128)(2,1)}, u32[]{:S(2)}) copy-start(bf16[4,64,256]{2,1,0:T(8,128)(2,1)} %param.24) | copy-start | bytes 393220
  26.6 14.3 %collective-permute-start.11 = (bf16[32,2048]{1,0:T(8,128)(2,1)S(1)}, bf16[32,2048]{1,0:T(8,128)(2,1)S(1)}, u32[]{:S(2)}, u32[]{:S(2)}) collective-permute-start(bf16[32,2048]{1,0:T(8,128)(2,1)S(1)} %get-tuple-element.65), channel_id=1, source_target_pairs={{0,12},{4,8},{8,4},{12,0},{1,13},{5,9},{9,5},{13,1},{2,14},{6,10},... | collective-permute-start | bytes 393224 | tf_op jit(solution)/shard_map/ppermute | solution.py:429
  27.8 10.3 %collective-permute-start.12 = (bf16[32,2048]{1,0:T(8,128)(2,1)S(1)}, bf16[32,2048]{1,0:T(8,128)(2,1)S(1)}, u32[]{:S(2)}, u32[]{:S(2)}) collective-permute-start(bf16[32,2048]{1,0:T(8,128)(2,1)S(1)} %get-tuple-element.64), channel_id=1, source_target_pairs={{0,8},{4,12},{8,0},{12,4},{1,9},{5,13},{9,1},{13,5},{2,10},{6,14},... | collective-permute-start | bytes 393224 | tf_op jit(solution)/shard_map/ppermute | solution.py:429
  29.1 8.6 %collective-permute-start.13 = (bf16[32,2048]{1,0:T(8,128)(2,1)S(1)}, bf16[32,2048]{1,0:T(8,128)(2,1)S(1)}, u32[]{:S(2)}, u32[]{:S(2)}) collective-permute-start(bf16[32,2048]{1,0:T(8,128)(2,1)S(1)} %get-tuple-element.63), channel_id=1, source_target_pairs={{0,4},{4,0},{8,12},{12,8},{1,5},{5,1},{9,13},{13,9},{2,6},{6,2},{1... | collective-permute-start | bytes 393224 | tf_op jit(solution)/shard_map/ppermute | solution.py:429
  31.4 5.7 %collective-permute-start.10 = (f32[128,128]{1,0:T(8,128)S(1)}, f32[128,128]{1,0:T(8,128)S(1)}, u32[]{:S(2)}, u32[]{:S(2)}) collective-permute-start(f32[128,128]{1,0:T(8,128)S(1)} %down.3.refs_0_), channel_id=1, source_target_pairs={{0,2},{2,0},{1,3},{3,1},{4,6},{6,4},{5,7},{7,5},{8,10},{10,8},{9,1... | collective-permute-start | bytes 196616 | tf_op jit(solution)/shard_map/ppermute | solution.py:438
  37.2 5.9 %copy-start.1 = (bf16[64,32,256]{2,1,0:T(8,128)(2,1)S(1)}, bf16[64,32,256]{2,1,0:T(8,128)(2,1)}, u32[]{:S(2)}) copy-start(bf16[64,32,256]{2,1,0:T(8,128)(2,1)} %refs_4_.7) | copy-start | bytes 3145732
  37.2 5.9 %copy-start.2 = (bf16[64,32,256]{2,1,0:T(8,128)(2,1)S(1)}, bf16[64,32,256]{2,1,0:T(8,128)(2,1)}, u32[]{:S(2)}) copy-start(bf16[64,32,256]{2,1,0:T(8,128)(2,1)} %refs_5_.3) | copy-start | bytes 3145732
  37.7 9.3 %collective-permute-start.14 = (bf16[32,2048]{1,0:T(8,128)(2,1)S(1)}, bf16[32,2048]{1,0:T(8,128)(2,1)S(1)}, u32[]{:S(2)}, u32[]{:S(2)}) collective-permute-start(bf16[32,2048]{1,0:T(8,128)(2,1)S(1)} %get-tuple-element.76), channel_id=1, source_target_pairs={{0,4},{4,0},{8,12},{12,8},{1,5},{5,1},{9,13},{13,9},{2,6},{6,2},{1... | collective-permute-start | bytes 393224 | tf_op jit(solution)/shard_map/ppermute | solution.py:429
  38.1 8.9 %collective-permute-start.15 = (bf16[32,2048]{1,0:T(8,128)(2,1)S(1)}, bf16[32,2048]{1,0:T(8,128)(2,1)S(1)}, u32[]{:S(2)}, u32[]{:S(2)}) collective-permute-start(bf16[32,2048]{1,0:T(8,128)(2,1)S(1)} %get-tuple-element.77), channel_id=1, source_target_pairs={{0,8},{4,12},{8,0},{12,4},{1,9},{5,13},{9,1},{13,5},{2,10},{6,14},... | collective-permute-start | bytes 393224 | tf_op jit(solution)/shard_map/ppermute | solution.py:429
  40.9 14.6 %collective-permute-start.16 = (bf16[32,2048]{1,0:T(8,128)(2,1)S(1)}, bf16[32,2048]{1,0:T(8,128)(2,1)S(1)}, u32[]{:S(2)}, u32[]{:S(2)}) collective-permute-start(bf16[32,2048]{1,0:T(8,128)(2,1)S(1)} %get-tuple-element.78), channel_id=1, source_target_pairs={{0,12},{4,8},{8,4},{12,0},{1,13},{5,9},{9,5},{13,1},{2,14},{6,10},... | collective-permute-start | bytes 393224 | tf_op jit(solution)/shard_map/ppermute | solution.py:429
  55.5 12.3 %collective-permute-start.19 = (bf16[64,1792]{1,0:T(8,128)(2,1)S(1)}, bf16[64,1792]{1,0:T(8,128)(2,1)S(1)}, u32[]{:S(2)}, u32[]{:S(2)}) collective-permute-start(bf16[64,1792]{1,0:T(8,128)(2,1)S(1)} %get-tuple-element.83), channel_id=1, source_target_pairs={{0,12},{4,8},{8,4},{12,0},{1,13},{5,9},{9,5},{13,1},{2,14},{6,10},... | collective-permute-start | bytes 688136 | tf_op jit(solution)/shard_map/ppermute | solution.py:429
  56.0 15.7 %collective-permute-start.18 = (bf16[64,1792]{1,0:T(8,128)(2,1)S(1)}, bf16[64,1792]{1,0:T(8,128)(2,1)S(1)}, u32[]{:S(2)}, u32[]{:S(2)}) collective-permute-start(bf16[64,1792]{1,0:T(8,128)(2,1)S(1)} %get-tuple-element.81), channel_id=1, source_target_pairs={{0,8},{4,12},{8,0},{12,4},{1,9},{5,13},{9,1},{13,5},{2,10},{6,14},... | collective-permute-start | bytes 688136 | tf_op jit(solution)/shard_map/ppermute | solution.py:429
  56.0 15.7 %collective-permute-start.17 = (bf16[64,1792]{1,0:T(8,128)(2,1)S(1)}, bf16[64,1792]{1,0:T(8,128)(2,1)S(1)}, u32[]{:S(2)}, u32[]{:S(2)}) collective-permute-start(bf16[64,1792]{1,0:T(8,128)(2,1)S(1)} %get-tuple-element.79), channel_id=1, source_target_pairs={{0,4},{4,0},{8,12},{12,8},{1,5},{5,1},{9,13},{13,9},{2,6},{6,2},{1... | collective-permute-start | bytes 688136 | tf_op jit(solution)/shard_map/ppermute | solution.py:429
  61.8 17.3 %collective-permute-start.21 = (bf16[64,1792]{1,0:T(8,128)(2,1)S(1)}, bf16[64,1792]{1,0:T(8,128)(2,1)S(1)}, u32[]{:S(2)}, u32[]{:S(2)}) collective-permute-start(bf16[64,1792]{1,0:T(8,128)(2,1)S(1)} %get-tuple-element.86), channel_id=1, source_target_pairs={{0,4},{4,0},{8,12},{12,8},{1,5},{5,1},{9,13},{13,9},{2,6},{6,2},{1... | collective-permute-start | bytes 688136 | tf_op jit(solution)/shard_map/ppermute | solution.py:429
  61.9 24.6 %collective-permute-start.22 = (bf16[64,1792]{1,0:T(8,128)(2,1)S(1)}, bf16[64,1792]{1,0:T(8,128)(2,1)S(1)}, u32[]{:S(2)}, u32[]{:S(2)}) collective-permute-start(bf16[64,1792]{1,0:T(8,128)(2,1)S(1)} %get-tuple-element.87), channel_id=1, source_target_pairs={{0,8},{4,12},{8,0},{12,4},{1,9},{5,13},{9,1},{13,5},{2,10},{6,14},... | collective-permute-start | bytes 688136 | tf_op jit(solution)/shard_map/ppermute | solution.py:429
  67.7 25.7 %collective-permute-start.23 = (bf16[64,1792]{1,0:T(8,128)(2,1)S(1)}, bf16[64,1792]{1,0:T(8,128)(2,1)S(1)}, u32[]{:S(2)}, u32[]{:S(2)}) collective-permute-start(bf16[64,1792]{1,0:T(8,128)(2,1)S(1)} %get-tuple-element.88), channel_id=1, source_target_pairs={{0,12},{4,8},{8,4},{12,0},{1,13},{5,9},{9,5},{13,1},{2,14},{6,10},... | collective-permute-start | bytes 688136 | tf_op jit(solution)/shard_map/ppermute | solution.py:429
  71.8 24.8 %collective-permute-start.20 = (bf16[128,1792]{1,0:T(8,128)(2,1)S(1)}, bf16[128,1792]{1,0:T(8,128)(2,1)S(1)}, u32[]{:S(2)}, u32[]{:S(2)}) collective-permute-start(bf16[128,1792]{1,0:T(8,128)(2,1)S(1)} %pad_maximum_fusion), channel_id=1, source_target_pairs={{0,1},{1,0},{2,3},{3,2},{4,5},{5,4},{6,7},{7,6},{8,9},{9,8},{10,11... | collective-permute-start | bytes 1376264 | tf_op jit(solution)/shard_map/ppermute | solution.py:691
  79.0 16.4 %collective-permute-start.24 = (bf16[64,1792]{1,0:T(8,128)(2,1)S(1)}, bf16[64,1792]{1,0:T(8,128)(2,1)S(1)}, u32[]{:S(2)}, u32[]{:S(2)}) collective-permute-start(bf16[64,1792]{1,0:T(8,128)(2,1)S(1)} %get-tuple-element.85.refs_5_), channel_id=1, source_target_pairs={{0,1},{1,0},{2,3},{3,2},{4,5},{5,4},{6,7},{7,6},{8,9},{9,8},{10,11... | collective-permute-start | bytes 688136 | tf_op jit(solution)/shard_map/ppermute | solution.py:695
  79.1 16.4 %collective-permute-start.25 = (bf16[64,1792]{1,0:T(8,128)(2,1)S(1)}, bf16[64,1792]{1,0:T(8,128)(2,1)S(1)}, u32[]{:S(2)}, u32[]{:S(2)}) collective-permute-start(bf16[64,1792]{1,0:T(8,128)(2,1)S(1)} %collective-permute-done.21.refs_6_), channel_id=1, source_target_pairs={{0,1},{1,0},{2,3},{3,2},{4,5},{5,4},{6,7},{7,6},{8,9},{9,8},{10,11... | collective-permute-start | bytes 688136 | tf_op jit(solution)/shard_map/ppermute | solution.py:695
  86.5 8.9 %collective-permute-start.26 = (bf16[64,1792]{1,0:T(8,128)(2,1)S(1)}, bf16[64,1792]{1,0:T(8,128)(2,1)S(1)}, u32[]{:S(2)}, u32[]{:S(2)}) collective-permute-start(bf16[64,1792]{1,0:T(8,128)(2,1)S(1)} %collective-permute-done.22.refs_7_), channel_id=1, source_target_pairs={{0,1},{1,0},{2,3},{3,2},{4,5},{5,4},{6,7},{7,6},{8,9},{9,8},{10,11... | collective-permute-start | bytes 688136 | tf_op jit(solution)/shard_map/ppermute | solution.py:695
  93.5 3.1 %collective-permute-start.27 = (bf16[64,1792]{1,0:T(8,128)(2,1)S(1)}, bf16[64,1792]{1,0:T(8,128)(2,1)S(1)}, u32[]{:S(2)}, u32[]{:S(2)}) collective-permute-start(bf16[64,1792]{1,0:T(8,128)(2,1)S(1)} %collective-permute-done.23.refs_8_), channel_id=1, source_target_pairs={{0,1},{1,0},{2,3},{3,2},{4,5},{5,4},{6,7},{7,6},{8,9},{9,8},{10,11... | collective-permute-start | bytes 688136 | tf_op jit(solution)/shard_map/ppermute | solution.py:695

commit v16 on v15

--- a/solution.py
+++ b/solution.py
@@ -672,7 +672,7 @@
         results = list(results)
         for lane in range(1, lanes):
             if not alongs:
-                results[lane] = held(results[lane], returned[-1][1:])
+                results[lane] = held(results[lane], returned[-1][lanes - lane])
         along = traded(results, "streams")
         alongs.append(along)
 

time: 98.7 us -> 95.8 us (0.971)
  the two profiles are of different devices: /device:TPU:11 before, /device:TPU:0 now
where the time goes in v16:
time: 95.8 us; the launch traced here: 94.3 us
  Pallas kernels  33.1 us (35%)
  waiting for transfers between devices  31.5 us (33%)
  starting transfers between devices  28.6 us (30%)
    ppermute x18, waiting for transfers between devices, traded(): landed[shift] = lax.ppermute(blocks[shift], axes, pairs)  30.2 us
    ppermute x18, starting transfers between devices, traded(): landed[shift] = lax.ppermute(blocks[shift], axes, pairs)  24.3 us
    pallas_call x1, Pallas kernels, on_device(): pl.pallas_call(functools.partial(norm_pack_project_kernel, chunk_steps, r...  8.69 us
    pallas_call x2, Pallas kernels, project(): pl.pallas_call(functools.partial(project_kernel, begin), in_specs=[VMEM,...  8.15 us
    pallas_call x2, Pallas kernels, on_device(): pl.pallas_call(functools.partial(attend_kernel, chunk * chunk_steps, chun...  7.6 us
    pallas_call x1, Pallas kernels, on_device(): pl.pallas_call(functools.partial(norm_pack_kernel, chunk_steps, rows, flo...  3.45 us
    ppermute x5, starting transfers between devices, from_others(): landed.append(lax.ppermute(block, axis, pairs))  3.2 us
    pallas_call x2, Pallas kernels, down(): pl.pallas_call(functools.partial(down_kernel, lanes, spots), in_specs=[VM...  2.3 us
  transfers between devices with their start and end apart: 28, of which 8 were waited for; matrix products, arithmetic and copies ran while one was open for 1% of the time, Pallas kernels for 33%

profile of v16, /device:TPU:0, one launch (start us, length us, event | category | flops | bytes accessed | tf_op | source)
XLA Modules:
  0.0 94.3 jit_solution(6111779572305507649)
XLA Ops:
  0.0 0.5 collective-permute-start
  0.5 0.1 collective-permute-start.1
  0.6 0.4 collective-permute-start.2
  1.1 3.5 %norm_and_pack.1 = (bf16[32,1792]{1,0:T(8,128)(2,1)}, bf16[32,1792]{1,0:T(8,128)(2,1)}, bf16[32,1792]{1,0:T(8,128)(2,1)}, bf16[32,1792]{1,0:T(8,128)(2,1)}) custom-call(s32[1,64]{1,0:T(1,128)} %bitcast.23, s32[1,32]{1,0:T(1,128)} %bitcast.25, s32[1,64]{1,0:T(1,128)} %bitcast.27, f32[28,128]{1,0:T(8,128)} %bitcast.19, bf16[256,3584]{1,0:T(8,128)(2,1)} %bitcast.29), custom_call_target="tpu_custom_call" | custom-call | flops 1 | bytes 1 | tf_op jit(solution)/shard_map/norm_and_pack/pallas_call | solution.py:514
  4.5 4.7 %collective-permute-start.6 = (bf16[32,1792]{1,0:T(8,128)(2,1)}, bf16[32,1792]{1,0:T(8,128)(2,1)S(1)}, u32[]{:S(2)}, u32[]{:S(2)}) collective-permute-start(bf16[32,1792]{1,0:T(8,128)(2,1)} %get-tuple-element.50), channel_id=1, source_target_pairs={{0,12},{4,8},{8,4},{12,0},{1,13},{5,9},{9,5},{13,1},{2,14},{6,10},... | collective-permute-start | bytes 344072 | tf_op jit(solution)/shard_map/ppermute | solution.py:429
  9.3 0.6 collective-permute-start.8
  10.0 0.0 copy-start.8
  10.0 0.0 copy-start
  10.0 0.0 copy-start.5
  10.0 8.7 %norm_pack_project.1 = (bf16[256,3584]{1,0:T(8,128)(2,1)S(1)}, f32[256,1024]{1,0:T(8,128)S(1)}, s32[8,64]{1,0:T(8,128)S(1)}, bf16[32,1792]{1,0:T(8,128)(2,1)S(1)...) custom-call(s32[1,64]{1,0:T(1,128)S(1)} %bitcast.24, ...), custom_call_target="tpu_custom_call" | custom-call | flops 1 | bytes 1 | tf_op jit(solution)/shard_map/norm_pack_project/pallas_call | solution.py:544
  18.7 3.8 %collective-permute-start.3 = (bf16[32,1792]{1,0:T(8,128)(2,1)S(1)}, bf16[32,1792]{1,0:T(8,128)(2,1)S(1)}, u32[]{:S(2)}, u32[]{:S(2)}) collective-permute-start(bf16[32,1792]{1,0:T(8,128)(2,1)S(1)} %get-tuple-element.53), channel_id=1, source_target_pairs={{0,12},{4,8},{8,4},{12,0},{1,13},{5,9},{9,5},{13,1},{2,14},{6,10},... | collective-permute-start | bytes 344072 | tf_op jit(solution)/shard_map/ppermute | solution.py:429
  22.5 0.6 collective-permute-start.5
  23.2 1.1 %down.2.refs_0_ = f32[128,128]{1,0:T(8,128)S(1)} custom-call(bf16[32,1792]{1,0:T(8,128)(2,1)S(1)} %collective-permute-done.6.refs_0_, bf16[32,1792]{1,0:T(8,128)(2,1)S(1)} %collective-permute-done.7.refs_1_, bf16[32,1792]{1,0:T(8,128)(2,1)S(1)} %collective-permute-done.8.refs_2_, bf16[32,1792]{1,0:T(8,128)(2,1)S(1)} %copy-done.5, ...), custom_call_target="tpu_custom_call" | custom-call | flops 1 | bytes 1 | tf_op jit(solution)/shard_map/down/pallas_call | solution.py:577
  24.3 1.7 %collective-permute-start.9 = (f32[128,128]{1,0:T(8,128)S(1)}, f32[128,128]{1,0:T(8,128)S(1)}, u32[]{:S(2)}, u32[]{:S(2)}) collective-permute-start(f32[128,128]{1,0:T(8,128)S(1)} %down.2.refs_0_), channel_id=1, source_target_pairs={{0,2},{2,0},{1,3},{3,1},{4,6},{6,4},{5,7},{7,5},{8,10},{10,8},{9,1... | collective-permute-start | bytes 196616 | tf_op jit(solution)/shard_map/ppermute | solution.py:438
  26.0 0.0 copy-start.4
  26.0 3.8 %project.2.refs_7_ = f32[256,512]{1,0:T(8,128)S(1)} custom-call(bf16[256,3584]{1,0:T(8,128)(2,1)S(1)} %get-tuple-element.59.rows_ref, f32[18,128]{1,0:T(8,128)S(1)} %bitcast.17, bf16[3584,2304]{1,0:T(8,128)(2,1)} %weight_hbm.3), custom_call_target="tpu_custom_call" | custom-call | flops 1 | bytes 1 | tf_op jit(solution)/shard_map/project/pallas_call | solution.py:565
  29.9 0.5 up.2
  30.4 3.7 %collective-permute-start.11 = (bf16[32,2048]{1,0:T(8,128)(2,1)S(1)}, bf16[32,2048]{1,0:T(8,128)(2,1)S(1)}, u32[]{:S(2)}, u32[]{:S(2)}) collective-permute-start(bf16[32,2048]{1,0:T(8,128)(2,1)S(1)} %get-tuple-element.65), channel_id=1, source_target_pairs={{0,12},{4,8},{8,4},{12,0},{1,13},{5,9},{9,5},{13,1},{2,14},{6,10},... | collective-permute-start | bytes 393224 | tf_op jit(solution)/shard_map/ppermute | solution.py:429
  34.0 0.8 collective-permute-start.13
  34.8 0.1 compare_select_fusion
  34.9 1.2 %down.3.refs_0_ = f32[128,128]{1,0:T(8,128)S(1)} custom-call(bf16[32,1792]{1,0:T(8,128)(2,1)S(1)} %collective-permute-done.3.refs_0_, bf16[32,1792]{1,0:T(8,128)(2,1)S(1)} %collective-permute-done.4.refs_1_, bf16[32,1792]{1,0:T(8,128)(2,1)S(1)} %collective-permute-done.5.refs_2_, bf16[32,1792]{1,0:T(8,128)(2,1)S(1)} %get-tuple-element.66.refs_3_, ...), custom_call_target="tpu_custom_call" | custom-call | flops 1 | bytes 1 | tf_op jit(solution)/shard_map/down/pallas_call | solution.py:577
  36.1 0.5 collective-permute-start.10
  36.6 0.1 add_convert_fusion
  36.6 4.4 %project.3.refs_8_ = f32[256,768]{1,0:T(8,128)S(1)} custom-call(bf16[256,3584]{1,0:T(8,128)(2,1)S(1)} %get-tuple-element.59.rows_ref, f32[18,128]{1,0:T(8,128)S(1)} %bitcast.18, bf16[3584,2304]{1,0:T(8,128)(2,1)} %weight_hbm.3), custom_call_target="tpu_custom_call" | custom-call | flops 1 | bytes 1 | tf_op jit(solution)/shard_map/project/pallas_call | solution.py:565
  41.0 0.0 copy-start.1
  41.0 0.0 copy-start.2
  41.0 0.5 up.3
  41.5 3.8 %collective-permute-start.14 = (bf16[32,2048]{1,0:T(8,128)(2,1)S(1)}, bf16[32,2048]{1,0:T(8,128)(2,1)S(1)}, u32[]{:S(2)}, u32[]{:S(2)}) collective-permute-start(bf16[32,2048]{1,0:T(8,128)(2,1)S(1)} %get-tuple-element.76), channel_id=1, source_target_pairs={{0,12},{4,8},{8,4},{12,0},{1,13},{5,9},{9,5},{13,1},{2,14},{6,10},... | collective-permute-start | bytes 393224 | tf_op jit(solution)/shard_map/ppermute | solution.py:429
  45.3 3.5 %collective-permute-done.12.refs_10_ = bf16[32,2048]{1,0:T(8,128)(2,1)S(1)} collective-permute-done((bf16[32,2048]{1,0:T(8,128)(2,1)S(1)}, bf16[32,2048]{1,0:T(8,128)(2,1)S(1)}, u32[]{:S(2)}, u32[]{:S(2)}) %collective-permute-start.12) | collective-permute-done | bytes 131104 | tf_op jit(solution)/shard_map/ppermute | solution.py:429
  48.8 0.5 fusion
  49.4 3.9 %attend.2 = (f32[128,512]{1,0:T(8,128)S(1)}, bf16[64,1792]{1,0:T(8,128)(2,1)S(1)}, bf16[64,1792]{1,0:T(8,128)(2,1)S(1)}, bf16[64,1792]{1,0:T(8,128)(2,1)S(1)}, bf16[64,1792]{1,0:T(8,128)(2,1)S(1)}) custom-call(s32[8,64]{1,0:T(8,128)S(1)} %get-tuple-element.73.refs_0_, s32[1,64]{1,0:T(1,128)S(1)} %bitcast.21, f32[256,128]{1,0:T(8,128)S(1)} %get-tuple-element.90.refs_2_, ...), custom_call_target="tpu_custom_call" | custom-call | flops 1 | bytes 1 | tf_op jit(solution)/shard_map/attend/pallas_call | solution.py:630
  53.3 4.6 %collective-permute-done.18.refs_11_ = bf16[32,2048]{1,0:T(8,128)(2,1)S(1)} collective-permute-done((bf16[32,2048]{1,0:T(8,128)(2,1)S(1)}, bf16[32,2048]{1,0:T(8,128)(2,1)S(1)}, u32[]{:S(2)}, u32[]{:S(2)}) %collective-permute-start.18) | collective-permute-done | bytes 131104 | tf_op jit(solution)/shard_map/ppermute | solution.py:429
  57.9 0.5 collective-permute-start.19
  58.4 2.6 %collective-permute-done.16.refs_10_ = bf16[32,2048]{1,0:T(8,128)(2,1)S(1)} collective-permute-done((bf16[32,2048]{1,0:T(8,128)(2,1)S(1)}, bf16[32,2048]{1,0:T(8,128)(2,1)S(1)}, u32[]{:S(2)}, u32[]{:S(2)}) %collective-permute-start.16) | collective-permute-done | bytes 131104 | tf_op jit(solution)/shard_map/ppermute | solution.py:429
  61.1 1.3 %collective-permute-start.15 = (bf16[64,1792]{1,0:T(8,128)(2,1)S(1)}, bf16[64,1792]{1,0:T(8,128)(2,1)S(1)}, u32[]{:S(2)}, u32[]{:S(2)}) collective-permute-start(bf16[64,1792]{1,0:T(8,128)(2,1)S(1)} %get-tuple-element.77), channel_id=1, source_target_pairs={{0,4},{4,0},{8,12},{12,8},{1,5},{5,1},{9,13},{13,9},{2,6},{6,2},{1... | collective-permute-start | bytes 688136 | tf_op jit(solution)/shard_map/ppermute | solution.py:429
  62.3 3.7 %attend.3 = (bf16[64,1792]{1,0:T(8,128)(2,1)S(1)}, bf16[64,1792]{1,0:T(8,128)(2,1)S(1)}, bf16[64,1792]{1,0:T(8,128)(2,1)S(1)}, bf16[64,1792]{1,0:T(8,128)(2,1)S(1)}) custom-call(s32[8,64]{1,0:T(8,128)S(1)} %get-tuple-element.73.refs_0_, s32[1,64]{1,0:T(1,128)S(1)} %bitcast.22, f32[256,128]{1,0:T(8,128)S(1)} %get-tuple-element.90.refs_2_, ...), custom_call_target="tpu_custom_call" | custom-call | flops 1 | bytes 1 | tf_op jit(solution)/shard_map/attend/pallas_call | solution.py:630
  66.1 0.8 collective-permute-start.21
  66.9 2.9 %collective-permute-start.22 = (bf16[64,1792]{1,0:T(8,128)(2,1)S(1)}, bf16[64,1792]{1,0:T(8,128)(2,1)S(1)}, u32[]{:S(2)}, u32[]{:S(2)}) collective-permute-start(bf16[64,1792]{1,0:T(8,128)(2,1)S(1)} %get-tuple-element.87), channel_id=1, source_target_pairs={{0,8},{4,12},{8,0},{12,4},{1,9},{5,13},{9,1},{13,5},{2,10},{6,14},... | collective-permute-start | bytes 688136 | tf_op jit(solution)/shard_map/ppermute | solution.py:429
  69.8 0.7 collective-permute-start.23
  70.5 10.3 %collective-permute-done.17.refs_2_ = bf16[64,1792]{1,0:T(8,128)(2,1)S(1)} collective-permute-done((bf16[64,1792]{1,0:T(8,128)(2,1)S(1)}, bf16[64,1792]{1,0:T(8,128)(2,1)S(1)}, u32[]{:S(2)}, u32[]{:S(2)}) %collective-permute-start.17) | collective-permute-done | bytes 229408 | tf_op jit(solution)/shard_map/ppermute | solution.py:429
  80.9 0.1 collective-permute-start.20
  81.0 0.5 collective-permute-start.24
  81.5 0.2 collective-permute-done.21.refs_6_
  81.7 8.9 %collective-permute-done.22.refs_7_ = bf16[64,1792]{1,0:T(8,128)(2,1)S(1)} collective-permute-done((bf16[64,1792]{1,0:T(8,128)(2,1)S(1)}, bf16[64,1792]{1,0:T(8,128)(2,1)S(1)}, u32[]{:S(2)}, u32[]{:S(2)}) %collective-permute-start.22) | collective-permute-done | bytes 229408 | tf_op jit(solution)/shard_map/ppermute | solution.py:429
  90.6 0.5 collective-permute-start.27
  91.1 1.0 %collective-permute-done.26.refs_11_ = bf16[64,1792]{1,0:T(8,128)(2,1)S(1)} collective-permute-done((bf16[64,1792]{1,0:T(8,128)(2,1)S(1)}, bf16[64,1792]{1,0:T(8,128)(2,1)S(1)}, u32[]{:S(2)}, u32[]{:S(2)}) %collective-permute-start.26) | collective-permute-done | bytes 229408 | tf_op jit(solution)/shard_map/ppermute | solution.py:695
  92.1 0.3 collective-permute-done.27.refs_12_
  92.4 1.9 %place.1 = bf16[128,4,1792]{2,1,0:T(4,128)(2,1)} custom-call(bf16[64,1792]{1,0:T(8,128)(2,1)S(1)} %get-tuple-element.74.refs_0_, bf16[64,1792]{1,0:T(8,128)(2,1)S(1)} %collective-permute-done.15.refs_1_, bf16[64,1792]{1,0:T(8,128)(2,1)S(1)} %collective-permute-done.17.refs_2_, bf16[64,1792]{1,0:T(8,128)(2,1)S(1)} %collective-permute-done.19.refs_3_, ...), custom_call_target="tpu_custom_call" | custom-call | flops 1 | bytes 1 | tf_op jit(solution)/shard_map/place/pallas_call | solution.py:698
  (53 shorter events, 0.2 us)
Async XLA Ops:
  0.0 9.9 %copy-start.9 = (s32[64,1]{0,1:T(1,128)S(1)}, s32[64,1]{0,1:T(1,128)}, u32[]{:S(2)}) copy-start(s32[64,1]{0,1:T(1,128)} %param.17) | copy-start | bytes 772
  0.0 9.9 %copy-start.10 = (s32[32]{0:T(128)S(1)}, s32[32]{0:T(128)}, u32[]{:S(2)}) copy-start(s32[32]{0:T(128)} %param.18) | copy-start | bytes 388
  0.0 9.9 %copy-start.11 = (s32[64,1]{0,1:T(1,128)S(1)}, s32[64,1]{0,1:T(1,128)}, u32[]{:S(2)}) copy-start(s32[64,1]{0,1:T(1,128)} %param.25) | copy-start | bytes 772
  0.0 9.9 %copy-start.7 = (f32[3584]{0:T(1024)S(1)}, f32[3584]{0:T(1024)}, u32[]{:S(2)}) copy-start(f32[3584]{0:T(1024)} %param.14) | copy-start | bytes 43012
  0.0 9.9 %copy-start.6 = (f32[2304]{0:T(1024)S(1)}, f32[2304]{0:T(1024)}, u32[]{:S(2)}) copy-start(f32[2304]{0:T(1024)} %param.16) | copy-start | bytes 27652
  0.0 9.9 %collective-permute-start = (bf16[4,1792,128]{2,1,0:T(8,128)(2,1)}, bf16[4,1792,128]{2,1,0:T(8,128)(2,1)S(1)}, u32[]{:S(2)}, u32[]{:S(2)}) collective-permute-start(bf16[4,1792,128]{2,1,0:T(8,128)(2,1)} %refs_4_.5), channel_id=1, source_target_pairs={{0,1},{1,0},{2,3},{3,2},{4,5},{5,4},{6,7},{7,6},{8,9},{9,8},{10,11... | collective-permute-start | bytes 5505032 | tf_op jit(solution)/shard_map/ppermute | solution.py:438
  0.5 9.4 %collective-permute-start.1 = (bf16[256,1792]{1,0:T(8,128)(2,1)}, bf16[256,1792]{1,0:T(8,128)(2,1)S(1)}, u32[]{:S(2)}, u32[]{:S(2)}) collective-permute-start(bf16[256,1792]{1,0:T(8,128)(2,1)} %bitcast.10), channel_id=1, source_target_pairs={{0,1},{1,0},{2,3},{3,2},{4,5},{5,4},{6,7},{7,6},{8,9},{9,8},{10,11... | collective-permute-start | bytes 2752520 | tf_op jit(solution)/shard_map/ppermute | solution.py:438
  0.6 8.6 %collective-permute-start.2 = (bf16[256,256]{1,0:T(8,128)(2,1)}, bf16[256,256]{1,0:T(8,128)(2,1)S(1)}, u32[]{:S(2)}, u32[]{:S(2)}) collective-permute-start(bf16[256,256]{1,0:T(8,128)(2,1)} %bitcast.13), channel_id=1, source_target_pairs={{0,1},{1,0},{2,3},{3,2},{4,5},{5,4},{6,7},{7,6},{8,9},{9,8},{10,11... | collective-permute-start | bytes 393224 | tf_op jit(solution)/shard_map/ppermute | solution.py:438
  4.5 18.0 %collective-permute-start.6 = (bf16[32,1792]{1,0:T(8,128)(2,1)}, bf16[32,1792]{1,0:T(8,128)(2,1)S(1)}, u32[]{:S(2)}, u32[]{:S(2)}) collective-permute-start(bf16[32,1792]{1,0:T(8,128)(2,1)} %get-tuple-element.50), channel_id=1, source_target_pairs={{0,12},{4,8},{8,4},{12,0},{1,13},{5,9},{9,5},{13,1},{2,14},{6,10},... | collective-permute-start | bytes 344072 | tf_op jit(solution)/shard_map/ppermute | solution.py:429
  9.3 13.9 %collective-permute-start.7 = (bf16[32,1792]{1,0:T(8,128)(2,1)}, bf16[32,1792]{1,0:T(8,128)(2,1)S(1)}, u32[]{:S(2)}, u32[]{:S(2)}) collective-permute-start(bf16[32,1792]{1,0:T(8,128)(2,1)} %get-tuple-element.49), channel_id=1, source_target_pairs={{0,8},{4,12},{8,0},{12,4},{1,9},{5,13},{9,1},{13,5},{2,10},{6,14},... | collective-permute-start | bytes 344072 | tf_op jit(solution)/shard_map/ppermute | solution.py:429
  9.3 13.9 %collective-permute-start.8 = (bf16[32,1792]{1,0:T(8,128)(2,1)}, bf16[32,1792]{1,0:T(8,128)(2,1)S(1)}, u32[]{:S(2)}, u32[]{:S(2)}) collective-permute-start(bf16[32,1792]{1,0:T(8,128)(2,1)} %get-tuple-element.48), channel_id=1, source_target_pairs={{0,4},{4,0},{8,12},{12,8},{1,5},{5,1},{9,13},{13,9},{2,6},{6,2},{1... | collective-permute-start | bytes 344072 | tf_op jit(solution)/shard_map/ppermute | solution.py:429
  10.0 12.6 %copy-start.8 = (s32[64]{0:T(128)S(1)}, s32[64]{0:T(128)}, u32[]{:S(2)}) copy-start(s32[64]{0:T(128)} %param.19) | copy-start | bytes 772
  10.0 13.2 %copy-start = (bf16[4,1792,128]{2,1,0:T(8,128)(2,1)S(1)}, bf16[4,1792,128]{2,1,0:T(8,128)(2,1)}, u32[]{:S(2)}) copy-start(bf16[4,1792,128]{2,1,0:T(8,128)(2,1)} %refs_4_.5) | copy-start | bytes 5505028
  10.0 13.2 %copy-start.5 = (bf16[32,1792]{1,0:T(8,128)(2,1)S(1)}, bf16[32,1792]{1,0:T(8,128)(2,1)}, u32[]{:S(2)}) copy-start(bf16[32,1792]{1,0:T(8,128)(2,1)} %get-tuple-element.58.refs_3_) | copy-start | bytes 344068
  18.7 15.3 %collective-permute-start.3 = (bf16[32,1792]{1,0:T(8,128)(2,1)S(1)}, bf16[32,1792]{1,0:T(8,128)(2,1)S(1)}, u32[]{:S(2)}, u32[]{:S(2)}) collective-permute-start(bf16[32,1792]{1,0:T(8,128)(2,1)S(1)} %get-tuple-element.53), channel_id=1, source_target_pairs={{0,12},{4,8},{8,4},{12,0},{1,13},{5,9},{9,5},{13,1},{2,14},{6,10},... | collective-permute-start | bytes 344072 | tf_op jit(solution)/shard_map/ppermute | solution.py:429
  22.5 12.4 %collective-permute-start.4 = (bf16[32,1792]{1,0:T(8,128)(2,1)S(1)}, bf16[32,1792]{1,0:T(8,128)(2,1)S(1)}, u32[]{:S(2)}, u32[]{:S(2)}) collective-permute-start(bf16[32,1792]{1,0:T(8,128)(2,1)S(1)} %get-tuple-element.54), channel_id=1, source_target_pairs={{0,8},{4,12},{8,0},{12,4},{1,9},{5,13},{9,1},{13,5},{2,10},{6,14},... | collective-permute-start | bytes 344072 | tf_op jit(solution)/shard_map/ppermute | solution.py:429
  22.5 12.4 %collective-permute-start.5 = (bf16[32,1792]{1,0:T(8,128)(2,1)S(1)}, bf16[32,1792]{1,0:T(8,128)(2,1)S(1)}, u32[]{:S(2)}, u32[]{:S(2)}) collective-permute-start(bf16[32,1792]{1,0:T(8,128)(2,1)S(1)} %get-tuple-element.55), channel_id=1, source_target_pairs={{0,4},{4,0},{8,12},{12,8},{1,5},{5,1},{9,13},{13,9},{2,6},{6,2},{1... | collective-permute-start | bytes 344072 | tf_op jit(solution)/shard_map/ppermute | solution.py:429
  24.3 5.5 %collective-permute-start.9 = (f32[128,128]{1,0:T(8,128)S(1)}, f32[128,128]{1,0:T(8,128)S(1)}, u32[]{:S(2)}, u32[]{:S(2)}) collective-permute-start(f32[128,128]{1,0:T(8,128)S(1)} %down.2.refs_0_), channel_id=1, source_target_pairs={{0,2},{2,0},{1,3},{3,1},{4,6},{6,4},{5,7},{7,5},{8,10},{10,8},{9,1... | collective-permute-start | bytes 196616 | tf_op jit(solution)/shard_map/ppermute | solution.py:438
  26.0 3.8 %copy-start.3 = (bf16[4,64,1792]{2,1,0:T(8,128)(2,1)S(1)}, bf16[4,64,1792]{2,1,0:T(8,128)(2,1)}, u32[]{:S(2)}) copy-start(bf16[4,64,1792]{2,1,0:T(8,128)(2,1)} %param.23) | copy-start | bytes 2752516
  26.0 3.8 %copy-start.4 = (bf16[4,64,256]{2,1,0:T(8,128)(2,1)S(1)}, bf16[4,64,256]{2,1,0:T(8,128)(2,1)}, u32[]{:S(2)}) copy-start(bf16[4,64,256]{2,1,0:T(8,128)(2,1)} %param.24) | copy-start | bytes 393220
  30.4 11.2 %collective-permute-start.11 = (bf16[32,2048]{1,0:T(8,128)(2,1)S(1)}, bf16[32,2048]{1,0:T(8,128)(2,1)S(1)}, u32[]{:S(2)}, u32[]{:S(2)}) collective-permute-start(bf16[32,2048]{1,0:T(8,128)(2,1)S(1)} %get-tuple-element.65), channel_id=1, source_target_pairs={{0,12},{4,8},{8,4},{12,0},{1,13},{5,9},{9,5},{13,1},{2,14},{6,10},... | collective-permute-start | bytes 393224 | tf_op jit(solution)/shard_map/ppermute | solution.py:429
  34.0 14.8 %collective-permute-start.12 = (bf16[32,2048]{1,0:T(8,128)(2,1)S(1)}, bf16[32,2048]{1,0:T(8,128)(2,1)S(1)}, u32[]{:S(2)}, u32[]{:S(2)}) collective-permute-start(bf16[32,2048]{1,0:T(8,128)(2,1)S(1)} %get-tuple-element.64), channel_id=1, source_target_pairs={{0,8},{4,12},{8,0},{12,4},{1,9},{5,13},{9,1},{13,5},{2,10},{6,14},... | collective-permute-start | bytes 393224 | tf_op jit(solution)/shard_map/ppermute | solution.py:429
  34.0 14.8 %collective-permute-start.13 = (bf16[32,2048]{1,0:T(8,128)(2,1)S(1)}, bf16[32,2048]{1,0:T(8,128)(2,1)S(1)}, u32[]{:S(2)}, u32[]{:S(2)}) collective-permute-start(bf16[32,2048]{1,0:T(8,128)(2,1)S(1)} %get-tuple-element.63), channel_id=1, source_target_pairs={{0,4},{4,0},{8,12},{12,8},{1,5},{5,1},{9,13},{13,9},{2,6},{6,2},{1... | collective-permute-start | bytes 393224 | tf_op jit(solution)/shard_map/ppermute | solution.py:429
  36.1 4.9 %collective-permute-start.10 = (f32[128,128]{1,0:T(8,128)S(1)}, f32[128,128]{1,0:T(8,128)S(1)}, u32[]{:S(2)}, u32[]{:S(2)}) collective-permute-start(f32[128,128]{1,0:T(8,128)S(1)} %down.3.refs_0_), channel_id=1, source_target_pairs={{0,2},{2,0},{1,3},{3,1},{4,6},{6,4},{5,7},{7,5},{8,10},{10,8},{9,1... | collective-permute-start | bytes 196616 | tf_op jit(solution)/shard_map/ppermute | solution.py:438
  41.0 8.4 %copy-start.1 = (bf16[64,32,256]{2,1,0:T(8,128)(2,1)S(1)}, bf16[64,32,256]{2,1,0:T(8,128)(2,1)}, u32[]{:S(2)}) copy-start(bf16[64,32,256]{2,1,0:T(8,128)(2,1)} %refs_4_.7) | copy-start | bytes 3145732
  41.0 8.4 %copy-start.2 = (bf16[64,32,256]{2,1,0:T(8,128)(2,1)S(1)}, bf16[64,32,256]{2,1,0:T(8,128)(2,1)}, u32[]{:S(2)}) copy-start(bf16[64,32,256]{2,1,0:T(8,128)(2,1)} %refs_5_.3) | copy-start | bytes 3145732
  41.5 11.8 %collective-permute-start.14 = (bf16[32,2048]{1,0:T(8,128)(2,1)S(1)}, bf16[32,2048]{1,0:T(8,128)(2,1)S(1)}, u32[]{:S(2)}, u32[]{:S(2)}) collective-permute-start(bf16[32,2048]{1,0:T(8,128)(2,1)S(1)} %get-tuple-element.76), channel_id=1, source_target_pairs={{0,12},{4,8},{8,4},{12,0},{1,13},{5,9},{9,5},{13,1},{2,14},{6,10},... | collective-permute-start | bytes 393224 | tf_op jit(solution)/shard_map/ppermute | solution.py:429
  48.8 12.2 %collective-permute-start.16 = (bf16[32,2048]{1,0:T(8,128)(2,1)S(1)}, bf16[32,2048]{1,0:T(8,128)(2,1)S(1)}, u32[]{:S(2)}, u32[]{:S(2)}) collective-permute-start(bf16[32,2048]{1,0:T(8,128)(2,1)S(1)} %get-tuple-element.79), channel_id=1, source_target_pairs={{0,8},{4,12},{8,0},{12,4},{1,9},{5,13},{9,1},{13,5},{2,10},{6,14},... | collective-permute-start | bytes 393224 | tf_op jit(solution)/shard_map/ppermute | solution.py:429
  48.8 9.1 %collective-permute-start.18 = (bf16[32,2048]{1,0:T(8,128)(2,1)S(1)}, bf16[32,2048]{1,0:T(8,128)(2,1)S(1)}, u32[]{:S(2)}, u32[]{:S(2)}) collective-permute-start(bf16[32,2048]{1,0:T(8,128)(2,1)S(1)} %get-tuple-element.82), channel_id=1, source_target_pairs={{0,4},{4,0},{8,12},{12,8},{1,5},{5,1},{9,13},{13,9},{2,6},{6,2},{1... | collective-permute-start | bytes 393224 | tf_op jit(solution)/shard_map/ppermute | solution.py:429
  57.9 11.9 %collective-permute-start.19 = (bf16[64,1792]{1,0:T(8,128)(2,1)S(1)}, bf16[64,1792]{1,0:T(8,128)(2,1)S(1)}, u32[]{:S(2)}, u32[]{:S(2)}) collective-permute-start(bf16[64,1792]{1,0:T(8,128)(2,1)S(1)} %get-tuple-element.83), channel_id=1, source_target_pairs={{0,12},{4,8},{8,4},{12,0},{1,13},{5,9},{9,5},{13,1},{2,14},{6,10},... | collective-permute-start | bytes 688136 | tf_op jit(solution)/shard_map/ppermute | solution.py:429
  61.1 19.8 %collective-permute-start.17 = (bf16[64,1792]{1,0:T(8,128)(2,1)S(1)}, bf16[64,1792]{1,0:T(8,128)(2,1)S(1)}, u32[]{:S(2)}, u32[]{:S(2)}) collective-permute-start(bf16[64,1792]{1,0:T(8,128)(2,1)S(1)} %get-tuple-element.80), channel_id=1, source_target_pairs={{0,8},{4,12},{8,0},{12,4},{1,9},{5,13},{9,1},{13,5},{2,10},{6,14},... | collective-permute-start | bytes 688136 | tf_op jit(solution)/shard_map/ppermute | solution.py:429
  61.1 19.8 %collective-permute-start.15 = (bf16[64,1792]{1,0:T(8,128)(2,1)S(1)}, bf16[64,1792]{1,0:T(8,128)(2,1)S(1)}, u32[]{:S(2)}, u32[]{:S(2)}) collective-permute-start(bf16[64,1792]{1,0:T(8,128)(2,1)S(1)} %get-tuple-element.77), channel_id=1, source_target_pairs={{0,4},{4,0},{8,12},{12,8},{1,5},{5,1},{9,13},{13,9},{2,6},{6,2},{1... | collective-permute-start | bytes 688136 | tf_op jit(solution)/shard_map/ppermute | solution.py:429
  66.1 15.7 %collective-permute-start.21 = (bf16[64,1792]{1,0:T(8,128)(2,1)S(1)}, bf16[64,1792]{1,0:T(8,128)(2,1)S(1)}, u32[]{:S(2)}, u32[]{:S(2)}) collective-permute-start(bf16[64,1792]{1,0:T(8,128)(2,1)S(1)} %get-tuple-element.86), channel_id=1, source_target_pairs={{0,4},{4,0},{8,12},{12,8},{1,5},{5,1},{9,13},{13,9},{2,6},{6,2},{1... | collective-permute-start | bytes 688136 | tf_op jit(solution)/shard_map/ppermute | solution.py:429
  66.9 23.7 %collective-permute-start.22 = (bf16[64,1792]{1,0:T(8,128)(2,1)S(1)}, bf16[64,1792]{1,0:T(8,128)(2,1)S(1)}, u32[]{:S(2)}, u32[]{:S(2)}) collective-permute-start(bf16[64,1792]{1,0:T(8,128)(2,1)S(1)} %get-tuple-element.87), channel_id=1, source_target_pairs={{0,8},{4,12},{8,0},{12,4},{1,9},{5,13},{9,1},{13,5},{2,10},{6,14},... | collective-permute-start | bytes 688136 | tf_op jit(solution)/shard_map/ppermute | solution.py:429
  69.8 20.8 %collective-permute-start.23 = (bf16[64,1792]{1,0:T(8,128)(2,1)S(1)}, bf16[64,1792]{1,0:T(8,128)(2,1)S(1)}, u32[]{:S(2)}, u32[]{:S(2)}) collective-permute-start(bf16[64,1792]{1,0:T(8,128)(2,1)S(1)} %get-tuple-element.88), channel_id=1, source_target_pairs={{0,12},{4,8},{8,4},{12,0},{1,13},{5,9},{9,5},{13,1},{2,14},{6,10},... | collective-permute-start | bytes 688136 | tf_op jit(solution)/shard_map/ppermute | solution.py:429
  80.9 11.5 %collective-permute-start.20 = (bf16[128,1792]{1,0:T(8,128)(2,1)S(1)}, bf16[128,1792]{1,0:T(8,128)(2,1)S(1)}, u32[]{:S(2)}, u32[]{:S(2)}) collective-permute-start(bf16[128,1792]{1,0:T(8,128)(2,1)S(1)} %pad_maximum_fusion), channel_id=1, source_target_pairs={{0,1},{1,0},{2,3},{3,2},{4,5},{5,4},{6,7},{7,6},{8,9},{9,8},{10,11... | collective-permute-start | bytes 1376264 | tf_op jit(solution)/shard_map/ppermute | solution.py:691
  81.0 10.1 %collective-permute-start.24 = (bf16[64,1792]{1,0:T(8,128)(2,1)S(1)}, bf16[64,1792]{1,0:T(8,128)(2,1)S(1)}, u32[]{:S(2)}, u32[]{:S(2)}) collective-permute-start(bf16[64,1792]{1,0:T(8,128)(2,1)S(1)} %get-tuple-element.85.refs_5_), channel_id=1, source_target_pairs={{0,1},{1,0},{2,3},{3,2},{4,5},{5,4},{6,7},{7,6},{8,9},{9,8},{10,11... | collective-permute-start | bytes 688136 | tf_op jit(solution)/shard_map/ppermute | solution.py:695
  81.7 9.4 %collective-permute-start.25 = (bf16[64,1792]{1,0:T(8,128)(2,1)S(1)}, bf16[64,1792]{1,0:T(8,128)(2,1)S(1)}, u32[]{:S(2)}, u32[]{:S(2)}) collective-permute-start(bf16[64,1792]{1,0:T(8,128)(2,1)S(1)} %collective-permute-done.21.refs_6_), channel_id=1, source_target_pairs={{0,1},{1,0},{2,3},{3,2},{4,5},{5,4},{6,7},{7,6},{8,9},{9,8},{10,11... | collective-permute-start | bytes 688136 | tf_op jit(solution)/shard_map/ppermute | solution.py:695
  90.6 1.5 %collective-permute-start.26 = (bf16[64,1792]{1,0:T(8,128)(2,1)S(1)}, bf16[64,1792]{1,0:T(8,128)(2,1)S(1)}, u32[]{:S(2)}, u32[]{:S(2)}) collective-permute-start(bf16[64,1792]{1,0:T(8,128)(2,1)S(1)} %collective-permute-done.22.refs_7_), channel_id=1, source_target_pairs={{0,1},{1,0},{2,3},{3,2},{4,5},{5,4},{6,7},{7,6},{8,9},{9,8},{10,11... | collective-permute-start | bytes 688136 | tf_op jit(solution)/shard_map/ppermute | solution.py:695
  90.6 1.8 %collective-permute-start.27 = (bf16[64,1792]{1,0:T(8,128)(2,1)S(1)}, bf16[64,1792]{1,0:T(8,128)(2,1)S(1)}, u32[]{:S(2)}, u32[]{:S(2)}) collective-permute-start(bf16[64,1792]{1,0:T(8,128)(2,1)S(1)} %collective-permute-done.23.refs_8_), channel_id=1, source_target_pairs={{0,1},{1,0},{2,3},{3,2},{4,5},{5,4},{6,7},{7,6},{8,9},{9,8},{10,11... | collective-permute-start | bytes 688136 | tf_op jit(solution)/shard_map/ppermute | solution.py:695

commit v17 on v16

--- a/solution.py
+++ b/solution.py
@@ -616,7 +616,7 @@
         messages = list(after)
         if chunk:
             for lane in range(1, lanes):
-                messages[lane] = held(messages[lane], returned[-1][lane])
+                messages[lane] = held(messages[lane], returned[-1][min(lane + 1, lanes - 1)])
         returned.append(traded(messages, "streams"))
 
     length_row = cache_fill_length.reshape(1, rows)

time: 95.8 us -> 95.7 us (level); the launches traced: 94.3 us -> 95.5 us
  starting transfers between devices: 28.6 us -> 29.7 us
where the time goes in v17:
time: 95.7 us; the launch traced here: 95.5 us
  Pallas kernels  33.1 us (35%)
  waiting for transfers between devices  31.5 us (33%)
  starting transfers between devices  29.7 us (31%)
    ppermute x18, waiting for transfers between devices, traded(): landed[shift] = lax.ppermute(blocks[shift], axes, pairs)  30.2 us
    ppermute x18, starting transfers between devices, traded(): landed[shift] = lax.ppermute(blocks[shift], axes, pairs)  25.2 us
    pallas_call x1, Pallas kernels, on_device(): pl.pallas_call(functools.partial(norm_pack_project_kernel, chunk_steps, r...  8.69 us
    pallas_call x2, Pallas kernels, project(): pl.pallas_call(functools.partial(project_kernel, begin), in_specs=[VMEM,...  8.15 us
    pallas_call x2, Pallas kernels, on_device(): pl.pallas_call(functools.partial(attend_kernel, chunk * chunk_steps, chun...  7.58 us
    pallas_call x1, Pallas kernels, on_device(): pl.pallas_call(functools.partial(norm_pack_kernel, chunk_steps, rows, flo...  3.45 us
    ppermute x5, starting transfers between devices, from_others(): landed.append(lax.ppermute(block, axis, pairs))  3.35 us
    pallas_call x2, Pallas kernels, down(): pl.pallas_call(functools.partial(down_kernel, lanes, spots), in_specs=[VM...  2.3 us
  transfers between devices with their start and end apart: 28, of which 8 were waited for; matrix products, arithmetic and copies ran while one was open for 1% of the time, Pallas kernels for 33%

profile of v17, /device:TPU:0, one launch (start us, length us, event | category | flops | bytes accessed | tf_op | source)
XLA Modules:
  0.0 95.5 jit_solution(15266895280339511226)
XLA Ops:
  0.0 0.5 collective-permute-start
  0.6 0.1 collective-permute-start.1
  0.6 0.4 collective-permute-start.2
  1.1 3.5 %norm_and_pack.1 = (bf16[32,1792]{1,0:T(8,128)(2,1)}, bf16[32,1792]{1,0:T(8,128)(2,1)}, bf16[32,1792]{1,0:T(8,128)(2,1)}, bf16[32,1792]{1,0:T(8,128)(2,1)}) custom-call(s32[1,64]{1,0:T(1,128)} %bitcast.23, s32[1,32]{1,0:T(1,128)} %bitcast.25, s32[1,64]{1,0:T(1,128)} %bitcast.27, f32[28,128]{1,0:T(8,128)} %bitcast.19, bf16[256,3584]{1,0:T(8,128)(2,1)} %bitcast.29), custom_call_target="tpu_custom_call" | custom-call | flops 1 | bytes 1 | tf_op jit(solution)/shard_map/norm_and_pack/pallas_call | solution.py:514
  4.5 4.7 %collective-permute-start.6 = (bf16[32,1792]{1,0:T(8,128)(2,1)}, bf16[32,1792]{1,0:T(8,128)(2,1)S(1)}, u32[]{:S(2)}, u32[]{:S(2)}) collective-permute-start(bf16[32,1792]{1,0:T(8,128)(2,1)} %get-tuple-element.50), channel_id=1, source_target_pairs={{0,12},{4,8},{8,4},{12,0},{1,13},{5,9},{9,5},{13,1},{2,14},{6,10},... | collective-permute-start | bytes 344072 | tf_op jit(solution)/shard_map/ppermute | solution.py:429
  9.3 0.6 collective-permute-start.8
  10.0 0.0 copy-start
  10.0 0.0 copy-start.5
  10.0 8.7 %norm_pack_project.1 = (bf16[256,3584]{1,0:T(8,128)(2,1)S(1)}, f32[256,1024]{1,0:T(8,128)S(1)}, s32[8,64]{1,0:T(8,128)S(1)}, bf16[32,1792]{1,0:T(8,128)(2,1)S(1)...) custom-call(s32[1,64]{1,0:T(1,128)S(1)} %bitcast.24, ...), custom_call_target="tpu_custom_call" | custom-call | flops 1 | bytes 1 | tf_op jit(solution)/shard_map/norm_pack_project/pallas_call | solution.py:544
  18.7 3.8 %collective-permute-start.3 = (bf16[32,1792]{1,0:T(8,128)(2,1)S(1)}, bf16[32,1792]{1,0:T(8,128)(2,1)S(1)}, u32[]{:S(2)}, u32[]{:S(2)}) collective-permute-start(bf16[32,1792]{1,0:T(8,128)(2,1)S(1)} %get-tuple-element.53), channel_id=1, source_target_pairs={{0,12},{4,8},{8,4},{12,0},{1,13},{5,9},{9,5},{13,1},{2,14},{6,10},... | collective-permute-start | bytes 344072 | tf_op jit(solution)/shard_map/ppermute | solution.py:429
  22.5 0.6 collective-permute-start.5
  23.2 1.1 %down.2.refs_0_ = f32[128,128]{1,0:T(8,128)S(1)} custom-call(bf16[32,1792]{1,0:T(8,128)(2,1)S(1)} %collective-permute-done.6.refs_0_, bf16[32,1792]{1,0:T(8,128)(2,1)S(1)} %collective-permute-done.7.refs_1_, bf16[32,1792]{1,0:T(8,128)(2,1)S(1)} %collective-permute-done.8.refs_2_, bf16[32,1792]{1,0:T(8,128)(2,1)S(1)} %copy-done.5, ...), custom_call_target="tpu_custom_call" | custom-call | flops 1 | bytes 1 | tf_op jit(solution)/shard_map/down/pallas_call | solution.py:577
  24.3 1.7 %collective-permute-start.9 = (f32[128,128]{1,0:T(8,128)S(1)}, f32[128,128]{1,0:T(8,128)S(1)}, u32[]{:S(2)}, u32[]{:S(2)}) collective-permute-start(f32[128,128]{1,0:T(8,128)S(1)} %down.2.refs_0_), channel_id=1, source_target_pairs={{0,2},{2,0},{1,3},{3,1},{4,6},{6,4},{5,7},{7,5},{8,10},{10,8},{9,1... | collective-permute-start | bytes 196616 | tf_op jit(solution)/shard_map/ppermute | solution.py:438
  26.0 0.0 copy-start.4
  26.1 3.8 %project.2.refs_7_ = f32[256,512]{1,0:T(8,128)S(1)} custom-call(bf16[256,3584]{1,0:T(8,128)(2,1)S(1)} %get-tuple-element.59.rows_ref, f32[18,128]{1,0:T(8,128)S(1)} %bitcast.17, bf16[3584,2304]{1,0:T(8,128)(2,1)} %weight_hbm.3), custom_call_target="tpu_custom_call" | custom-call | flops 1 | bytes 1 | tf_op jit(solution)/shard_map/project/pallas_call | solution.py:565
  29.9 0.5 up.2
  30.4 3.7 %collective-permute-start.11 = (bf16[32,2048]{1,0:T(8,128)(2,1)S(1)}, bf16[32,2048]{1,0:T(8,128)(2,1)S(1)}, u32[]{:S(2)}, u32[]{:S(2)}) collective-permute-start(bf16[32,2048]{1,0:T(8,128)(2,1)S(1)} %get-tuple-element.65), channel_id=1, source_target_pairs={{0,12},{4,8},{8,4},{12,0},{1,13},{5,9},{9,5},{13,1},{2,14},{6,10},... | collective-permute-start | bytes 393224 | tf_op jit(solution)/shard_map/ppermute | solution.py:429
  34.1 0.1 compare_select_fusion
  34.1 1.2 %down.3.refs_0_ = f32[128,128]{1,0:T(8,128)S(1)} custom-call(bf16[32,1792]{1,0:T(8,128)(2,1)S(1)} %collective-permute-done.3.refs_0_, bf16[32,1792]{1,0:T(8,128)(2,1)S(1)} %collective-permute-done.4.refs_1_, bf16[32,1792]{1,0:T(8,128)(2,1)S(1)} %collective-permute-done.5.refs_2_, bf16[32,1792]{1,0:T(8,128)(2,1)S(1)} %get-tuple-element.66.refs_3_, ...), custom_call_target="tpu_custom_call" | custom-call | flops 1 | bytes 1 | tf_op jit(solution)/shard_map/down/pallas_call | solution.py:577
  35.3 0.6 collective-permute-start.10
  35.9 0.1 add_convert_fusion
  36.0 0.7 collective-permute-start.13
  36.7 4.4 %project.3.refs_8_ = f32[256,768]{1,0:T(8,128)S(1)} custom-call(bf16[256,3584]{1,0:T(8,128)(2,1)S(1)} %get-tuple-element.59.rows_ref, f32[18,128]{1,0:T(8,128)S(1)} %bitcast.18, bf16[3584,2304]{1,0:T(8,128)(2,1)} %weight_hbm.3), custom_call_target="tpu_custom_call" | custom-call | flops 1 | bytes 1 | tf_op jit(solution)/shard_map/project/pallas_call | solution.py:565
  41.0 0.0 copy-start.1
  41.0 0.0 copy-start.2
  41.1 0.5 up.3
  41.6 3.8 %collective-permute-start.14 = (bf16[32,2048]{1,0:T(8,128)(2,1)S(1)}, bf16[32,2048]{1,0:T(8,128)(2,1)S(1)}, u32[]{:S(2)}, u32[]{:S(2)}) collective-permute-start(bf16[32,2048]{1,0:T(8,128)(2,1)S(1)} %get-tuple-element.76), channel_id=1, source_target_pairs={{0,12},{4,8},{8,4},{12,0},{1,13},{5,9},{9,5},{13,1},{2,14},{6,10},... | collective-permute-start | bytes 393224 | tf_op jit(solution)/shard_map/ppermute | solution.py:429
  45.4 2.8 %collective-permute-done.12.refs_10_ = bf16[32,2048]{1,0:T(8,128)(2,1)S(1)} collective-permute-done((bf16[32,2048]{1,0:T(8,128)(2,1)S(1)}, bf16[32,2048]{1,0:T(8,128)(2,1)S(1)}, u32[]{:S(2)}, u32[]{:S(2)}) %collective-permute-start.12) | collective-permute-done | bytes 131104 | tf_op jit(solution)/shard_map/ppermute | solution.py:429
  48.2 0.5 fusion
  48.8 3.9 %attend.2 = (f32[128,512]{1,0:T(8,128)S(1)}, bf16[64,1792]{1,0:T(8,128)(2,1)S(1)}, bf16[64,1792]{1,0:T(8,128)(2,1)S(1)}, bf16[64,1792]{1,0:T(8,128)(2,1)S(1)}, bf16[64,1792]{1,0:T(8,128)(2,1)S(1)}) custom-call(s32[8,64]{1,0:T(8,128)S(1)} %get-tuple-element.73.refs_0_, s32[1,64]{1,0:T(1,128)S(1)} %bitcast.21, f32[256,128]{1,0:T(8,128)S(1)} %get-tuple-element.90.refs_2_, ...), custom_call_target="tpu_custom_call" | custom-call | flops 1 | bytes 1 | tf_op jit(solution)/shard_map/attend/pallas_call | solution.py:630
  52.7 5.2 %collective-permute-done.18.refs_11_ = bf16[32,2048]{1,0:T(8,128)(2,1)S(1)} collective-permute-done((bf16[32,2048]{1,0:T(8,128)(2,1)S(1)}, bf16[32,2048]{1,0:T(8,128)(2,1)S(1)}, u32[]{:S(2)}, u32[]{:S(2)}) %collective-permute-start.18) | collective-permute-done | bytes 131104 | tf_op jit(solution)/shard_map/ppermute | solution.py:429
  57.8 0.6 collective-permute-done.16.refs_10_
  58.4 0.3 collective-permute-start.17
  58.7 3.5 %collective-permute-start.15 = (bf16[64,1792]{1,0:T(8,128)(2,1)S(1)}, bf16[64,1792]{1,0:T(8,128)(2,1)S(1)}, u32[]{:S(2)}, u32[]{:S(2)}) collective-permute-start(bf16[64,1792]{1,0:T(8,128)(2,1)S(1)} %get-tuple-element.77), channel_id=1, source_target_pairs={{0,4},{4,0},{8,12},{12,8},{1,5},{5,1},{9,13},{13,9},{2,6},{6,2},{1... | collective-permute-start | bytes 688136 | tf_op jit(solution)/shard_map/ppermute | solution.py:429
  62.2 3.7 %attend.3 = (bf16[64,1792]{1,0:T(8,128)(2,1)S(1)}, bf16[64,1792]{1,0:T(8,128)(2,1)S(1)}, bf16[64,1792]{1,0:T(8,128)(2,1)S(1)}, bf16[64,1792]{1,0:T(8,128)(2,1)S(1)}) custom-call(s32[8,64]{1,0:T(8,128)S(1)} %get-tuple-element.73.refs_0_, s32[1,64]{1,0:T(1,128)S(1)} %bitcast.22, f32[256,128]{1,0:T(8,128)S(1)} %get-tuple-element.90.refs_2_, ...), custom_call_target="tpu_custom_call" | custom-call | flops 1 | bytes 1 | tf_op jit(solution)/shard_map/attend/pallas_call | solution.py:630
  65.9 0.1 collective-permute-start.21
  66.0 1.1 %collective-permute-start.22 = (bf16[64,1792]{1,0:T(8,128)(2,1)S(1)}, bf16[64,1792]{1,0:T(8,128)(2,1)S(1)}, u32[]{:S(2)}, u32[]{:S(2)}) collective-permute-start(bf16[64,1792]{1,0:T(8,128)(2,1)S(1)} %get-tuple-element.87), channel_id=1, source_target_pairs={{0,8},{4,12},{8,0},{12,4},{1,9},{5,13},{9,1},{13,5},{2,10},{6,14},... | collective-permute-start | bytes 688136 | tf_op jit(solution)/shard_map/ppermute | solution.py:429
  67.2 1.0 %collective-permute-done.19.refs_3_ = bf16[64,1792]{1,0:T(8,128)(2,1)S(1)} collective-permute-done((bf16[64,1792]{1,0:T(8,128)(2,1)S(1)}, bf16[64,1792]{1,0:T(8,128)(2,1)S(1)}, u32[]{:S(2)}, u32[]{:S(2)}) %collective-permute-start.19) | collective-permute-done | bytes 229408 | tf_op jit(solution)/shard_map/ppermute | solution.py:429
  68.2 2.2 %collective-permute-start.23 = (bf16[64,1792]{1,0:T(8,128)(2,1)S(1)}, bf16[64,1792]{1,0:T(8,128)(2,1)S(1)}, u32[]{:S(2)}, u32[]{:S(2)}) collective-permute-start(bf16[64,1792]{1,0:T(8,128)(2,1)S(1)} %get-tuple-element.88), channel_id=1, source_target_pairs={{0,12},{4,8},{8,4},{12,0},{1,13},{5,9},{9,5},{13,1},{2,14},{6,10},... | collective-permute-start | bytes 688136 | tf_op jit(solution)/shard_map/ppermute | solution.py:429
  70.4 16.4 %collective-permute-done.17.refs_2_ = bf16[64,1792]{1,0:T(8,128)(2,1)S(1)} collective-permute-done((bf16[64,1792]{1,0:T(8,128)(2,1)S(1)}, bf16[64,1792]{1,0:T(8,128)(2,1)S(1)}, u32[]{:S(2)}, u32[]{:S(2)}) %collective-permute-start.17) | collective-permute-done | bytes 229408 | tf_op jit(solution)/shard_map/ppermute | solution.py:429
  86.9 0.1 collective-permute-start.20
  87.0 0.5 collective-permute-start.24
  87.5 0.1 collective-permute-start.25
  87.6 4.2 %collective-permute-done.22.refs_7_ = bf16[64,1792]{1,0:T(8,128)(2,1)S(1)} collective-permute-done((bf16[64,1792]{1,0:T(8,128)(2,1)S(1)}, bf16[64,1792]{1,0:T(8,128)(2,1)S(1)}, u32[]{:S(2)}, u32[]{:S(2)}) %collective-permute-start.22) | collective-permute-done | bytes 229408 | tf_op jit(solution)/shard_map/ppermute | solution.py:429
  91.8 0.5 collective-permute-start.27
  92.3 1.0 %collective-permute-done.26.refs_11_ = bf16[64,1792]{1,0:T(8,128)(2,1)S(1)} collective-permute-done((bf16[64,1792]{1,0:T(8,128)(2,1)S(1)}, bf16[64,1792]{1,0:T(8,128)(2,1)S(1)}, u32[]{:S(2)}, u32[]{:S(2)}) %collective-permute-start.26) | collective-permute-done | bytes 229408 | tf_op jit(solution)/shard_map/ppermute | solution.py:695
  93.2 0.3 collective-permute-done.27.refs_12_
  93.6 1.9 %place.1 = bf16[128,4,1792]{2,1,0:T(4,128)(2,1)} custom-call(bf16[64,1792]{1,0:T(8,128)(2,1)S(1)} %get-tuple-element.74.refs_0_, bf16[64,1792]{1,0:T(8,128)(2,1)S(1)} %collective-permute-done.15.refs_1_, bf16[64,1792]{1,0:T(8,128)(2,1)S(1)} %collective-permute-done.17.refs_2_, bf16[64,1792]{1,0:T(8,128)(2,1)S(1)} %collective-permute-done.19.refs_3_, ...), custom_call_target="tpu_custom_call" | custom-call | flops 1 | bytes 1 | tf_op jit(solution)/shard_map/place/pallas_call | solution.py:698
  (53 shorter events, 0.2 us)
Async XLA Ops:
  0.0 9.9 %copy-start.9 = (s32[64,1]{0,1:T(1,128)S(1)}, s32[64,1]{0,1:T(1,128)}, u32[]{:S(2)}) copy-start(s32[64,1]{0,1:T(1,128)} %param.17) | copy-start | bytes 772
  0.0 9.9 %copy-start.10 = (s32[32]{0:T(128)S(1)}, s32[32]{0:T(128)}, u32[]{:S(2)}) copy-start(s32[32]{0:T(128)} %param.18) | copy-start | bytes 388
  0.0 10.0 %copy-start.11 = (s32[64,1]{0,1:T(1,128)S(1)}, s32[64,1]{0,1:T(1,128)}, u32[]{:S(2)}) copy-start(s32[64,1]{0,1:T(1,128)} %param.25) | copy-start | bytes 772
  0.0 10.0 %copy-start.7 = (f32[3584]{0:T(1024)S(1)}, f32[3584]{0:T(1024)}, u32[]{:S(2)}) copy-start(f32[3584]{0:T(1024)} %param.14) | copy-start | bytes 43012
  0.0 9.9 %copy-start.8 = (s32[64]{0:T(128)S(1)}, s32[64]{0:T(128)}, u32[]{:S(2)}) copy-start(s32[64]{0:T(128)} %param.19) | copy-start | bytes 772
  0.0 10.0 %copy-start.6 = (f32[2304]{0:T(1024)S(1)}, f32[2304]{0:T(1024)}, u32[]{:S(2)}) copy-start(f32[2304]{0:T(1024)} %param.16) | copy-start | bytes 27652
  0.0 9.9 %collective-permute-start = (bf16[4,1792,128]{2,1,0:T(8,128)(2,1)}, bf16[4,1792,128]{2,1,0:T(8,128)(2,1)S(1)}, u32[]{:S(2)}, u32[]{:S(2)}) collective-permute-start(bf16[4,1792,128]{2,1,0:T(8,128)(2,1)} %refs_4_.5), channel_id=1, source_target_pairs={{0,1},{1,0},{2,3},{3,2},{4,5},{5,4},{6,7},{7,6},{8,9},{9,8},{10,11... | collective-permute-start | bytes 5505032 | tf_op jit(solution)/shard_map/ppermute | solution.py:438
  0.6 9.4 %collective-permute-start.1 = (bf16[256,1792]{1,0:T(8,128)(2,1)}, bf16[256,1792]{1,0:T(8,128)(2,1)S(1)}, u32[]{:S(2)}, u32[]{:S(2)}) collective-permute-start(bf16[256,1792]{1,0:T(8,128)(2,1)} %bitcast.10), channel_id=1, source_target_pairs={{0,1},{1,0},{2,3},{3,2},{4,5},{5,4},{6,7},{7,6},{8,9},{9,8},{10,11... | collective-permute-start | bytes 2752520 | tf_op jit(solution)/shard_map/ppermute | solution.py:438
  0.6 8.6 %collective-permute-start.2 = (bf16[256,256]{1,0:T(8,128)(2,1)}, bf16[256,256]{1,0:T(8,128)(2,1)S(1)}, u32[]{:S(2)}, u32[]{:S(2)}) collective-permute-start(bf16[256,256]{1,0:T(8,128)(2,1)} %bitcast.13), channel_id=1, source_target_pairs={{0,1},{1,0},{2,3},{3,2},{4,5},{5,4},{6,7},{7,6},{8,9},{9,8},{10,11... | collective-permute-start | bytes 393224 | tf_op jit(solution)/shard_map/ppermute | solution.py:438
  4.5 18.0 %collective-permute-start.6 = (bf16[32,1792]{1,0:T(8,128)(2,1)}, bf16[32,1792]{1,0:T(8,128)(2,1)S(1)}, u32[]{:S(2)}, u32[]{:S(2)}) collective-permute-start(bf16[32,1792]{1,0:T(8,128)(2,1)} %get-tuple-element.50), channel_id=1, source_target_pairs={{0,12},{4,8},{8,4},{12,0},{1,13},{5,9},{9,5},{13,1},{2,14},{6,10},... | collective-permute-start | bytes 344072 | tf_op jit(solution)/shard_map/ppermute | solution.py:429
  9.3 13.9 %collective-permute-start.7 = (bf16[32,1792]{1,0:T(8,128)(2,1)}, bf16[32,1792]{1,0:T(8,128)(2,1)S(1)}, u32[]{:S(2)}, u32[]{:S(2)}) collective-permute-start(bf16[32,1792]{1,0:T(8,128)(2,1)} %get-tuple-element.49), channel_id=1, source_target_pairs={{0,8},{4,12},{8,0},{12,4},{1,9},{5,13},{9,1},{13,5},{2,10},{6,14},... | collective-permute-start | bytes 344072 | tf_op jit(solution)/shard_map/ppermute | solution.py:429
  9.3 13.9 %collective-permute-start.8 = (bf16[32,1792]{1,0:T(8,128)(2,1)}, bf16[32,1792]{1,0:T(8,128)(2,1)S(1)}, u32[]{:S(2)}, u32[]{:S(2)}) collective-permute-start(bf16[32,1792]{1,0:T(8,128)(2,1)} %get-tuple-element.48), channel_id=1, source_target_pairs={{0,4},{4,0},{8,12},{12,8},{1,5},{5,1},{9,13},{13,9},{2,6},{6,2},{1... | collective-permute-start | bytes 344072 | tf_op jit(solution)/shard_map/ppermute | solution.py:429
  10.0 13.2 %copy-start = (bf16[4,1792,128]{2,1,0:T(8,128)(2,1)S(1)}, bf16[4,1792,128]{2,1,0:T(8,128)(2,1)}, u32[]{:S(2)}) copy-start(bf16[4,1792,128]{2,1,0:T(8,128)(2,1)} %refs_4_.5) | copy-start | bytes 5505028
  10.0 13.2 %copy-start.5 = (bf16[32,1792]{1,0:T(8,128)(2,1)S(1)}, bf16[32,1792]{1,0:T(8,128)(2,1)}, u32[]{:S(2)}) copy-start(bf16[32,1792]{1,0:T(8,128)(2,1)} %get-tuple-element.58.refs_3_) | copy-start | bytes 344068
  18.7 15.4 %collective-permute-start.3 = (bf16[32,1792]{1,0:T(8,128)(2,1)S(1)}, bf16[32,1792]{1,0:T(8,128)(2,1)S(1)}, u32[]{:S(2)}, u32[]{:S(2)}) collective-permute-start(bf16[32,1792]{1,0:T(8,128)(2,1)S(1)} %get-tuple-element.53), channel_id=1, source_target_pairs={{0,12},{4,8},{8,4},{12,0},{1,13},{5,9},{9,5},{13,1},{2,14},{6,10},... | collective-permute-start | bytes 344072 | tf_op jit(solution)/shard_map/ppermute | solution.py:429
  22.5 11.6 %collective-permute-start.4 = (bf16[32,1792]{1,0:T(8,128)(2,1)S(1)}, bf16[32,1792]{1,0:T(8,128)(2,1)S(1)}, u32[]{:S(2)}, u32[]{:S(2)}) collective-permute-start(bf16[32,1792]{1,0:T(8,128)(2,1)S(1)} %get-tuple-element.54), channel_id=1, source_target_pairs={{0,8},{4,12},{8,0},{12,4},{1,9},{5,13},{9,1},{13,5},{2,10},{6,14},... | collective-permute-start | bytes 344072 | tf_op jit(solution)/shard_map/ppermute | solution.py:429
  22.5 11.6 %collective-permute-start.5 = (bf16[32,1792]{1,0:T(8,128)(2,1)S(1)}, bf16[32,1792]{1,0:T(8,128)(2,1)S(1)}, u32[]{:S(2)}, u32[]{:S(2)}) collective-permute-start(bf16[32,1792]{1,0:T(8,128)(2,1)S(1)} %get-tuple-element.55), channel_id=1, source_target_pairs={{0,4},{4,0},{8,12},{12,8},{1,5},{5,1},{9,13},{13,9},{2,6},{6,2},{1... | collective-permute-start | bytes 344072 | tf_op jit(solution)/shard_map/ppermute | solution.py:429
  24.3 5.5 %collective-permute-start.9 = (f32[128,128]{1,0:T(8,128)S(1)}, f32[128,128]{1,0:T(8,128)S(1)}, u32[]{:S(2)}, u32[]{:S(2)}) collective-permute-start(f32[128,128]{1,0:T(8,128)S(1)} %down.2.refs_0_), channel_id=1, source_target_pairs={{0,2},{2,0},{1,3},{3,1},{4,6},{6,4},{5,7},{7,5},{8,10},{10,8},{9,1... | collective-permute-start | bytes 196616 | tf_op jit(solution)/shard_map/ppermute | solution.py:438
  26.0 3.8 %copy-start.3 = (bf16[4,64,1792]{2,1,0:T(8,128)(2,1)S(1)}, bf16[4,64,1792]{2,1,0:T(8,128)(2,1)}, u32[]{:S(2)}) copy-start(bf16[4,64,1792]{2,1,0:T(8,128)(2,1)} %param.23) | copy-start | bytes 2752516
  26.0 3.8 %copy-start.4 = (bf16[4,64,256]{2,1,0:T(8,128)(2,1)S(1)}, bf16[4,64,256]{2,1,0:T(8,128)(2,1)}, u32[]{:S(2)}) copy-start(bf16[4,64,256]{2,1,0:T(8,128)(2,1)} %param.24) | copy-start | bytes 393220
  30.4 11.2 %collective-permute-start.11 = (bf16[32,2048]{1,0:T(8,128)(2,1)S(1)}, bf16[32,2048]{1,0:T(8,128)(2,1)S(1)}, u32[]{:S(2)}, u32[]{:S(2)}) collective-permute-start(bf16[32,2048]{1,0:T(8,128)(2,1)S(1)} %get-tuple-element.65), channel_id=1, source_target_pairs={{0,12},{4,8},{8,4},{12,0},{1,13},{5,9},{9,5},{13,1},{2,14},{6,10},... | collective-permute-start | bytes 393224 | tf_op jit(solution)/shard_map/ppermute | solution.py:429
  34.1 14.1 %collective-permute-start.12 = (bf16[32,2048]{1,0:T(8,128)(2,1)S(1)}, bf16[32,2048]{1,0:T(8,128)(2,1)S(1)}, u32[]{:S(2)}, u32[]{:S(2)}) collective-permute-start(bf16[32,2048]{1,0:T(8,128)(2,1)S(1)} %get-tuple-element.64), channel_id=1, source_target_pairs={{0,8},{4,12},{8,0},{12,4},{1,9},{5,13},{9,1},{13,5},{2,10},{6,14},... | collective-permute-start | bytes 393224 | tf_op jit(solution)/shard_map/ppermute | solution.py:429
  35.3 5.7 %collective-permute-start.10 = (f32[128,128]{1,0:T(8,128)S(1)}, f32[128,128]{1,0:T(8,128)S(1)}, u32[]{:S(2)}, u32[]{:S(2)}) collective-permute-start(f32[128,128]{1,0:T(8,128)S(1)} %down.3.refs_0_), channel_id=1, source_target_pairs={{0,2},{2,0},{1,3},{3,1},{4,6},{6,4},{5,7},{7,5},{8,10},{10,8},{9,1... | collective-permute-start | bytes 196616 | tf_op jit(solution)/shard_map/ppermute | solution.py:438
  36.0 12.7 %collective-permute-start.13 = (bf16[32,2048]{1,0:T(8,128)(2,1)S(1)}, bf16[32,2048]{1,0:T(8,128)(2,1)S(1)}, u32[]{:S(2)}, u32[]{:S(2)}) collective-permute-start(bf16[32,2048]{1,0:T(8,128)(2,1)S(1)} %get-tuple-element.63), channel_id=1, source_target_pairs={{0,4},{4,0},{8,12},{12,8},{1,5},{5,1},{9,13},{13,9},{2,6},{6,2},{1... | collective-permute-start | bytes 393224 | tf_op jit(solution)/shard_map/ppermute | solution.py:429
  41.0 7.7 %copy-start.1 = (bf16[64,32,256]{2,1,0:T(8,128)(2,1)S(1)}, bf16[64,32,256]{2,1,0:T(8,128)(2,1)}, u32[]{:S(2)}) copy-start(bf16[64,32,256]{2,1,0:T(8,128)(2,1)} %refs_4_.7) | copy-start | bytes 3145732
  41.0 7.7 %copy-start.2 = (bf16[64,32,256]{2,1,0:T(8,128)(2,1)S(1)}, bf16[64,32,256]{2,1,0:T(8,128)(2,1)}, u32[]{:S(2)}) copy-start(bf16[64,32,256]{2,1,0:T(8,128)(2,1)} %refs_5_.3) | copy-start | bytes 3145732
  41.6 11.1 %collective-permute-start.14 = (bf16[32,2048]{1,0:T(8,128)(2,1)S(1)}, bf16[32,2048]{1,0:T(8,128)(2,1)S(1)}, u32[]{:S(2)}, u32[]{:S(2)}) collective-permute-start(bf16[32,2048]{1,0:T(8,128)(2,1)S(1)} %get-tuple-element.76), channel_id=1, source_target_pairs={{0,12},{4,8},{8,4},{12,0},{1,13},{5,9},{9,5},{13,1},{2,14},{6,10},... | collective-permute-start | bytes 393224 | tf_op jit(solution)/shard_map/ppermute | solution.py:429
  45.4 13.1 %collective-permute-start.16 = (bf16[32,2048]{1,0:T(8,128)(2,1)S(1)}, bf16[32,2048]{1,0:T(8,128)(2,1)S(1)}, u32[]{:S(2)}, u32[]{:S(2)}) collective-permute-start(bf16[32,2048]{1,0:T(8,128)(2,1)S(1)} %get-tuple-element.79), channel_id=1, source_target_pairs={{0,8},{4,12},{8,0},{12,4},{1,9},{5,13},{9,1},{13,5},{2,10},{6,14},... | collective-permute-start | bytes 393224 | tf_op jit(solution)/shard_map/ppermute | solution.py:429
  48.2 9.6 %collective-permute-start.18 = (bf16[32,2048]{1,0:T(8,128)(2,1)S(1)}, bf16[32,2048]{1,0:T(8,128)(2,1)S(1)}, u32[]{:S(2)}, u32[]{:S(2)}) collective-permute-start(bf16[32,2048]{1,0:T(8,128)(2,1)S(1)} %get-tuple-element.82), channel_id=1, source_target_pairs={{0,4},{4,0},{8,12},{12,8},{1,5},{5,1},{9,13},{13,9},{2,6},{6,2},{1... | collective-permute-start | bytes 393224 | tf_op jit(solution)/shard_map/ppermute | solution.py:429
  57.8 10.3 %collective-permute-start.19 = (bf16[64,1792]{1,0:T(8,128)(2,1)S(1)}, bf16[64,1792]{1,0:T(8,128)(2,1)S(1)}, u32[]{:S(2)}, u32[]{:S(2)}) collective-permute-start(bf16[64,1792]{1,0:T(8,128)(2,1)S(1)} %get-tuple-element.83), channel_id=1, source_target_pairs={{0,12},{4,8},{8,4},{12,0},{1,13},{5,9},{9,5},{13,1},{2,14},{6,10},... | collective-permute-start | bytes 688136 | tf_op jit(solution)/shard_map/ppermute | solution.py:429
  58.4 28.4 %collective-permute-start.17 = (bf16[64,1792]{1,0:T(8,128)(2,1)S(1)}, bf16[64,1792]{1,0:T(8,128)(2,1)S(1)}, u32[]{:S(2)}, u32[]{:S(2)}) collective-permute-start(bf16[64,1792]{1,0:T(8,128)(2,1)S(1)} %get-tuple-element.80), channel_id=1, source_target_pairs={{0,8},{4,12},{8,0},{12,4},{1,9},{5,13},{9,1},{13,5},{2,10},{6,14},... | collective-permute-start | bytes 688136 | tf_op jit(solution)/shard_map/ppermute | solution.py:429
  58.7 28.1 %collective-permute-start.15 = (bf16[64,1792]{1,0:T(8,128)(2,1)S(1)}, bf16[64,1792]{1,0:T(8,128)(2,1)S(1)}, u32[]{:S(2)}, u32[]{:S(2)}) collective-permute-start(bf16[64,1792]{1,0:T(8,128)(2,1)S(1)} %get-tuple-element.77), channel_id=1, source_target_pairs={{0,4},{4,0},{8,12},{12,8},{1,5},{5,1},{9,13},{13,9},{2,6},{6,2},{1... | collective-permute-start | bytes 688136 | tf_op jit(solution)/shard_map/ppermute | solution.py:429
  65.9 21.6 %collective-permute-start.21 = (bf16[64,1792]{1,0:T(8,128)(2,1)S(1)}, bf16[64,1792]{1,0:T(8,128)(2,1)S(1)}, u32[]{:S(2)}, u32[]{:S(2)}) collective-permute-start(bf16[64,1792]{1,0:T(8,128)(2,1)S(1)} %get-tuple-element.86), channel_id=1, source_target_pairs={{0,4},{4,0},{8,12},{12,8},{1,5},{5,1},{9,13},{13,9},{2,6},{6,2},{1... | collective-permute-start | bytes 688136 | tf_op jit(solution)/shard_map/ppermute | solution.py:429
  66.0 25.7 %collective-permute-start.22 = (bf16[64,1792]{1,0:T(8,128)(2,1)S(1)}, bf16[64,1792]{1,0:T(8,128)(2,1)S(1)}, u32[]{:S(2)}, u32[]{:S(2)}) collective-permute-start(bf16[64,1792]{1,0:T(8,128)(2,1)S(1)} %get-tuple-element.87), channel_id=1, source_target_pairs={{0,8},{4,12},{8,0},{12,4},{1,9},{5,13},{9,1},{13,5},{2,10},{6,14},... | collective-permute-start | bytes 688136 | tf_op jit(solution)/shard_map/ppermute | solution.py:429
  68.2 23.6 %collective-permute-start.23 = (bf16[64,1792]{1,0:T(8,128)(2,1)S(1)}, bf16[64,1792]{1,0:T(8,128)(2,1)S(1)}, u32[]{:S(2)}, u32[]{:S(2)}) collective-permute-start(bf16[64,1792]{1,0:T(8,128)(2,1)S(1)} %get-tuple-element.88), channel_id=1, source_target_pairs={{0,12},{4,8},{8,4},{12,0},{1,13},{5,9},{9,5},{13,1},{2,14},{6,10},... | collective-permute-start | bytes 688136 | tf_op jit(solution)/shard_map/ppermute | solution.py:429
  86.9 6.7 %collective-permute-start.20 = (bf16[128,1792]{1,0:T(8,128)(2,1)S(1)}, bf16[128,1792]{1,0:T(8,128)(2,1)S(1)}, u32[]{:S(2)}, u32[]{:S(2)}) collective-permute-start(bf16[128,1792]{1,0:T(8,128)(2,1)S(1)} %pad_maximum_fusion), channel_id=1, source_target_pairs={{0,1},{1,0},{2,3},{3,2},{4,5},{5,4},{6,7},{7,6},{8,9},{9,8},{10,11... | collective-permute-start | bytes 1376264 | tf_op jit(solution)/shard_map/ppermute | solution.py:691
  87.0 5.3 %collective-permute-start.24 = (bf16[64,1792]{1,0:T(8,128)(2,1)S(1)}, bf16[64,1792]{1,0:T(8,128)(2,1)S(1)}, u32[]{:S(2)}, u32[]{:S(2)}) collective-permute-start(bf16[64,1792]{1,0:T(8,128)(2,1)S(1)} %get-tuple-element.85.refs_5_), channel_id=1, source_target_pairs={{0,1},{1,0},{2,3},{3,2},{4,5},{5,4},{6,7},{7,6},{8,9},{9,8},{10,11... | collective-permute-start | bytes 688136 | tf_op jit(solution)/shard_map/ppermute | solution.py:695
  87.5 4.8 %collective-permute-start.25 = (bf16[64,1792]{1,0:T(8,128)(2,1)S(1)}, bf16[64,1792]{1,0:T(8,128)(2,1)S(1)}, u32[]{:S(2)}, u32[]{:S(2)}) collective-permute-start(bf16[64,1792]{1,0:T(8,128)(2,1)S(1)} %collective-permute-done.21.refs_6_), channel_id=1, source_target_pairs={{0,1},{1,0},{2,3},{3,2},{4,5},{5,4},{6,7},{7,6},{8,9},{9,8},{10,11... | collective-permute-start | bytes 688136 | tf_op jit(solution)/shard_map/ppermute | solution.py:695
  91.7 1.5 %collective-permute-start.26 = (bf16[64,1792]{1,0:T(8,128)(2,1)S(1)}, bf16[64,1792]{1,0:T(8,128)(2,1)S(1)}, u32[]{:S(2)}, u32[]{:S(2)}) collective-permute-start(bf16[64,1792]{1,0:T(8,128)(2,1)S(1)} %collective-permute-done.22.refs_7_), channel_id=1, source_target_pairs={{0,1},{1,0},{2,3},{3,2},{4,5},{5,4},{6,7},{7,6},{8,9},{9,8},{10,11... | collective-permute-start | bytes 688136 | tf_op jit(solution)/shard_map/ppermute | solution.py:695
  91.8 1.8 %collective-permute-start.27 = (bf16[64,1792]{1,0:T(8,128)(2,1)S(1)}, bf16[64,1792]{1,0:T(8,128)(2,1)S(1)}, u32[]{:S(2)}, u32[]{:S(2)}) collective-permute-start(bf16[64,1792]{1,0:T(8,128)(2,1)S(1)} %collective-permute-done.23.refs_8_), channel_id=1, source_target_pairs={{0,1},{1,0},{2,3},{3,2},{4,5},{5,4},{6,7},{7,6},{8,9},{9,8},{10,11... | collective-permute-start | bytes 688136 | tf_op jit(solution)/shard_map/ppermute | solution.py:695

commit v18 on v16

--- a/solution.py
+++ b/solution.py
@@ -415,9 +415,8 @@
                 pick, jnp.concatenate(pieces, axis=0), preferred_element_type=jnp.float32
             )
             source = (here ^ number) * subs + (core ^ other)
-            out_ref[pl.ds(source * most, most)] = rows.reshape(
-                most, steps, rows.shape[1]
-            ).astype(jnp.bfloat16)
+            rows = rows.astype(jnp.bfloat16)
+            out_ref[pl.ds(source * most, most)] = rows.reshape(most, steps, rows.shape[1])
 
 
 def traded(blocks, axes):

time: 95.8 us -> 95.8 us (level)
  no operation moved by 1% of the time
where the time goes in v18:
time: 95.8 us; the launch traced here: 94.3 us
  Pallas kernels  33 us (34%)
  waiting for transfers between devices  31.5 us (33%)
  starting transfers between devices  28.6 us (30%)
    ppermute x18, waiting for transfers between devices, traded(): landed[shift] = lax.ppermute(blocks[shift], axes, pairs)  30.2 us
    ppermute x18, starting transfers between devices, traded(): landed[shift] = lax.ppermute(blocks[shift], axes, pairs)  24.3 us
    pallas_call x1, Pallas kernels, on_device(): pl.pallas_call(functools.partial(norm_pack_project_kernel, chunk_steps, r...  8.69 us
    pallas_call x2, Pallas kernels, project(): pl.pallas_call(functools.partial(project_kernel, begin), in_specs=[VMEM,...  8.15 us
    pallas_call x2, Pallas kernels, on_device(): pl.pallas_call(functools.partial(attend_kernel, chunk * chunk_steps, chun...  7.6 us
    pallas_call x1, Pallas kernels, on_device(): pl.pallas_call(functools.partial(norm_pack_kernel, chunk_steps, rows, flo...  3.45 us
    ppermute x5, starting transfers between devices, from_others(): landed.append(lax.ppermute(block, axis, pairs))  3.2 us
    pallas_call x2, Pallas kernels, down(): pl.pallas_call(functools.partial(down_kernel, lanes, spots), in_specs=[VM...  2.3 us
  transfers between devices with their start and end apart: 28, of which 8 were waited for; matrix products, arithmetic and copies ran while one was open for 1% of the time, Pallas kernels for 33%

profile of v18, /device:TPU:0, one launch (start us, length us, event | category | flops | bytes accessed | tf_op | source)
XLA Modules:
  0.0 94.3 jit_solution(16922342808766547387)
XLA Ops:
  0.0 0.5 collective-permute-start
  0.5 0.1 collective-permute-start.1
  0.6 0.4 collective-permute-start.2
  1.1 3.5 %norm_and_pack.1 = (bf16[32,1792]{1,0:T(8,128)(2,1)}, bf16[32,1792]{1,0:T(8,128)(2,1)}, bf16[32,1792]{1,0:T(8,128)(2,1)}, bf16[32,1792]{1,0:T(8,128)(2,1)}) custom-call(s32[1,64]{1,0:T(1,128)} %bitcast.23, s32[1,32]{1,0:T(1,128)} %bitcast.25, s32[1,64]{1,0:T(1,128)} %bitcast.27, f32[28,128]{1,0:T(8,128)} %bitcast.19, bf16[256,3584]{1,0:T(8,128)(2,1)} %bitcast.29), custom_call_target="tpu_custom_call" | custom-call | flops 1 | bytes 1 | tf_op jit(solution)/shard_map/norm_and_pack/pallas_call | solution.py:513
  4.5 4.7 %collective-permute-start.6 = (bf16[32,1792]{1,0:T(8,128)(2,1)}, bf16[32,1792]{1,0:T(8,128)(2,1)S(1)}, u32[]{:S(2)}, u32[]{:S(2)}) collective-permute-start(bf16[32,1792]{1,0:T(8,128)(2,1)} %get-tuple-element.50), channel_id=1, source_target_pairs={{0,12},{4,8},{8,4},{12,0},{1,13},{5,9},{9,5},{13,1},{2,14},{6,10},... | collective-permute-start | bytes 344072 | tf_op jit(solution)/shard_map/ppermute | solution.py:428
  9.3 0.6 collective-permute-start.8
  10.0 0.0 copy-start.8
  10.0 0.0 copy-start
  10.0 0.0 copy-start.5
  10.0 8.7 %norm_pack_project.1 = (bf16[256,3584]{1,0:T(8,128)(2,1)S(1)}, f32[256,1024]{1,0:T(8,128)S(1)}, s32[8,64]{1,0:T(8,128)S(1)}, bf16[32,1792]{1,0:T(8,128)(2,1)S(1)...) custom-call(s32[1,64]{1,0:T(1,128)S(1)} %bitcast.24, ...), custom_call_target="tpu_custom_call" | custom-call | flops 1 | bytes 1 | tf_op jit(solution)/shard_map/norm_pack_project/pallas_call | solution.py:543
  18.7 3.8 %collective-permute-start.3 = (bf16[32,1792]{1,0:T(8,128)(2,1)S(1)}, bf16[32,1792]{1,0:T(8,128)(2,1)S(1)}, u32[]{:S(2)}, u32[]{:S(2)}) collective-permute-start(bf16[32,1792]{1,0:T(8,128)(2,1)S(1)} %get-tuple-element.53), channel_id=1, source_target_pairs={{0,12},{4,8},{8,4},{12,0},{1,13},{5,9},{9,5},{13,1},{2,14},{6,10},... | collective-permute-start | bytes 344072 | tf_op jit(solution)/shard_map/ppermute | solution.py:428
  22.5 0.6 collective-permute-start.5
  23.2 1.1 %down.2.refs_0_ = f32[128,128]{1,0:T(8,128)S(1)} custom-call(bf16[32,1792]{1,0:T(8,128)(2,1)S(1)} %collective-permute-done.6.refs_0_, bf16[32,1792]{1,0:T(8,128)(2,1)S(1)} %collective-permute-done.7.refs_1_, bf16[32,1792]{1,0:T(8,128)(2,1)S(1)} %collective-permute-done.8.refs_2_, bf16[32,1792]{1,0:T(8,128)(2,1)S(1)} %copy-done.5, ...), custom_call_target="tpu_custom_call" | custom-call | flops 1 | bytes 1 | tf_op jit(solution)/shard_map/down/pallas_call | solution.py:576
  24.3 1.7 %collective-permute-start.9 = (f32[128,128]{1,0:T(8,128)S(1)}, f32[128,128]{1,0:T(8,128)S(1)}, u32[]{:S(2)}, u32[]{:S(2)}) collective-permute-start(f32[128,128]{1,0:T(8,128)S(1)} %down.2.refs_0_), channel_id=1, source_target_pairs={{0,2},{2,0},{1,3},{3,1},{4,6},{6,4},{5,7},{7,5},{8,10},{10,8},{9,1... | collective-permute-start | bytes 196616 | tf_op jit(solution)/shard_map/ppermute | solution.py:437
  26.0 0.0 copy-start.4
  26.0 3.8 %project.2.refs_7_ = f32[256,512]{1,0:T(8,128)S(1)} custom-call(bf16[256,3584]{1,0:T(8,128)(2,1)S(1)} %get-tuple-element.59.rows_ref, f32[18,128]{1,0:T(8,128)S(1)} %bitcast.17, bf16[3584,2304]{1,0:T(8,128)(2,1)} %weight_hbm.3), custom_call_target="tpu_custom_call" | custom-call | flops 1 | bytes 1 | tf_op jit(solution)/shard_map/project/pallas_call | solution.py:564
  29.9 0.5 up.2
  30.4 3.7 %collective-permute-start.11 = (bf16[32,2048]{1,0:T(8,128)(2,1)S(1)}, bf16[32,2048]{1,0:T(8,128)(2,1)S(1)}, u32[]{:S(2)}, u32[]{:S(2)}) collective-permute-start(bf16[32,2048]{1,0:T(8,128)(2,1)S(1)} %get-tuple-element.65), channel_id=1, source_target_pairs={{0,12},{4,8},{8,4},{12,0},{1,13},{5,9},{9,5},{13,1},{2,14},{6,10},... | collective-permute-start | bytes 393224 | tf_op jit(solution)/shard_map/ppermute | solution.py:428
  34.0 0.8 collective-permute-start.13
  34.8 0.1 compare_select_fusion
  34.9 1.2 %down.3.refs_0_ = f32[128,128]{1,0:T(8,128)S(1)} custom-call(bf16[32,1792]{1,0:T(8,128)(2,1)S(1)} %collective-permute-done.3.refs_0_, bf16[32,1792]{1,0:T(8,128)(2,1)S(1)} %collective-permute-done.4.refs_1_, bf16[32,1792]{1,0:T(8,128)(2,1)S(1)} %collective-permute-done.5.refs_2_, bf16[32,1792]{1,0:T(8,128)(2,1)S(1)} %get-tuple-element.66.refs_3_, ...), custom_call_target="tpu_custom_call" | custom-call | flops 1 | bytes 1 | tf_op jit(solution)/shard_map/down/pallas_call | solution.py:576
  36.1 0.5 collective-permute-start.10
  36.6 0.1 add_convert_fusion
  36.6 4.4 %project.3.refs_8_ = f32[256,768]{1,0:T(8,128)S(1)} custom-call(bf16[256,3584]{1,0:T(8,128)(2,1)S(1)} %get-tuple-element.59.rows_ref, f32[18,128]{1,0:T(8,128)S(1)} %bitcast.18, bf16[3584,2304]{1,0:T(8,128)(2,1)} %weight_hbm.3), custom_call_target="tpu_custom_call" | custom-call | flops 1 | bytes 1 | tf_op jit(solution)/shard_map/project/pallas_call | solution.py:564
  41.0 0.0 copy-start.1
  41.0 0.0 copy-start.2
  41.0 0.5 up.3
  41.5 3.8 %collective-permute-start.14 = (bf16[32,2048]{1,0:T(8,128)(2,1)S(1)}, bf16[32,2048]{1,0:T(8,128)(2,1)S(1)}, u32[]{:S(2)}, u32[]{:S(2)}) collective-permute-start(bf16[32,2048]{1,0:T(8,128)(2,1)S(1)} %get-tuple-element.76), channel_id=1, source_target_pairs={{0,12},{4,8},{8,4},{12,0},{1,13},{5,9},{9,5},{13,1},{2,14},{6,10},... | collective-permute-start | bytes 393224 | tf_op jit(solution)/shard_map/ppermute | solution.py:428
  45.3 3.5 %collective-permute-done.12.refs_10_ = bf16[32,2048]{1,0:T(8,128)(2,1)S(1)} collective-permute-done((bf16[32,2048]{1,0:T(8,128)(2,1)S(1)}, bf16[32,2048]{1,0:T(8,128)(2,1)S(1)}, u32[]{:S(2)}, u32[]{:S(2)}) %collective-permute-start.12) | collective-permute-done | bytes 131104 | tf_op jit(solution)/shard_map/ppermute | solution.py:428
  48.8 0.5 fusion
  49.4 3.9 %attend.2 = (f32[128,512]{1,0:T(8,128)S(1)}, bf16[64,1792]{1,0:T(8,128)(2,1)S(1)}, bf16[64,1792]{1,0:T(8,128)(2,1)S(1)}, bf16[64,1792]{1,0:T(8,128)(2,1)S(1)}, bf16[64,1792]{1,0:T(8,128)(2,1)S(1)}) custom-call(s32[8,64]{1,0:T(8,128)S(1)} %get-tuple-element.73.refs_0_, s32[1,64]{1,0:T(1,128)S(1)} %bitcast.21, f32[256,128]{1,0:T(8,128)S(1)} %get-tuple-element.90.refs_2_, ...), custom_call_target="tpu_custom_call" | custom-call | flops 1 | bytes 1 | tf_op jit(solution)/shard_map/attend/pallas_call | solution.py:629
  53.3 4.6 %collective-permute-done.18.refs_11_ = bf16[32,2048]{1,0:T(8,128)(2,1)S(1)} collective-permute-done((bf16[32,2048]{1,0:T(8,128)(2,1)S(1)}, bf16[32,2048]{1,0:T(8,128)(2,1)S(1)}, u32[]{:S(2)}, u32[]{:S(2)}) %collective-permute-start.18) | collective-permute-done | bytes 131104 | tf_op jit(solution)/shard_map/ppermute | solution.py:428
  57.9 0.5 collective-permute-start.19
  58.4 2.6 %collective-permute-done.16.refs_10_ = bf16[32,2048]{1,0:T(8,128)(2,1)S(1)} collective-permute-done((bf16[32,2048]{1,0:T(8,128)(2,1)S(1)}, bf16[32,2048]{1,0:T(8,128)(2,1)S(1)}, u32[]{:S(2)}, u32[]{:S(2)}) %collective-permute-start.16) | collective-permute-done | bytes 131104 | tf_op jit(solution)/shard_map/ppermute | solution.py:428
  61.1 1.3 %collective-permute-start.15 = (bf16[64,1792]{1,0:T(8,128)(2,1)S(1)}, bf16[64,1792]{1,0:T(8,128)(2,1)S(1)}, u32[]{:S(2)}, u32[]{:S(2)}) collective-permute-start(bf16[64,1792]{1,0:T(8,128)(2,1)S(1)} %get-tuple-element.77), channel_id=1, source_target_pairs={{0,4},{4,0},{8,12},{12,8},{1,5},{5,1},{9,13},{13,9},{2,6},{6,2},{1... | collective-permute-start | bytes 688136 | tf_op jit(solution)/shard_map/ppermute | solution.py:428
  62.3 3.7 %attend.3 = (bf16[64,1792]{1,0:T(8,128)(2,1)S(1)}, bf16[64,1792]{1,0:T(8,128)(2,1)S(1)}, bf16[64,1792]{1,0:T(8,128)(2,1)S(1)}, bf16[64,1792]{1,0:T(8,128)(2,1)S(1)}) custom-call(s32[8,64]{1,0:T(8,128)S(1)} %get-tuple-element.73.refs_0_, s32[1,64]{1,0:T(1,128)S(1)} %bitcast.22, f32[256,128]{1,0:T(8,128)S(1)} %get-tuple-element.90.refs_2_, ...), custom_call_target="tpu_custom_call" | custom-call | flops 1 | bytes 1 | tf_op jit(solution)/shard_map/attend/pallas_call | solution.py:629
  66.1 0.8 collective-permute-start.21
  66.9 2.9 %collective-permute-start.22 = (bf16[64,1792]{1,0:T(8,128)(2,1)S(1)}, bf16[64,1792]{1,0:T(8,128)(2,1)S(1)}, u32[]{:S(2)}, u32[]{:S(2)}) collective-permute-start(bf16[64,1792]{1,0:T(8,128)(2,1)S(1)} %get-tuple-element.87), channel_id=1, source_target_pairs={{0,8},{4,12},{8,0},{12,4},{1,9},{5,13},{9,1},{13,5},{2,10},{6,14},... | collective-permute-start | bytes 688136 | tf_op jit(solution)/shard_map/ppermute | solution.py:428
  69.8 0.7 collective-permute-start.23
  70.5 10.3 %collective-permute-done.17.refs_2_ = bf16[64,1792]{1,0:T(8,128)(2,1)S(1)} collective-permute-done((bf16[64,1792]{1,0:T(8,128)(2,1)S(1)}, bf16[64,1792]{1,0:T(8,128)(2,1)S(1)}, u32[]{:S(2)}, u32[]{:S(2)}) %collective-permute-start.17) | collective-permute-done | bytes 229408 | tf_op jit(solution)/shard_map/ppermute | solution.py:428
  80.9 0.1 collective-permute-start.20
  81.0 0.5 collective-permute-start.24
  81.5 0.2 collective-permute-done.21.refs_6_
  81.7 8.9 %collective-permute-done.22.refs_7_ = bf16[64,1792]{1,0:T(8,128)(2,1)S(1)} collective-permute-done((bf16[64,1792]{1,0:T(8,128)(2,1)S(1)}, bf16[64,1792]{1,0:T(8,128)(2,1)S(1)}, u32[]{:S(2)}, u32[]{:S(2)}) %collective-permute-start.22) | collective-permute-done | bytes 229408 | tf_op jit(solution)/shard_map/ppermute | solution.py:428
  90.6 0.5 collective-permute-start.27
  91.1 1.0 %collective-permute-done.26.refs_11_ = bf16[64,1792]{1,0:T(8,128)(2,1)S(1)} collective-permute-done((bf16[64,1792]{1,0:T(8,128)(2,1)S(1)}, bf16[64,1792]{1,0:T(8,128)(2,1)S(1)}, u32[]{:S(2)}, u32[]{:S(2)}) %collective-permute-start.26) | collective-permute-done | bytes 229408 | tf_op jit(solution)/shard_map/ppermute | solution.py:694
  92.1 0.3 collective-permute-done.27.refs_12_
  92.4 1.9 %place.1 = bf16[128,4,1792]{2,1,0:T(4,128)(2,1)} custom-call(bf16[64,1792]{1,0:T(8,128)(2,1)S(1)} %get-tuple-element.74.refs_0_, bf16[64,1792]{1,0:T(8,128)(2,1)S(1)} %collective-permute-done.15.refs_1_, bf16[64,1792]{1,0:T(8,128)(2,1)S(1)} %collective-permute-done.17.refs_2_, bf16[64,1792]{1,0:T(8,128)(2,1)S(1)} %collective-permute-done.19.refs_3_, ...), custom_call_target="tpu_custom_call" | custom-call | flops 1 | bytes 1 | tf_op jit(solution)/shard_map/place/pallas_call | solution.py:697
  (53 shorter events, 0.2 us)
Async XLA Ops:
  0.0 9.9 %copy-start.9 = (s32[64,1]{0,1:T(1,128)S(1)}, s32[64,1]{0,1:T(1,128)}, u32[]{:S(2)}) copy-start(s32[64,1]{0,1:T(1,128)} %param.17) | copy-start | bytes 772
  0.0 9.9 %copy-start.10 = (s32[32]{0:T(128)S(1)}, s32[32]{0:T(128)}, u32[]{:S(2)}) copy-start(s32[32]{0:T(128)} %param.18) | copy-start | bytes 388
  0.0 9.9 %copy-start.11 = (s32[64,1]{0,1:T(1,128)S(1)}, s32[64,1]{0,1:T(1,128)}, u32[]{:S(2)}) copy-start(s32[64,1]{0,1:T(1,128)} %param.25) | copy-start | bytes 772
  0.0 9.9 %copy-start.7 = (f32[3584]{0:T(1024)S(1)}, f32[3584]{0:T(1024)}, u32[]{:S(2)}) copy-start(f32[3584]{0:T(1024)} %param.14) | copy-start | bytes 43012
  0.0 9.9 %copy-start.6 = (f32[2304]{0:T(1024)S(1)}, f32[2304]{0:T(1024)}, u32[]{:S(2)}) copy-start(f32[2304]{0:T(1024)} %param.16) | copy-start | bytes 27652
  0.0 9.9 %collective-permute-start = (bf16[4,1792,128]{2,1,0:T(8,128)(2,1)}, bf16[4,1792,128]{2,1,0:T(8,128)(2,1)S(1)}, u32[]{:S(2)}, u32[]{:S(2)}) collective-permute-start(bf16[4,1792,128]{2,1,0:T(8,128)(2,1)} %refs_4_.5), channel_id=1, source_target_pairs={{0,1},{1,0},{2,3},{3,2},{4,5},{5,4},{6,7},{7,6},{8,9},{9,8},{10,11... | collective-permute-start | bytes 5505032 | tf_op jit(solution)/shard_map/ppermute | solution.py:437
  0.5 9.4 %collective-permute-start.1 = (bf16[256,1792]{1,0:T(8,128)(2,1)}, bf16[256,1792]{1,0:T(8,128)(2,1)S(1)}, u32[]{:S(2)}, u32[]{:S(2)}) collective-permute-start(bf16[256,1792]{1,0:T(8,128)(2,1)} %bitcast.10), channel_id=1, source_target_pairs={{0,1},{1,0},{2,3},{3,2},{4,5},{5,4},{6,7},{7,6},{8,9},{9,8},{10,11... | collective-permute-start | bytes 2752520 | tf_op jit(solution)/shard_map/ppermute | solution.py:437
  0.6 8.6 %collective-permute-start.2 = (bf16[256,256]{1,0:T(8,128)(2,1)}, bf16[256,256]{1,0:T(8,128)(2,1)S(1)}, u32[]{:S(2)}, u32[]{:S(2)}) collective-permute-start(bf16[256,256]{1,0:T(8,128)(2,1)} %bitcast.13), channel_id=1, source_target_pairs={{0,1},{1,0},{2,3},{3,2},{4,5},{5,4},{6,7},{7,6},{8,9},{9,8},{10,11... | collective-permute-start | bytes 393224 | tf_op jit(solution)/shard_map/ppermute | solution.py:437
  4.5 18.0 %collective-permute-start.6 = (bf16[32,1792]{1,0:T(8,128)(2,1)}, bf16[32,1792]{1,0:T(8,128)(2,1)S(1)}, u32[]{:S(2)}, u32[]{:S(2)}) collective-permute-start(bf16[32,1792]{1,0:T(8,128)(2,1)} %get-tuple-element.50), channel_id=1, source_target_pairs={{0,12},{4,8},{8,4},{12,0},{1,13},{5,9},{9,5},{13,1},{2,14},{6,10},... | collective-permute-start | bytes 344072 | tf_op jit(solution)/shard_map/ppermute | solution.py:428
  9.3 13.9 %collective-permute-start.7 = (bf16[32,1792]{1,0:T(8,128)(2,1)}, bf16[32,1792]{1,0:T(8,128)(2,1)S(1)}, u32[]{:S(2)}, u32[]{:S(2)}) collective-permute-start(bf16[32,1792]{1,0:T(8,128)(2,1)} %get-tuple-element.49), channel_id=1, source_target_pairs={{0,8},{4,12},{8,0},{12,4},{1,9},{5,13},{9,1},{13,5},{2,10},{6,14},... | collective-permute-start | bytes 344072 | tf_op jit(solution)/shard_map/ppermute | solution.py:428
  9.3 13.9 %collective-permute-start.8 = (bf16[32,1792]{1,0:T(8,128)(2,1)}, bf16[32,1792]{1,0:T(8,128)(2,1)S(1)}, u32[]{:S(2)}, u32[]{:S(2)}) collective-permute-start(bf16[32,1792]{1,0:T(8,128)(2,1)} %get-tuple-element.48), channel_id=1, source_target_pairs={{0,4},{4,0},{8,12},{12,8},{1,5},{5,1},{9,13},{13,9},{2,6},{6,2},{1... | collective-permute-start | bytes 344072 | tf_op jit(solution)/shard_map/ppermute | solution.py:428
  10.0 12.6 %copy-start.8 = (s32[64]{0:T(128)S(1)}, s32[64]{0:T(128)}, u32[]{:S(2)}) copy-start(s32[64]{0:T(128)} %param.19) | copy-start | bytes 772
  10.0 13.2 %copy-start = (bf16[4,1792,128]{2,1,0:T(8,128)(2,1)S(1)}, bf16[4,1792,128]{2,1,0:T(8,128)(2,1)}, u32[]{:S(2)}) copy-start(bf16[4,1792,128]{2,1,0:T(8,128)(2,1)} %refs_4_.5) | copy-start | bytes 5505028
  10.0 13.2 %copy-start.5 = (bf16[32,1792]{1,0:T(8,128)(2,1)S(1)}, bf16[32,1792]{1,0:T(8,128)(2,1)}, u32[]{:S(2)}) copy-start(bf16[32,1792]{1,0:T(8,128)(2,1)} %get-tuple-element.58.refs_3_) | copy-start | bytes 344068
  18.7 15.3 %collective-permute-start.3 = (bf16[32,1792]{1,0:T(8,128)(2,1)S(1)}, bf16[32,1792]{1,0:T(8,128)(2,1)S(1)}, u32[]{:S(2)}, u32[]{:S(2)}) collective-permute-start(bf16[32,1792]{1,0:T(8,128)(2,1)S(1)} %get-tuple-element.53), channel_id=1, source_target_pairs={{0,12},{4,8},{8,4},{12,0},{1,13},{5,9},{9,5},{13,1},{2,14},{6,10},... | collective-permute-start | bytes 344072 | tf_op jit(solution)/shard_map/ppermute | solution.py:428
  22.5 12.4 %collective-permute-start.4 = (bf16[32,1792]{1,0:T(8,128)(2,1)S(1)}, bf16[32,1792]{1,0:T(8,128)(2,1)S(1)}, u32[]{:S(2)}, u32[]{:S(2)}) collective-permute-start(bf16[32,1792]{1,0:T(8,128)(2,1)S(1)} %get-tuple-element.54), channel_id=1, source_target_pairs={{0,8},{4,12},{8,0},{12,4},{1,9},{5,13},{9,1},{13,5},{2,10},{6,14},... | collective-permute-start | bytes 344072 | tf_op jit(solution)/shard_map/ppermute | solution.py:428
  22.5 12.4 %collective-permute-start.5 = (bf16[32,1792]{1,0:T(8,128)(2,1)S(1)}, bf16[32,1792]{1,0:T(8,128)(2,1)S(1)}, u32[]{:S(2)}, u32[]{:S(2)}) collective-permute-start(bf16[32,1792]{1,0:T(8,128)(2,1)S(1)} %get-tuple-element.55), channel_id=1, source_target_pairs={{0,4},{4,0},{8,12},{12,8},{1,5},{5,1},{9,13},{13,9},{2,6},{6,2},{1... | collective-permute-start | bytes 344072 | tf_op jit(solution)/shard_map/ppermute | solution.py:428
  24.3 5.5 %collective-permute-start.9 = (f32[128,128]{1,0:T(8,128)S(1)}, f32[128,128]{1,0:T(8,128)S(1)}, u32[]{:S(2)}, u32[]{:S(2)}) collective-permute-start(f32[128,128]{1,0:T(8,128)S(1)} %down.2.refs_0_), channel_id=1, source_target_pairs={{0,2},{2,0},{1,3},{3,1},{4,6},{6,4},{5,7},{7,5},{8,10},{10,8},{9,1... | collective-permute-start | bytes 196616 | tf_op jit(solution)/shard_map/ppermute | solution.py:437
  26.0 3.8 %copy-start.3 = (bf16[4,64,1792]{2,1,0:T(8,128)(2,1)S(1)}, bf16[4,64,1792]{2,1,0:T(8,128)(2,1)}, u32[]{:S(2)}) copy-start(bf16[4,64,1792]{2,1,0:T(8,128)(2,1)} %param.23) | copy-start | bytes 2752516
  26.0 3.8 %copy-start.4 = (bf16[4,64,256]{2,1,0:T(8,128)(2,1)S(1)}, bf16[4,64,256]{2,1,0:T(8,128)(2,1)}, u32[]{:S(2)}) copy-start(bf16[4,64,256]{2,1,0:T(8,128)(2,1)} %param.24) | copy-start | bytes 393220
  30.4 11.2 %collective-permute-start.11 = (bf16[32,2048]{1,0:T(8,128)(2,1)S(1)}, bf16[32,2048]{1,0:T(8,128)(2,1)S(1)}, u32[]{:S(2)}, u32[]{:S(2)}) collective-permute-start(bf16[32,2048]{1,0:T(8,128)(2,1)S(1)} %get-tuple-element.65), channel_id=1, source_target_pairs={{0,12},{4,8},{8,4},{12,0},{1,13},{5,9},{9,5},{13,1},{2,14},{6,10},... | collective-permute-start | bytes 393224 | tf_op jit(solution)/shard_map/ppermute | solution.py:428
  34.0 14.8 %collective-permute-start.12 = (bf16[32,2048]{1,0:T(8,128)(2,1)S(1)}, bf16[32,2048]{1,0:T(8,128)(2,1)S(1)}, u32[]{:S(2)}, u32[]{:S(2)}) collective-permute-start(bf16[32,2048]{1,0:T(8,128)(2,1)S(1)} %get-tuple-element.64), channel_id=1, source_target_pairs={{0,8},{4,12},{8,0},{12,4},{1,9},{5,13},{9,1},{13,5},{2,10},{6,14},... | collective-permute-start | bytes 393224 | tf_op jit(solution)/shard_map/ppermute | solution.py:428
  34.0 14.8 %collective-permute-start.13 = (bf16[32,2048]{1,0:T(8,128)(2,1)S(1)}, bf16[32,2048]{1,0:T(8,128)(2,1)S(1)}, u32[]{:S(2)}, u32[]{:S(2)}) collective-permute-start(bf16[32,2048]{1,0:T(8,128)(2,1)S(1)} %get-tuple-element.63), channel_id=1, source_target_pairs={{0,4},{4,0},{8,12},{12,8},{1,5},{5,1},{9,13},{13,9},{2,6},{6,2},{1... | collective-permute-start | bytes 393224 | tf_op jit(solution)/shard_map/ppermute | solution.py:428
  36.1 4.9 %collective-permute-start.10 = (f32[128,128]{1,0:T(8,128)S(1)}, f32[128,128]{1,0:T(8,128)S(1)}, u32[]{:S(2)}, u32[]{:S(2)}) collective-permute-start(f32[128,128]{1,0:T(8,128)S(1)} %down.3.refs_0_), channel_id=1, source_target_pairs={{0,2},{2,0},{1,3},{3,1},{4,6},{6,4},{5,7},{7,5},{8,10},{10,8},{9,1... | collective-permute-start | bytes 196616 | tf_op jit(solution)/shard_map/ppermute | solution.py:437
  41.0 8.4 %copy-start.1 = (bf16[64,32,256]{2,1,0:T(8,128)(2,1)S(1)}, bf16[64,32,256]{2,1,0:T(8,128)(2,1)}, u32[]{:S(2)}) copy-start(bf16[64,32,256]{2,1,0:T(8,128)(2,1)} %refs_4_.7) | copy-start | bytes 3145732
  41.0 8.4 %copy-start.2 = (bf16[64,32,256]{2,1,0:T(8,128)(2,1)S(1)}, bf16[64,32,256]{2,1,0:T(8,128)(2,1)}, u32[]{:S(2)}) copy-start(bf16[64,32,256]{2,1,0:T(8,128)(2,1)} %refs_5_.3) | copy-start | bytes 3145732
  41.5 11.8 %collective-permute-start.14 = (bf16[32,2048]{1,0:T(8,128)(2,1)S(1)}, bf16[32,2048]{1,0:T(8,128)(2,1)S(1)}, u32[]{:S(2)}, u32[]{:S(2)}) collective-permute-start(bf16[32,2048]{1,0:T(8,128)(2,1)S(1)} %get-tuple-element.76), channel_id=1, source_target_pairs={{0,12},{4,8},{8,4},{12,0},{1,13},{5,9},{9,5},{13,1},{2,14},{6,10},... | collective-permute-start | bytes 393224 | tf_op jit(solution)/shard_map/ppermute | solution.py:428
  48.8 12.2 %collective-permute-start.16 = (bf16[32,2048]{1,0:T(8,128)(2,1)S(1)}, bf16[32,2048]{1,0:T(8,128)(2,1)S(1)}, u32[]{:S(2)}, u32[]{:S(2)}) collective-permute-start(bf16[32,2048]{1,0:T(8,128)(2,1)S(1)} %get-tuple-element.79), channel_id=1, source_target_pairs={{0,8},{4,12},{8,0},{12,4},{1,9},{5,13},{9,1},{13,5},{2,10},{6,14},... | collective-permute-start | bytes 393224 | tf_op jit(solution)/shard_map/ppermute | solution.py:428
  48.8 9.1 %collective-permute-start.18 = (bf16[32,2048]{1,0:T(8,128)(2,1)S(1)}, bf16[32,2048]{1,0:T(8,128)(2,1)S(1)}, u32[]{:S(2)}, u32[]{:S(2)}) collective-permute-start(bf16[32,2048]{1,0:T(8,128)(2,1)S(1)} %get-tuple-element.82), channel_id=1, source_target_pairs={{0,4},{4,0},{8,12},{12,8},{1,5},{5,1},{9,13},{13,9},{2,6},{6,2},{1... | collective-permute-start | bytes 393224 | tf_op jit(solution)/shard_map/ppermute | solution.py:428
  57.9 11.9 %collective-permute-start.19 = (bf16[64,1792]{1,0:T(8,128)(2,1)S(1)}, bf16[64,1792]{1,0:T(8,128)(2,1)S(1)}, u32[]{:S(2)}, u32[]{:S(2)}) collective-permute-start(bf16[64,1792]{1,0:T(8,128)(2,1)S(1)} %get-tuple-element.83), channel_id=1, source_target_pairs={{0,12},{4,8},{8,4},{12,0},{1,13},{5,9},{9,5},{13,1},{2,14},{6,10},... | collective-permute-start | bytes 688136 | tf_op jit(solution)/shard_map/ppermute | solution.py:428
  61.1 19.8 %collective-permute-start.17 = (bf16[64,1792]{1,0:T(8,128)(2,1)S(1)}, bf16[64,1792]{1,0:T(8,128)(2,1)S(1)}, u32[]{:S(2)}, u32[]{:S(2)}) collective-permute-start(bf16[64,1792]{1,0:T(8,128)(2,1)S(1)} %get-tuple-element.80), channel_id=1, source_target_pairs={{0,8},{4,12},{8,0},{12,4},{1,9},{5,13},{9,1},{13,5},{2,10},{6,14},... | collective-permute-start | bytes 688136 | tf_op jit(solution)/shard_map/ppermute | solution.py:428
  61.1 19.8 %collective-permute-start.15 = (bf16[64,1792]{1,0:T(8,128)(2,1)S(1)}, bf16[64,1792]{1,0:T(8,128)(2,1)S(1)}, u32[]{:S(2)}, u32[]{:S(2)}) collective-permute-start(bf16[64,1792]{1,0:T(8,128)(2,1)S(1)} %get-tuple-element.77), channel_id=1, source_target_pairs={{0,4},{4,0},{8,12},{12,8},{1,5},{5,1},{9,13},{13,9},{2,6},{6,2},{1... | collective-permute-start | bytes 688136 | tf_op jit(solution)/shard_map/ppermute | solution.py:428
  66.1 15.7 %collective-permute-start.21 = (bf16[64,1792]{1,0:T(8,128)(2,1)S(1)}, bf16[64,1792]{1,0:T(8,128)(2,1)S(1)}, u32[]{:S(2)}, u32[]{:S(2)}) collective-permute-start(bf16[64,1792]{1,0:T(8,128)(2,1)S(1)} %get-tuple-element.86), channel_id=1, source_target_pairs={{0,4},{4,0},{8,12},{12,8},{1,5},{5,1},{9,13},{13,9},{2,6},{6,2},{1... | collective-permute-start | bytes 688136 | tf_op jit(solution)/shard_map/ppermute | solution.py:428
  66.9 23.7 %collective-permute-start.22 = (bf16[64,1792]{1,0:T(8,128)(2,1)S(1)}, bf16[64,1792]{1,0:T(8,128)(2,1)S(1)}, u32[]{:S(2)}, u32[]{:S(2)}) collective-permute-start(bf16[64,1792]{1,0:T(8,128)(2,1)S(1)} %get-tuple-element.87), channel_id=1, source_target_pairs={{0,8},{4,12},{8,0},{12,4},{1,9},{5,13},{9,1},{13,5},{2,10},{6,14},... | collective-permute-start | bytes 688136 | tf_op jit(solution)/shard_map/ppermute | solution.py:428
  69.8 20.8 %collective-permute-start.23 = (bf16[64,1792]{1,0:T(8,128)(2,1)S(1)}, bf16[64,1792]{1,0:T(8,128)(2,1)S(1)}, u32[]{:S(2)}, u32[]{:S(2)}) collective-permute-start(bf16[64,1792]{1,0:T(8,128)(2,1)S(1)} %get-tuple-element.88), channel_id=1, source_target_pairs={{0,12},{4,8},{8,4},{12,0},{1,13},{5,9},{9,5},{13,1},{2,14},{6,10},... | collective-permute-start | bytes 688136 | tf_op jit(solution)/shard_map/ppermute | solution.py:428
  80.9 11.5 %collective-permute-start.20 = (bf16[128,1792]{1,0:T(8,128)(2,1)S(1)}, bf16[128,1792]{1,0:T(8,128)(2,1)S(1)}, u32[]{:S(2)}, u32[]{:S(2)}) collective-permute-start(bf16[128,1792]{1,0:T(8,128)(2,1)S(1)} %pad_maximum_fusion), channel_id=1, source_target_pairs={{0,1},{1,0},{2,3},{3,2},{4,5},{5,4},{6,7},{7,6},{8,9},{9,8},{10,11... | collective-permute-start | bytes 1376264 | tf_op jit(solution)/shard_map/ppermute | solution.py:690
  81.0 10.1 %collective-permute-start.24 = (bf16[64,1792]{1,0:T(8,128)(2,1)S(1)}, bf16[64,1792]{1,0:T(8,128)(2,1)S(1)}, u32[]{:S(2)}, u32[]{:S(2)}) collective-permute-start(bf16[64,1792]{1,0:T(8,128)(2,1)S(1)} %get-tuple-element.85.refs_5_), channel_id=1, source_target_pairs={{0,1},{1,0},{2,3},{3,2},{4,5},{5,4},{6,7},{7,6},{8,9},{9,8},{10,11... | collective-permute-start | bytes 688136 | tf_op jit(solution)/shard_map/ppermute | solution.py:694
  81.7 9.4 %collective-permute-start.25 = (bf16[64,1792]{1,0:T(8,128)(2,1)S(1)}, bf16[64,1792]{1,0:T(8,128)(2,1)S(1)}, u32[]{:S(2)}, u32[]{:S(2)}) collective-permute-start(bf16[64,1792]{1,0:T(8,128)(2,1)S(1)} %collective-permute-done.21.refs_6_), channel_id=1, source_target_pairs={{0,1},{1,0},{2,3},{3,2},{4,5},{5,4},{6,7},{7,6},{8,9},{9,8},{10,11... | collective-permute-start | bytes 688136 | tf_op jit(solution)/shard_map/ppermute | solution.py:694
  90.6 1.5 %collective-permute-start.26 = (bf16[64,1792]{1,0:T(8,128)(2,1)S(1)}, bf16[64,1792]{1,0:T(8,128)(2,1)S(1)}, u32[]{:S(2)}, u32[]{:S(2)}) collective-permute-start(bf16[64,1792]{1,0:T(8,128)(2,1)S(1)} %collective-permute-done.22.refs_7_), channel_id=1, source_target_pairs={{0,1},{1,0},{2,3},{3,2},{4,5},{5,4},{6,7},{7,6},{8,9},{9,8},{10,11... | collective-permute-start | bytes 688136 | tf_op jit(solution)/shard_map/ppermute | solution.py:694
  90.6 1.8 %collective-permute-start.27 = (bf16[64,1792]{1,0:T(8,128)(2,1)S(1)}, bf16[64,1792]{1,0:T(8,128)(2,1)S(1)}, u32[]{:S(2)}, u32[]{:S(2)}) collective-permute-start(bf16[64,1792]{1,0:T(8,128)(2,1)S(1)} %collective-permute-done.23.refs_8_), channel_id=1, source_target_pairs={{0,1},{1,0},{2,3},{3,2},{4,5},{5,4},{6,7},{7,6},{8,9},{9,8},{10,11... | collective-permute-start | bytes 688136 | tf_op jit(solution)/shard_map/ppermute | solution.py:694
